TPU v7x, 32 devices: a whole 2x2x4 slice. The times are simulated.
32 devices in a mesh: wide: 16 (over z, y, x), narrow: 2 (over core).
Axes of the slice: x: 2, y: 2, z: 4, core: 2. Of those that a mesh axis runs over, the one named last changes fastest.
Arguments:
- tokens: bfloat16 [64, 1024, 768], P(('wide', 'narrow')), may hold values from -6 to 6
- lengths: int32 [64], P(('wide', 'narrow')), may hold values from 64 to 1024, as said below
- rand_mix: bfloat16 [12288, 1024], P(('wide', 'narrow')), may hold values from -6 to 6
- w_value: bfloat16 [768, 768], P(('wide', 'narrow')), may hold values from -0.21875 to 0.21875
- w_out: bfloat16 [768, 768], P(('wide', 'narrow')), may hold values from -0.875 to 0.875
- w_up: bfloat16 [768, 3072], P(('wide', 'narrow')), may hold values from -0.21875 to 0.21875
- w_down: bfloat16 [3072, 768], P(('wide', 'narrow')), may hold values from -0.109375 to 0.109375
- gain_mix: bfloat16 [768], P(('wide', 'narrow')), may hold values from 0.099609375 to 1.8984375
- gain_ffn: bfloat16 [768], P(('wide', 'narrow')), may hold values from 0.099609375 to 1.8984375
- grad_out: bfloat16 [64, 1024, 768], P(('wide', 'narrow')), may hold values from -6 to 6
Outputs:
- output: float32 [64, 1024, 768], P(('wide', 'narrow'))
- grad_tokens: float32 [64, 1024, 768], P(('wide', 'narrow'))
- grad_rand: float32 [12288, 1024], P(('wide', 'narrow'))
- grad_value: float32 [768, 768], P(('wide', 'narrow'))
- grad_outproj: float32 [768, 768], P(('wide', 'narrow'))
- grad_up: float32 [768, 3072], P(('wide', 'narrow'))
- grad_down: float32 [3072, 768], P(('wide', 'narrow'))
- grad_gain_mix: float32 [768], P(('wide', 'narrow'))
- grad_gain_ffn: float32 [768], P(('wide', 'narrow'))
Inputs may be any that keep to these rules, and one draw needn't show every extreme that they name: `lengths`: some item has exactly 1024 valid tokens and some exactly 64.
All inputs are finite; a program needn't handle non-finite values.
Results may differ from a plain program's by a relative error of at most 0.009.
Values may be sent and summed in bfloat16 or wider, within the bound.
No kernel may reach another device: no remote copies, remote signals or barrier semaphores. Data moves between devices by JAX's collectives and lax.ppermute only.
A program may use at most 448 MiB of HBM per device.

v0:
```python
from functools import partial

import jax
import jax.numpy as jnp
from jax import lax
from jax.sharding import PartitionSpec as P

HEADS = 12
HEAD = 64
LMAX = 1024


EPSILON = 1e-05


def rms_norm(values, gain):
    scale = lax.rsqrt(jnp.mean(values * values, axis=-1, keepdims=True) + EPSILON)
    return values * scale * gain


def split_heads(block):
    return block.reshape(LMAX, HEADS, HEAD).transpose(1, 0, 2)


def merge_heads(block):
    return block.transpose(1, 0, 2).reshape(LMAX, HEADS * HEAD)


def masked_scores(key_mask, rand_head):
    return jnp.where(key_mask[None, :] > 0, rand_head.astype(jnp.float32), -1e30)


def head_forward(key_mask, paired):
    rand_head, value_head = paired
    scores = masked_scores(key_mask, rand_head)
    row_peak = jnp.max(scores, axis=-1, keepdims=True)
    exponent = jnp.exp(scores - row_peak)
    denom_sum = jnp.sum(exponent, axis=-1, keepdims=True)
    attention = exponent / denom_sum * key_mask[:, None]
    mixed = jnp.dot(attention.astype(jnp.bfloat16), value_head, preferred_element_type=jnp.float32)
    return (mixed.astype(jnp.bfloat16), row_peak + jnp.log(denom_sum))


def head_backward(key_mask, paired):
    rand_head, value_head, mix_grad, log_total = paired
    scores = masked_scores(key_mask, rand_head)
    attention = jnp.exp(scores - log_total) * key_mask[:, None]
    prob_grad = jnp.einsum("id,jd->ij", mix_grad, value_head, preferred_element_type=jnp.float32)
    value_grad = jnp.einsum(
        "ij,id->jd", attention.astype(jnp.bfloat16), mix_grad, preferred_element_type=jnp.float32
    )
    score_grad = attention * (prob_grad - jnp.sum(prob_grad * attention, axis=-1, keepdims=True))
    return (score_grad, value_grad)


def shards(tokens, lengths, rand_mix, w_value, w_out, w_up, w_down, gain_mix, gain_ffn, grad_out):
    item_count = tokens.shape[0]
    width = tokens.shape[2]
    row_count = item_count * LMAX
    tokens_flat = tokens.reshape(row_count, width).astype(jnp.float32)
    positions = jnp.arange(LMAX, dtype=jnp.int32)
    valid_table = (positions[None, :] < lengths[:, None]).astype(jnp.float32)
    row_valid = valid_table.reshape(row_count, 1)
    forward_set = (
        lax.all_gather(rand_mix, ("wide", "narrow"), axis=0, tiled=True),
        lax.all_gather(w_value, ("wide", "narrow"), axis=0, tiled=True),
        lax.all_gather(w_out, ("wide", "narrow"), axis=0, tiled=True),
        lax.all_gather(w_up, ("wide", "narrow"), axis=0, tiled=True),
        lax.all_gather(w_down, ("wide", "narrow"), axis=0, tiled=True),
        lax.all_gather(gain_mix, ("wide", "narrow"), axis=0, tiled=True),
        lax.all_gather(gain_ffn, ("wide", "narrow"), axis=0, tiled=True),
    )
    rand_all, value_all, out_all, up_all, down_all, gain_first, gain_second = forward_set
    normed = rms_norm(tokens_flat, gain_first.astype(jnp.float32)).astype(jnp.bfloat16)
    values = jnp.dot(normed, value_all, preferred_element_type=jnp.float32).astype(jnp.bfloat16)
    rand_heads = rand_all.reshape(HEADS, LMAX, LMAX)
    mixed_parts = []
    totals_kept = []
    for item_index in range(item_count):
        item_values = split_heads(values[item_index * LMAX : (item_index + 1) * LMAX])
        mixed_heads, log_total = lax.map(
            partial(head_forward, valid_table[item_index]), (rand_heads, item_values)
        )
        mixed_parts.append(merge_heads(mixed_heads))
        totals_kept.append(log_total)
    mixed = jnp.concatenate(mixed_parts, axis=0)
    residual = tokens_flat + jnp.dot(mixed, out_all, preferred_element_type=jnp.float32)
    normed_two = rms_norm(residual, gain_second.astype(jnp.float32)).astype(jnp.bfloat16)
    up_proj = jnp.dot(normed_two, up_all, preferred_element_type=jnp.float32)
    active = jax.nn.gelu(up_proj).astype(jnp.bfloat16)
    branch = jnp.dot(active, down_all, preferred_element_type=jnp.float32)
    output = row_valid * (residual + branch)
    back_set = (
        lax.all_gather(rand_mix, ("wide", "narrow"), axis=0, tiled=True),
        lax.all_gather(w_value, ("wide", "narrow"), axis=0, tiled=True),
        lax.all_gather(w_out, ("wide", "narrow"), axis=0, tiled=True),
        lax.all_gather(w_up, ("wide", "narrow"), axis=0, tiled=True),
        lax.all_gather(w_down, ("wide", "narrow"), axis=0, tiled=True),
        lax.all_gather(gain_mix, ("wide", "narrow"), axis=0, tiled=True),
        lax.all_gather(gain_ffn, ("wide", "narrow"), axis=0, tiled=True),
    )
    rand_back, value_back, out_back, up_back, down_back, gain_back_one, gain_back_two = back_set
    cotangent = grad_out.reshape(row_count, width).astype(jnp.float32)
    masked = row_valid * cotangent
    branch_grad = masked.astype(jnp.bfloat16)
    grad_down = jnp.einsum("rk,rd->kd", active, branch_grad, preferred_element_type=jnp.float32)
    active_grad = jnp.einsum(
        "rd,kd->rk", branch_grad, down_back, preferred_element_type=jnp.float32
    )
    gelu_value, gelu_pull = jax.vjp(jax.nn.gelu, up_proj)
    up_grad = gelu_pull(active_grad)[0].astype(jnp.bfloat16)
    grad_up = jnp.einsum("rd,rk->dk", normed_two, up_grad, preferred_element_type=jnp.float32)
    normed_two_grad = jnp.einsum("rk,dk->rd", up_grad, up_back, preferred_element_type=jnp.float32)
    norm_value, norm_pull = jax.vjp(rms_norm, residual, gain_back_two.astype(jnp.float32))
    residual_part, gain_two_grad = norm_pull(normed_two_grad)
    residual_grad = masked + residual_part
    attn_grad = residual_grad.astype(jnp.bfloat16)
    grad_outproj = jnp.einsum("rd,re->de", mixed, attn_grad, preferred_element_type=jnp.float32)
    mixed_grad = jnp.einsum(
        "re,de->rd", attn_grad, out_back, preferred_element_type=jnp.float32
    ).astype(jnp.bfloat16)
    rand_heads_back = rand_back.reshape(HEADS, LMAX, LMAX)
    rand_grad = jnp.zeros((HEADS, LMAX, LMAX), jnp.float32)
    value_parts = []
    for item_index in range(item_count):
        lower_row = item_index * LMAX
        upper_row = lower_row + LMAX
        item_values = split_heads(values[lower_row:upper_row])
        item_mix_grad = split_heads(mixed_grad[lower_row:upper_row])
        score_grad, value_grad = lax.map(
            partial(head_backward, valid_table[item_index]),
            (rand_heads_back, item_values, item_mix_grad, totals_kept[item_index]),
        )
        rand_grad = rand_grad + score_grad
        value_parts.append(merge_heads(value_grad))
    values_grad = jnp.concatenate(value_parts, axis=0).astype(jnp.bfloat16)
    grad_value = jnp.einsum("rd,re->de", normed, values_grad, preferred_element_type=jnp.float32)
    normed_grad = jnp.einsum(
        "re,de->rd", values_grad, value_back, preferred_element_type=jnp.float32
    )
    norm_first, first_pull = jax.vjp(rms_norm, tokens_flat, gain_back_one.astype(jnp.float32))
    token_part, gain_one_grad = first_pull(normed_grad)
    tokens_grad = residual_grad + token_part
    rand_flat = rand_grad.reshape(HEADS * LMAX, LMAX)
    all_shards = (
        lax.psum_scatter(rand_flat, ("wide", "narrow"), scatter_dimension=0, tiled=True),
        lax.psum_scatter(grad_value, ("wide", "narrow"), scatter_dimension=0, tiled=True),
        lax.psum_scatter(grad_outproj, ("wide", "narrow"), scatter_dimension=0, tiled=True),
        lax.psum_scatter(grad_up, ("wide", "narrow"), scatter_dimension=0, tiled=True),
        lax.psum_scatter(grad_down, ("wide", "narrow"), scatter_dimension=0, tiled=True),
        lax.psum_scatter(gain_one_grad, ("wide", "narrow"), scatter_dimension=0, tiled=True),
        lax.psum_scatter(gain_two_grad, ("wide", "narrow"), scatter_dimension=0, tiled=True),
    )
    rand_shard, value_shard, outproj_shard, up_shard, down_shard, gain_one_shard, gain_two_shard = (
        all_shards
    )
    return (
        output.reshape(item_count, LMAX, width),
        tokens_grad.reshape(item_count, LMAX, width),
        rand_shard,
        value_shard,
        outproj_shard,
        up_shard,
        down_shard,
        gain_one_shard,
        gain_two_shard,
    )


def solution(mesh):
    in_specs = (
        P(("wide", "narrow"), None, None),
        P(("wide", "narrow")),
        P(("wide", "narrow"), None),
        P(("wide", "narrow"), None),
        P(("wide", "narrow"), None),
        P(("wide", "narrow"), None),
        P(("wide", "narrow"), None),
        P(("wide", "narrow")),
        P(("wide", "narrow")),
        P(("wide", "narrow"), None, None),
    )
    out_specs = (
        P(("wide", "narrow"), None, None),
        P(("wide", "narrow"), None, None),
        P(("wide", "narrow"), None),
        P(("wide", "narrow"), None),
        P(("wide", "narrow"), None),
        P(("wide", "narrow"), None),
        P(("wide", "narrow"), None),
        P(("wide", "narrow")),
        P(("wide", "narrow")),
    )
    return jax.shard_map(shards, mesh=mesh, in_specs=in_specs, out_specs=out_specs, check_vma=False)
```

profile of v0, /device:TPU:0, one launch (start us, length us, event | category | flops | bytes accessed | tf_op | source)
XLA Modules:
  0.0 1686.3 jit_solution(10737242797934667315)
XLA Ops:
  12.3 42.0 %all-reduce.5 = (bf16[768]{0:T(1024)(128)(2,1)S(1)}, bf16[768]{0:T(1024)(128)(2,1)S(1)}) all-reduce(bf16[768]{0:T(1024)(128)(2,1)S(1)} %dynamic-update-slice, bf16[768]{0:T(1024)(128)(2,1)S(1)} %dynamic-update-slice.1), channel_id=1, replica_groups=mesh['wide'=16,'narrow'=2] {'wide','narrow'}, use_global_device_ids=true, to_apply=%add | all-reduce | flops 1536 | bytes 6144
  82.9 141.4 %all-gather.6.cloned.1.call-done = bf16[12288,1024]{1,0:T(8,128)(2,1)} async-done(((bf16[384,1024]{1,0:T(8,128)(2,1)}), bf16[12288,1024]{1,0:T(8,128)(2,1)}) %all-gather.6.cloned.1.call-update) | async-done | bytes 25165840 | tf_op jit(solution)/shard_map/all_gather | solution.py:65
  225.6 100.5 %while.49 = (s32[]{:T(128)}, bf16[12,1024,64]{1,2,0:T(8,128)(2,1)}, f32[12,1024,1]{1,2,0:T(1,128)S(1)}, f32[1,1024]{1,0:T(1,128)S(1)}, bf16[12,1024,1024]{2,1,0:...) while((s32[]{:T(128)}, bf16[12,1024,64]{1,2,0:T(8,128)(2,1)}, f32[12,1024,1]{1,2,0:T(1,128)S(1)}, ...), condition=%wide.region_8.9_spmd, body=%wide.region_5.8_spmd.sunk | while | flops 147914752 | bytes 6739553 | solution.py:81
  328.1 100.7 %while.48 = (s32[]{:T(128)}, bf16[12,1024,64]{1,2,0:T(8,128)(2,1)}, f32[12,1024,1]{1,2,0:T(1,128)S(1)}, f32[1,1024]{1,0:T(1,128)S(1)}, bf16[12,1024,1024]{2,1,0:...) while((s32[]{:T(128)}, bf16[12,1024,64]{1,2,0:T(8,128)(2,1)}, f32[12,1024,1]{1,2,0:T(1,128)S(1)}, ...), condition=%wide.region_4.5_spmd, body=%wide.region_1.4_spmd.sunk | while | flops 147914752 | bytes 6739553 | solution.py:81
  428.8 32.7 %copy.36 = bf16[12,1024,1024]{1,2,0:T(8,128)(2,1)} copy(bf16[12,1024,1024]{2,1,0:T(8,128)(2,1)} %get-tuple-element.583) | data formatting | bytes 50331648 | tf_op jit(solution)/shard_map/while | solution.py:130
  461.5 7.8 multiply_reduce_fusion.2
  469.3 18.1 %fusion.155 = f32[2048,3072]{1,0:T(8,128)} fusion(bf16[768,3072]{1,0:T(8,128)(2,1)} %all-gather.12.cloned.1.call-done, f32[2048,768]{1,0:T(8,128)} %get-tuple-element.290, f32[768]{0:T(1024)S(1)} %convert_element_type.135, f32[2048]{0:T(1024)S(1)} %fusion.148), kind=kOutput, calls=%fused_computation.176 | convolution fusion | flops 9668395008 | bytes 36187136 | tf_op jit(solution)/shard_map/dot_general | solution.py:89
  487.5 27.5 %fusion.130 = bf16[2048,3072]{1,0:T(8,128)(2,1)} fusion(f32[2048,3072]{1,0:T(8,128)} %fusion.155, bf16[2048,768]{1,0:T(8,128)(2,1)S(1)} %copy-done.6, bf16[3072,768]{1,0:T(8,128)(2,1)} %all-gather.14.cloned.1.call-done), kind=kOutput, calls=%fused_computation.126 | convolution fusion | flops 9789505536 | bytes 45613056 | tf_op jit(solution)/shard_map/rd,kd->rk/dot_general | solution.py:107
  515.0 17.3 %multiply_reduce_fusion = (f32[768]{0:T(1024)}, f32[2048]{0:T(1024)S(1)}, f32[2048,768]{1,0:T(8,128)}) fusion(f32[2048,768]{1,0:T(8,128)S(1)} %copy-done.5, f32[2048]{0:T(1024)S(1)} %fusion.148, f32[768]{0:T(1024)S(1)} %convert_element_type.135, bf16[2048,3072]{1,0:T(8,128)(2,1)} %fusion.130, bf16[768,3072]{1,0:T(8,128)(2,1)} %all-gather.12.cloned.1.call-done), kind=kOutput, calls=%fused_computation.145 | convolution fusion | flops 9673110528 | bytes 29906944 | tf_op jit(solution)/shard_map/rk,dk->rd/dot_general | solution.py:113
  556.1 16.5 broadcast.192.clone
  572.6 131.0 %while.51 = (s32[]{:T(128)}, f32[12,1024,1024]{1,2,0:T(8,128)}, bf16[12,1024,64]{1,2,0:T(8,128)(2,1)S(1)}, f32[1,1024]{1,0:T(1,128)S(1)}, bf16[12,1024,1024]{1,2...) while((s32[]{:T(128)}, f32[12,1024,1024]{1,2,0:T(8,128)}, ...), condition=%wide.region_16.17_spmd, body=%wide.region_14.16_spmd.sunk | while | flops 286261248 | bytes 19975276 | solution.py:130
  703.8 16.4 broadcast.192.clone.1
  720.2 130.8 %while.50 = (s32[]{:T(128)}, f32[12,1024,1024]{1,2,0:T(8,128)}, bf16[12,1024,64]{1,2,0:T(8,128)(2,1)S(1)}, f32[1,1024]{1,0:T(1,128)S(1)}, bf16[12,1024,1024]{1,2...) while((s32[]{:T(128)}, f32[12,1024,1024]{1,2,0:T(8,128)}, ...), condition=%wide.region_13.14_spmd, body=%wide.region_11.13_spmd.sunk | while | flops 286261248 | bytes 19975276 | solution.py:130
  859.3 20.6 %fusion.156 = f32[3072,768]{1,0:T(8,128)} fusion(bf16[2048,768]{1,0:T(8,128)(2,1)S(1)} %copy-done.7, f32[2048,3072]{1,0:T(8,128)} %fusion.155), kind=kOutput, calls=%fused_computation.177 | convolution fusion | flops 9720299520 | bytes 37748736 | tf_op jit(solution)/shard_map/rk,rd->kd/dot_general | solution.py:106
  880.6 17.6 %fusion.154 = f32[768,3072]{1,0:T(8,128)} fusion(bf16[2048,3072]{1,0:T(8,128)(2,1)} %fusion.130, f32[2048,768]{1,0:T(8,128)} %get-tuple-element.290, f32[768]{0:T(1024)S(1)} %copy-done.30, f32[2048]{0:T(1024)S(1)} %copy-done.28), kind=kOutput, calls=%fused_computation.175 | convolution fusion | flops 9668395008 | bytes 28322816 | tf_op jit(solution)/shard_map/rd,rk->dk/dot_general | solution.py:112
  898.3 48.7 %add.114 = f32[12,1024,1024]{1,2,0:T(8,128)} add(f32[12,1024,1024]{1,2,0:T(8,128)} %get-tuple-element.167, f32[12,1024,1024]{1,2,0:T(8,128)} %get-tuple-element.168) | non-fusion elementwise | flops 12582912 | bytes 150994944 | tf_op jit(solution)/shard_map/add | solution.py:134
  947.0 49.7 %copy.39 = f32[12,1024,1024]{2,1,0:T(8,128)} copy(f32[12,1024,1024]{1,2,0:T(8,128)} %add.114) | data formatting | bytes 100663296 | tf_op jit(solution)/shard_map/add | solution.py:134
  998.8 9.1 fusion.137
  1007.8 41.9 %all-reduce.4 = (f32[768]{0:T(1024)S(1)}, f32[768]{0:T(1024)S(1)}) all-reduce(f32[768]{0:T(1024)S(1)} %get-tuple-element.215, f32[768]{0:T(1024)S(1)} %copy-done.31), channel_id=7, replica_groups=mesh['wide'=16,'narrow'=2] {'wide','narrow'}, use_global_device_ids=true, to_apply=%region_24.25.clone | all-reduce | flops 1536 | bytes 12288
  1050.9 7.4 fusion.132
  1058.3 23.8 %add_multiply_fusion = f32[2048,768]{1,0:T(8,128)} fusion(f32[2048,768]{1,0:T(8,128)} %get-tuple-element.290, bf16[3072,768]{1,0:T(8,128)(2,1)} %all-gather.14.cloned.1.call-done, f32[2048]{0:T(1024)S(1)} %bitcast.344, f32[2048,3072]{1,0:T(8,128)} %fusion.155), kind=kOutput, calls=%fused_computation.147 | convolution fusion | flops 9723445248 | bytes 42475520 | tf_op jit(solution)/shard_map/dot_general | solution.py:91
  1082.1 17.3 %reduce-scatter.14.cloned.1.call-done = f32[96,768]{1,0:T(8,128)} async-done(((f32[3072,768]{1,0:T(8,128)}), f32[96,768]{1,0:T(8,128)}) %reduce-scatter.14.cloned.1.call-update) | async-done | bytes 294928 | tf_op jit(solution)/shard_map/reduce_scatter | solution.py:150
  1099.4 142.2 %reduce-scatter.12.cloned.1.call-done = f32[24,3072]{1,0:T(8,128)} async-done(((f32[768,3072]{1,0:T(8,128)}), f32[24,3072]{1,0:T(8,128)}) %reduce-scatter.12.cloned.1.call-update) | async-done | bytes 294928 | tf_op jit(solution)/shard_map/reduce_scatter | solution.py:149
  1241.5 437.5 %reduce-scatter.6.cloned.1.call-done = f32[384,1024]{1,0:T(8,128)} async-done(((f32[12288,1024]{1,0:T(8,128)}), f32[384,1024]{1,0:T(8,128)}) %reduce-scatter.6.cloned.1.call-update) | async-done | bytes 1572880 | tf_op jit(solution)/shard_map/reduce_scatter | solution.py:146
  (394 shorter events, 535.3 us)
Async XLA Ops:
  7.2 49.9 %copy-start.32 = (s32[2]{0:T(128)S(1)}, s32[2]{0:T(128)}, u32[]{:S(2)}) copy-start(s32[2]{0:T(128)} %param.19) | copy-start | bytes 28
  7.2 60.6 %all-gather.8.cloned.1.call-start = ((), (), s32[]{:S(2)}) async-start(), calls=%async_computation.6 | async-start | bytes 1216512 | tf_op jit(solution)/shard_map/all_gather | solution.py:66
  7.9 216.3 %all-gather.6.cloned.1.call-start = ((), (), s32[]{:S(2)}) async-start(), calls=%async_computation.5 | async-start | bytes 25952256 | tf_op jit(solution)/shard_map/all_gather | solution.py:65
  8.7 452.8 %all-gather.10.cloned.1.call-start = ((), (), s32[]{:S(2)}) async-start(), calls=%async_computation.7 | async-start | bytes 1216512 | tf_op jit(solution)/shard_map/all_gather | solution.py:67
  9.4 459.9 %all-gather.12.cloned.1.call-start = ((), (), s32[]{:S(2)}) async-start(), calls=%async_computation.8 | async-start | bytes 4866048 | tf_op jit(solution)/shard_map/all_gather | solution.py:68
  10.0 477.5 %all-gather.14.cloned.1.call-start = ((), (), s32[]{:S(2)}) async-start(), calls=%async_computation.9 | async-start | bytes 4866048 | tf_op jit(solution)/shard_map/all_gather | solution.py:69
  10.6 1071.5 %reduce-scatter.10.cloned.1.call-start = ((), (), s32[]{:S(2)}) async-start(), calls=%async_computation.12 | async-start | bytes 2433024 | tf_op jit(solution)/shard_map/reduce_scatter | solution.py:148
  54.3 478.0 %copy-start.29 = (f32[768]{0:T(1024)}, f32[768]{0:T(1024)S(1)}, u32[]{:S(2)}) copy-start(f32[768]{0:T(1024)S(1)} %convert_element_type.135) | copy-start | bytes 9220
  428.8 32.7 %copy-start.12 = (f32[1,1024]{1,0:T(1,128)}, f32[1,1024]{1,0:T(1,128)S(1)}, u32[]{:S(2)}) copy-start(f32[1,1024]{1,0:T(1,128)S(1)} %get-tuple-element.595) | copy-start | bytes 12292
  428.8 32.7 %copy-start.16 = (f32[12,1024,1]{1,2,0:T(1,128)}, f32[12,1024,1]{1,2,0:T(1,128)S(1)}, u32[]{:S(2)}) copy-start(f32[12,1024,1]{1,2,0:T(1,128)S(1)} %get-tuple-element.547) | copy-start | bytes 147460
  469.3 63.0 %copy-start.27 = (f32[2048]{0:T(1024)}, f32[2048]{0:T(1024)S(1)}, u32[]{:S(2)}) copy-start(f32[2048]{0:T(1024)S(1)} %fusion.148) | copy-start | bytes 24580
  469.3 18.2 %copy-start.6 = (bf16[2048,768]{1,0:T(8,128)(2,1)S(1)}, bf16[2048,768]{1,0:T(8,128)(2,1)}, u32[]{:S(2)}) copy-start(bf16[2048,768]{1,0:T(8,128)(2,1)} %fusion.133) | copy-start | bytes 9437188
  487.5 27.5 %copy-start.5 = (f32[2048,768]{1,0:T(8,128)S(1)}, f32[2048,768]{1,0:T(8,128)}, u32[]{:S(2)}) copy-start(f32[2048,768]{1,0:T(8,128)} %get-tuple-element.290) | copy-start | bytes 18874372
  515.0 17.3 %copy-start.4 = (bf16[2,1024,768]{2,1,0:T(8,128)(2,1)S(1)}, bf16[2,1024,768]{2,1,0:T(8,128)(2,1)}, u32[]{:S(2)}) copy-start(bf16[2,1024,768]{2,1,0:T(8,128)(2,1)} %param.27) | copy-start | bytes 9437188
  515.0 17.3 %copy-start.19 = (f32[1,8,2,128]{3,1,2,0:T(8,128)S(1)}, f32[1,8,2,128]{3,1,2,0:T(8,128)}, u32[]{:S(2)}) copy-start(f32[1,8,2,128]{3,1,2,0:T(8,128)} %copy-done.18) | copy-start | bytes 24580
  543.9 538.1 %reduce-scatter.8.cloned.1.call-start = ((), (), s32[]{:S(2)}) async-start(), calls=%async_computation.11 | async-start | bytes 2433024 | tf_op jit(solution)/shard_map/reduce_scatter | solution.py:147
  556.1 16.5 copy-start.15
  703.6 16.6 copy-start.11
  703.8 16.4 copy-start.13
  859.2 240.1 %reduce-scatter.14.cloned.1.call-start = ((), (), s32[]{:S(2)}) async-start(), calls=%async_computation.14 | async-start | bytes 9732096 | tf_op jit(solution)/shard_map/reduce_scatter | solution.py:150
  880.0 361.6 %reduce-scatter.12.cloned.1.call-start = ((), (), s32[]{:S(2)}) async-start(), calls=%async_computation.13 | async-start | bytes 9732096 | tf_op jit(solution)/shard_map/reduce_scatter | solution.py:149
  898.3 780.8 %reduce-scatter.6.cloned.1.call-start = ((), (), s32[]{:S(2)}) async-start(), calls=%async_computation.10 | async-start | bytes 51904512 | tf_op jit(solution)/shard_map/reduce_scatter | solution.py:146
  998.8 9.1 copy-start.31
  998.8 52.2 %copy-start.24 = (f32[1,8,2,128]{3,2,1,0:T(2,128)S(1)}, f32[1,8,2,128]{3,2,1,0:T(2,128)}, u32[]{:S(2)}) copy-start(f32[1,8,2,128]{3,2,1,0:T(2,128)} %copy-done.23) | copy-start | bytes 24580
  (20 other events, 68.3 us)
Sparse Core Ops, SparseCore 0:
  10.9 56.8 all-gather.7
  70.6 153.5 all-gather.5
  227.1 52.2 all-gather.9
  282.2 62.5 all-gather.11
  347.5 62.4 all-gather.13
  544.1 97.3 reduce-scatter.9
  859.4 97.2 reduce-scatter.7
  963.1 136.2 reduce-scatter.13
  1106.8 134.6 reduce-scatter.11
  1248.4 430.6 reduce-scatter.5
where the time goes:
time: 1700 us; the launch traced here: 1690 us
  waiting for transfers between devices  747 us (44%)
  matrix products  397 us (23%)
  other arithmetic  280 us (16%)
  local copies, waits for them, and re-layouts  162 us (10%)
  blocking collectives  83.9 us (5%)
    reduce_scatter x1, waiting for transfers between devices, shards(): lax.psum_scatter(rand_flat, ('wide', 'narrow'), scatter_dimension=0, tile...  438 us
    reduce_scatter x1, waiting for transfers between devices, shards(): lax.psum_scatter(grad_up, ('wide', 'narrow'), scatter_dimension=0, tiled=...  142 us
    all_gather x1, waiting for transfers between devices, shards(): lax.all_gather(rand_mix, ('wide', 'narrow'), axis=0, tiled=True)  141 us
    dynamic_update_slice x24, other arithmetic, shards(): lax.map(partial(head_backward, valid_table[item_index]), (rand_heads_back...  99.8 us
    dot_general x24, matrix products, head_forward(): jnp.dot(attention.astype(jnp.bfloat16), value_head, preferred_element_typ...  88.4 us
    unnamed x2, blocking collectives  83.9 us
    dot_general x24, matrix products, head_backward(): jnp.einsum('id,jd->ij', mix_grad, value_head, preferred_element_type=jnp....  75.2 us
    dot_general x24, matrix products, head_backward(): jnp.einsum('ij,id->jd', attention.astype(jnp.bfloat16), mix_grad, preferr...  69.7 us
  transfers between devices with their start and end apart: 10, of which 5 were waited for; matrix products, arithmetic and copies ran while one was open for 46% of the time, Pallas kernels for 0%

commit v1 on v0

--- a/solution.py
+++ b/solution.py
@@ -3,14 +3,779 @@
 import jax
 import jax.numpy as jnp
 from jax import lax
+from jax.experimental import pallas as pl
+from jax.experimental.pallas import tpu as pltpu
 from jax.sharding import PartitionSpec as P
 
 HEADS = 12
 HEAD = 64
 LMAX = 1024
-
-
+WIDTH = 768
+FF = 3072
 EPSILON = 1e-05
+
+BOTH = ("wide", "narrow")
+BF16 = jnp.bfloat16
+F32 = jnp.float32
+MIB = 1 << 20
+
+PARTS = 2
+SUBS = 6 // PARTS
+RUNS = 8 // PARTS
+HALF = 64
+HROWS = RUNS * HALF
+PLANES = 4
+PHEADS = HEADS // PLANES
+COL_A, COL_B, COL_C = 384, 384, 256
+FSTEP = 384
+
+
+def dot(a, b, ca, cb):
+    return lax.dot_general(a, b, (((ca,), (cb,)), ((), ())), preferred_element_type=F32)
+
+
+CORE, PLANE, PLACE, LENGTHS = 0, 1, 2, 3
+
+
+def spec(shape, index):
+    return pl.BlockSpec(shape, index)
+
+
+def held(shape):
+    zeros = (0,) * len(shape)
+    return pl.BlockSpec(shape, lambda *_: zeros, pipeline_mode=pl.Buffered(1))
+
+
+def params(limit):
+    return pltpu.CompilerParams(vmem_limit_bytes=limit * MIB)
+
+
+def values_kernel(sc, tok, gain, weight, out):
+    step = pl.program_id(0)
+    rows = tok.shape[1]
+    position = step * rows + lax.broadcasted_iota(jnp.int32, (rows, 1), 0)
+    for item in range(2):
+        x = tok[item].astype(F32)
+        scale = lax.rsqrt(jnp.mean(x * x, axis=-1, keepdims=True) + EPSILON)
+        normed = (x * scale * gain[...]).astype(BF16)
+        found = dot(normed, weight[...], 1, 0)
+        found = jnp.where(position < sc[LENGTHS + item], found, 0.0).astype(BF16)
+        for head in range(HEADS):
+            out[head, :, item * HEAD : (item + 1) * HEAD] = found[:, head * HEAD : (head + 1) * HEAD]
+
+
+def run_values(sc, tokens, gain, weight):
+    rows = 256
+    return pl.pallas_call(
+        values_kernel,
+        grid_spec=pltpu.PrefetchScalarGridSpec(
+            num_scalar_prefetch=1,
+            grid=(LMAX // rows,),
+            in_specs=[
+                spec((2, rows, WIDTH), lambda j, s: (0, j, 0)),
+                held((1, WIDTH)),
+                held((WIDTH, WIDTH)),
+            ],
+            out_specs=spec((HEADS, rows, 2 * HEAD), lambda j, s: (0, j, 0)),
+        ),
+        out_shape=jax.ShapeDtypeStruct((HEADS, LMAX, 2 * HEAD), BF16),
+        compiler_params=params(32),
+        cost_estimate=pl.CostEstimate(
+            flops=2 * 2 * LMAX * WIDTH * WIDTH, bytes_accessed=8 * LMAX * WIDTH, transcendentals=0
+        ),
+        name="values",
+    )(sc, tokens, gain, weight)
+
+
+def fill_exponents(place, rand, scratch):
+    a_near, a_far, b_near, b_far, c_all = rand
+    for rel in range(4):
+        ry, rx = rel // 2, rel % 2
+        where = place ^ rel
+        a = (a_near, a_far)[ry]
+        b = (b_near, b_far)[rx]
+        for k in range(SUBS):
+            row = where * SUBS + k
+            scratch[row, :, :COL_A] = jnp.exp(a[rx, 0, k].astype(F32)).astype(BF16)
+            scratch[row, :, COL_A : COL_A + COL_B] = jnp.exp(b[ry, 0, k].astype(F32)).astype(BF16)
+            scratch[row, :, COL_A + COL_B :] = jnp.exp(c_all[0, rel, k].astype(F32)).astype(BF16)
+
+
+def lane_lengths(sc, shape):
+    slot = lax.broadcasted_iota(jnp.int32, shape, 1) // HEAD
+    length = jnp.where(slot == 0, sc[LENGTHS], sc[LENGTHS + 1])
+    return jnp.where(slot >= 2, jnp.where(slot == 2, sc[LENGTHS + 2], sc[LENGTHS + 3]), length)
+
+
+def mix_kernel(part, sc, a_near, a_far, b_near, b_far, c_all, v_own, v_far, own, far, mean, inverse, exps, mask):
+    @pl.when(pl.program_id(0) == 0)
+    def _():
+        shape = (LMAX, 4 * HEAD)
+        column = lax.broadcasted_iota(jnp.int32, shape, 0)
+        mask[...] = (column < lane_lengths(sc, shape)).astype(F32).astype(BF16)
+
+    fill_exponents(sc[PLACE], (a_near, a_far, b_near, b_far, c_all), exps)
+    shape = (HROWS, 4 * HEAD)
+    line = lax.broadcasted_iota(jnp.int32, shape, 0)
+    position = 128 * (PARTS * (line // HALF) + part) + HALF * sc[CORE] + line % HALF
+    valid = position < lane_lengths(sc, shape)
+    for head in range(PHEADS):
+        weights = exps[head * RUNS : (head + 1) * RUNS].reshape(HROWS, LMAX)
+        total = dot(weights, mask[...], 1, 0)
+        flip = jnp.where(valid, 1.0 / total, 0.0)
+        mixed = dot(weights, jnp.concatenate([v_own[head], v_far[head]], axis=1), 1, 0) * flip
+        inverse[head] = flip
+        mean[head] = mixed
+        low = mixed.astype(BF16)
+        own[head] = low[:, : 2 * HEAD]
+        far[head] = low[:, 2 * HEAD :]
+
+
+def plane_of(k, sc):
+    return lax.rem(sc[PLANE] + PLANES - k, PLANES)
+
+
+def rand_specs():
+    return [
+        spec((2, 1, SUBS, HALF, COL_A), lambda k, s: (0, k, 0, 0, 0)),
+        spec((2, 1, SUBS, HALF, COL_A), lambda k, s: (0, k, 0, 0, 0)),
+        spec((2, 1, SUBS, HALF, COL_B), lambda k, s: (0, k, 0, 0, 0)),
+        spec((2, 1, SUBS, HALF, COL_B), lambda k, s: (0, k, 0, 0, 0)),
+        spec((1, 4, SUBS, HALF, COL_C), lambda k, s: (k, 0, 0, 0, 0)),
+    ]
+
+
+def plane_spec(rows, lanes):
+    return spec((PHEADS, rows, lanes), lambda k, s: (plane_of(k, s), 0, 0))
+
+
+def run_mix(part, sc, rand, v_own, v_far):
+    return pl.pallas_call(
+        partial(mix_kernel, part),
+        grid_spec=pltpu.PrefetchScalarGridSpec(
+            num_scalar_prefetch=1,
+            grid=(PLANES,),
+            in_specs=rand_specs() + [plane_spec(LMAX, 2 * HEAD)] * 2,
+            out_specs=[
+                plane_spec(HROWS, 2 * HEAD),
+                plane_spec(HROWS, 2 * HEAD),
+                plane_spec(HROWS, 4 * HEAD),
+                plane_spec(HROWS, 4 * HEAD),
+            ],
+            scratch_shapes=[
+                pltpu.VMEM((4 * SUBS, HALF, LMAX), BF16),
+                pltpu.VMEM((LMAX, 4 * HEAD), BF16),
+            ],
+        ),
+        out_shape=[
+            jax.ShapeDtypeStruct((HEADS, HROWS, 2 * HEAD), BF16),
+            jax.ShapeDtypeStruct((HEADS, HROWS, 2 * HEAD), BF16),
+            jax.ShapeDtypeStruct((HEADS, HROWS, 4 * HEAD), F32),
+            jax.ShapeDtypeStruct((HEADS, HROWS, 4 * HEAD), F32),
+        ],
+        compiler_params=params(40),
+        cost_estimate=pl.CostEstimate(
+            flops=4 * HEADS * HROWS * LMAX * 4 * HEAD,
+            bytes_accessed=HEADS * (2 * HROWS * LMAX + 10 * HROWS * 256),
+            transcendentals=HEADS * HROWS * LMAX,
+        ),
+        name="mix",
+    )(sc, *rand, v_own, v_far)
+
+
+def feed_kernel(part, carried, *refs):
+    (sc, tok, cot, near, far, w_out, gain, up_w, down_w, *rest) = refs
+    if carried:
+        (down_in, up_in, out_in, gain_in, _, _, *rest) = rest
+    last = part == PARTS - 1
+    (output, res_grad, g_own, g_far, d_down, d_up, d_out, d_gain, mixed, resid, normed, branch_grad, back) = rest
+    step = pl.program_id(0)
+    core = sc[CORE]
+    tile = RUNS * 128
+    shape = (tile, 1)
+    line = lax.broadcasted_iota(jnp.int32, shape, 0)
+    position = 128 * (PARTS * (line // 128) + part) + line % 128
+
+    @pl.when(step == 0)
+    def _():
+        for item in range(2):
+            for source, slot in ((near, core), (far, 1 - core)):
+                for pair in range(HEADS // 2):
+                    for run in range(RUNS):
+                        rows = slice(run * HALF, (run + 1) * HALF)
+                        lanes = slice(item * HEAD, (item + 1) * HEAD)
+                        both = jnp.concatenate(
+                            [source[2 * pair, rows, lanes], source[2 * pair + 1, rows, lanes]], axis=1
+                        )
+                        mixed[item, run, slot, :, pair * 128 : (pair + 1) * 128] = both
+        for item in range(2):
+            rows = pl.ds(item * tile, tile)
+            x = tok[item, :, 0].reshape(tile, WIDTH).astype(F32)
+            res = x + dot(mixed[item].reshape(tile, WIDTH), w_out[...], 1, 0)
+            resid[rows] = res
+            scale = lax.rsqrt(jnp.mean(res * res, axis=-1, keepdims=True) + EPSILON)
+            normed[rows] = (res * scale * gain[...]).astype(BF16)
+            valid = position < sc[LENGTHS + item]
+            grad = cot[item, :, 0].reshape(tile, WIDTH).astype(F32)
+            branch_grad[rows] = jnp.where(valid, grad, 0.0).astype(BF16)
+
+    up_block = up_w[0]
+    down_block = down_w[...]
+    for piece in range(2):
+        rows = pl.ds(piece * tile, tile)
+        two = normed[rows]
+        grad = branch_grad[rows]
+        up = dot(two, up_block, 1, 0)
+        square = up * up
+        inner = 0.7978845608028654 * (up * (1.0 + 0.044715 * square))
+        bend = jnp.tanh(inner)
+        share = 0.5 * (1.0 + bend)
+        active = (up * share).astype(BF16)
+        slope = share + 0.5 * up * (1.0 - bend * bend) * (0.7978845608028654 * (1.0 + 3 * 0.044715 * square))
+        branch = dot(active, down_block, 1, 0)
+        up_grad = (dot(grad, down_block, 1, 1) * slope).astype(BF16)
+        two_grad = dot(up_grad, up_block, 1, 1)
+        add_down = dot(active, grad, 0, 0)
+        add_up = dot(two, up_grad, 0, 0)
+        view = output.at[piece, :, 0]
+        if piece == 0:
+            total_down, total_up = add_down, add_up
+        else:
+            total_down, total_up = total_down + add_down, total_up + add_up
+
+        @pl.when(step == 0)
+        def _():
+            view[...] = branch.reshape(RUNS, 2, HALF, WIDTH)
+            back[rows] = two_grad
+
+        @pl.when(step > 0)
+        def _():
+            view[...] += branch.reshape(RUNS, 2, HALF, WIDTH)
+            back[rows] += two_grad
+
+    if carried:
+        total_down = total_down + down_in[...]
+        total_up = total_up + up_in[0]
+    if last:
+        low = total_down.astype(BF16)
+        d_down[0] = low[:, : WIDTH // 2]
+        d_down[1] = low[:, WIDTH // 2 :]
+        d_up[0] = total_up.astype(BF16)
+    else:
+        d_down[...] = total_down
+        d_up[0] = total_up
+
+    @pl.when(step == pl.num_programs(0) - 1)
+    def _():
+        for item in range(2):
+            rows = pl.ds(item * tile, tile)
+            valid = position < sc[LENGTHS + item]
+            res = resid[rows]
+            branch = output[item, :, 0].reshape(tile, WIDTH)
+            output[item, :, 0] = jnp.where(valid, res + branch, 0.0).reshape(RUNS, 2, HALF, WIDTH)
+            scale = lax.rsqrt(jnp.mean(res * res, axis=-1, keepdims=True) + EPSILON)
+            unit = res * scale
+            two_grad = back[rows]
+            gained = two_grad * gain[...]
+            grad = branch_grad[rows].astype(F32) + scale * (
+                gained - unit * jnp.mean(gained * unit, axis=-1, keepdims=True)
+            )
+            res_grad[item, :, 0] = grad.reshape(RUNS, 2, HALF, WIDTH)
+            low = grad.astype(BF16)
+            gain_sum = jnp.sum(two_grad * unit, axis=0, keepdims=True)
+            out_sum = dot(mixed[item].reshape(tile, WIDTH), low, 0, 0)
+            if item == 0:
+                gain_total, out_total = gain_sum, out_sum
+            else:
+                gain_total, out_total = gain_total + gain_sum, out_total + out_sum
+            spread = dot(low, w_out[...], 1, 1).astype(BF16)
+            mixed[item] = spread.reshape(RUNS, 2, HALF, WIDTH)
+        if carried:
+            gain_total = gain_total + gain_in[...]
+            out_total = out_total + out_in[...]
+        d_gain[...] = gain_total
+        if last:
+            low = out_total.astype(BF16)
+            d_out[0] = low[:, : WIDTH // 2]
+            d_out[1] = low[:, WIDTH // 2 :]
+        else:
+            d_out[...] = out_total
+        for target, slot in ((g_own, core), (g_far, 1 - core)):
+            for pair in range(HEADS // 2):
+                for run in range(RUNS):
+                    rows = slice(run * HALF, (run + 1) * HALF)
+                    lanes = slice(pair * 128, (pair + 1) * 128)
+                    one, two = mixed[0, run, slot, :, lanes], mixed[1, run, slot, :, lanes]
+                    target[2 * pair, rows, :] = jnp.concatenate([one[:, :HEAD], two[:, :HEAD]], axis=1)
+                    target[2 * pair + 1, rows, :] = jnp.concatenate([one[:, HEAD:], two[:, HEAD:]], axis=1)
+
+
+def run_feed(part, sc, tokens, cotangent, near, far, w_out, gain, up_blocks, w_down, carry):
+    last = part == PARTS - 1
+    rows = 2 * RUNS * 128
+    slab = (2, RUNS, PARTS, 2, HALF, WIDTH)
+    block = (2, RUNS, 1, 2, HALF, WIDTH)
+    here = lambda f, s: (0, 0, part, 0, 0, 0)
+    fixed = lambda shape: pl.BlockSpec(shape, here, pipeline_mode=pl.Buffered(1))
+    in_specs = [
+        fixed(block),
+        fixed(block),
+        held((HEADS, HROWS, 2 * HEAD)),
+        held((HEADS, HROWS, 2 * HEAD)),
+        held((WIDTH, WIDTH)),
+        held((1, WIDTH)),
+        spec((1, WIDTH, FSTEP), lambda f, s: (f, 0, 0)),
+        spec((FSTEP, WIDTH), lambda f, s: (f, 0)),
+    ]
+    args = [tokens.reshape(slab), cotangent.reshape(slab), near, far, w_out, gain, up_blocks, w_down]
+    aliases = {}
+    if carry is not None:
+        in_specs += [
+            spec((FSTEP, WIDTH), lambda f, s: (f, 0)),
+            spec((1, WIDTH, FSTEP), lambda f, s: (f, 0, 0)),
+            held((WIDTH, WIDTH)),
+            held((1, WIDTH)),
+            pl.BlockSpec(memory_space=pl.ANY),
+            pl.BlockSpec(memory_space=pl.ANY),
+        ]
+        output, res_grad, d_down, d_up, d_out, d_gain = carry
+        args += [d_down, d_up, d_out, d_gain, output, res_grad]
+        aliases = {len(args) - 1: 0, len(args): 1}
+    if last:
+        grad_specs = [
+            spec((2, FSTEP, WIDTH // 2), lambda f, s: (0, f, 0)),
+            spec((1, WIDTH, FSTEP), lambda f, s: (f, 0, 0)),
+            held((2, WIDTH, WIDTH // 2)),
+            held((1, WIDTH)),
+        ]
+        grad_shapes = [
+            jax.ShapeDtypeStruct((2, FF, WIDTH // 2), BF16),
+            jax.ShapeDtypeStruct((FF // FSTEP, WIDTH, FSTEP), BF16),
+            jax.ShapeDtypeStruct((2, WIDTH, WIDTH // 2), BF16),
+            jax.ShapeDtypeStruct((1, WIDTH), F32),
+        ]
+    else:
+        grad_specs = [
+            spec((FSTEP, WIDTH), lambda f, s: (f, 0)),
+            spec((1, WIDTH, FSTEP), lambda f, s: (f, 0, 0)),
+            held((WIDTH, WIDTH)),
+            held((1, WIDTH)),
+        ]
+        grad_shapes = [
+            jax.ShapeDtypeStruct((FF, WIDTH), F32),
+            jax.ShapeDtypeStruct((FF // FSTEP, WIDTH, FSTEP), F32),
+            jax.ShapeDtypeStruct((WIDTH, WIDTH), F32),
+            jax.ShapeDtypeStruct((1, WIDTH), F32),
+        ]
+    return pl.pallas_call(
+        partial(feed_kernel, part, carry is not None),
+        grid_spec=pltpu.PrefetchScalarGridSpec(
+            num_scalar_prefetch=1,
+            grid=(FF // FSTEP,),
+            in_specs=in_specs,
+            out_specs=[
+                fixed(block),
+                fixed(block),
+                held((HEADS, HROWS, 2 * HEAD)),
+                held((HEADS, HROWS, 2 * HEAD)),
+                *grad_specs,
+            ],
+            scratch_shapes=[
+                pltpu.VMEM((2, RUNS, 2, HALF, WIDTH), BF16),
+                pltpu.VMEM((rows, WIDTH), F32),
+                pltpu.VMEM((rows, WIDTH), BF16),
+                pltpu.VMEM((rows, WIDTH), BF16),
+                pltpu.VMEM((rows, WIDTH), F32),
+            ],
+        ),
+        out_shape=[
+            jax.ShapeDtypeStruct(slab, F32),
+            jax.ShapeDtypeStruct(slab, F32),
+            jax.ShapeDtypeStruct((HEADS, HROWS, 2 * HEAD), BF16),
+            jax.ShapeDtypeStruct((HEADS, HROWS, 2 * HEAD), BF16),
+            *grad_shapes,
+        ],
+        input_output_aliases=aliases,
+        compiler_params=params(60),
+        cost_estimate=pl.CostEstimate(
+            flops=2 * rows * (6 * WIDTH * FF + 3 * WIDTH * WIDTH),
+            bytes_accessed=16 * rows * WIDTH + 8 * WIDTH * FF,
+            transcendentals=rows * FF,
+        ),
+        name="feed",
+    )(sc, *args)
+
+
+def unmix_kernel(part, carried, *refs):
+    (sc, a_near, a_far, b_near, b_far, c_all, v_own, v_far, g_own, g_far, mean, inverse, *rest) = refs
+    if carried:
+        (own_in, far_in, *rest) = rest
+    (ga_keep, ga_send, gb_keep, gb_send, gc_all, own, far, exps, grads) = rest
+    place = sc[PLACE]
+    fill_exponents(place, (a_near, a_far, b_near, b_far, c_all), exps)
+    column = lax.broadcasted_iota(jnp.int32, (1, LMAX), 1)
+    line = lax.broadcasted_iota(jnp.int32, (LMAX, 2 * HEAD), 0)
+    slot = lax.broadcasted_iota(jnp.int32, (LMAX, 2 * HEAD), 1) // HEAD
+    for head in range(PHEADS):
+        weights = exps[head * RUNS : (head + 1) * RUNS].reshape(HROWS, LMAX)
+        scaled = jnp.concatenate([g_own[head], g_far[head]], axis=1).astype(F32) * inverse[head]
+        low = scaled.astype(BF16)
+        product = low.astype(F32) * mean[head]
+        score = dot(low, jnp.concatenate([v_own[head], v_far[head]], axis=1), 1, 1)
+        for item in range(4):
+            delta = jnp.sum(product[:, item * HEAD : (item + 1) * HEAD], axis=-1, keepdims=True)
+            score = score - delta * (column < sc[LENGTHS + item]).astype(F32)
+        score = score * weights.astype(F32)
+        grads[head * RUNS : (head + 1) * RUNS] = score.astype(BF16).reshape(RUNS, HALF, LMAX)
+        back = dot(weights, low, 0, 0)
+        for target, extra, first in ((own, own_in if carried else None, 0), (far, far_in if carried else None, 2)):
+            found = back[:, first * HEAD : (first + 2) * HEAD]
+            length = jnp.where(slot == 0, sc[LENGTHS + first], sc[LENGTHS + first + 1])
+            found = jnp.where(line < length, found, 0.0)
+            if carried:
+                found = found + extra[head]
+            target[head] = found.astype(target.dtype)
+    for rel in range(4):
+        ry, rx = rel // 2, rel % 2
+        a = (ga_keep, ga_send)[ry]
+        b = (gb_keep, gb_send)[rx]
+        for k in range(SUBS):
+            row = (place ^ rel) * SUBS + k
+            a[rx, 0, k] = grads[row, :, :COL_A]
+            b[ry, 0, k] = grads[row, :, COL_A : COL_A + COL_B]
+            gc_all[0, rel, k] = grads[row, :, COL_A + COL_B :]
+
+
+def run_unmix(part, sc, rand, v_own, v_far, g_own, g_far, mean, inverse, carry):
+    last = part == PARTS - 1
+    in_specs = rand_specs() + [
+        plane_spec(LMAX, 2 * HEAD),
+        plane_spec(LMAX, 2 * HEAD),
+        plane_spec(HROWS, 2 * HEAD),
+        plane_spec(HROWS, 2 * HEAD),
+        plane_spec(HROWS, 4 * HEAD),
+        plane_spec(HROWS, 4 * HEAD),
+    ]
+    args = [*rand, v_own, v_far, g_own, g_far, mean, inverse]
+    if carry is not None:
+        in_specs += [plane_spec(LMAX, 2 * HEAD)] * 2
+        args += list(carry)
+    return pl.pallas_call(
+        partial(unmix_kernel, part, carry is not None),
+        grid_spec=pltpu.PrefetchScalarGridSpec(
+            num_scalar_prefetch=1,
+            grid=(PLANES,),
+            in_specs=in_specs,
+            out_specs=rand_specs() + [plane_spec(LMAX, 2 * HEAD)] * 2,
+            scratch_shapes=[
+                pltpu.VMEM((4 * SUBS, HALF, LMAX), BF16),
+                pltpu.VMEM((4 * SUBS, HALF, LMAX), BF16),
+            ],
+        ),
+        out_shape=[jax.ShapeDtypeStruct((2, PLANES, SUBS, HALF, COL_A), BF16)] * 2
+        + [jax.ShapeDtypeStruct((2, PLANES, SUBS, HALF, COL_B), BF16)] * 2
+        + [jax.ShapeDtypeStruct((PLANES, 4, SUBS, HALF, COL_C), BF16)]
+        + [
+            jax.ShapeDtypeStruct((HEADS, LMAX, 2 * HEAD), F32),
+            jax.ShapeDtypeStruct((HEADS, LMAX, 2 * HEAD), BF16 if last else F32),
+        ],
+        compiler_params=params(56),
+        cost_estimate=pl.CostEstimate(
+            flops=4 * HEADS * HROWS * LMAX * 4 * HEAD,
+            bytes_accessed=HEADS * (4 * HROWS * LMAX + 10 * HROWS * 256 + 8 * LMAX * 256),
+            transcendentals=HEADS * HROWS * LMAX,
+        ),
+        name="unmix",
+    )(sc, *args)
+
+
+def close_kernel(sc, tok, res_grad, own, far, gain, weight, tok_grad, d_value, d_gain, total):
+    step = pl.program_id(0)
+    rows = tok.shape[1]
+    for item in range(2):
+        lanes = slice(item * HEAD, (item + 1) * HEAD)
+        pieces = [
+            (own[head, :, lanes] + far[head, :, lanes].astype(F32)).astype(BF16) for head in range(HEADS)
+        ]
+        back = jnp.concatenate(pieces, axis=1)
+        x = tok[item].astype(F32)
+        scale = lax.rsqrt(jnp.mean(x * x, axis=-1, keepdims=True) + EPSILON)
+        unit = x * scale
+        normed = (unit * gain[...]).astype(BF16)
+        normed_grad = dot(back, weight[...], 1, 1)
+        gained = normed_grad * gain[...]
+        tok_grad[item] = res_grad[item] + scale * (gained - unit * jnp.mean(gained * unit, axis=-1, keepdims=True))
+        gain_sum = jnp.sum(normed_grad * unit, axis=0, keepdims=True)
+        value_sum = dot(normed, back, 0, 0)
+        if item == 0:
+            gain_total, value_total = gain_sum, value_sum
+        else:
+            gain_total, value_total = gain_total + gain_sum, value_total + value_sum
+
+    @pl.when(step == 0)
+    def _():
+        d_gain[...] = gain_total
+        total[...] = value_total
+
+    @pl.when(step > 0)
+    def _():
+        d_gain[...] += gain_total
+        total[...] += value_total
+
+    @pl.when(step == pl.num_programs(0) - 1)
+    def _():
+        low = total[...].astype(BF16)
+        d_value[0] = low[:, : WIDTH // 2]
+        d_value[1] = low[:, WIDTH // 2 :]
+
+
+def run_close(sc, tokens, res_grad, own, far, gain, weight):
+    rows = 256
+    return pl.pallas_call(
+        close_kernel,
+        grid_spec=pltpu.PrefetchScalarGridSpec(
+            num_scalar_prefetch=1,
+            grid=(LMAX // rows,),
+            in_specs=[
+                spec((2, rows, WIDTH), lambda j, s: (0, j, 0)),
+                spec((2, rows, WIDTH), lambda j, s: (0, j, 0)),
+                spec((HEADS, rows, 2 * HEAD), lambda j, s: (0, j, 0)),
+                spec((HEADS, rows, 2 * HEAD), lambda j, s: (0, j, 0)),
+                held((1, WIDTH)),
+                held((WIDTH, WIDTH)),
+            ],
+            out_specs=[
+                spec((2, rows, WIDTH), lambda j, s: (0, j, 0)),
+                held((2, WIDTH, WIDTH // 2)),
+                held((1, WIDTH)),
+            ],
+            scratch_shapes=[pltpu.VMEM((WIDTH, WIDTH), F32)],
+        ),
+        out_shape=[
+            jax.ShapeDtypeStruct((2, LMAX, WIDTH), F32),
+            jax.ShapeDtypeStruct((2, WIDTH, WIDTH // 2), BF16),
+            jax.ShapeDtypeStruct((1, WIDTH), F32),
+        ],
+        compiler_params=params(40),
+        cost_estimate=pl.CostEstimate(
+            flops=4 * 2 * LMAX * WIDTH * WIDTH, bytes_accessed=26 * LMAX * WIDTH, transcendentals=0
+        ),
+        name="close",
+    )(sc, tokens, res_grad, own, far, gain, weight)
+
+
+DEVICES = 32
+TO_CORE, TO_X, TO_Y = 1, 2, 4
+
+
+def swap(x, bit):
+    return lax.ppermute(x, BOTH, [(d, d ^ bit) for d in range(DEVICES)])
+
+
+def ring(x):
+    return lax.ppermute(x, BOTH, [(d, (d + 8) % DEVICES) for d in range(DEVICES)])
+
+
+def pick(x, index, axis=0):
+    return lax.dynamic_index_in_dim(x, index, axis, keepdims=False)
+
+
+def ordered(flag, one, two, axis=0, joined=jnp.stack):
+    return jnp.where(flag == 0, joined([one, two], axis), joined([two, one], axis))
+
+
+def ring_pieces(x):
+    pieces = [x]
+    for _ in range(PLANES - 1):
+        pieces.append(ring(pieces[-1]))
+    return pieces
+
+
+def gather_rand(shard):
+    both = jnp.stack([shard[..., :COL_A], shard[..., COL_A : COL_A + COL_B]])
+    c_own = shard[..., COL_A + COL_B :]
+    c_line = jnp.stack([c_own, swap(c_own, TO_X)])
+    c_plane = jnp.concatenate([c_line, swap(c_line, TO_Y)])
+    pieces = ring_pieces(both)
+    c_all = jnp.stack(ring_pieces(c_plane))
+    a_own = jnp.stack([p[0] for p in pieces])
+    b_own = jnp.stack([p[1] for p in pieces])
+    a_near = jnp.stack([a_own, swap(a_own, TO_X)])
+    b_near = jnp.stack([b_own, swap(b_own, TO_Y)])
+    return a_near, swap(a_near, TO_Y), b_near, swap(b_near, TO_X), c_all
+
+
+def add_low(one, two):
+    return (one.astype(F32) + two.astype(F32)).astype(BF16)
+
+
+def ring_sum(pieces):
+    moving = pieces[1]
+    for k in (2, 3):
+        moving = add_low(ring(moving), pieces[k])
+    return ring(moving).astype(F32) + pieces[0].astype(F32)
+
+
+def scatter_rand(a_keep, a_send, b_keep, b_send, c_all):
+    a_line = add_low(a_keep, swap(a_send, TO_Y))
+    b_line = add_low(b_keep, swap(b_send, TO_X))
+    a_own = add_low(a_line[0], swap(a_line[1], TO_X))
+    b_own = add_low(b_line[0], swap(b_line[1], TO_Y))
+    c_plane = ring_sum([c_all[k] for k in range(PLANES)])
+    c_line = c_plane[:2] + swap(c_plane[2:].astype(BF16), TO_Y).astype(F32)
+    c_own = c_line[0] + swap(c_line[1].astype(BF16), TO_X).astype(F32)
+    both = ring_sum([jnp.stack([a_own[k], b_own[k]]) for k in range(PLANES)])
+    return jnp.concatenate([both[0], both[1], c_own], axis=-1)
+
+
+def gather_chips(x, place, order):
+    z, y, x_at = place
+    done = []
+    for axis in order:
+        at = sorted(done + [axis]).index(axis)
+        if axis == 0:
+            own = ring_pieces(x)
+            line = jnp.stack([own[k] for k in (3, 2, 1, 0, 3, 2, 1)], at)
+            x = lax.dynamic_slice_in_dim(line, PLANES - 1 - z, PLANES, at)
+        elif axis == 1:
+            x = ordered(y, x, swap(x, TO_Y), at)
+        else:
+            x = ordered(x_at, x, swap(x, TO_X), at)
+        done.append(axis)
+    return x.reshape((16,) + x.shape[3:])
+
+
+def scatter_chips(x, place, order, lead=0):
+    z, y, x_at = place
+    x = x.reshape(x.shape[:lead] + (4, 2, 2) + x.shape[lead + 1 :])
+    left = [0, 1, 2]
+    for axis in order:
+        at = lead + left.index(axis)
+        if axis == 0:
+            x = ring_sum([pick(x, lax.rem(z + PLANES - k, PLANES), at).astype(BF16) for k in range(PLANES)])
+        else:
+            mine, bit = (y, TO_Y) if axis == 1 else (x_at, TO_X)
+            got = swap(pick(x, 1 - mine, at).astype(BF16), bit)
+            x = pick(x, mine, at).astype(F32) + got.astype(F32)
+        left.remove(axis)
+    return x
+
+
+def chip_shards(tokens, lengths, rand_mix, w_value, w_out, w_up, w_down, gain_mix, gain_ffn, grad_out):
+    wide = lax.axis_index("wide")
+    core = lax.axis_index("narrow")
+    place = (wide // 4, (wide // 2) % 2, wide % 2)
+    half = WIDTH // 2
+
+    far_lengths = swap(lengths, TO_CORE)
+    head = jnp.stack([core, place[0], wide % 4]).astype(jnp.int32)
+    sc = jnp.concatenate([head, lengths, far_lengths])
+
+    gains = jnp.pad(jnp.concatenate([gain_mix, gain_ffn])[None], ((0, 7), (0, half - 48)))
+    halves = [
+        jnp.concatenate(
+            [
+                w_value[:, c * half : (c + 1) * half],
+                gains,
+                w_out[:, c * half : (c + 1) * half],
+                *[w_up[:, (4 * c + j) * half : (4 * c + j + 1) * half] for j in range(4)],
+                w_down[:, c * half : (c + 1) * half],
+            ]
+        )
+        for c in range(2)
+    ]
+    both = jnp.stack(halves)
+    joined = ordered(core, pick(both, core), swap(pick(both, 1 - core), TO_CORE))
+    part_of = lambda start, rows: joined[:, start : start + rows].reshape(2 * rows, half)
+    rand = rand_mix.reshape(3, 2, HALF, LMAX)
+    blocks = ordered(core, pick(rand, core, 1), swap(pick(rand, 1 - core, 1), TO_CORE), 0, jnp.concatenate)
+
+    first = gather_chips(joined[:, :32].reshape(64, half), place, (2, 1, 0))
+    rands = [gather_rand(blocks[part::PARTS]) for part in range(PARTS)]
+    up_rows = joined[:, 56:152].reshape(2, 4, 24, half).transpose(1, 0, 2, 3).reshape(4, 48, half)
+    second = gather_chips(jnp.concatenate([part_of(32, 24)[None], up_rows]), place, (0, 1, 2))
+    third = gather_chips(part_of(152, 96), place, (0, 2, 1))
+
+    first_far = swap(first, TO_CORE)
+    second_far = swap(second, TO_CORE)
+    third_far = swap(third, TO_CORE)
+    side = partial(ordered, core, joined=jnp.concatenate)
+    split_first = lambda x: x.reshape(16, 2, 32, half)[:, :, :24].reshape(WIDTH, half)
+    value_all = side(split_first(first), split_first(first_far), 1)
+    gain_rows = first.reshape(16, 2, 32, half)[:, :, 24]
+    gain_one = gain_rows[..., :24].reshape(1, WIDTH).astype(F32)
+    gain_two = gain_rows[..., 24:48].reshape(1, WIDTH).astype(F32)
+    out_all = side(second[:, 0].reshape(WIDTH, half), second_far[:, 0].reshape(WIDTH, half), 1)
+    up_part = lambda x: x[:, 1:].transpose(1, 0, 2, 3).reshape(4, WIDTH, half)
+    up_all = side(up_part(second), up_part(second_far), 0)
+    down_all = side(third.reshape(FF, half), third_far.reshape(FF, half), 1)
+
+    v_own = run_values(sc, tokens, gain_one, value_all)
+    v_far = swap(v_own, TO_CORE)
+
+    carry = None
+    back = None
+    rand_grads = []
+    for part in range(PARTS):
+        own, far, mean, inverse = run_mix(part, sc, rands[part], v_own, v_far)
+        got = swap(far, TO_CORE)
+        output, res_grad, g_own, g_far, d_down, d_up, d_out, d_gain_two = run_feed(
+            part, sc, tokens, grad_out, own, got, out_all, gain_two, up_all, down_all, carry
+        )
+        carry = (output, res_grad, d_down, d_up, d_out, d_gain_two)
+        g_got = swap(g_far, TO_CORE)
+        *pieces, back_own, back_far = run_unmix(
+            part, sc, rands[part], v_own, v_far, g_own, g_got, mean, inverse, back
+        )
+        back = (back_own, back_far)
+        rand_grads.append(pieces)
+    back_got = swap(back_far, TO_CORE)
+    tokens_grad, d_value, d_gain_one = run_close(
+        sc, tokens, res_grad.reshape(2, LMAX, WIDTH), back_own, back_got, gain_one, value_all
+    )
+
+    def over_cores(x):
+        return add_low(pick(x, core), swap(pick(x, 1 - core), TO_CORE))
+
+    down_sum = scatter_chips(over_cores(d_down).reshape(16, 192, half), place, (1, 2, 0))
+    up_sum = scatter_chips(
+        over_cores(d_up.reshape(2, 4, WIDTH, half)).reshape(4, 16, 48, half), place, (2, 1, 0), 1
+    )
+    gain_pair = jnp.concatenate([d_gain_one, d_gain_two]).reshape(2, 16, 1, 48).astype(BF16)
+    gain_pair = jnp.pad(gain_pair, ((0, 0), (0, 0), (0, 15), (0, half - 48)))
+    small = jnp.concatenate([d_out.reshape(2, 16, 48, half), d_value.reshape(2, 16, 48, half), gain_pair], 2)
+    small_sum = scatter_chips(over_cores(small), place, (2, 1, 0))
+    rand_sums = [scatter_rand(*pieces) for pieces in rand_grads]
+
+    weights = jnp.concatenate([small_sum, up_sum.reshape(192, half), down_sum])
+    weights_far = swap(weights, TO_CORE)
+    rows_of = lambda x, rows: pick(x.reshape(x.shape[0] // (2 * rows), 2, rows, half), core, 1)
+    mine = lambda start, rows: side(
+        rows_of(weights[start : start + 2 * rows], rows)[0], rows_of(weights_far[start : start + 2 * rows], rows)[0], 1
+    )
+    outproj_shard = mine(0, 24)
+    value_shard = mine(48, 24)
+    down_shard = mine(304, 96)
+    up_side = lambda x: rows_of(x[112:304], 24).transpose(1, 0, 2).reshape(24, 4 * half)
+    up_shard = side(up_side(weights), up_side(weights_far), 1)
+    gains_pair = ordered(core, weights[96, :48], weights_far[96, :48])
+    gain_pair = pick(gains_pair.reshape(2, 2, 24), core, 1)
+
+    blocks = jnp.stack(rand_sums, 1).reshape(6, HALF, LMAX)
+    blocks = blocks.reshape(2, 3, HALF, LMAX)
+    rand_shard = ordered(core, pick(blocks, core), swap(pick(blocks, 1 - core), TO_CORE), 1)
+
+    return (
+        output.reshape(2, LMAX, WIDTH),
+        tokens_grad,
+        rand_shard.reshape(3 * 128, LMAX),
+        value_shard,
+        outproj_shard,
+        up_shard,
+        down_shard,
+        gain_pair[0],
+        gain_pair[1],
+    )
 
 
 def rms_norm(values, gain):
@@ -191,4 +956,5 @@
         P(("wide", "narrow")),
         P(("wide", "narrow")),
     )
-    return jax.shard_map(shards, mesh=mesh, in_specs=in_specs, out_specs=out_specs, check_vma=False)
+    fits = dict(mesh.shape) == {"wide": 16, "narrow": 2}
+    return jax.shard_map(chip_shards if fits else shards, mesh=mesh, in_specs=in_specs, out_specs=out_specs, check_vma=False)

time: 1700 us -> 706 us (0.42)
  waiting for transfers between devices: 747 us -> 305 us
  matrix products: 397 us -> 0 us
  other arithmetic: 280 us -> 45.7 us
  Pallas kernels: 0 us -> 219 us
  local copies, waits for them, and re-layouts: 162 us -> 56.4 us
  blocking collectives: 83.9 us -> 0 us
  starting transfers between devices: 0.39 us -> 65.4 us
    reduce_scatter x5 -> x0, waiting for transfers between devices: 597 us -> none  [the longest x1 438 us: shards(): lax.psum_scatter(rand_flat, ('wide', 'narrow'), scatter_dimension=0, tile...]
    dot_general x84 -> x0, matrix products: 397 us -> none  [the longest x24 88.4 us: head_forward(): jnp.dot(attention.astype(jnp.bfloat16), value_head, preferred_element_typ...]
    ppermute x0 -> x95, waiting for transfers between devices: none -> 305 us  [the longest x42 158 us: ring(): lax.ppermute(x, BOTH, [(d, (d + 8) % DEVICES) for d in range(DEVICES)])]
    pallas_call x0 -> x8, Pallas kernels: none -> 219 us  [the longest x2 144 us: run_feed(): pl.pallas_call(partial(feed_kernel, part, carry is not None), grid_spec=p...]
    all_gather x5 -> x0, waiting for transfers between devices: 147 us -> none  [the longest x1 141 us: shards(): lax.all_gather(rand_mix, ('wide', 'narrow'), axis=0, tiled=True)]
    dynamic_update_slice x24 -> x0, other arithmetic: 99.8 us -> none  [shards(): lax.map(partial(head_backward, valid_table[item_index]), (rand_heads_back...]
    unnamed x2 -> x0, blocking collectives: 83.9 us -> none
    ppermute x0 -> x95, starting transfers between devices: none -> 65.4 us  [the longest x53 43.3 us: swap(): return lax.ppermute(x, BOTH, [(d, d ^ bit) for d in range(DEVICES)])]
  transfers between devices with their start and end apart: 10 -> 95, of which waited for: 5 -> 51; matrix products, arithmetic and copies ran while one was open for 46% -> 11% of each run, Pallas kernels for 0% -> 28%
where the time goes in v1:
time: 706 us; the launch traced here: 695 us
  waiting for transfers between devices  305 us (43%)
  Pallas kernels  219 us (31%)
  starting transfers between devices  65.4 us (9%)
  local copies, waits for them, and re-layouts  56.4 us (8%)
  other arithmetic  45.7 us (6%)
    ppermute x42, waiting for transfers between devices, ring(): lax.ppermute(x, BOTH, [(d, (d + 8) % DEVICES) for d in range(DEVICES)])  158 us
    ppermute x53, waiting for transfers between devices, swap(): return lax.ppermute(x, BOTH, [(d, d ^ bit) for d in range(DEVICES)])  147 us
    pallas_call x2, Pallas kernels, run_feed(): pl.pallas_call(partial(feed_kernel, part, carry is not None), grid_spec=p...  144 us
    ppermute x53, starting transfers between devices, swap(): return lax.ppermute(x, BOTH, [(d, d ^ bit) for d in range(DEVICES)])  43.3 us
    pallas_call x2, Pallas kernels, run_unmix(): pl.pallas_call(partial(unmix_kernel, part, carry is not None), grid_spec=...  40.9 us
    ppermute x42, starting transfers between devices, ring(): lax.ppermute(x, BOTH, [(d, (d + 8) % DEVICES) for d in range(DEVICES)])  22.2 us
    unnamed x186, local copies, waits for them, and re-layouts  21.5 us
    select_n x21, other arithmetic, ordered(): jnp.where(flag == 0, joined([one, two], axis), joined([two, one], axis))  20.1 us
  transfers between devices with their start and end apart: 95, of which 51 were waited for; matrix products, arithmetic and copies ran while one was open for 11% of the time, Pallas kernels for 28%

profile of v1, /device:TPU:0, one launch (start us, length us, event | category | flops | bytes accessed | tf_op | source)
XLA Modules:
  0.0 694.8 jit_solution(10953187910039374428)
XLA Ops:
  70.1 20.2 %collective-permute-done.19 = bf16[2,2,64,384]{3,2,1,0:T(8,128)(2,1)S(1)} collective-permute-done((bf16[2,2,64,384]{3,2,1,0:T(8,128)(2,1)S(1)}, bf16[2,2,64,384]{3,2,1,0:T(8,128)(2,1)S(1)}, u32[]{:S(2)}, u32[]{:S(2)}) %collective-permute-start.19) | collective-permute-done | bytes 196640 | tf_op jit(solution)/shard_map/ppermute | solution.py:576
  97.4 12.5 %collective-permute-done.26 = bf16[4,5,48,384]{3,2,1,0:T(8,128)(2,1)S(1)} collective-permute-done((bf16[4,5,48,384]{3,2,1,0:T(8,128)(2,1)}, bf16[4,5,48,384]{3,2,1,0:T(8,128)(2,1)S(1)}, u32[]{:S(2)}, u32[]{:S(2)}) %collective-permute-start.26) | collective-permute-done | bytes 737312 | tf_op jit(solution)/shard_map/ppermute | solution.py:572
  112.7 10.7 %collective-permute-done.44 = bf16[4,3,64,256]{3,2,1,0:T(8,128)(2,1)S(1)} collective-permute-done((bf16[4,3,64,256]{3,2,1,0:T(8,128)(2,1)S(1)}, bf16[4,3,64,256]{3,2,1,0:T(8,128)(2,1)S(1)}, u32[]{:S(2)}, u32[]{:S(2)}) %collective-permute-start.44) | collective-permute-done | bytes 393248 | tf_op jit(solution)/shard_map/ppermute | solution.py:576
  141.7 14.1 %collective-permute-done.5 = bf16[4,3,64,384]{3,2,1,0:T(8,128)(2,1)S(1)} collective-permute-done((bf16[4,3,64,384]{3,2,1,0:T(8,128)(2,1)S(1)}, bf16[4,3,64,384]{3,2,1,0:T(8,128)(2,1)S(1)}, u32[]{:S(2)}, u32[]{:S(2)}) %collective-permute-start.5) | collective-permute-done | bytes 589856 | tf_op jit(solution)/shard_map/ppermute | solution.py:572
  169.6 13.1 %collective-permute-done.40 = bf16[4,3,64,384]{3,2,1,0:T(8,128)(2,1)S(1)} collective-permute-done((bf16[4,3,64,384]{3,2,1,0:T(8,128)(2,1)S(1)}, bf16[4,3,64,384]{3,2,1,0:T(8,128)(2,1)S(1)}, u32[]{:S(2)}, u32[]{:S(2)}) %collective-permute-start.40) | collective-permute-done | bytes 589856 | tf_op jit(solution)/shard_map/ppermute | solution.py:572
  195.8 9.4 %collective-permute-done.6.a_far.refs_2_ = bf16[2,4,3,64,384]{4,3,2,1,0:T(8,128)(2,1)} collective-permute-done((bf16[2,4,3,64,384]{4,3,2,1,0:T(8,128)(2,1)}, bf16[2,4,3,64,384]{4,3,2,1,0:T(8,128)(2,1)}, u32[]{:S(2)}, u32[]{:S(2)}) %collective-permute-start.6) | collective-permute-done | bytes 1179680 | tf_op jit(solution)/shard_map/ppermute | solution.py:572
  213.5 7.8 %maximum_select_fusion.1.refs_8_ = bf16[3072,768]{1,0:T(8,128)(2,1)} fusion(bf16[3072,384]{1,0:T(8,128)(2,1)} %bitcast.74, bf16[3072,384]{1,0:T(8,128)(2,1)} %bitcast.72, pred[]{:T(512)S(6)} %eq.10), kind=kLoop, calls=%fused_computation.3 | loop fusion | flops 21233664 | bytes 9437185 | tf_op jit(solution)/shard_map/jit(_where)/select_n | solution.py:584
  221.3 8.2 %mix.2 = (bf16[12,256,128]{2,1,0:T(8,128)(2,1)S(1)}, bf16[12,256,128]{2,1,0:T(8,128)(2,1)S(1)}, f32[12,256,256]{2,1,0:T(8,128)S(1)}, f32[12,256,256]{2,1,0:T(8,128)S(1)}) custom-call(s32[7]{0:T(128)S(1)} %concatenate.169.sc.refs_0_, bf16[2,4,3,64,384]{4,3,2,1,0:T(8,128)(2,1)} %pad_maximum_fusion.4.a_near.refs_1_, ...), custom_call_target="tpu_custom_call" | custom-call | flops 3221225472 | bytes 14155776 | tf_op jit(solution)/shard_map/mix/pallas_call | solution.py:153
  234.1 8.2 %mix.3 = (bf16[12,256,128]{2,1,0:T(8,128)(2,1)S(1)}, bf16[12,256,128]{2,1,0:T(8,128)(2,1)S(1)}, f32[12,256,256]{2,1,0:T(8,128)S(1)}, f32[12,256,256]{2,1,0:T(8,128)S(1)}) custom-call(s32[7]{0:T(128)S(1)} %concatenate.169.sc.refs_0_, bf16[2,4,3,64,384]{4,3,2,1,0:T(8,128)(2,1)S(1)} %pad_maximum_fusion.8.a_near.refs_1_, ...), custom_call_target="tpu_custom_call" | custom-call | flops 3221225472 | bytes 14155776 | tf_op jit(solution)/shard_map/mix/pallas_call | solution.py:153
  254.6 66.8 %feed.2 = (f32[2,4,2,2,64,768]{5,4,3,2,1,0:T(8,128)}, f32[2,4,2,2,64,768]{5,4,3,2,1,0:T(8,128)}, bf16[12,256,128]{2,1,0:T(8,128)(2,1)}, bf16[12,256,128]{2,1,0:T...) custom-call(s32[7]{0:T(128)} %copy-done.17, ...), custom_call_target="tpu_custom_call" | custom-call | flops 32614907904 | bytes 31457280 | tf_op jit(solution)/shard_map/feed/pallas_call | solution.py:370
  322.5 77.2 %feed.3 = (f32[2,4,2,2,64,768]{5,4,3,2,1,0:T(8,128)}, f32[2,4,2,2,64,768]{5,4,3,2,1,0:T(8,128)}, bf16[12,256,128]{2,1,0:T(8,128)(2,1)}, bf16[12,256,128]{2,1,0:T...) custom-call(s32[7]{0:T(128)} %copy-done.17, ...), custom_call_target="tpu_custom_call", output_to_operand_aliasing={{0}: (13, {}), {1}: (14, {})} | custom-call | flops 32614907904 | bytes 31457280 | tf_op jit(solution)/shard_map/feed/pallas_call | solution.py:370
  401.1 19.0 %unmix.2 = (bf16[2,4,3,64,384]{4,3,2,1,0:T(8,128)(2,1)}, bf16[2,4,3,64,384]{4,3,2,1,0:T(8,128)(2,1)}, bf16[2,4,3,64,384]{4,3,2,1,0:T(8,128)(2,1)}, bf16[2,4,3,64...) custom-call(s32[7]{0:T(128)} %copy-done.17, ...), custom_call_target="tpu_custom_call" | custom-call | flops 3221225472 | bytes 45613056 | tf_op jit(solution)/shard_map/unmix/pallas_call | solution.py:463
  421.0 21.9 %unmix.3 = (bf16[2,4,3,64,384]{4,3,2,1,0:T(8,128)(2,1)}, bf16[2,4,3,64,384]{4,3,2,1,0:T(8,128)(2,1)}, bf16[2,4,3,64,384]{4,3,2,1,0:T(8,128)(2,1)}, bf16[2,4,3,64...) custom-call(s32[7]{0:T(128)} %copy-done.17, ...), custom_call_target="tpu_custom_call" | custom-call | flops 3221225472 | bytes 45613056 | tf_op jit(solution)/shard_map/unmix/pallas_call | solution.py:463
  458.1 8.1 %collective-permute-done.58 = bf16[4,3,64,256]{3,2,1,0:T(8,128)(2,1)S(1)} collective-permute-done((bf16[4,3,64,256]{3,2,1,0:T(8,128)(2,1)S(1)}, bf16[4,3,64,256]{3,2,1,0:T(8,128)(2,1)S(1)}, u32[]{:S(2)}, u32[]{:S(2)}) %collective-permute-start.58) | collective-permute-done | bytes 393248 | tf_op jit(solution)/shard_map/ppermute | solution.py:576
  466.8 7.8 %collective-permute-done.71 = bf16[4,3,64,256]{3,2,1,0:T(8,128)(2,1)S(1)} collective-permute-done((bf16[4,3,64,256]{3,2,1,0:T(8,128)(2,1)S(1)}, bf16[4,3,64,256]{3,2,1,0:T(8,128)(2,1)S(1)}, u32[]{:S(2)}, u32[]{:S(2)}) %collective-permute-start.71) | collective-permute-done | bytes 393248 | tf_op jit(solution)/shard_map/ppermute | solution.py:576
  474.8 7.5 %collective-permute-done.59 = bf16[4,3,64,256]{3,2,1,0:T(8,128)(2,1)S(1)} collective-permute-done((bf16[4,3,64,256]{3,2,1,0:T(8,128)(2,1)S(1)}, bf16[4,3,64,256]{3,2,1,0:T(8,128)(2,1)S(1)}, u32[]{:S(2)}, u32[]{:S(2)}) %collective-permute-start.59) | collective-permute-done | bytes 393248 | tf_op jit(solution)/shard_map/ppermute | solution.py:576
  487.4 22.1 %collective-permute-done.53 = bf16[2,4,3,64,384]{4,3,2,1,0:T(8,128)(2,1)S(1)} collective-permute-done((bf16[2,4,3,64,384]{4,3,2,1,0:T(8,128)(2,1)S(1)}, bf16[2,4,3,64,384]{4,3,2,1,0:T(8,128)(2,1)S(1)}, u32[]{:S(2)}, u32[]{:S(2)}) %collective-permute-start.53) | collective-permute-done | bytes 1179680 | tf_op jit(solution)/shard_map/ppermute | solution.py:572
  513.2 10.2 %collective-permute-done.72 = bf16[4,3,64,256]{3,2,1,0:T(8,128)(2,1)S(1)} collective-permute-done((bf16[4,3,64,256]{3,2,1,0:T(8,128)(2,1)S(1)}, bf16[4,3,64,256]{3,2,1,0:T(8,128)(2,1)S(1)}, u32[]{:S(2)}, u32[]{:S(2)}) %collective-permute-start.72) | collective-permute-done | bytes 393248 | tf_op jit(solution)/shard_map/ppermute | solution.py:576
  531.5 8.3 %collective-permute-done.73 = bf16[2,3,64,256]{3,2,1,0:T(8,128)(2,1)S(1)} collective-permute-done((bf16[2,3,64,256]{3,2,1,0:T(8,128)(2,1)S(1)}, bf16[2,3,64,256]{3,2,1,0:T(8,128)(2,1)S(1)}, u32[]{:S(2)}, u32[]{:S(2)}) %collective-permute-start.73) | collective-permute-done | bytes 196640 | tf_op jit(solution)/shard_map/ppermute | solution.py:572
  562.1 8.2 %collective-permute-done.64 = bf16[4,3,64,384]{3,2,1,0:T(8,128)(2,1)S(1)} collective-permute-done((bf16[4,3,64,384]{3,2,1,0:T(8,128)(2,1)S(1)}, bf16[4,3,64,384]{3,2,1,0:T(8,128)(2,1)S(1)}, u32[]{:S(2)}, u32[]{:S(2)}) %collective-permute-start.64) | collective-permute-done | bytes 589856 | tf_op jit(solution)/shard_map/ppermute | solution.py:572
  577.0 7.4 %collective-permute-done.67 = bf16[2,3,64,384]{3,2,1,0:T(8,128)(2,1)S(1)} collective-permute-done((bf16[2,3,64,384]{3,2,1,0:T(8,128)(2,1)S(1)}, bf16[2,3,64,384]{3,2,1,0:T(8,128)(2,1)S(1)}, u32[]{:S(2)}, u32[]{:S(2)}) %collective-permute-start.67) | collective-permute-done | bytes 294944 | tf_op jit(solution)/shard_map/ppermute | solution.py:576
  612.0 12.9 %close.1 = (f32[2,1024,768]{2,1,0:T(8,128)}, bf16[2,768,384]{2,1,0:T(8,128)(2,1)S(1)}, f32[1,768]{1,0:T(1,128)S(1)}) custom-call(s32[7]{0:T(128)S(1)} %copy-done.18, bf16[2,1024,768]{2,1,0:T(8,128)(2,1)S(1)} %copy-done.12, f32[2,1024,768]{2,1,0:T(8,128)} %bitcast.374, f32[12,1024,128]{2,1,0:T(8,128)} %get-tuple-element.72.own, ...), custom_call_target="tpu_custom_call" | custom-call | flops 4831838208 | bytes 20447232 | tf_op jit(solution)/shard_map/close/pallas_call | solution.py:534
  634.9 10.2 %collective-permute-done.90 = bf16[4,192,384]{2,1,0:T(8,128)(2,1)S(1)} collective-permute-done((bf16[4,192,384]{2,1,0:T(8,128)(2,1)S(1)}, bf16[4,192,384]{2,1,0:T(8,128)(2,1)S(1)}, u32[]{:S(2)}, u32[]{:S(2)}) %collective-permute-start.90) | collective-permute-done | bytes 589856 | tf_op jit(solution)/shard_map/ppermute | solution.py:572
  653.9 7.8 %collective-permute-done.77 = bf16[4,2,112,384]{3,2,1,0:T(8,128)(2,1)S(1)} collective-permute-done((bf16[4,2,112,384]{3,2,1,0:T(8,128)(2,1)S(1)}, bf16[4,2,112,384]{3,2,1,0:T(8,128)(2,1)S(1)}, u32[]{:S(2)}, u32[]{:S(2)}) %collective-permute-start.77) | collective-permute-done | bytes 688160 | tf_op jit(solution)/shard_map/ppermute | solution.py:572
  (550 shorter events, 292.3 us)
Async XLA Ops:
  51.8 43.4 %collective-permute-start.32 = (bf16[4,192,384]{2,1,0:T(8,128)(2,1)}, bf16[4,192,384]{2,1,0:T(8,128)(2,1)S(1)}, u32[]{:S(2)}, u32[]{:S(2)}) collective-permute-start(bf16[4,192,384]{2,1,0:T(8,128)(2,1)} %constant_dynamic-slice_fusion.9), channel_id=1, source_target_pairs={{0,2},{1,3},{2,0},{3,1},{4,6},{5,7},{6,4},{7,5},{8,10},{9,11},{10,... | collective-permute-start | bytes 1769480 | tf_op jit(solution)/shard_map/ppermute | solution.py:572
  53.3 59.5 %collective-permute-start.11 = (bf16[4,3,64,256]{3,2,1,0:T(8,128)(2,1)}, bf16[4,3,64,256]{3,2,1,0:T(8,128)(2,1)}, u32[]{:S(2)}, u32[]{:S(2)}) collective-permute-start(bf16[4,3,64,256]{3,2,1,0:T(8,128)(2,1)} %get-tuple-element.143), channel_id=1, source_target_pairs={{0,8},{1,9},{2,10},{3,11},{4,12},{5,13},{6,14},{7,15},{8,16},{9,17... | collective-permute-start | bytes 1179656 | tf_op jit(solution)/shard_map/ppermute | solution.py:576
  59.8 33.1 %collective-permute-start.3 = (bf16[2,3,64,384]{3,2,1,0:T(8,128)(2,1)}, bf16[2,3,64,384]{3,2,1,0:T(8,128)(2,1)}, u32[]{:S(2)}, u32[]{:S(2)}) collective-permute-start(bf16[2,3,64,384]{3,2,1,0:T(8,128)(2,1)} %collective-permute-done.2), channel_id=1, source_target_pairs={{0,8},{1,9},{2,10},{3,11},{4,12},{5,13},{6,14},{7,15},{8,16},{9,17... | collective-permute-start | bytes 884744 | tf_op jit(solution)/shard_map/ppermute | solution.py:576
  63.9 30.2 %collective-permute-start.36 = (bf16[2,3,64,384]{3,2,1,0:T(8,128)(2,1)}, bf16[2,3,64,384]{3,2,1,0:T(8,128)(2,1)}, u32[]{:S(2)}, u32[]{:S(2)}) collective-permute-start(bf16[2,3,64,384]{3,2,1,0:T(8,128)(2,1)} %collective-permute-done.35), channel_id=1, source_target_pairs={{0,8},{1,9},{2,10},{3,11},{4,12},{5,13},{6,14},{7,15},{8,16},{9,17... | collective-permute-start | bytes 884744 | tf_op jit(solution)/shard_map/ppermute | solution.py:576
  92.9 30.5 %collective-permute-start.20 = (bf16[16,64,384]{2,1,0:T(8,128)(2,1)S(1)}, bf16[16,64,384]{2,1,0:T(8,128)(2,1)S(1)}, u32[]{:S(2)}, u32[]{:S(2)}) collective-permute-start(bf16[16,64,384]{2,1,0:T(8,128)(2,1)S(1)} %bitcast.389), channel_id=1, source_target_pairs={{0,1},{1,0},{2,3},{3,2},{4,5},{5,4},{6,7},{7,6},{8,9},{9,8},{10,11... | collective-permute-start | bytes 2359304 | tf_op jit(solution)/shard_map/ppermute | solution.py:572
  95.4 36.1 %collective-permute-start.33 = (bf16[4,2,192,384]{3,2,1,0:T(8,128)(2,1)S(1)}, bf16[4,2,192,384]{3,2,1,0:T(8,128)(2,1)S(1)}, u32[]{:S(2)}, u32[]{:S(2)}) collective-permute-start(bf16[4,2,192,384]{3,2,1,0:T(8,128)(2,1)S(1)} %maximum_select_fusion.9), channel_id=1, source_target_pairs={{0,4},{1,5},{2,6},{3,7},{4,0},{5,1},{6,2},{7,3},{8,12},{9,13},{10,... | collective-permute-start | bytes 3538952 | tf_op jit(solution)/shard_map/ppermute | solution.py:572
  110.8 46.0 %collective-permute-start.27 = (bf16[4,2,5,48,384]{4,3,2,0,1:T(8,128)(2,1)S(1)}, bf16[4,2,5,48,384]{4,3,2,0,1:T(8,128)(2,1)S(1)}, u32[]{:S(2)}, u32[]{:S(2)}) collective-permute-start(bf16[4,2,5,48,384]{4,3,2,0,1:T(8,128)(2,1)S(1)} %maximum_select_fusion.6), channel_id=1, source_target_pairs={{0,2},{1,3},{2,0},{3,1},{4,6},{5,7},{6,4},{7,5},{8,10},{9,11},{10,... | collective-permute-start | bytes 4423688 | tf_op jit(solution)/shard_map/ppermute | solution.py:572
  134.1 71.6 %collective-permute-start.34 = (bf16[16,192,384]{2,1,0:T(8,128)(2,1)}, bf16[16,192,384]{2,1,0:T(8,128)(2,1)}, u32[]{:S(2)}, u32[]{:S(2)}) collective-permute-start(bf16[16,192,384]{2,1,0:T(8,128)(2,1)} %bitcast.73), channel_id=1, source_target_pairs={{0,1},{1,0},{2,3},{3,2},{4,5},{5,4},{6,7},{7,6},{8,9},{9,8},{10,11... | collective-permute-start | bytes 7077896 | tf_op jit(solution)/shard_map/ppermute | solution.py:572
  140.7 80.5 %collective-permute-start.21 = (bf16[12,1024,128]{2,1,0:T(8,128)(2,1)S(1)}, bf16[12,1024,128]{2,1,0:T(8,128)(2,1)}, u32[]{:S(2)}, u32[]{:S(2)}) collective-permute-start(bf16[12,1024,128]{2,1,0:T(8,128)(2,1)S(1)} %values.1.v_own.refs_6_), channel_id=1, source_target_pairs={{0,1},{1,0},{2,3},{3,2},{4,5},{5,4},{6,7},{7,6},{8,9},{9,8},{10,11... | collective-permute-start | bytes 9437192 | tf_op jit(solution)/shard_map/ppermute | solution.py:572
  159.4 84.8 %collective-permute-start.28 = (bf16[16,5,48,384]{3,2,1,0:T(8,128)(2,1)}, bf16[16,5,48,384]{3,2,1,0:T(8,128)(2,1)}, u32[]{:S(2)}, u32[]{:S(2)}) collective-permute-start(bf16[16,5,48,384]{3,2,1,0:T(8,128)(2,1)} %bitcast.55), channel_id=1, source_target_pairs={{0,1},{1,0},{2,3},{3,2},{4,5},{5,4},{6,7},{7,6},{8,9},{9,8},{10,11... | collective-permute-start | bytes 8847368 | tf_op jit(solution)/shard_map/ppermute | solution.py:572
  168.1 37.1 %collective-permute-start.6 = (bf16[2,4,3,64,384]{4,3,2,1,0:T(8,128)(2,1)}, bf16[2,4,3,64,384]{4,3,2,1,0:T(8,128)(2,1)}, u32[]{:S(2)}, u32[]{:S(2)}) collective-permute-start(bf16[2,4,3,64,384]{4,3,2,1,0:T(8,128)(2,1)} %pad_maximum_fusion.4.a_near.refs_1_), channel_id=1, source_target_pairs={{0,4},{1,5},{2,6},{3,7},{4,0},{5,1},{6,2},{7,3},{8,12},{9,13},{10,... | collective-permute-start | bytes 3538952 | tf_op jit(solution)/shard_map/ppermute | solution.py:572
  192.6 28.6 %collective-permute-start.8 = (bf16[2,4,3,64,384]{4,3,2,1,0:T(8,128)(2,1)S(1)}, bf16[2,4,3,64,384]{4,3,2,1,0:T(8,128)(2,1)S(1)}, u32[]{:S(2)}, u32[]{:S(2)}) collective-permute-start(bf16[2,4,3,64,384]{4,3,2,1,0:T(8,128)(2,1)S(1)} %pad_maximum_fusion.5.b_near.refs_3_), channel_id=1, source_target_pairs={{0,2},{1,3},{2,0},{3,1},{4,6},{5,7},{6,4},{7,5},{8,10},{9,11},{10,... | collective-permute-start | bytes 3538952 | tf_op jit(solution)/shard_map/ppermute | solution.py:572
  205.2 28.5 %collective-permute-start.39 = (bf16[2,4,3,64,384]{4,3,2,1,0:T(8,128)(2,1)S(1)}, bf16[2,4,3,64,384]{4,3,2,1,0:T(8,128)(2,1)S(1)}, u32[]{:S(2)}, u32[]{:S(2)}) collective-permute-start(bf16[2,4,3,64,384]{4,3,2,1,0:T(8,128)(2,1)S(1)} %pad_maximum_fusion.8.a_near.refs_1_), channel_id=1, source_target_pairs={{0,4},{1,5},{2,6},{3,7},{4,0},{5,1},{6,2},{7,3},{8,12},{9,13},{10,... | collective-permute-start | bytes 3538952 | tf_op jit(solution)/shard_map/ppermute | solution.py:572
  233.7 88.0 %collective-permute-start.22 = (bf16[12,256,128]{2,1,0:T(8,128)(2,1)S(1)}, bf16[12,256,128]{2,1,0:T(8,128)(2,1)S(1)}, u32[]{:S(2)}, u32[]{:S(2)}) collective-permute-start(bf16[12,256,128]{2,1,0:T(8,128)(2,1)S(1)} %get-tuple-element.51), channel_id=1, source_target_pairs={{0,1},{1,0},{2,3},{3,2},{4,5},{5,4},{6,7},{7,6},{8,9},{9,8},{10,11... | collective-permute-start | bytes 2359304 | tf_op jit(solution)/shard_map/ppermute | solution.py:572
  321.4 78.8 %collective-permute-start.49 = (bf16[12,256,128]{2,1,0:T(8,128)(2,1)}, bf16[12,256,128]{2,1,0:T(8,128)(2,1)S(1)}, u32[]{:S(2)}, u32[]{:S(2)}) collective-permute-start(bf16[12,256,128]{2,1,0:T(8,128)(2,1)} %get-tuple-element.67), channel_id=1, source_target_pairs={{0,1},{1,0},{2,3},{3,2},{4,5},{5,4},{6,7},{7,6},{8,9},{9,8},{10,11... | collective-permute-start | bytes 2359304 | tf_op jit(solution)/shard_map/ppermute | solution.py:572
  450.6 105.8 %collective-permute-start.88 = (bf16[3072,384]{1,0:T(8,128)(2,1)S(1)}, bf16[3072,384]{1,0:T(8,128)(2,1)S(1)}, u32[]{:S(2)}, u32[]{:S(2)}) collective-permute-start(bf16[3072,384]{1,0:T(8,128)(2,1)S(1)} %dynamic-slice_bitcast_fusion), channel_id=1, source_target_pairs={{0,1},{1,0},{2,3},{3,2},{4,5},{5,4},{6,7},{7,6},{8,9},{9,8},{10,11... | collective-permute-start | bytes 7077896 | tf_op jit(solution)/shard_map/ppermute | solution.py:572
  450.7 33.1 %collective-permute-start.65 = (bf16[2,4,3,64,384]{4,3,2,1,0:T(8,128)(2,1)S(1)}, bf16[2,4,3,64,384]{4,3,2,1,0:T(8,128)(2,1)S(1)}, u32[]{:S(2)}, u32[]{:S(2)}) collective-permute-start(bf16[2,4,3,64,384]{4,3,2,1,0:T(8,128)(2,1)S(1)} %copy-done.73), channel_id=1, source_target_pairs={{0,2},{1,3},{2,0},{3,1},{4,6},{5,7},{6,4},{7,5},{8,10},{9,11},{10,... | collective-permute-start | bytes 3538952 | tf_op jit(solution)/shard_map/ppermute | solution.py:572
  452.2 32.9 %collective-permute-start.63 = (bf16[2,4,3,64,384]{4,3,2,1,0:T(8,128)(2,1)S(1)}, bf16[2,4,3,64,384]{4,3,2,1,0:T(8,128)(2,1)S(1)}, u32[]{:S(2)}, u32[]{:S(2)}) collective-permute-start(bf16[2,4,3,64,384]{4,3,2,1,0:T(8,128)(2,1)S(1)} %copy-done.72), channel_id=1, source_target_pairs={{0,4},{1,5},{2,6},{3,7},{4,0},{5,1},{6,2},{7,3},{8,12},{9,13},{10,... | collective-permute-start | bytes 3538952 | tf_op jit(solution)/shard_map/ppermute | solution.py:572
  474.6 109.9 %collective-permute-start.82 = (bf16[4,768,384]{2,1,0:T(8,128)(2,1)S(1)}, bf16[4,768,384]{2,1,0:T(8,128)(2,1)S(1)}, u32[]{:S(2)}, u32[]{:S(2)}) collective-permute-start(bf16[4,768,384]{2,1,0:T(8,128)(2,1)S(1)} %dynamic-slice_bitcast_fusion.1), channel_id=1, source_target_pairs={{0,1},{1,0},{2,3},{3,2},{4,5},{5,4},{6,7},{7,6},{8,9},{9,8},{10,11... | collective-permute-start | bytes 7077896 | tf_op jit(solution)/shard_map/ppermute | solution.py:572
  486.6 124.9 %collective-permute-start.50 = (bf16[12,1024,128]{2,1,0:T(8,128)(2,1)S(1)}, bf16[12,1024,128]{2,1,0:T(8,128)(2,1)S(1)}, u32[]{:S(2)}, u32[]{:S(2)}) collective-permute-start(bf16[12,1024,128]{2,1,0:T(8,128)(2,1)S(1)} %copy-done.69), channel_id=1, source_target_pairs={{0,1},{1,0},{2,3},{3,2},{4,5},{5,4},{6,7},{7,6},{8,9},{9,8},{10,11... | collective-permute-start | bytes 9437192 | tf_op jit(solution)/shard_map/ppermute | solution.py:572
  523.4 37.1 %collective-permute-start.66 = (bf16[4,3,64,384]{3,2,1,0:T(8,128)(2,1)S(1)}, bf16[4,3,64,384]{3,2,1,0:T(8,128)(2,1)S(1)}, u32[]{:S(2)}, u32[]{:S(2)}) collective-permute-start(bf16[4,3,64,384]{3,2,1,0:T(8,128)(2,1)S(1)} %slice_bitcast_fusion.2), channel_id=1, source_target_pairs={{0,4},{1,5},{2,6},{3,7},{4,0},{5,1},{6,2},{7,3},{8,12},{9,13},{10,... | collective-permute-start | bytes 1769480 | tf_op jit(solution)/shard_map/ppermute | solution.py:572
  570.2 58.5 %collective-permute-start.89 = (bf16[4,2,192,384]{3,2,0,1:T(8,128)(2,1)}, bf16[4,2,192,384]{3,2,0,1:T(8,128)(2,1)}, u32[]{:S(2)}, u32[]{:S(2)}) collective-permute-start(bf16[4,2,192,384]{3,2,0,1:T(8,128)(2,1)} %bitcast.362), channel_id=1, source_target_pairs={{0,4},{1,5},{2,6},{3,7},{4,0},{5,1},{6,2},{7,3},{8,12},{9,13},{10,... | collective-permute-start | bytes 3538952 | tf_op jit(solution)/shard_map/ppermute | solution.py:572
  598.6 32.9 %collective-permute-start.83 = (bf16[4,4,2,48,384]{4,3,0,1,2:T(8,128)(2,1)}, bf16[4,4,2,48,384]{4,3,0,1,2:T(8,128)(2,1)}, u32[]{:S(2)}, u32[]{:S(2)}) collective-permute-start(bf16[4,4,2,48,384]{4,3,0,1,2:T(8,128)(2,1)} %bitcast.363), channel_id=1, source_target_pairs={{0,2},{1,3},{2,0},{3,1},{4,6},{5,7},{6,4},{7,5},{8,10},{9,11},{10,... | collective-permute-start | bytes 3538952 | tf_op jit(solution)/shard_map/ppermute | solution.py:572
  631.4 57.4 %collective-permute-start.75 = (f32[3,64,1024]{2,1,0:T(8,128)S(1)}, f32[3,64,1024]{2,1,0:T(8,128)S(1)}, u32[]{:S(2)}, u32[]{:S(2)}) collective-permute-start(f32[3,64,1024]{2,1,0:T(8,128)S(1)} %get-tuple-element.97), channel_id=1, source_target_pairs={{0,1},{1,0},{2,3},{3,2},{4,5},{5,4},{6,7},{7,6},{8,9},{9,8},{10,11... | collective-permute-start | bytes 2359304 | tf_op jit(solution)/shard_map/ppermute | solution.py:572
  (151 other events, 2087.6 us)

commit v2 on v0

--- a/solution.py
+++ b/solution.py
@@ -3,14 +3,958 @@
 import jax
 import jax.numpy as jnp
 from jax import lax
+from jax.experimental import pallas as pl
+from jax.experimental.pallas import tpu as pltpu
 from jax.sharding import PartitionSpec as P
 
 HEADS = 12
 HEAD = 64
 LMAX = 1024
-
-
+WIDTH = 768
+FF = 3072
 EPSILON = 1e-05
+
+BOTH = ("wide", "narrow")
+BF16 = jnp.bfloat16
+F32 = jnp.float32
+MIB = 1 << 20
+
+SUBS = 6
+RUNS = 8
+HALF = 64
+HROWS = RUNS * HALF
+PLANES = 4
+PHEADS = HEADS // PLANES
+ROWS = 2 * LMAX
+FSTEP = 512
+FSIDE = FF // 2 // FSTEP
+TILE = 512
+SIDE = WIDTH // 2
+
+
+def dot(a, b, ca, cb):
+    return lax.dot_general(a, b, (((ca,), (cb,)), ((), ())), preferred_element_type=F32)
+
+
+CORE, PLANE, PLACE, LENGTHS = 0, 1, 2, 3
+
+
+def spec(shape, index):
+    return pl.BlockSpec(shape, index)
+
+
+def held(shape):
+    zeros = (0,) * len(shape)
+    return pl.BlockSpec(shape, lambda *_: zeros, pipeline_mode=pl.Buffered(1))
+
+
+def params(limit):
+    return pltpu.CompilerParams(vmem_limit_bytes=limit * MIB)
+
+
+def whole_weight(sc, step, own, far, weight):
+    @pl.when(step == 0)
+    def _():
+        weight[:, pl.ds(pl.multiple_of(sc[CORE] * SIDE, 128), SIDE)] = own[...]
+        weight[:, pl.ds(pl.multiple_of((1 - sc[CORE]) * SIDE, 128), SIDE)] = far[...]
+
+
+def values_kernel(sc, tok, gain, w_own, w_far, out, weight):
+    step = pl.program_id(0)
+    whole_weight(sc, step, w_own, w_far, weight)
+    rows = tok.shape[1]
+    position = step * rows + lax.broadcasted_iota(jnp.int32, (rows, 1), 0)
+    for item in range(2):
+        x = tok[item].astype(F32)
+        scale = lax.rsqrt(jnp.mean(x * x, axis=-1, keepdims=True) + EPSILON)
+        normed = (x * scale * gain[...]).astype(BF16)
+        found = dot(normed, weight[...], 1, 0)
+        found = jnp.where(position < sc[LENGTHS + item], found, 0.0).astype(BF16)
+        for head in range(HEADS):
+            out[head, :, item * HEAD : (item + 1) * HEAD] = found[:, head * HEAD : (head + 1) * HEAD]
+
+
+def run_values(sc, tokens, gain, w_own, w_far):
+    rows = 256
+    return pl.pallas_call(
+        values_kernel,
+        grid_spec=pltpu.PrefetchScalarGridSpec(
+            num_scalar_prefetch=1,
+            grid=(LMAX // rows,),
+            in_specs=[
+                spec((2, rows, WIDTH), lambda j, s: (0, j, 0)),
+                held((1, WIDTH)),
+                held((WIDTH, SIDE)),
+                held((WIDTH, SIDE)),
+            ],
+            out_specs=spec((HEADS, rows, 2 * HEAD), lambda j, s: (0, j, 0)),
+            scratch_shapes=[pltpu.VMEM((WIDTH, WIDTH), BF16)],
+        ),
+        out_shape=jax.ShapeDtypeStruct((HEADS, LMAX, 2 * HEAD), BF16),
+        compiler_params=params(32),
+        cost_estimate=pl.CostEstimate(
+            flops=2 * 2 * LMAX * WIDTH * WIDTH, bytes_accessed=8 * LMAX * WIDTH, transcendentals=0
+        ),
+        name="values",
+    )(sc, tokens, gain, w_own, w_far)
+
+
+def lane_lengths(sc, shape):
+    slot = lax.broadcasted_iota(jnp.int32, shape, 1) // HEAD
+    length = jnp.where(slot == 0, sc[LENGTHS], sc[LENGTHS + 1])
+    return jnp.where(slot >= 2, jnp.where(slot == 2, sc[LENGTHS + 2], sc[LENGTHS + 3]), length)
+
+
+def plane_of(k, sc):
+    return lax.rem(sc[PLANE] + PLANES - k, PLANES)
+
+
+def plane_spec(planes, rows, lanes):
+    def index(step, sc):
+        k = planes[0] + step * (planes[1] - planes[0])
+        return (plane_of(k, sc), 0, 0)
+
+    return spec((PHEADS, rows, lanes), index)
+
+
+def in_hbm(count):
+    return [pl.BlockSpec(memory_space=pltpu.HBM)] * count
+
+
+def plane_fetch(place, shards, raw, sems, slot):
+    return [
+        pltpu.make_async_copy(
+            shards[4 * slot + rel].at[pl.ds(0, SUBS * HALF)],
+            raw.at[slot, pl.ds(pl.multiple_of((place ^ rel) * SUBS * HALF, SUBS * HALF), SUBS * HALF)],
+            sems.at[slot, rel],
+        )
+        for rel in range(4)
+    ]
+
+
+def take_plane(place, shards, raw, sems):
+    step = pl.program_id(0)
+
+    @pl.when(step == 0)
+    def _():
+        for slot in range(2):
+            for copy in plane_fetch(place, shards, raw, sems, slot):
+                copy.start()
+
+    for slot in range(2):
+
+        @pl.when(step == slot)
+        def _():
+            for copy in plane_fetch(place, shards, raw, sems, slot):
+                copy.wait()
+
+    return step
+
+
+def exponents(raw, slot, head):
+    return jnp.exp(raw[slot, head * HROWS : (head + 1) * HROWS].astype(F32)).astype(BF16)
+
+
+def mix_kernel(carried, sc, *refs):
+    shards, (v_own, v_far, *rest) = refs[:8], refs[8:]
+    mixed, mean, inverse, raw, mask, sems = rest[3:] if carried else rest
+
+    @pl.when(pl.program_id(0) == 0)
+    def _():
+        shape = (LMAX, 4 * HEAD)
+        column = lax.broadcasted_iota(jnp.int32, shape, 0)
+        mask[...] = (column < lane_lengths(sc, shape)).astype(F32).astype(BF16)
+
+    slot = take_plane(sc[PLACE], shards, raw, sems)
+    shape = (HROWS, 4 * HEAD)
+    line = lax.broadcasted_iota(jnp.int32, shape, 0)
+    position = 128 * (line // HALF) + HALF * sc[CORE] + line % HALF
+    valid = position < lane_lengths(sc, shape)
+    for head in range(PHEADS):
+        weights = exponents(raw, slot, head)
+        total = dot(weights, mask[...], 1, 0)
+        flip = jnp.where(valid, 1.0 / total, 0.0)
+        found = dot(weights, jnp.concatenate([v_own[head], v_far[head]], axis=1), 1, 0) * flip
+        inverse[head] = flip
+        mean[head] = found
+        mixed[head] = found.astype(BF16)
+
+
+def run_mix(sc, planes, shards, v_own, v_far, carry):
+    out_shape = [
+        jax.ShapeDtypeStruct((HEADS, HROWS, 4 * HEAD), BF16),
+        jax.ShapeDtypeStruct((HEADS, HROWS, 4 * HEAD), F32),
+        jax.ShapeDtypeStruct((HEADS, HROWS, 4 * HEAD), F32),
+    ]
+    carry = list(carry)
+    return pl.pallas_call(
+        partial(mix_kernel, bool(carry)),
+        grid_spec=pltpu.PrefetchScalarGridSpec(
+            num_scalar_prefetch=1,
+            grid=(2,),
+            in_specs=in_hbm(8) + [plane_spec(planes, LMAX, 2 * HEAD)] * 2 + in_hbm(len(carry)),
+            out_specs=[plane_spec(planes, HROWS, 4 * HEAD)] * 3,
+            scratch_shapes=[
+                pltpu.VMEM((2, 4 * SUBS * HALF, LMAX), BF16),
+                pltpu.VMEM((LMAX, 4 * HEAD), BF16),
+                pltpu.SemaphoreType.DMA((2, 4)),
+            ],
+        ),
+        out_shape=out_shape,
+        input_output_aliases={11 + i: i for i in range(len(carry))},
+        compiler_params=params(48),
+        cost_estimate=pl.CostEstimate(
+            flops=2 * HEADS * HROWS * LMAX * 4 * HEAD,
+            bytes_accessed=HEADS * (HROWS * LMAX + 5 * HROWS * 256),
+            transcendentals=HEADS * HROWS * LMAX // 2,
+        ),
+        name="mix",
+    )(sc, *shards, v_own, v_far, *carry)
+
+
+def row_valid(sc, step):
+    line = lax.broadcasted_iota(jnp.int32, (256, 1), 0)
+    item = line // HALF
+    low = jnp.where(item == 0, sc[LENGTHS], sc[LENGTHS + 1])
+    high = jnp.where(item == 2, sc[LENGTHS + 2], sc[LENGTHS + 3])
+    return 128 * step + HALF * sc[CORE] + line % HALF < jnp.where(item >= 2, high, low)
+
+
+def four_items(own, far):
+    return jnp.concatenate([own[:, 0, 0], far[:, 0]], axis=0).reshape(256, WIDTH)
+
+
+def pre_kernel(sc, tok, tok_far, cot, cot_far, heads, wo_own, wo_far, gain, mixed, resid, normed, grad, weight):
+    step = pl.program_id(0)
+    whole_weight(sc, step, wo_own, wo_far, weight)
+    for item in range(4):
+        lanes = slice(item * HEAD, (item + 1) * HEAD)
+        for pair in range(HEADS // 2):
+            both = jnp.concatenate([heads[2 * pair, :, lanes], heads[2 * pair + 1, :, lanes]], axis=1)
+            mixed[item, :, pair * 128 : (pair + 1) * 128] = both
+    res = four_items(tok, tok_far).astype(F32) + dot(mixed[...].reshape(256, WIDTH), weight[...], 1, 0)
+    resid[...] = res.reshape(4, HALF, WIDTH)
+    scale = lax.rsqrt(jnp.mean(res * res, axis=-1, keepdims=True) + EPSILON)
+    valid = row_valid(sc, step)
+    normed[...] = jnp.where(valid, res * scale * gain[...], 0.0).astype(BF16).reshape(4, HALF, WIDTH)
+    masked = jnp.where(valid, four_items(cot, cot_far).astype(F32), 0.0)
+    grad[...] = masked.astype(BF16).reshape(4, HALF, WIDTH)
+
+
+def slab_spec(items=4):
+    return spec((items, HALF, WIDTH), lambda r, s: (0, r, 0))
+
+
+def half_specs():
+    return [
+        spec((2, 1, 1, HALF, WIDTH), lambda r, s: (0, r, s[CORE], 0, 0)),
+        spec((2, 1, HALF, WIDTH), lambda r, s: (0, r, 0, 0)),
+    ]
+
+
+def heads_spec():
+    return spec((HEADS, HALF, 4 * HEAD), lambda r, s: (0, r, 0))
+
+
+def run_pre(sc, tokens, tokens_far, cotangent, cotangent_far, heads, wo, gain):
+    return pl.pallas_call(
+        pre_kernel,
+        grid_spec=pltpu.PrefetchScalarGridSpec(
+            num_scalar_prefetch=1,
+            grid=(RUNS,),
+            in_specs=half_specs()
+            + half_specs()
+            + [heads_spec(), held((WIDTH, SIDE)), held((WIDTH, SIDE)), held((1, WIDTH))],
+            out_specs=[slab_spec()] * 4,
+            scratch_shapes=[pltpu.VMEM((WIDTH, WIDTH), BF16)],
+        ),
+        out_shape=[
+            jax.ShapeDtypeStruct((4, HROWS, WIDTH), BF16),
+            jax.ShapeDtypeStruct((4, HROWS, WIDTH), F32),
+            jax.ShapeDtypeStruct((4, HROWS, WIDTH), BF16),
+            jax.ShapeDtypeStruct((4, HROWS, WIDTH), BF16),
+        ],
+        compiler_params=params(32),
+        cost_estimate=pl.CostEstimate(
+            flops=2 * ROWS * WIDTH * WIDTH, bytes_accessed=16 * ROWS * WIDTH, transcendentals=0
+        ),
+        name="pre",
+    )(sc, tokens, tokens_far, cotangent, cotangent_far, heads, *wo, gain)
+
+
+def feed_kernel(sc, normed, cot, up_own, up_far, dn_own, dn_far, *refs):
+    (branch, back, d_down_own, d_down_far, d_up_own, d_up_far, w_down, active, up_grad) = refs
+    step = pl.program_id(0)
+    core = sc[CORE]
+    own_lanes = pl.ds(pl.multiple_of(core * SIDE, 128), SIDE)
+    far_lanes = pl.ds(pl.multiple_of((1 - core) * SIDE, 128), SIDE)
+    w_down[:, own_lanes] = dn_own[...]
+    w_down[:, far_lanes] = dn_far[...]
+
+    def units(up_w, d_up):
+        for piece in range(ROWS // TILE):
+            rows = slice(piece * TILE, (piece + 1) * TILE)
+            up = dot(normed[rows], up_w[...], 1, 0)
+            square = up * up
+            bend = jnp.tanh(up * (0.7978845608028654 + (0.044715 * 0.7978845608028654) * square))
+            share = 0.5 + 0.5 * bend
+            act = (up * share).astype(BF16)
+            active[rows] = act
+            slope = share + (0.5 * up) * (1.0 - bend * bend) * (
+                0.7978845608028654 + (3 * 0.044715 * 0.7978845608028654) * square
+            )
+            low = (dot(cot[rows], w_down[...], 1, 1) * slope).astype(BF16)
+            up_grad[rows] = low
+            out = dot(act, w_down[...], 1, 0)
+            two_grad = dot(low, up_w[...], 1, 1)
+
+            @pl.when(step == 0)
+            def _():
+                branch[rows] = out
+                back[rows] = two_grad
+
+            @pl.when(step > 0)
+            def _():
+                branch[rows] += out
+                back[rows] += two_grad
+
+        d_up[...] = dot(normed[...], up_grad[...], 0, 0).astype(BF16)
+
+    @pl.when(step < FSIDE)
+    def _():
+        units(up_own, d_up_own)
+
+    @pl.when(step >= FSIDE)
+    def _():
+        units(up_far, d_up_far)
+
+    w_down[...] = dot(active[...], cot[...], 0, 0).astype(BF16)
+    d_down_own[...] = w_down[:, own_lanes]
+    d_down_far[...] = w_down[:, far_lanes]
+
+
+def run_feed(sc, normed, cotangent, up, down):
+    units = lambda f, s: (lax.rem(FSIDE * s[CORE] + f, 2 * FSIDE), 0)
+    early = lambda f, s: (0, lax.min(f, FSIDE - 1))
+    late = lambda f, s: (0, lax.max(f - FSIDE, 0))
+    return pl.pallas_call(
+        feed_kernel,
+        grid_spec=pltpu.PrefetchScalarGridSpec(
+            num_scalar_prefetch=1,
+            grid=(FF // FSTEP,),
+            in_specs=[
+                held((ROWS, WIDTH)),
+                held((ROWS, WIDTH)),
+                spec((WIDTH, FSTEP), early),
+                spec((WIDTH, FSTEP), late),
+                spec((FSTEP, SIDE), units),
+                spec((FSTEP, SIDE), units),
+            ],
+            out_specs=[
+                held((ROWS, WIDTH)),
+                held((ROWS, WIDTH)),
+                spec((FSTEP, SIDE), units),
+                spec((FSTEP, SIDE), units),
+                spec((WIDTH, FSTEP), early),
+                spec((WIDTH, FSTEP), late),
+            ],
+            scratch_shapes=[
+                pltpu.VMEM((FSTEP, WIDTH), BF16),
+                pltpu.VMEM((ROWS, FSTEP), BF16),
+                pltpu.VMEM((ROWS, FSTEP), BF16),
+            ],
+        ),
+        out_shape=[
+            jax.ShapeDtypeStruct((ROWS, WIDTH), F32),
+            jax.ShapeDtypeStruct((ROWS, WIDTH), F32),
+            jax.ShapeDtypeStruct((FF, SIDE), BF16),
+            jax.ShapeDtypeStruct((FF, SIDE), BF16),
+            jax.ShapeDtypeStruct((WIDTH, FF // 2), BF16),
+            jax.ShapeDtypeStruct((WIDTH, FF // 2), BF16),
+        ],
+        compiler_params=params(56),
+        cost_estimate=pl.CostEstimate(
+            flops=12 * ROWS * WIDTH * FF, bytes_accessed=12 * ROWS * WIDTH + 8 * WIDTH * FF, transcendentals=ROWS * FF
+        ),
+        name="feed",
+    )(sc, normed.reshape(ROWS, WIDTH), cotangent.reshape(ROWS, WIDTH), *up, *down)
+
+
+def post_kernel(sc, resid, branch, back, cot, mixed, wo_own, wo_far, gain, *refs):
+    (out_own, out_far, res_own, res_far, heads, d_out_own, d_out_far, d_gain, weight, total, spread) = refs
+    step = pl.program_id(0)
+    whole_weight(sc, step, wo_own, wo_far, weight)
+    core = sc[CORE]
+    shape, slab = (256, WIDTH), (4, HALF, WIDTH)
+    valid = row_valid(sc, step)
+    res = resid[...].reshape(shape)
+    output = jnp.where(valid, res + branch[...].reshape(shape), 0.0).reshape(slab)
+    out_own[...] = output[:2]
+    out_far[...] = output[2:].astype(BF16)
+    scale = lax.rsqrt(jnp.mean(res * res, axis=-1, keepdims=True) + EPSILON)
+    unit = res * scale
+    two_grad = jnp.where(valid, back[...].reshape(shape), 0.0)
+    gained = two_grad * gain[...]
+    masked = cot[...].reshape(shape).astype(F32)
+    grad = masked + scale * (gained - unit * jnp.mean(gained * unit, axis=-1, keepdims=True))
+    low = grad.astype(BF16)
+    res_own[...] = grad.reshape(slab)[:2]
+    res_far[...] = low.reshape(slab)[2:]
+    gain_sum = jnp.sum(two_grad * unit, axis=0, keepdims=True)
+    out_sum = dot(mixed[...].reshape(shape), low, 0, 0)
+
+    @pl.when(step == 0)
+    def _():
+        d_gain[...] = gain_sum
+        total[...] = out_sum
+
+    @pl.when(step > 0)
+    def _():
+        d_gain[...] += gain_sum
+        total[...] += out_sum
+
+    spread[...] = dot(low, weight[...], 1, 1).astype(BF16).reshape(slab)
+    for pair in range(HEADS // 2):
+        lanes = slice(pair * 128, (pair + 1) * 128)
+        for side in range(2):
+            one, two = spread[2 * side, :, lanes], spread[2 * side + 1, :, lanes]
+            half = slice(side * 128, (side + 1) * 128)
+            heads[2 * pair, :, half] = jnp.concatenate([one[:, :HEAD], two[:, :HEAD]], axis=1)
+            heads[2 * pair + 1, :, half] = jnp.concatenate([one[:, HEAD:], two[:, HEAD:]], axis=1)
+
+    @pl.when(step == pl.num_programs(0) - 1)
+    def _():
+        weight[...] = total[...].astype(BF16)
+        d_out_own[...] = weight[:, pl.ds(pl.multiple_of(core * SIDE, 128), SIDE)]
+        d_out_far[...] = weight[:, pl.ds(pl.multiple_of((1 - core) * SIDE, 128), SIDE)]
+
+
+def run_post(sc, resid, branch, back, cotangent, mixed, wo, gain):
+    whole = (4, HROWS, WIDTH)
+    return pl.pallas_call(
+        post_kernel,
+        grid_spec=pltpu.PrefetchScalarGridSpec(
+            num_scalar_prefetch=1,
+            grid=(RUNS,),
+            in_specs=[slab_spec()] * 5 + [held((WIDTH, SIDE)), held((WIDTH, SIDE)), held((1, WIDTH))],
+            out_specs=[slab_spec(2)] * 4
+            + [heads_spec(), held((WIDTH, SIDE)), held((WIDTH, SIDE)), held((1, WIDTH))],
+            scratch_shapes=[
+                pltpu.VMEM((WIDTH, WIDTH), BF16),
+                pltpu.VMEM((WIDTH, WIDTH), F32),
+                pltpu.VMEM((4, HALF, WIDTH), BF16),
+            ],
+        ),
+        out_shape=[
+            jax.ShapeDtypeStruct((2, HROWS, WIDTH), F32),
+            jax.ShapeDtypeStruct((2, HROWS, WIDTH), BF16),
+            jax.ShapeDtypeStruct((2, HROWS, WIDTH), F32),
+            jax.ShapeDtypeStruct((2, HROWS, WIDTH), BF16),
+            jax.ShapeDtypeStruct((HEADS, HROWS, 4 * HEAD), BF16),
+            jax.ShapeDtypeStruct((WIDTH, SIDE), BF16),
+            jax.ShapeDtypeStruct((WIDTH, SIDE), BF16),
+            jax.ShapeDtypeStruct((1, WIDTH), F32),
+        ],
+        compiler_params=params(40),
+        cost_estimate=pl.CostEstimate(
+            flops=4 * ROWS * WIDTH * WIDTH, bytes_accessed=28 * ROWS * WIDTH, transcendentals=0
+        ),
+        name="post",
+    )(sc, resid, branch.reshape(whole), back.reshape(whole), cotangent, mixed, *wo, gain)
+
+
+def unmix_kernel(carried, sc, *refs):
+    shards, (v_own, v_far, grad_heads, mean, inverse, *rest) = refs[:8], refs[8:]
+    rest = rest[2:] if carried else rest
+    outs, (own, far, raw, grads, sems, out_sems) = rest[:8], rest[8:]
+    place = sc[PLACE]
+    step = pl.program_id(0)
+
+    def leave(slot):
+        return [
+            pltpu.make_async_copy(
+                grads.at[slot, pl.ds(pl.multiple_of((place ^ rel) * SUBS * HALF, SUBS * HALF), SUBS * HALF)],
+                outs[4 * slot + rel],
+                out_sems.at[slot, rel],
+            )
+            for rel in range(4)
+        ]
+
+    slot = take_plane(place, shards, raw, sems)
+    column = lax.broadcasted_iota(jnp.int32, (1, LMAX), 1)
+    line = lax.broadcasted_iota(jnp.int32, (LMAX, 2 * HEAD), 0)
+    side = lax.broadcasted_iota(jnp.int32, (LMAX, 2 * HEAD), 1) // HEAD
+    for head in range(PHEADS):
+        weights = exponents(raw, slot, head)
+        low = (grad_heads[head].astype(F32) * inverse[head]).astype(BF16)
+        product = low.astype(F32) * mean[head]
+        score = dot(low, jnp.concatenate([v_own[head], v_far[head]], axis=1), 1, 1)
+        for item in range(4):
+            delta = jnp.sum(product[:, item * HEAD : (item + 1) * HEAD], axis=-1, keepdims=True)
+            score = score - delta * (column < sc[LENGTHS + item]).astype(F32)
+        score = score * weights.astype(F32)
+        grads[slot, head * HROWS : (head + 1) * HROWS] = score.astype(BF16)
+        back = dot(weights, low, 0, 0)
+        for target, first in ((own, 0), (far, 2)):
+            found = back[:, first * HEAD : (first + 2) * HEAD]
+            length = jnp.where(side == 0, sc[LENGTHS + first], sc[LENGTHS + first + 1])
+            target[head] = jnp.where(line < length, found, 0.0).astype(target.dtype)
+    for which in range(2):
+
+        @pl.when(step == which)
+        def _():
+            for copy in leave(which):
+                copy.start()
+            if which == 1:
+                for copy in leave(0) + leave(1):
+                    copy.wait()
+
+
+def run_unmix(sc, planes, shards, v_own, v_far, grad_heads, mean, inverse, carry):
+    carry = list(carry)
+    return pl.pallas_call(
+        partial(unmix_kernel, bool(carry)),
+        grid_spec=pltpu.PrefetchScalarGridSpec(
+            num_scalar_prefetch=1,
+            grid=(2,),
+            in_specs=in_hbm(8)
+            + [plane_spec(planes, LMAX, 2 * HEAD)] * 2
+            + [plane_spec(planes, HROWS, 4 * HEAD)] * 3
+            + in_hbm(len(carry)),
+            out_specs=in_hbm(8) + [plane_spec(planes, LMAX, 2 * HEAD)] * 2,
+            scratch_shapes=[
+                pltpu.VMEM((2, 4 * SUBS * HALF, LMAX), BF16),
+                pltpu.VMEM((2, 4 * SUBS * HALF, LMAX), BF16),
+                pltpu.SemaphoreType.DMA((2, 4)),
+                pltpu.SemaphoreType.DMA((2, 4)),
+            ],
+        ),
+        out_shape=[jax.ShapeDtypeStruct((SUBS * HALF, LMAX), BF16)] * 8
+        + [
+            jax.ShapeDtypeStruct((HEADS, LMAX, 2 * HEAD), F32),
+            jax.ShapeDtypeStruct((HEADS, LMAX, 2 * HEAD), BF16),
+        ],
+        input_output_aliases={14 + i: 8 + i for i in range(len(carry))},
+        compiler_params=params(56),
+        cost_estimate=pl.CostEstimate(
+            flops=2 * HEADS * HROWS * LMAX * 4 * HEAD,
+            bytes_accessed=HEADS * (2 * HROWS * LMAX + 5 * HROWS * 256 + 4 * LMAX * 256),
+            transcendentals=HEADS * HROWS * LMAX // 2,
+        ),
+        name="unmix",
+    )(sc, *shards, v_own, v_far, grad_heads, mean, inverse, *carry)
+
+
+def close_kernel(sc, tok, res_own, res_got, out_own, out_got, own, far, gain, w_own, w_far, *refs):
+    (output, tok_grad, d_value, d_gain, total, weight) = refs
+    step = pl.program_id(0)
+    whole_weight(sc, step, w_own, w_far, weight)
+    core = sc[CORE]
+    output[:, :, core] = out_own[...]
+    output[:, :, 1 - core] = out_got[...].astype(F32)
+    tok_grad[:, :, core] = res_own[...]
+    tok_grad[:, :, 1 - core] = res_got[...].astype(F32)
+    runs = tok.shape[1]
+    rows = runs * 128
+    for item in range(2):
+        lanes = slice(item * HEAD, (item + 1) * HEAD)
+        pieces = [
+            (own[head, :, lanes] + far[head, :, lanes].astype(F32)).astype(BF16) for head in range(HEADS)
+        ]
+        back = jnp.concatenate(pieces, axis=1)
+        x = tok[item].reshape(rows, WIDTH).astype(F32)
+        scale = lax.rsqrt(jnp.mean(x * x, axis=-1, keepdims=True) + EPSILON)
+        unit = x * scale
+        normed = (unit * gain[...]).astype(BF16)
+        normed_grad = dot(back, weight[...], 1, 1)
+        gained = normed_grad * gain[...]
+        update = scale * (gained - unit * jnp.mean(gained * unit, axis=-1, keepdims=True))
+        tok_grad[item] += update.reshape(runs, 2, HALF, WIDTH)
+        gain_sum = jnp.sum(normed_grad * unit, axis=0, keepdims=True)
+        value_sum = dot(normed, back, 0, 0)
+        if item == 0:
+            gain_total, value_total = gain_sum, value_sum
+        else:
+            gain_total, value_total = gain_total + gain_sum, value_total + value_sum
+
+    @pl.when(step == 0)
+    def _():
+        d_gain[...] = gain_total
+        total[...] = value_total
+
+    @pl.when(step > 0)
+    def _():
+        d_gain[...] += gain_total
+        total[...] += value_total
+
+    @pl.when(step == pl.num_programs(0) - 1)
+    def _():
+        low = total[...].astype(BF16)
+        d_value[0] = low[:, :SIDE]
+        d_value[1] = low[:, SIDE:]
+
+
+def run_close(sc, tokens, res_own, res_got, out_own, out_got, own, far, gain, w_own, w_far):
+    runs = 2
+    slab = (2, RUNS, 2, HALF, WIDTH)
+    half = (2, RUNS, HALF, WIDTH)
+    whole_spec = spec((2, runs, 2, HALF, WIDTH), lambda j, s: (0, j, 0, 0, 0))
+    half_spec = spec((2, runs, HALF, WIDTH), lambda j, s: (0, j, 0, 0))
+    back_spec = spec((HEADS, runs * 128, 2 * HEAD), lambda j, s: (0, j, 0))
+    return pl.pallas_call(
+        close_kernel,
+        grid_spec=pltpu.PrefetchScalarGridSpec(
+            num_scalar_prefetch=1,
+            grid=(RUNS // runs,),
+            in_specs=[whole_spec]
+            + [half_spec] * 4
+            + [back_spec, back_spec, held((1, WIDTH)), held((WIDTH, SIDE)), held((WIDTH, SIDE))],
+            out_specs=[whole_spec, whole_spec, held((2, WIDTH, SIDE)), held((1, WIDTH))],
+            scratch_shapes=[pltpu.VMEM((WIDTH, WIDTH), F32), pltpu.VMEM((WIDTH, WIDTH), BF16)],
+        ),
+        out_shape=[
+            jax.ShapeDtypeStruct(slab, F32),
+            jax.ShapeDtypeStruct(slab, F32),
+            jax.ShapeDtypeStruct((2, WIDTH, SIDE), BF16),
+            jax.ShapeDtypeStruct((1, WIDTH), F32),
+        ],
+        compiler_params=params(48),
+        cost_estimate=pl.CostEstimate(
+            flops=4 * 2 * LMAX * WIDTH * WIDTH, bytes_accessed=38 * LMAX * WIDTH, transcendentals=0
+        ),
+        name="close",
+    )(
+        sc,
+        tokens.reshape(slab),
+        *(x.reshape(half) for x in (res_own, res_got, out_own, out_got)),
+        own,
+        far,
+        gain,
+        w_own,
+        w_far,
+    )
+
+
+PACK_DOWN, PACK_UP, PACK_OUT, PACK = 0, 192, 384, 432
+SHARE = SUBS * HALF + 32
+
+
+def chip_of(sc, k, rel):
+    return plane_of(k, sc) * 4 + (sc[PLACE] ^ rel)
+
+
+def place_kernel(moves, sc, *refs):
+    pieces, targets, sems = refs[:16], refs[16:-1], refs[-1]
+    copies = []
+    for index, piece in enumerate(pieces):
+        chip = chip_of(sc, index // 4, index % 4)
+        for which, (start, count, lane, target, step, offset, column) in enumerate(moves):
+            rows = pl.ds(pl.multiple_of(chip * step + offset, 16), count)
+            copies.append(
+                pltpu.make_async_copy(
+                    piece.at[pl.ds(start, count), pl.ds(lane, SIDE)],
+                    targets[target].at[rows, pl.ds(column, SIDE)],
+                    sems.at[index, which],
+                )
+            )
+    for copy in copies:
+        copy.start()
+    for copy in copies:
+        copy.wait()
+
+
+def run_place(sc, pieces, moves, shapes):
+    return pl.pallas_call(
+        partial(place_kernel, moves),
+        grid_spec=pltpu.PrefetchScalarGridSpec(
+            num_scalar_prefetch=1,
+            grid=(1,),
+            in_specs=in_hbm(16),
+            out_specs=in_hbm(len(shapes)),
+            scratch_shapes=[pltpu.SemaphoreType.DMA((16, len(moves)))],
+        ),
+        out_shape=[jax.ShapeDtypeStruct(shape, BF16) for shape in shapes],
+        compiler_params=params(16),
+        cost_estimate=pl.CostEstimate(
+            flops=0, bytes_accessed=4 * sum(a * b for a, b in shapes), transcendentals=0
+        ),
+        name="place",
+    )(sc, *pieces)
+
+
+def place_values(sc, shares):
+    start = SUBS * HALF
+    moves = (
+        (start, 32, 0, 0, 48, 0, 0),
+        (start, 16, SIDE, 0, 48, 32, 0),
+        (start + 16, 16, SIDE, 1, 16, 0, 0),
+    )
+    return run_place(sc, shares, moves, [(WIDTH, SIDE), (256, SIDE)])
+
+
+def place_weights(sc, pieces):
+    moves = (
+        (PACK_DOWN, 192, 0, 0, 192, 0, 0),
+        *((PACK_UP + 48 * j, 48, 0, 1, 48, 0, j * SIDE) for j in range(4)),
+        (PACK_OUT, 48, 0, 2, 48, 0, 0),
+    )
+    return run_place(sc, pieces, moves, [(FF, SIDE), (WIDTH, FF // 2), (WIDTH, SIDE)])
+
+
+def collect_kernel(sc, down, down_got, up, up_got, out, out_got, packed):
+    both = lambda a, b: (a.astype(F32) + b.astype(F32)).astype(BF16)
+    packed[0, 0:192] = both(down[...], down_got[...])
+    for j in range(4):
+        lanes = slice(j * SIDE, (j + 1) * SIDE)
+        packed[0, 192 + 48 * j : 240 + 48 * j] = both(up[:, lanes], up_got[:, lanes])
+    packed[0, 384:432] = both(out[...], out_got[...])
+
+
+def run_collect(sc, down, down_got, up, up_got, out, out_got):
+    chip = lambda i, s: (chip_of(s, i // 4, i % 4), 0)
+    rows = lambda x: spec((x.shape[0] // 16, x.shape[1]), chip)
+    args = (down, down_got, up, up_got, out, out_got)
+    return pl.pallas_call(
+        collect_kernel,
+        grid_spec=pltpu.PrefetchScalarGridSpec(
+            num_scalar_prefetch=1,
+            grid=(16,),
+            in_specs=[rows(x) for x in args],
+            out_specs=spec((1, PACK, SIDE), lambda i, s: (i, 0, 0)),
+        ),
+        out_shape=jax.ShapeDtypeStruct((16, PACK, SIDE), BF16),
+        compiler_params=params(16),
+        cost_estimate=pl.CostEstimate(flops=0, bytes_accessed=3 * 16 * PACK * SIDE * 2, transcendentals=0),
+        name="collect",
+    )(sc, *args)
+
+
+DEVICES = 32
+TO_CORE, TO_X, TO_Y = 1, 2, 4
+
+
+def swap(x, bit):
+    return lax.ppermute(x, BOTH, [(d, d ^ bit) for d in range(DEVICES)])
+
+
+def ring(x, way=1):
+    return lax.ppermute(x, BOTH, [(d, (d + 8 * way) % DEVICES) for d in range(DEVICES)])
+
+
+def pick(x, index, axis=0):
+    return lax.dynamic_index_in_dim(x, index, axis, keepdims=False)
+
+
+def ordered(flag, one, two, axis=0, joined=jnp.stack):
+    return jnp.where(flag == 0, joined([one, two], axis), joined([two, one], axis))
+
+
+def add_low(one, two):
+    return (one.astype(F32) + two.astype(F32)).astype(BF16)
+
+
+STEPS = (
+    ((0, 0, 1), (0, 1, 0), (1, 0, 0)),
+    ((1, 0, 1), (0, 1, 1), (2, 0, 0)),
+    ((2, 0, 1), (1, 1, 0), (3, 0, 0)),
+    ((3, 0, 1), (2, 1, 0), (1, 1, 1)),
+    ((2, 1, 1), (3, 1, 1), (3, 1, 0)),
+)
+
+
+def gather16(own, works=(), made=()):
+    have = {(0, 0, 0): own}
+    for step, (by_x, by_y, by_z) in enumerate(STEPS):
+        got = {
+            by_z: ring(have[by_z[0] - 1, by_z[1], by_z[2]]),
+            by_x: swap(have[by_x[0], by_x[1], 0], TO_X),
+            by_y: swap(have[by_y[0], 0, by_y[2]], TO_Y),
+        }
+        if step < len(works):
+            made = works[step](made)
+        have, made = lax.optimization_barrier(({**have, **got}, made))
+    return [have[k, y, x] for k in range(4) for y in range(2) for x in range(2)], made
+
+
+def scatter16(shares, works=(), made=()):
+    have = {(k, y, x): shares[4 * k + 2 * y + x] for k in range(4) for y in range(2) for x in range(2)}
+    for step, (by_x, by_y, by_z) in enumerate(reversed(STEPS)):
+        got = [
+            ((by_z[0] - 1, by_z[1], by_z[2]), ring(have[by_z], -1)),
+            ((by_x[0], by_x[1], 0), swap(have[by_x], TO_X)),
+            ((by_y[0], 0, by_y[2]), swap(have[by_y], TO_Y)),
+        ]
+        for at in (by_x, by_y, by_z):
+            del have[at]
+        if step < len(works):
+            made = works[step](made)
+        values, have, made = lax.optimization_barrier(([value for _, value in got], have, made))
+        for at in dict.fromkeys(at for at, _ in got):
+            total = have[at].astype(F32)
+            for (target, _), value in zip(got, values):
+                if target == at:
+                    total = total + value.astype(F32)
+            have[at] = total if step == len(STEPS) - 1 else total.astype(BF16)
+    return have[0, 0, 0], made
+
+
+def after(x, *others):
+    return lax.optimization_barrier((x, others))[0]
+
+
+def chip_shards(tokens, lengths, rand_mix, w_value, w_out, w_up, w_down, gain_mix, gain_ffn, grad_out):
+    wide = lax.axis_index("wide")
+    core = lax.axis_index("narrow")
+    z, y, x = wide // 4, (wide // 2) % 2, wide % 2
+    other = lambda value: swap(value, TO_CORE)
+    side = partial(ordered, core, joined=jnp.concatenate)
+
+    gains = jnp.pad(jnp.concatenate([gain_mix, gain_ffn])[None], ((0, 7), (0, SIDE - 48)))
+    halves = [
+        jnp.concatenate(
+            [
+                w_value[:, c * SIDE : (c + 1) * SIDE],
+                gains,
+                w_down[:, c * SIDE : (c + 1) * SIDE],
+                *[w_up[:, (4 * c + j) * SIDE : (4 * c + j + 1) * SIDE] for j in range(4)],
+                w_out[:, c * SIDE : (c + 1) * SIDE],
+            ]
+        )
+        for c in range(2)
+    ]
+    both = jnp.stack(halves)
+    joined = ordered(core, pick(both, core), other(pick(both, 1 - core)))
+    part_of = lambda start, rows: joined[:, start : start + rows].reshape(2 * rows, SIDE)
+    up_rows = joined[:, 128:224].reshape(2, 4, 24, SIDE).transpose(1, 0, 2, 3).reshape(192, SIDE)
+    packed = jnp.concatenate([part_of(32, 96), up_rows, part_of(224, 24)])
+    first = jnp.concatenate([part_of(0, 24), part_of(24, 8)])
+    first = jnp.pad(jnp.concatenate([first[:32], first[32:]], axis=1), ((0, 0), (0, LMAX - WIDTH)))
+    rand = rand_mix.reshape(3, 2, HALF, LMAX)
+    blocks = side(pick(rand, core, 1), other(pick(rand, 1 - core, 1)), 0)
+    share = jnp.concatenate([blocks.reshape(SUBS * HALF, LMAX), first])
+    share, packed = lax.optimization_barrier((share, packed))
+
+    slab = (2, RUNS, 2, HALF, WIDTH)
+    tokens, grad_out = tokens.reshape(slab), grad_out.reshape(slab)
+
+    def from_other(_):
+        return other(lengths), other(pick(tokens, 1 - core, 2)), other(pick(grad_out, 1 - core, 2))
+
+    shares, (far_lengths, tokens_far, grad_far) = gather16(share, [from_other])
+    sc = jnp.concatenate([jnp.stack([core, z, wide % 4]).astype(jnp.int32), lengths, far_lengths])
+
+    def make_values(_):
+        value, gain_rows = place_values(sc, shares)
+        value_far = other(value)
+        gain_rows = gain_rows.reshape(16, 2, 8, SIDE)[:, :, 0]
+        gain_one = gain_rows[..., :24].reshape(1, WIDTH).astype(F32)
+        gain_two = gain_rows[..., 24:48].reshape(1, WIDTH).astype(F32)
+        v_own = run_values(sc, tokens.reshape(2, LMAX, WIDTH), gain_one, value, value_far)
+        return value, value_far, gain_one, gain_two, v_own
+
+    def share_values(made):
+        return *made, other(made[-1])
+
+    def mix_near(made):
+        return *made, run_mix(sc, (0, 1), shares[:8], made[-2], made[-1], ())
+
+    def mix_far(made):
+        *made, near = made
+        return *made, run_mix(sc, (2, 3), shares[8:], made[-2], made[-1], near)
+
+    pieces, made = gather16(after(packed, *shares[-3:]), [make_values, share_values, mix_near, mix_far])
+    value, value_far, gain_one, gain_two, v_own, v_far, (heads, mean, inverse) = made
+    down, up, out = place_weights(sc, pieces)
+    down_far, up_far, out_far = other(down), other(up), other(out)
+
+    mixed, resid, normed, masked = run_pre(
+        sc, tokens, tokens_far, grad_out, grad_far, heads, (out, out_far), gain_two
+    )
+    branch, back, down_own, down_far, up_own, up_far = run_feed(sc, normed, masked, (up, up_far), (down, down_far))
+    down_got, up_got = other(down_far), other(up_far)
+    out_own, out_far, res_own, res_far, grad_heads, d_out_own, d_out_far, d_gain_two = run_post(
+        sc, resid, branch, back, masked, mixed, (out, out_far), gain_two
+    )
+
+    packed = run_collect(sc, down_own, down_got, up_own, up_got, d_out_own, other(d_out_far))
+
+    def unmix_far(_):
+        return run_unmix(sc, (3, 2), shares[12:] + shares[8:12], v_own, v_far, grad_heads, mean, inverse, ())
+
+    def unmix_near(made):
+        *far, back_own, back_far = made
+        near = run_unmix(
+            sc, (1, 0), shares[4:8] + shares[:4], v_own, v_far, grad_heads, mean, inverse, (back_own, back_far)
+        )
+        return far, near
+
+    def exchange(made):
+        far, (*near, back_own, back_far) = made
+        return far, near, back_own, other(back_far), other(out_far), other(res_far)
+
+    big_sum, made = scatter16([packed[i] for i in range(16)], [unmix_far, unmix_near, exchange])
+    far, near, back_own, back_got, out_got, res_got = made
+    rand_grads = near[4:] + near[:4] + far[4:] + far[:4]
+
+    def finish(_):
+        output, tokens_grad, d_value, d_gain_one = run_close(
+            sc, tokens, res_own, res_got, out_own, out_got, back_own, back_got, gain_one, value, value_far
+        )
+        gain_pair = jnp.concatenate([d_gain_one, d_gain_two]).reshape(2, 16, 1, 48).astype(BF16)
+        gain_pair = jnp.pad(gain_pair, ((0, 0), (0, 0), (0, 15), (0, SIDE - 48)))
+        small = jnp.concatenate([d_value.reshape(2, 16, 48, SIDE), gain_pair], 2)
+        return output, tokens_grad, small, other(big_sum)
+
+    def small_core(made):
+        *kept, small, big_far = made
+        small = add_low(pick(small, core), other(pick(small, 1 - core))).reshape(4, 2, 2, 64, SIDE)
+        return *kept, big_far, small
+
+    def small_line(made):
+        *kept, small = made
+        return *kept, add_low(pick(small, x, 2), swap(pick(small, 1 - x, 2), TO_X))
+
+    def small_plane(made):
+        *kept, small = made
+        return *kept, add_low(pick(small, y, 1), swap(pick(small, 1 - y, 1), TO_Y))
+
+    def small_planes(made):
+        *kept, small = made
+        total = pick(small, z).astype(F32)
+        for k in range(1, PLANES):
+            total = total + ring(pick(small, lax.rem(z + PLANES - k, PLANES)), -k).astype(F32)
+        return *kept, total
+
+    rand_sum, made = scatter16(
+        after(rand_grads, big_sum), [finish, small_core, small_line, small_plane, small_planes]
+    )
+    output, tokens_grad, big_far, small_sum = made
+    small_far = other(small_sum)
+
+    rows_of = lambda value, rows: pick(value.reshape(-1, 2, rows, SIDE), core, 1)
+    mine = lambda own, far, rows: side(rows_of(own, rows)[0], rows_of(far, rows)[0], 1)
+    down_shard = mine(big_sum[PACK_DOWN:PACK_UP], big_far[PACK_DOWN:PACK_UP], 96)
+    up_side = lambda value: rows_of(value[PACK_UP:PACK_OUT], 24).transpose(1, 0, 2).reshape(24, 4 * SIDE)
+    up_shard = side(up_side(big_sum), up_side(big_far), 1)
+    outproj_shard = mine(big_sum[PACK_OUT:], big_far[PACK_OUT:], 24)
+    value_shard = mine(small_sum[:48], small_far[:48], 24)
+    gains_pair = ordered(core, small_sum[48, :48], small_far[48, :48])
+    gain_pair = pick(gains_pair.reshape(2, 2, 24), core, 1)
+
+    blocks = rand_sum.reshape(2, 3, HALF, LMAX)
+    rand_shard = ordered(core, pick(blocks, core), other(pick(blocks, 1 - core)), 1)
+
+    return (
+        output.reshape(2, LMAX, WIDTH),
+        tokens_grad.reshape(2, LMAX, WIDTH),
+        rand_shard.reshape(3 * 128, LMAX),
+        value_shard,
+        outproj_shard,
+        up_shard,
+        down_shard,
+        gain_pair[0],
+        gain_pair[1],
+    )
 
 
 def rms_norm(values, gain):
@@ -191,4 +1135,5 @@
         P(("wide", "narrow")),
         P(("wide", "narrow")),
     )
-    return jax.shard_map(shards, mesh=mesh, in_specs=in_specs, out_specs=out_specs, check_vma=False)
+    fits = dict(mesh.shape) == {"wide": 16, "narrow": 2}
+    return jax.shard_map(chip_shards if fits else shards, mesh=mesh, in_specs=in_specs, out_specs=out_specs, check_vma=False)

time: 1700 us -> 589 us (0.35)
  waiting for transfers between devices: 747 us -> 222 us
  matrix products: 397 us -> 0 us
  other arithmetic: 280 us -> 28.5 us
  Pallas kernels: 0 us -> 209 us
  local copies, waits for them, and re-layouts: 162 us -> 51.7 us
  blocking collectives: 83.9 us -> 0 us
  starting transfers between devices: 0.39 us -> 66.8 us
    reduce_scatter x5 -> x0, waiting for transfers between devices: 597 us -> none  [the longest x1 438 us: shards(): lax.psum_scatter(rand_flat, ('wide', 'narrow'), scatter_dimension=0, tile...]
    dot_general x84 -> x0, matrix products: 397 us -> none  [the longest x24 88.4 us: head_forward(): jnp.dot(attention.astype(jnp.bfloat16), value_head, preferred_element_typ...]
    ppermute x0 -> x85, waiting for transfers between devices: none -> 222 us  [the longest x62 154 us: swap(): return lax.ppermute(x, BOTH, [(d, d ^ bit) for d in range(DEVICES)])]
    pallas_call x0 -> x12, Pallas kernels: none -> 209 us  [the longest x1 83.9 us: run_feed(): pl.pallas_call(feed_kernel, grid_spec=pltpu.PrefetchScalarGridSpec(num_sc...]
    all_gather x5 -> x0, waiting for transfers between devices: 147 us -> none  [the longest x1 141 us: shards(): lax.all_gather(rand_mix, ('wide', 'narrow'), axis=0, tiled=True)]
    dynamic_update_slice x24 -> x0, other arithmetic: 99.8 us -> none  [shards(): lax.map(partial(head_backward, valid_table[item_index]), (rand_heads_back...]
    unnamed x2 -> x0, blocking collectives: 83.9 us -> none
    ppermute x0 -> x85, starting transfers between devices: none -> 66.8 us  [the longest x62 49.7 us: swap(): return lax.ppermute(x, BOTH, [(d, d ^ bit) for d in range(DEVICES)])]
  transfers between devices with their start and end apart: 10 -> 85, of which waited for: 5 -> 43; matrix products, arithmetic and copies ran while one was open for 46% -> 5% of each run, Pallas kernels for 0% -> 19%
where the time goes in v2:
time: 589 us; the launch traced here: 580 us
  waiting for transfers between devices  222 us (38%)
  Pallas kernels  209 us (35%)
  starting transfers between devices  66.8 us (11%)
  local copies, waits for them, and re-layouts  51.7 us (9%)
  other arithmetic  28.5 us (5%)
    ppermute x62, waiting for transfers between devices, swap(): return lax.ppermute(x, BOTH, [(d, d ^ bit) for d in range(DEVICES)])  154 us
    pallas_call x1, Pallas kernels, run_feed(): pl.pallas_call(feed_kernel, grid_spec=pltpu.PrefetchScalarGridSpec(num_sc...  83.9 us
    ppermute x23, waiting for transfers between devices, ring(): lax.ppermute(x, BOTH, [(d, (d + 8 * way) % DEVICES) for d in range(DEVICE...  68.5 us
    ppermute x62, starting transfers between devices, swap(): return lax.ppermute(x, BOTH, [(d, d ^ bit) for d in range(DEVICES)])  49.7 us
    unnamed x170, local copies, waits for them, and re-layouts  40.2 us
    pallas_call x2, Pallas kernels, run_unmix(): pl.pallas_call(partial(unmix_kernel, bool(carry)), grid_spec=pltpu.Prefet...  37.4 us
    pallas_call x1, Pallas kernels, run_post(): pl.pallas_call(post_kernel, grid_spec=pltpu.PrefetchScalarGridSpec(num_sc...  20.6 us
    convert_element_type x18, other arithmetic, scatter16(): have[at] = total if step == len(STEPS) - 1 else total.astype(BF16)  18.6 us
  transfers between devices with their start and end apart: 85, of which 43 were waited for; matrix products, arithmetic and copies ran while one was open for 5% of the time, Pallas kernels for 19%

profile of v2, /device:TPU:0, one launch (start us, length us, event | category | flops | bytes accessed | tf_op | source)
XLA Modules:
  0.0 580.0 jit_solution(831623802366130765)
XLA Ops:
  25.3 15.1 %collective-permute-done.2.refs_1_.refs_5_ = bf16[416,1024]{1,0:T(8,128)(2,1)S(1)} collective-permute-done((bf16[416,1024]{1,0:T(8,128)(2,1)S(1)}, bf16[416,1024]{1,0:T(8,128)(2,1)S(1)}, u32[]{:S(2)}, u32[]{:S(2)}) %collective-permute-start.2) | collective-permute-done | bytes 852000 | tf_op jit(solution)/shard_map/ppermute | solution.py:737
  47.4 17.0 %collective-permute-done.8.refs_3_.refs_7_ = bf16[416,1024]{1,0:T(8,128)(2,1)S(1)} collective-permute-done((bf16[416,1024]{1,0:T(8,128)(2,1)S(1)}, bf16[416,1024]{1,0:T(8,128)(2,1)S(1)}, u32[]{:S(2)}, u32[]{:S(2)}) %collective-permute-start.8) | collective-permute-done | bytes 852000 | tf_op jit(solution)/shard_map/ppermute | solution.py:737
  71.5 14.5 %collective-permute-done.11.refs_6_.refs_2_ = bf16[416,1024]{1,0:T(8,128)(2,1)S(1)} collective-permute-done((bf16[416,1024]{1,0:T(8,128)(2,1)S(1)}, bf16[416,1024]{1,0:T(8,128)(2,1)S(1)}, u32[]{:S(2)}, u32[]{:S(2)}) %collective-permute-start.11) | collective-permute-done | bytes 852000 | tf_op jit(solution)/shard_map/ppermute | solution.py:737
  95.1 14.0 %collective-permute-done.14.refs_7_.refs_3_ = bf16[416,1024]{1,0:T(8,128)(2,1)S(1)} collective-permute-done((bf16[416,1024]{1,0:T(8,128)(2,1)S(1)}, bf16[416,1024]{1,0:T(8,128)(2,1)S(1)}, u32[]{:S(2)}, u32[]{:S(2)}) %collective-permute-start.14) | collective-permute-done | bytes 852000 | tf_op jit(solution)/shard_map/ppermute | solution.py:741
  113.5 14.2 %collective-permute-done.17.refs_11_.refs_3_.refs_7_ = bf16[416,1024]{1,0:T(8,128)(2,1)} collective-permute-done((bf16[416,1024]{1,0:T(8,128)(2,1)}, bf16[416,1024]{1,0:T(8,128)(2,1)}, u32[]{:S(2)}, u32[]{:S(2)}) %collective-permute-start.17) | collective-permute-done | bytes 852000 | tf_op jit(solution)/shard_map/ppermute | solution.py:737
  140.9 7.8 %place.2 = (bf16[768,384]{1,0:T(8,128)(2,1)}, bf16[256,384]{1,0:T(8,128)(2,1)S(1)}) custom-call(s32[7]{0:T(128)S(1)} %concatenate.72.sc, bf16[416,1024]{1,0:T(8,128)(2,1)S(1)} %copy-done.3, bf16[416,1024]{1,0:T(8,128)(2,1)S(1)} %copy-done.6, bf16[416,1024]{1,0:T(8,128)(2,1)S(1)} %copy-done.9, bf16[416,1024]{1,0:T(8,128)(2,1)S(1)} %copy-done.15, ...), custom_call_target="tpu_custom_call" | custom-call | bytes 1572864 | tf_op jit(solution)/shard_map/place/pallas_call | solution.py:667
  151.6 6.7 %values.1.refs_8_ = bf16[12,1024,128]{2,1,0:T(8,128)(2,1)S(1)} custom-call(s32[7]{0:T(128)S(1)} %concatenate.72.sc, bf16[2,1024,768]{2,1,0:T(8,128)(2,1)S(1)} %copy-done.1, f32[1,768]{1,0:T(1,128)S(1)} %reshape.228.gain, bf16[768,384]{1,0:T(8,128)(2,1)} %get-tuple-element.798.w_own, bf16[768,384]{1,0:T(8,128)(2,1)} %collective-permute-done.23.w_far), custom_call_target="tpu_custom_call" | custom-call | flops 2415919104 | bytes 6291456 | tf_op jit(solution)/shard_map/values/pallas_call | solution.py:79
  164.5 8.6 %collective-permute-done.24.refs_3_ = bf16[432,384]{1,0:T(8,128)(2,1)S(1)} collective-permute-done((bf16[432,384]{1,0:T(8,128)(2,1)}, bf16[432,384]{1,0:T(8,128)(2,1)S(1)}, u32[]{:S(2)}, u32[]{:S(2)}) %collective-permute-start.24) | collective-permute-done | bytes 331808 | tf_op jit(solution)/shard_map/ppermute | solution.py:737
  179.3 8.1 %mix.2 = (bf16[12,512,256]{2,1,0:T(8,128)(2,1)}, f32[12,512,256]{2,1,0:T(8,128)}, f32[12,512,256]{2,1,0:T(8,128)}) custom-call(s32[7]{0:T(128)S(1)} %concatenate.72.sc, bf16[416,1024]{1,0:T(8,128)(2,1)S(1)} %copy-done.4, bf16[416,1024]{1,0:T(8,128)(2,1)S(1)} %copy-done.7, bf16[416,1024]{1,0:T(8,128)(2,1)S(1)} %copy-done.10, ...), custom_call_target="tpu_custom_call" | custom-call | flops 3221225472 | bytes 14155776 | tf_op jit(solution)/shard_map/mix/pallas_call | solution.py:190
  192.8 9.3 %mix.3 = (bf16[12,512,256]{2,1,0:T(8,128)(2,1)}, f32[12,512,256]{2,1,0:T(8,128)}, f32[12,512,256]{2,1,0:T(8,128)}) custom-call(s32[7]{0:T(128)S(1)} %concatenate.72.sc, bf16[416,1024]{1,0:T(8,128)(2,1)S(1)} %copy-done.27, bf16[416,1024]{1,0:T(8,128)(2,1)S(1)} %copy-done.30, ...), custom_call_target="tpu_custom_call", output_to_operand_aliasing={{0}: (11, {}), {1}: (12, {}), {2}: (13, {})} | custom-call | flops 3221225472 | bytes 14155776 | tf_op jit(solution)/shard_map/mix/pallas_call | solution.py:190
  212.4 5.5 place.3
  218.7 8.2 %collective-permute-done.37.wo_far = bf16[768,384]{1,0:T(8,128)(2,1)S(1)} collective-permute-done((bf16[768,384]{1,0:T(8,128)(2,1)S(1)}, bf16[768,384]{1,0:T(8,128)(2,1)S(1)}, u32[]{:S(2)}, u32[]{:S(2)}) %collective-permute-start.37) | collective-permute-done | bytes 589856 | tf_op jit(solution)/shard_map/ppermute | solution.py:737
  226.8 11.2 %pre.1 = (bf16[4,512,768]{2,1,0:T(8,128)(2,1)S(1)}, f32[4,512,768]{2,1,0:T(8,128)}, bf16[4,512,768]{2,1,0:T(8,128)(2,1)S(1)}, bf16[4,512,768]{2,1,0:T(8,128)(2,1)S(1)}) custom-call(s32[7]{0:T(128)S(1)} %concatenate.72.sc, bf16[2,8,2,64,768]{4,3,2,1,0:T(8,128)(2,1)S(1)} %bitcast.152, bf16[2,8,64,768]{3,2,1,0:T(8,128)(2,1)} %collective-permute-done.6.tok_far, ...), custom_call_target="tpu_custom_call" | custom-call | flops 2415919104 | bytes 25165824 | tf_op jit(solution)/shard_map/pre/pallas_call | solution.py:260
  245.3 83.9 %feed.1 = (f32[2048,768]{1,0:T(8,128)}, f32[2048,768]{1,0:T(8,128)}, bf16[3072,384]{1,0:T(8,128)(2,1)}, bf16[3072,384]{1,0:T(8,128)(2,1)}, bf16[768,1536]{1,0:T(8,128)(2,1)}, /*index=5*/bf16[768,1536]{1,0:T(8,128)(2,1)}) custom-call(s32[7]{0:T(128)} %copy-done.48, bf16[2048,768]{1,0:T(8,128)(2,1)} %bitcast.162, bf16[2048,768]{1,0:T(8,128)(2,1)} %bitcast.155, ...), custom_call_target="tpu_custom_call" | custom-call | flops 57982058496 | bytes 37748736 | tf_op jit(solution)/shard_map/feed/pallas_call | solution.py:340
  329.8 20.6 %post.1 = (f32[2,512,768]{2,1,0:T(8,128)S(1)}, bf16[2,512,768]{2,1,0:T(8,128)(2,1)S(1)}, f32[2,512,768]{2,1,0:T(8,128)S(1)}, bf16[2,512,768]{2,1,0:T(8,128)(2,1)...) custom-call(s32[7]{0:T(128)S(1)} %copy-done.49, ...), custom_call_target="tpu_custom_call" | custom-call | flops 4831838208 | bytes 44040192 | tf_op jit(solution)/shard_map/post/pallas_call | solution.py:434
  360.3 18.6 %unmix.2 = (bf16[384,1024]{1,0:T(8,128)(2,1)}, bf16[384,1024]{1,0:T(8,128)(2,1)}, bf16[384,1024]{1,0:T(8,128)(2,1)}, bf16[384,1024]{1,0:T(8,128)(2,1)}, bf16[384...) custom-call(s32[7]{0:T(128)} %copy-done.48, ...), custom_call_target="tpu_custom_call" | custom-call | flops 3221225472 | bytes 33030144 | tf_op jit(solution)/shard_map/unmix/pallas_call | solution.py:515
  383.6 18.8 %unmix.3 = (bf16[384,1024]{1,0:T(8,128)(2,1)}, bf16[384,1024]{1,0:T(8,128)(2,1)}, bf16[384,1024]{1,0:T(8,128)(2,1)}, bf16[384,1024]{1,0:T(8,128)(2,1)}, bf16[384...) custom-call(s32[7]{0:T(128)} %copy-done.48, ...), custom_call_target="tpu_custom_call", output_to_operand_aliasing={{8}: (14, {}), {9}: (15, {})} | custom-call | flops 3221225472 | bytes 33030144 | tf_op jit(solution)/shard_map/unmix/pallas_call | solution.py:515
  415.9 5.3 collective-permute-done.51
  423.9 6.8 %collective-permute-done.55 = bf16[432,384]{1,0:T(8,128)(2,1)S(1)} collective-permute-done((bf16[432,384]{1,0:T(8,128)(2,1)S(1)}, bf16[432,384]{1,0:T(8,128)(2,1)S(1)}, u32[]{:S(2)}, u32[]{:S(2)}) %collective-permute-start.55) | collective-permute-done | bytes 331808 | tf_op jit(solution)/shard_map/ppermute | solution.py:741
  445.4 15.8 %close.1 = (f32[2,8,2,64,768]{4,3,2,1,0:T(8,128)}, f32[2,8,2,64,768]{4,3,2,1,0:T(8,128)}, bf16[2,768,384]{2,1,0:T(8,128)(2,1)S(1)}, f32[1,768]{1,0:T(1,128)S(1)}) custom-call(s32[7]{0:T(128)S(1)} %copy-done.50, bf16[2,8,2,64,768]{4,3,2,1,0:T(8,128)(2,1)} %bitcast.150, f32[2,8,64,768]{3,2,1,0:T(8,128)} %bitcast.157, bf16[2,8,64,768]{3,2,1,0:T(8,128)(2,1)S(1)} %bitcast.159, ...), custom_call_target="tpu_custom_call" | custom-call | flops 4831838208 | bytes 29884416 | tf_op jit(solution)/shard_map/close/pallas_call | solution.py:604
  472.0 10.2 %collective-permute-done.65 = bf16[384,1024]{1,0:T(8,128)(2,1)} collective-permute-done((bf16[384,1024]{1,0:T(8,128)(2,1)}, bf16[384,1024]{1,0:T(8,128)(2,1)}, u32[]{:S(2)}, u32[]{:S(2)}) %collective-permute-start.65) | collective-permute-done | bytes 786464 | tf_op jit(solution)/shard_map/ppermute | solution.py:741
  499.3 21.3 %collective-permute-done.72 = bf16[4,2,64,384]{3,2,1,0:T(8,128)(2,1)S(1)} collective-permute-done((bf16[4,2,64,384]{3,2,1,0:T(8,128)(2,1)S(1)}, bf16[4,2,64,384]{3,2,1,0:T(8,128)(2,1)S(1)}, u32[]{:S(2)}, u32[]{:S(2)}) %collective-permute-start.72) | collective-permute-done | bytes 393248 | tf_op jit(solution)/shard_map/ppermute | solution.py:737
  528.5 18.1 %collective-permute-done.76 = bf16[4,64,384]{2,1,0:T(8,128)(2,1)S(1)} collective-permute-done((bf16[4,64,384]{2,1,0:T(8,128)(2,1)S(1)}, bf16[4,64,384]{2,1,0:T(8,128)(2,1)S(1)}, u32[]{:S(2)}, u32[]{:S(2)}) %collective-permute-start.76) | collective-permute-done | bytes 196640 | tf_op jit(solution)/shard_map/ppermute | solution.py:737
  555.4 11.8 %collective-permute-done.82 = bf16[64,384]{1,0:T(8,128)(2,1)S(1)} collective-permute-done((bf16[64,384]{1,0:T(8,128)(2,1)S(1)}, bf16[64,384]{1,0:T(8,128)(2,1)S(1)}, u32[]{:S(2)}, u32[]{:S(2)}) %collective-permute-start.82) | collective-permute-done | bytes 49184 | tf_op jit(solution)/shard_map/ppermute | solution.py:741
  (408 shorter events, 206.2 us)
Async XLA Ops:
  13.9 31.1 %collective-permute-start.6 = (bf16[2,8,64,768]{3,2,1,0:T(8,128)(2,1)}, bf16[2,8,64,768]{3,2,1,0:T(8,128)(2,1)}, u32[]{:S(2)}, u32[]{:S(2)}) collective-permute-start(bf16[2,8,64,768]{3,2,1,0:T(8,128)(2,1)} %dynamic-slice_bitcast_fusion.1), channel_id=1, source_target_pairs={{0,1},{1,0},{2,3},{3,2},{4,5},{5,4},{6,7},{7,6},{8,9},{9,8},{10,11... | collective-permute-start | bytes 4718600 | tf_op jit(solution)/shard_map/ppermute | solution.py:737
  16.3 28.6 %collective-permute-start.7 = (bf16[2,8,64,768]{3,2,1,0:T(8,128)(2,1)}, bf16[2,8,64,768]{3,2,1,0:T(8,128)(2,1)}, u32[]{:S(2)}, u32[]{:S(2)}) collective-permute-start(bf16[2,8,64,768]{3,2,1,0:T(8,128)(2,1)} %dynamic-slice_bitcast_fusion), channel_id=1, source_target_pairs={{0,1},{1,0},{2,3},{3,2},{4,5},{5,4},{6,7},{7,6},{8,9},{9,8},{10,11... | collective-permute-start | bytes 4718600 | tf_op jit(solution)/shard_map/ppermute | solution.py:737
  18.2 22.1 %collective-permute-start.2 = (bf16[416,1024]{1,0:T(8,128)(2,1)S(1)}, bf16[416,1024]{1,0:T(8,128)(2,1)S(1)}, u32[]{:S(2)}, u32[]{:S(2)}) collective-permute-start(bf16[416,1024]{1,0:T(8,128)(2,1)S(1)} %pad_maximum_fusion.refs_0_.refs_4_), channel_id=1, source_target_pairs={{0,2},{1,3},{2,0},{3,1},{4,6},{5,7},{6,4},{7,5},{8,10},{9,11},{10,... | collective-permute-start | bytes 2555912 | tf_op jit(solution)/shard_map/ppermute | solution.py:737
  21.2 20.6 %collective-permute-start.3 = (bf16[416,1024]{1,0:T(8,128)(2,1)S(1)}, bf16[416,1024]{1,0:T(8,128)(2,1)S(1)}, u32[]{:S(2)}, u32[]{:S(2)}) collective-permute-start(bf16[416,1024]{1,0:T(8,128)(2,1)S(1)} %pad_maximum_fusion.refs_0_.refs_4_), channel_id=1, source_target_pairs={{0,4},{1,5},{2,6},{3,7},{4,0},{5,1},{6,2},{7,3},{8,12},{9,13},{10,... | collective-permute-start | bytes 2555912 | tf_op jit(solution)/shard_map/ppermute | solution.py:737
  22.8 22.2 %collective-permute-start.4 = (bf16[416,1024]{1,0:T(8,128)(2,1)S(1)}, bf16[416,1024]{1,0:T(8,128)(2,1)S(1)}, u32[]{:S(2)}, u32[]{:S(2)}) collective-permute-start(bf16[416,1024]{1,0:T(8,128)(2,1)S(1)} %pad_maximum_fusion.refs_0_.refs_4_), channel_id=1, source_target_pairs={{0,8},{1,9},{2,10},{3,11},{4,12},{5,13},{6,14},{7,15},{8,16},{9,17... | collective-permute-start | bytes 2555912 | tf_op jit(solution)/shard_map/ppermute | solution.py:741
  46.9 21.0 %collective-permute-start.10 = (bf16[416,1024]{1,0:T(8,128)(2,1)S(1)}, bf16[416,1024]{1,0:T(8,128)(2,1)S(1)}, u32[]{:S(2)}, u32[]{:S(2)}) collective-permute-start(bf16[416,1024]{1,0:T(8,128)(2,1)S(1)} %collective-permute-done.4.refs_4_.refs_0_), channel_id=1, source_target_pairs={{0,8},{1,9},{2,10},{3,11},{4,12},{5,13},{6,14},{7,15},{8,16},{9,17... | collective-permute-start | bytes 2555912 | tf_op jit(solution)/shard_map/ppermute | solution.py:741
  218.0 25.1 %collective-permute-start.38 = (bf16[768,1536]{1,0:T(8,128)(2,1)S(1)}, bf16[768,1536]{1,0:T(8,128)(2,1)S(1)}, u32[]{:S(2)}, u32[]{:S(2)}) collective-permute-start(bf16[768,1536]{1,0:T(8,128)(2,1)S(1)} %get-tuple-element.602.up_own), channel_id=1, source_target_pairs={{0,1},{1,0},{2,3},{3,2},{4,5},{5,4},{6,7},{7,6},{8,9},{9,8},{10,11... | collective-permute-start | bytes 7077896 | tf_op jit(solution)/shard_map/ppermute | solution.py:737
  218.1 25.1 %collective-permute-start.39 = (bf16[3072,384]{1,0:T(8,128)(2,1)S(1)}, bf16[3072,384]{1,0:T(8,128)(2,1)S(1)}, u32[]{:S(2)}, u32[]{:S(2)}) collective-permute-start(bf16[3072,384]{1,0:T(8,128)(2,1)S(1)} %get-tuple-element.603.dn_own), channel_id=1, source_target_pairs={{0,1},{1,0},{2,3},{3,2},{4,5},{5,4},{6,7},{7,6},{8,9},{9,8},{10,11... | collective-permute-start | bytes 7077896 | tf_op jit(solution)/shard_map/ppermute | solution.py:737
  329.2 23.3 %collective-permute-start.40 = (bf16[3072,384]{1,0:T(8,128)(2,1)}, bf16[3072,384]{1,0:T(8,128)(2,1)S(1)}, u32[]{:S(2)}, u32[]{:S(2)}) collective-permute-start(bf16[3072,384]{1,0:T(8,128)(2,1)} %get-tuple-element.605), channel_id=1, source_target_pairs={{0,1},{1,0},{2,3},{3,2},{4,5},{5,4},{6,7},{7,6},{8,9},{9,8},{10,11... | collective-permute-start | bytes 7077896 | tf_op jit(solution)/shard_map/ppermute | solution.py:737
  329.4 23.1 %collective-permute-start.41 = (bf16[768,1536]{1,0:T(8,128)(2,1)}, bf16[768,1536]{1,0:T(8,128)(2,1)S(1)}, u32[]{:S(2)}, u32[]{:S(2)}) collective-permute-start(bf16[768,1536]{1,0:T(8,128)(2,1)} %get-tuple-element.607), channel_id=1, source_target_pairs={{0,1},{1,0},{2,3},{3,2},{4,5},{5,4},{6,7},{7,6},{8,9},{9,8},{10,11... | collective-permute-start | bytes 7077896 | tf_op jit(solution)/shard_map/ppermute | solution.py:737
  356.4 22.5 %collective-permute-start.43 = (bf16[432,384]{1,0:T(8,128)(2,1)S(1)}, bf16[432,384]{1,0:T(8,128)(2,1)S(1)}, u32[]{:S(2)}, u32[]{:S(2)}) collective-permute-start(bf16[432,384]{1,0:T(8,128)(2,1)S(1)} %get-tuple-element.890), channel_id=1, source_target_pairs={{0,24},{1,25},{2,26},{3,27},{4,28},{5,29},{6,30},{7,31},{8,0},{9,1... | collective-permute-start | bytes 995336 | tf_op jit(solution)/shard_map/ppermute | solution.py:741
  358.5 20.4 %collective-permute-start.44 = (bf16[432,384]{1,0:T(8,128)(2,1)S(1)}, bf16[432,384]{1,0:T(8,128)(2,1)S(1)}, u32[]{:S(2)}, u32[]{:S(2)}) collective-permute-start(bf16[432,384]{1,0:T(8,128)(2,1)S(1)} %get-tuple-element.889), channel_id=1, source_target_pairs={{0,2},{1,3},{2,0},{3,1},{4,6},{5,7},{6,4},{7,5},{8,10},{9,11},{10,... | collective-permute-start | bytes 995336 | tf_op jit(solution)/shard_map/ppermute | solution.py:737
  378.9 23.5 %collective-permute-start.46 = (bf16[432,384]{1,0:T(8,128)(2,1)S(1)}, bf16[432,384]{1,0:T(8,128)(2,1)S(1)}, u32[]{:S(2)}, u32[]{:S(2)}) collective-permute-start(bf16[432,384]{1,0:T(8,128)(2,1)S(1)} %get-tuple-element.629), channel_id=1, source_target_pairs={{0,24},{1,25},{2,26},{3,27},{4,28},{5,29},{6,30},{7,31},{8,0},{9,1... | collective-permute-start | bytes 995336 | tf_op jit(solution)/shard_map/ppermute | solution.py:741
  381.0 21.4 %collective-permute-start.47 = (bf16[432,384]{1,0:T(8,128)(2,1)S(1)}, bf16[432,384]{1,0:T(8,128)(2,1)S(1)}, u32[]{:S(2)}, u32[]{:S(2)}) collective-permute-start(bf16[432,384]{1,0:T(8,128)(2,1)S(1)} %add_convert_fusion.17), channel_id=1, source_target_pairs={{0,2},{1,3},{2,0},{3,1},{4,6},{5,7},{6,4},{7,5},{8,10},{9,11},{10,... | collective-permute-start | bytes 995336 | tf_op jit(solution)/shard_map/ppermute | solution.py:737
  461.7 20.5 %collective-permute-start.65 = (bf16[384,1024]{1,0:T(8,128)(2,1)}, bf16[384,1024]{1,0:T(8,128)(2,1)}, u32[]{:S(2)}, u32[]{:S(2)}) collective-permute-start(bf16[384,1024]{1,0:T(8,128)(2,1)} %get-tuple-element.805), channel_id=1, source_target_pairs={{0,24},{1,25},{2,26},{3,27},{4,28},{5,29},{6,30},{7,31},{8,0},{9,1... | collective-permute-start | bytes 2359304 | tf_op jit(solution)/shard_map/ppermute | solution.py:741
  492.6 28.1 %collective-permute-start.69 = (bf16[384,1024]{1,0:T(8,128)(2,1)S(1)}, bf16[384,1024]{1,0:T(8,128)(2,1)S(1)}, u32[]{:S(2)}, u32[]{:S(2)}) collective-permute-start(bf16[384,1024]{1,0:T(8,128)(2,1)S(1)} %add_convert_fusion.6), channel_id=1, source_target_pairs={{0,24},{1,25},{2,26},{3,27},{4,28},{5,29},{6,30},{7,31},{8,0},{9,1... | collective-permute-start | bytes 2359304 | tf_op jit(solution)/shard_map/ppermute | solution.py:741
  493.2 27.4 %collective-permute-start.70 = (bf16[384,1024]{1,0:T(8,128)(2,1)S(1)}, bf16[384,1024]{1,0:T(8,128)(2,1)S(1)}, u32[]{:S(2)}, u32[]{:S(2)}) collective-permute-start(bf16[384,1024]{1,0:T(8,128)(2,1)S(1)} %copy-done.78), channel_id=1, source_target_pairs={{0,2},{1,3},{2,0},{3,1},{4,6},{5,7},{6,4},{7,5},{8,10},{9,11},{10,... | collective-permute-start | bytes 2359304 | tf_op jit(solution)/shard_map/ppermute | solution.py:737
  493.9 26.7 %collective-permute-start.71 = (bf16[384,1024]{1,0:T(8,128)(2,1)S(1)}, bf16[384,1024]{1,0:T(8,128)(2,1)S(1)}, u32[]{:S(2)}, u32[]{:S(2)}) collective-permute-start(bf16[384,1024]{1,0:T(8,128)(2,1)S(1)} %copy-done.79), channel_id=1, source_target_pairs={{0,4},{1,5},{2,6},{3,7},{4,0},{5,1},{6,2},{7,3},{8,12},{9,13},{10,... | collective-permute-start | bytes 2359304 | tf_op jit(solution)/shard_map/ppermute | solution.py:737
  495.3 25.2 %collective-permute-start.72 = (bf16[4,2,64,384]{3,2,1,0:T(8,128)(2,1)S(1)}, bf16[4,2,64,384]{3,2,1,0:T(8,128)(2,1)S(1)}, u32[]{:S(2)}, u32[]{:S(2)}) collective-permute-start(bf16[4,2,64,384]{3,2,1,0:T(8,128)(2,1)S(1)} %dynamic-slice_bitcast_fusion.5), channel_id=1, source_target_pairs={{0,2},{1,3},{2,0},{3,1},{4,6},{5,7},{6,4},{7,5},{8,10},{9,11},{10,... | collective-permute-start | bytes 1179656 | tf_op jit(solution)/shard_map/ppermute | solution.py:737
  522.0 24.6 %collective-permute-start.73 = (bf16[384,1024]{1,0:T(8,128)(2,1)}, bf16[384,1024]{1,0:T(8,128)(2,1)}, u32[]{:S(2)}, u32[]{:S(2)}) collective-permute-start(bf16[384,1024]{1,0:T(8,128)(2,1)} %add_convert_fusion.3), channel_id=1, source_target_pairs={{0,24},{1,25},{2,26},{3,27},{4,28},{5,29},{6,30},{7,31},{8,0},{9,1... | collective-permute-start | bytes 2359304 | tf_op jit(solution)/shard_map/ppermute | solution.py:741
  523.6 23.0 %collective-permute-start.74 = (bf16[384,1024]{1,0:T(8,128)(2,1)}, bf16[384,1024]{1,0:T(8,128)(2,1)}, u32[]{:S(2)}, u32[]{:S(2)}) collective-permute-start(bf16[384,1024]{1,0:T(8,128)(2,1)} %get-tuple-element.845), channel_id=1, source_target_pairs={{0,2},{1,3},{2,0},{3,1},{4,6},{5,7},{6,4},{7,5},{8,10},{9,11},{10,... | collective-permute-start | bytes 2359304 | tf_op jit(solution)/shard_map/ppermute | solution.py:737
  525.0 21.7 %collective-permute-start.75 = (bf16[384,1024]{1,0:T(8,128)(2,1)S(1)}, bf16[384,1024]{1,0:T(8,128)(2,1)}, u32[]{:S(2)}, u32[]{:S(2)}) collective-permute-start(bf16[384,1024]{1,0:T(8,128)(2,1)S(1)} %add_convert_fusion.5), channel_id=1, source_target_pairs={{0,4},{1,5},{2,6},{3,7},{4,0},{5,1},{6,2},{7,3},{8,12},{9,13},{10,... | collective-permute-start | bytes 2359304 | tf_op jit(solution)/shard_map/ppermute | solution.py:737
  525.9 20.6 %collective-permute-start.76 = (bf16[4,64,384]{2,1,0:T(8,128)(2,1)S(1)}, bf16[4,64,384]{2,1,0:T(8,128)(2,1)S(1)}, u32[]{:S(2)}, u32[]{:S(2)}) collective-permute-start(bf16[4,64,384]{2,1,0:T(8,128)(2,1)S(1)} %dynamic-slice_bitcast_fusion.8), channel_id=1, source_target_pairs={{0,4},{1,5},{2,6},{3,7},{4,0},{5,1},{6,2},{7,3},{8,12},{9,13},{10,... | collective-permute-start | bytes 589832 | tf_op jit(solution)/shard_map/ppermute | solution.py:737
  548.6 22.7 %collective-permute-start.77 = (bf16[384,1024]{1,0:T(8,128)(2,1)S(1)}, bf16[384,1024]{1,0:T(8,128)(2,1)S(1)}, u32[]{:S(2)}, u32[]{:S(2)}) collective-permute-start(bf16[384,1024]{1,0:T(8,128)(2,1)S(1)} %add_convert_fusion.1), channel_id=1, source_target_pairs={{0,24},{1,25},{2,26},{3,27},{4,28},{5,29},{6,30},{7,31},{8,0},{9,1... | collective-permute-start | bytes 2359304 | tf_op jit(solution)/shard_map/ppermute | solution.py:741
  (141 other events, 1828.9 us)

commit v3 on v2

--- a/solution.py
+++ b/solution.py
@@ -26,7 +26,7 @@
 PLANES = 4
 PHEADS = HEADS // PLANES
 ROWS = 2 * LMAX
-FSTEP = 512
+FSTEP = 768
 FSIDE = FF // 2 // FSTEP
 TILE = 512
 SIDE = WIDTH // 2
@@ -109,16 +109,16 @@
     return lax.rem(sc[PLANE] + PLANES - k, PLANES)
 
 
-def plane_spec(planes, rows, lanes):
+def head_spec(planes, rows, lanes):
     def index(step, sc):
-        k = planes[0] + step * (planes[1] - planes[0])
-        return (plane_of(k, sc), 0, 0)
-
-    return spec((PHEADS, rows, lanes), index)
-
-
-def in_hbm(count):
-    return [pl.BlockSpec(memory_space=pltpu.HBM)] * count
+        k = planes[0] + step // PHEADS * (planes[1] - planes[0])
+        return (plane_of(k, sc) * PHEADS + step % PHEADS, 0, 0)
+
+    return spec((1, rows, lanes), index)
+
+
+def anywhere(count):
+    return [pl.BlockSpec(memory_space=pl.ANY)] * count
 
 
 def plane_fetch(place, shards, raw, sems, slot):
@@ -143,66 +143,61 @@
 
     for slot in range(2):
 
-        @pl.when(step == slot)
+        @pl.when(step == slot * PHEADS)
         def _():
             for copy in plane_fetch(place, shards, raw, sems, slot):
                 copy.wait()
 
-    return step
-
-
-def exponents(raw, slot, head):
-    return jnp.exp(raw[slot, head * HROWS : (head + 1) * HROWS].astype(F32)).astype(BF16)
-
-
-def mix_kernel(carried, sc, *refs):
-    shards, (v_own, v_far, *rest) = refs[:8], refs[8:]
-    mixed, mean, inverse, raw, mask, sems = rest[3:] if carried else rest
-
+    return step // PHEADS, pl.ds(pl.multiple_of(step % PHEADS * HROWS, HROWS), HROWS)
+
+
+def fill_mask(sc, mask):
     @pl.when(pl.program_id(0) == 0)
     def _():
         shape = (LMAX, 4 * HEAD)
         column = lax.broadcasted_iota(jnp.int32, shape, 0)
         mask[...] = (column < lane_lengths(sc, shape)).astype(F32).astype(BF16)
 
-    slot = take_plane(sc[PLACE], shards, raw, sems)
+
+def inverse_sums(sc, weights, mask):
     shape = (HROWS, 4 * HEAD)
     line = lax.broadcasted_iota(jnp.int32, shape, 0)
     position = 128 * (line // HALF) + HALF * sc[CORE] + line % HALF
-    valid = position < lane_lengths(sc, shape)
-    for head in range(PHEADS):
-        weights = exponents(raw, slot, head)
-        total = dot(weights, mask[...], 1, 0)
-        flip = jnp.where(valid, 1.0 / total, 0.0)
-        found = dot(weights, jnp.concatenate([v_own[head], v_far[head]], axis=1), 1, 0) * flip
-        inverse[head] = flip
-        mean[head] = found
-        mixed[head] = found.astype(BF16)
+    return jnp.where(position < lane_lengths(sc, shape), 1.0 / dot(weights, mask[...], 1, 0), 0.0)
+
+
+def mix_kernel(carried, sc, *refs):
+    shards, (v_own, v_far, *rest) = refs[:8], refs[8:]
+    mixed, mean, raw, mask, sems = rest[2:] if carried else rest
+    fill_mask(sc, mask)
+    slot, rows = take_plane(sc[PLACE], shards, raw, sems)
+    weights = jnp.exp(raw[slot, rows].astype(F32)).astype(BF16)
+    found = dot(weights, jnp.concatenate([v_own[0], v_far[0]], axis=1), 1, 0) * inverse_sums(sc, weights, mask)
+    mean[0] = found
+    mixed[0] = found.astype(BF16)
 
 
 def run_mix(sc, planes, shards, v_own, v_far, carry):
-    out_shape = [
-        jax.ShapeDtypeStruct((HEADS, HROWS, 4 * HEAD), BF16),
-        jax.ShapeDtypeStruct((HEADS, HROWS, 4 * HEAD), F32),
-        jax.ShapeDtypeStruct((HEADS, HROWS, 4 * HEAD), F32),
-    ]
     carry = list(carry)
     return pl.pallas_call(
         partial(mix_kernel, bool(carry)),
         grid_spec=pltpu.PrefetchScalarGridSpec(
             num_scalar_prefetch=1,
-            grid=(2,),
-            in_specs=in_hbm(8) + [plane_spec(planes, LMAX, 2 * HEAD)] * 2 + in_hbm(len(carry)),
-            out_specs=[plane_spec(planes, HROWS, 4 * HEAD)] * 3,
+            grid=(2 * PHEADS,),
+            in_specs=anywhere(8) + [head_spec(planes, LMAX, 2 * HEAD)] * 2 + anywhere(len(carry)),
+            out_specs=[head_spec(planes, HROWS, 4 * HEAD)] * 2,
             scratch_shapes=[
                 pltpu.VMEM((2, 4 * SUBS * HALF, LMAX), BF16),
                 pltpu.VMEM((LMAX, 4 * HEAD), BF16),
                 pltpu.SemaphoreType.DMA((2, 4)),
             ],
         ),
-        out_shape=out_shape,
+        out_shape=[
+            jax.ShapeDtypeStruct((HEADS, HROWS, 4 * HEAD), BF16),
+            jax.ShapeDtypeStruct((HEADS, HROWS, 4 * HEAD), F32),
+        ],
         input_output_aliases={11 + i: i for i in range(len(carry))},
-        compiler_params=params(48),
+        compiler_params=params(60),
         cost_estimate=pl.CostEstimate(
             flops=2 * HEADS * HROWS * LMAX * 4 * HEAD,
             bytes_accessed=HEADS * (HROWS * LMAX + 5 * HROWS * 256),
@@ -282,115 +277,202 @@
     )(sc, tokens, tokens_far, cotangent, cotangent_far, heads, *wo, gain)
 
 
-def feed_kernel(sc, normed, cot, up_own, up_far, dn_own, dn_far, *refs):
-    (branch, back, d_down_own, d_down_far, d_up_own, d_up_far, w_down, active, up_grad) = refs
+def own_lanes(sc):
+    return pl.ds(pl.multiple_of(sc[CORE] * SIDE, 128), SIDE)
+
+
+def far_lanes(sc):
+    return pl.ds(pl.multiple_of((1 - sc[CORE]) * SIDE, 128), SIDE)
+
+
+def unit_rows(f, sc):
+    return (lax.rem(FSIDE * sc[CORE] + f, 2 * FSIDE), 0)
+
+
+def unit_columns(f, sc):
+    return (0, lax.rem(FSIDE * sc[CORE] + f, 2 * FSIDE))
+
+
+def early(f, sc):
+    return (0, lax.min(f, FSIDE - 1))
+
+
+def late(f, sc):
+    return (0, lax.max(f - FSIDE, 0))
+
+
+def units_kernel(sc, normed, cot, up_own, up_far, dn_own, dn_far, active, up_grad, back, w_down):
     step = pl.program_id(0)
-    core = sc[CORE]
-    own_lanes = pl.ds(pl.multiple_of(core * SIDE, 128), SIDE)
-    far_lanes = pl.ds(pl.multiple_of((1 - core) * SIDE, 128), SIDE)
-    w_down[:, own_lanes] = dn_own[...]
-    w_down[:, far_lanes] = dn_far[...]
-
-    def units(up_w, d_up):
+    w_down[:, own_lanes(sc)] = dn_own[...]
+    w_down[:, far_lanes(sc)] = dn_far[...]
+
+    def units(up_w):
         for piece in range(ROWS // TILE):
             rows = slice(piece * TILE, (piece + 1) * TILE)
             up = dot(normed[rows], up_w[...], 1, 0)
             square = up * up
             bend = jnp.tanh(up * (0.7978845608028654 + (0.044715 * 0.7978845608028654) * square))
             share = 0.5 + 0.5 * bend
-            act = (up * share).astype(BF16)
-            active[rows] = act
-            slope = share + (0.5 * up) * (1.0 - bend * bend) * (
-                0.7978845608028654 + (3 * 0.044715 * 0.7978845608028654) * square
+            act = up * share
+            active[rows] = act.astype(BF16)
+            slope = share + act * (1.0 - share) * (
+                2 * 0.7978845608028654 + (6 * 0.044715 * 0.7978845608028654) * square
             )
             low = (dot(cot[rows], w_down[...], 1, 1) * slope).astype(BF16)
             up_grad[rows] = low
-            out = dot(act, w_down[...], 1, 0)
             two_grad = dot(low, up_w[...], 1, 1)
 
             @pl.when(step == 0)
             def _():
-                branch[rows] = out
                 back[rows] = two_grad
 
             @pl.when(step > 0)
             def _():
-                branch[rows] += out
                 back[rows] += two_grad
 
-        d_up[...] = dot(normed[...], up_grad[...], 0, 0).astype(BF16)
-
     @pl.when(step < FSIDE)
     def _():
-        units(up_own, d_up_own)
+        units(up_own)
 
     @pl.when(step >= FSIDE)
     def _():
-        units(up_far, d_up_far)
-
-    w_down[...] = dot(active[...], cot[...], 0, 0).astype(BF16)
-    d_down_own[...] = w_down[:, own_lanes]
-    d_down_far[...] = w_down[:, far_lanes]
-
-
-def run_feed(sc, normed, cotangent, up, down):
-    units = lambda f, s: (lax.rem(FSIDE * s[CORE] + f, 2 * FSIDE), 0)
-    early = lambda f, s: (0, lax.min(f, FSIDE - 1))
-    late = lambda f, s: (0, lax.max(f - FSIDE, 0))
+        units(up_far)
+
+
+def run_units(sc, normed, cotangent, up, down):
     return pl.pallas_call(
-        feed_kernel,
+        units_kernel,
         grid_spec=pltpu.PrefetchScalarGridSpec(
             num_scalar_prefetch=1,
-            grid=(FF // FSTEP,),
+            grid=(2 * FSIDE,),
             in_specs=[
                 held((ROWS, WIDTH)),
                 held((ROWS, WIDTH)),
                 spec((WIDTH, FSTEP), early),
                 spec((WIDTH, FSTEP), late),
-                spec((FSTEP, SIDE), units),
-                spec((FSTEP, SIDE), units),
+                spec((FSTEP, SIDE), unit_rows),
+                spec((FSTEP, SIDE), unit_rows),
             ],
-            out_specs=[
-                held((ROWS, WIDTH)),
-                held((ROWS, WIDTH)),
-                spec((FSTEP, SIDE), units),
-                spec((FSTEP, SIDE), units),
-                spec((WIDTH, FSTEP), early),
-                spec((WIDTH, FSTEP), late),
-            ],
-            scratch_shapes=[
-                pltpu.VMEM((FSTEP, WIDTH), BF16),
-                pltpu.VMEM((ROWS, FSTEP), BF16),
-                pltpu.VMEM((ROWS, FSTEP), BF16),
-            ],
+            out_specs=[spec((ROWS, FSTEP), unit_columns), spec((ROWS, FSTEP), unit_columns), held((ROWS, WIDTH))],
+            scratch_shapes=[pltpu.VMEM((FSTEP, WIDTH), BF16)],
         ),
         out_shape=[
+            jax.ShapeDtypeStruct((ROWS, FF), BF16),
+            jax.ShapeDtypeStruct((ROWS, FF), BF16),
             jax.ShapeDtypeStruct((ROWS, WIDTH), F32),
-            jax.ShapeDtypeStruct((ROWS, WIDTH), F32),
-            jax.ShapeDtypeStruct((FF, SIDE), BF16),
-            jax.ShapeDtypeStruct((FF, SIDE), BF16),
-            jax.ShapeDtypeStruct((WIDTH, FF // 2), BF16),
-            jax.ShapeDtypeStruct((WIDTH, FF // 2), BF16),
         ],
         compiler_params=params(56),
         cost_estimate=pl.CostEstimate(
-            flops=12 * ROWS * WIDTH * FF, bytes_accessed=12 * ROWS * WIDTH + 8 * WIDTH * FF, transcendentals=ROWS * FF
-        ),
-        name="feed",
+            flops=6 * ROWS * WIDTH * FF, bytes_accessed=8 * ROWS * WIDTH + 4 * ROWS * FF, transcendentals=ROWS * FF
+        ),
+        name="units",
     )(sc, normed.reshape(ROWS, WIDTH), cotangent.reshape(ROWS, WIDTH), *up, *down)
 
 
-def post_kernel(sc, resid, branch, back, cot, mixed, wo_own, wo_far, gain, *refs):
-    (out_own, out_far, res_own, res_far, heads, d_out_own, d_out_far, d_gain, weight, total, spread) = refs
+def down_grad_kernel(sc, active, cot, own, far, total):
+    total[...] = dot(active[...], cot[...], 0, 0).astype(BF16)
+    own[...] = total[:, own_lanes(sc)]
+    far[...] = total[:, far_lanes(sc)]
+
+
+def run_down_grad(sc, active, cotangent):
+    return pl.pallas_call(
+        down_grad_kernel,
+        grid_spec=pltpu.PrefetchScalarGridSpec(
+            num_scalar_prefetch=1,
+            grid=(FF // 512,),
+            in_specs=[spec((ROWS, 512), lambda f, s: (0, f)), held((ROWS, WIDTH))],
+            out_specs=[spec((512, SIDE), lambda f, s: (f, 0))] * 2,
+            scratch_shapes=[pltpu.VMEM((512, WIDTH), BF16)],
+        ),
+        out_shape=[jax.ShapeDtypeStruct((FF, SIDE), BF16)] * 2,
+        compiler_params=params(48),
+        cost_estimate=pl.CostEstimate(
+            flops=2 * ROWS * WIDTH * FF, bytes_accessed=2 * ROWS * (WIDTH + FF), transcendentals=0
+        ),
+        name="down_grad",
+    )(sc, active, cotangent.reshape(ROWS, WIDTH))
+
+
+def up_grad_kernel(sc, normed, up_grad, own, far):
+    total = dot(normed[...], up_grad[...], 0, 0).astype(BF16)
+
+    @pl.when(pl.program_id(0) < FSIDE)
+    def _():
+        own[...] = total
+
+    @pl.when(pl.program_id(0) >= FSIDE)
+    def _():
+        far[...] = total
+
+
+def run_up_grad(sc, normed, up_grad):
+    return pl.pallas_call(
+        up_grad_kernel,
+        grid_spec=pltpu.PrefetchScalarGridSpec(
+            num_scalar_prefetch=1,
+            grid=(2 * FSIDE,),
+            in_specs=[held((ROWS, WIDTH)), spec((ROWS, FSTEP), unit_columns)],
+            out_specs=[spec((WIDTH, FSTEP), early), spec((WIDTH, FSTEP), late)],
+        ),
+        out_shape=[jax.ShapeDtypeStruct((WIDTH, FF // 2), BF16)] * 2,
+        compiler_params=params(48),
+        cost_estimate=pl.CostEstimate(
+            flops=2 * ROWS * WIDTH * FF, bytes_accessed=2 * ROWS * (WIDTH + FF), transcendentals=0
+        ),
+        name="up_grad",
+    )(sc, normed.reshape(ROWS, WIDTH), up_grad)
+
+
+def out_kernel(sc, active, resid, dn_own, dn_far, own, far, w_down):
+    step = pl.program_id(0)
+
+    @pl.when(step == 0)
+    def _():
+        w_down[:, own_lanes(sc)] = dn_own[...]
+        w_down[:, far_lanes(sc)] = dn_far[...]
+
+    branch = dot(active[...].reshape(256, FF), w_down[...], 1, 0)
+    output = jnp.where(row_valid(sc, step), resid[...].reshape(256, WIDTH) + branch, 0.0)
+    output = output.reshape(4, HALF, WIDTH)
+    own[...] = output[:2]
+    far[...] = output[2:].astype(BF16)
+
+
+def run_out(sc, active, resid, down):
+    return pl.pallas_call(
+        out_kernel,
+        grid_spec=pltpu.PrefetchScalarGridSpec(
+            num_scalar_prefetch=1,
+            grid=(RUNS,),
+            in_specs=[
+                spec((4, HALF, FF), lambda r, s: (0, r, 0)),
+                slab_spec(),
+                held((FF, SIDE)),
+                held((FF, SIDE)),
+            ],
+            out_specs=[slab_spec(2)] * 2,
+            scratch_shapes=[pltpu.VMEM((FF, WIDTH), BF16)],
+        ),
+        out_shape=[
+            jax.ShapeDtypeStruct((2, HROWS, WIDTH), F32),
+            jax.ShapeDtypeStruct((2, HROWS, WIDTH), BF16),
+        ],
+        compiler_params=params(48),
+        cost_estimate=pl.CostEstimate(
+            flops=2 * ROWS * WIDTH * FF, bytes_accessed=ROWS * (2 * FF + 7 * WIDTH), transcendentals=0
+        ),
+        name="out",
+    )(sc, active.reshape(4, HROWS, FF), resid, *down)
+
+
+def post_kernel(sc, resid, back, cot, mixed, wo_own, wo_far, gain, *refs):
+    (res_own, res_far, heads, d_out_own, d_out_far, d_gain, weight, total, spread) = refs
     step = pl.program_id(0)
     whole_weight(sc, step, wo_own, wo_far, weight)
-    core = sc[CORE]
     shape, slab = (256, WIDTH), (4, HALF, WIDTH)
     valid = row_valid(sc, step)
     res = resid[...].reshape(shape)
-    output = jnp.where(valid, res + branch[...].reshape(shape), 0.0).reshape(slab)
-    out_own[...] = output[:2]
-    out_far[...] = output[2:].astype(BF16)
     scale = lax.rsqrt(jnp.mean(res * res, axis=-1, keepdims=True) + EPSILON)
     unit = res * scale
     two_grad = jnp.where(valid, back[...].reshape(shape), 0.0)
@@ -425,19 +507,19 @@
     @pl.when(step == pl.num_programs(0) - 1)
     def _():
         weight[...] = total[...].astype(BF16)
-        d_out_own[...] = weight[:, pl.ds(pl.multiple_of(core * SIDE, 128), SIDE)]
-        d_out_far[...] = weight[:, pl.ds(pl.multiple_of((1 - core) * SIDE, 128), SIDE)]
-
-
-def run_post(sc, resid, branch, back, cotangent, mixed, wo, gain):
+        d_out_own[...] = weight[:, own_lanes(sc)]
+        d_out_far[...] = weight[:, far_lanes(sc)]
+
+
+def run_post(sc, resid, back, cotangent, mixed, wo, gain):
     whole = (4, HROWS, WIDTH)
     return pl.pallas_call(
         post_kernel,
         grid_spec=pltpu.PrefetchScalarGridSpec(
             num_scalar_prefetch=1,
             grid=(RUNS,),
-            in_specs=[slab_spec()] * 5 + [held((WIDTH, SIDE)), held((WIDTH, SIDE)), held((1, WIDTH))],
-            out_specs=[slab_spec(2)] * 4
+            in_specs=[slab_spec()] * 4 + [held((WIDTH, SIDE)), held((WIDTH, SIDE)), held((1, WIDTH))],
+            out_specs=[slab_spec(2)] * 2
             + [heads_spec(), held((WIDTH, SIDE)), held((WIDTH, SIDE)), held((1, WIDTH))],
             scratch_shapes=[
                 pltpu.VMEM((WIDTH, WIDTH), BF16),
@@ -446,8 +528,6 @@
             ],
         ),
         out_shape=[
-            jax.ShapeDtypeStruct((2, HROWS, WIDTH), F32),
-            jax.ShapeDtypeStruct((2, HROWS, WIDTH), BF16),
             jax.ShapeDtypeStruct((2, HROWS, WIDTH), F32),
             jax.ShapeDtypeStruct((2, HROWS, WIDTH), BF16),
             jax.ShapeDtypeStruct((HEADS, HROWS, 4 * HEAD), BF16),
@@ -460,13 +540,13 @@
             flops=4 * ROWS * WIDTH * WIDTH, bytes_accessed=28 * ROWS * WIDTH, transcendentals=0
         ),
         name="post",
-    )(sc, resid, branch.reshape(whole), back.reshape(whole), cotangent, mixed, *wo, gain)
+    )(sc, resid, back.reshape(whole), cotangent, mixed, *wo, gain)
 
 
 def unmix_kernel(carried, sc, *refs):
-    shards, (v_own, v_far, grad_heads, mean, inverse, *rest) = refs[:8], refs[8:]
+    shards, (v_own, v_far, grad_heads, mean, *rest) = refs[:8], refs[8:]
     rest = rest[2:] if carried else rest
-    outs, (own, far, raw, grads, sems, out_sems) = rest[:8], rest[8:]
+    outs, (own, far, raw, grads, mask, sems, out_sems) = rest[:8], rest[8:]
     place = sc[PLACE]
     step = pl.program_id(0)
 
@@ -480,28 +560,23 @@
             for rel in range(4)
         ]
 
-    slot = take_plane(place, shards, raw, sems)
+    fill_mask(sc, mask)
+    slot, rows = take_plane(place, shards, raw, sems)
+    weights = jnp.exp(raw[slot, rows].astype(F32)).astype(BF16)
+    low = (grad_heads[0].astype(F32) * inverse_sums(sc, weights, mask)).astype(BF16)
+    product = low.astype(F32) * mean[0]
+    score = dot(low, jnp.concatenate([v_own[0], v_far[0]], axis=1), 1, 1)
     column = lax.broadcasted_iota(jnp.int32, (1, LMAX), 1)
-    line = lax.broadcasted_iota(jnp.int32, (LMAX, 2 * HEAD), 0)
-    side = lax.broadcasted_iota(jnp.int32, (LMAX, 2 * HEAD), 1) // HEAD
-    for head in range(PHEADS):
-        weights = exponents(raw, slot, head)
-        low = (grad_heads[head].astype(F32) * inverse[head]).astype(BF16)
-        product = low.astype(F32) * mean[head]
-        score = dot(low, jnp.concatenate([v_own[head], v_far[head]], axis=1), 1, 1)
-        for item in range(4):
-            delta = jnp.sum(product[:, item * HEAD : (item + 1) * HEAD], axis=-1, keepdims=True)
-            score = score - delta * (column < sc[LENGTHS + item]).astype(F32)
-        score = score * weights.astype(F32)
-        grads[slot, head * HROWS : (head + 1) * HROWS] = score.astype(BF16)
-        back = dot(weights, low, 0, 0)
-        for target, first in ((own, 0), (far, 2)):
-            found = back[:, first * HEAD : (first + 2) * HEAD]
-            length = jnp.where(side == 0, sc[LENGTHS + first], sc[LENGTHS + first + 1])
-            target[head] = jnp.where(line < length, found, 0.0).astype(target.dtype)
+    for item in range(4):
+        delta = jnp.sum(product[:, item * HEAD : (item + 1) * HEAD], axis=-1, keepdims=True)
+        score = score - delta * (column < sc[LENGTHS + item]).astype(F32)
+    grads[slot, rows] = (score * weights.astype(F32)).astype(BF16)
+    back = (dot(weights, low, 0, 0) * mask[...].astype(F32)).astype(BF16)
+    own[0] = back[:, : 2 * HEAD]
+    far[0] = back[:, 2 * HEAD :]
     for which in range(2):
 
-        @pl.when(step == which)
+        @pl.when(step == which * PHEADS + PHEADS - 1)
         def _():
             for copy in leave(which):
                 copy.start()
@@ -510,39 +585,37 @@
                     copy.wait()
 
 
-def run_unmix(sc, planes, shards, v_own, v_far, grad_heads, mean, inverse, carry):
+def run_unmix(sc, planes, shards, v_own, v_far, grad_heads, mean, carry):
     carry = list(carry)
     return pl.pallas_call(
         partial(unmix_kernel, bool(carry)),
         grid_spec=pltpu.PrefetchScalarGridSpec(
             num_scalar_prefetch=1,
-            grid=(2,),
-            in_specs=in_hbm(8)
-            + [plane_spec(planes, LMAX, 2 * HEAD)] * 2
-            + [plane_spec(planes, HROWS, 4 * HEAD)] * 3
-            + in_hbm(len(carry)),
-            out_specs=in_hbm(8) + [plane_spec(planes, LMAX, 2 * HEAD)] * 2,
+            grid=(2 * PHEADS,),
+            in_specs=anywhere(8)
+            + [head_spec(planes, LMAX, 2 * HEAD)] * 2
+            + [head_spec(planes, HROWS, 4 * HEAD)] * 2
+            + anywhere(len(carry)),
+            out_specs=anywhere(8) + [head_spec(planes, LMAX, 2 * HEAD)] * 2,
             scratch_shapes=[
                 pltpu.VMEM((2, 4 * SUBS * HALF, LMAX), BF16),
                 pltpu.VMEM((2, 4 * SUBS * HALF, LMAX), BF16),
+                pltpu.VMEM((LMAX, 4 * HEAD), BF16),
                 pltpu.SemaphoreType.DMA((2, 4)),
                 pltpu.SemaphoreType.DMA((2, 4)),
             ],
         ),
         out_shape=[jax.ShapeDtypeStruct((SUBS * HALF, LMAX), BF16)] * 8
-        + [
-            jax.ShapeDtypeStruct((HEADS, LMAX, 2 * HEAD), F32),
-            jax.ShapeDtypeStruct((HEADS, LMAX, 2 * HEAD), BF16),
-        ],
-        input_output_aliases={14 + i: 8 + i for i in range(len(carry))},
-        compiler_params=params(56),
+        + [jax.ShapeDtypeStruct((HEADS, LMAX, 2 * HEAD), BF16)] * 2,
+        input_output_aliases={13 + i: 8 + i for i in range(len(carry))},
+        compiler_params=params(60),
         cost_estimate=pl.CostEstimate(
-            flops=2 * HEADS * HROWS * LMAX * 4 * HEAD,
-            bytes_accessed=HEADS * (2 * HROWS * LMAX + 5 * HROWS * 256 + 4 * LMAX * 256),
+            flops=3 * HEADS * HROWS * LMAX * 4 * HEAD,
+            bytes_accessed=HEADS * (2 * HROWS * LMAX + 4 * HROWS * 256 + 4 * LMAX * 256),
             transcendentals=HEADS * HROWS * LMAX // 2,
         ),
         name="unmix",
-    )(sc, *shards, v_own, v_far, grad_heads, mean, inverse, *carry)
+    )(sc, *shards, v_own, v_far, grad_heads, mean, *carry)
 
 
 def close_kernel(sc, tok, res_own, res_got, out_own, out_got, own, far, gain, w_own, w_far, *refs):
@@ -559,7 +632,7 @@
     for item in range(2):
         lanes = slice(item * HEAD, (item + 1) * HEAD)
         pieces = [
-            (own[head, :, lanes] + far[head, :, lanes].astype(F32)).astype(BF16) for head in range(HEADS)
+            add_low(own[head, :, lanes], far[head, :, lanes]) for head in range(HEADS)
         ]
         back = jnp.concatenate(pieces, axis=1)
         x = tok[item].reshape(rows, WIDTH).astype(F32)
@@ -669,12 +742,12 @@
         grid_spec=pltpu.PrefetchScalarGridSpec(
             num_scalar_prefetch=1,
             grid=(1,),
-            in_specs=in_hbm(16),
-            out_specs=in_hbm(len(shapes)),
+            in_specs=anywhere(16),
+            out_specs=anywhere(len(shapes)),
             scratch_shapes=[pltpu.SemaphoreType.DMA((16, len(moves)))],
         ),
         out_shape=[jax.ShapeDtypeStruct(shape, BF16) for shape in shapes],
-        compiler_params=params(16),
+        compiler_params=params(60),
         cost_estimate=pl.CostEstimate(
             flops=0, bytes_accessed=4 * sum(a * b for a, b in shapes), transcendentals=0
         ),
@@ -777,7 +850,13 @@
 
 
 def scatter16(shares, works=(), made=()):
-    have = {(k, y, x): shares[4 * k + 2 * y + x] for k in range(4) for y in range(2) for x in range(2)}
+    have = {}
+
+    def put(planes, values):
+        for index, value in enumerate(values):
+            have[planes[index // 4], index // 2 % 2, index % 2] = value
+
+    put((0, 1, 2, 3) if len(shares) == 16 else (3, 2), shares)
     for step, (by_x, by_y, by_z) in enumerate(reversed(STEPS)):
         got = [
             ((by_z[0] - 1, by_z[1], by_z[2]), ring(have[by_z], -1)),
@@ -789,6 +868,8 @@
         if step < len(works):
             made = works[step](made)
         values, have, made = lax.optimization_barrier(([value for _, value in got], have, made))
+        if step == 0 and len(shares) == 8:
+            put((1, 0), made[0])
         for at in dict.fromkeys(at for at, _ in got):
             total = have[at].astype(F32)
             for (target, _), value in zip(got, values):
@@ -863,73 +944,75 @@
         return *made, run_mix(sc, (2, 3), shares[8:], made[-2], made[-1], near)
 
     pieces, made = gather16(after(packed, *shares[-3:]), [make_values, share_values, mix_near, mix_far])
-    value, value_far, gain_one, gain_two, v_own, v_far, (heads, mean, inverse) = made
+    value, value_far, gain_one, gain_two, v_own, v_far, (heads, mean) = made
     down, up, out = place_weights(sc, pieces)
-    down_far, up_far, out_far = other(down), other(up), other(out)
-
-    mixed, resid, normed, masked = run_pre(
-        sc, tokens, tokens_far, grad_out, grad_far, heads, (out, out_far), gain_two
-    )
-    branch, back, down_own, down_far, up_own, up_far = run_feed(sc, normed, masked, (up, up_far), (down, down_far))
-    down_got, up_got = other(down_far), other(up_far)
-    out_own, out_far, res_own, res_far, grad_heads, d_out_own, d_out_far, d_gain_two = run_post(
-        sc, resid, branch, back, masked, mixed, (out, out_far), gain_two
-    )
-
-    packed = run_collect(sc, down_own, down_got, up_own, up_got, d_out_own, other(d_out_far))
-
-    def unmix_far(_):
-        return run_unmix(sc, (3, 2), shares[12:] + shares[8:12], v_own, v_far, grad_heads, mean, inverse, ())
-
-    def unmix_near(made):
-        *far, back_own, back_far = made
-        near = run_unmix(
-            sc, (1, 0), shares[4:8] + shares[:4], v_own, v_far, grad_heads, mean, inverse, (back_own, back_far)
+    down, up, out = (down, other(down)), (up, other(up)), (out, other(out))
+
+    mixed, resid, normed, masked = run_pre(sc, tokens, tokens_far, grad_out, grad_far, heads, out, gain_two)
+    active, up_grad, back = run_units(sc, normed, masked, up, down)
+    res_own, res_far, grad_heads, d_out_own, d_out_far, d_gain_two = run_post(
+        sc, resid, back, masked, mixed, out, gain_two
+    )
+    *far, back_own, back_far = run_unmix(
+        sc, (3, 2), shares[12:] + shares[8:12], v_own, v_far, grad_heads, mean, ()
+    )
+
+    def unmix_near(_):
+        *near, own, far = run_unmix(
+            sc, (1, 0), shares[4:8] + shares[:4], v_own, v_far, grad_heads, mean, (back_own, back_far)
         )
-        return far, near
-
-    def exchange(made):
-        far, (*near, back_own, back_far) = made
-        return far, near, back_own, other(back_far), other(out_far), other(res_far)
-
-    big_sum, made = scatter16([packed[i] for i in range(16)], [unmix_far, unmix_near, exchange])
-    far, near, back_own, back_got, out_got, res_got = made
-    rand_grads = near[4:] + near[:4] + far[4:] + far[:4]
-
-    def finish(_):
+        return near, own, far, other(res_far), other(d_out_far)
+
+    def make_output(made):
+        near, own, far, *rest = made
+        return near, own, other(far), *rest, *run_out(sc, active, resid, down)
+
+    def make_down(made):
+        *rest, out_own, out_far = made
+        return *rest, out_own, other(out_far), *run_down_grad(sc, active, masked)
+
+    def make_up(made):
+        *rest, down_own, down_far = made
+        return *rest, (down_own, other(down_far)), run_up_grad(sc, normed, up_grad)
+
+    def finish(made):
+        _, own, got, res_got, d_out_got, out_own, out_got, down_sides, (up_own, up_far) = made
         output, tokens_grad, d_value, d_gain_one = run_close(
-            sc, tokens, res_own, res_got, out_own, out_got, back_own, back_got, gain_one, value, value_far
+            sc, tokens, res_own, res_got, out_own, out_got, own, got, gain_one, value, value_far
         )
         gain_pair = jnp.concatenate([d_gain_one, d_gain_two]).reshape(2, 16, 1, 48).astype(BF16)
         gain_pair = jnp.pad(gain_pair, ((0, 0), (0, 0), (0, 15), (0, SIDE - 48)))
         small = jnp.concatenate([d_value.reshape(2, 16, 48, SIDE), gain_pair], 2)
-        return output, tokens_grad, small, other(big_sum)
-
-    def small_core(made):
-        *kept, small, big_far = made
-        small = add_low(pick(small, core), other(pick(small, 1 - core))).reshape(4, 2, 2, 64, SIDE)
-        return *kept, big_far, small
+        return output, tokens_grad, small, (*down_sides, up_own, other(up_far), d_out_own, d_out_got)
+
+    rand_sum, made = scatter16(far, [unmix_near, make_output, make_down, make_up, finish])
+    output, tokens_grad, small, sides = made
+    packed = run_collect(sc, *sides)
+
+    def small_core(_):
+        return add_low(pick(small, core), other(pick(small, 1 - core))).reshape(4, 2, 2, 64, SIDE)
 
     def small_line(made):
-        *kept, small = made
-        return *kept, add_low(pick(small, x, 2), swap(pick(small, 1 - x, 2), TO_X))
+        return add_low(pick(made, x, 2), swap(pick(made, 1 - x, 2), TO_X))
 
     def small_plane(made):
-        *kept, small = made
-        return *kept, add_low(pick(small, y, 1), swap(pick(small, 1 - y, 1), TO_Y))
+        return add_low(pick(made, y, 1), swap(pick(made, 1 - y, 1), TO_Y))
 
     def small_planes(made):
-        *kept, small = made
-        total = pick(small, z).astype(F32)
+        total = pick(made, z).astype(F32)
         for k in range(1, PLANES):
-            total = total + ring(pick(small, lax.rem(z + PLANES - k, PLANES)), -k).astype(F32)
-        return *kept, total
-
-    rand_sum, made = scatter16(
-        after(rand_grads, big_sum), [finish, small_core, small_line, small_plane, small_planes]
-    )
-    output, tokens_grad, big_far, small_sum = made
-    small_far = other(small_sum)
+            total = total + ring(pick(made, lax.rem(z + PLANES - k, PLANES)), -k).astype(F32)
+        return total
+
+    def rand_home(made):
+        blocks = rand_sum.reshape(2, 3, HALF, LMAX)
+        return made, pick(blocks, core), other(pick(blocks, 1 - core))
+
+    big_sum, made = scatter16(
+        after([packed[i] for i in range(16)], rand_sum), [small_core, small_line, small_plane, small_planes, rand_home]
+    )
+    small_sum, blocks, blocks_far = made
+    big_far, small_far = other(big_sum), other(small_sum)
 
     rows_of = lambda value, rows: pick(value.reshape(-1, 2, rows, SIDE), core, 1)
     mine = lambda own, far, rows: side(rows_of(own, rows)[0], rows_of(far, rows)[0], 1)
@@ -941,8 +1024,7 @@
     gains_pair = ordered(core, small_sum[48, :48], small_far[48, :48])
     gain_pair = pick(gains_pair.reshape(2, 2, 24), core, 1)
 
-    blocks = rand_sum.reshape(2, 3, HALF, LMAX)
-    rand_shard = ordered(core, pick(blocks, core), other(pick(blocks, 1 - core)), 1)
+    rand_shard = ordered(core, blocks, blocks_far, 1)
 
     return (
         output.reshape(2, LMAX, WIDTH),

time: 589 us -> 754 us (1.28)
  Pallas kernels: 209 us -> 421 us
  waiting for transfers between devices: 222 us -> 163 us
  starting transfers between devices: 66.8 us -> 75.5 us
    pallas_call x2, Pallas kernels: 13.4 us -> 190 us  [run_place(): pl.pallas_call(partial(place_kernel, moves), grid_spec=pltpu.PrefetchScal...]
    ppermute x62, waiting for transfers between devices: 154 us -> 98.3 us  [swap(): return lax.ppermute(x, BOTH, [(d, d ^ bit) for d in range(DEVICES)])]
    pallas_call x1 -> x4, Pallas kernels: 83.9 us -> 105 us  [the longest x1 57.4 us: run_units(): pl.pallas_call(units_kernel, grid_spec=pltpu.PrefetchScalarGridSpec(num_s...]
    pallas_call x2, Pallas kernels: 37.4 us -> 47.9 us  [run_unmix(): pl.pallas_call(partial(unmix_kernel, bool(carry)), grid_spec=pltpu.Prefet...]
    ppermute x23, starting transfers between devices: 17.1 us -> 27.1 us  [ring(): lax.ppermute(x, BOTH, [(d, (d + 8 * way) % DEVICES) for d in range(DEVICE...]
    unnamed x170 -> x179, local copies, waits for them, and re-layouts: 40.2 us -> 33.4 us
  transfers between devices with their start and end apart: 85 -> 85, of which waited for: 43 -> 39; matrix products, arithmetic and copies ran while one was open for 5% -> 6% of each run, Pallas kernels for 19% -> 21%
where the time goes in v3:
time: 754 us; the launch traced here: 745 us
  Pallas kernels  421 us (56%)
  waiting for transfers between devices  163 us (22%)
  starting transfers between devices  75.5 us (10%)
  local copies, waits for them, and re-layouts  47.7 us (6%)
  other arithmetic  35.3 us (5%)
    pallas_call x2, Pallas kernels, run_place(): pl.pallas_call(partial(place_kernel, moves), grid_spec=pltpu.PrefetchScal...  190 us
    ppermute x62, waiting for transfers between devices, swap(): return lax.ppermute(x, BOTH, [(d, d ^ bit) for d in range(DEVICES)])  98.3 us
    ppermute x23, waiting for transfers between devices, ring(): lax.ppermute(x, BOTH, [(d, (d + 8 * way) % DEVICES) for d in range(DEVICE...  64.4 us
    pallas_call x1, Pallas kernels, run_units(): pl.pallas_call(units_kernel, grid_spec=pltpu.PrefetchScalarGridSpec(num_s...  57.4 us
    ppermute x62, starting transfers between devices, swap(): return lax.ppermute(x, BOTH, [(d, d ^ bit) for d in range(DEVICES)])  48.4 us
    pallas_call x2, Pallas kernels, run_unmix(): pl.pallas_call(partial(unmix_kernel, bool(carry)), grid_spec=pltpu.Prefet...  47.9 us
    unnamed x179, local copies, waits for them, and re-layouts  33.4 us
    ppermute x23, starting transfers between devices, ring(): lax.ppermute(x, BOTH, [(d, (d + 8 * way) % DEVICES) for d in range(DEVICE...  27.1 us
  transfers between devices with their start and end apart: 85, of which 39 were waited for; matrix products, arithmetic and copies ran while one was open for 6% of the time, Pallas kernels for 21%

profile of v3, /device:TPU:0, one launch (start us, length us, event | category | flops | bytes accessed | tf_op | source)
XLA Modules:
  0.0 744.9 jit_solution(10393527102065795321)
XLA Ops:
  24.3 16.0 %collective-permute-done.2.refs_1_.refs_5_ = bf16[416,1024]{1,0:T(8,128)(2,1)S(1)} collective-permute-done((bf16[416,1024]{1,0:T(8,128)(2,1)S(1)}, bf16[416,1024]{1,0:T(8,128)(2,1)S(1)}, u32[]{:S(2)}, u32[]{:S(2)}) %collective-permute-start.2) | collective-permute-done | bytes 852000 | tf_op jit(solution)/shard_map/ppermute | solution.py:810
  46.1 20.1 %collective-permute-done.10.refs_8_.refs_0_.refs_4_ = bf16[416,1024]{1,0:T(8,128)(2,1)S(1)} collective-permute-done((bf16[416,1024]{1,0:T(8,128)(2,1)S(1)}, bf16[416,1024]{1,0:T(8,128)(2,1)S(1)}, u32[]{:S(2)}, u32[]{:S(2)}) %collective-permute-start.10) | collective-permute-done | bytes 852000 | tf_op jit(solution)/shard_map/ppermute | solution.py:814
  67.6 17.2 %collective-permute-done.11.refs_6_.refs_2_ = bf16[416,1024]{1,0:T(8,128)(2,1)S(1)} collective-permute-done((bf16[416,1024]{1,0:T(8,128)(2,1)S(1)}, bf16[416,1024]{1,0:T(8,128)(2,1)S(1)}, u32[]{:S(2)}, u32[]{:S(2)}) %collective-permute-start.11) | collective-permute-done | bytes 852000 | tf_op jit(solution)/shard_map/ppermute | solution.py:810
  90.2 16.5 %collective-permute-done.14.refs_7_.refs_3_ = bf16[416,1024]{1,0:T(8,128)(2,1)S(1)} collective-permute-done((bf16[416,1024]{1,0:T(8,128)(2,1)S(1)}, bf16[416,1024]{1,0:T(8,128)(2,1)S(1)}, u32[]{:S(2)}, u32[]{:S(2)}) %collective-permute-start.14) | collective-permute-done | bytes 852000 | tf_op jit(solution)/shard_map/ppermute | solution.py:814
  110.0 14.3 %collective-permute-done.17.refs_11_.refs_3_.refs_7_ = bf16[416,1024]{1,0:T(8,128)(2,1)} collective-permute-done((bf16[416,1024]{1,0:T(8,128)(2,1)}, bf16[416,1024]{1,0:T(8,128)(2,1)}, u32[]{:S(2)}, u32[]{:S(2)}) %collective-permute-start.17) | collective-permute-done | bytes 852000 | tf_op jit(solution)/shard_map/ppermute | solution.py:810
  126.9 26.2 %place.2 = (bf16[768,384]{1,0:T(8,128)(2,1)}, bf16[256,384]{1,0:T(8,128)(2,1)}) custom-call(s32[7]{0:T(128)} %concatenate.72.sc, bf16[416,1024]{1,0:T(8,128)(2,1)} %copy-done.39, bf16[416,1024]{1,0:T(8,128)(2,1)} %copy-done.40, bf16[416,1024]{1,0:T(8,128)(2,1)} %copy-done.41, bf16[416,1024]{1,0:T(8,128)(2,1)} %copy-done.43, bf16[416,1024]{1,0:T(8,128)(2,1)} %copy-done.42, ...), custom_call_target="tpu_custom_call" | custom-call | bytes 1572864 | tf_op jit(solution)/shard_map/place/pallas_call | solution.py:740
  159.6 5.2 values.1.refs_8_
  168.8 8.4 %collective-permute-done.24.refs_3_ = bf16[432,384]{1,0:T(8,128)(2,1)S(1)} collective-permute-done((bf16[432,384]{1,0:T(8,128)(2,1)}, bf16[432,384]{1,0:T(8,128)(2,1)S(1)}, u32[]{:S(2)}, u32[]{:S(2)}) %collective-permute-start.24) | collective-permute-done | bytes 331808 | tf_op jit(solution)/shard_map/ppermute | solution.py:810
  184.3 10.4 %mix.2 = (bf16[12,512,256]{2,1,0:T(8,128)(2,1)}, f32[12,512,256]{2,1,0:T(8,128)}) custom-call(s32[7]{0:T(128)} %concatenate.72.sc, bf16[416,1024]{1,0:T(8,128)(2,1)} %copy-done.39, bf16[416,1024]{1,0:T(8,128)(2,1)} %copy-done.40, bf16[416,1024]{1,0:T(8,128)(2,1)} %copy-done.41, bf16[416,1024]{1,0:T(8,128)(2,1)} %copy-done.43, bf16[416,1024]{1,0:T(8,128)(2,1)} %copy-done.42, ...), custom_call_target="tpu_custom_call" | custom-call | flops 3221225472 | bytes 14155776 | tf_op jit(solution)/shard_map/mix/pallas_call | solution.py:182
  196.9 10.4 %mix.3 = (bf16[12,512,256]{2,1,0:T(8,128)(2,1)}, f32[12,512,256]{2,1,0:T(8,128)}) custom-call(s32[7]{0:T(128)} %concatenate.72.sc, bf16[416,1024]{1,0:T(8,128)(2,1)} %copy-done.47, bf16[416,1024]{1,0:T(8,128)(2,1)} %copy-done.48, bf16[416,1024]{1,0:T(8,128)(2,1)} %collective-permute-done.15.refs_10_.refs_2_.refs_6_, ...), custom_call_target="tpu_custom_call", output_to_operand_aliasing={{0}: (11, {}), {1}: (12, {})} | custom-call | flops 3221225472 | bytes 14155776 | tf_op jit(solution)/shard_map/mix/pallas_call | solution.py:182
  219.4 163.5 %place.3 = (bf16[3072,384]{1,0:T(8,128)(2,1)}, bf16[768,1536]{1,0:T(8,128)(2,1)}, bf16[768,384]{1,0:T(8,128)(2,1)}) custom-call(s32[7]{0:T(128)} %concatenate.72.sc, bf16[432,384]{1,0:T(8,128)(2,1)} %pad_maximum_fusion.1.refs_0_, bf16[432,384]{1,0:T(8,128)(2,1)} %collective-permute-done.20.refs_1_, bf16[432,384]{1,0:T(8,128)(2,1)} %collective-permute-done.21.refs_2_, ...), custom_call_target="tpu_custom_call" | custom-call | bytes 10616832 | tf_op jit(solution)/shard_map/place/pallas_call | solution.py:740
  383.5 8.4 %collective-permute-done.37.wo_far = bf16[768,384]{1,0:T(8,128)(2,1)S(1)} collective-permute-done((bf16[768,384]{1,0:T(8,128)(2,1)}, bf16[768,384]{1,0:T(8,128)(2,1)S(1)}, u32[]{:S(2)}, u32[]{:S(2)}) %collective-permute-start.37) | collective-permute-done | bytes 589856 | tf_op jit(solution)/shard_map/ppermute | solution.py:810
  397.7 10.5 %pre.1 = (bf16[4,512,768]{2,1,0:T(8,128)(2,1)S(1)}, f32[4,512,768]{2,1,0:T(8,128)}, bf16[4,512,768]{2,1,0:T(8,128)(2,1)S(1)}, bf16[4,512,768]{2,1,0:T(8,128)(2,1)S(1)}) custom-call(s32[7]{0:T(128)S(1)} %copy-done.32, bf16[2,8,2,64,768]{4,3,2,1,0:T(8,128)(2,1)S(1)} %bitcast.153, bf16[2,8,64,768]{3,2,1,0:T(8,128)(2,1)S(1)} %copy-done.18, ...), custom_call_target="tpu_custom_call" | custom-call | flops 2415919104 | bytes 25165824 | tf_op jit(solution)/shard_map/pre/pallas_call | solution.py:255
  415.3 57.4 %units.1 = (bf16[2048,3072]{1,0:T(8,128)(2,1)}, bf16[2048,3072]{1,0:T(8,128)(2,1)}, f32[2048,768]{1,0:T(8,128)}) custom-call(s32[7]{0:T(128)} %concatenate.72.sc, bf16[2048,768]{1,0:T(8,128)(2,1)} %bitcast.162, bf16[2048,768]{1,0:T(8,128)(2,1)} %bitcast.157, bf16[768,1536]{1,0:T(8,128)(2,1)} %get-tuple-element.533.up_own, bf16[768,1536]{1,0:T(8,128)(2,1)} %copy-done.83, ...), custom_call_target="tpu_custom_call" | custom-call | flops 28991029248 | bytes 37748736 | tf_op jit(solution)/shard_map/units/pallas_call | solution.py:343
  472.7 18.7 %post.1 = (f32[2,512,768]{2,1,0:T(8,128)S(1)}, bf16[2,512,768]{2,1,0:T(8,128)(2,1)S(1)}, bf16[12,512,256]{2,1,0:T(8,128)(2,1)S(1)}, bf16[768,384]{1,0:T(8,128)(2...) custom-call(s32[7]{0:T(128)S(1)} %copy-done.33, f32[4,512,768]{2,1,0:T(8,128)} %get-tuple-element.530.resid, ...), custom_call_target="tpu_custom_call" | custom-call | flops 4831838208 | bytes 44040192 | tf_op jit(solution)/shard_map/post/pallas_call | solution.py:516
  496.4 23.9 %unmix.2 = (bf16[384,1024]{1,0:T(8,128)(2,1)}, bf16[384,1024]{1,0:T(8,128)(2,1)}, bf16[384,1024]{1,0:T(8,128)(2,1)}, bf16[384,1024]{1,0:T(8,128)(2,1)}, bf16[384...) custom-call(s32[7]{0:T(128)} %concatenate.72.sc, ...), custom_call_target="tpu_custom_call" | custom-call | flops 4831838208 | bytes 31457280 | tf_op jit(solution)/shard_map/unmix/pallas_call | solution.py:590
  524.2 24.0 %unmix.3 = (bf16[384,1024]{1,0:T(8,128)(2,1)}, bf16[384,1024]{1,0:T(8,128)(2,1)}, bf16[384,1024]{1,0:T(8,128)(2,1)}, bf16[384,1024]{1,0:T(8,128)(2,1)}, bf16[384...) custom-call(s32[7]{0:T(128)} %concatenate.72.sc, ...), custom_call_target="tpu_custom_call", output_to_operand_aliasing={{8}: (13, {}), {9}: (14, {})} | custom-call | flops 4831838208 | bytes 31457280 | tf_op jit(solution)/shard_map/unmix/pallas_call | solution.py:590
  556.9 16.6 %out.1 = (f32[2,512,768]{2,1,0:T(8,128)}, bf16[2,512,768]{2,1,0:T(8,128)(2,1)S(1)}) custom-call(s32[7]{0:T(128)S(1)} %copy-done.34, bf16[4,512,3072]{2,1,0:T(8,128)(2,1)} %bitcast.196, f32[4,512,768]{2,1,0:T(8,128)} %get-tuple-element.530.resid, bf16[3072,384]{1,0:T(8,128)(2,1)S(1)} %copy-done.36, bf16[3072,384]{1,0:T(8,128)(2,1)} %copy-done.82), custom_call_target="tpu_custom_call" | custom-call | flops 9663676416 | bytes 23592960 | tf_op jit(solution)/shard_map/out/pallas_call | solution.py:443
  581.4 14.8 %down_grad.1 = (bf16[3072,384]{1,0:T(8,128)(2,1)S(1)}, bf16[3072,384]{1,0:T(8,128)(2,1)S(1)}) custom-call(s32[7]{0:T(128)S(1)} %copy-done.34, bf16[2048,3072]{1,0:T(8,128)(2,1)} %get-tuple-element.581.active, bf16[2048,768]{1,0:T(8,128)(2,1)} %bitcast.158), custom_call_target="tpu_custom_call" | custom-call | flops 9663676416 | bytes 15728640 | tf_op jit(solution)/shard_map/down_grad/pallas_call | solution.py:379
  606.2 15.9 %up_grad.1 = (bf16[768,1536]{1,0:T(8,128)(2,1)S(1)}, bf16[768,1536]{1,0:T(8,128)(2,1)}) custom-call(s32[7]{0:T(128)S(1)} %copy-done.34, bf16[2048,768]{1,0:T(8,128)(2,1)} %bitcast.163, bf16[2048,3072]{1,0:T(8,128)(2,1)} %get-tuple-element.623.up_grad), custom_call_target="tpu_custom_call" | custom-call | flops 9663676416 | bytes 15728640 | tf_op jit(solution)/shard_map/up_grad/pallas_call | solution.py:410
  633.9 14.9 %close.1 = (f32[2,8,2,64,768]{4,3,2,1,0:T(8,128)}, f32[2,8,2,64,768]{4,3,2,1,0:T(8,128)}, bf16[2,768,384]{2,1,0:T(8,128)(2,1)S(1)}, f32[1,768]{1,0:T(1,128)S(1)}) custom-call(s32[7]{0:T(128)S(1)} %copy-done.34, bf16[2,8,2,64,768]{4,3,2,1,0:T(8,128)(2,1)} %bitcast.151, f32[2,8,64,768]{3,2,1,0:T(8,128)} %bitcast.156, bf16[2,8,64,768]{3,2,1,0:T(8,128)(2,1)S(1)} %bitcast.159, ...), custom_call_target="tpu_custom_call" | custom-call | flops 4831838208 | bytes 29884416 | tf_op jit(solution)/shard_map/close/pallas_call | solution.py:677
  654.8 9.0 %collect.1 = bf16[16,432,384]{2,1,0:T(8,128)(2,1)S(1)} custom-call(s32[7]{0:T(128)S(1)} %copy-done.34, bf16[3072,384]{1,0:T(8,128)(2,1)S(1)} %get-tuple-element.655.down, bf16[3072,384]{1,0:T(8,128)(2,1)S(1)} %copy-done.12, bf16[768,1536]{1,0:T(8,128)(2,1)S(1)} %copy-done.14, bf16[768,1536]{1,0:T(8,128)(2,1)} %collective-permute-done.60.up_got, ...), custom_call_target="tpu_custom_call" | custom-call | bytes 15925248 | tf_op jit(solution)/shard_map/collect/pallas_call | solution.py:790
  673.9 5.1 collective-permute-done.61
  688.5 5.1 collective-permute-done.68
  (418 shorter events, 210.1 us)
Async XLA Ops:
  11.7 33.2 %collective-permute-start.6 = (bf16[2,8,64,768]{3,2,1,0:T(8,128)(2,1)}, bf16[2,8,64,768]{3,2,1,0:T(8,128)(2,1)S(1)}, u32[]{:S(2)}, u32[]{:S(2)}) collective-permute-start(bf16[2,8,64,768]{3,2,1,0:T(8,128)(2,1)} %dynamic-slice_bitcast_fusion.1), channel_id=1, source_target_pairs={{0,1},{1,0},{2,3},{3,2},{4,5},{5,4},{6,7},{7,6},{8,9},{9,8},{10,11... | collective-permute-start | bytes 4718600 | tf_op jit(solution)/shard_map/ppermute | solution.py:810
  14.2 30.7 %collective-permute-start.7 = (bf16[2,8,64,768]{3,2,1,0:T(8,128)(2,1)}, bf16[2,8,64,768]{3,2,1,0:T(8,128)(2,1)S(1)}, u32[]{:S(2)}, u32[]{:S(2)}) collective-permute-start(bf16[2,8,64,768]{3,2,1,0:T(8,128)(2,1)} %dynamic-slice_bitcast_fusion), channel_id=1, source_target_pairs={{0,1},{1,0},{2,3},{3,2},{4,5},{5,4},{6,7},{7,6},{8,9},{9,8},{10,11... | collective-permute-start | bytes 4718600 | tf_op jit(solution)/shard_map/ppermute | solution.py:810
  18.2 22.1 %collective-permute-start.2 = (bf16[416,1024]{1,0:T(8,128)(2,1)S(1)}, bf16[416,1024]{1,0:T(8,128)(2,1)S(1)}, u32[]{:S(2)}, u32[]{:S(2)}) collective-permute-start(bf16[416,1024]{1,0:T(8,128)(2,1)S(1)} %pad_maximum_fusion.refs_0_.refs_4_), channel_id=1, source_target_pairs={{0,2},{1,3},{2,0},{3,1},{4,6},{5,7},{6,4},{7,5},{8,10},{9,11},{10,... | collective-permute-start | bytes 2555912 | tf_op jit(solution)/shard_map/ppermute | solution.py:810
  21.2 20.6 %collective-permute-start.3 = (bf16[416,1024]{1,0:T(8,128)(2,1)S(1)}, bf16[416,1024]{1,0:T(8,128)(2,1)S(1)}, u32[]{:S(2)}, u32[]{:S(2)}) collective-permute-start(bf16[416,1024]{1,0:T(8,128)(2,1)S(1)} %pad_maximum_fusion.refs_0_.refs_4_), channel_id=1, source_target_pairs={{0,4},{1,5},{2,6},{3,7},{4,0},{5,1},{6,2},{7,3},{8,12},{9,13},{10,... | collective-permute-start | bytes 2555912 | tf_op jit(solution)/shard_map/ppermute | solution.py:810
  22.7 22.2 %collective-permute-start.4 = (bf16[416,1024]{1,0:T(8,128)(2,1)S(1)}, bf16[416,1024]{1,0:T(8,128)(2,1)S(1)}, u32[]{:S(2)}, u32[]{:S(2)}) collective-permute-start(bf16[416,1024]{1,0:T(8,128)(2,1)S(1)} %pad_maximum_fusion.refs_0_.refs_4_), channel_id=1, source_target_pairs={{0,8},{1,9},{2,10},{3,11},{4,12},{5,13},{6,14},{7,15},{8,16},{9,17... | collective-permute-start | bytes 2555912 | tf_op jit(solution)/shard_map/ppermute | solution.py:814
  44.9 21.3 %collective-permute-start.10 = (bf16[416,1024]{1,0:T(8,128)(2,1)S(1)}, bf16[416,1024]{1,0:T(8,128)(2,1)S(1)}, u32[]{:S(2)}, u32[]{:S(2)}) collective-permute-start(bf16[416,1024]{1,0:T(8,128)(2,1)S(1)} %collective-permute-done.4.refs_4_.refs_0_), channel_id=1, source_target_pairs={{0,8},{1,9},{2,10},{3,11},{4,12},{5,13},{6,14},{7,15},{8,16},{9,17... | collective-permute-start | bytes 2555912 | tf_op jit(solution)/shard_map/ppermute | solution.py:814
  45.0 21.2 %collective-permute-start.8 = (bf16[416,1024]{1,0:T(8,128)(2,1)S(1)}, bf16[416,1024]{1,0:T(8,128)(2,1)S(1)}, u32[]{:S(2)}, u32[]{:S(2)}) collective-permute-start(bf16[416,1024]{1,0:T(8,128)(2,1)S(1)} %collective-permute-done.2.refs_1_.refs_5_), channel_id=1, source_target_pairs={{0,4},{1,5},{2,6},{3,7},{4,0},{5,1},{6,2},{7,3},{8,12},{9,13},{10,... | collective-permute-start | bytes 2555912 | tf_op jit(solution)/shard_map/ppermute | solution.py:810
  45.6 20.7 %collective-permute-start.9 = (bf16[416,1024]{1,0:T(8,128)(2,1)S(1)}, bf16[416,1024]{1,0:T(8,128)(2,1)S(1)}, u32[]{:S(2)}, u32[]{:S(2)}) collective-permute-start(bf16[416,1024]{1,0:T(8,128)(2,1)S(1)} %collective-permute-done.4.refs_4_.refs_0_), channel_id=1, source_target_pairs={{0,2},{1,3},{2,0},{3,1},{4,6},{5,7},{6,4},{7,5},{8,10},{9,11},{10,... | collective-permute-start | bytes 2555912 | tf_op jit(solution)/shard_map/ppermute | solution.py:810
  67.6 20.0 %collective-permute-start.13 = (bf16[416,1024]{1,0:T(8,128)(2,1)S(1)}, bf16[416,1024]{1,0:T(8,128)(2,1)S(1)}, u32[]{:S(2)}, u32[]{:S(2)}) collective-permute-start(bf16[416,1024]{1,0:T(8,128)(2,1)S(1)} %collective-permute-done.10.refs_8_.refs_0_.refs_4_), channel_id=1, source_target_pairs={{0,8},{1,9},{2,10},{3,11},{4,12},{5,13},{6,14},{7,15},{8,16},{9,17... | collective-permute-start | bytes 2555912 | tf_op jit(solution)/shard_map/ppermute | solution.py:814
  382.9 30.4 %collective-permute-start.38 = (bf16[768,1536]{1,0:T(8,128)(2,1)}, bf16[768,1536]{1,0:T(8,128)(2,1)S(1)}, u32[]{:S(2)}, u32[]{:S(2)}) collective-permute-start(bf16[768,1536]{1,0:T(8,128)(2,1)} %get-tuple-element.533.up_own), channel_id=1, source_target_pairs={{0,1},{1,0},{2,3},{3,2},{4,5},{5,4},{6,7},{7,6},{8,9},{9,8},{10,11... | collective-permute-start | bytes 7077896 | tf_op jit(solution)/shard_map/ppermute | solution.py:810
  382.9 30.3 %collective-permute-start.39 = (bf16[3072,384]{1,0:T(8,128)(2,1)}, bf16[3072,384]{1,0:T(8,128)(2,1)S(1)}, u32[]{:S(2)}, u32[]{:S(2)}) collective-permute-start(bf16[3072,384]{1,0:T(8,128)(2,1)} %get-tuple-element.534.dn_own), channel_id=1, source_target_pairs={{0,1},{1,0},{2,3},{3,2},{4,5},{5,4},{6,7},{7,6},{8,9},{9,8},{10,11... | collective-permute-start | bytes 7077896 | tf_op jit(solution)/shard_map/ppermute | solution.py:810
  495.6 52.6 %collective-permute-start.43 = (bf16[2,512,768]{2,1,0:T(8,128)(2,1)S(1)}, bf16[2,512,768]{2,1,0:T(8,128)(2,1)S(1)}, u32[]{:S(2)}, u32[]{:S(2)}) collective-permute-start(bf16[2,512,768]{2,1,0:T(8,128)(2,1)S(1)} %get-tuple-element.559), channel_id=1, source_target_pairs={{0,1},{1,0},{2,3},{3,2},{4,5},{5,4},{6,7},{7,6},{8,9},{9,8},{10,11... | collective-permute-start | bytes 4718600 | tf_op jit(solution)/shard_map/ppermute | solution.py:810
  520.4 27.8 %collective-permute-start.40 = (bf16[384,1024]{1,0:T(8,128)(2,1)}, bf16[384,1024]{1,0:T(8,128)(2,1)}, u32[]{:S(2)}, u32[]{:S(2)}) collective-permute-start(bf16[384,1024]{1,0:T(8,128)(2,1)} %get-tuple-element.539), channel_id=1, source_target_pairs={{0,24},{1,25},{2,26},{3,27},{4,28},{5,29},{6,30},{7,31},{8,0},{9,1... | collective-permute-start | bytes 2359304 | tf_op jit(solution)/shard_map/ppermute | solution.py:814
  522.2 26.0 %collective-permute-start.41 = (bf16[384,1024]{1,0:T(8,128)(2,1)}, bf16[384,1024]{1,0:T(8,128)(2,1)}, u32[]{:S(2)}, u32[]{:S(2)}) collective-permute-start(bf16[384,1024]{1,0:T(8,128)(2,1)} %get-tuple-element.540), channel_id=1, source_target_pairs={{0,2},{1,3},{2,0},{3,1},{4,6},{5,7},{6,4},{7,5},{8,10},{9,11},{10,... | collective-permute-start | bytes 2359304 | tf_op jit(solution)/shard_map/ppermute | solution.py:810
  523.1 25.1 %collective-permute-start.42 = (bf16[384,1024]{1,0:T(8,128)(2,1)}, bf16[384,1024]{1,0:T(8,128)(2,1)}, u32[]{:S(2)}, u32[]{:S(2)}) collective-permute-start(bf16[384,1024]{1,0:T(8,128)(2,1)} %get-tuple-element.541), channel_id=1, source_target_pairs={{0,4},{1,5},{2,6},{3,7},{4,0},{5,1},{6,2},{7,3},{8,12},{9,13},{10,... | collective-permute-start | bytes 2359304 | tf_op jit(solution)/shard_map/ppermute | solution.py:810
  524.2 24.0 %collective-permute-start.44 = (bf16[768,384]{1,0:T(8,128)(2,1)}, bf16[768,384]{1,0:T(8,128)(2,1)S(1)}, u32[]{:S(2)}, u32[]{:S(2)}) collective-permute-start(bf16[768,384]{1,0:T(8,128)(2,1)} %copy-done.37), channel_id=1, source_target_pairs={{0,1},{1,0},{2,3},{3,2},{4,5},{5,4},{6,7},{7,6},{8,9},{9,8},{10,11... | collective-permute-start | bytes 1769480 | tf_op jit(solution)/shard_map/ppermute | solution.py:810
  548.2 26.0 %collective-permute-start.48 = (bf16[12,1024,128]{2,1,0:T(8,128)(2,1)}, bf16[12,1024,128]{2,1,0:T(8,128)(2,1)S(1)}, u32[]{:S(2)}, u32[]{:S(2)}) collective-permute-start(bf16[12,1024,128]{2,1,0:T(8,128)(2,1)} %get-tuple-element.578), channel_id=1, source_target_pairs={{0,1},{1,0},{2,3},{3,2},{4,5},{5,4},{6,7},{7,6},{8,9},{9,8},{10,11... | collective-permute-start | bytes 9437192 | tf_op jit(solution)/shard_map/ppermute | solution.py:810
  551.3 22.3 %collective-permute-start.47 = (bf16[384,1024]{1,0:T(8,128)(2,1)S(1)}, bf16[384,1024]{1,0:T(8,128)(2,1)S(1)}, u32[]{:S(2)}, u32[]{:S(2)}) collective-permute-start(bf16[384,1024]{1,0:T(8,128)(2,1)S(1)} %add_convert_fusion.7), channel_id=1, source_target_pairs={{0,4},{1,5},{2,6},{3,7},{4,0},{5,1},{6,2},{7,3},{8,12},{9,13},{10,... | collective-permute-start | bytes 2359304 | tf_op jit(solution)/shard_map/ppermute | solution.py:810
  574.3 25.4 %collective-permute-start.52 = (bf16[2,512,768]{2,1,0:T(8,128)(2,1)S(1)}, bf16[2,512,768]{2,1,0:T(8,128)(2,1)S(1)}, u32[]{:S(2)}, u32[]{:S(2)}) collective-permute-start(bf16[2,512,768]{2,1,0:T(8,128)(2,1)S(1)} %get-tuple-element.602), channel_id=1, source_target_pairs={{0,1},{1,0},{2,3},{3,2},{4,5},{5,4},{6,7},{7,6},{8,9},{9,8},{10,11... | collective-permute-start | bytes 4718600 | tf_op jit(solution)/shard_map/ppermute | solution.py:810
  575.7 22.9 %collective-permute-start.49 = (bf16[384,1024]{1,0:T(8,128)(2,1)}, bf16[384,1024]{1,0:T(8,128)(2,1)}, u32[]{:S(2)}, u32[]{:S(2)}) collective-permute-start(bf16[384,1024]{1,0:T(8,128)(2,1)} %add_convert_fusion.6), channel_id=1, source_target_pairs={{0,24},{1,25},{2,26},{3,27},{4,28},{5,29},{6,30},{7,31},{8,0},{9,1... | collective-permute-start | bytes 2359304 | tf_op jit(solution)/shard_map/ppermute | solution.py:814
  599.6 24.9 %collective-permute-start.56 = (bf16[3072,384]{1,0:T(8,128)(2,1)S(1)}, bf16[3072,384]{1,0:T(8,128)(2,1)S(1)}, u32[]{:S(2)}, u32[]{:S(2)}) collective-permute-start(bf16[3072,384]{1,0:T(8,128)(2,1)S(1)} %get-tuple-element.622), channel_id=1, source_target_pairs={{0,1},{1,0},{2,3},{3,2},{4,5},{5,4},{6,7},{7,6},{8,9},{9,8},{10,11... | collective-permute-start | bytes 7077896 | tf_op jit(solution)/shard_map/ppermute | solution.py:810
  602.6 21.6 %collective-permute-start.53 = (bf16[384,1024]{1,0:T(8,128)(2,1)}, bf16[384,1024]{1,0:T(8,128)(2,1)}, u32[]{:S(2)}, u32[]{:S(2)}) collective-permute-start(bf16[384,1024]{1,0:T(8,128)(2,1)} %add_convert_fusion.3), channel_id=1, source_target_pairs={{0,24},{1,25},{2,26},{3,27},{4,28},{5,29},{6,30},{7,31},{8,0},{9,1... | collective-permute-start | bytes 2359304 | tf_op jit(solution)/shard_map/ppermute | solution.py:814
  624.6 27.5 %collective-permute-start.60 = (bf16[768,1536]{1,0:T(8,128)(2,1)}, bf16[768,1536]{1,0:T(8,128)(2,1)}, u32[]{:S(2)}, u32[]{:S(2)}) collective-permute-start(bf16[768,1536]{1,0:T(8,128)(2,1)} %get-tuple-element.650), channel_id=1, source_target_pairs={{0,1},{1,0},{2,3},{3,2},{4,5},{5,4},{6,7},{7,6},{8,9},{9,8},{10,11... | collective-permute-start | bytes 7077896 | tf_op jit(solution)/shard_map/ppermute | solution.py:810
  627.5 23.2 %collective-permute-start.58 = (bf16[384,1024]{1,0:T(8,128)(2,1)}, bf16[384,1024]{1,0:T(8,128)(2,1)}, u32[]{:S(2)}, u32[]{:S(2)}) collective-permute-start(bf16[384,1024]{1,0:T(8,128)(2,1)} %add_convert_fusion), channel_id=1, source_target_pairs={{0,2},{1,3},{2,0},{3,1},{4,6},{5,7},{6,4},{7,5},{8,10},{9,11},{10,... | collective-permute-start | bytes 2359304 | tf_op jit(solution)/shard_map/ppermute | solution.py:810
  (146 other events, 2218.9 us)

commit v4 on v3

--- a/solution.py
+++ b/solution.py
@@ -30,6 +30,7 @@
 FSIDE = FF // 2 // FSTEP
 TILE = 512
 SIDE = WIDTH // 2
+SPAN = 2 * HALF
 
 
 def dot(a, b, ca, cb):
@@ -109,12 +110,11 @@
     return lax.rem(sc[PLANE] + PLANES - k, PLANES)
 
 
-def head_spec(planes, rows, lanes):
+def plane_spec(planes, rows, lanes):
     def index(step, sc):
-        k = planes[0] + step // PHEADS * (planes[1] - planes[0])
-        return (plane_of(k, sc) * PHEADS + step % PHEADS, 0, 0)
-
-    return spec((1, rows, lanes), index)
+        return (plane_of(planes[0] + step * (planes[1] - planes[0]), sc), 0, 0)
+
+    return spec((PHEADS, rows, lanes), index)
 
 
 def anywhere(count):
@@ -143,12 +143,16 @@
 
     for slot in range(2):
 
-        @pl.when(step == slot * PHEADS)
+        @pl.when(step == slot)
         def _():
             for copy in plane_fetch(place, shards, raw, sems, slot):
                 copy.wait()
 
-    return step // PHEADS, pl.ds(pl.multiple_of(step % PHEADS * HROWS, HROWS), HROWS)
+    return step
+
+
+def head_rows(head):
+    return slice(head * HROWS, (head + 1) * HROWS)
 
 
 def fill_mask(sc, mask):
@@ -170,11 +174,13 @@
     shards, (v_own, v_far, *rest) = refs[:8], refs[8:]
     mixed, mean, raw, mask, sems = rest[2:] if carried else rest
     fill_mask(sc, mask)
-    slot, rows = take_plane(sc[PLACE], shards, raw, sems)
-    weights = jnp.exp(raw[slot, rows].astype(F32)).astype(BF16)
-    found = dot(weights, jnp.concatenate([v_own[0], v_far[0]], axis=1), 1, 0) * inverse_sums(sc, weights, mask)
-    mean[0] = found
-    mixed[0] = found.astype(BF16)
+    slot = take_plane(sc[PLACE], shards, raw, sems)
+    for head in range(PHEADS):
+        weights = jnp.exp(raw[slot, head_rows(head)].astype(F32)).astype(BF16)
+        values = jnp.concatenate([v_own[head], v_far[head]], axis=1)
+        found = dot(weights, values, 1, 0) * inverse_sums(sc, weights, mask)
+        mean[head] = found
+        mixed[head] = found.astype(BF16)
 
 
 def run_mix(sc, planes, shards, v_own, v_far, carry):
@@ -183,9 +189,9 @@
         partial(mix_kernel, bool(carry)),
         grid_spec=pltpu.PrefetchScalarGridSpec(
             num_scalar_prefetch=1,
-            grid=(2 * PHEADS,),
-            in_specs=anywhere(8) + [head_spec(planes, LMAX, 2 * HEAD)] * 2 + anywhere(len(carry)),
-            out_specs=[head_spec(planes, HROWS, 4 * HEAD)] * 2,
+            grid=(2,),
+            in_specs=anywhere(8) + [plane_spec(planes, LMAX, 2 * HEAD)] * 2 + anywhere(len(carry)),
+            out_specs=[plane_spec(planes, HROWS, 4 * HEAD)] * 2,
             scratch_shapes=[
                 pltpu.VMEM((2, 4 * SUBS * HALF, LMAX), BF16),
                 pltpu.VMEM((LMAX, 4 * HEAD), BF16),
@@ -208,15 +214,16 @@
 
 
 def row_valid(sc, step):
-    line = lax.broadcasted_iota(jnp.int32, (256, 1), 0)
-    item = line // HALF
+    line = lax.broadcasted_iota(jnp.int32, (4 * SPAN, 1), 0)
+    item = line // SPAN
+    row = step * SPAN + line % SPAN
     low = jnp.where(item == 0, sc[LENGTHS], sc[LENGTHS + 1])
     high = jnp.where(item == 2, sc[LENGTHS + 2], sc[LENGTHS + 3])
-    return 128 * step + HALF * sc[CORE] + line % HALF < jnp.where(item >= 2, high, low)
+    return 128 * (row // HALF) + HALF * sc[CORE] + row % HALF < jnp.where(item >= 2, high, low)
 
 
 def four_items(own, far):
-    return jnp.concatenate([own[:, 0, 0], far[:, 0]], axis=0).reshape(256, WIDTH)
+    return jnp.concatenate([own[:, :, 0], far[...]], axis=0).reshape(4 * SPAN, WIDTH)
 
 
 def pre_kernel(sc, tok, tok_far, cot, cot_far, heads, wo_own, wo_far, gain, mixed, resid, normed, grad, weight):
@@ -227,28 +234,28 @@
         for pair in range(HEADS // 2):
             both = jnp.concatenate([heads[2 * pair, :, lanes], heads[2 * pair + 1, :, lanes]], axis=1)
             mixed[item, :, pair * 128 : (pair + 1) * 128] = both
-    res = four_items(tok, tok_far).astype(F32) + dot(mixed[...].reshape(256, WIDTH), weight[...], 1, 0)
-    resid[...] = res.reshape(4, HALF, WIDTH)
+    res = four_items(tok, tok_far).astype(F32) + dot(mixed[...].reshape(4 * SPAN, WIDTH), weight[...], 1, 0)
+    resid[...] = res.reshape(4, SPAN, WIDTH)
     scale = lax.rsqrt(jnp.mean(res * res, axis=-1, keepdims=True) + EPSILON)
     valid = row_valid(sc, step)
-    normed[...] = jnp.where(valid, res * scale * gain[...], 0.0).astype(BF16).reshape(4, HALF, WIDTH)
+    normed[...] = jnp.where(valid, res * scale * gain[...], 0.0).astype(BF16).reshape(4, SPAN, WIDTH)
     masked = jnp.where(valid, four_items(cot, cot_far).astype(F32), 0.0)
-    grad[...] = masked.astype(BF16).reshape(4, HALF, WIDTH)
+    grad[...] = masked.astype(BF16).reshape(4, SPAN, WIDTH)
 
 
 def slab_spec(items=4):
-    return spec((items, HALF, WIDTH), lambda r, s: (0, r, 0))
+    return spec((items, SPAN, WIDTH), lambda r, s: (0, r, 0))
 
 
 def half_specs():
     return [
-        spec((2, 1, 1, HALF, WIDTH), lambda r, s: (0, r, s[CORE], 0, 0)),
-        spec((2, 1, HALF, WIDTH), lambda r, s: (0, r, 0, 0)),
+        spec((2, SPAN // HALF, 1, HALF, WIDTH), lambda r, s: (0, r, s[CORE], 0, 0)),
+        spec((2, SPAN // HALF, HALF, WIDTH), lambda r, s: (0, r, 0, 0)),
     ]
 
 
 def heads_spec():
-    return spec((HEADS, HALF, 4 * HEAD), lambda r, s: (0, r, 0))
+    return spec((HEADS, SPAN, 4 * HEAD), lambda r, s: (0, r, 0))
 
 
 def run_pre(sc, tokens, tokens_far, cotangent, cotangent_far, heads, wo, gain):
@@ -256,7 +263,7 @@
         pre_kernel,
         grid_spec=pltpu.PrefetchScalarGridSpec(
             num_scalar_prefetch=1,
-            grid=(RUNS,),
+            grid=(HROWS // SPAN,),
             in_specs=half_specs()
             + half_specs()
             + [heads_spec(), held((WIDTH, SIDE)), held((WIDTH, SIDE)), held((1, WIDTH))],
@@ -301,42 +308,41 @@
     return (0, lax.max(f - FSIDE, 0))
 
 
-def units_kernel(sc, normed, cot, up_own, up_far, dn_own, dn_far, active, up_grad, back, w_down):
+def units_kernel(sc, normed, cot, up_own, up_far, dn_own, dn_far, active, up_grad, back, w_up, w_down):
     step = pl.program_id(0)
     w_down[:, own_lanes(sc)] = dn_own[...]
     w_down[:, far_lanes(sc)] = dn_far[...]
 
-    def units(up_w):
-        for piece in range(ROWS // TILE):
-            rows = slice(piece * TILE, (piece + 1) * TILE)
-            up = dot(normed[rows], up_w[...], 1, 0)
-            square = up * up
-            bend = jnp.tanh(up * (0.7978845608028654 + (0.044715 * 0.7978845608028654) * square))
-            share = 0.5 + 0.5 * bend
-            act = up * share
-            active[rows] = act.astype(BF16)
-            slope = share + act * (1.0 - share) * (
-                2 * 0.7978845608028654 + (6 * 0.044715 * 0.7978845608028654) * square
-            )
-            low = (dot(cot[rows], w_down[...], 1, 1) * slope).astype(BF16)
-            up_grad[rows] = low
-            two_grad = dot(low, up_w[...], 1, 1)
-
-            @pl.when(step == 0)
-            def _():
-                back[rows] = two_grad
-
-            @pl.when(step > 0)
-            def _():
-                back[rows] += two_grad
-
     @pl.when(step < FSIDE)
     def _():
-        units(up_own)
+        w_up[...] = up_own[...]
 
     @pl.when(step >= FSIDE)
     def _():
-        units(up_far)
+        w_up[...] = up_far[...]
+
+    for piece in range(ROWS // TILE):
+        rows = slice(piece * TILE, (piece + 1) * TILE)
+        up = dot(normed[rows], w_up[...], 1, 0)
+        square = up * up
+        bend = jnp.tanh(up * (0.7978845608028654 + (0.044715 * 0.7978845608028654) * square))
+        share = 0.5 + 0.5 * bend
+        act = up * share
+        active[rows] = act.astype(BF16)
+        slope = share + act * (1.0 - share) * (
+            2 * 0.7978845608028654 + (6 * 0.044715 * 0.7978845608028654) * square
+        )
+        low = (dot(cot[rows], w_down[...], 1, 1) * slope).astype(BF16)
+        up_grad[rows] = low
+        two_grad = dot(low, w_up[...], 1, 1)
+
+        @pl.when(step == 0)
+        def _():
+            back[rows] = two_grad
+
+        @pl.when(step > 0)
+        def _():
+            back[rows] += two_grad
 
 
 def run_units(sc, normed, cotangent, up, down):
@@ -354,7 +360,7 @@
                 spec((FSTEP, SIDE), unit_rows),
             ],
             out_specs=[spec((ROWS, FSTEP), unit_columns), spec((ROWS, FSTEP), unit_columns), held((ROWS, WIDTH))],
-            scratch_shapes=[pltpu.VMEM((FSTEP, WIDTH), BF16)],
+            scratch_shapes=[pltpu.VMEM((WIDTH, FSTEP), BF16), pltpu.VMEM((FSTEP, WIDTH), BF16)],
         ),
         out_shape=[
             jax.ShapeDtypeStruct((ROWS, FF), BF16),
@@ -432,9 +438,9 @@
         w_down[:, own_lanes(sc)] = dn_own[...]
         w_down[:, far_lanes(sc)] = dn_far[...]
 
-    branch = dot(active[...].reshape(256, FF), w_down[...], 1, 0)
-    output = jnp.where(row_valid(sc, step), resid[...].reshape(256, WIDTH) + branch, 0.0)
-    output = output.reshape(4, HALF, WIDTH)
+    branch = dot(active[...].reshape(4 * SPAN, FF), w_down[...], 1, 0)
+    output = jnp.where(row_valid(sc, step), resid[...].reshape(4 * SPAN, WIDTH) + branch, 0.0)
+    output = output.reshape(4, SPAN, WIDTH)
     own[...] = output[:2]
     far[...] = output[2:].astype(BF16)
 
@@ -444,9 +450,9 @@
         out_kernel,
         grid_spec=pltpu.PrefetchScalarGridSpec(
             num_scalar_prefetch=1,
-            grid=(RUNS,),
+            grid=(HROWS // SPAN,),
             in_specs=[
-                spec((4, HALF, FF), lambda r, s: (0, r, 0)),
+                spec((4, SPAN, FF), lambda r, s: (0, r, 0)),
                 slab_spec(),
                 held((FF, SIDE)),
                 held((FF, SIDE)),
@@ -470,7 +476,7 @@
     (res_own, res_far, heads, d_out_own, d_out_far, d_gain, weight, total, spread) = refs
     step = pl.program_id(0)
     whole_weight(sc, step, wo_own, wo_far, weight)
-    shape, slab = (256, WIDTH), (4, HALF, WIDTH)
+    shape, slab = (4 * SPAN, WIDTH), (4, SPAN, WIDTH)
     valid = row_valid(sc, step)
     res = resid[...].reshape(shape)
     scale = lax.rsqrt(jnp.mean(res * res, axis=-1, keepdims=True) + EPSILON)
@@ -517,14 +523,14 @@
         post_kernel,
         grid_spec=pltpu.PrefetchScalarGridSpec(
             num_scalar_prefetch=1,
-            grid=(RUNS,),
+            grid=(HROWS // SPAN,),
             in_specs=[slab_spec()] * 4 + [held((WIDTH, SIDE)), held((WIDTH, SIDE)), held((1, WIDTH))],
             out_specs=[slab_spec(2)] * 2
             + [heads_spec(), held((WIDTH, SIDE)), held((WIDTH, SIDE)), held((1, WIDTH))],
             scratch_shapes=[
                 pltpu.VMEM((WIDTH, WIDTH), BF16),
                 pltpu.VMEM((WIDTH, WIDTH), F32),
-                pltpu.VMEM((4, HALF, WIDTH), BF16),
+                pltpu.VMEM((4, SPAN, WIDTH), BF16),
             ],
         ),
         out_shape=[
@@ -546,7 +552,7 @@
 def unmix_kernel(carried, sc, *refs):
     shards, (v_own, v_far, grad_heads, mean, *rest) = refs[:8], refs[8:]
     rest = rest[2:] if carried else rest
-    outs, (own, far, raw, grads, mask, sems, out_sems) = rest[:8], rest[8:]
+    outs, (own, far, raw, grads, mask, adder, bound, sems, out_sems) = rest[:8], rest[8:]
     place = sc[PLACE]
     step = pl.program_id(0)
 
@@ -561,22 +567,39 @@
         ]
 
     fill_mask(sc, mask)
-    slot, rows = take_plane(place, shards, raw, sems)
-    weights = jnp.exp(raw[slot, rows].astype(F32)).astype(BF16)
-    low = (grad_heads[0].astype(F32) * inverse_sums(sc, weights, mask)).astype(BF16)
-    product = low.astype(F32) * mean[0]
-    score = dot(low, jnp.concatenate([v_own[0], v_far[0]], axis=1), 1, 1)
-    column = lax.broadcasted_iota(jnp.int32, (1, LMAX), 1)
-    for item in range(4):
-        delta = jnp.sum(product[:, item * HEAD : (item + 1) * HEAD], axis=-1, keepdims=True)
-        score = score - delta * (column < sc[LENGTHS + item]).astype(F32)
-    grads[slot, rows] = (score * weights.astype(F32)).astype(BF16)
-    back = (dot(weights, low, 0, 0) * mask[...].astype(F32)).astype(BF16)
-    own[0] = back[:, : 2 * HEAD]
-    far[0] = back[:, 2 * HEAD :]
+
+    @pl.when(step == 0)
+    def _():
+        lane = lax.broadcasted_iota(jnp.int32, (4 * HEAD, 128), 0) // HEAD
+        column = lax.broadcasted_iota(jnp.int32, (4 * HEAD, 128), 1)
+        adder[...] = jnp.where((lane == column) | (lane + 4 == column), -1.0, 0.0).astype(BF16)
+        row = lax.broadcasted_iota(jnp.int32, (LMAX, 128), 0)
+        item = lax.broadcasted_iota(jnp.int32, (LMAX, 128), 1)
+        length = jnp.where(item % 4 == 0, sc[LENGTHS], sc[LENGTHS + 1])
+        length = jnp.where(item % 4 == 2, sc[LENGTHS + 2], length)
+        length = jnp.where(item % 4 == 3, sc[LENGTHS + 3], length)
+        bound[...] = jnp.where((item < 8) & (row < length), 1.0, 0.0).astype(BF16)
+
+    slot = take_plane(place, shards, raw, sems)
+    high_lanes = lax.broadcasted_iota(jnp.int32, (HROWS, 128), 1) < 4
+    for head in range(PHEADS):
+        weights = jnp.exp(raw[slot, head_rows(head)].astype(F32)).astype(BF16)
+        low = (grad_heads[head].astype(F32) * inverse_sums(sc, weights, mask)).astype(BF16)
+        product = low.astype(F32) * mean[head]
+        coarse = product.astype(BF16)
+        fine = (product - coarse.astype(F32)).astype(BF16)
+        delta = dot(coarse, adder[...], 1, 0) + dot(fine, adder[...], 1, 0)
+        coarse = delta.astype(BF16)
+        fine = (delta - coarse.astype(F32)).astype(BF16)
+        left = jnp.concatenate([low, jnp.where(high_lanes, coarse, fine)], axis=1)
+        score = dot(left, jnp.concatenate([v_own[head], v_far[head], bound[...]], axis=1), 1, 1)
+        grads[slot, head_rows(head)] = (score * weights.astype(F32)).astype(BF16)
+        back = (dot(weights, low, 0, 0) * mask[...].astype(F32)).astype(BF16)
+        own[head] = back[:, : 2 * HEAD]
+        far[head] = back[:, 2 * HEAD :]
     for which in range(2):
 
-        @pl.when(step == which * PHEADS + PHEADS - 1)
+        @pl.when(step == which)
         def _():
             for copy in leave(which):
                 copy.start()
@@ -591,16 +614,18 @@
         partial(unmix_kernel, bool(carry)),
         grid_spec=pltpu.PrefetchScalarGridSpec(
             num_scalar_prefetch=1,
-            grid=(2 * PHEADS,),
+            grid=(2,),
             in_specs=anywhere(8)
-            + [head_spec(planes, LMAX, 2 * HEAD)] * 2
-            + [head_spec(planes, HROWS, 4 * HEAD)] * 2
+            + [plane_spec(planes, LMAX, 2 * HEAD)] * 2
+            + [plane_spec(planes, HROWS, 4 * HEAD)] * 2
             + anywhere(len(carry)),
-            out_specs=anywhere(8) + [head_spec(planes, LMAX, 2 * HEAD)] * 2,
+            out_specs=anywhere(8) + [plane_spec(planes, LMAX, 2 * HEAD)] * 2,
             scratch_shapes=[
                 pltpu.VMEM((2, 4 * SUBS * HALF, LMAX), BF16),
                 pltpu.VMEM((2, 4 * SUBS * HALF, LMAX), BF16),
                 pltpu.VMEM((LMAX, 4 * HEAD), BF16),
+                pltpu.VMEM((4 * HEAD, 128), BF16),
+                pltpu.VMEM((LMAX, 128), BF16),
                 pltpu.SemaphoreType.DMA((2, 4)),
                 pltpu.SemaphoreType.DMA((2, 4)),
             ],
@@ -743,7 +768,7 @@
             num_scalar_prefetch=1,
             grid=(1,),
             in_specs=anywhere(16),
-            out_specs=anywhere(len(shapes)),
+            out_specs=[held(shape) for shape in shapes],
             scratch_shapes=[pltpu.SemaphoreType.DMA((16, len(moves)))],
         ),
         out_shape=[jax.ShapeDtypeStruct(shape, BF16) for shape in shapes],
@@ -774,32 +799,34 @@
     return run_place(sc, pieces, moves, [(FF, SIDE), (WIDTH, FF // 2), (WIDTH, SIDE)])
 
 
-def collect_kernel(sc, down, down_got, up, up_got, out, out_got, packed):
-    both = lambda a, b: (a.astype(F32) + b.astype(F32)).astype(BF16)
-    packed[0, 0:192] = both(down[...], down_got[...])
-    for j in range(4):
-        lanes = slice(j * SIDE, (j + 1) * SIDE)
-        packed[0, 192 + 48 * j : 240 + 48 * j] = both(up[:, lanes], up_got[:, lanes])
-    packed[0, 384:432] = both(out[...], out_got[...])
-
-
-def run_collect(sc, down, down_got, up, up_got, out, out_got):
-    chip = lambda i, s: (chip_of(s, i // 4, i % 4), 0)
-    rows = lambda x: spec((x.shape[0] // 16, x.shape[1]), chip)
-    args = (down, down_got, up, up_got, out, out_got)
+def collect_kernel(sc, *refs):
+    packed = refs[-1]
+    for rel in range(4):
+        down, down_got, up, up_got, out, out_got = refs[6 * rel : 6 * rel + 6]
+        packed[rel, PACK_DOWN:PACK_UP] = add_low(down[...], down_got[...])
+        for j in range(4):
+            lanes = slice(j * SIDE, (j + 1) * SIDE)
+            packed[rel, PACK_UP + 48 * j : PACK_UP + 48 * (j + 1)] = add_low(up[:, lanes], up_got[:, lanes])
+        packed[rel, PACK_OUT:] = add_low(out[...], out_got[...])
+
+
+def run_collect(sc, *sides):
+    def rows(x, rel):
+        return spec((x.shape[0] // 16, x.shape[1]), lambda k, s: (chip_of(s, k, rel), 0))
+
     return pl.pallas_call(
         collect_kernel,
         grid_spec=pltpu.PrefetchScalarGridSpec(
             num_scalar_prefetch=1,
-            grid=(16,),
-            in_specs=[rows(x) for x in args],
-            out_specs=spec((1, PACK, SIDE), lambda i, s: (i, 0, 0)),
+            grid=(PLANES,),
+            in_specs=[rows(x, rel) for rel in range(4) for x in sides],
+            out_specs=spec((4, PACK, SIDE), lambda k, s: (k, 0, 0)),
         ),
         out_shape=jax.ShapeDtypeStruct((16, PACK, SIDE), BF16),
-        compiler_params=params(16),
+        compiler_params=params(32),
         cost_estimate=pl.CostEstimate(flops=0, bytes_accessed=3 * 16 * PACK * SIDE * 2, transcendentals=0),
         name="collect",
-    )(sc, *args)
+    )(sc, *(x for _ in range(4) for x in sides))
 
 
 DEVICES = 32
@@ -963,55 +990,60 @@
         )
         return near, own, far, other(res_far), other(d_out_far)
 
-    def make_output(made):
+    def make_down(made):
         near, own, far, *rest = made
-        return near, own, other(far), *rest, *run_out(sc, active, resid, down)
-
-    def make_down(made):
-        *rest, out_own, out_far = made
-        return *rest, out_own, other(out_far), *run_down_grad(sc, active, masked)
+        return near, own, other(far), *rest, *run_down_grad(sc, active, masked)
 
     def make_up(made):
         *rest, down_own, down_far = made
-        return *rest, (down_own, other(down_far)), run_up_grad(sc, normed, up_grad)
+        return *rest, down_own, other(down_far), *run_up_grad(sc, normed, up_grad)
+
+    def share_up(made):
+        *rest, up_far = made
+        return *rest, other(up_far)
+
+    def pack(made):
+        _, own, got, res_got, d_out_got, *sides = made
+        return own, got, res_got, run_collect(sc, *sides, d_out_own, d_out_got)
+
+    rand_sum, made = scatter16(far, [unmix_near, make_down, make_up, share_up, pack])
+    back_own, back_got, res_got, packed = made
+
+    def make_output(_):
+        out_own, out_far = run_out(sc, active, resid, down)
+        blocks = rand_sum.reshape(2, 3, HALF, LMAX)
+        return pick(blocks, core), other(pick(blocks, 1 - core)), out_own, other(out_far)
 
     def finish(made):
-        _, own, got, res_got, d_out_got, out_own, out_got, down_sides, (up_own, up_far) = made
+        *blocks, out_own, out_got = made
         output, tokens_grad, d_value, d_gain_one = run_close(
-            sc, tokens, res_own, res_got, out_own, out_got, own, got, gain_one, value, value_far
+            sc, tokens, res_own, res_got, out_own, out_got, back_own, back_got, gain_one, value, value_far
         )
         gain_pair = jnp.concatenate([d_gain_one, d_gain_two]).reshape(2, 16, 1, 48).astype(BF16)
         gain_pair = jnp.pad(gain_pair, ((0, 0), (0, 0), (0, 15), (0, SIDE - 48)))
         small = jnp.concatenate([d_value.reshape(2, 16, 48, SIDE), gain_pair], 2)
-        return output, tokens_grad, small, (*down_sides, up_own, other(up_far), d_out_own, d_out_got)
-
-    rand_sum, made = scatter16(far, [unmix_near, make_output, make_down, make_up, finish])
-    output, tokens_grad, small, sides = made
-    packed = run_collect(sc, *sides)
-
-    def small_core(_):
-        return add_low(pick(small, core), other(pick(small, 1 - core))).reshape(4, 2, 2, 64, SIDE)
+        small = add_low(pick(small, core), other(pick(small, 1 - core))).reshape(4, 2, 2, 64, SIDE)
+        return *blocks, output, tokens_grad, small
 
     def small_line(made):
-        return add_low(pick(made, x, 2), swap(pick(made, 1 - x, 2), TO_X))
+        *kept, small = made
+        return *kept, add_low(pick(small, x, 2), swap(pick(small, 1 - x, 2), TO_X))
 
     def small_plane(made):
-        return add_low(pick(made, y, 1), swap(pick(made, 1 - y, 1), TO_Y))
+        *kept, small = made
+        return *kept, add_low(pick(small, y, 1), swap(pick(small, 1 - y, 1), TO_Y))
 
     def small_planes(made):
-        total = pick(made, z).astype(F32)
+        *kept, small = made
+        total = pick(small, z).astype(F32)
         for k in range(1, PLANES):
-            total = total + ring(pick(made, lax.rem(z + PLANES - k, PLANES)), -k).astype(F32)
-        return total
-
-    def rand_home(made):
-        blocks = rand_sum.reshape(2, 3, HALF, LMAX)
-        return made, pick(blocks, core), other(pick(blocks, 1 - core))
+            total = total + ring(pick(small, lax.rem(z + PLANES - k, PLANES)), -k).astype(F32)
+        return *kept, total
 
     big_sum, made = scatter16(
-        after([packed[i] for i in range(16)], rand_sum), [small_core, small_line, small_plane, small_planes, rand_home]
-    )
-    small_sum, blocks, blocks_far = made
+        after([packed[i] for i in range(16)], rand_sum), [make_output, finish, small_line, small_plane, small_planes]
+    )
+    blocks, blocks_far, output, tokens_grad, small_sum = made
     big_far, small_far = other(big_sum), other(small_sum)
 
     rows_of = lambda value, rows: pick(value.reshape(-1, 2, rows, SIDE), core, 1)

time: 754 us -> 561 us (0.74)
  Pallas kernels: 421 us -> 207 us
  waiting for transfers between devices: 163 us -> 181 us
    pallas_call x2, Pallas kernels: 190 us -> 9.56 us  [run_place(): pl.pallas_call(partial(place_kernel, moves), grid_spec=pltpu.PrefetchScal...]
    ppermute x23, waiting for transfers between devices: 64.4 us -> 86.4 us  [ring(): lax.ppermute(x, BOTH, [(d, (d + 8 * way) % DEVICES) for d in range(DEVICE...]
    pallas_call x2, Pallas kernels: 47.9 us -> 34.6 us  [run_unmix(): pl.pallas_call(partial(unmix_kernel, bool(carry)), grid_spec=pltpu.Prefet...]
    pallas_call x1, Pallas kernels: 57.4 us -> 49.3 us  [run_units(): pl.pallas_call(units_kernel, grid_spec=pltpu.PrefetchScalarGridSpec(num_s...]
    unnamed x179 -> x197, local copies, waits for them, and re-layouts: 33.4 us -> 37.4 us
  transfers between devices with their start and end apart: 85 -> 85, of which waited for: 39 -> 41; matrix products, arithmetic and copies ran while one was open for 6% -> 8% of each run, Pallas kernels for 21% -> 21%
where the time goes in v4:
time: 561 us; the launch traced here: 552 us
  Pallas kernels  207 us (37%)
  waiting for transfers between devices  181 us (32%)
  starting transfers between devices  75.7 us (13%)
  local copies, waits for them, and re-layouts  53.9 us (10%)
  other arithmetic  32.3 us (6%)
    ppermute x62, waiting for transfers between devices, swap(): return lax.ppermute(x, BOTH, [(d, d ^ bit) for d in range(DEVICES)])  94.7 us
    ppermute x23, waiting for transfers between devices, ring(): lax.ppermute(x, BOTH, [(d, (d + 8 * way) % DEVICES) for d in range(DEVICE...  86.4 us
    pallas_call x1, Pallas kernels, run_units(): pl.pallas_call(units_kernel, grid_spec=pltpu.PrefetchScalarGridSpec(num_s...  49.3 us
    ppermute x62, starting transfers between devices, swap(): return lax.ppermute(x, BOTH, [(d, d ^ bit) for d in range(DEVICES)])  48.2 us
    unnamed x197, local copies, waits for them, and re-layouts  37.4 us
    pallas_call x2, Pallas kernels, run_unmix(): pl.pallas_call(partial(unmix_kernel, bool(carry)), grid_spec=pltpu.Prefet...  34.6 us
    ppermute x23, starting transfers between devices, ring(): lax.ppermute(x, BOTH, [(d, (d + 8 * way) % DEVICES) for d in range(DEVICE...  27.5 us
    pallas_call x2, Pallas kernels, run_mix(): pl.pallas_call(partial(mix_kernel, bool(carry)), grid_spec=pltpu.Prefetch...  18.6 us
  transfers between devices with their start and end apart: 85, of which 41 were waited for; matrix products, arithmetic and copies ran while one was open for 8% of the time, Pallas kernels for 21%

profile of v4, /device:TPU:0, one launch (start us, length us, event | category | flops | bytes accessed | tf_op | source)
XLA Modules:
  0.0 552.1 jit_solution(16815179694342984431)
XLA Ops:
  24.3 16.0 %collective-permute-done.2.refs_1_.refs_5_ = bf16[416,1024]{1,0:T(8,128)(2,1)S(1)} collective-permute-done((bf16[416,1024]{1,0:T(8,128)(2,1)S(1)}, bf16[416,1024]{1,0:T(8,128)(2,1)S(1)}, u32[]{:S(2)}, u32[]{:S(2)}) %collective-permute-start.2) | collective-permute-done | bytes 852000 | tf_op jit(solution)/shard_map/ppermute | solution.py:837
  46.1 20.1 %collective-permute-done.10.refs_8_.refs_0_.refs_4_ = bf16[416,1024]{1,0:T(8,128)(2,1)S(1)} collective-permute-done((bf16[416,1024]{1,0:T(8,128)(2,1)S(1)}, bf16[416,1024]{1,0:T(8,128)(2,1)S(1)}, u32[]{:S(2)}, u32[]{:S(2)}) %collective-permute-start.10) | collective-permute-done | bytes 852000 | tf_op jit(solution)/shard_map/ppermute | solution.py:841
  67.6 17.2 %collective-permute-done.11.refs_6_.refs_2_ = bf16[416,1024]{1,0:T(8,128)(2,1)S(1)} collective-permute-done((bf16[416,1024]{1,0:T(8,128)(2,1)S(1)}, bf16[416,1024]{1,0:T(8,128)(2,1)S(1)}, u32[]{:S(2)}, u32[]{:S(2)}) %collective-permute-start.11) | collective-permute-done | bytes 852000 | tf_op jit(solution)/shard_map/ppermute | solution.py:837
  90.2 16.5 %collective-permute-done.14.refs_7_.refs_3_ = bf16[416,1024]{1,0:T(8,128)(2,1)S(1)} collective-permute-done((bf16[416,1024]{1,0:T(8,128)(2,1)S(1)}, bf16[416,1024]{1,0:T(8,128)(2,1)S(1)}, u32[]{:S(2)}, u32[]{:S(2)}) %collective-permute-start.14) | collective-permute-done | bytes 852000 | tf_op jit(solution)/shard_map/ppermute | solution.py:841
  109.9 14.3 %collective-permute-done.17.refs_11_.refs_3_.refs_7_ = bf16[416,1024]{1,0:T(8,128)(2,1)} collective-permute-done((bf16[416,1024]{1,0:T(8,128)(2,1)}, bf16[416,1024]{1,0:T(8,128)(2,1)}, u32[]{:S(2)}, u32[]{:S(2)}) %collective-permute-start.17) | collective-permute-done | bytes 852000 | tf_op jit(solution)/shard_map/ppermute | solution.py:837
  137.1 5.2 values.1.refs_8_
  145.9 8.2 %collective-permute-done.24.refs_3_ = bf16[432,384]{1,0:T(8,128)(2,1)S(1)} collective-permute-done((bf16[432,384]{1,0:T(8,128)(2,1)S(1)}, bf16[432,384]{1,0:T(8,128)(2,1)S(1)}, u32[]{:S(2)}, u32[]{:S(2)}) %collective-permute-start.24) | collective-permute-done | bytes 331808 | tf_op jit(solution)/shard_map/ppermute | solution.py:837
  161.4 9.3 %mix.2 = (bf16[12,512,256]{2,1,0:T(8,128)(2,1)}, f32[12,512,256]{2,1,0:T(8,128)}) custom-call(s32[7]{0:T(128)} %concatenate.72.sc, bf16[416,1024]{1,0:T(8,128)(2,1)} %copy-done.35, bf16[416,1024]{1,0:T(8,128)(2,1)} %copy-done.36, bf16[416,1024]{1,0:T(8,128)(2,1)} %copy-done.37, bf16[416,1024]{1,0:T(8,128)(2,1)} %copy-done.39, bf16[416,1024]{1,0:T(8,128)(2,1)} %copy-done.38, ...), custom_call_target="tpu_custom_call" | custom-call | flops 3221225472 | bytes 14155776 | tf_op jit(solution)/shard_map/mix/pallas_call | solution.py:188
  173.7 9.3 %mix.3 = (bf16[12,512,256]{2,1,0:T(8,128)(2,1)}, f32[12,512,256]{2,1,0:T(8,128)}) custom-call(s32[7]{0:T(128)} %concatenate.72.sc, bf16[416,1024]{1,0:T(8,128)(2,1)} %copy-done.43, bf16[416,1024]{1,0:T(8,128)(2,1)} %copy-done.44, bf16[416,1024]{1,0:T(8,128)(2,1)} %collective-permute-done.15.refs_10_.refs_2_.refs_6_, ...), custom_call_target="tpu_custom_call", output_to_operand_aliasing={{0}: (11, {}), {1}: (12, {})} | custom-call | flops 3221225472 | bytes 14155776 | tf_op jit(solution)/shard_map/mix/pallas_call | solution.py:188
  195.2 6.5 %place.3 = (bf16[3072,384]{1,0:T(8,128)(2,1)}, bf16[768,1536]{1,0:T(8,128)(2,1)}, bf16[768,384]{1,0:T(8,128)(2,1)}) custom-call(s32[7]{0:T(128)} %concatenate.72.sc, bf16[432,384]{1,0:T(8,128)(2,1)} %pad_maximum_fusion.1.refs_0_, bf16[432,384]{1,0:T(8,128)(2,1)} %copy-done.81, bf16[432,384]{1,0:T(8,128)(2,1)} %collective-permute-done.21.refs_2_, ...), custom_call_target="tpu_custom_call" | custom-call | bytes 10616832 | tf_op jit(solution)/shard_map/place/pallas_call | solution.py:765
  202.3 8.4 %collective-permute-done.37.wo_far = bf16[768,384]{1,0:T(8,128)(2,1)S(1)} collective-permute-done((bf16[768,384]{1,0:T(8,128)(2,1)}, bf16[768,384]{1,0:T(8,128)(2,1)S(1)}, u32[]{:S(2)}, u32[]{:S(2)}) %collective-permute-start.37) | collective-permute-done | bytes 589856 | tf_op jit(solution)/shard_map/ppermute | solution.py:837
  216.5 10.0 %pre.1 = (bf16[4,512,768]{2,1,0:T(8,128)(2,1)S(1)}, f32[4,512,768]{2,1,0:T(8,128)}, bf16[4,512,768]{2,1,0:T(8,128)(2,1)S(1)}, bf16[4,512,768]{2,1,0:T(8,128)(2,1)S(1)}) custom-call(s32[7]{0:T(128)S(1)} %copy-done.22, bf16[2,8,2,64,768]{4,3,2,1,0:T(8,128)(2,1)S(1)} %bitcast.153, bf16[2,8,64,768]{3,2,1,0:T(8,128)(2,1)S(1)} %copy-done.14, ...), custom_call_target="tpu_custom_call" | custom-call | flops 2415919104 | bytes 25165824 | tf_op jit(solution)/shard_map/pre/pallas_call | solution.py:262
  233.7 49.3 %units.1 = (bf16[2048,3072]{1,0:T(8,128)(2,1)}, bf16[2048,3072]{1,0:T(8,128)(2,1)}, f32[2048,768]{1,0:T(8,128)}) custom-call(s32[7]{0:T(128)} %concatenate.72.sc, bf16[2048,768]{1,0:T(8,128)(2,1)} %bitcast.162, bf16[2048,768]{1,0:T(8,128)(2,1)} %bitcast.157, bf16[768,1536]{1,0:T(8,128)(2,1)} %get-tuple-element.543.up_own, bf16[768,1536]{1,0:T(8,128)(2,1)} %copy-done.91, ...), custom_call_target="tpu_custom_call" | custom-call | flops 28991029248 | bytes 37748736 | tf_op jit(solution)/shard_map/units/pallas_call | solution.py:349
  283.0 17.4 %post.1 = (f32[2,512,768]{2,1,0:T(8,128)S(1)}, bf16[2,512,768]{2,1,0:T(8,128)(2,1)}, bf16[12,512,256]{2,1,0:T(8,128)(2,1)S(1)}, bf16[768,384]{1,0:T(8,128)(2,1)S...) custom-call(s32[7]{0:T(128)S(1)} %copy-done.23, f32[4,512,768]{2,1,0:T(8,128)} %get-tuple-element.540.resid, ...), custom_call_target="tpu_custom_call" | custom-call | flops 4831838208 | bytes 44040192 | tf_op jit(solution)/shard_map/post/pallas_call | solution.py:522
  304.6 17.2 %unmix.2 = (bf16[384,1024]{1,0:T(8,128)(2,1)}, bf16[384,1024]{1,0:T(8,128)(2,1)}, bf16[384,1024]{1,0:T(8,128)(2,1)}, bf16[384,1024]{1,0:T(8,128)(2,1)}, bf16[384...) custom-call(s32[7]{0:T(128)} %concatenate.72.sc, ...), custom_call_target="tpu_custom_call" | custom-call | flops 4831838208 | bytes 31457280 | tf_op jit(solution)/shard_map/unmix/pallas_call | solution.py:613
  326.1 17.4 %unmix.3 = (bf16[384,1024]{1,0:T(8,128)(2,1)}, bf16[384,1024]{1,0:T(8,128)(2,1)}, bf16[384,1024]{1,0:T(8,128)(2,1)}, bf16[384,1024]{1,0:T(8,128)(2,1)}, bf16[384...) custom-call(s32[7]{0:T(128)} %concatenate.72.sc, ...), custom_call_target="tpu_custom_call", output_to_operand_aliasing={{8}: (13, {}), {9}: (14, {})} | custom-call | flops 4831838208 | bytes 31457280 | tf_op jit(solution)/shard_map/unmix/pallas_call | solution.py:613
  352.6 14.6 %down_grad.1 = (bf16[3072,384]{1,0:T(8,128)(2,1)S(1)}, bf16[3072,384]{1,0:T(8,128)(2,1)S(1)}) custom-call(s32[7]{0:T(128)S(1)} %copy-done.24, bf16[2048,3072]{1,0:T(8,128)(2,1)} %get-tuple-element.591.active, bf16[2048,768]{1,0:T(8,128)(2,1)} %bitcast.158), custom_call_target="tpu_custom_call" | custom-call | flops 9663676416 | bytes 15728640 | tf_op jit(solution)/shard_map/down_grad/pallas_call | solution.py:385
  378.6 14.9 %up_grad.1 = (bf16[768,1536]{1,0:T(8,128)(2,1)S(1)}, bf16[768,1536]{1,0:T(8,128)(2,1)S(1)}) custom-call(s32[7]{0:T(128)S(1)} %copy-done.24, bf16[2048,768]{1,0:T(8,128)(2,1)} %bitcast.163, bf16[2048,3072]{1,0:T(8,128)(2,1)} %get-tuple-element.613.up_grad), custom_call_target="tpu_custom_call" | custom-call | flops 9663676416 | bytes 15728640 | tf_op jit(solution)/shard_map/up_grad/pallas_call | solution.py:416
  404.4 14.8 %collective-permute-done.53 = bf16[384,1024]{1,0:T(8,128)(2,1)S(1)} collective-permute-done((bf16[384,1024]{1,0:T(8,128)(2,1)S(1)}, bf16[384,1024]{1,0:T(8,128)(2,1)S(1)}, u32[]{:S(2)}, u32[]{:S(2)}) %collective-permute-start.53) | collective-permute-done | bytes 786464 | tf_op jit(solution)/shard_map/ppermute | solution.py:841
  427.2 15.8 %out.1 = (f32[2,512,768]{2,1,0:T(8,128)}, bf16[2,512,768]{2,1,0:T(8,128)(2,1)S(1)}) custom-call(s32[7]{0:T(128)S(1)} %copy-done.24, bf16[4,512,3072]{2,1,0:T(8,128)(2,1)} %bitcast.196, f32[4,512,768]{2,1,0:T(8,128)} %get-tuple-element.540.resid, bf16[3072,384]{1,0:T(8,128)(2,1)S(1)} %copy-done.30, bf16[3072,384]{1,0:T(8,128)(2,1)} %copy-done.90), custom_call_target="tpu_custom_call" | custom-call | flops 9663676416 | bytes 23592960 | tf_op jit(solution)/shard_map/out/pallas_call | solution.py:449
  455.1 7.5 %collective-permute-done.60 = bf16[432,384]{1,0:T(8,128)(2,1)S(1)} collective-permute-done((bf16[432,384]{1,0:T(8,128)(2,1)S(1)}, bf16[432,384]{1,0:T(8,128)(2,1)S(1)}, u32[]{:S(2)}, u32[]{:S(2)}) %collective-permute-start.60) | collective-permute-done | bytes 331808 | tf_op jit(solution)/shard_map/ppermute | solution.py:841
  464.7 14.9 %close.1 = (f32[2,8,2,64,768]{4,3,2,1,0:T(8,128)}, f32[2,8,2,64,768]{4,3,2,1,0:T(8,128)}, bf16[2,768,384]{2,1,0:T(8,128)(2,1)S(1)}, f32[1,768]{1,0:T(1,128)S(1)}) custom-call(s32[7]{0:T(128)S(1)} %copy-done.24, bf16[2,8,2,64,768]{4,3,2,1,0:T(8,128)(2,1)} %bitcast.151, f32[2,8,64,768]{3,2,1,0:T(8,128)} %bitcast.156, bf16[2,8,64,768]{3,2,1,0:T(8,128)(2,1)S(1)} %bitcast.159, ...), custom_call_target="tpu_custom_call" | custom-call | flops 4831838208 | bytes 29884416 | tf_op jit(solution)/shard_map/close/pallas_call | solution.py:702
  486.4 5.2 collective-permute-done.67
  533.3 5.3 collective-permute-done.82
  (436 shorter events, 214.5 us)
Async XLA Ops:
  11.7 33.2 %collective-permute-start.6 = (bf16[2,8,64,768]{3,2,1,0:T(8,128)(2,1)}, bf16[2,8,64,768]{3,2,1,0:T(8,128)(2,1)S(1)}, u32[]{:S(2)}, u32[]{:S(2)}) collective-permute-start(bf16[2,8,64,768]{3,2,1,0:T(8,128)(2,1)} %dynamic-slice_bitcast_fusion.1), channel_id=1, source_target_pairs={{0,1},{1,0},{2,3},{3,2},{4,5},{5,4},{6,7},{7,6},{8,9},{9,8},{10,11... | collective-permute-start | bytes 4718600 | tf_op jit(solution)/shard_map/ppermute | solution.py:837
  14.2 30.7 %collective-permute-start.7 = (bf16[2,8,64,768]{3,2,1,0:T(8,128)(2,1)}, bf16[2,8,64,768]{3,2,1,0:T(8,128)(2,1)S(1)}, u32[]{:S(2)}, u32[]{:S(2)}) collective-permute-start(bf16[2,8,64,768]{3,2,1,0:T(8,128)(2,1)} %dynamic-slice_bitcast_fusion), channel_id=1, source_target_pairs={{0,1},{1,0},{2,3},{3,2},{4,5},{5,4},{6,7},{7,6},{8,9},{9,8},{10,11... | collective-permute-start | bytes 4718600 | tf_op jit(solution)/shard_map/ppermute | solution.py:837
  18.2 22.1 %collective-permute-start.2 = (bf16[416,1024]{1,0:T(8,128)(2,1)S(1)}, bf16[416,1024]{1,0:T(8,128)(2,1)S(1)}, u32[]{:S(2)}, u32[]{:S(2)}) collective-permute-start(bf16[416,1024]{1,0:T(8,128)(2,1)S(1)} %pad_maximum_fusion.refs_0_.refs_4_), channel_id=1, source_target_pairs={{0,2},{1,3},{2,0},{3,1},{4,6},{5,7},{6,4},{7,5},{8,10},{9,11},{10,... | collective-permute-start | bytes 2555912 | tf_op jit(solution)/shard_map/ppermute | solution.py:837
  21.2 20.6 %collective-permute-start.3 = (bf16[416,1024]{1,0:T(8,128)(2,1)S(1)}, bf16[416,1024]{1,0:T(8,128)(2,1)S(1)}, u32[]{:S(2)}, u32[]{:S(2)}) collective-permute-start(bf16[416,1024]{1,0:T(8,128)(2,1)S(1)} %pad_maximum_fusion.refs_0_.refs_4_), channel_id=1, source_target_pairs={{0,4},{1,5},{2,6},{3,7},{4,0},{5,1},{6,2},{7,3},{8,12},{9,13},{10,... | collective-permute-start | bytes 2555912 | tf_op jit(solution)/shard_map/ppermute | solution.py:837
  22.7 22.2 %collective-permute-start.4 = (bf16[416,1024]{1,0:T(8,128)(2,1)S(1)}, bf16[416,1024]{1,0:T(8,128)(2,1)S(1)}, u32[]{:S(2)}, u32[]{:S(2)}) collective-permute-start(bf16[416,1024]{1,0:T(8,128)(2,1)S(1)} %pad_maximum_fusion.refs_0_.refs_4_), channel_id=1, source_target_pairs={{0,8},{1,9},{2,10},{3,11},{4,12},{5,13},{6,14},{7,15},{8,16},{9,17... | collective-permute-start | bytes 2555912 | tf_op jit(solution)/shard_map/ppermute | solution.py:841
  44.9 21.3 %collective-permute-start.10 = (bf16[416,1024]{1,0:T(8,128)(2,1)S(1)}, bf16[416,1024]{1,0:T(8,128)(2,1)S(1)}, u32[]{:S(2)}, u32[]{:S(2)}) collective-permute-start(bf16[416,1024]{1,0:T(8,128)(2,1)S(1)} %collective-permute-done.4.refs_4_.refs_0_), channel_id=1, source_target_pairs={{0,8},{1,9},{2,10},{3,11},{4,12},{5,13},{6,14},{7,15},{8,16},{9,17... | collective-permute-start | bytes 2555912 | tf_op jit(solution)/shard_map/ppermute | solution.py:841
  45.0 21.2 %collective-permute-start.8 = (bf16[416,1024]{1,0:T(8,128)(2,1)S(1)}, bf16[416,1024]{1,0:T(8,128)(2,1)S(1)}, u32[]{:S(2)}, u32[]{:S(2)}) collective-permute-start(bf16[416,1024]{1,0:T(8,128)(2,1)S(1)} %collective-permute-done.2.refs_1_.refs_5_), channel_id=1, source_target_pairs={{0,4},{1,5},{2,6},{3,7},{4,0},{5,1},{6,2},{7,3},{8,12},{9,13},{10,... | collective-permute-start | bytes 2555912 | tf_op jit(solution)/shard_map/ppermute | solution.py:837
  45.6 20.7 %collective-permute-start.9 = (bf16[416,1024]{1,0:T(8,128)(2,1)S(1)}, bf16[416,1024]{1,0:T(8,128)(2,1)S(1)}, u32[]{:S(2)}, u32[]{:S(2)}) collective-permute-start(bf16[416,1024]{1,0:T(8,128)(2,1)S(1)} %collective-permute-done.4.refs_4_.refs_0_), channel_id=1, source_target_pairs={{0,2},{1,3},{2,0},{3,1},{4,6},{5,7},{6,4},{7,5},{8,10},{9,11},{10,... | collective-permute-start | bytes 2555912 | tf_op jit(solution)/shard_map/ppermute | solution.py:837
  67.6 20.0 %collective-permute-start.13 = (bf16[416,1024]{1,0:T(8,128)(2,1)S(1)}, bf16[416,1024]{1,0:T(8,128)(2,1)S(1)}, u32[]{:S(2)}, u32[]{:S(2)}) collective-permute-start(bf16[416,1024]{1,0:T(8,128)(2,1)S(1)} %collective-permute-done.10.refs_8_.refs_0_.refs_4_), channel_id=1, source_target_pairs={{0,8},{1,9},{2,10},{3,11},{4,12},{5,13},{6,14},{7,15},{8,16},{9,17... | collective-permute-start | bytes 2555912 | tf_op jit(solution)/shard_map/ppermute | solution.py:841
  201.7 29.8 %collective-permute-start.38 = (bf16[768,1536]{1,0:T(8,128)(2,1)}, bf16[768,1536]{1,0:T(8,128)(2,1)S(1)}, u32[]{:S(2)}, u32[]{:S(2)}) collective-permute-start(bf16[768,1536]{1,0:T(8,128)(2,1)} %get-tuple-element.543.up_own), channel_id=1, source_target_pairs={{0,1},{1,0},{2,3},{3,2},{4,5},{5,4},{6,7},{7,6},{8,9},{9,8},{10,11... | collective-permute-start | bytes 7077896 | tf_op jit(solution)/shard_map/ppermute | solution.py:837
  201.8 29.8 %collective-permute-start.39 = (bf16[3072,384]{1,0:T(8,128)(2,1)}, bf16[3072,384]{1,0:T(8,128)(2,1)S(1)}, u32[]{:S(2)}, u32[]{:S(2)}) collective-permute-start(bf16[3072,384]{1,0:T(8,128)(2,1)} %get-tuple-element.544.dn_own), channel_id=1, source_target_pairs={{0,1},{1,0},{2,3},{3,2},{4,5},{5,4},{6,7},{7,6},{8,9},{9,8},{10,11... | collective-permute-start | bytes 7077896 | tf_op jit(solution)/shard_map/ppermute | solution.py:837
  304.5 39.6 %collective-permute-start.43 = (bf16[2,512,768]{2,1,0:T(8,128)(2,1)}, bf16[2,512,768]{2,1,0:T(8,128)(2,1)S(1)}, u32[]{:S(2)}, u32[]{:S(2)}) collective-permute-start(bf16[2,512,768]{2,1,0:T(8,128)(2,1)} %get-tuple-element.569), channel_id=1, source_target_pairs={{0,1},{1,0},{2,3},{3,2},{4,5},{5,4},{6,7},{7,6},{8,9},{9,8},{10,11... | collective-permute-start | bytes 4718600 | tf_op jit(solution)/shard_map/ppermute | solution.py:837
  321.9 21.6 %collective-permute-start.40 = (bf16[384,1024]{1,0:T(8,128)(2,1)}, bf16[384,1024]{1,0:T(8,128)(2,1)S(1)}, u32[]{:S(2)}, u32[]{:S(2)}) collective-permute-start(bf16[384,1024]{1,0:T(8,128)(2,1)} %get-tuple-element.549), channel_id=1, source_target_pairs={{0,24},{1,25},{2,26},{3,27},{4,28},{5,29},{6,30},{7,31},{8,0},{9,1... | collective-permute-start | bytes 2359304 | tf_op jit(solution)/shard_map/ppermute | solution.py:841
  324.0 19.9 %collective-permute-start.41 = (bf16[384,1024]{1,0:T(8,128)(2,1)}, bf16[384,1024]{1,0:T(8,128)(2,1)}, u32[]{:S(2)}, u32[]{:S(2)}) collective-permute-start(bf16[384,1024]{1,0:T(8,128)(2,1)} %get-tuple-element.550), channel_id=1, source_target_pairs={{0,2},{1,3},{2,0},{3,1},{4,6},{5,7},{6,4},{7,5},{8,10},{9,11},{10,... | collective-permute-start | bytes 2359304 | tf_op jit(solution)/shard_map/ppermute | solution.py:837
  344.4 25.1 %collective-permute-start.48 = (bf16[12,1024,128]{2,1,0:T(8,128)(2,1)}, bf16[12,1024,128]{2,1,0:T(8,128)(2,1)S(1)}, u32[]{:S(2)}, u32[]{:S(2)}) collective-permute-start(bf16[12,1024,128]{2,1,0:T(8,128)(2,1)} %get-tuple-element.588), channel_id=1, source_target_pairs={{0,1},{1,0},{2,3},{3,2},{4,5},{5,4},{6,7},{7,6},{8,9},{9,8},{10,11... | collective-permute-start | bytes 9437192 | tf_op jit(solution)/shard_map/ppermute | solution.py:837
  347.1 20.1 %collective-permute-start.47 = (bf16[384,1024]{1,0:T(8,128)(2,1)S(1)}, bf16[384,1024]{1,0:T(8,128)(2,1)S(1)}, u32[]{:S(2)}, u32[]{:S(2)}) collective-permute-start(bf16[384,1024]{1,0:T(8,128)(2,1)S(1)} %add_convert_fusion.7), channel_id=1, source_target_pairs={{0,4},{1,5},{2,6},{3,7},{4,0},{5,1},{6,2},{7,3},{8,12},{9,13},{10,... | collective-permute-start | bytes 2359304 | tf_op jit(solution)/shard_map/ppermute | solution.py:837
  371.2 26.0 %collective-permute-start.52 = (bf16[3072,384]{1,0:T(8,128)(2,1)S(1)}, bf16[3072,384]{1,0:T(8,128)(2,1)S(1)}, u32[]{:S(2)}, u32[]{:S(2)}) collective-permute-start(bf16[3072,384]{1,0:T(8,128)(2,1)S(1)} %get-tuple-element.612), channel_id=1, source_target_pairs={{0,1},{1,0},{2,3},{3,2},{4,5},{5,4},{6,7},{7,6},{8,9},{9,8},{10,11... | collective-permute-start | bytes 7077896 | tf_op jit(solution)/shard_map/ppermute | solution.py:837
  372.4 23.9 %collective-permute-start.49 = (bf16[384,1024]{1,0:T(8,128)(2,1)}, bf16[384,1024]{1,0:T(8,128)(2,1)}, u32[]{:S(2)}, u32[]{:S(2)}) collective-permute-start(bf16[384,1024]{1,0:T(8,128)(2,1)} %add_convert_fusion.6), channel_id=1, source_target_pairs={{0,24},{1,25},{2,26},{3,27},{4,28},{5,29},{6,30},{7,31},{8,0},{9,1... | collective-permute-start | bytes 2359304 | tf_op jit(solution)/shard_map/ppermute | solution.py:841
  376.5 20.0 %collective-permute-start.50 = (bf16[384,1024]{1,0:T(8,128)(2,1)}, bf16[384,1024]{1,0:T(8,128)(2,1)}, u32[]{:S(2)}, u32[]{:S(2)}) collective-permute-start(bf16[384,1024]{1,0:T(8,128)(2,1)} %get-tuple-element.596), channel_id=1, source_target_pairs={{0,2},{1,3},{2,0},{3,1},{4,6},{5,7},{6,4},{7,5},{8,10},{9,11},{10,... | collective-permute-start | bytes 2359304 | tf_op jit(solution)/shard_map/ppermute | solution.py:837
  397.1 24.0 %collective-permute-start.56 = (bf16[768,1536]{1,0:T(8,128)(2,1)}, bf16[768,1536]{1,0:T(8,128)(2,1)S(1)}, u32[]{:S(2)}, u32[]{:S(2)}) collective-permute-start(bf16[768,1536]{1,0:T(8,128)(2,1)} %copy-done.31), channel_id=1, source_target_pairs={{0,1},{1,0},{2,3},{3,2},{4,5},{5,4},{6,7},{7,6},{8,9},{9,8},{10,11... | collective-permute-start | bytes 7077896 | tf_op jit(solution)/shard_map/ppermute | solution.py:837
  399.1 20.1 %collective-permute-start.53 = (bf16[384,1024]{1,0:T(8,128)(2,1)S(1)}, bf16[384,1024]{1,0:T(8,128)(2,1)S(1)}, u32[]{:S(2)}, u32[]{:S(2)}) collective-permute-start(bf16[384,1024]{1,0:T(8,128)(2,1)S(1)} %add_convert_fusion.3), channel_id=1, source_target_pairs={{0,24},{1,25},{2,26},{3,27},{4,28},{5,29},{6,30},{7,31},{8,0},{9,1... | collective-permute-start | bytes 2359304 | tf_op jit(solution)/shard_map/ppermute | solution.py:841
  422.3 23.8 %collective-permute-start.58 = (bf16[384,1024]{1,0:T(8,128)(2,1)}, bf16[384,1024]{1,0:T(8,128)(2,1)}, u32[]{:S(2)}, u32[]{:S(2)}) collective-permute-start(bf16[384,1024]{1,0:T(8,128)(2,1)} %add_convert_fusion), channel_id=1, source_target_pairs={{0,2},{1,3},{2,0},{3,1},{4,6},{5,7},{6,4},{7,5},{8,10},{9,11},{10,... | collective-permute-start | bytes 2359304 | tf_op jit(solution)/shard_map/ppermute | solution.py:837
  424.8 21.3 %collective-permute-start.57 = (bf16[384,1024]{1,0:T(8,128)(2,1)}, bf16[384,1024]{1,0:T(8,128)(2,1)S(1)}, u32[]{:S(2)}, u32[]{:S(2)}) collective-permute-start(bf16[384,1024]{1,0:T(8,128)(2,1)} %add_convert_fusion.1), channel_id=1, source_target_pairs={{0,24},{1,25},{2,26},{3,27},{4,28},{5,29},{6,30},{7,31},{8,0},{9,1... | collective-permute-start | bytes 2359304 | tf_op jit(solution)/shard_map/ppermute | solution.py:841
  426.0 21.0 %collective-permute-start.59 = (bf16[384,1024]{1,0:T(8,128)(2,1)}, bf16[384,1024]{1,0:T(8,128)(2,1)}, u32[]{:S(2)}, u32[]{:S(2)}) collective-permute-start(bf16[384,1024]{1,0:T(8,128)(2,1)} %get-tuple-element.639), channel_id=1, source_target_pairs={{0,4},{1,5},{2,6},{3,7},{4,0},{5,1},{6,2},{7,3},{8,12},{9,13},{10,... | collective-permute-start | bytes 2359304 | tf_op jit(solution)/shard_map/ppermute | solution.py:837
  (155 other events, 1838.9 us)

commit v5 on v4

--- a/solution.py
+++ b/solution.py
@@ -17,7 +17,7 @@
 BOTH = ("wide", "narrow")
 BF16 = jnp.bfloat16
 F32 = jnp.float32
-MIB = 1 << 20
+VMEM = 61 << 20
 
 SUBS = 6
 RUNS = 8
@@ -50,7 +50,7 @@
 
 
 def params(limit):
-    return pltpu.CompilerParams(vmem_limit_bytes=limit * MIB)
+    return pltpu.CompilerParams(vmem_limit_bytes=limit)
 
 
 def whole_weight(sc, step, own, far, weight):
@@ -92,7 +92,7 @@
             scratch_shapes=[pltpu.VMEM((WIDTH, WIDTH), BF16)],
         ),
         out_shape=jax.ShapeDtypeStruct((HEADS, LMAX, 2 * HEAD), BF16),
-        compiler_params=params(32),
+        compiler_params=params(VMEM),
         cost_estimate=pl.CostEstimate(
             flops=2 * 2 * LMAX * WIDTH * WIDTH, bytes_accessed=8 * LMAX * WIDTH, transcendentals=0
         ),
@@ -124,7 +124,7 @@
 def plane_fetch(place, shards, raw, sems, slot):
     return [
         pltpu.make_async_copy(
-            shards[4 * slot + rel].at[pl.ds(0, SUBS * HALF)],
+            shards[4 * slot + rel],
             raw.at[slot, pl.ds(pl.multiple_of((place ^ rel) * SUBS * HALF, SUBS * HALF), SUBS * HALF)],
             sems.at[slot, rel],
         )
@@ -203,7 +203,7 @@
             jax.ShapeDtypeStruct((HEADS, HROWS, 4 * HEAD), F32),
         ],
         input_output_aliases={11 + i: i for i in range(len(carry))},
-        compiler_params=params(60),
+        compiler_params=params(VMEM),
         cost_estimate=pl.CostEstimate(
             flops=2 * HEADS * HROWS * LMAX * 4 * HEAD,
             bytes_accessed=HEADS * (HROWS * LMAX + 5 * HROWS * 256),
@@ -276,7 +276,7 @@
             jax.ShapeDtypeStruct((4, HROWS, WIDTH), BF16),
             jax.ShapeDtypeStruct((4, HROWS, WIDTH), BF16),
         ],
-        compiler_params=params(32),
+        compiler_params=params(VMEM),
         cost_estimate=pl.CostEstimate(
             flops=2 * ROWS * WIDTH * WIDTH, bytes_accessed=16 * ROWS * WIDTH, transcendentals=0
         ),
@@ -367,7 +367,7 @@
             jax.ShapeDtypeStruct((ROWS, FF), BF16),
             jax.ShapeDtypeStruct((ROWS, WIDTH), F32),
         ],
-        compiler_params=params(56),
+        compiler_params=params(VMEM),
         cost_estimate=pl.CostEstimate(
             flops=6 * ROWS * WIDTH * FF, bytes_accessed=8 * ROWS * WIDTH + 4 * ROWS * FF, transcendentals=ROWS * FF
         ),
@@ -392,7 +392,7 @@
             scratch_shapes=[pltpu.VMEM((512, WIDTH), BF16)],
         ),
         out_shape=[jax.ShapeDtypeStruct((FF, SIDE), BF16)] * 2,
-        compiler_params=params(48),
+        compiler_params=params(VMEM),
         cost_estimate=pl.CostEstimate(
             flops=2 * ROWS * WIDTH * FF, bytes_accessed=2 * ROWS * (WIDTH + FF), transcendentals=0
         ),
@@ -422,7 +422,7 @@
             out_specs=[spec((WIDTH, FSTEP), early), spec((WIDTH, FSTEP), late)],
         ),
         out_shape=[jax.ShapeDtypeStruct((WIDTH, FF // 2), BF16)] * 2,
-        compiler_params=params(48),
+        compiler_params=params(VMEM),
         cost_estimate=pl.CostEstimate(
             flops=2 * ROWS * WIDTH * FF, bytes_accessed=2 * ROWS * (WIDTH + FF), transcendentals=0
         ),
@@ -464,7 +464,7 @@
             jax.ShapeDtypeStruct((2, HROWS, WIDTH), F32),
             jax.ShapeDtypeStruct((2, HROWS, WIDTH), BF16),
         ],
-        compiler_params=params(48),
+        compiler_params=params(VMEM),
         cost_estimate=pl.CostEstimate(
             flops=2 * ROWS * WIDTH * FF, bytes_accessed=ROWS * (2 * FF + 7 * WIDTH), transcendentals=0
         ),
@@ -541,7 +541,7 @@
             jax.ShapeDtypeStruct((WIDTH, SIDE), BF16),
             jax.ShapeDtypeStruct((1, WIDTH), F32),
         ],
-        compiler_params=params(40),
+        compiler_params=params(VMEM),
         cost_estimate=pl.CostEstimate(
             flops=4 * ROWS * WIDTH * WIDTH, bytes_accessed=28 * ROWS * WIDTH, transcendentals=0
         ),
@@ -633,7 +633,7 @@
         out_shape=[jax.ShapeDtypeStruct((SUBS * HALF, LMAX), BF16)] * 8
         + [jax.ShapeDtypeStruct((HEADS, LMAX, 2 * HEAD), BF16)] * 2,
         input_output_aliases={13 + i: 8 + i for i in range(len(carry))},
-        compiler_params=params(60),
+        compiler_params=params(VMEM),
         cost_estimate=pl.CostEstimate(
             flops=3 * HEADS * HROWS * LMAX * 4 * HEAD,
             bytes_accessed=HEADS * (2 * HROWS * LMAX + 4 * HROWS * 256 + 4 * LMAX * 256),
@@ -716,7 +716,7 @@
             jax.ShapeDtypeStruct((2, WIDTH, SIDE), BF16),
             jax.ShapeDtypeStruct((1, WIDTH), F32),
         ],
-        compiler_params=params(48),
+        compiler_params=params(VMEM),
         cost_estimate=pl.CostEstimate(
             flops=4 * 2 * LMAX * WIDTH * WIDTH, bytes_accessed=38 * LMAX * WIDTH, transcendentals=0
         ),
@@ -733,8 +733,42 @@
     )
 
 
-PACK_DOWN, PACK_UP, PACK_OUT, PACK = 0, 192, 384, 432
-SHARE = SUBS * HALF + 32
+PACK_DOWN, PACK_UP, PACK_OUT, PACK_VALUE, PACK_GAIN, PACK = 0, 192, 384, 432, 480, 496
+
+
+def pack_kernel(sc, down, up, out, value, gain, down_far, up_far, out_far, value_far, gain_far, packed):
+    first = sc[CORE] == 0
+
+    def both(own, far, lanes):
+        own, far = own[:, lanes], far[:, lanes]
+        return jnp.concatenate([jnp.where(first, own, far), jnp.where(first, far, own)], axis=0)
+
+    def side(own, far):
+        return both(own, far, own_lanes(sc))
+
+    packed[PACK_DOWN:PACK_UP] = side(down, down_far)
+    for j in range(4):
+        lanes = pl.ds(pl.multiple_of((4 * sc[CORE] + j) * SIDE, 128), SIDE)
+        packed[PACK_UP + 48 * j : PACK_UP + 48 * (j + 1)] = both(up, up_far, lanes)
+    packed[PACK_OUT:PACK_VALUE] = side(out, out_far)
+    packed[PACK_VALUE:PACK_GAIN] = side(value, value_far)
+    packed[PACK_GAIN:] = both(gain, gain_far, slice(0, SIDE))
+
+
+def run_pack(sc, own, far):
+    return pl.pallas_call(
+        pack_kernel,
+        grid_spec=pltpu.PrefetchScalarGridSpec(
+            num_scalar_prefetch=1,
+            grid=(1,),
+            in_specs=[held(x.shape) for x in (*own, *far)],
+            out_specs=held((PACK, SIDE)),
+        ),
+        out_shape=jax.ShapeDtypeStruct((PACK, SIDE), BF16),
+        compiler_params=params(VMEM),
+        cost_estimate=pl.CostEstimate(flops=0, bytes_accessed=6 * PACK * SIDE, transcendentals=0),
+        name="pack",
+    )(sc, *own, *far)
 
 
 def chip_of(sc, k, rel):
@@ -772,22 +806,12 @@
             scratch_shapes=[pltpu.SemaphoreType.DMA((16, len(moves)))],
         ),
         out_shape=[jax.ShapeDtypeStruct(shape, BF16) for shape in shapes],
-        compiler_params=params(60),
+        compiler_params=params(VMEM),
         cost_estimate=pl.CostEstimate(
             flops=0, bytes_accessed=4 * sum(a * b for a, b in shapes), transcendentals=0
         ),
         name="place",
     )(sc, *pieces)
-
-
-def place_values(sc, shares):
-    start = SUBS * HALF
-    moves = (
-        (start, 32, 0, 0, 48, 0, 0),
-        (start, 16, SIDE, 0, 48, 32, 0),
-        (start + 16, 16, SIDE, 1, 16, 0, 0),
-    )
-    return run_place(sc, shares, moves, [(WIDTH, SIDE), (256, SIDE)])
 
 
 def place_weights(sc, pieces):
@@ -795,8 +819,11 @@
         (PACK_DOWN, 192, 0, 0, 192, 0, 0),
         *((PACK_UP + 48 * j, 48, 0, 1, 48, 0, j * SIDE) for j in range(4)),
         (PACK_OUT, 48, 0, 2, 48, 0, 0),
-    )
-    return run_place(sc, pieces, moves, [(FF, SIDE), (WIDTH, FF // 2), (WIDTH, SIDE)])
+        (PACK_VALUE, 48, 0, 3, 48, 0, 0),
+        (PACK_GAIN, 16, 0, 4, 16, 0, 0),
+    )
+    shapes = [(FF, SIDE), (WIDTH, FF // 2), (WIDTH, SIDE), (WIDTH, SIDE), (256, SIDE)]
+    return run_place(sc, pieces, moves, shapes)
 
 
 def collect_kernel(sc, *refs):
@@ -807,7 +834,7 @@
         for j in range(4):
             lanes = slice(j * SIDE, (j + 1) * SIDE)
             packed[rel, PACK_UP + 48 * j : PACK_UP + 48 * (j + 1)] = add_low(up[:, lanes], up_got[:, lanes])
-        packed[rel, PACK_OUT:] = add_low(out[...], out_got[...])
+        packed[rel, PACK_OUT:PACK_VALUE] = add_low(out[...], out_got[...])
 
 
 def run_collect(sc, *sides):
@@ -820,11 +847,11 @@
             num_scalar_prefetch=1,
             grid=(PLANES,),
             in_specs=[rows(x, rel) for rel in range(4) for x in sides],
-            out_specs=spec((4, PACK, SIDE), lambda k, s: (k, 0, 0)),
-        ),
-        out_shape=jax.ShapeDtypeStruct((16, PACK, SIDE), BF16),
-        compiler_params=params(32),
-        cost_estimate=pl.CostEstimate(flops=0, bytes_accessed=3 * 16 * PACK * SIDE * 2, transcendentals=0),
+            out_specs=spec((4, PACK_VALUE, SIDE), lambda k, s: (k, 0, 0)),
+        ),
+        out_shape=jax.ShapeDtypeStruct((16, PACK_VALUE, SIDE), BF16),
+        compiler_params=params(VMEM),
+        cost_estimate=pl.CostEstimate(flops=0, bytes_accessed=3 * 16 * PACK_VALUE * SIDE * 2, transcendentals=0),
         name="collect",
     )(sc, *(x for _ in range(4) for x in sides))
 
@@ -862,52 +889,44 @@
 )
 
 
-def gather16(own, works=(), made=()):
-    have = {(0, 0, 0): own}
-    for step, (by_x, by_y, by_z) in enumerate(STEPS):
-        got = {
-            by_z: ring(have[by_z[0] - 1, by_z[1], by_z[2]]),
-            by_x: swap(have[by_x[0], by_x[1], 0], TO_X),
-            by_y: swap(have[by_y[0], 0, by_y[2]], TO_Y),
-        }
-        if step < len(works):
-            made = works[step](made)
-        have, made = lax.optimization_barrier(({**have, **got}, made))
-    return [have[k, y, x] for k in range(4) for y in range(2) for x in range(2)], made
-
-
-def scatter16(shares, works=(), made=()):
-    have = {}
-
-    def put(planes, values):
-        for index, value in enumerate(values):
-            have[planes[index // 4], index // 2 % 2, index % 2] = value
-
-    put((0, 1, 2, 3) if len(shares) == 16 else (3, 2), shares)
-    for step, (by_x, by_y, by_z) in enumerate(reversed(STEPS)):
-        got = [
-            ((by_z[0] - 1, by_z[1], by_z[2]), ring(have[by_z], -1)),
-            ((by_x[0], by_x[1], 0), swap(have[by_x], TO_X)),
-            ((by_y[0], 0, by_y[2]), swap(have[by_y], TO_Y)),
-        ]
-        for at in (by_x, by_y, by_z):
-            del have[at]
-        if step < len(works):
-            made = works[step](made)
-        values, have, made = lax.optimization_barrier(([value for _, value in got], have, made))
-        if step == 0 and len(shares) == 8:
-            put((1, 0), made[0])
-        for at in dict.fromkeys(at for at, _ in got):
-            total = have[at].astype(F32)
-            for (target, _), value in zip(got, values):
-                if target == at:
-                    total = total + value.astype(F32)
-            have[at] = total if step == len(STEPS) - 1 else total.astype(BF16)
-    return have[0, 0, 0], made
-
-
-def after(x, *others):
-    return lax.optimization_barrier((x, others))[0]
+def gather_step(have, step):
+    by_x, by_y, by_z = STEPS[step]
+    return {
+        **have,
+        by_z: ring(have[by_z[0] - 1, by_z[1], by_z[2]]),
+        by_x: swap(have[by_x[0], by_x[1], 0], TO_X),
+        by_y: swap(have[by_y[0], 0, by_y[2]], TO_Y),
+    }
+
+
+def in_order(have):
+    return [have[k, y, x] for k in range(4) for y in range(2) for x in range(2)]
+
+
+def by_place(shares, planes=range(PLANES)):
+    return {(k, i // 2, i % 2): shares[4 * at + i] for at, k in enumerate(planes) for i in range(4)}
+
+
+def scatter_send(have, step):
+    by_x, by_y, by_z = STEPS[len(STEPS) - 1 - step]
+    got = (ring(have[by_z], -1), swap(have[by_x], TO_X), swap(have[by_y], TO_Y))
+    return {at: value for at, value in have.items() if at not in (by_x, by_y, by_z)}, got
+
+
+def scatter_add(have, got, step):
+    by_x, by_y, by_z = STEPS[len(STEPS) - 1 - step]
+    targets = ((by_z[0] - 1, by_z[1], by_z[2]), (by_x[0], by_x[1], 0), (by_y[0], 0, by_y[2]))
+    have = dict(have)
+    for at in dict.fromkeys(targets):
+        total = have[at].astype(F32)
+        for target, value in zip(targets, got):
+            if target == at:
+                total = total + value.astype(F32)
+        have[at] = total if step == len(STEPS) - 1 else total.astype(BF16)
+    return have
+
+
+together = lax.optimization_barrier
 
 
 def chip_shards(tokens, lengths, rand_mix, w_value, w_out, w_up, w_down, gain_mix, gain_ffn, grad_out):
@@ -916,134 +935,110 @@
     z, y, x = wide // 4, (wide // 2) % 2, wide % 2
     other = lambda value: swap(value, TO_CORE)
     side = partial(ordered, core, joined=jnp.concatenate)
+    slab = (2, RUNS, 2, HALF, WIDTH)
+    tokens, grad_out = tokens.reshape(slab), grad_out.reshape(slab)
 
     gains = jnp.pad(jnp.concatenate([gain_mix, gain_ffn])[None], ((0, 7), (0, SIDE - 48)))
-    halves = [
-        jnp.concatenate(
-            [
-                w_value[:, c * SIDE : (c + 1) * SIDE],
-                gains,
-                w_down[:, c * SIDE : (c + 1) * SIDE],
-                *[w_up[:, (4 * c + j) * SIDE : (4 * c + j + 1) * SIDE] for j in range(4)],
-                w_out[:, c * SIDE : (c + 1) * SIDE],
-            ]
-        )
-        for c in range(2)
-    ]
-    both = jnp.stack(halves)
-    joined = ordered(core, pick(both, core), other(pick(both, 1 - core)))
-    part_of = lambda start, rows: joined[:, start : start + rows].reshape(2 * rows, SIDE)
-    up_rows = joined[:, 128:224].reshape(2, 4, 24, SIDE).transpose(1, 0, 2, 3).reshape(192, SIDE)
-    packed = jnp.concatenate([part_of(32, 96), up_rows, part_of(224, 24)])
-    first = jnp.concatenate([part_of(0, 24), part_of(24, 8)])
-    first = jnp.pad(jnp.concatenate([first[:32], first[32:]], axis=1), ((0, 0), (0, LMAX - WIDTH)))
+    own = (w_down, w_up, w_out, w_value, gains)
+    far = tuple(other(value) for value in own)
+    near_sc = jnp.concatenate([jnp.stack([core, z, wide % 4]).astype(jnp.int32), lengths, lengths])
+    weights = {(0, 0, 0): run_pack(near_sc, own, far)}
+
     rand = rand_mix.reshape(3, 2, HALF, LMAX)
     blocks = side(pick(rand, core, 1), other(pick(rand, 1 - core, 1)), 0)
-    share = jnp.concatenate([blocks.reshape(SUBS * HALF, LMAX), first])
-    share, packed = lax.optimization_barrier((share, packed))
-
-    slab = (2, RUNS, 2, HALF, WIDTH)
-    tokens, grad_out = tokens.reshape(slab), grad_out.reshape(slab)
-
-    def from_other(_):
-        return other(lengths), other(pick(tokens, 1 - core, 2)), other(pick(grad_out, 1 - core, 2))
-
-    shares, (far_lengths, tokens_far, grad_far) = gather16(share, [from_other])
-    sc = jnp.concatenate([jnp.stack([core, z, wide % 4]).astype(jnp.int32), lengths, far_lengths])
-
-    def make_values(_):
-        value, gain_rows = place_values(sc, shares)
-        value_far = other(value)
-        gain_rows = gain_rows.reshape(16, 2, 8, SIDE)[:, :, 0]
-        gain_one = gain_rows[..., :24].reshape(1, WIDTH).astype(F32)
-        gain_two = gain_rows[..., 24:48].reshape(1, WIDTH).astype(F32)
-        v_own = run_values(sc, tokens.reshape(2, LMAX, WIDTH), gain_one, value, value_far)
-        return value, value_far, gain_one, gain_two, v_own
-
-    def share_values(made):
-        return *made, other(made[-1])
-
-    def mix_near(made):
-        return *made, run_mix(sc, (0, 1), shares[:8], made[-2], made[-1], ())
-
-    def mix_far(made):
-        *made, near = made
-        return *made, run_mix(sc, (2, 3), shares[8:], made[-2], made[-1], near)
-
-    pieces, made = gather16(after(packed, *shares[-3:]), [make_values, share_values, mix_near, mix_far])
-    value, value_far, gain_one, gain_two, v_own, v_far, (heads, mean) = made
-    down, up, out = place_weights(sc, pieces)
-    down, up, out = (down, other(down)), (up, other(up)), (out, other(out))
+    weights, (rands, far_lengths) = together(
+        (gather_step(weights, 0), ({(0, 0, 0): blocks.reshape(SUBS * HALF, LMAX)}, other(lengths)))
+    )
+    sc = jnp.concatenate([near_sc[:5], far_lengths])
+
+    rands, weights, tokens_far = together(
+        (gather_step(rands, 0), gather_step(gather_step(weights, 1), 2), other(pick(tokens, 1 - core, 2)))
+    )
+    rands, weights, grad_far = together(
+        (gather_step(rands, 1), gather_step(gather_step(weights, 3), 4), other(pick(grad_out, 1 - core, 2)))
+    )
+    down, up, out, value, gain_rows = place_weights(sc, in_order(weights))
+    value_far = other(value)
+    gain_rows = gain_rows.reshape(16, 2, 8, SIDE)[:, :, 0]
+    gain_one = gain_rows[..., :24].reshape(1, WIDTH).astype(F32)
+    gain_two = gain_rows[..., 24:48].reshape(1, WIDTH).astype(F32)
+    v_own = run_values(sc, tokens.reshape(2, LMAX, WIDTH), gain_one, value, value_far)
+    rands, value_far, v_own, gain_one, gain_two, out, down, up = together(
+        (gather_step(rands, 2), value_far, v_own, gain_one, gain_two, out, down, up)
+    )
+    rands, v_far, out, down = together(
+        (gather_step(rands, 3), other(v_own), (out, other(out)), (down, other(down)))
+    )
+    mixing = run_mix(sc, (0, 1), in_order({**rands, (2, 1, 1): 0, (3, 1, 0): 0, (3, 1, 1): 0})[:8], v_own, v_far, ())
+    rands, up, mixing = together((gather_step(rands, 4), (up, other(up)), mixing))
+    shares = in_order(rands)
+    heads, mean = run_mix(sc, (2, 3), shares[8:], v_own, v_far, mixing)
 
     mixed, resid, normed, masked = run_pre(sc, tokens, tokens_far, grad_out, grad_far, heads, out, gain_two)
     active, up_grad, back = run_units(sc, normed, masked, up, down)
     res_own, res_far, grad_heads, d_out_own, d_out_far, d_gain_two = run_post(
         sc, resid, back, masked, mixed, out, gain_two
     )
+
     *far, back_own, back_far = run_unmix(
         sc, (3, 2), shares[12:] + shares[8:12], v_own, v_far, grad_heads, mean, ()
     )
-
-    def unmix_near(_):
-        *near, own, far = run_unmix(
-            sc, (1, 0), shares[4:8] + shares[:4], v_own, v_far, grad_heads, mean, (back_own, back_far)
-        )
-        return near, own, far, other(res_far), other(d_out_far)
-
-    def make_down(made):
-        near, own, far, *rest = made
-        return near, own, other(far), *rest, *run_down_grad(sc, active, masked)
-
-    def make_up(made):
-        *rest, down_own, down_far = made
-        return *rest, down_own, other(down_far), *run_up_grad(sc, normed, up_grad)
-
-    def share_up(made):
-        *rest, up_far = made
-        return *rest, other(up_far)
-
-    def pack(made):
-        _, own, got, res_got, d_out_got, *sides = made
-        return own, got, res_got, run_collect(sc, *sides, d_out_own, d_out_got)
-
-    rand_sum, made = scatter16(far, [unmix_near, make_down, make_up, share_up, pack])
-    back_own, back_got, res_got, packed = made
-
-    def make_output(_):
-        out_own, out_far = run_out(sc, active, resid, down)
-        blocks = rand_sum.reshape(2, 3, HALF, LMAX)
-        return pick(blocks, core), other(pick(blocks, 1 - core)), out_own, other(out_far)
-
-    def finish(made):
-        *blocks, out_own, out_got = made
-        output, tokens_grad, d_value, d_gain_one = run_close(
-            sc, tokens, res_own, res_got, out_own, out_got, back_own, back_got, gain_one, value, value_far
-        )
-        gain_pair = jnp.concatenate([d_gain_one, d_gain_two]).reshape(2, 16, 1, 48).astype(BF16)
-        gain_pair = jnp.pad(gain_pair, ((0, 0), (0, 0), (0, 15), (0, SIDE - 48)))
-        small = jnp.concatenate([d_value.reshape(2, 16, 48, SIDE), gain_pair], 2)
-        small = add_low(pick(small, core), other(pick(small, 1 - core))).reshape(4, 2, 2, 64, SIDE)
-        return *blocks, output, tokens_grad, small
-
-    def small_line(made):
-        *kept, small = made
-        return *kept, add_low(pick(small, x, 2), swap(pick(small, 1 - x, 2), TO_X))
-
-    def small_plane(made):
-        *kept, small = made
-        return *kept, add_low(pick(small, y, 1), swap(pick(small, 1 - y, 1), TO_Y))
-
-    def small_planes(made):
-        *kept, small = made
-        total = pick(small, z).astype(F32)
-        for k in range(1, PLANES):
-            total = total + ring(pick(small, lax.rem(z + PLANES - k, PLANES)), -k).astype(F32)
-        return *kept, total
-
-    big_sum, made = scatter16(
-        after([packed[i] for i in range(16)], rand_sum), [make_output, finish, small_line, small_plane, small_planes]
-    )
-    blocks, blocks_far, output, tokens_grad, small_sum = made
+    have, got = scatter_send(by_place(far, (3, 2)), 0)
+    *near, back_own, back_far = run_unmix(
+        sc, (1, 0), shares[4:8] + shares[:4], v_own, v_far, grad_heads, mean, (back_own, back_far)
+    )
+    have, got, near, back_own, back_far, res_got, d_out_got = together(
+        (have, got, near, back_own, back_far, other(res_far), other(d_out_far))
+    )
+    have = {**scatter_add(have, got, 0), **by_place(near, (1, 0))}
+
+    have, got = scatter_send(have, 1)
+    up_own, up_far = run_up_grad(sc, normed, up_grad)
+    have, got, up_own, up_far, back_got = together((have, got, up_own, up_far, other(back_far)))
+    have = scatter_add(have, got, 1)
+
+    have, got = scatter_send(have, 2)
+    down_own, down_far = run_down_grad(sc, active, masked)
+    have, got, down_own, down_far, up_got = together((have, got, down_own, down_far, other(up_far)))
+    have = scatter_add(have, got, 2)
+
+    have, got = scatter_send(have, 3)
+    packed = run_collect(sc, down_own, other(down_far), up_own, up_got, d_out_own, d_out_got)
+    sums, sums_got = scatter_send(by_place([packed[i] for i in range(16)]), 0)
+    out_own, out_far = run_out(sc, active, resid, down)
+    have, got, sums, sums_got, out_own, out_far = together((have, got, sums, sums_got, out_own, out_far))
+    have, sums = scatter_add(have, got, 3), scatter_add(sums, sums_got, 0)
+
+    have, got = scatter_send(have, 4)
+    sums, sums_got = scatter_send(sums, 1)
+    sums, sums_got = scatter_send(scatter_add(sums, sums_got, 1), 2)
+    output, tokens_grad, d_value, d_gain_one = run_close(
+        sc, tokens, res_own, res_got, out_own, other(out_far), back_own, back_got, gain_one, value, value_far
+    )
+    gain_pair = jnp.concatenate([d_gain_one, d_gain_two]).reshape(2, 16, 1, 48).astype(BF16)
+    gain_pair = jnp.pad(gain_pair, ((0, 0), (0, 0), (0, 15), (0, SIDE - 48)))
+    small = jnp.concatenate([d_value.reshape(2, 16, 48, SIDE), gain_pair], 2)
+    small = add_low(pick(small, core), other(pick(small, 1 - core))).reshape(4, 2, 2, 64, SIDE)
+    have, got, sums, sums_got, small, output, tokens_grad = together(
+        (have, got, sums, sums_got, small, output, tokens_grad)
+    )
+    rand_sum = scatter_add(have, got, 4)[0, 0, 0].reshape(2, 3, HALF, LMAX)
+    sums = scatter_add(sums, sums_got, 2)
+
+    sums, sums_got = scatter_send(sums, 3)
+    small = add_low(pick(small, x, 2), swap(pick(small, 1 - x, 2), TO_X))
+    blocks, blocks_far = pick(rand_sum, core), other(pick(rand_sum, 1 - core))
+    sums, sums_got, small, blocks, blocks_far = together((sums, sums_got, small, blocks, blocks_far))
+    sums = scatter_add(sums, sums_got, 3)
+
+    sums, sums_got = scatter_send(sums, 4)
+    small = add_low(pick(small, y, 1), swap(pick(small, 1 - y, 1), TO_Y))
+    sums, sums_got, small = together((sums, sums_got, small))
+    big_sum = scatter_add(sums, sums_got, 4)[0, 0, 0]
+
+    small_sum = pick(small, z).astype(F32)
+    for k in range(1, PLANES):
+        small_sum = small_sum + ring(pick(small, lax.rem(z + PLANES - k, PLANES)), -k).astype(F32)
     big_far, small_far = other(big_sum), other(small_sum)
 
     rows_of = lambda value, rows: pick(value.reshape(-1, 2, rows, SIDE), core, 1)
@@ -1051,7 +1046,7 @@
     down_shard = mine(big_sum[PACK_DOWN:PACK_UP], big_far[PACK_DOWN:PACK_UP], 96)
     up_side = lambda value: rows_of(value[PACK_UP:PACK_OUT], 24).transpose(1, 0, 2).reshape(24, 4 * SIDE)
     up_shard = side(up_side(big_sum), up_side(big_far), 1)
-    outproj_shard = mine(big_sum[PACK_OUT:], big_far[PACK_OUT:], 24)
+    outproj_shard = mine(big_sum[PACK_OUT:PACK_VALUE], big_far[PACK_OUT:PACK_VALUE], 24)
     value_shard = mine(small_sum[:48], small_far[:48], 24)
     gains_pair = ordered(core, small_sum[48, :48], small_far[48, :48])
     gain_pair = pick(gains_pair.reshape(2, 2, 24), core, 1)

time: 561 us -> 545 us (0.971)
  local copies, waits for them, and re-layouts: 53.9 us -> 20.7 us
  Pallas kernels: 207 us -> 225 us
  starting transfers between devices: 75.7 us -> 68.4 us
  waiting for transfers between devices: 181 us -> 187 us
    unnamed x197 -> x136, local copies, waits for them, and re-layouts: 37.4 us -> 8.15 us
    ppermute x62 -> x66, waiting for transfers between devices: 94.7 us -> 119 us  [swap(): return lax.ppermute(x, BOTH, [(d, d ^ bit) for d in range(DEVICES)])]
    ppermute x23, waiting for transfers between devices: 86.4 us -> 68.5 us  [ring(): lax.ppermute(x, BOTH, [(d, (d + 8 * way) % DEVICES) for d in range(DEVICE...]
    convert_element_type x19, other arithmetic: 18.4 us -> 26.7 us  [the longest x18 26.6 us: scatter_add(): have[at] = total if step == len(STEPS) - 1 else total.astype(BF16)]
    ppermute x23, starting transfers between devices: 27.5 us -> 19.3 us  [ring(): lax.ppermute(x, BOTH, [(d, (d + 8 * way) % DEVICES) for d in range(DEVICE...]
    pallas_call x1, Pallas kernels: 1.92 us -> 7.9 us  [run_collect(): pl.pallas_call(collect_kernel, grid_spec=pltpu.PrefetchScalarGridSpec(num...]
    ppermute x62 -> x66, starting transfers between devices: 48.2 us -> 49.1 us  [swap(): return lax.ppermute(x, BOTH, [(d, d ^ bit) for d in range(DEVICES)])]
  transfers between devices with their start and end apart: 85 -> 89, of which waited for: 41 -> 43; matrix products, arithmetic and copies ran while one was open for 8% -> 8% of each run, Pallas kernels for 21% -> 24%
where the time goes in v5:
time: 545 us; the launch traced here: 539 us
  Pallas kernels  225 us (41%)
  waiting for transfers between devices  187 us (34%)
  starting transfers between devices  68.4 us (13%)
  other arithmetic  35.5 us (7%)
  local copies, waits for them, and re-layouts  20.7 us (4%)
    ppermute x66, waiting for transfers between devices, swap(): return lax.ppermute(x, BOTH, [(d, d ^ bit) for d in range(DEVICES)])  119 us
    ppermute x23, waiting for transfers between devices, ring(): lax.ppermute(x, BOTH, [(d, (d + 8 * way) % DEVICES) for d in range(DEVICE...  68.5 us
    ppermute x66, starting transfers between devices, swap(): return lax.ppermute(x, BOTH, [(d, d ^ bit) for d in range(DEVICES)])  49.1 us
    pallas_call x1, Pallas kernels, run_units(): pl.pallas_call(units_kernel, grid_spec=pltpu.PrefetchScalarGridSpec(num_s...  49 us
    pallas_call x2, Pallas kernels, run_unmix(): pl.pallas_call(partial(unmix_kernel, bool(carry)), grid_spec=pltpu.Prefet...  34.9 us
    convert_element_type x18, other arithmetic, scatter_add(): have[at] = total if step == len(STEPS) - 1 else total.astype(BF16)  26.6 us
    ppermute x23, starting transfers between devices, ring(): lax.ppermute(x, BOTH, [(d, (d + 8 * way) % DEVICES) for d in range(DEVICE...  19.3 us
    pallas_call x2, Pallas kernels, run_mix(): pl.pallas_call(partial(mix_kernel, bool(carry)), grid_spec=pltpu.Prefetch...  18.7 us
  transfers between devices with their start and end apart: 89, of which 43 were waited for; matrix products, arithmetic and copies ran while one was open for 8% of the time, Pallas kernels for 24%

profile of v5, /device:TPU:0, one launch (start us, length us, event | category | flops | bytes accessed | tf_op | source)
XLA Modules:
  0.0 538.8 jit_solution(16111454958557200772)
XLA Ops:
  27.7 10.1 %collective-permute-done.16.refs_8_ = bf16[496,384]{1,0:T(8,128)(2,1)S(1)} collective-permute-done((bf16[496,384]{1,0:T(8,128)(2,1)S(1)}, bf16[496,384]{1,0:T(8,128)(2,1)S(1)}, u32[]{:S(2)}, u32[]{:S(2)}) %collective-permute-start.16) | collective-permute-done | bytes 380960 | tf_op jit(solution)/shard_map/ppermute | solution.py:868
  39.8 6.7 %collective-permute-done.15.refs_6_ = bf16[496,384]{1,0:T(8,128)(2,1)S(1)} collective-permute-done((bf16[496,384]{1,0:T(8,128)(2,1)S(1)}, bf16[496,384]{1,0:T(8,128)(2,1)S(1)}, u32[]{:S(2)}, u32[]{:S(2)}) %collective-permute-start.15) | collective-permute-done | bytes 380960 | tf_op jit(solution)/shard_map/ppermute | solution.py:864
  49.8 13.6 %collective-permute-done.10.refs_1_.refs_5_ = bf16[384,1024]{1,0:T(8,128)(2,1)S(1)} collective-permute-done((bf16[384,1024]{1,0:T(8,128)(2,1)S(1)}, bf16[384,1024]{1,0:T(8,128)(2,1)S(1)}, u32[]{:S(2)}, u32[]{:S(2)}) %collective-permute-start.10) | collective-permute-done | bytes 786464 | tf_op jit(solution)/shard_map/ppermute | solution.py:864
  81.4 15.9 %collective-permute-done.23.refs_7_ = bf16[496,384]{1,0:T(8,128)(2,1)S(1)} collective-permute-done((bf16[496,384]{1,0:T(8,128)(2,1)S(1)}, bf16[496,384]{1,0:T(8,128)(2,1)S(1)}, u32[]{:S(2)}, u32[]{:S(2)}) %collective-permute-start.23) | collective-permute-done | bytes 380960 | tf_op jit(solution)/shard_map/ppermute | solution.py:868
  107.7 7.2 %place.1 = (bf16[3072,384]{1,0:T(8,128)(2,1)}, bf16[768,1536]{1,0:T(8,128)(2,1)}, bf16[768,384]{1,0:T(8,128)(2,1)}, bf16[768,384]{1,0:T(8,128)(2,1)}, bf16[256,384]{1,0:T(8,128)(2,1)}) custom-call(s32[7]{0:T(128)} %concatenate.54.sc, bf16[496,384]{1,0:T(8,128)(2,1)} %pack.1.refs_0_, bf16[496,384]{1,0:T(8,128)(2,1)} %copy-done.36, ...), custom_call_target="tpu_custom_call" | custom-call | bytes 12189696 | tf_op jit(solution)/shard_map/place/pallas_call | solution.py:799
  119.5 7.9 %values.1.refs_8_ = bf16[12,1024,128]{2,1,0:T(8,128)(2,1)} custom-call(s32[7]{0:T(128)} %concatenate.54.sc, bf16[2,1024,768]{2,1,0:T(8,128)(2,1)} %tok.1, f32[1,768]{1,0:T(1,128)} %reshape.205.gain, bf16[768,384]{1,0:T(8,128)(2,1)} %get-tuple-element.310.w_own, bf16[768,384]{1,0:T(8,128)(2,1)} %collective-permute-done.33.w_far), custom_call_target="tpu_custom_call" | custom-call | flops 2415919104 | bytes 6291456 | tf_op jit(solution)/shard_map/values/pallas_call | solution.py:80
  127.5 7.9 %collective-permute-done.30.refs_6_.refs_2_ = bf16[384,1024]{1,0:T(8,128)(2,1)} collective-permute-done((bf16[384,1024]{1,0:T(8,128)(2,1)}, bf16[384,1024]{1,0:T(8,128)(2,1)}, u32[]{:S(2)}, u32[]{:S(2)}) %collective-permute-start.30) | collective-permute-done | bytes 786464 | tf_op jit(solution)/shard_map/ppermute | solution.py:864
  139.3 8.6 %collective-permute-done.38.wo_far = bf16[768,384]{1,0:T(8,128)(2,1)S(1)} collective-permute-done((bf16[768,384]{1,0:T(8,128)(2,1)S(1)}, bf16[768,384]{1,0:T(8,128)(2,1)S(1)}, u32[]{:S(2)}, u32[]{:S(2)}) %collective-permute-start.38) | collective-permute-done | bytes 589856 | tf_op jit(solution)/shard_map/ppermute | solution.py:864
  149.4 10.8 %collective-permute-done.34.refs_7_.refs_3_ = bf16[384,1024]{1,0:T(8,128)(2,1)S(1)} collective-permute-done((bf16[384,1024]{1,0:T(8,128)(2,1)}, bf16[384,1024]{1,0:T(8,128)(2,1)S(1)}, u32[]{:S(2)}, u32[]{:S(2)}) %collective-permute-start.34) | collective-permute-done | bytes 786464 | tf_op jit(solution)/shard_map/ppermute | solution.py:868
  167.6 11.3 %collective-permute-done.36.refs_5_.refs_1_ = bf16[384,1024]{1,0:T(8,128)(2,1)} collective-permute-done((bf16[384,1024]{1,0:T(8,128)(2,1)S(1)}, bf16[384,1024]{1,0:T(8,128)(2,1)}, u32[]{:S(2)}, u32[]{:S(2)}) %collective-permute-start.36) | collective-permute-done | bytes 786464 | tf_op jit(solution)/shard_map/ppermute | solution.py:864
  182.3 9.3 %mix.2 = (bf16[12,512,256]{2,1,0:T(8,128)(2,1)}, f32[12,512,256]{2,1,0:T(8,128)}) custom-call(s32[7]{0:T(128)} %concatenate.54.sc, bf16[384,1024]{1,0:T(8,128)(2,1)} %bitcast.145, bf16[384,1024]{1,0:T(8,128)(2,1)} %copy-done.8, bf16[384,1024]{1,0:T(8,128)(2,1)} %copy-done.9, bf16[384,1024]{1,0:T(8,128)(2,1)} %copy-done.10, ...), custom_call_target="tpu_custom_call" | custom-call | flops 3221225472 | bytes 14155776 | tf_op jit(solution)/shard_map/mix/pallas_call | solution.py:188
  200.4 9.3 %mix.3 = (bf16[12,512,256]{2,1,0:T(8,128)(2,1)}, f32[12,512,256]{2,1,0:T(8,128)}) custom-call(s32[7]{0:T(128)} %concatenate.54.sc, bf16[384,1024]{1,0:T(8,128)(2,1)} %copy-done.4, bf16[384,1024]{1,0:T(8,128)(2,1)} %copy-done.5, bf16[384,1024]{1,0:T(8,128)(2,1)} %collective-permute-done.35.refs_2_.refs_6_, ...), custom_call_target="tpu_custom_call", output_to_operand_aliasing={{0}: (11, {}), {1}: (12, {})} | custom-call | flops 3221225472 | bytes 14155776 | tf_op jit(solution)/shard_map/mix/pallas_call | solution.py:188
  209.8 12.8 %pre.1 = (bf16[4,512,768]{2,1,0:T(8,128)(2,1)}, f32[4,512,768]{2,1,0:T(8,128)}, bf16[4,512,768]{2,1,0:T(8,128)(2,1)}, bf16[4,512,768]{2,1,0:T(8,128)(2,1)}) custom-call(s32[7]{0:T(128)} %concatenate.54.sc, bf16[2,8,2,64,768]{4,3,2,1,0:T(8,128)(2,1)} %bitcast.138, bf16[2,8,64,768]{3,2,1,0:T(8,128)(2,1)} %copy-done.15, bf16[2,8,2,64,768]{4,3,2,1,0:T(8,128)(2,1)} %bitcast.140, ...), custom_call_target="tpu_custom_call" | custom-call | flops 2415919104 | bytes 25165824 | tf_op jit(solution)/shard_map/pre/pallas_call | solution.py:262
  222.6 49.0 %units.1 = (bf16[2048,3072]{1,0:T(8,128)(2,1)}, bf16[2048,3072]{1,0:T(8,128)(2,1)}, f32[2048,768]{1,0:T(8,128)}) custom-call(s32[7]{0:T(128)} %concatenate.54.sc, bf16[2048,768]{1,0:T(8,128)(2,1)} %bitcast.176, bf16[2048,768]{1,0:T(8,128)(2,1)} %bitcast.151, bf16[768,1536]{1,0:T(8,128)(2,1)} %get-tuple-element.364.up_own, ...), custom_call_target="tpu_custom_call" | custom-call | flops 28991029248 | bytes 37748736 | tf_op jit(solution)/shard_map/units/pallas_call | solution.py:349
  271.6 18.4 %post.1 = (f32[2,512,768]{2,1,0:T(8,128)}, bf16[2,512,768]{2,1,0:T(8,128)(2,1)}, bf16[12,512,256]{2,1,0:T(8,128)(2,1)}, bf16[768,384]{1,0:T(8,128)(2,1)}, bf16[768,384]{1,0:T(8,128)(2,1)}, /*index=5*/f32[1,768]{1,0:T(1,128)}) custom-call(s32[7]{0:T(128)} %concatenate.54.sc, f32[4,512,768]{2,1,0:T(8,128)} %get-tuple-element.361.resid, ...), custom_call_target="tpu_custom_call" | custom-call | flops 4831838208 | bytes 44040192 | tf_op jit(solution)/shard_map/post/pallas_call | solution.py:522
  290.1 17.6 %unmix.2 = (bf16[384,1024]{1,0:T(8,128)(2,1)}, bf16[384,1024]{1,0:T(8,128)(2,1)}, bf16[384,1024]{1,0:T(8,128)(2,1)}, bf16[384,1024]{1,0:T(8,128)(2,1)}, bf16[384...) custom-call(s32[7]{0:T(128)} %concatenate.54.sc, ...), custom_call_target="tpu_custom_call" | custom-call | flops 4831838208 | bytes 31457280 | tf_op jit(solution)/shard_map/unmix/pallas_call | solution.py:613
  311.5 17.3 %unmix.3 = (bf16[384,1024]{1,0:T(8,128)(2,1)}, bf16[384,1024]{1,0:T(8,128)(2,1)}, bf16[384,1024]{1,0:T(8,128)(2,1)}, bf16[384,1024]{1,0:T(8,128)(2,1)}, bf16[384...) custom-call(s32[7]{0:T(128)} %concatenate.54.sc, ...), custom_call_target="tpu_custom_call", output_to_operand_aliasing={{8}: (13, {}), {9}: (14, {})} | custom-call | flops 4831838208 | bytes 31457280 | tf_op jit(solution)/shard_map/unmix/pallas_call | solution.py:613
  339.3 16.5 %up_grad.1 = (bf16[768,1536]{1,0:T(8,128)(2,1)}, bf16[768,1536]{1,0:T(8,128)(2,1)}) custom-call(s32[7]{0:T(128)} %concatenate.54.sc, bf16[2048,768]{1,0:T(8,128)(2,1)} %bitcast.177, bf16[2048,3072]{1,0:T(8,128)(2,1)} %get-tuple-element.418.up_grad), custom_call_target="tpu_custom_call" | custom-call | flops 9663676416 | bytes 15728640 | tf_op jit(solution)/shard_map/up_grad/pallas_call | solution.py:416
  365.5 15.6 %down_grad.1 = (bf16[3072,384]{1,0:T(8,128)(2,1)}, bf16[3072,384]{1,0:T(8,128)(2,1)}) custom-call(s32[7]{0:T(128)} %concatenate.54.sc, bf16[2048,3072]{1,0:T(8,128)(2,1)} %get-tuple-element.435.active, bf16[2048,768]{1,0:T(8,128)(2,1)} %bitcast.152), custom_call_target="tpu_custom_call" | custom-call | flops 9663676416 | bytes 15728640 | tf_op jit(solution)/shard_map/down_grad/pallas_call | solution.py:385
  391.2 7.9 %collect.1 = bf16[16,432,384]{2,1,0:T(8,128)(2,1)} custom-call(s32[7]{0:T(128)} %concatenate.54.sc, bf16[3072,384]{1,0:T(8,128)(2,1)} %get-tuple-element.449.refs_0_.refs_6_.refs_12_.refs_18_, bf16[3072,384]{1,0:T(8,128)(2,1)} %collective-permute-done.60.refs_1_.refs_7_.refs_13_.refs_19_, ...), custom_call_target="tpu_custom_call" | custom-call | bytes 15925248 | tf_op jit(solution)/shard_map/collect/pallas_call | solution.py:844
  409.9 16.7 %out.3 = (f32[2,512,768]{2,1,0:T(8,128)}, bf16[2,512,768]{2,1,0:T(8,128)(2,1)}) custom-call(s32[7]{0:T(128)} %concatenate.54.sc, bf16[4,512,3072]{2,1,0:T(8,128)(2,1)} %bitcast.178, f32[4,512,768]{2,1,0:T(8,128)} %get-tuple-element.361.resid, bf16[3072,384]{1,0:T(8,128)(2,1)} %get-tuple-element.366.dn_own, bf16[3072,384]{1,0:T(8,128)(2,1)} %copy-done.62), custom_call_target="tpu_custom_call" | custom-call | flops 9663676416 | bytes 23592960 | tf_op jit(solution)/shard_map/out/pallas_call | solution.py:449
  441.7 16.6 %close.1 = (f32[2,8,2,64,768]{4,3,2,1,0:T(8,128)}, f32[2,8,2,64,768]{4,3,2,1,0:T(8,128)}, bf16[2,768,384]{2,1,0:T(8,128)(2,1)}, f32[1,768]{1,0:T(1,128)}) custom-call(s32[7]{0:T(128)} %concatenate.54.sc, bf16[2,8,2,64,768]{4,3,2,1,0:T(8,128)(2,1)} %bitcast.139, f32[2,8,64,768]{3,2,1,0:T(8,128)} %bitcast.149, bf16[2,8,64,768]{3,2,1,0:T(8,128)(2,1)} %bitcast.156, ...), custom_call_target="tpu_custom_call" | custom-call | flops 4831838208 | bytes 29884416 | tf_op jit(solution)/shard_map/close/pallas_call | solution.py:702
  476.0 13.8 %collective-permute-done.72 = bf16[432,384]{1,0:T(8,128)(2,1)S(1)} collective-permute-done((bf16[432,384]{1,0:T(8,128)(2,1)S(1)}, bf16[432,384]{1,0:T(8,128)(2,1)S(1)}, u32[]{:S(2)}, u32[]{:S(2)}) %collective-permute-start.72) | collective-permute-done | bytes 331808 | tf_op jit(solution)/shard_map/ppermute | solution.py:864
  496.8 7.1 %collective-permute-done.78 = bf16[4,2,64,384]{3,2,1,0:T(8,128)(2,1)S(1)} collective-permute-done((bf16[4,2,64,384]{3,2,1,0:T(8,128)(2,1)S(1)}, bf16[4,2,64,384]{3,2,1,0:T(8,128)(2,1)S(1)}, u32[]{:S(2)}, u32[]{:S(2)}) %collective-permute-start.78) | collective-permute-done | bytes 393248 | tf_op jit(solution)/shard_map/ppermute | solution.py:864
  (374 shorter events, 208.5 us)
Async XLA Ops:
  17.2 49.9 %collective-permute-start.19 = (bf16[2,8,64,768]{3,2,1,0:T(8,128)(2,1)S(1)}, bf16[2,8,64,768]{3,2,1,0:T(8,128)(2,1)S(1)}, u32[]{:S(2)}, u32[]{:S(2)}) collective-permute-start(bf16[2,8,64,768]{3,2,1,0:T(8,128)(2,1)S(1)} %dynamic-slice_bitcast_fusion.1), channel_id=1, source_target_pairs={{0,1},{1,0},{2,3},{3,2},{4,5},{5,4},{6,7},{7,6},{8,9},{9,8},{10,11... | collective-permute-start | bytes 4718600 | tf_op jit(solution)/shard_map/ppermute | solution.py:864
  27.6 43.5 %collective-permute-start.29 = (bf16[2,8,64,768]{3,2,1,0:T(8,128)(2,1)S(1)}, bf16[2,8,64,768]{3,2,1,0:T(8,128)(2,1)S(1)}, u32[]{:S(2)}, u32[]{:S(2)}) collective-permute-start(bf16[2,8,64,768]{3,2,1,0:T(8,128)(2,1)S(1)} %dynamic-slice_bitcast_fusion), channel_id=1, source_target_pairs={{0,1},{1,0},{2,3},{3,2},{4,5},{5,4},{6,7},{7,6},{8,9},{9,8},{10,11... | collective-permute-start | bytes 4718600 | tf_op jit(solution)/shard_map/ppermute | solution.py:864
  69.5 38.2 %collective-permute-start.20 = (bf16[384,1024]{1,0:T(8,128)(2,1)S(1)}, bf16[384,1024]{1,0:T(8,128)(2,1)S(1)}, u32[]{:S(2)}, u32[]{:S(2)}) collective-permute-start(bf16[384,1024]{1,0:T(8,128)(2,1)S(1)} %collective-permute-done.10.refs_1_.refs_5_), channel_id=1, source_target_pairs={{0,4},{1,5},{2,6},{3,7},{4,0},{5,1},{6,2},{7,3},{8,12},{9,13},{10,... | collective-permute-start | bytes 2359304 | tf_op jit(solution)/shard_map/ppermute | solution.py:864
  70.0 37.7 %collective-permute-start.21 = (bf16[384,1024]{1,0:T(8,128)(2,1)}, bf16[384,1024]{1,0:T(8,128)(2,1)}, u32[]{:S(2)}, u32[]{:S(2)}) collective-permute-start(bf16[384,1024]{1,0:T(8,128)(2,1)} %collective-permute-done.12.refs_4_.refs_0_), channel_id=1, source_target_pairs={{0,2},{1,3},{2,0},{3,1},{4,6},{5,7},{6,4},{7,5},{8,10},{9,11},{10,... | collective-permute-start | bytes 2359304 | tf_op jit(solution)/shard_map/ppermute | solution.py:864
  71.2 36.5 %collective-permute-start.22 = (bf16[384,1024]{1,0:T(8,128)(2,1)}, bf16[384,1024]{1,0:T(8,128)(2,1)S(1)}, u32[]{:S(2)}, u32[]{:S(2)}) collective-permute-start(bf16[384,1024]{1,0:T(8,128)(2,1)} %collective-permute-done.12.refs_4_.refs_0_), channel_id=1, source_target_pairs={{0,8},{1,9},{2,10},{3,11},{4,12},{5,13},{6,14},{7,15},{8,16},{9,17... | collective-permute-start | bytes 2359304 | tf_op jit(solution)/shard_map/ppermute | solution.py:868
  138.2 40.7 %collective-permute-start.37 = (bf16[12,1024,128]{2,1,0:T(8,128)(2,1)}, bf16[12,1024,128]{2,1,0:T(8,128)(2,1)}, u32[]{:S(2)}, u32[]{:S(2)}) collective-permute-start(bf16[12,1024,128]{2,1,0:T(8,128)(2,1)} %values.1.refs_8_), channel_id=1, source_target_pairs={{0,1},{1,0},{2,3},{3,2},{4,5},{5,4},{6,7},{7,6},{8,9},{9,8},{10,11... | collective-permute-start | bytes 9437192 | tf_op jit(solution)/shard_map/ppermute | solution.py:864
  138.2 40.7 %collective-permute-start.39 = (bf16[3072,384]{1,0:T(8,128)(2,1)}, bf16[3072,384]{1,0:T(8,128)(2,1)S(1)}, u32[]{:S(2)}, u32[]{:S(2)}) collective-permute-start(bf16[3072,384]{1,0:T(8,128)(2,1)} %get-tuple-element.366.dn_own), channel_id=1, source_target_pairs={{0,1},{1,0},{2,3},{3,2},{4,5},{5,4},{6,7},{7,6},{8,9},{9,8},{10,11... | collective-permute-start | bytes 7077896 | tf_op jit(solution)/shard_map/ppermute | solution.py:864
  138.8 21.5 %collective-permute-start.34 = (bf16[384,1024]{1,0:T(8,128)(2,1)}, bf16[384,1024]{1,0:T(8,128)(2,1)S(1)}, u32[]{:S(2)}, u32[]{:S(2)}) collective-permute-start(bf16[384,1024]{1,0:T(8,128)(2,1)} %copy-done.10), channel_id=1, source_target_pairs={{0,8},{1,9},{2,10},{3,11},{4,12},{5,13},{6,14},{7,15},{8,16},{9,17... | collective-permute-start | bytes 2359304 | tf_op jit(solution)/shard_map/ppermute | solution.py:868
  138.8 52.9 %collective-permute-start.43 = (bf16[768,1536]{1,0:T(8,128)(2,1)}, bf16[768,1536]{1,0:T(8,128)(2,1)}, u32[]{:S(2)}, u32[]{:S(2)}) collective-permute-start(bf16[768,1536]{1,0:T(8,128)(2,1)} %get-tuple-element.364.up_own), channel_id=1, source_target_pairs={{0,1},{1,0},{2,3},{3,2},{4,5},{5,4},{6,7},{7,6},{8,9},{9,8},{10,11... | collective-permute-start | bytes 7077896 | tf_op jit(solution)/shard_map/ppermute | solution.py:864
  290.0 39.8 %collective-permute-start.47 = (bf16[2,512,768]{2,1,0:T(8,128)(2,1)}, bf16[2,512,768]{2,1,0:T(8,128)(2,1)S(1)}, u32[]{:S(2)}, u32[]{:S(2)}) collective-permute-start(bf16[2,512,768]{2,1,0:T(8,128)(2,1)} %get-tuple-element.400), channel_id=1, source_target_pairs={{0,1},{1,0},{2,3},{3,2},{4,5},{5,4},{6,7},{7,6},{8,9},{9,8},{10,11... | collective-permute-start | bytes 4718600 | tf_op jit(solution)/shard_map/ppermute | solution.py:864
  329.8 27.6 %collective-permute-start.52 = (bf16[12,1024,128]{2,1,0:T(8,128)(2,1)}, bf16[12,1024,128]{2,1,0:T(8,128)(2,1)}, u32[]{:S(2)}, u32[]{:S(2)}) collective-permute-start(bf16[12,1024,128]{2,1,0:T(8,128)(2,1)} %get-tuple-element.421), channel_id=1, source_target_pairs={{0,1},{1,0},{2,3},{3,2},{4,5},{5,4},{6,7},{7,6},{8,9},{9,8},{10,11... | collective-permute-start | bytes 9437192 | tf_op jit(solution)/shard_map/ppermute | solution.py:864
  333.2 22.6 %collective-permute-start.51 = (bf16[384,1024]{1,0:T(8,128)(2,1)}, bf16[384,1024]{1,0:T(8,128)(2,1)S(1)}, u32[]{:S(2)}, u32[]{:S(2)}) collective-permute-start(bf16[384,1024]{1,0:T(8,128)(2,1)} %add_convert_fusion.7), channel_id=1, source_target_pairs={{0,4},{1,5},{2,6},{3,7},{4,0},{5,1},{6,2},{7,3},{8,12},{9,13},{10,... | collective-permute-start | bytes 2359304 | tf_op jit(solution)/shard_map/ppermute | solution.py:864
  358.3 26.5 %collective-permute-start.56 = (bf16[768,1536]{1,0:T(8,128)(2,1)}, bf16[768,1536]{1,0:T(8,128)(2,1)S(1)}, u32[]{:S(2)}, u32[]{:S(2)}) collective-permute-start(bf16[768,1536]{1,0:T(8,128)(2,1)} %get-tuple-element.438), channel_id=1, source_target_pairs={{0,1},{1,0},{2,3},{3,2},{4,5},{5,4},{6,7},{7,6},{8,9},{9,8},{10,11... | collective-permute-start | bytes 7077896 | tf_op jit(solution)/shard_map/ppermute | solution.py:864
  360.8 23.3 %collective-permute-start.53 = (bf16[384,1024]{1,0:T(8,128)(2,1)}, bf16[384,1024]{1,0:T(8,128)(2,1)}, u32[]{:S(2)}, u32[]{:S(2)}) collective-permute-start(bf16[384,1024]{1,0:T(8,128)(2,1)} %add_convert_fusion.4), channel_id=1, source_target_pairs={{0,24},{1,25},{2,26},{3,27},{4,28},{5,29},{6,30},{7,31},{8,0},{9,1... | collective-permute-start | bytes 2359304 | tf_op jit(solution)/shard_map/ppermute | solution.py:868
  389.2 39.2 %collective-permute-start.58 = (bf16[384,1024]{1,0:T(8,128)(2,1)}, bf16[384,1024]{1,0:T(8,128)(2,1)S(1)}, u32[]{:S(2)}, u32[]{:S(2)}) collective-permute-start(bf16[384,1024]{1,0:T(8,128)(2,1)} %get-tuple-element.447), channel_id=1, source_target_pairs={{0,2},{1,3},{2,0},{3,1},{4,6},{5,7},{6,4},{7,5},{8,10},{9,11},{10,... | collective-permute-start | bytes 2359304 | tf_op jit(solution)/shard_map/ppermute | solution.py:864
  390.7 37.7 %collective-permute-start.59 = (bf16[384,1024]{1,0:T(8,128)(2,1)}, bf16[384,1024]{1,0:T(8,128)(2,1)S(1)}, u32[]{:S(2)}, u32[]{:S(2)}) collective-permute-start(bf16[384,1024]{1,0:T(8,128)(2,1)} %add_convert_fusion.6), channel_id=1, source_target_pairs={{0,4},{1,5},{2,6},{3,7},{4,0},{5,1},{6,2},{7,3},{8,12},{9,13},{10,... | collective-permute-start | bytes 2359304 | tf_op jit(solution)/shard_map/ppermute | solution.py:864
  403.7 24.7 %collective-permute-start.61 = (bf16[432,384]{1,0:T(8,128)(2,1)}, bf16[432,384]{1,0:T(8,128)(2,1)}, u32[]{:S(2)}, u32[]{:S(2)}) collective-permute-start(bf16[432,384]{1,0:T(8,128)(2,1)} %get-tuple-element.527), channel_id=1, source_target_pairs={{0,24},{1,25},{2,26},{3,27},{4,28},{5,29},{6,30},{7,31},{8,0},{9,1... | collective-permute-start | bytes 995336 | tf_op jit(solution)/shard_map/ppermute | solution.py:868
  403.8 24.6 %collective-permute-start.62 = (bf16[432,384]{1,0:T(8,128)(2,1)}, bf16[432,384]{1,0:T(8,128)(2,1)}, u32[]{:S(2)}, u32[]{:S(2)}) collective-permute-start(bf16[432,384]{1,0:T(8,128)(2,1)} %get-tuple-element.526), channel_id=1, source_target_pairs={{0,2},{1,3},{2,0},{3,1},{4,6},{5,7},{6,4},{7,5},{8,10},{9,11},{10,... | collective-permute-start | bytes 995336 | tf_op jit(solution)/shard_map/ppermute | solution.py:864
  431.5 31.1 %collective-permute-start.69 = (bf16[432,384]{1,0:T(8,128)(2,1)}, bf16[432,384]{1,0:T(8,128)(2,1)}, u32[]{:S(2)}, u32[]{:S(2)}) collective-permute-start(bf16[432,384]{1,0:T(8,128)(2,1)} %add_convert_fusion.14), channel_id=1, source_target_pairs={{0,2},{1,3},{2,0},{3,1},{4,6},{5,7},{6,4},{7,5},{8,10},{9,11},{10,... | collective-permute-start | bytes 995336 | tf_op jit(solution)/shard_map/ppermute | solution.py:864
  434.0 28.8 %collective-permute-start.68 = (bf16[432,384]{1,0:T(8,128)(2,1)}, bf16[432,384]{1,0:T(8,128)(2,1)}, u32[]{:S(2)}, u32[]{:S(2)}) collective-permute-start(bf16[432,384]{1,0:T(8,128)(2,1)} %add_convert_fusion.16), channel_id=1, source_target_pairs={{0,4},{1,5},{2,6},{3,7},{4,0},{5,1},{6,2},{7,3},{8,12},{9,13},{10,... | collective-permute-start | bytes 995336 | tf_op jit(solution)/shard_map/ppermute | solution.py:864
  435.2 28.3 %collective-permute-start.67 = (bf16[432,384]{1,0:T(8,128)(2,1)}, bf16[432,384]{1,0:T(8,128)(2,1)}, u32[]{:S(2)}, u32[]{:S(2)}) collective-permute-start(bf16[432,384]{1,0:T(8,128)(2,1)} %get-tuple-element.468), channel_id=1, source_target_pairs={{0,24},{1,25},{2,26},{3,27},{4,28},{5,29},{6,30},{7,31},{8,0},{9,1... | collective-permute-start | bytes 995336 | tf_op jit(solution)/shard_map/ppermute | solution.py:868
  440.0 49.8 %collective-permute-start.65 = (bf16[384,1024]{1,0:T(8,128)(2,1)}, bf16[384,1024]{1,0:T(8,128)(2,1)}, u32[]{:S(2)}, u32[]{:S(2)}) collective-permute-start(bf16[384,1024]{1,0:T(8,128)(2,1)} %add_convert_fusion), channel_id=1, source_target_pairs={{0,2},{1,3},{2,0},{3,1},{4,6},{5,7},{6,4},{7,5},{8,10},{9,11},{10,... | collective-permute-start | bytes 2359304 | tf_op jit(solution)/shard_map/ppermute | solution.py:864
  462.7 27.1 %collective-permute-start.64 = (bf16[384,1024]{1,0:T(8,128)(2,1)S(1)}, bf16[384,1024]{1,0:T(8,128)(2,1)S(1)}, u32[]{:S(2)}, u32[]{:S(2)}) collective-permute-start(bf16[384,1024]{1,0:T(8,128)(2,1)S(1)} %add_convert_fusion.1), channel_id=1, source_target_pairs={{0,24},{1,25},{2,26},{3,27},{4,28},{5,29},{6,30},{7,31},{8,0},{9,1... | collective-permute-start | bytes 2359304 | tf_op jit(solution)/shard_map/ppermute | solution.py:868
  462.8 27.0 %collective-permute-start.66 = (bf16[384,1024]{1,0:T(8,128)(2,1)S(1)}, bf16[384,1024]{1,0:T(8,128)(2,1)S(1)}, u32[]{:S(2)}, u32[]{:S(2)}) collective-permute-start(bf16[384,1024]{1,0:T(8,128)(2,1)S(1)} %copy-done.64), channel_id=1, source_target_pairs={{0,4},{1,5},{2,6},{3,7},{4,0},{5,1},{6,2},{7,3},{8,12},{9,13},{10,... | collective-permute-start | bytes 2359304 | tf_op jit(solution)/shard_map/ppermute | solution.py:864
  (132 other events, 1615.9 us)

commit v6 on v5

--- a/solution.py
+++ b/solution.py
@@ -235,7 +235,7 @@
             both = jnp.concatenate([heads[2 * pair, :, lanes], heads[2 * pair + 1, :, lanes]], axis=1)
             mixed[item, :, pair * 128 : (pair + 1) * 128] = both
     res = four_items(tok, tok_far).astype(F32) + dot(mixed[...].reshape(4 * SPAN, WIDTH), weight[...], 1, 0)
-    resid[...] = res.reshape(4, SPAN, WIDTH)
+    resid[...] = res.astype(BF16).reshape(4, SPAN, WIDTH)
     scale = lax.rsqrt(jnp.mean(res * res, axis=-1, keepdims=True) + EPSILON)
     valid = row_valid(sc, step)
     normed[...] = jnp.where(valid, res * scale * gain[...], 0.0).astype(BF16).reshape(4, SPAN, WIDTH)
@@ -272,7 +272,7 @@
         ),
         out_shape=[
             jax.ShapeDtypeStruct((4, HROWS, WIDTH), BF16),
-            jax.ShapeDtypeStruct((4, HROWS, WIDTH), F32),
+            jax.ShapeDtypeStruct((4, HROWS, WIDTH), BF16),
             jax.ShapeDtypeStruct((4, HROWS, WIDTH), BF16),
             jax.ShapeDtypeStruct((4, HROWS, WIDTH), BF16),
         ],
@@ -308,7 +308,7 @@
     return (0, lax.max(f - FSIDE, 0))
 
 
-def units_kernel(sc, normed, cot, up_own, up_far, dn_own, dn_far, active, up_grad, back, w_up, w_down):
+def units_kernel(sc, normed, cot, up_own, up_far, dn_own, dn_far, active, up_grad, back, w_up, w_down, total):
     step = pl.program_id(0)
     w_down[:, own_lanes(sc)] = dn_own[...]
     w_down[:, far_lanes(sc)] = dn_far[...]
@@ -322,27 +322,34 @@
         w_up[...] = up_far[...]
 
     for piece in range(ROWS // TILE):
-        rows = slice(piece * TILE, (piece + 1) * TILE)
-        up = dot(normed[rows], w_up[...], 1, 0)
-        square = up * up
-        bend = jnp.tanh(up * (0.7978845608028654 + (0.044715 * 0.7978845608028654) * square))
-        share = 0.5 + 0.5 * bend
-        act = up * share
-        active[rows] = act.astype(BF16)
-        slope = share + act * (1.0 - share) * (
-            2 * 0.7978845608028654 + (6 * 0.044715 * 0.7978845608028654) * square
-        )
-        low = (dot(cot[rows], w_down[...], 1, 1) * slope).astype(BF16)
-        up_grad[rows] = low
-        two_grad = dot(low, w_up[...], 1, 1)
+        whole = slice(piece * TILE, (piece + 1) * TILE)
+        for row in range(piece * TILE, (piece + 1) * TILE, 256):
+            rows = slice(row, row + 256)
+            for column in range(0, FSTEP, 256):
+                columns = slice(column, column + 256)
+                up = dot(normed[rows], w_up[:, columns], 1, 0)
+                square = up * up
+                bend = jnp.tanh(up * (0.7978845608028654 + (0.044715 * 0.7978845608028654) * square))
+                share = 0.5 + 0.5 * bend
+                act = up * share
+                active[rows, columns] = act.astype(BF16)
+                slope = share + act * (1.0 - share) * (
+                    2 * 0.7978845608028654 + (6 * 0.044715 * 0.7978845608028654) * square
+                )
+                up_grad[rows, columns] = (dot(cot[rows], w_down[columns], 1, 1) * slope).astype(BF16)
+        two_grad = dot(up_grad[whole], w_up[...], 1, 1)
 
         @pl.when(step == 0)
         def _():
-            back[rows] = two_grad
-
-        @pl.when(step > 0)
+            total[whole] = two_grad
+
+        @pl.when((step > 0) & (step < 2 * FSIDE - 1))
         def _():
-            back[rows] += two_grad
+            total[whole] += two_grad
+
+        @pl.when(step == 2 * FSIDE - 1)
+        def _():
+            back[whole] = (total[whole] + two_grad).astype(BF16)
 
 
 def run_units(sc, normed, cotangent, up, down):
@@ -360,12 +367,16 @@
                 spec((FSTEP, SIDE), unit_rows),
             ],
             out_specs=[spec((ROWS, FSTEP), unit_columns), spec((ROWS, FSTEP), unit_columns), held((ROWS, WIDTH))],
-            scratch_shapes=[pltpu.VMEM((WIDTH, FSTEP), BF16), pltpu.VMEM((FSTEP, WIDTH), BF16)],
+            scratch_shapes=[
+                pltpu.VMEM((WIDTH, FSTEP), BF16),
+                pltpu.VMEM((FSTEP, WIDTH), BF16),
+                pltpu.VMEM((ROWS, WIDTH), F32),
+            ],
         ),
         out_shape=[
             jax.ShapeDtypeStruct((ROWS, FF), BF16),
             jax.ShapeDtypeStruct((ROWS, FF), BF16),
-            jax.ShapeDtypeStruct((ROWS, WIDTH), F32),
+            jax.ShapeDtypeStruct((ROWS, WIDTH), BF16),
         ],
         compiler_params=params(VMEM),
         cost_estimate=pl.CostEstimate(
@@ -439,10 +450,10 @@
         w_down[:, far_lanes(sc)] = dn_far[...]
 
     branch = dot(active[...].reshape(4 * SPAN, FF), w_down[...], 1, 0)
-    output = jnp.where(row_valid(sc, step), resid[...].reshape(4 * SPAN, WIDTH) + branch, 0.0)
-    output = output.reshape(4, SPAN, WIDTH)
+    output = jnp.where(row_valid(sc, step), resid[...].reshape(4 * SPAN, WIDTH).astype(F32) + branch, 0.0)
+    output = output.astype(BF16).reshape(4, SPAN, WIDTH)
     own[...] = output[:2]
-    far[...] = output[2:].astype(BF16)
+    far[...] = output[2:]
 
 
 def run_out(sc, active, resid, down):
@@ -461,7 +472,7 @@
             scratch_shapes=[pltpu.VMEM((FF, WIDTH), BF16)],
         ),
         out_shape=[
-            jax.ShapeDtypeStruct((2, HROWS, WIDTH), F32),
+            jax.ShapeDtypeStruct((2, HROWS, WIDTH), BF16),
             jax.ShapeDtypeStruct((2, HROWS, WIDTH), BF16),
         ],
         compiler_params=params(VMEM),
@@ -478,15 +489,15 @@
     whole_weight(sc, step, wo_own, wo_far, weight)
     shape, slab = (4 * SPAN, WIDTH), (4, SPAN, WIDTH)
     valid = row_valid(sc, step)
-    res = resid[...].reshape(shape)
+    res = resid[...].reshape(shape).astype(F32)
     scale = lax.rsqrt(jnp.mean(res * res, axis=-1, keepdims=True) + EPSILON)
     unit = res * scale
-    two_grad = jnp.where(valid, back[...].reshape(shape), 0.0)
+    two_grad = jnp.where(valid, back[...].reshape(shape).astype(F32), 0.0)
     gained = two_grad * gain[...]
     masked = cot[...].reshape(shape).astype(F32)
     grad = masked + scale * (gained - unit * jnp.mean(gained * unit, axis=-1, keepdims=True))
     low = grad.astype(BF16)
-    res_own[...] = grad.reshape(slab)[:2]
+    res_own[...] = low.reshape(slab)[:2]
     res_far[...] = low.reshape(slab)[2:]
     gain_sum = jnp.sum(two_grad * unit, axis=0, keepdims=True)
     out_sum = dot(mixed[...].reshape(shape), low, 0, 0)
@@ -534,7 +545,7 @@
             ],
         ),
         out_shape=[
-            jax.ShapeDtypeStruct((2, HROWS, WIDTH), F32),
+            jax.ShapeDtypeStruct((2, HROWS, WIDTH), BF16),
             jax.ShapeDtypeStruct((2, HROWS, WIDTH), BF16),
             jax.ShapeDtypeStruct((HEADS, HROWS, 4 * HEAD), BF16),
             jax.ShapeDtypeStruct((WIDTH, SIDE), BF16),
@@ -648,9 +659,9 @@
     step = pl.program_id(0)
     whole_weight(sc, step, w_own, w_far, weight)
     core = sc[CORE]
-    output[:, :, core] = out_own[...]
+    output[:, :, core] = out_own[...].astype(F32)
     output[:, :, 1 - core] = out_got[...].astype(F32)
-    tok_grad[:, :, core] = res_own[...]
+    tok_grad[:, :, core] = res_own[...].astype(F32)
     tok_grad[:, :, 1 - core] = res_got[...].astype(F32)
     runs = tok.shape[1]
     rows = runs * 128
@@ -827,14 +838,19 @@
 
 
 def collect_kernel(sc, *refs):
-    packed = refs[-1]
-    for rel in range(4):
-        down, down_got, up, up_got, out, out_got = refs[6 * rel : 6 * rel + 6]
-        packed[rel, PACK_DOWN:PACK_UP] = add_low(down[...], down_got[...])
-        for j in range(4):
-            lanes = slice(j * SIDE, (j + 1) * SIDE)
-            packed[rel, PACK_UP + 48 * j : PACK_UP + 48 * (j + 1)] = add_low(up[:, lanes], up_got[:, lanes])
-        packed[rel, PACK_OUT:PACK_VALUE] = add_low(out[...], out_got[...])
+    outs = refs[24:]
+    for k in range(PLANES):
+
+        @pl.when(pl.program_id(0) == k)
+        def _():
+            for rel in range(4):
+                down, down_got, up, up_got, out, out_got = refs[6 * rel : 6 * rel + 6]
+                packed = outs[4 * k + rel]
+                packed[PACK_DOWN:PACK_UP] = add_low(down[...], down_got[...])
+                for j in range(4):
+                    lanes = slice(j * SIDE, (j + 1) * SIDE)
+                    packed[PACK_UP + 48 * j : PACK_UP + 48 * (j + 1)] = add_low(up[:, lanes], up_got[:, lanes])
+                packed[PACK_OUT:PACK_VALUE] = add_low(out[...], out_got[...])
 
 
 def run_collect(sc, *sides):
@@ -847,13 +863,39 @@
             num_scalar_prefetch=1,
             grid=(PLANES,),
             in_specs=[rows(x, rel) for rel in range(4) for x in sides],
-            out_specs=spec((4, PACK_VALUE, SIDE), lambda k, s: (k, 0, 0)),
-        ),
-        out_shape=jax.ShapeDtypeStruct((16, PACK_VALUE, SIDE), BF16),
+            out_specs=[held((PACK_VALUE, SIDE))] * 16,
+        ),
+        out_shape=[jax.ShapeDtypeStruct((PACK_VALUE, SIDE), BF16)] * 16,
         compiler_params=params(VMEM),
         cost_estimate=pl.CostEstimate(flops=0, bytes_accessed=3 * 16 * PACK_VALUE * SIDE * 2, transcendentals=0),
         name="collect",
     )(sc, *(x for _ in range(4) for x in sides))
+
+
+def add_kernel(groups, *refs):
+    for group, total in zip(groups, refs[-len(groups) :]):
+        value = refs[group[0]][...].astype(F32)
+        for index in group[1:]:
+            value = value + refs[index][...].astype(F32)
+        total[...] = value.astype(total.dtype)
+
+
+def run_add(groups, values, dtype):
+    rows, columns = values[0].shape
+    parts = 2 if columns == LMAX else 1
+    block = pl.BlockSpec((rows // parts, columns), lambda i: (i, 0))
+    return pl.pallas_call(
+        partial(add_kernel, groups),
+        grid=(parts,),
+        in_specs=[block] * len(values),
+        out_specs=[block] * len(groups),
+        out_shape=[jax.ShapeDtypeStruct((rows, columns), dtype)] * len(groups),
+        compiler_params=params(VMEM),
+        cost_estimate=pl.CostEstimate(
+            flops=0, bytes_accessed=2 * rows * columns * (len(values) + len(groups)), transcendentals=0
+        ),
+        name="add",
+    )(*values)
 
 
 DEVICES = 32
@@ -916,14 +958,10 @@
 def scatter_add(have, got, step):
     by_x, by_y, by_z = STEPS[len(STEPS) - 1 - step]
     targets = ((by_z[0] - 1, by_z[1], by_z[2]), (by_x[0], by_x[1], 0), (by_y[0], 0, by_y[2]))
-    have = dict(have)
-    for at in dict.fromkeys(targets):
-        total = have[at].astype(F32)
-        for target, value in zip(targets, got):
-            if target == at:
-                total = total + value.astype(F32)
-        have[at] = total if step == len(STEPS) - 1 else total.astype(BF16)
-    return have
+    sums = list(dict.fromkeys(targets))
+    groups = [(len(got) + i, *(j for j in range(len(got)) if targets[j] == at)) for i, at in enumerate(sums)]
+    values = [*got, *(have[at] for at in sums)]
+    return {**have, **dict(zip(sums, run_add(groups, values, F32 if step == len(STEPS) - 1 else BF16)))}
 
 
 together = lax.optimization_barrier
@@ -946,17 +984,15 @@
 
     rand = rand_mix.reshape(3, 2, HALF, LMAX)
     blocks = side(pick(rand, core, 1), other(pick(rand, 1 - core, 1)), 0)
-    weights, (rands, far_lengths) = together(
-        (gather_step(weights, 0), ({(0, 0, 0): blocks.reshape(SUBS * HALF, LMAX)}, other(lengths)))
+    weights, rands, far_lengths = together(
+        (gather_step(weights, 0), {(0, 0, 0): blocks.reshape(SUBS * HALF, LMAX)}, other(lengths))
     )
     sc = jnp.concatenate([near_sc[:5], far_lengths])
-
-    rands, weights, tokens_far = together(
-        (gather_step(rands, 0), gather_step(gather_step(weights, 1), 2), other(pick(tokens, 1 - core, 2)))
-    )
-    rands, weights, grad_far = together(
-        (gather_step(rands, 1), gather_step(gather_step(weights, 3), 4), other(pick(grad_out, 1 - core, 2)))
-    )
+    weights, tokens_far = together((gather_step(weights, 1), other(pick(tokens, 1 - core, 2))))
+    weights, grad_far = together((gather_step(weights, 2), other(pick(grad_out, 1 - core, 2))))
+    rands, weights = together((gather_step(rands, 0), gather_step(weights, 3)))
+    rands, weights = together((gather_step(rands, 1), gather_step(weights, 4)))
+
     down, up, out, value, gain_rows = place_weights(sc, in_order(weights))
     value_far = other(value)
     gain_rows = gain_rows.reshape(16, 2, 8, SIDE)[:, :, 0]
@@ -966,11 +1002,10 @@
     rands, value_far, v_own, gain_one, gain_two, out, down, up = together(
         (gather_step(rands, 2), value_far, v_own, gain_one, gain_two, out, down, up)
     )
-    rands, v_far, out, down = together(
-        (gather_step(rands, 3), other(v_own), (out, other(out)), (down, other(down)))
-    )
-    mixing = run_mix(sc, (0, 1), in_order({**rands, (2, 1, 1): 0, (3, 1, 0): 0, (3, 1, 1): 0})[:8], v_own, v_far, ())
-    rands, up, mixing = together((gather_step(rands, 4), (up, other(up)), mixing))
+    rands, v_far, out = together((gather_step(rands, 3), other(v_own), (out, other(out))))
+    near = [rands[k, y_at, x_at] for k in range(2) for y_at in range(2) for x_at in range(2)]
+    mixing = run_mix(sc, (0, 1), near, v_own, v_far, ())
+    rands, up, down, mixing = together((gather_step(rands, 4), (up, other(up)), (down, other(down)), mixing))
     shares = in_order(rands)
     heads, mean = run_mix(sc, (2, 3), shares[8:], v_own, v_far, mixing)
 
@@ -1004,7 +1039,7 @@
 
     have, got = scatter_send(have, 3)
     packed = run_collect(sc, down_own, other(down_far), up_own, up_got, d_out_own, d_out_got)
-    sums, sums_got = scatter_send(by_place([packed[i] for i in range(16)]), 0)
+    sums, sums_got = scatter_send(by_place(packed), 0)
     out_own, out_far = run_out(sc, active, resid, down)
     have, got, sums, sums_got, out_own, out_far = together((have, got, sums, sums_got, out_own, out_far))
     have, sums = scatter_add(have, got, 3), scatter_add(sums, sums_got, 0)

time: 545 us -> 560 us (1.028)
  Pallas kernels: 225 us -> 250 us
  other arithmetic: 35.5 us -> 11.6 us
  waiting for transfers between devices: 187 us -> 195 us
  starting transfers between devices: 68.4 us -> 74.4 us
    pallas_call x0 -> x10, Pallas kernels: none -> 28.5 us  [run_add(): pl.pallas_call(partial(add_kernel, groups), grid=(parts,), in_specs=[bloc...]
    convert_element_type x18 -> x0, other arithmetic: 26.6 us -> none  [scatter_add(): have[at] = total if step == len(STEPS) - 1 else total.astype(BF16)]
    ppermute x66, waiting for transfers between devices: 119 us -> 144 us  [swap(): return lax.ppermute(x, BOTH, [(d, d ^ bit) for d in range(DEVICES)])]
    ppermute x23, waiting for transfers between devices: 68.5 us -> 50.6 us  [ring(): lax.ppermute(x, BOTH, [(d, (d + 8 * way) % DEVICES) for d in range(DEVICE...]
    squeeze x8, local copies, waits for them, and re-layouts: 3.37 us -> 9.57 us  [pick(): return lax.dynamic_index_in_dim(x, index, axis, keepdims=False)]
  transfers between devices with their start and end apart: 89 -> 89, of which waited for: 43 -> 43; matrix products, arithmetic and copies ran while one was open for 8% -> 4% of each run, Pallas kernels for 24% -> 28%
where the time goes in v6:
time: 560 us; the launch traced here: 554 us
  Pallas kernels  250 us (45%)
  waiting for transfers between devices  195 us (35%)
  starting transfers between devices  74.4 us (13%)
  local copies, waits for them, and re-layouts  21.7 us (4%)
  other arithmetic  11.6 us (2%)
    ppermute x66, waiting for transfers between devices, swap(): return lax.ppermute(x, BOTH, [(d, d ^ bit) for d in range(DEVICES)])  144 us
    ppermute x66, starting transfers between devices, swap(): return lax.ppermute(x, BOTH, [(d, d ^ bit) for d in range(DEVICES)])  50.8 us
    ppermute x23, waiting for transfers between devices, ring(): lax.ppermute(x, BOTH, [(d, (d + 8 * way) % DEVICES) for d in range(DEVICE...  50.6 us
    pallas_call x1, Pallas kernels, run_units(): pl.pallas_call(units_kernel, grid_spec=pltpu.PrefetchScalarGridSpec(num_s...  46.4 us
    pallas_call x2, Pallas kernels, run_unmix(): pl.pallas_call(partial(unmix_kernel, bool(carry)), grid_spec=pltpu.Prefet...  34.8 us
    pallas_call x10, Pallas kernels, run_add(): pl.pallas_call(partial(add_kernel, groups), grid=(parts,), in_specs=[bloc...  28.5 us
    ppermute x23, starting transfers between devices, ring(): lax.ppermute(x, BOTH, [(d, (d + 8 * way) % DEVICES) for d in range(DEVICE...  23.6 us
    pallas_call x2, Pallas kernels, run_mix(): pl.pallas_call(partial(mix_kernel, bool(carry)), grid_spec=pltpu.Prefetch...  18.7 us
  transfers between devices with their start and end apart: 89, of which 43 were waited for; matrix products, arithmetic and copies ran while one was open for 4% of the time, Pallas kernels for 28%

profile of v6, /device:TPU:0, one launch (start us, length us, event | category | flops | bytes accessed | tf_op | source)
XLA Modules:
  0.0 554.3 jit_solution(6469392872745307351)
XLA Ops:
  33.5 8.5 %collective-permute-done.13.refs_3_ = bf16[496,384]{1,0:T(8,128)(2,1)S(1)} collective-permute-done((bf16[496,384]{1,0:T(8,128)(2,1)S(1)}, bf16[496,384]{1,0:T(8,128)(2,1)S(1)}, u32[]{:S(2)}, u32[]{:S(2)}) %collective-permute-start.13) | collective-permute-done | bytes 380960 | tf_op jit(solution)/shard_map/ppermute | solution.py:906
  48.2 8.6 %collective-permute-done.17.refs_6_ = bf16[496,384]{1,0:T(8,128)(2,1)S(1)} collective-permute-done((bf16[496,384]{1,0:T(8,128)(2,1)}, bf16[496,384]{1,0:T(8,128)(2,1)S(1)}, u32[]{:S(2)}, u32[]{:S(2)}) %collective-permute-start.17) | collective-permute-done | bytes 380960 | tf_op jit(solution)/shard_map/ppermute | solution.py:906
  56.8 10.7 %collective-permute-done.18.refs_9_ = bf16[496,384]{1,0:T(8,128)(2,1)S(1)} collective-permute-done((bf16[496,384]{1,0:T(8,128)(2,1)S(1)}, bf16[496,384]{1,0:T(8,128)(2,1)S(1)}, u32[]{:S(2)}, u32[]{:S(2)}) %collective-permute-start.18) | collective-permute-done | bytes 380960 | tf_op jit(solution)/shard_map/ppermute | solution.py:906
  75.8 6.8 %collective-permute-done.21.refs_7_ = bf16[496,384]{1,0:T(8,128)(2,1)S(1)} collective-permute-done((bf16[496,384]{1,0:T(8,128)(2,1)S(1)}, bf16[496,384]{1,0:T(8,128)(2,1)S(1)}, u32[]{:S(2)}, u32[]{:S(2)}) %collective-permute-start.21) | collective-permute-done | bytes 380960 | tf_op jit(solution)/shard_map/ppermute | solution.py:910
  87.6 19.4 %collective-permute-done.27.refs_11_ = bf16[496,384]{1,0:T(8,128)(2,1)S(1)} collective-permute-done((bf16[496,384]{1,0:T(8,128)(2,1)}, bf16[496,384]{1,0:T(8,128)(2,1)S(1)}, u32[]{:S(2)}, u32[]{:S(2)}) %collective-permute-start.27) | collective-permute-done | bytes 380960 | tf_op jit(solution)/shard_map/ppermute | solution.py:906
  115.7 7.2 %place.1 = (bf16[3072,384]{1,0:T(8,128)(2,1)}, bf16[768,1536]{1,0:T(8,128)(2,1)}, bf16[768,384]{1,0:T(8,128)(2,1)}, bf16[768,384]{1,0:T(8,128)(2,1)}, bf16[256,384]{1,0:T(8,128)(2,1)}) custom-call(s32[7]{0:T(128)} %concatenate.54.sc, bf16[496,384]{1,0:T(8,128)(2,1)} %pack.1.refs_0_, bf16[496,384]{1,0:T(8,128)(2,1)} %copy-done.23, ...), custom_call_target="tpu_custom_call" | custom-call | bytes 12189696 | tf_op jit(solution)/shard_map/place/pallas_call | solution.py:810
  127.6 7.9 %values.1.refs_8_ = bf16[12,1024,128]{2,1,0:T(8,128)(2,1)} custom-call(s32[7]{0:T(128)} %concatenate.54.sc, bf16[2,1024,768]{2,1,0:T(8,128)(2,1)} %tok.1, f32[1,768]{1,0:T(1,128)} %reshape.205.gain, bf16[768,384]{1,0:T(8,128)(2,1)} %get-tuple-element.384.w_own, bf16[768,384]{1,0:T(8,128)(2,1)} %collective-permute-done.33.w_far), custom_call_target="tpu_custom_call" | custom-call | flops 2415919104 | bytes 6291456 | tf_op jit(solution)/shard_map/values/pallas_call | solution.py:80
  135.5 7.9 %collective-permute-done.30.refs_6_.refs_2_ = bf16[384,1024]{1,0:T(8,128)(2,1)} collective-permute-done((bf16[384,1024]{1,0:T(8,128)(2,1)}, bf16[384,1024]{1,0:T(8,128)(2,1)}, u32[]{:S(2)}, u32[]{:S(2)}) %collective-permute-start.30) | collective-permute-done | bytes 786464 | tf_op jit(solution)/shard_map/ppermute | solution.py:906
  155.4 13.1 %collective-permute-done.34.refs_7_.refs_3_ = bf16[384,1024]{1,0:T(8,128)(2,1)S(1)} collective-permute-done((bf16[384,1024]{1,0:T(8,128)(2,1)}, bf16[384,1024]{1,0:T(8,128)(2,1)S(1)}, u32[]{:S(2)}, u32[]{:S(2)}) %collective-permute-start.34) | collective-permute-done | bytes 786464 | tf_op jit(solution)/shard_map/ppermute | solution.py:910
  173.6 14.2 %collective-permute-done.36.refs_5_.refs_1_ = bf16[384,1024]{1,0:T(8,128)(2,1)} collective-permute-done((bf16[384,1024]{1,0:T(8,128)(2,1)S(1)}, bf16[384,1024]{1,0:T(8,128)(2,1)}, u32[]{:S(2)}, u32[]{:S(2)}) %collective-permute-start.36) | collective-permute-done | bytes 786464 | tf_op jit(solution)/shard_map/ppermute | solution.py:906
  190.3 9.3 %mix.2 = (bf16[12,512,256]{2,1,0:T(8,128)(2,1)}, f32[12,512,256]{2,1,0:T(8,128)}) custom-call(s32[7]{0:T(128)} %concatenate.54.sc, bf16[384,1024]{1,0:T(8,128)(2,1)} %bitcast.113, bf16[384,1024]{1,0:T(8,128)(2,1)} %copy-done.8, bf16[384,1024]{1,0:T(8,128)(2,1)} %copy-done.9, bf16[384,1024]{1,0:T(8,128)(2,1)} %copy-done.10, ...), custom_call_target="tpu_custom_call" | custom-call | flops 3221225472 | bytes 14155776 | tf_op jit(solution)/shard_map/mix/pallas_call | solution.py:188
  209.2 9.3 %mix.3 = (bf16[12,512,256]{2,1,0:T(8,128)(2,1)}, f32[12,512,256]{2,1,0:T(8,128)}) custom-call(s32[7]{0:T(128)} %concatenate.54.sc, bf16[384,1024]{1,0:T(8,128)(2,1)} %copy-done.4, bf16[384,1024]{1,0:T(8,128)(2,1)} %copy-done.5, bf16[384,1024]{1,0:T(8,128)(2,1)} %collective-permute-done.35.refs_2_.refs_6_, ...), custom_call_target="tpu_custom_call", output_to_operand_aliasing={{0}: (11, {}), {1}: (12, {})} | custom-call | flops 3221225472 | bytes 14155776 | tf_op jit(solution)/shard_map/mix/pallas_call | solution.py:188
  218.6 12.4 %pre.1 = (bf16[4,512,768]{2,1,0:T(8,128)(2,1)}, bf16[4,512,768]{2,1,0:T(8,128)(2,1)}, bf16[4,512,768]{2,1,0:T(8,128)(2,1)}, bf16[4,512,768]{2,1,0:T(8,128)(2,1)}) custom-call(s32[7]{0:T(128)} %concatenate.54.sc, bf16[2,8,2,64,768]{4,3,2,1,0:T(8,128)(2,1)} %bitcast.108, bf16[2,8,64,768]{3,2,1,0:T(8,128)(2,1)} %collective-permute-done.16.tok_far, ...), custom_call_target="tpu_custom_call" | custom-call | flops 2415919104 | bytes 25165824 | tf_op jit(solution)/shard_map/pre/pallas_call | solution.py:262
  231.0 46.4 %units.1 = (bf16[2048,3072]{1,0:T(8,128)(2,1)}, bf16[2048,3072]{1,0:T(8,128)(2,1)}, bf16[2048,768]{1,0:T(8,128)(2,1)}) custom-call(s32[7]{0:T(128)} %concatenate.54.sc, bf16[2048,768]{1,0:T(8,128)(2,1)} %bitcast.136, bf16[2048,768]{1,0:T(8,128)(2,1)} %bitcast.134, bf16[768,1536]{1,0:T(8,128)(2,1)} %get-tuple-element.438.up_own, ...), custom_call_target="tpu_custom_call" | custom-call | flops 28991029248 | bytes 37748736 | tf_op jit(solution)/shard_map/units/pallas_call | solution.py:356
  277.4 18.4 %post.1 = (bf16[2,512,768]{2,1,0:T(8,128)(2,1)}, bf16[2,512,768]{2,1,0:T(8,128)(2,1)}, bf16[12,512,256]{2,1,0:T(8,128)(2,1)}, bf16[768,384]{1,0:T(8,128)(2,1)}, ...) custom-call(s32[7]{0:T(128)} %concatenate.54.sc, bf16[4,512,768]{2,1,0:T(8,128)(2,1)} %get-tuple-element.435.resid, ...), custom_call_target="tpu_custom_call" | custom-call | flops 4831838208 | bytes 44040192 | tf_op jit(solution)/shard_map/post/pallas_call | solution.py:533
  295.8 17.3 %unmix.2 = (bf16[384,1024]{1,0:T(8,128)(2,1)}, bf16[384,1024]{1,0:T(8,128)(2,1)}, bf16[384,1024]{1,0:T(8,128)(2,1)}, bf16[384,1024]{1,0:T(8,128)(2,1)}, bf16[384...) custom-call(s32[7]{0:T(128)} %concatenate.54.sc, ...), custom_call_target="tpu_custom_call" | custom-call | flops 4831838208 | bytes 31457280 | tf_op jit(solution)/shard_map/unmix/pallas_call | solution.py:624
  317.5 17.4 %unmix.3 = (bf16[384,1024]{1,0:T(8,128)(2,1)}, bf16[384,1024]{1,0:T(8,128)(2,1)}, bf16[384,1024]{1,0:T(8,128)(2,1)}, bf16[384,1024]{1,0:T(8,128)(2,1)}, bf16[384...) custom-call(s32[7]{0:T(128)} %concatenate.54.sc, ...), custom_call_target="tpu_custom_call", output_to_operand_aliasing={{8}: (13, {}), {9}: (14, {})} | custom-call | flops 4831838208 | bytes 31457280 | tf_op jit(solution)/shard_map/unmix/pallas_call | solution.py:624
  344.0 16.3 %up_grad.1 = (bf16[768,1536]{1,0:T(8,128)(2,1)}, bf16[768,1536]{1,0:T(8,128)(2,1)}) custom-call(s32[7]{0:T(128)} %concatenate.54.sc, bf16[2048,768]{1,0:T(8,128)(2,1)} %bitcast.137, bf16[2048,3072]{1,0:T(8,128)(2,1)} %get-tuple-element.494.up_grad), custom_call_target="tpu_custom_call" | custom-call | flops 9663676416 | bytes 15728640 | tf_op jit(solution)/shard_map/up_grad/pallas_call | solution.py:427
  370.4 15.6 %down_grad.1 = (bf16[3072,384]{1,0:T(8,128)(2,1)}, bf16[3072,384]{1,0:T(8,128)(2,1)}) custom-call(s32[7]{0:T(128)} %concatenate.54.sc, bf16[2048,3072]{1,0:T(8,128)(2,1)} %get-tuple-element.514.active, bf16[2048,768]{1,0:T(8,128)(2,1)} %bitcast.135), custom_call_target="tpu_custom_call" | custom-call | flops 9663676416 | bytes 15728640 | tf_op jit(solution)/shard_map/down_grad/pallas_call | solution.py:396
  396.5 8.9 %collect.1 = (bf16[432,384]{1,0:T(8,128)(2,1)}, bf16[432,384]{1,0:T(8,128)(2,1)}, bf16[432,384]{1,0:T(8,128)(2,1)}, bf16[432,384]{1,0:T(8,128)(2,1)}, bf16[432,3...) custom-call(s32[7]{0:T(128)} %concatenate.54.sc, ...), custom_call_target="tpu_custom_call" | custom-call | bytes 15925248 | tf_op jit(solution)/shard_map/collect/pallas_call | solution.py:860
  406.6 7.4 %collective-permute-done.57.refs_0_ = bf16[384,1024]{1,0:T(8,128)(2,1)} collective-permute-done((bf16[384,1024]{1,0:T(8,128)(2,1)}, bf16[384,1024]{1,0:T(8,128)(2,1)}, u32[]{:S(2)}, u32[]{:S(2)}) %collective-permute-start.57) | collective-permute-done | bytes 786464 | tf_op jit(solution)/shard_map/ppermute | solution.py:910
  414.9 16.5 %out.3 = (bf16[2,512,768]{2,1,0:T(8,128)(2,1)}, bf16[2,512,768]{2,1,0:T(8,128)(2,1)}) custom-call(s32[7]{0:T(128)} %concatenate.54.sc, bf16[4,512,3072]{2,1,0:T(8,128)(2,1)} %bitcast.139, bf16[4,512,768]{2,1,0:T(8,128)(2,1)} %get-tuple-element.435.resid, bf16[3072,384]{1,0:T(8,128)(2,1)} %get-tuple-element.440.dn_own, ...), custom_call_target="tpu_custom_call" | custom-call | flops 9663676416 | bytes 23592960 | tf_op jit(solution)/shard_map/out/pallas_call | solution.py:460
  437.0 15.7 %close.1 = (f32[2,8,2,64,768]{4,3,2,1,0:T(8,128)}, f32[2,8,2,64,768]{4,3,2,1,0:T(8,128)}, bf16[2,768,384]{2,1,0:T(8,128)(2,1)}, f32[1,768]{1,0:T(1,128)}) custom-call(s32[7]{0:T(128)} %concatenate.54.sc, bf16[2,8,2,64,768]{4,3,2,1,0:T(8,128)(2,1)} %bitcast.109, bf16[2,8,64,768]{3,2,1,0:T(8,128)(2,1)} %bitcast.143, bf16[2,8,64,768]{3,2,1,0:T(8,128)(2,1)} %bitcast.19.res_got, ...), custom_call_target="tpu_custom_call" | custom-call | flops 4831838208 | bytes 29884416 | tf_op jit(solution)/shard_map/close/pallas_call | solution.py:713
  472.7 17.4 %collective-permute-done.71.refs_1_ = bf16[432,384]{1,0:T(8,128)(2,1)S(1)} collective-permute-done((bf16[432,384]{1,0:T(8,128)(2,1)}, bf16[432,384]{1,0:T(8,128)(2,1)S(1)}, u32[]{:S(2)}, u32[]{:S(2)}) %collective-permute-start.71) | collective-permute-done | bytes 331808 | tf_op jit(solution)/shard_map/ppermute | solution.py:906
  (341 shorter events, 219.8 us)
Async XLA Ops:
  3.5 41.2 %collective-permute-start.16 = (bf16[2,8,64,768]{3,2,1,0:T(8,128)(2,1)}, bf16[2,8,64,768]{3,2,1,0:T(8,128)(2,1)}, u32[]{:S(2)}, u32[]{:S(2)}) collective-permute-start(bf16[2,8,64,768]{3,2,1,0:T(8,128)(2,1)} %dynamic-slice_bitcast_fusion.1), channel_id=1, source_target_pairs={{0,1},{1,0},{2,3},{3,2},{4,5},{5,4},{6,7},{7,6},{8,9},{9,8},{10,11... | collective-permute-start | bytes 4718600 | tf_op jit(solution)/shard_map/ppermute | solution.py:906
  5.3 41.6 %collective-permute-start.20 = (bf16[2,8,64,768]{3,2,1,0:T(8,128)(2,1)}, bf16[2,8,64,768]{3,2,1,0:T(8,128)(2,1)S(1)}, u32[]{:S(2)}, u32[]{:S(2)}) collective-permute-start(bf16[2,8,64,768]{3,2,1,0:T(8,128)(2,1)} %dynamic-slice_bitcast_fusion), channel_id=1, source_target_pairs={{0,1},{1,0},{2,3},{3,2},{4,5},{5,4},{6,7},{7,6},{8,9},{9,8},{10,11... | collective-permute-start | bytes 4718600 | tf_op jit(solution)/shard_map/ppermute | solution.py:906
  42.0 32.3 %collective-permute-start.10 = (bf16[384,1024]{1,0:T(8,128)(2,1)S(1)}, bf16[384,1024]{1,0:T(8,128)(2,1)S(1)}, u32[]{:S(2)}, u32[]{:S(2)}) collective-permute-start(bf16[384,1024]{1,0:T(8,128)(2,1)S(1)} %bitcast.110), channel_id=1, source_target_pairs={{0,2},{1,3},{2,0},{3,1},{4,6},{5,7},{6,4},{7,5},{8,10},{9,11},{10,... | collective-permute-start | bytes 2359304 | tf_op jit(solution)/shard_map/ppermute | solution.py:906
  46.1 29.7 %collective-permute-start.11 = (bf16[384,1024]{1,0:T(8,128)(2,1)S(1)}, bf16[384,1024]{1,0:T(8,128)(2,1)S(1)}, u32[]{:S(2)}, u32[]{:S(2)}) collective-permute-start(bf16[384,1024]{1,0:T(8,128)(2,1)S(1)} %bitcast.111), channel_id=1, source_target_pairs={{0,4},{1,5},{2,6},{3,7},{4,0},{5,1},{6,2},{7,3},{8,12},{9,13},{10,... | collective-permute-start | bytes 2359304 | tf_op jit(solution)/shard_map/ppermute | solution.py:906
  46.8 29.0 %collective-permute-start.12 = (bf16[384,1024]{1,0:T(8,128)(2,1)S(1)}, bf16[384,1024]{1,0:T(8,128)(2,1)}, u32[]{:S(2)}, u32[]{:S(2)}) collective-permute-start(bf16[384,1024]{1,0:T(8,128)(2,1)S(1)} %bitcast.112), channel_id=1, source_target_pairs={{0,8},{1,9},{2,10},{3,11},{4,12},{5,13},{6,14},{7,15},{8,16},{9,17... | collective-permute-start | bytes 2359304 | tf_op jit(solution)/shard_map/ppermute | solution.py:910
  82.8 32.9 %collective-permute-start.24 = (bf16[384,1024]{1,0:T(8,128)(2,1)S(1)}, bf16[384,1024]{1,0:T(8,128)(2,1)S(1)}, u32[]{:S(2)}, u32[]{:S(2)}) collective-permute-start(bf16[384,1024]{1,0:T(8,128)(2,1)S(1)} %collective-permute-done.10.refs_1_.refs_5_), channel_id=1, source_target_pairs={{0,4},{1,5},{2,6},{3,7},{4,0},{5,1},{6,2},{7,3},{8,12},{9,13},{10,... | collective-permute-start | bytes 2359304 | tf_op jit(solution)/shard_map/ppermute | solution.py:906
  83.8 31.9 %collective-permute-start.25 = (bf16[384,1024]{1,0:T(8,128)(2,1)}, bf16[384,1024]{1,0:T(8,128)(2,1)}, u32[]{:S(2)}, u32[]{:S(2)}) collective-permute-start(bf16[384,1024]{1,0:T(8,128)(2,1)} %collective-permute-done.12.refs_4_.refs_0_), channel_id=1, source_target_pairs={{0,2},{1,3},{2,0},{3,1},{4,6},{5,7},{6,4},{7,5},{8,10},{9,11},{10,... | collective-permute-start | bytes 2359304 | tf_op jit(solution)/shard_map/ppermute | solution.py:906
  85.3 30.4 %collective-permute-start.26 = (bf16[384,1024]{1,0:T(8,128)(2,1)}, bf16[384,1024]{1,0:T(8,128)(2,1)S(1)}, u32[]{:S(2)}, u32[]{:S(2)}) collective-permute-start(bf16[384,1024]{1,0:T(8,128)(2,1)} %collective-permute-done.12.refs_4_.refs_0_), channel_id=1, source_target_pairs={{0,8},{1,9},{2,10},{3,11},{4,12},{5,13},{6,14},{7,15},{8,16},{9,17... | collective-permute-start | bytes 2359304 | tf_op jit(solution)/shard_map/ppermute | solution.py:910
  85.9 23.3 %collective-permute-start.28 = (bf16[496,384]{1,0:T(8,128)(2,1)}, bf16[496,384]{1,0:T(8,128)(2,1)}, u32[]{:S(2)}, u32[]{:S(2)}) collective-permute-start(bf16[496,384]{1,0:T(8,128)(2,1)} %collective-permute-done.22.refs_10_), channel_id=1, source_target_pairs={{0,8},{1,9},{2,10},{3,11},{4,12},{5,13},{6,14},{7,15},{8,16},{9,17... | collective-permute-start | bytes 1142792 | tf_op jit(solution)/shard_map/ppermute | solution.py:910
  146.5 41.3 %collective-permute-start.37 = (bf16[12,1024,128]{2,1,0:T(8,128)(2,1)}, bf16[12,1024,128]{2,1,0:T(8,128)(2,1)}, u32[]{:S(2)}, u32[]{:S(2)}) collective-permute-start(bf16[12,1024,128]{2,1,0:T(8,128)(2,1)} %values.1.refs_8_), channel_id=1, source_target_pairs={{0,1},{1,0},{2,3},{3,2},{4,5},{5,4},{6,7},{7,6},{8,9},{9,8},{10,11... | collective-permute-start | bytes 9437192 | tf_op jit(solution)/shard_map/ppermute | solution.py:906
  146.5 53.1 %collective-permute-start.42 = (bf16[768,1536]{1,0:T(8,128)(2,1)}, bf16[768,1536]{1,0:T(8,128)(2,1)}, u32[]{:S(2)}, u32[]{:S(2)}) collective-permute-start(bf16[768,1536]{1,0:T(8,128)(2,1)} %get-tuple-element.438.up_own), channel_id=1, source_target_pairs={{0,1},{1,0},{2,3},{3,2},{4,5},{5,4},{6,7},{7,6},{8,9},{9,8},{10,11... | collective-permute-start | bytes 7077896 | tf_op jit(solution)/shard_map/ppermute | solution.py:906
  147.0 52.6 %collective-permute-start.43 = (bf16[3072,384]{1,0:T(8,128)(2,1)}, bf16[3072,384]{1,0:T(8,128)(2,1)}, u32[]{:S(2)}, u32[]{:S(2)}) collective-permute-start(bf16[3072,384]{1,0:T(8,128)(2,1)} %get-tuple-element.440.dn_own), channel_id=1, source_target_pairs={{0,1},{1,0},{2,3},{3,2},{4,5},{5,4},{6,7},{7,6},{8,9},{9,8},{10,11... | collective-permute-start | bytes 7077896 | tf_op jit(solution)/shard_map/ppermute | solution.py:906
  295.8 39.8 %collective-permute-start.47 = (bf16[2,512,768]{2,1,0:T(8,128)(2,1)}, bf16[2,512,768]{2,1,0:T(8,128)(2,1)}, u32[]{:S(2)}, u32[]{:S(2)}) collective-permute-start(bf16[2,512,768]{2,1,0:T(8,128)(2,1)} %get-tuple-element.474), channel_id=1, source_target_pairs={{0,1},{1,0},{2,3},{3,2},{4,5},{5,4},{6,7},{7,6},{8,9},{9,8},{10,11... | collective-permute-start | bytes 4718600 | tf_op jit(solution)/shard_map/ppermute | solution.py:906
  335.6 25.1 %collective-permute-start.52 = (bf16[12,1024,128]{2,1,0:T(8,128)(2,1)}, bf16[12,1024,128]{2,1,0:T(8,128)(2,1)}, u32[]{:S(2)}, u32[]{:S(2)}) collective-permute-start(bf16[12,1024,128]{2,1,0:T(8,128)(2,1)} %get-tuple-element.497), channel_id=1, source_target_pairs={{0,1},{1,0},{2,3},{3,2},{4,5},{5,4},{6,7},{7,6},{8,9},{9,8},{10,11... | collective-permute-start | bytes 9437192 | tf_op jit(solution)/shard_map/ppermute | solution.py:906
  361.7 27.5 %collective-permute-start.56 = (bf16[768,1536]{1,0:T(8,128)(2,1)}, bf16[768,1536]{1,0:T(8,128)(2,1)S(1)}, u32[]{:S(2)}, u32[]{:S(2)}) collective-permute-start(bf16[768,1536]{1,0:T(8,128)(2,1)} %get-tuple-element.517), channel_id=1, source_target_pairs={{0,1},{1,0},{2,3},{3,2},{4,5},{5,4},{6,7},{7,6},{8,9},{9,8},{10,11... | collective-permute-start | bytes 7077896 | tf_op jit(solution)/shard_map/ppermute | solution.py:906
  395.0 36.4 %collective-permute-start.58 = (bf16[384,1024]{1,0:T(8,128)(2,1)}, bf16[384,1024]{1,0:T(8,128)(2,1)}, u32[]{:S(2)}, u32[]{:S(2)}) collective-permute-start(bf16[384,1024]{1,0:T(8,128)(2,1)} %get-tuple-element.528), channel_id=1, source_target_pairs={{0,2},{1,3},{2,0},{3,1},{4,6},{5,7},{6,4},{7,5},{8,10},{9,11},{10,... | collective-permute-start | bytes 2359304 | tf_op jit(solution)/shard_map/ppermute | solution.py:906
  395.6 35.9 %collective-permute-start.59 = (bf16[384,1024]{1,0:T(8,128)(2,1)}, bf16[384,1024]{1,0:T(8,128)(2,1)}, u32[]{:S(2)}, u32[]{:S(2)}) collective-permute-start(bf16[384,1024]{1,0:T(8,128)(2,1)} %get-tuple-element.529), channel_id=1, source_target_pairs={{0,4},{1,5},{2,6},{3,7},{4,0},{5,1},{6,2},{7,3},{8,12},{9,13},{10,... | collective-permute-start | bytes 2359304 | tf_op jit(solution)/shard_map/ppermute | solution.py:906
  405.4 26.1 %collective-permute-start.61 = (bf16[432,384]{1,0:T(8,128)(2,1)}, bf16[432,384]{1,0:T(8,128)(2,1)S(1)}, u32[]{:S(2)}, u32[]{:S(2)}) collective-permute-start(bf16[432,384]{1,0:T(8,128)(2,1)} %get-tuple-element.549), channel_id=1, source_target_pairs={{0,24},{1,25},{2,26},{3,27},{4,28},{5,29},{6,30},{7,31},{8,0},{9,1... | collective-permute-start | bytes 995336 | tf_op jit(solution)/shard_map/ppermute | solution.py:910
  405.5 26.0 %collective-permute-start.62 = (bf16[432,384]{1,0:T(8,128)(2,1)}, bf16[432,384]{1,0:T(8,128)(2,1)S(1)}, u32[]{:S(2)}, u32[]{:S(2)}) collective-permute-start(bf16[432,384]{1,0:T(8,128)(2,1)} %get-tuple-element.550), channel_id=1, source_target_pairs={{0,2},{1,3},{2,0},{3,1},{4,6},{5,7},{6,4},{7,5},{8,10},{9,11},{10,... | collective-permute-start | bytes 995336 | tf_op jit(solution)/shard_map/ppermute | solution.py:906
  434.8 28.5 %collective-permute-start.68 = (bf16[432,384]{1,0:T(8,128)(2,1)}, bf16[432,384]{1,0:T(8,128)(2,1)S(1)}, u32[]{:S(2)}, u32[]{:S(2)}) collective-permute-start(bf16[432,384]{1,0:T(8,128)(2,1)} %get-tuple-element.572), channel_id=1, source_target_pairs={{0,2},{1,3},{2,0},{3,1},{4,6},{5,7},{6,4},{7,5},{8,10},{9,11},{10,... | collective-permute-start | bytes 995336 | tf_op jit(solution)/shard_map/ppermute | solution.py:906
  456.1 35.0 %collective-permute-start.74 = (bf16[16,64,384]{2,1,0:T(8,128)(2,1)}, bf16[16,64,384]{2,1,0:T(8,128)(2,1)S(1)}, u32[]{:S(2)}, u32[]{:S(2)}) collective-permute-start(bf16[16,64,384]{2,1,0:T(8,128)(2,1)} %dynamic-slice_bitcast_fusion.4), channel_id=1, source_target_pairs={{0,1},{1,0},{2,3},{3,2},{4,5},{5,4},{6,7},{7,6},{8,9},{9,8},{10,11... | collective-permute-start | bytes 2359304 | tf_op jit(solution)/shard_map/ppermute | solution.py:906
  463.3 37.5 %collective-permute-start.64 = (bf16[384,1024]{1,0:T(8,128)(2,1)}, bf16[384,1024]{1,0:T(8,128)(2,1)}, u32[]{:S(2)}, u32[]{:S(2)}) collective-permute-start(bf16[384,1024]{1,0:T(8,128)(2,1)} %get-tuple-element.560), channel_id=1, source_target_pairs={{0,24},{1,25},{2,26},{3,27},{4,28},{5,29},{6,30},{7,31},{8,0},{9,1... | collective-permute-start | bytes 2359304 | tf_op jit(solution)/shard_map/ppermute | solution.py:910
  463.3 37.5 %collective-permute-start.65 = (bf16[384,1024]{1,0:T(8,128)(2,1)}, bf16[384,1024]{1,0:T(8,128)(2,1)}, u32[]{:S(2)}, u32[]{:S(2)}) collective-permute-start(bf16[384,1024]{1,0:T(8,128)(2,1)} %get-tuple-element.561), channel_id=1, source_target_pairs={{0,2},{1,3},{2,0},{3,1},{4,6},{5,7},{6,4},{7,5},{8,10},{9,11},{10,... | collective-permute-start | bytes 2359304 | tf_op jit(solution)/shard_map/ppermute | solution.py:906
  466.5 34.3 %collective-permute-start.66 = (bf16[384,1024]{1,0:T(8,128)(2,1)}, bf16[384,1024]{1,0:T(8,128)(2,1)}, u32[]{:S(2)}, u32[]{:S(2)}) collective-permute-start(bf16[384,1024]{1,0:T(8,128)(2,1)} %get-tuple-element.562), channel_id=1, source_target_pairs={{0,4},{1,5},{2,6},{3,7},{4,0},{5,1},{6,2},{7,3},{8,12},{9,13},{10,... | collective-permute-start | bytes 2359304 | tf_op jit(solution)/shard_map/ppermute | solution.py:906
  (121 other events, 1602.3 us)

commit v7 on v6

--- a/solution.py
+++ b/solution.py
@@ -984,28 +984,30 @@
 
     rand = rand_mix.reshape(3, 2, HALF, LMAX)
     blocks = side(pick(rand, core, 1), other(pick(rand, 1 - core, 1)), 0)
-    weights, rands, far_lengths = together(
-        (gather_step(weights, 0), {(0, 0, 0): blocks.reshape(SUBS * HALF, LMAX)}, other(lengths))
-    )
-    sc = jnp.concatenate([near_sc[:5], far_lengths])
+    weights, rands = together((gather_step(weights, 0), {(0, 0, 0): blocks.reshape(SUBS * HALF, LMAX)}))
     weights, tokens_far = together((gather_step(weights, 1), other(pick(tokens, 1 - core, 2))))
     weights, grad_far = together((gather_step(weights, 2), other(pick(grad_out, 1 - core, 2))))
-    rands, weights = together((gather_step(rands, 0), gather_step(weights, 3)))
-    rands, weights = together((gather_step(rands, 1), gather_step(weights, 4)))
-
+    weights, far_lengths = together((gather_step(weights, 3), other(lengths)))
+    sc = jnp.concatenate([near_sc[:5], far_lengths])
+    weights, rands = together((gather_step(weights, 4), rands))
+
+    rands = gather_step(rands, 0)
     down, up, out, value, gain_rows = place_weights(sc, in_order(weights))
-    value_far = other(value)
+    rands, value, value_far, gain_rows, out, down, up = together(
+        (rands, value, other(value), gain_rows, out, down, up)
+    )
     gain_rows = gain_rows.reshape(16, 2, 8, SIDE)[:, :, 0]
     gain_one = gain_rows[..., :24].reshape(1, WIDTH).astype(F32)
     gain_two = gain_rows[..., 24:48].reshape(1, WIDTH).astype(F32)
+    rands = gather_step(rands, 1)
     v_own = run_values(sc, tokens.reshape(2, LMAX, WIDTH), gain_one, value, value_far)
-    rands, value_far, v_own, gain_one, gain_two, out, down, up = together(
-        (gather_step(rands, 2), value_far, v_own, gain_one, gain_two, out, down, up)
-    )
-    rands, v_far, out = together((gather_step(rands, 3), other(v_own), (out, other(out))))
+    rands, v_own, out, down, up = together((rands, v_own, (out, other(out)), down, up))
+    rands, v_own, v_far, down, up = together((gather_step(rands, 2), v_own, other(v_own), down, up))
+    rands, v_far, down, up = together((gather_step(rands, 3), v_far, (down, other(down)), up))
     near = [rands[k, y_at, x_at] for k in range(2) for y_at in range(2) for x_at in range(2)]
+    rands = gather_step(rands, 4)
     mixing = run_mix(sc, (0, 1), near, v_own, v_far, ())
-    rands, up, down, mixing = together((gather_step(rands, 4), (up, other(up)), (down, other(down)), mixing))
+    rands, up, mixing = together((rands, (up, other(up)), mixing))
     shares = in_order(rands)
     heads, mean = run_mix(sc, (2, 3), shares[8:], v_own, v_far, mixing)
 
@@ -1018,13 +1020,12 @@
     *far, back_own, back_far = run_unmix(
         sc, (3, 2), shares[12:] + shares[8:12], v_own, v_far, grad_heads, mean, ()
     )
+    far, back_own, back_far, res_got, d_out_got = together((far, back_own, back_far, other(res_far), other(d_out_far)))
     have, got = scatter_send(by_place(far, (3, 2)), 0)
     *near, back_own, back_far = run_unmix(
         sc, (1, 0), shares[4:8] + shares[:4], v_own, v_far, grad_heads, mean, (back_own, back_far)
     )
-    have, got, near, back_own, back_far, res_got, d_out_got = together(
-        (have, got, near, back_own, back_far, other(res_far), other(d_out_far))
-    )
+    have, got, near, back_own, back_far = together((have, got, near, back_own, back_far))
     have = {**scatter_add(have, got, 0), **by_place(near, (1, 0))}
 
     have, got = scatter_send(have, 1)
@@ -1038,42 +1039,49 @@
     have = scatter_add(have, got, 2)
 
     have, got = scatter_send(have, 3)
-    packed = run_collect(sc, down_own, other(down_far), up_own, up_got, d_out_own, d_out_got)
-    sums, sums_got = scatter_send(by_place(packed), 0)
     out_own, out_far = run_out(sc, active, resid, down)
-    have, got, sums, sums_got, out_own, out_far = together((have, got, sums, sums_got, out_own, out_far))
-    have, sums = scatter_add(have, got, 3), scatter_add(sums, sums_got, 0)
+    have, got, out_own, out_far, down_got = together((have, got, out_own, out_far, other(down_far)))
+    have = scatter_add(have, got, 3)
 
     have, got = scatter_send(have, 4)
-    sums, sums_got = scatter_send(sums, 1)
-    sums, sums_got = scatter_send(scatter_add(sums, sums_got, 1), 2)
+    packed = run_collect(sc, down_own, down_got, up_own, up_got, d_out_own, d_out_got)
+    have, got, packed, out_got = together((have, got, packed, other(out_far)))
+    rand_sum = scatter_add(have, got, 4)[0, 0, 0].reshape(2, 3, HALF, LMAX)
+
+    sums, got = scatter_send(by_place(packed), 0)
     output, tokens_grad, d_value, d_gain_one = run_close(
-        sc, tokens, res_own, res_got, out_own, other(out_far), back_own, back_got, gain_one, value, value_far
-    )
+        sc, tokens, res_own, res_got, out_own, out_got, back_own, back_got, gain_one, value, value_far
+    )
+    blocks, blocks_far = pick(rand_sum, core), other(pick(rand_sum, 1 - core))
+    sums, got, output, tokens_grad, d_value, d_gain_one, blocks, blocks_far = together(
+        (sums, got, output, tokens_grad, d_value, d_gain_one, blocks, blocks_far)
+    )
+    sums = scatter_add(sums, got, 0)
+
+    sums, got = scatter_send(sums, 1)
     gain_pair = jnp.concatenate([d_gain_one, d_gain_two]).reshape(2, 16, 1, 48).astype(BF16)
     gain_pair = jnp.pad(gain_pair, ((0, 0), (0, 0), (0, 15), (0, SIDE - 48)))
     small = jnp.concatenate([d_value.reshape(2, 16, 48, SIDE), gain_pair], 2)
     small = add_low(pick(small, core), other(pick(small, 1 - core))).reshape(4, 2, 2, 64, SIDE)
-    have, got, sums, sums_got, small, output, tokens_grad = together(
-        (have, got, sums, sums_got, small, output, tokens_grad)
-    )
-    rand_sum = scatter_add(have, got, 4)[0, 0, 0].reshape(2, 3, HALF, LMAX)
-    sums = scatter_add(sums, sums_got, 2)
-
-    sums, sums_got = scatter_send(sums, 3)
+    sums, got, small = together((sums, got, small))
+    sums = scatter_add(sums, got, 1)
+
+    sums, got = scatter_send(sums, 2)
     small = add_low(pick(small, x, 2), swap(pick(small, 1 - x, 2), TO_X))
-    blocks, blocks_far = pick(rand_sum, core), other(pick(rand_sum, 1 - core))
-    sums, sums_got, small, blocks, blocks_far = together((sums, sums_got, small, blocks, blocks_far))
-    sums = scatter_add(sums, sums_got, 3)
-
-    sums, sums_got = scatter_send(sums, 4)
+    sums, got, small = together((sums, got, small))
+    sums = scatter_add(sums, got, 2)
+
+    sums, got = scatter_send(sums, 3)
     small = add_low(pick(small, y, 1), swap(pick(small, 1 - y, 1), TO_Y))
-    sums, sums_got, small = together((sums, sums_got, small))
-    big_sum = scatter_add(sums, sums_got, 4)[0, 0, 0]
-
+    sums, got, small = together((sums, got, small))
+    sums = scatter_add(sums, got, 3)
+
+    sums, got = scatter_send(sums, 4)
     small_sum = pick(small, z).astype(F32)
     for k in range(1, PLANES):
         small_sum = small_sum + ring(pick(small, lax.rem(z + PLANES - k, PLANES)), -k).astype(F32)
+    sums, got, small_sum = together((sums, got, small_sum))
+    big_sum = scatter_add(sums, got, 4)[0, 0, 0]
     big_far, small_far = other(big_sum), other(small_sum)
 
     rows_of = lambda value, rows: pick(value.reshape(-1, 2, rows, SIDE), core, 1)

time: 560 us -> 527 us (0.941)
  waiting for transfers between devices: 195 us -> 160 us
    ppermute x66, waiting for transfers between devices: 144 us -> 98.4 us  [swap(): return lax.ppermute(x, BOTH, [(d, d ^ bit) for d in range(DEVICES)])]
    ppermute x23, waiting for transfers between devices: 50.6 us -> 61.9 us  [ring(): lax.ppermute(x, BOTH, [(d, (d + 8 * way) % DEVICES) for d in range(DEVICE...]
    ppermute x23, starting transfers between devices: 23.6 us -> 31.8 us  [ring(): lax.ppermute(x, BOTH, [(d, (d + 8 * way) % DEVICES) for d in range(DEVICE...]
    ppermute x66, starting transfers between devices: 50.8 us -> 43 us  [swap(): return lax.ppermute(x, BOTH, [(d, d ^ bit) for d in range(DEVICES)])]
  transfers between devices with their start and end apart: 89 -> 89, of which waited for: 43 -> 46; matrix products, arithmetic and copies ran while one was open for 4% -> 3% of each run, Pallas kernels for 28% -> 30%
where the time goes in v7:
time: 527 us; the launch traced here: 521 us
  Pallas kernels  250 us (47%)
  waiting for transfers between devices  160 us (30%)
  starting transfers between devices  74.8 us (14%)
  local copies, waits for them, and re-layouts  24.8 us (5%)
  other arithmetic  9.33 us (2%)
    ppermute x66, waiting for transfers between devices, swap(): return lax.ppermute(x, BOTH, [(d, d ^ bit) for d in range(DEVICES)])  98.4 us
    ppermute x23, waiting for transfers between devices, ring(): lax.ppermute(x, BOTH, [(d, (d + 8 * way) % DEVICES) for d in range(DEVICE...  61.9 us
    pallas_call x1, Pallas kernels, run_units(): pl.pallas_call(units_kernel, grid_spec=pltpu.PrefetchScalarGridSpec(num_s...  46.5 us
    ppermute x66, starting transfers between devices, swap(): return lax.ppermute(x, BOTH, [(d, d ^ bit) for d in range(DEVICES)])  43 us
    pallas_call x2, Pallas kernels, run_unmix(): pl.pallas_call(partial(unmix_kernel, bool(carry)), grid_spec=pltpu.Prefet...  34.6 us
    ppermute x23, starting transfers between devices, ring(): lax.ppermute(x, BOTH, [(d, (d + 8 * way) % DEVICES) for d in range(DEVICE...  31.8 us
    pallas_call x10, Pallas kernels, run_add(): pl.pallas_call(partial(add_kernel, groups), grid=(parts,), in_specs=[bloc...  28.6 us
    pallas_call x2, Pallas kernels, run_mix(): pl.pallas_call(partial(mix_kernel, bool(carry)), grid_spec=pltpu.Prefetch...  18.7 us
  transfers between devices with their start and end apart: 89, of which 46 were waited for; matrix products, arithmetic and copies ran while one was open for 3% of the time, Pallas kernels for 30%

profile of v7, /device:TPU:0, one launch (start us, length us, event | category | flops | bytes accessed | tf_op | source)
XLA Modules:
  0.0 521.1 jit_solution(4158818253585469710)
XLA Ops:
  33.7 8.9 %collective-permute-done.10.refs_5_ = bf16[496,384]{1,0:T(8,128)(2,1)S(1)} collective-permute-done((bf16[496,384]{1,0:T(8,128)(2,1)}, bf16[496,384]{1,0:T(8,128)(2,1)S(1)}, u32[]{:S(2)}, u32[]{:S(2)}) %collective-permute-start.10) | collective-permute-done | bytes 380960 | tf_op jit(solution)/shard_map/ppermute | solution.py:906
  46.8 6.8 %collective-permute-done.13.refs_6_ = bf16[496,384]{1,0:T(8,128)(2,1)S(1)} collective-permute-done((bf16[496,384]{1,0:T(8,128)(2,1)}, bf16[496,384]{1,0:T(8,128)(2,1)S(1)}, u32[]{:S(2)}, u32[]{:S(2)}) %collective-permute-start.13) | collective-permute-done | bytes 380960 | tf_op jit(solution)/shard_map/ppermute | solution.py:906
  59.8 6.3 %collective-permute-done.17.refs_7_ = bf16[496,384]{1,0:T(8,128)(2,1)S(1)} collective-permute-done((bf16[496,384]{1,0:T(8,128)(2,1)S(1)}, bf16[496,384]{1,0:T(8,128)(2,1)S(1)}, u32[]{:S(2)}, u32[]{:S(2)}) %collective-permute-start.17) | collective-permute-done | bytes 380960 | tf_op jit(solution)/shard_map/ppermute | solution.py:910
  68.5 8.7 %collective-permute-done.21.refs_11_ = bf16[496,384]{1,0:T(8,128)(2,1)S(1)} collective-permute-done((bf16[496,384]{1,0:T(8,128)(2,1)S(1)}, bf16[496,384]{1,0:T(8,128)(2,1)S(1)}, u32[]{:S(2)}, u32[]{:S(2)}) %collective-permute-start.21) | collective-permute-done | bytes 380960 | tf_op jit(solution)/shard_map/ppermute | solution.py:906
  85.0 7.2 %place.1 = (bf16[3072,384]{1,0:T(8,128)(2,1)}, bf16[768,1536]{1,0:T(8,128)(2,1)}, bf16[768,384]{1,0:T(8,128)(2,1)}, bf16[768,384]{1,0:T(8,128)(2,1)}, bf16[256,384]{1,0:T(8,128)(2,1)}) custom-call(s32[7]{0:T(128)} %concatenate.54.sc, bf16[496,384]{1,0:T(8,128)(2,1)} %pack.1.refs_0_, bf16[496,384]{1,0:T(8,128)(2,1)} %copy-done.26, ...), custom_call_target="tpu_custom_call" | custom-call | bytes 12189696 | tf_op jit(solution)/shard_map/place/pallas_call | solution.py:810
  101.2 7.8 %values.1.refs_8_ = bf16[12,1024,128]{2,1,0:T(8,128)(2,1)} custom-call(s32[7]{0:T(128)} %concatenate.54.sc, bf16[2,1024,768]{2,1,0:T(8,128)(2,1)} %tok.1, f32[1,768]{1,0:T(1,128)} %reshape.205.gain, bf16[768,384]{1,0:T(8,128)(2,1)} %get-tuple-element.436.w_own, bf16[768,384]{1,0:T(8,128)(2,1)} %copy-done.63), custom_call_target="tpu_custom_call" | custom-call | flops 2415919104 | bytes 6291456 | tf_op jit(solution)/shard_map/values/pallas_call | solution.py:80
  109.0 5.4 %collective-permute-done.28.refs_3_.refs_7_ = bf16[384,1024]{1,0:T(8,128)(2,1)} collective-permute-done((bf16[384,1024]{1,0:T(8,128)(2,1)S(1)}, bf16[384,1024]{1,0:T(8,128)(2,1)}, u32[]{:S(2)}, u32[]{:S(2)}) %collective-permute-start.28) | collective-permute-done | bytes 786464 | tf_op jit(solution)/shard_map/ppermute | solution.py:906
  121.1 16.8 %collective-permute-done.32.refs_6_.refs_2_ = bf16[384,1024]{1,0:T(8,128)(2,1)S(1)} collective-permute-done((bf16[384,1024]{1,0:T(8,128)(2,1)}, bf16[384,1024]{1,0:T(8,128)(2,1)S(1)}, u32[]{:S(2)}, u32[]{:S(2)}) %collective-permute-start.32) | collective-permute-done | bytes 786464 | tf_op jit(solution)/shard_map/ppermute | solution.py:906
  143.1 19.9 %collective-permute-done.36.refs_7_.refs_3_ = bf16[384,1024]{1,0:T(8,128)(2,1)S(1)} collective-permute-done((bf16[384,1024]{1,0:T(8,128)(2,1)}, bf16[384,1024]{1,0:T(8,128)(2,1)S(1)}, u32[]{:S(2)}, u32[]{:S(2)}) %collective-permute-start.36) | collective-permute-done | bytes 786464 | tf_op jit(solution)/shard_map/ppermute | solution.py:910
  168.3 9.3 %mix.2 = (bf16[12,512,256]{2,1,0:T(8,128)(2,1)}, f32[12,512,256]{2,1,0:T(8,128)}) custom-call(s32[7]{0:T(128)} %concatenate.54.sc, bf16[384,1024]{1,0:T(8,128)(2,1)} %bitcast.113, bf16[384,1024]{1,0:T(8,128)(2,1)} %copy-done.8, bf16[384,1024]{1,0:T(8,128)(2,1)} %copy-done.9, bf16[384,1024]{1,0:T(8,128)(2,1)} %collective-permute-done.28.refs_3_.refs_7_, ...), custom_call_target="tpu_custom_call" | custom-call | flops 3221225472 | bytes 14155776 | tf_op jit(solution)/shard_map/mix/pallas_call | solution.py:188
  177.7 7.1 %collective-permute-done.40.refs_3_.refs_7_ = bf16[384,1024]{1,0:T(8,128)(2,1)} collective-permute-done((bf16[384,1024]{1,0:T(8,128)(2,1)}, bf16[384,1024]{1,0:T(8,128)(2,1)}, u32[]{:S(2)}, u32[]{:S(2)}) %collective-permute-start.40) | collective-permute-done | bytes 786464 | tf_op jit(solution)/shard_map/ppermute | solution.py:906
  186.9 9.4 %mix.3 = (bf16[12,512,256]{2,1,0:T(8,128)(2,1)}, f32[12,512,256]{2,1,0:T(8,128)}) custom-call(s32[7]{0:T(128)} %concatenate.54.sc, bf16[384,1024]{1,0:T(8,128)(2,1)} %copy-done.4, bf16[384,1024]{1,0:T(8,128)(2,1)} %copy-done.5, bf16[384,1024]{1,0:T(8,128)(2,1)} %collective-permute-done.37.refs_2_.refs_6_, ...), custom_call_target="tpu_custom_call", output_to_operand_aliasing={{0}: (11, {}), {1}: (12, {})} | custom-call | flops 3221225472 | bytes 14155776 | tf_op jit(solution)/shard_map/mix/pallas_call | solution.py:188
  196.3 12.5 %pre.1 = (bf16[4,512,768]{2,1,0:T(8,128)(2,1)}, bf16[4,512,768]{2,1,0:T(8,128)(2,1)}, bf16[4,512,768]{2,1,0:T(8,128)(2,1)}, bf16[4,512,768]{2,1,0:T(8,128)(2,1)}) custom-call(s32[7]{0:T(128)} %concatenate.54.sc, bf16[2,8,2,64,768]{4,3,2,1,0:T(8,128)(2,1)} %bitcast.108, bf16[2,8,64,768]{3,2,1,0:T(8,128)(2,1)} %collective-permute-done.12.tok_far, ...), custom_call_target="tpu_custom_call" | custom-call | flops 2415919104 | bytes 25165824 | tf_op jit(solution)/shard_map/pre/pallas_call | solution.py:262
  208.8 46.5 %units.1 = (bf16[2048,3072]{1,0:T(8,128)(2,1)}, bf16[2048,3072]{1,0:T(8,128)(2,1)}, bf16[2048,768]{1,0:T(8,128)(2,1)}) custom-call(s32[7]{0:T(128)} %concatenate.54.sc, bf16[2048,768]{1,0:T(8,128)(2,1)} %bitcast.137, bf16[2048,768]{1,0:T(8,128)(2,1)} %bitcast.135, bf16[768,1536]{1,0:T(8,128)(2,1)} %get-tuple-element.500.up_own, ...), custom_call_target="tpu_custom_call" | custom-call | flops 28991029248 | bytes 37748736 | tf_op jit(solution)/shard_map/units/pallas_call | solution.py:356
  255.3 18.4 %post.1 = (bf16[2,512,768]{2,1,0:T(8,128)(2,1)}, bf16[2,512,768]{2,1,0:T(8,128)(2,1)}, bf16[12,512,256]{2,1,0:T(8,128)(2,1)}, bf16[768,384]{1,0:T(8,128)(2,1)}, ...) custom-call(s32[7]{0:T(128)} %concatenate.54.sc, bf16[4,512,768]{2,1,0:T(8,128)(2,1)} %get-tuple-element.497.resid, ...), custom_call_target="tpu_custom_call" | custom-call | flops 4831838208 | bytes 44040192 | tf_op jit(solution)/shard_map/post/pallas_call | solution.py:533
  274.3 17.2 %unmix.2 = (bf16[384,1024]{1,0:T(8,128)(2,1)}, bf16[384,1024]{1,0:T(8,128)(2,1)}, bf16[384,1024]{1,0:T(8,128)(2,1)}, bf16[384,1024]{1,0:T(8,128)(2,1)}, bf16[384...) custom-call(s32[7]{0:T(128)} %concatenate.54.sc, ...), custom_call_target="tpu_custom_call" | custom-call | flops 4831838208 | bytes 31457280 | tf_op jit(solution)/shard_map/unmix/pallas_call | solution.py:624
  297.7 17.4 %unmix.3 = (bf16[384,1024]{1,0:T(8,128)(2,1)}, bf16[384,1024]{1,0:T(8,128)(2,1)}, bf16[384,1024]{1,0:T(8,128)(2,1)}, bf16[384,1024]{1,0:T(8,128)(2,1)}, bf16[384...) custom-call(s32[7]{0:T(128)} %concatenate.54.sc, ...), custom_call_target="tpu_custom_call", output_to_operand_aliasing={{8}: (13, {}), {9}: (14, {})} | custom-call | flops 4831838208 | bytes 31457280 | tf_op jit(solution)/shard_map/unmix/pallas_call | solution.py:624
  323.8 16.2 %up_grad.1 = (bf16[768,1536]{1,0:T(8,128)(2,1)}, bf16[768,1536]{1,0:T(8,128)(2,1)}) custom-call(s32[7]{0:T(128)} %concatenate.54.sc, bf16[2048,768]{1,0:T(8,128)(2,1)} %bitcast.138, bf16[2048,3072]{1,0:T(8,128)(2,1)} %get-tuple-element.566.up_grad), custom_call_target="tpu_custom_call" | custom-call | flops 9663676416 | bytes 15728640 | tf_op jit(solution)/shard_map/up_grad/pallas_call | solution.py:427
  349.2 15.6 %down_grad.1 = (bf16[3072,384]{1,0:T(8,128)(2,1)}, bf16[3072,384]{1,0:T(8,128)(2,1)}) custom-call(s32[7]{0:T(128)} %concatenate.54.sc, bf16[2048,3072]{1,0:T(8,128)(2,1)} %get-tuple-element.586.active, bf16[2048,768]{1,0:T(8,128)(2,1)} %bitcast.136), custom_call_target="tpu_custom_call" | custom-call | flops 9663676416 | bytes 15728640 | tf_op jit(solution)/shard_map/down_grad/pallas_call | solution.py:396
  375.2 16.7 %out.3 = (bf16[2,512,768]{2,1,0:T(8,128)(2,1)}, bf16[2,512,768]{2,1,0:T(8,128)(2,1)}) custom-call(s32[7]{0:T(128)} %concatenate.54.sc, bf16[4,512,3072]{2,1,0:T(8,128)(2,1)} %bitcast.140, bf16[4,512,768]{2,1,0:T(8,128)(2,1)} %get-tuple-element.497.resid, bf16[3072,384]{1,0:T(8,128)(2,1)} %get-tuple-element.502.dn_own, bf16[3072,384]{1,0:T(8,128)(2,1)} %copy-done.61), custom_call_target="tpu_custom_call" | custom-call | flops 9663676416 | bytes 23592960 | tf_op jit(solution)/shard_map/out/pallas_call | solution.py:460
  399.7 8.6 %collect.1 = (bf16[432,384]{1,0:T(8,128)(2,1)}, bf16[432,384]{1,0:T(8,128)(2,1)}, bf16[432,384]{1,0:T(8,128)(2,1)}, bf16[432,384]{1,0:T(8,128)(2,1)}, bf16[432,3...) custom-call(s32[7]{0:T(128)} %concatenate.54.sc, ...), custom_call_target="tpu_custom_call" | custom-call | bytes 15925248 | tf_op jit(solution)/shard_map/collect/pallas_call | solution.py:860
  408.3 8.7 %collective-permute-done.61.refs_0_ = bf16[384,1024]{1,0:T(8,128)(2,1)S(1)} collective-permute-done((bf16[384,1024]{1,0:T(8,128)(2,1)}, bf16[384,1024]{1,0:T(8,128)(2,1)S(1)}, u32[]{:S(2)}, u32[]{:S(2)}) %collective-permute-start.61) | collective-permute-done | bytes 786464 | tf_op jit(solution)/shard_map/ppermute | solution.py:910
  428.5 15.8 %close.1 = (f32[2,8,2,64,768]{4,3,2,1,0:T(8,128)}, f32[2,8,2,64,768]{4,3,2,1,0:T(8,128)}, bf16[2,768,384]{2,1,0:T(8,128)(2,1)}, f32[1,768]{1,0:T(1,128)}) custom-call(s32[7]{0:T(128)} %concatenate.54.sc, bf16[2,8,2,64,768]{4,3,2,1,0:T(8,128)(2,1)} %bitcast.109, bf16[2,8,64,768]{3,2,1,0:T(8,128)(2,1)} %bitcast.144, bf16[2,8,64,768]{3,2,1,0:T(8,128)(2,1)} %bitcast.139, ...), custom_call_target="tpu_custom_call" | custom-call | flops 4831838208 | bytes 29884416 | tf_op jit(solution)/shard_map/close/pallas_call | solution.py:713
  454.3 5.6 %collective-permute-done.70.refs_1_ = bf16[432,384]{1,0:T(8,128)(2,1)S(1)} collective-permute-done((bf16[432,384]{1,0:T(8,128)(2,1)}, bf16[432,384]{1,0:T(8,128)(2,1)S(1)}, u32[]{:S(2)}, u32[]{:S(2)}) %collective-permute-start.70) | collective-permute-done | bytes 331808 | tf_op jit(solution)/shard_map/ppermute | solution.py:906
  (363 shorter events, 206.4 us)
Async XLA Ops:
  3.5 41.2 %collective-permute-start.12 = (bf16[2,8,64,768]{3,2,1,0:T(8,128)(2,1)}, bf16[2,8,64,768]{3,2,1,0:T(8,128)(2,1)}, u32[]{:S(2)}, u32[]{:S(2)}) collective-permute-start(bf16[2,8,64,768]{3,2,1,0:T(8,128)(2,1)} %dynamic-slice_bitcast_fusion.1), channel_id=1, source_target_pairs={{0,1},{1,0},{2,3},{3,2},{4,5},{5,4},{6,7},{7,6},{8,9},{9,8},{10,11... | collective-permute-start | bytes 4718600 | tf_op jit(solution)/shard_map/ppermute | solution.py:906
  5.3 41.5 %collective-permute-start.16 = (bf16[2,8,64,768]{3,2,1,0:T(8,128)(2,1)}, bf16[2,8,64,768]{3,2,1,0:T(8,128)(2,1)S(1)}, u32[]{:S(2)}, u32[]{:S(2)}) collective-permute-start(bf16[2,8,64,768]{3,2,1,0:T(8,128)(2,1)} %dynamic-slice_bitcast_fusion), channel_id=1, source_target_pairs={{0,1},{1,0},{2,3},{3,2},{4,5},{5,4},{6,7},{7,6},{8,9},{9,8},{10,11... | collective-permute-start | bytes 4718600 | tf_op jit(solution)/shard_map/ppermute | solution.py:906
  117.7 23.3 %collective-permute-start.35 = (bf16[12,1024,128]{2,1,0:T(8,128)(2,1)}, bf16[12,1024,128]{2,1,0:T(8,128)(2,1)}, u32[]{:S(2)}, u32[]{:S(2)}) collective-permute-start(bf16[12,1024,128]{2,1,0:T(8,128)(2,1)} %values.1.refs_8_), channel_id=1, source_target_pairs={{0,1},{1,0},{2,3},{3,2},{4,5},{5,4},{6,7},{7,6},{8,9},{9,8},{10,11... | collective-permute-start | bytes 9437192 | tf_op jit(solution)/shard_map/ppermute | solution.py:906
  117.7 20.2 %collective-permute-start.32 = (bf16[384,1024]{1,0:T(8,128)(2,1)}, bf16[384,1024]{1,0:T(8,128)(2,1)S(1)}, u32[]{:S(2)}, u32[]{:S(2)}) collective-permute-start(bf16[384,1024]{1,0:T(8,128)(2,1)} %collective-permute-done.26.refs_4_.refs_0_), channel_id=1, source_target_pairs={{0,4},{1,5},{2,6},{3,7},{4,0},{5,1},{6,2},{7,3},{8,12},{9,13},{10,... | collective-permute-start | bytes 2359304 | tf_op jit(solution)/shard_map/ppermute | solution.py:906
  119.8 21.2 %collective-permute-start.34 = (bf16[384,1024]{1,0:T(8,128)(2,1)S(1)}, bf16[384,1024]{1,0:T(8,128)(2,1)S(1)}, u32[]{:S(2)}, u32[]{:S(2)}) collective-permute-start(bf16[384,1024]{1,0:T(8,128)(2,1)S(1)} %collective-permute-done.30.refs_0_.refs_4_), channel_id=1, source_target_pairs={{0,8},{1,9},{2,10},{3,11},{4,12},{5,13},{6,14},{7,15},{8,16},{9,17... | collective-permute-start | bytes 2359304 | tf_op jit(solution)/shard_map/ppermute | solution.py:910
  141.0 22.0 %collective-permute-start.39 = (bf16[3072,384]{1,0:T(8,128)(2,1)}, bf16[3072,384]{1,0:T(8,128)(2,1)S(1)}, u32[]{:S(2)}, u32[]{:S(2)}) collective-permute-start(bf16[3072,384]{1,0:T(8,128)(2,1)} %get-tuple-element.502.dn_own), channel_id=1, source_target_pairs={{0,1},{1,0},{2,3},{3,2},{4,5},{5,4},{6,7},{7,6},{8,9},{9,8},{10,11... | collective-permute-start | bytes 7077896 | tf_op jit(solution)/shard_map/ppermute | solution.py:906
  141.0 22.0 %collective-permute-start.36 = (bf16[384,1024]{1,0:T(8,128)(2,1)}, bf16[384,1024]{1,0:T(8,128)(2,1)S(1)}, u32[]{:S(2)}, u32[]{:S(2)}) collective-permute-start(bf16[384,1024]{1,0:T(8,128)(2,1)} %collective-permute-done.28.refs_3_.refs_7_), channel_id=1, source_target_pairs={{0,8},{1,9},{2,10},{3,11},{4,12},{5,13},{6,14},{7,15},{8,16},{9,17... | collective-permute-start | bytes 2359304 | tf_op jit(solution)/shard_map/ppermute | solution.py:910
  141.1 21.9 %collective-permute-start.37 = (bf16[384,1024]{1,0:T(8,128)(2,1)S(1)}, bf16[384,1024]{1,0:T(8,128)(2,1)}, u32[]{:S(2)}, u32[]{:S(2)}) collective-permute-start(bf16[384,1024]{1,0:T(8,128)(2,1)S(1)} %collective-permute-done.30.refs_0_.refs_4_), channel_id=1, source_target_pairs={{0,4},{1,5},{2,6},{3,7},{4,0},{5,1},{6,2},{7,3},{8,12},{9,13},{10,... | collective-permute-start | bytes 2359304 | tf_op jit(solution)/shard_map/ppermute | solution.py:906
  142.8 20.2 %collective-permute-start.38 = (bf16[384,1024]{1,0:T(8,128)(2,1)S(1)}, bf16[384,1024]{1,0:T(8,128)(2,1)}, u32[]{:S(2)}, u32[]{:S(2)}) collective-permute-start(bf16[384,1024]{1,0:T(8,128)(2,1)S(1)} %collective-permute-done.34.refs_4_.refs_0_), channel_id=1, source_target_pairs={{0,2},{1,3},{2,0},{3,1},{4,6},{5,7},{6,4},{7,5},{8,10},{9,11},{10,... | collective-permute-start | bytes 2359304 | tf_op jit(solution)/shard_map/ppermute | solution.py:906
  163.9 23.0 %collective-permute-start.43 = (bf16[768,1536]{1,0:T(8,128)(2,1)}, bf16[768,1536]{1,0:T(8,128)(2,1)}, u32[]{:S(2)}, u32[]{:S(2)}) collective-permute-start(bf16[768,1536]{1,0:T(8,128)(2,1)} %get-tuple-element.500.up_own), channel_id=1, source_target_pairs={{0,1},{1,0},{2,3},{3,2},{4,5},{5,4},{6,7},{7,6},{8,9},{9,8},{10,11... | collective-permute-start | bytes 7077896 | tf_op jit(solution)/shard_map/ppermute | solution.py:906
  165.7 21.2 %collective-permute-start.41 = (bf16[384,1024]{1,0:T(8,128)(2,1)}, bf16[384,1024]{1,0:T(8,128)(2,1)}, u32[]{:S(2)}, u32[]{:S(2)}) collective-permute-start(bf16[384,1024]{1,0:T(8,128)(2,1)} %collective-permute-done.37.refs_2_.refs_6_), channel_id=1, source_target_pairs={{0,8},{1,9},{2,10},{3,11},{4,12},{5,13},{6,14},{7,15},{8,16},{9,17... | collective-permute-start | bytes 2359304 | tf_op jit(solution)/shard_map/ppermute | solution.py:910
  166.0 20.9 %collective-permute-start.42 = (bf16[384,1024]{1,0:T(8,128)(2,1)}, bf16[384,1024]{1,0:T(8,128)(2,1)}, u32[]{:S(2)}, u32[]{:S(2)}) collective-permute-start(bf16[384,1024]{1,0:T(8,128)(2,1)} %collective-permute-done.38.refs_5_.refs_1_), channel_id=1, source_target_pairs={{0,4},{1,5},{2,6},{3,7},{4,0},{5,1},{6,2},{7,3},{8,12},{9,13},{10,... | collective-permute-start | bytes 2359304 | tf_op jit(solution)/shard_map/ppermute | solution.py:906
  292.7 22.4 %collective-permute-start.46 = (bf16[384,1024]{1,0:T(8,128)(2,1)}, bf16[384,1024]{1,0:T(8,128)(2,1)S(1)}, u32[]{:S(2)}, u32[]{:S(2)}) collective-permute-start(bf16[384,1024]{1,0:T(8,128)(2,1)} %get-tuple-element.525), channel_id=1, source_target_pairs={{0,24},{1,25},{2,26},{3,27},{4,28},{5,29},{6,30},{7,31},{8,0},{9,1... | collective-permute-start | bytes 2359304 | tf_op jit(solution)/shard_map/ppermute | solution.py:910
  294.4 20.8 %collective-permute-start.47 = (bf16[384,1024]{1,0:T(8,128)(2,1)}, bf16[384,1024]{1,0:T(8,128)(2,1)S(1)}, u32[]{:S(2)}, u32[]{:S(2)}) collective-permute-start(bf16[384,1024]{1,0:T(8,128)(2,1)} %get-tuple-element.526), channel_id=1, source_target_pairs={{0,2},{1,3},{2,0},{3,1},{4,6},{5,7},{6,4},{7,5},{8,10},{9,11},{10,... | collective-permute-start | bytes 2359304 | tf_op jit(solution)/shard_map/ppermute | solution.py:906
  315.2 24.9 %collective-permute-start.52 = (bf16[12,1024,128]{2,1,0:T(8,128)(2,1)}, bf16[12,1024,128]{2,1,0:T(8,128)(2,1)}, u32[]{:S(2)}, u32[]{:S(2)}) collective-permute-start(bf16[12,1024,128]{2,1,0:T(8,128)(2,1)} %get-tuple-element.569), channel_id=1, source_target_pairs={{0,1},{1,0},{2,3},{3,2},{4,5},{5,4},{6,7},{7,6},{8,9},{9,8},{10,11... | collective-permute-start | bytes 9437192 | tf_op jit(solution)/shard_map/ppermute | solution.py:906
  319.7 20.3 %collective-permute-start.50 = (bf16[384,1024]{1,0:T(8,128)(2,1)}, bf16[384,1024]{1,0:T(8,128)(2,1)S(1)}, u32[]{:S(2)}, u32[]{:S(2)}) collective-permute-start(bf16[384,1024]{1,0:T(8,128)(2,1)} %get-tuple-element.564), channel_id=1, source_target_pairs={{0,2},{1,3},{2,0},{3,1},{4,6},{5,7},{6,4},{7,5},{8,10},{9,11},{10,... | collective-permute-start | bytes 2359304 | tf_op jit(solution)/shard_map/ppermute | solution.py:906
  320.0 20.1 %collective-permute-start.51 = (bf16[384,1024]{1,0:T(8,128)(2,1)}, bf16[384,1024]{1,0:T(8,128)(2,1)S(1)}, u32[]{:S(2)}, u32[]{:S(2)}) collective-permute-start(bf16[384,1024]{1,0:T(8,128)(2,1)} %get-tuple-element.565), channel_id=1, source_target_pairs={{0,4},{1,5},{2,6},{3,7},{4,0},{5,1},{6,2},{7,3},{8,12},{9,13},{10,... | collective-permute-start | bytes 2359304 | tf_op jit(solution)/shard_map/ppermute | solution.py:906
  341.5 27.1 %collective-permute-start.56 = (bf16[768,1536]{1,0:T(8,128)(2,1)}, bf16[768,1536]{1,0:T(8,128)(2,1)S(1)}, u32[]{:S(2)}, u32[]{:S(2)}) collective-permute-start(bf16[768,1536]{1,0:T(8,128)(2,1)} %get-tuple-element.589), channel_id=1, source_target_pairs={{0,1},{1,0},{2,3},{3,2},{4,5},{5,4},{6,7},{7,6},{8,9},{9,8},{10,11... | collective-permute-start | bytes 7077896 | tf_op jit(solution)/shard_map/ppermute | solution.py:906
  345.1 21.2 %collective-permute-start.53 = (bf16[384,1024]{1,0:T(8,128)(2,1)}, bf16[384,1024]{1,0:T(8,128)(2,1)}, u32[]{:S(2)}, u32[]{:S(2)}) collective-permute-start(bf16[384,1024]{1,0:T(8,128)(2,1)} %get-tuple-element.583), channel_id=1, source_target_pairs={{0,24},{1,25},{2,26},{3,27},{4,28},{5,29},{6,30},{7,31},{8,0},{9,1... | collective-permute-start | bytes 2359304 | tf_op jit(solution)/shard_map/ppermute | solution.py:910
  348.5 20.0 %collective-permute-start.54 = (bf16[384,1024]{1,0:T(8,128)(2,1)}, bf16[384,1024]{1,0:T(8,128)(2,1)}, u32[]{:S(2)}, u32[]{:S(2)}) collective-permute-start(bf16[384,1024]{1,0:T(8,128)(2,1)} %get-tuple-element.584), channel_id=1, source_target_pairs={{0,2},{1,3},{2,0},{3,1},{4,6},{5,7},{6,4},{7,5},{8,10},{9,11},{10,... | collective-permute-start | bytes 2359304 | tf_op jit(solution)/shard_map/ppermute | solution.py:906
  368.5 25.3 %collective-permute-start.60 = (bf16[3072,384]{1,0:T(8,128)(2,1)}, bf16[3072,384]{1,0:T(8,128)(2,1)}, u32[]{:S(2)}, u32[]{:S(2)}) collective-permute-start(bf16[3072,384]{1,0:T(8,128)(2,1)} %get-tuple-element.604), channel_id=1, source_target_pairs={{0,1},{1,0},{2,3},{3,2},{4,5},{5,4},{6,7},{7,6},{8,9},{9,8},{10,11... | collective-permute-start | bytes 7077896 | tf_op jit(solution)/shard_map/ppermute | solution.py:906
  393.8 25.1 %collective-permute-start.64 = (bf16[2,512,768]{2,1,0:T(8,128)(2,1)}, bf16[2,512,768]{2,1,0:T(8,128)(2,1)}, u32[]{:S(2)}, u32[]{:S(2)}) collective-permute-start(bf16[2,512,768]{2,1,0:T(8,128)(2,1)} %get-tuple-element.636), channel_id=1, source_target_pairs={{0,1},{1,0},{2,3},{3,2},{4,5},{5,4},{6,7},{7,6},{8,9},{9,8},{10,11... | collective-permute-start | bytes 4718600 | tf_op jit(solution)/shard_map/ppermute | solution.py:906
  396.9 20.2 %collective-permute-start.61 = (bf16[384,1024]{1,0:T(8,128)(2,1)}, bf16[384,1024]{1,0:T(8,128)(2,1)S(1)}, u32[]{:S(2)}, u32[]{:S(2)}) collective-permute-start(bf16[384,1024]{1,0:T(8,128)(2,1)} %get-tuple-element.611), channel_id=1, source_target_pairs={{0,24},{1,25},{2,26},{3,27},{4,28},{5,29},{6,30},{7,31},{8,0},{9,1... | collective-permute-start | bytes 2359304 | tf_op jit(solution)/shard_map/ppermute | solution.py:910
  399.0 19.9 %collective-permute-start.62 = (bf16[384,1024]{1,0:T(8,128)(2,1)}, bf16[384,1024]{1,0:T(8,128)(2,1)S(1)}, u32[]{:S(2)}, u32[]{:S(2)}) collective-permute-start(bf16[384,1024]{1,0:T(8,128)(2,1)} %get-tuple-element.612), channel_id=1, source_target_pairs={{0,2},{1,3},{2,0},{3,1},{4,6},{5,7},{6,4},{7,5},{8,10},{9,11},{10,... | collective-permute-start | bytes 2359304 | tf_op jit(solution)/shard_map/ppermute | solution.py:906
  (132 other events, 1636.9 us)

commit v8 on v7

--- a/solution.py
+++ b/solution.py
@@ -27,7 +27,6 @@
 PHEADS = HEADS // PLANES
 ROWS = 2 * LMAX
 FSTEP = 768
-FSIDE = FF // 2 // FSTEP
 TILE = 512
 SIDE = WIDTH // 2
 SPAN = 2 * HALF
@@ -53,16 +52,8 @@
     return pltpu.CompilerParams(vmem_limit_bytes=limit)
 
 
-def whole_weight(sc, step, own, far, weight):
-    @pl.when(step == 0)
-    def _():
-        weight[:, pl.ds(pl.multiple_of(sc[CORE] * SIDE, 128), SIDE)] = own[...]
-        weight[:, pl.ds(pl.multiple_of((1 - sc[CORE]) * SIDE, 128), SIDE)] = far[...]
-
-
-def values_kernel(sc, tok, gain, w_own, w_far, out, weight):
+def values_kernel(sc, tok, gain, weight, out):
     step = pl.program_id(0)
-    whole_weight(sc, step, w_own, w_far, weight)
     rows = tok.shape[1]
     position = step * rows + lax.broadcasted_iota(jnp.int32, (rows, 1), 0)
     for item in range(2):
@@ -75,7 +66,7 @@
             out[head, :, item * HEAD : (item + 1) * HEAD] = found[:, head * HEAD : (head + 1) * HEAD]
 
 
-def run_values(sc, tokens, gain, w_own, w_far):
+def run_values(sc, tokens, gain, weight):
     rows = 256
     return pl.pallas_call(
         values_kernel,
@@ -85,11 +76,9 @@
             in_specs=[
                 spec((2, rows, WIDTH), lambda j, s: (0, j, 0)),
                 held((1, WIDTH)),
-                held((WIDTH, SIDE)),
-                held((WIDTH, SIDE)),
+                held((WIDTH, WIDTH)),
             ],
             out_specs=spec((HEADS, rows, 2 * HEAD), lambda j, s: (0, j, 0)),
-            scratch_shapes=[pltpu.VMEM((WIDTH, WIDTH), BF16)],
         ),
         out_shape=jax.ShapeDtypeStruct((HEADS, LMAX, 2 * HEAD), BF16),
         compiler_params=params(VMEM),
@@ -97,7 +86,7 @@
             flops=2 * 2 * LMAX * WIDTH * WIDTH, bytes_accessed=8 * LMAX * WIDTH, transcendentals=0
         ),
         name="values",
-    )(sc, tokens, gain, w_own, w_far)
+    )(sc, tokens, gain, weight)
 
 
 def lane_lengths(sc, shape):
@@ -226,9 +215,8 @@
     return jnp.concatenate([own[:, :, 0], far[...]], axis=0).reshape(4 * SPAN, WIDTH)
 
 
-def pre_kernel(sc, tok, tok_far, cot, cot_far, heads, wo_own, wo_far, gain, mixed, resid, normed, grad, weight):
+def pre_kernel(sc, tok, tok_far, cot, cot_far, heads, weight, gain, mixed, resid, normed, grad):
     step = pl.program_id(0)
-    whole_weight(sc, step, wo_own, wo_far, weight)
     for item in range(4):
         lanes = slice(item * HEAD, (item + 1) * HEAD)
         for pair in range(HEADS // 2):
@@ -258,7 +246,7 @@
     return spec((HEADS, SPAN, 4 * HEAD), lambda r, s: (0, r, 0))
 
 
-def run_pre(sc, tokens, tokens_far, cotangent, cotangent_far, heads, wo, gain):
+def run_pre(sc, tokens, tokens_far, cotangent, cotangent_far, heads, weight, gain):
     return pl.pallas_call(
         pre_kernel,
         grid_spec=pltpu.PrefetchScalarGridSpec(
@@ -266,9 +254,8 @@
             grid=(HROWS // SPAN,),
             in_specs=half_specs()
             + half_specs()
-            + [heads_spec(), held((WIDTH, SIDE)), held((WIDTH, SIDE)), held((1, WIDTH))],
+            + [heads_spec(), held((WIDTH, WIDTH)), held((1, WIDTH))],
             out_specs=[slab_spec()] * 4,
-            scratch_shapes=[pltpu.VMEM((WIDTH, WIDTH), BF16)],
         ),
         out_shape=[
             jax.ShapeDtypeStruct((4, HROWS, WIDTH), BF16),
@@ -281,53 +268,18 @@
             flops=2 * ROWS * WIDTH * WIDTH, bytes_accessed=16 * ROWS * WIDTH, transcendentals=0
         ),
         name="pre",
-    )(sc, tokens, tokens_far, cotangent, cotangent_far, heads, *wo, gain)
-
-
-def own_lanes(sc):
-    return pl.ds(pl.multiple_of(sc[CORE] * SIDE, 128), SIDE)
-
-
-def far_lanes(sc):
-    return pl.ds(pl.multiple_of((1 - sc[CORE]) * SIDE, 128), SIDE)
-
-
-def unit_rows(f, sc):
-    return (lax.rem(FSIDE * sc[CORE] + f, 2 * FSIDE), 0)
-
-
-def unit_columns(f, sc):
-    return (0, lax.rem(FSIDE * sc[CORE] + f, 2 * FSIDE))
-
-
-def early(f, sc):
-    return (0, lax.min(f, FSIDE - 1))
-
-
-def late(f, sc):
-    return (0, lax.max(f - FSIDE, 0))
-
-
-def units_kernel(sc, normed, cot, up_own, up_far, dn_own, dn_far, active, up_grad, back, w_up, w_down, total):
+    )(sc, tokens, tokens_far, cotangent, cotangent_far, heads, weight, gain)
+
+
+def units_kernel(sc, normed, cot, w_up, w_down, active, up_grad, back, total):
     step = pl.program_id(0)
-    w_down[:, own_lanes(sc)] = dn_own[...]
-    w_down[:, far_lanes(sc)] = dn_far[...]
-
-    @pl.when(step < FSIDE)
-    def _():
-        w_up[...] = up_own[...]
-
-    @pl.when(step >= FSIDE)
-    def _():
-        w_up[...] = up_far[...]
-
     for piece in range(ROWS // TILE):
         whole = slice(piece * TILE, (piece + 1) * TILE)
         for row in range(piece * TILE, (piece + 1) * TILE, 256):
             rows = slice(row, row + 256)
             for column in range(0, FSTEP, 256):
                 columns = slice(column, column + 256)
-                up = dot(normed[rows], w_up[:, columns], 1, 0)
+                up = dot(normed[rows], w_up[0, :, columns], 1, 0)
                 square = up * up
                 bend = jnp.tanh(up * (0.7978845608028654 + (0.044715 * 0.7978845608028654) * square))
                 share = 0.5 + 0.5 * bend
@@ -337,41 +289,36 @@
                     2 * 0.7978845608028654 + (6 * 0.044715 * 0.7978845608028654) * square
                 )
                 up_grad[rows, columns] = (dot(cot[rows], w_down[columns], 1, 1) * slope).astype(BF16)
-        two_grad = dot(up_grad[whole], w_up[...], 1, 1)
+        two_grad = dot(up_grad[whole], w_up[0], 1, 1)
 
         @pl.when(step == 0)
         def _():
             total[whole] = two_grad
 
-        @pl.when((step > 0) & (step < 2 * FSIDE - 1))
+        @pl.when((step > 0) & (step < FF // FSTEP - 1))
         def _():
             total[whole] += two_grad
 
-        @pl.when(step == 2 * FSIDE - 1)
+        @pl.when(step == FF // FSTEP - 1)
         def _():
             back[whole] = (total[whole] + two_grad).astype(BF16)
 
 
-def run_units(sc, normed, cotangent, up, down):
+def run_units(sc, normed, cotangent, w_up, w_down):
+    columns = spec((ROWS, FSTEP), lambda f, s: (0, f))
     return pl.pallas_call(
         units_kernel,
         grid_spec=pltpu.PrefetchScalarGridSpec(
             num_scalar_prefetch=1,
-            grid=(2 * FSIDE,),
+            grid=(FF // FSTEP,),
             in_specs=[
                 held((ROWS, WIDTH)),
                 held((ROWS, WIDTH)),
-                spec((WIDTH, FSTEP), early),
-                spec((WIDTH, FSTEP), late),
-                spec((FSTEP, SIDE), unit_rows),
-                spec((FSTEP, SIDE), unit_rows),
+                spec((1, WIDTH, FSTEP), lambda f, s: (f, 0, 0)),
+                spec((FSTEP, WIDTH), lambda f, s: (f, 0)),
             ],
-            out_specs=[spec((ROWS, FSTEP), unit_columns), spec((ROWS, FSTEP), unit_columns), held((ROWS, WIDTH))],
-            scratch_shapes=[
-                pltpu.VMEM((WIDTH, FSTEP), BF16),
-                pltpu.VMEM((FSTEP, WIDTH), BF16),
-                pltpu.VMEM((ROWS, WIDTH), F32),
-            ],
+            out_specs=[columns, columns, held((ROWS, WIDTH))],
+            scratch_shapes=[pltpu.VMEM((ROWS, WIDTH), F32)],
         ),
         out_shape=[
             jax.ShapeDtypeStruct((ROWS, FF), BF16),
@@ -383,72 +330,49 @@
             flops=6 * ROWS * WIDTH * FF, bytes_accessed=8 * ROWS * WIDTH + 4 * ROWS * FF, transcendentals=ROWS * FF
         ),
         name="units",
-    )(sc, normed.reshape(ROWS, WIDTH), cotangent.reshape(ROWS, WIDTH), *up, *down)
-
-
-def down_grad_kernel(sc, active, cot, own, far, total):
+    )(sc, normed.reshape(ROWS, WIDTH), cotangent.reshape(ROWS, WIDTH), w_up, w_down)
+
+
+def down_grad_kernel(active, cot, total):
     total[...] = dot(active[...], cot[...], 0, 0).astype(BF16)
-    own[...] = total[:, own_lanes(sc)]
-    far[...] = total[:, far_lanes(sc)]
-
-
-def run_down_grad(sc, active, cotangent):
+
+
+def run_down_grad(active, cotangent):
     return pl.pallas_call(
         down_grad_kernel,
-        grid_spec=pltpu.PrefetchScalarGridSpec(
-            num_scalar_prefetch=1,
-            grid=(FF // 512,),
-            in_specs=[spec((ROWS, 512), lambda f, s: (0, f)), held((ROWS, WIDTH))],
-            out_specs=[spec((512, SIDE), lambda f, s: (f, 0))] * 2,
-            scratch_shapes=[pltpu.VMEM((512, WIDTH), BF16)],
-        ),
-        out_shape=[jax.ShapeDtypeStruct((FF, SIDE), BF16)] * 2,
+        grid=(FF // 512,),
+        in_specs=[spec((ROWS, 512), lambda f: (0, f)), held((ROWS, WIDTH))],
+        out_specs=spec((512, WIDTH), lambda f: (f, 0)),
+        out_shape=jax.ShapeDtypeStruct((FF, WIDTH), BF16),
         compiler_params=params(VMEM),
         cost_estimate=pl.CostEstimate(
             flops=2 * ROWS * WIDTH * FF, bytes_accessed=2 * ROWS * (WIDTH + FF), transcendentals=0
         ),
         name="down_grad",
-    )(sc, active, cotangent.reshape(ROWS, WIDTH))
-
-
-def up_grad_kernel(sc, normed, up_grad, own, far):
-    total = dot(normed[...], up_grad[...], 0, 0).astype(BF16)
-
-    @pl.when(pl.program_id(0) < FSIDE)
-    def _():
-        own[...] = total
-
-    @pl.when(pl.program_id(0) >= FSIDE)
-    def _():
-        far[...] = total
-
-
-def run_up_grad(sc, normed, up_grad):
+    )(active, cotangent.reshape(ROWS, WIDTH))
+
+
+def up_grad_kernel(normed, up_grad, total):
+    total[0] = dot(normed[...], up_grad[...], 0, 0).astype(BF16)
+
+
+def run_up_grad(normed, up_grad):
     return pl.pallas_call(
         up_grad_kernel,
-        grid_spec=pltpu.PrefetchScalarGridSpec(
-            num_scalar_prefetch=1,
-            grid=(2 * FSIDE,),
-            in_specs=[held((ROWS, WIDTH)), spec((ROWS, FSTEP), unit_columns)],
-            out_specs=[spec((WIDTH, FSTEP), early), spec((WIDTH, FSTEP), late)],
-        ),
-        out_shape=[jax.ShapeDtypeStruct((WIDTH, FF // 2), BF16)] * 2,
+        grid=(FF // FSTEP,),
+        in_specs=[held((ROWS, WIDTH)), spec((ROWS, FSTEP), lambda f: (0, f))],
+        out_specs=spec((1, WIDTH, FSTEP), lambda f: (f, 0, 0)),
+        out_shape=jax.ShapeDtypeStruct((FF // FSTEP, WIDTH, FSTEP), BF16),
         compiler_params=params(VMEM),
         cost_estimate=pl.CostEstimate(
             flops=2 * ROWS * WIDTH * FF, bytes_accessed=2 * ROWS * (WIDTH + FF), transcendentals=0
         ),
         name="up_grad",
-    )(sc, normed.reshape(ROWS, WIDTH), up_grad)
-
-
-def out_kernel(sc, active, resid, dn_own, dn_far, own, far, w_down):
+    )(normed.reshape(ROWS, WIDTH), up_grad)
+
+
+def out_kernel(sc, active, resid, w_down, own, far):
     step = pl.program_id(0)
-
-    @pl.when(step == 0)
-    def _():
-        w_down[:, own_lanes(sc)] = dn_own[...]
-        w_down[:, far_lanes(sc)] = dn_far[...]
-
     branch = dot(active[...].reshape(4 * SPAN, FF), w_down[...], 1, 0)
     output = jnp.where(row_valid(sc, step), resid[...].reshape(4 * SPAN, WIDTH).astype(F32) + branch, 0.0)
     output = output.astype(BF16).reshape(4, SPAN, WIDTH)
@@ -456,7 +380,7 @@
     far[...] = output[2:]
 
 
-def run_out(sc, active, resid, down):
+def run_out(sc, active, resid, w_down):
     return pl.pallas_call(
         out_kernel,
         grid_spec=pltpu.PrefetchScalarGridSpec(
@@ -465,11 +389,9 @@
             in_specs=[
                 spec((4, SPAN, FF), lambda r, s: (0, r, 0)),
                 slab_spec(),
-                held((FF, SIDE)),
-                held((FF, SIDE)),
+                held((FF, WIDTH)),
             ],
             out_specs=[slab_spec(2)] * 2,
-            scratch_shapes=[pltpu.VMEM((FF, WIDTH), BF16)],
         ),
         out_shape=[
             jax.ShapeDtypeStruct((2, HROWS, WIDTH), BF16),
@@ -480,13 +402,12 @@
             flops=2 * ROWS * WIDTH * FF, bytes_accessed=ROWS * (2 * FF + 7 * WIDTH), transcendentals=0
         ),
         name="out",
-    )(sc, active.reshape(4, HROWS, FF), resid, *down)
-
-
-def post_kernel(sc, resid, back, cot, mixed, wo_own, wo_far, gain, *refs):
-    (res_own, res_far, heads, d_out_own, d_out_far, d_gain, weight, total, spread) = refs
+    )(sc, active.reshape(4, HROWS, FF), resid, w_down)
+
+
+def post_kernel(sc, resid, back, cot, mixed, weight, gain, *refs):
+    (res_own, res_far, heads, d_out, d_gain, total, spread) = refs
     step = pl.program_id(0)
-    whole_weight(sc, step, wo_own, wo_far, weight)
     shape, slab = (4 * SPAN, WIDTH), (4, SPAN, WIDTH)
     valid = row_valid(sc, step)
     res = resid[...].reshape(shape).astype(F32)
@@ -523,23 +444,22 @@
 
     @pl.when(step == pl.num_programs(0) - 1)
     def _():
-        weight[...] = total[...].astype(BF16)
-        d_out_own[...] = weight[:, own_lanes(sc)]
-        d_out_far[...] = weight[:, far_lanes(sc)]
-
-
-def run_post(sc, resid, back, cotangent, mixed, wo, gain):
+        low = total[...].astype(BF16)
+        d_out[0] = low[:, :SIDE]
+        d_out[1] = low[:, SIDE:]
+
+
+def run_post(sc, resid, back, cotangent, mixed, weight, gain):
     whole = (4, HROWS, WIDTH)
     return pl.pallas_call(
         post_kernel,
         grid_spec=pltpu.PrefetchScalarGridSpec(
             num_scalar_prefetch=1,
             grid=(HROWS // SPAN,),
-            in_specs=[slab_spec()] * 4 + [held((WIDTH, SIDE)), held((WIDTH, SIDE)), held((1, WIDTH))],
+            in_specs=[slab_spec()] * 4 + [held((WIDTH, WIDTH)), held((1, WIDTH))],
             out_specs=[slab_spec(2)] * 2
-            + [heads_spec(), held((WIDTH, SIDE)), held((WIDTH, SIDE)), held((1, WIDTH))],
+            + [heads_spec(), held((2, WIDTH, SIDE)), held((1, WIDTH))],
             scratch_shapes=[
-                pltpu.VMEM((WIDTH, WIDTH), BF16),
                 pltpu.VMEM((WIDTH, WIDTH), F32),
                 pltpu.VMEM((4, SPAN, WIDTH), BF16),
             ],
@@ -548,8 +468,7 @@
             jax.ShapeDtypeStruct((2, HROWS, WIDTH), BF16),
             jax.ShapeDtypeStruct((2, HROWS, WIDTH), BF16),
             jax.ShapeDtypeStruct((HEADS, HROWS, 4 * HEAD), BF16),
-            jax.ShapeDtypeStruct((WIDTH, SIDE), BF16),
-            jax.ShapeDtypeStruct((WIDTH, SIDE), BF16),
+            jax.ShapeDtypeStruct((2, WIDTH, SIDE), BF16),
             jax.ShapeDtypeStruct((1, WIDTH), F32),
         ],
         compiler_params=params(VMEM),
@@ -557,7 +476,7 @@
             flops=4 * ROWS * WIDTH * WIDTH, bytes_accessed=28 * ROWS * WIDTH, transcendentals=0
         ),
         name="post",
-    )(sc, resid, back.reshape(whole), cotangent, mixed, *wo, gain)
+    )(sc, resid, back.reshape(whole), cotangent, mixed, weight, gain)
 
 
 def unmix_kernel(carried, sc, *refs):
@@ -654,10 +573,9 @@
     )(sc, *shards, v_own, v_far, grad_heads, mean, *carry)
 
 
-def close_kernel(sc, tok, res_own, res_got, out_own, out_got, own, far, gain, w_own, w_far, *refs):
-    (output, tok_grad, d_value, d_gain, total, weight) = refs
+def close_kernel(sc, tok, res_own, res_got, out_own, out_got, own, far, gain, weight, *refs):
+    (output, tok_grad, d_value, d_gain, total) = refs
     step = pl.program_id(0)
-    whole_weight(sc, step, w_own, w_far, weight)
     core = sc[CORE]
     output[:, :, core] = out_own[...].astype(F32)
     output[:, :, 1 - core] = out_got[...].astype(F32)
@@ -703,7 +621,7 @@
         d_value[1] = low[:, SIDE:]
 
 
-def run_close(sc, tokens, res_own, res_got, out_own, out_got, own, far, gain, w_own, w_far):
+def run_close(sc, tokens, res_own, res_got, out_own, out_got, own, far, gain, weight):
     runs = 2
     slab = (2, RUNS, 2, HALF, WIDTH)
     half = (2, RUNS, HALF, WIDTH)
@@ -717,9 +635,9 @@
             grid=(RUNS // runs,),
             in_specs=[whole_spec]
             + [half_spec] * 4
-            + [back_spec, back_spec, held((1, WIDTH)), held((WIDTH, SIDE)), held((WIDTH, SIDE))],
+            + [back_spec, back_spec, held((1, WIDTH)), held((WIDTH, WIDTH))],
             out_specs=[whole_spec, whole_spec, held((2, WIDTH, SIDE)), held((1, WIDTH))],
-            scratch_shapes=[pltpu.VMEM((WIDTH, WIDTH), F32), pltpu.VMEM((WIDTH, WIDTH), BF16)],
+            scratch_shapes=[pltpu.VMEM((WIDTH, WIDTH), F32)],
         ),
         out_shape=[
             jax.ShapeDtypeStruct(slab, F32),
@@ -739,137 +657,37 @@
         own,
         far,
         gain,
-        w_own,
-        w_far,
-    )
-
-
-PACK_DOWN, PACK_UP, PACK_OUT, PACK_VALUE, PACK_GAIN, PACK = 0, 192, 384, 432, 480, 496
-
-
-def pack_kernel(sc, down, up, out, value, gain, down_far, up_far, out_far, value_far, gain_far, packed):
-    first = sc[CORE] == 0
-
-    def both(own, far, lanes):
-        own, far = own[:, lanes], far[:, lanes]
-        return jnp.concatenate([jnp.where(first, own, far), jnp.where(first, far, own)], axis=0)
-
-    def side(own, far):
-        return both(own, far, own_lanes(sc))
-
-    packed[PACK_DOWN:PACK_UP] = side(down, down_far)
-    for j in range(4):
-        lanes = pl.ds(pl.multiple_of((4 * sc[CORE] + j) * SIDE, 128), SIDE)
-        packed[PACK_UP + 48 * j : PACK_UP + 48 * (j + 1)] = both(up, up_far, lanes)
-    packed[PACK_OUT:PACK_VALUE] = side(out, out_far)
-    packed[PACK_VALUE:PACK_GAIN] = side(value, value_far)
-    packed[PACK_GAIN:] = both(gain, gain_far, slice(0, SIDE))
-
-
-def run_pack(sc, own, far):
-    return pl.pallas_call(
-        pack_kernel,
-        grid_spec=pltpu.PrefetchScalarGridSpec(
-            num_scalar_prefetch=1,
-            grid=(1,),
-            in_specs=[held(x.shape) for x in (*own, *far)],
-            out_specs=held((PACK, SIDE)),
-        ),
-        out_shape=jax.ShapeDtypeStruct((PACK, SIDE), BF16),
-        compiler_params=params(VMEM),
-        cost_estimate=pl.CostEstimate(flops=0, bytes_accessed=6 * PACK * SIDE, transcendentals=0),
-        name="pack",
-    )(sc, *own, *far)
-
-
-def chip_of(sc, k, rel):
-    return plane_of(k, sc) * 4 + (sc[PLACE] ^ rel)
-
-
-def place_kernel(moves, sc, *refs):
-    pieces, targets, sems = refs[:16], refs[16:-1], refs[-1]
-    copies = []
-    for index, piece in enumerate(pieces):
-        chip = chip_of(sc, index // 4, index % 4)
-        for which, (start, count, lane, target, step, offset, column) in enumerate(moves):
-            rows = pl.ds(pl.multiple_of(chip * step + offset, 16), count)
-            copies.append(
-                pltpu.make_async_copy(
-                    piece.at[pl.ds(start, count), pl.ds(lane, SIDE)],
-                    targets[target].at[rows, pl.ds(column, SIDE)],
-                    sems.at[index, which],
-                )
-            )
+        weight,
+    )
+
+
+def place_kernel(sc, *refs):
+    pieces, target, sems = refs[:16], refs[16], refs[17]
+    copies = [
+        pltpu.make_async_copy(piece, target.at[plane_of(i // 4, sc) * 4 + (sc[PLACE] ^ (i % 4))], sems.at[i])
+        for i, piece in enumerate(pieces)
+    ]
     for copy in copies:
         copy.start()
     for copy in copies:
         copy.wait()
 
 
-def run_place(sc, pieces, moves, shapes):
-    return pl.pallas_call(
-        partial(place_kernel, moves),
+def run_place(sc, pieces):
+    shape = (16, *pieces[0].shape)
+    return pl.pallas_call(
+        place_kernel,
         grid_spec=pltpu.PrefetchScalarGridSpec(
             num_scalar_prefetch=1,
             grid=(1,),
             in_specs=anywhere(16),
-            out_specs=[held(shape) for shape in shapes],
-            scratch_shapes=[pltpu.SemaphoreType.DMA((16, len(moves)))],
-        ),
-        out_shape=[jax.ShapeDtypeStruct(shape, BF16) for shape in shapes],
-        compiler_params=params(VMEM),
-        cost_estimate=pl.CostEstimate(
-            flops=0, bytes_accessed=4 * sum(a * b for a, b in shapes), transcendentals=0
-        ),
+            out_specs=held(shape),
+            scratch_shapes=[pltpu.SemaphoreType.DMA((16,))],
+        ),
+        out_shape=jax.ShapeDtypeStruct(shape, BF16),
+        compiler_params=params(VMEM),
         name="place",
     )(sc, *pieces)
-
-
-def place_weights(sc, pieces):
-    moves = (
-        (PACK_DOWN, 192, 0, 0, 192, 0, 0),
-        *((PACK_UP + 48 * j, 48, 0, 1, 48, 0, j * SIDE) for j in range(4)),
-        (PACK_OUT, 48, 0, 2, 48, 0, 0),
-        (PACK_VALUE, 48, 0, 3, 48, 0, 0),
-        (PACK_GAIN, 16, 0, 4, 16, 0, 0),
-    )
-    shapes = [(FF, SIDE), (WIDTH, FF // 2), (WIDTH, SIDE), (WIDTH, SIDE), (256, SIDE)]
-    return run_place(sc, pieces, moves, shapes)
-
-
-def collect_kernel(sc, *refs):
-    outs = refs[24:]
-    for k in range(PLANES):
-
-        @pl.when(pl.program_id(0) == k)
-        def _():
-            for rel in range(4):
-                down, down_got, up, up_got, out, out_got = refs[6 * rel : 6 * rel + 6]
-                packed = outs[4 * k + rel]
-                packed[PACK_DOWN:PACK_UP] = add_low(down[...], down_got[...])
-                for j in range(4):
-                    lanes = slice(j * SIDE, (j + 1) * SIDE)
-                    packed[PACK_UP + 48 * j : PACK_UP + 48 * (j + 1)] = add_low(up[:, lanes], up_got[:, lanes])
-                packed[PACK_OUT:PACK_VALUE] = add_low(out[...], out_got[...])
-
-
-def run_collect(sc, *sides):
-    def rows(x, rel):
-        return spec((x.shape[0] // 16, x.shape[1]), lambda k, s: (chip_of(s, k, rel), 0))
-
-    return pl.pallas_call(
-        collect_kernel,
-        grid_spec=pltpu.PrefetchScalarGridSpec(
-            num_scalar_prefetch=1,
-            grid=(PLANES,),
-            in_specs=[rows(x, rel) for rel in range(4) for x in sides],
-            out_specs=[held((PACK_VALUE, SIDE))] * 16,
-        ),
-        out_shape=[jax.ShapeDtypeStruct((PACK_VALUE, SIDE), BF16)] * 16,
-        compiler_params=params(VMEM),
-        cost_estimate=pl.CostEstimate(flops=0, bytes_accessed=3 * 16 * PACK_VALUE * SIDE * 2, transcendentals=0),
-        name="collect",
-    )(sc, *(x for _ in range(4) for x in sides))
 
 
 def add_kernel(groups, *refs):
@@ -976,51 +794,56 @@
     slab = (2, RUNS, 2, HALF, WIDTH)
     tokens, grad_out = tokens.reshape(slab), grad_out.reshape(slab)
 
-    gains = jnp.pad(jnp.concatenate([gain_mix, gain_ffn])[None], ((0, 7), (0, SIDE - 48)))
-    own = (w_down, w_up, w_out, w_value, gains)
-    far = tuple(other(value) for value in own)
-    near_sc = jnp.concatenate([jnp.stack([core, z, wide % 4]).astype(jnp.int32), lengths, lengths])
-    weights = {(0, 0, 0): run_pack(near_sc, own, far)}
-
+    packed = jnp.concatenate([w_out, w_down, *(w_up[:, j * WIDTH : (j + 1) * WIDTH] for j in range(4))])
+    packed = lax.all_gather(packed, BOTH, axis=0)
+
+    gains = jnp.pad(jnp.concatenate([gain_mix, gain_ffn])[None], ((0, 7), (0, WIDTH - 48)))
+    firsts = {(0, 0, 0): jnp.concatenate([w_value, gains])}
     rand = rand_mix.reshape(3, 2, HALF, LMAX)
     blocks = side(pick(rand, core, 1), other(pick(rand, 1 - core, 1)), 0)
-    weights, rands = together((gather_step(weights, 0), {(0, 0, 0): blocks.reshape(SUBS * HALF, LMAX)}))
-    weights, tokens_far = together((gather_step(weights, 1), other(pick(tokens, 1 - core, 2))))
-    weights, grad_far = together((gather_step(weights, 2), other(pick(grad_out, 1 - core, 2))))
-    weights, far_lengths = together((gather_step(weights, 3), other(lengths)))
-    sc = jnp.concatenate([near_sc[:5], far_lengths])
-    weights, rands = together((gather_step(weights, 4), rands))
+    firsts, rands, far_lengths = together(
+        (gather_step(firsts, 0), {(0, 0, 0): blocks.reshape(SUBS * HALF, LMAX)}, other(lengths))
+    )
+    sc = jnp.concatenate([jnp.stack([core, z, wide % 4]).astype(jnp.int32), lengths, far_lengths])
+    for step in range(1, 5):
+        firsts = together(gather_step(firsts, step))
+    firsts, rands = together((firsts, rands))
 
     rands = gather_step(rands, 0)
-    down, up, out, value, gain_rows = place_weights(sc, in_order(weights))
-    rands, value, value_far, gain_rows, out, down, up = together(
-        (rands, value, other(value), gain_rows, out, down, up)
-    )
-    gain_rows = gain_rows.reshape(16, 2, 8, SIDE)[:, :, 0]
-    gain_one = gain_rows[..., :24].reshape(1, WIDTH).astype(F32)
-    gain_two = gain_rows[..., 24:48].reshape(1, WIDTH).astype(F32)
+    first = run_place(sc, in_order(firsts))
+    rands, first, first_far = together((rands, first, other(first)))
+    both = ordered(core, first, first_far, 1)
+    value = both[:, :, :24].reshape(WIDTH, WIDTH)
+    gain_one = both[:, :, 24, :24].reshape(1, WIDTH).astype(F32)
+    gain_two = both[:, :, 24, 24:48].reshape(1, WIDTH).astype(F32)
     rands = gather_step(rands, 1)
-    v_own = run_values(sc, tokens.reshape(2, LMAX, WIDTH), gain_one, value, value_far)
-    rands, v_own, out, down, up = together((rands, v_own, (out, other(out)), down, up))
-    rands, v_own, v_far, down, up = together((gather_step(rands, 2), v_own, other(v_own), down, up))
-    rands, v_far, down, up = together((gather_step(rands, 3), v_far, (down, other(down)), up))
+    v_own = run_values(sc, tokens.reshape(2, LMAX, WIDTH), gain_one, value)
+    rands, v_own, tokens_far = together((rands, v_own, other(pick(tokens, 1 - core, 2))))
+    rands, v_own, v_far = together((gather_step(rands, 2), v_own, other(v_own)))
+    rands, v_far, grad_far = together((gather_step(rands, 3), v_far, other(pick(grad_out, 1 - core, 2))))
     near = [rands[k, y_at, x_at] for k in range(2) for y_at in range(2) for x_at in range(2)]
     rands = gather_step(rands, 4)
     mixing = run_mix(sc, (0, 1), near, v_own, v_far, ())
-    rands, up, mixing = together((rands, (up, other(up)), mixing))
+    rands, mixing = together((rands, mixing))
     shares = in_order(rands)
     heads, mean = run_mix(sc, (2, 3), shares[8:], v_own, v_far, mixing)
 
+    out = packed[:, :24].reshape(WIDTH, WIDTH)
+    down = packed[:, 24:120].reshape(FF, WIDTH)
+    up = packed[:, 120:].reshape(32, 4, 24, WIDTH).transpose(1, 0, 2, 3).reshape(4, WIDTH, WIDTH)
     mixed, resid, normed, masked = run_pre(sc, tokens, tokens_far, grad_out, grad_far, heads, out, gain_two)
     active, up_grad, back = run_units(sc, normed, masked, up, down)
-    res_own, res_far, grad_heads, d_out_own, d_out_far, d_gain_two = run_post(
-        sc, resid, back, masked, mixed, out, gain_two
-    )
-
+
+    d_down = run_down_grad(active, masked).reshape(32, 96, WIDTH)
+    d_up = run_up_grad(normed, up_grad).reshape(4, 32, 24, WIDTH).transpose(1, 0, 2, 3).reshape(32, 96, WIDTH)
+    packed, back = together((jnp.concatenate([d_down, d_up], axis=1), back))
+    packed = lax.psum_scatter(packed, BOTH, scatter_dimension=0)
+
+    res_own, res_far, grad_heads, d_out, d_gain_two = run_post(sc, resid, back, masked, mixed, out, gain_two)
     *far, back_own, back_far = run_unmix(
         sc, (3, 2), shares[12:] + shares[8:12], v_own, v_far, grad_heads, mean, ()
     )
-    far, back_own, back_far, res_got, d_out_got = together((far, back_own, back_far, other(res_far), other(d_out_far)))
+    far, back_own, back_far, res_got = together((far, back_own, back_far, other(res_far)))
     have, got = scatter_send(by_place(far, (3, 2)), 0)
     *near, back_own, back_far = run_unmix(
         sc, (1, 0), shares[4:8] + shares[:4], v_own, v_far, grad_heads, mean, (back_own, back_far)
@@ -1029,69 +852,42 @@
     have = {**scatter_add(have, got, 0), **by_place(near, (1, 0))}
 
     have, got = scatter_send(have, 1)
-    up_own, up_far = run_up_grad(sc, normed, up_grad)
-    have, got, up_own, up_far, back_got = together((have, got, up_own, up_far, other(back_far)))
+    out_own, out_far = run_out(sc, active, resid, down)
+    have, got, out_own, out_far, back_got = together((have, got, out_own, out_far, other(back_far)))
     have = scatter_add(have, got, 1)
 
     have, got = scatter_send(have, 2)
-    down_own, down_far = run_down_grad(sc, active, masked)
-    have, got, down_own, down_far, up_got = together((have, got, down_own, down_far, other(up_far)))
-    have = scatter_add(have, got, 2)
-
-    have, got = scatter_send(have, 3)
-    out_own, out_far = run_out(sc, active, resid, down)
-    have, got, out_own, out_far, down_got = together((have, got, out_own, out_far, other(down_far)))
-    have = scatter_add(have, got, 3)
-
-    have, got = scatter_send(have, 4)
-    packed = run_collect(sc, down_own, down_got, up_own, up_got, d_out_own, d_out_got)
-    have, got, packed, out_got = together((have, got, packed, other(out_far)))
-    rand_sum = scatter_add(have, got, 4)[0, 0, 0].reshape(2, 3, HALF, LMAX)
-
-    sums, got = scatter_send(by_place(packed), 0)
     output, tokens_grad, d_value, d_gain_one = run_close(
-        sc, tokens, res_own, res_got, out_own, out_got, back_own, back_got, gain_one, value, value_far
-    )
-    blocks, blocks_far = pick(rand_sum, core), other(pick(rand_sum, 1 - core))
-    sums, got, output, tokens_grad, d_value, d_gain_one, blocks, blocks_far = together(
-        (sums, got, output, tokens_grad, d_value, d_gain_one, blocks, blocks_far)
-    )
-    sums = scatter_add(sums, got, 0)
-
-    sums, got = scatter_send(sums, 1)
+        sc, tokens, res_own, res_got, out_own, other(out_far), back_own, back_got, gain_one, value
+    )
     gain_pair = jnp.concatenate([d_gain_one, d_gain_two]).reshape(2, 16, 1, 48).astype(BF16)
     gain_pair = jnp.pad(gain_pair, ((0, 0), (0, 0), (0, 15), (0, SIDE - 48)))
-    small = jnp.concatenate([d_value.reshape(2, 16, 48, SIDE), gain_pair], 2)
-    small = add_low(pick(small, core), other(pick(small, 1 - core))).reshape(4, 2, 2, 64, SIDE)
-    sums, got, small = together((sums, got, small))
-    sums = scatter_add(sums, got, 1)
-
-    sums, got = scatter_send(sums, 2)
+    small = jnp.concatenate([d_value.reshape(2, 16, 48, SIDE), d_out.reshape(2, 16, 48, SIDE), gain_pair], 2)
+    have, got, small, output, tokens_grad = together((have, got, small, output, tokens_grad))
+    have = scatter_add(have, got, 2)
+
+    have, got = scatter_send(have, 3)
+    small = add_low(pick(small, core), other(pick(small, 1 - core))).reshape(4, 2, 2, 112, SIDE)
     small = add_low(pick(small, x, 2), swap(pick(small, 1 - x, 2), TO_X))
-    sums, got, small = together((sums, got, small))
-    sums = scatter_add(sums, got, 2)
-
-    sums, got = scatter_send(sums, 3)
+    have, got, small = together((have, got, small))
+    have = scatter_add(have, got, 3)
+
+    have, got = scatter_send(have, 4)
     small = add_low(pick(small, y, 1), swap(pick(small, 1 - y, 1), TO_Y))
-    sums, got, small = together((sums, got, small))
-    sums = scatter_add(sums, got, 3)
-
-    sums, got = scatter_send(sums, 4)
     small_sum = pick(small, z).astype(F32)
     for k in range(1, PLANES):
         small_sum = small_sum + ring(pick(small, lax.rem(z + PLANES - k, PLANES)), -k).astype(F32)
-    sums, got, small_sum = together((sums, got, small_sum))
-    big_sum = scatter_add(sums, got, 4)[0, 0, 0]
-    big_far, small_far = other(big_sum), other(small_sum)
-
-    rows_of = lambda value, rows: pick(value.reshape(-1, 2, rows, SIDE), core, 1)
-    mine = lambda own, far, rows: side(rows_of(own, rows)[0], rows_of(far, rows)[0], 1)
-    down_shard = mine(big_sum[PACK_DOWN:PACK_UP], big_far[PACK_DOWN:PACK_UP], 96)
-    up_side = lambda value: rows_of(value[PACK_UP:PACK_OUT], 24).transpose(1, 0, 2).reshape(24, 4 * SIDE)
-    up_shard = side(up_side(big_sum), up_side(big_far), 1)
-    outproj_shard = mine(big_sum[PACK_OUT:PACK_VALUE], big_far[PACK_OUT:PACK_VALUE], 24)
-    value_shard = mine(small_sum[:48], small_far[:48], 24)
-    gains_pair = ordered(core, small_sum[48, :48], small_far[48, :48])
+    have, got, small_sum = together((have, got, small_sum))
+    rand_sum = scatter_add(have, got, 4)[0, 0, 0].reshape(2, 3, HALF, LMAX)
+    blocks, blocks_far = pick(rand_sum, core), other(pick(rand_sum, 1 - core))
+    small_far = other(small_sum)
+
+    rows_of = lambda value: pick(value.reshape(2, 24, SIDE), core)
+    value_shard = side(rows_of(small_sum[:48]), rows_of(small_far[:48]), 1)
+    outproj_shard = side(rows_of(small_sum[48:96]), rows_of(small_far[48:96]), 1)
+    down_shard = packed[:96].astype(F32)
+    up_shard = packed[96:].reshape(4, 24, WIDTH).transpose(1, 0, 2).reshape(24, FF).astype(F32)
+    gains_pair = ordered(core, small_sum[96, :48], small_far[96, :48])
     gain_pair = pick(gains_pair.reshape(2, 2, 24), core, 1)
 
     rand_shard = ordered(core, blocks, blocks_far, 1)

time: 527 us -> 538 us (1.021)
  Pallas kernels: 250 us -> 217 us
  waiting for transfers between devices: 160 us -> 192 us
  starting transfers between devices: 74.8 us -> 52.7 us
  local copies, waits for them, and re-layouts: 24.8 us -> 40 us
  between operations: 1.93 us -> 15 us
  other arithmetic: 9.33 us -> 15.9 us
    ppermute x23 -> x18, waiting for transfers between devices: 61.9 us -> 97.1 us  [ring(): lax.ppermute(x, BOTH, [(d, (d + 8 * way) % DEVICES) for d in range(DEVICE...]
    pallas_call x5 -> x3, Pallas kernels: 50.4 us -> 32.1 us  [the longest x1 14.7 us: run_up_grad(): pl.pallas_call(up_grad_kernel, grid=(FF // FSTEP,), in_specs=[held((ROWS,...]
    ppermute x23 -> x18, starting transfers between devices: 31.8 us -> 18.6 us  [ring(): lax.ppermute(x, BOTH, [(d, (d + 8 * way) % DEVICES) for d in range(DEVICE...]
    pallas_call x10 -> x5, Pallas kernels: 28.6 us -> 16 us  [run_add(): pl.pallas_call(partial(add_kernel, groups), grid=(parts,), in_specs=[bloc...]
    ppermute x66 -> x44, starting transfers between devices: 43 us -> 34.1 us  [swap(): return lax.ppermute(x, BOTH, [(d, d ^ bit) for d in range(DEVICES)])]
    slice x9 -> x8, local copies, waits for them, and re-layouts: 3.03 us -> 10.3 us  [the longest x1 6.57 us: chip_shards(): down = packed[:, 24:120].reshape(FF, WIDTH)]
    ppermute x66 -> x44, waiting for transfers between devices: 98.4 us -> 94.5 us  [swap(): return lax.ppermute(x, BOTH, [(d, d ^ bit) for d in range(DEVICES)])]
  transfers between devices with their start and end apart: 89 -> 64, of which waited for: 46 -> 33; matrix products, arithmetic and copies ran while one was open for 3% -> 4% of each run, Pallas kernels for 30% -> 21%
where the time goes in v8:
time: 538 us; the launch traced here: 532 us
  Pallas kernels  217 us (40%)
  waiting for transfers between devices  192 us (36%)
  starting transfers between devices  52.7 us (10%)
  local copies, waits for them, and re-layouts  40 us (7%)
  other arithmetic  15.9 us (3%)
  between operations  15 us (3%)
    ppermute x18, waiting for transfers between devices, ring(): lax.ppermute(x, BOTH, [(d, (d + 8 * way) % DEVICES) for d in range(DEVICE...  97.1 us
    ppermute x44, waiting for transfers between devices, swap(): return lax.ppermute(x, BOTH, [(d, d ^ bit) for d in range(DEVICES)])  94.5 us
    pallas_call x1, Pallas kernels, run_units(): pl.pallas_call(units_kernel, grid_spec=pltpu.PrefetchScalarGridSpec(num_s...  45 us
    pallas_call x2, Pallas kernels, run_unmix(): pl.pallas_call(partial(unmix_kernel, bool(carry)), grid_spec=pltpu.Prefet...  35.4 us
    ppermute x44, starting transfers between devices, swap(): return lax.ppermute(x, BOTH, [(d, d ^ bit) for d in range(DEVICES)])  34.1 us
    pallas_call x2, Pallas kernels, run_mix(): pl.pallas_call(partial(mix_kernel, bool(carry)), grid_spec=pltpu.Prefetch...  18.6 us
    ppermute x18, starting transfers between devices, ring(): lax.ppermute(x, BOTH, [(d, (d + 8 * way) % DEVICES) for d in range(DEVICE...  18.6 us
    pallas_call x1, Pallas kernels, run_post(): pl.pallas_call(post_kernel, grid_spec=pltpu.PrefetchScalarGridSpec(num_sc...  18 us
  transfers between devices with their start and end apart: 64, of which 33 were waited for; matrix products, arithmetic and copies ran while one was open for 4% of the time, Pallas kernels for 21%

profile of v8, /device:TPU:0, one launch (start us, length us, event | category | flops | bytes accessed | tf_op | source)
XLA Modules:
  0.0 532.4 jit_solution(3712429647761613368)
XLA Ops:
  61.9 10.4 %collective-permute-done.17.refs_1_.refs_5_ = bf16[384,1024]{1,0:T(8,128)(2,1)S(1)} collective-permute-done((bf16[384,1024]{1,0:T(8,128)(2,1)S(1)}, bf16[384,1024]{1,0:T(8,128)(2,1)S(1)}, u32[]{:S(2)}, u32[]{:S(2)}) %collective-permute-start.17) | collective-permute-done | bytes 786464 | tf_op jit(solution)/shard_map/ppermute | solution.py:724
  72.3 6.7 %collective-permute-done.19.refs_4_.refs_0_ = bf16[384,1024]{1,0:T(8,128)(2,1)} collective-permute-done((bf16[384,1024]{1,0:T(8,128)(2,1)S(1)}, bf16[384,1024]{1,0:T(8,128)(2,1)}, u32[]{:S(2)}, u32[]{:S(2)}) %collective-permute-start.19) | collective-permute-done | bytes 786464 | tf_op jit(solution)/shard_map/ppermute | solution.py:728
  84.2 7.7 %values.1.refs_8_ = bf16[12,1024,128]{2,1,0:T(8,128)(2,1)} custom-call(s32[7]{0:T(128)} %concatenate.46.sc, bf16[2,1024,768]{2,1,0:T(8,128)(2,1)} %tok.1, f32[1,768]{1,0:T(1,128)} %reshape.217.gain, bf16[768,768]{1,0:T(8,128)(2,1)} %bitcast.137), custom_call_target="tpu_custom_call" | custom-call | flops 2415919104 | bytes 6291456 | tf_op jit(solution)/shard_map/values/pallas_call | solution.py:71
  91.9 21.0 %collective-permute-done.21.refs_3_.refs_7_ = bf16[384,1024]{1,0:T(8,128)(2,1)} collective-permute-done((bf16[384,1024]{1,0:T(8,128)(2,1)S(1)}, bf16[384,1024]{1,0:T(8,128)(2,1)}, u32[]{:S(2)}, u32[]{:S(2)}) %collective-permute-start.21) | collective-permute-done | bytes 786464 | tf_op jit(solution)/shard_map/ppermute | solution.py:724
  121.8 17.1 %collective-permute-done.25.refs_6_.refs_2_ = bf16[384,1024]{1,0:T(8,128)(2,1)S(1)} collective-permute-done((bf16[384,1024]{1,0:T(8,128)(2,1)}, bf16[384,1024]{1,0:T(8,128)(2,1)S(1)}, u32[]{:S(2)}, u32[]{:S(2)}) %collective-permute-start.25) | collective-permute-done | bytes 786464 | tf_op jit(solution)/shard_map/ppermute | solution.py:724
  146.7 19.0 %collective-permute-done.29.refs_7_.refs_3_ = bf16[384,1024]{1,0:T(8,128)(2,1)S(1)} collective-permute-done((bf16[384,1024]{1,0:T(8,128)(2,1)}, bf16[384,1024]{1,0:T(8,128)(2,1)S(1)}, u32[]{:S(2)}, u32[]{:S(2)}) %collective-permute-start.29) | collective-permute-done | bytes 786464 | tf_op jit(solution)/shard_map/ppermute | solution.py:728
  168.6 9.3 %mix.2 = (bf16[12,512,256]{2,1,0:T(8,128)(2,1)}, f32[12,512,256]{2,1,0:T(8,128)}) custom-call(s32[7]{0:T(128)} %concatenate.46.sc, bf16[384,1024]{1,0:T(8,128)(2,1)} %bitcast.119, bf16[384,1024]{1,0:T(8,128)(2,1)} %copy-done.7, bf16[384,1024]{1,0:T(8,128)(2,1)} %copy-done.8, bf16[384,1024]{1,0:T(8,128)(2,1)} %collective-permute-done.21.refs_3_.refs_7_, ...), custom_call_target="tpu_custom_call" | custom-call | flops 3221225472 | bytes 14155776 | tf_op jit(solution)/shard_map/mix/pallas_call | solution.py:177
  178.0 6.7 %collective-permute-done.33.refs_3_.refs_7_ = bf16[384,1024]{1,0:T(8,128)(2,1)} collective-permute-done((bf16[384,1024]{1,0:T(8,128)(2,1)}, bf16[384,1024]{1,0:T(8,128)(2,1)}, u32[]{:S(2)}, u32[]{:S(2)}) %collective-permute-start.33) | collective-permute-done | bytes 786464 | tf_op jit(solution)/shard_map/ppermute | solution.py:724
  187.5 9.3 %mix.3 = (bf16[12,512,256]{2,1,0:T(8,128)(2,1)}, f32[12,512,256]{2,1,0:T(8,128)}) custom-call(s32[7]{0:T(128)} %concatenate.46.sc, bf16[384,1024]{1,0:T(8,128)(2,1)} %copy-done.3, bf16[384,1024]{1,0:T(8,128)(2,1)} %copy-done.4, bf16[384,1024]{1,0:T(8,128)(2,1)} %collective-permute-done.30.refs_2_.refs_6_, ...), custom_call_target="tpu_custom_call", output_to_operand_aliasing={{0}: (11, {}), {1}: (12, {})} | custom-call | flops 3221225472 | bytes 14155776 | tf_op jit(solution)/shard_map/mix/pallas_call | solution.py:177
  199.3 6.6 %fusion.12 = (bf16[32,96,768]{2,1,0:T(8,128)(2,1)}, bf16[32,96,768]{2,1,0:T(8,128)(2,1)S(1)}) fusion(bf16[32,216,768]{2,1,0:T(8,128)(2,1)} %bitcast.110), kind=kLoop, calls=%fused_computation.61 | loop fusion | bytes 18874368 | tf_op jit(solution)/shard_map/slice | solution.py:832
  208.4 12.4 %pre.1 = (bf16[4,512,768]{2,1,0:T(8,128)(2,1)}, bf16[4,512,768]{2,1,0:T(8,128)(2,1)}, bf16[4,512,768]{2,1,0:T(8,128)(2,1)}, bf16[4,512,768]{2,1,0:T(8,128)(2,1)}) custom-call(s32[7]{0:T(128)} %concatenate.46.sc, bf16[2,8,2,64,768]{4,3,2,1,0:T(8,128)(2,1)} %bitcast.114, bf16[2,8,64,768]{3,2,1,0:T(8,128)(2,1)} %collective-permute-done.24.tok_far, ...), custom_call_target="tpu_custom_call" | custom-call | flops 2415919104 | bytes 25165824 | tf_op jit(solution)/shard_map/pre/pallas_call | solution.py:250
  220.8 45.0 %units.1 = (bf16[2048,3072]{1,0:T(8,128)(2,1)}, bf16[2048,3072]{1,0:T(8,128)(2,1)}, bf16[2048,768]{1,0:T(8,128)(2,1)}) custom-call(s32[7]{0:T(128)} %concatenate.46.sc, bf16[2048,768]{1,0:T(8,128)(2,1)} %bitcast.150, bf16[2048,768]{1,0:T(8,128)(2,1)} %bitcast.148, bf16[4,768,768]{2,1,0:T(8,128)(2,1)} %bitcast.126, bf16[3072,768]{1,0:T(8,128)(2,1)} %bitcast.128), custom_call_target="tpu_custom_call" | custom-call | flops 28991029248 | bytes 37748736 | tf_op jit(solution)/shard_map/units/pallas_call | solution.py:309
  265.8 14.6 %down_grad.1 = bf16[3072,768]{1,0:T(8,128)(2,1)} custom-call(bf16[2048,3072]{1,0:T(8,128)(2,1)} %get-tuple-element.389.active, bf16[2048,768]{1,0:T(8,128)(2,1)} %bitcast.149), custom_call_target="tpu_custom_call" | custom-call | flops 9663676416 | bytes 15728640 | tf_op jit(solution)/shard_map/down_grad/pallas_call | solution.py:341
  280.4 14.7 %up_grad.1 = bf16[4,768,768]{2,1,0:T(8,128)(2,1)} custom-call(bf16[2048,768]{1,0:T(8,128)(2,1)} %bitcast.151, bf16[2048,3072]{1,0:T(8,128)(2,1)} %get-tuple-element.390.up_grad), custom_call_target="tpu_custom_call" | custom-call | flops 9663676416 | bytes 15728640 | tf_op jit(solution)/shard_map/up_grad/pallas_call | solution.py:360
  302.7 18.0 %post.1 = (bf16[2,512,768]{2,1,0:T(8,128)(2,1)}, bf16[2,512,768]{2,1,0:T(8,128)(2,1)}, bf16[12,512,256]{2,1,0:T(8,128)(2,1)}, bf16[2,768,384]{2,1,0:T(8,128)(2,1)}, f32[1,768]{1,0:T(1,128)}) custom-call(s32[7]{0:T(128)} %concatenate.46.sc, bf16[4,512,768]{2,1,0:T(8,128)(2,1)} %get-tuple-element.386.resid, bf16[4,512,768]{2,1,0:T(8,128)(2,1)} %bitcast.156, ...), custom_call_target="tpu_custom_call" | custom-call | flops 4831838208 | bytes 44040192 | tf_op jit(solution)/shard_map/post/pallas_call | solution.py:454
  320.8 17.4 %unmix.2 = (bf16[384,1024]{1,0:T(8,128)(2,1)}, bf16[384,1024]{1,0:T(8,128)(2,1)}, bf16[384,1024]{1,0:T(8,128)(2,1)}, bf16[384,1024]{1,0:T(8,128)(2,1)}, bf16[384...) custom-call(s32[7]{0:T(128)} %concatenate.46.sc, ...), custom_call_target="tpu_custom_call" | custom-call | flops 4831838208 | bytes 31457280 | tf_op jit(solution)/shard_map/unmix/pallas_call | solution.py:543
  342.9 17.9 %unmix.3 = (bf16[384,1024]{1,0:T(8,128)(2,1)}, bf16[384,1024]{1,0:T(8,128)(2,1)}, bf16[384,1024]{1,0:T(8,128)(2,1)}, bf16[384,1024]{1,0:T(8,128)(2,1)}, bf16[384...) custom-call(s32[7]{0:T(128)} %concatenate.46.sc, ...), custom_call_target="tpu_custom_call", output_to_operand_aliasing={{8}: (13, {}), {9}: (14, {})} | custom-call | flops 4831838208 | bytes 31457280 | tf_op jit(solution)/shard_map/unmix/pallas_call | solution.py:543
  369.5 16.1 %out.1 = (bf16[2,512,768]{2,1,0:T(8,128)(2,1)}, bf16[2,512,768]{2,1,0:T(8,128)(2,1)}) custom-call(s32[7]{0:T(128)} %concatenate.46.sc, bf16[4,512,3072]{2,1,0:T(8,128)(2,1)} %bitcast.153, bf16[4,512,768]{2,1,0:T(8,128)(2,1)} %get-tuple-element.386.resid, bf16[3072,768]{1,0:T(8,128)(2,1)} %bitcast.129), custom_call_target="tpu_custom_call" | custom-call | flops 9663676416 | bytes 23592960 | tf_op jit(solution)/shard_map/out/pallas_call | solution.py:384
  385.6 7.7 %collective-permute-done.41.refs_1_ = bf16[384,1024]{1,0:T(8,128)(2,1)S(1)} collective-permute-done((bf16[384,1024]{1,0:T(8,128)(2,1)}, bf16[384,1024]{1,0:T(8,128)(2,1)S(1)}, u32[]{:S(2)}, u32[]{:S(2)}) %collective-permute-start.41) | collective-permute-done | bytes 786464 | tf_op jit(solution)/shard_map/ppermute | solution.py:724
  394.1 14.7 %collective-permute-done.40.refs_0_ = bf16[384,1024]{1,0:T(8,128)(2,1)S(1)} collective-permute-done((bf16[384,1024]{1,0:T(8,128)(2,1)}, bf16[384,1024]{1,0:T(8,128)(2,1)S(1)}, u32[]{:S(2)}, u32[]{:S(2)}) %collective-permute-start.40) | collective-permute-done | bytes 786464 | tf_op jit(solution)/shard_map/ppermute | solution.py:728
  414.0 15.9 %close.1 = (f32[2,8,2,64,768]{4,3,2,1,0:T(8,128)}, f32[2,8,2,64,768]{4,3,2,1,0:T(8,128)}, bf16[2,768,384]{2,1,0:T(8,128)(2,1)}, f32[1,768]{1,0:T(1,128)}) custom-call(s32[7]{0:T(128)} %concatenate.46.sc, bf16[2,8,2,64,768]{4,3,2,1,0:T(8,128)(2,1)} %bitcast.115, bf16[2,8,64,768]{3,2,1,0:T(8,128)(2,1)} %bitcast.157, bf16[2,8,64,768]{3,2,1,0:T(8,128)(2,1)} %bitcast.152, ...), custom_call_target="tpu_custom_call" | custom-call | flops 4831838208 | bytes 29884416 | tf_op jit(solution)/shard_map/close/pallas_call | solution.py:631
  451.4 9.0 %collective-permute-done.52 = bf16[4,2,112,384]{3,2,1,0:T(8,128)(2,1)} collective-permute-done((bf16[4,2,112,384]{3,2,1,0:T(8,128)(2,1)S(1)}, bf16[4,2,112,384]{3,2,1,0:T(8,128)(2,1)}, u32[]{:S(2)}, u32[]{:S(2)}) %collective-permute-start.52) | collective-permute-done | bytes 688160 | tf_op jit(solution)/shard_map/ppermute | solution.py:724
  461.7 10.6 %collective-permute-done.48.refs_0_ = bf16[384,1024]{1,0:T(8,128)(2,1)S(1)} collective-permute-done((bf16[384,1024]{1,0:T(8,128)(2,1)}, bf16[384,1024]{1,0:T(8,128)(2,1)S(1)}, u32[]{:S(2)}, u32[]{:S(2)}) %collective-permute-start.48) | collective-permute-done | bytes 786464 | tf_op jit(solution)/shard_map/ppermute | solution.py:728
  493.3 13.7 %collective-permute-done.57 = bf16[112,384]{1,0:T(8,128)(2,1)S(1)} collective-permute-done((bf16[112,384]{1,0:T(8,128)(2,1)S(1)}, bf16[112,384]{1,0:T(8,128)(2,1)S(1)}, u32[]{:S(2)}, u32[]{:S(2)}) %collective-permute-start.57) | collective-permute-done | bytes 86048 | tf_op jit(solution)/shard_map/ppermute | solution.py:728
  (269 shorter events, 175.9 us)
Async XLA Ops:
  7.2 189.7 %all-gather.3.cloned.1.call-start = ((), (), s32[]{:S(2)}) async-start(), calls=%async_computation.2 | async-start | bytes 10948608 | tf_op jit(solution)/shard_map/all_gather | solution.py:798
  12.8 510.1 %reduce-scatter.2.cloned.1.call-start = ((), (), s32[]{:S(2)}) async-start(), calls=%async_computation.1 | async-start | bytes 9732096 | tf_op jit(solution)/shard_map/reduce_scatter | solution.py:840
  55.6 23.4 %collective-permute-start.19 = (bf16[384,1024]{1,0:T(8,128)(2,1)S(1)}, bf16[384,1024]{1,0:T(8,128)(2,1)}, u32[]{:S(2)}, u32[]{:S(2)}) collective-permute-start(bf16[384,1024]{1,0:T(8,128)(2,1)S(1)} %bitcast.118), channel_id=1, source_target_pairs={{0,8},{1,9},{2,10},{3,11},{4,12},{5,13},{6,14},{7,15},{8,16},{9,17... | collective-permute-start | bytes 2359304 | tf_op jit(solution)/shard_map/ppermute | solution.py:728
  61.5 30.5 %collective-permute-start.24 = (bf16[2,8,64,768]{3,2,1,0:T(8,128)(2,1)}, bf16[2,8,64,768]{3,2,1,0:T(8,128)(2,1)}, u32[]{:S(2)}, u32[]{:S(2)}) collective-permute-start(bf16[2,8,64,768]{3,2,1,0:T(8,128)(2,1)} %dynamic-slice_bitcast_fusion.1), channel_id=1, source_target_pairs={{0,1},{1,0},{2,3},{3,2},{4,5},{5,4},{6,7},{7,6},{8,9},{9,8},{10,11... | collective-permute-start | bytes 4718600 | tf_op jit(solution)/shard_map/ppermute | solution.py:724
  79.0 33.9 %collective-permute-start.21 = (bf16[384,1024]{1,0:T(8,128)(2,1)S(1)}, bf16[384,1024]{1,0:T(8,128)(2,1)}, u32[]{:S(2)}, u32[]{:S(2)}) collective-permute-start(bf16[384,1024]{1,0:T(8,128)(2,1)S(1)} %collective-permute-done.17.refs_1_.refs_5_), channel_id=1, source_target_pairs={{0,4},{1,5},{2,6},{3,7},{4,0},{5,1},{6,2},{7,3},{8,12},{9,13},{10,... | collective-permute-start | bytes 2359304 | tf_op jit(solution)/shard_map/ppermute | solution.py:724
  80.5 34.5 %collective-permute-start.22 = (bf16[384,1024]{1,0:T(8,128)(2,1)}, bf16[384,1024]{1,0:T(8,128)(2,1)}, u32[]{:S(2)}, u32[]{:S(2)}) collective-permute-start(bf16[384,1024]{1,0:T(8,128)(2,1)} %collective-permute-done.19.refs_4_.refs_0_), channel_id=1, source_target_pairs={{0,2},{1,3},{2,0},{3,1},{4,6},{5,7},{6,4},{7,5},{8,10},{9,11},{10,... | collective-permute-start | bytes 2359304 | tf_op jit(solution)/shard_map/ppermute | solution.py:724
  82.0 36.8 %collective-permute-start.23 = (bf16[384,1024]{1,0:T(8,128)(2,1)}, bf16[384,1024]{1,0:T(8,128)(2,1)S(1)}, u32[]{:S(2)}, u32[]{:S(2)}) collective-permute-start(bf16[384,1024]{1,0:T(8,128)(2,1)} %collective-permute-done.19.refs_4_.refs_0_), channel_id=1, source_target_pairs={{0,8},{1,9},{2,10},{3,11},{4,12},{5,13},{6,14},{7,15},{8,16},{9,17... | collective-permute-start | bytes 2359304 | tf_op jit(solution)/shard_map/ppermute | solution.py:728
  118.7 25.6 %collective-permute-start.28 = (bf16[12,1024,128]{2,1,0:T(8,128)(2,1)}, bf16[12,1024,128]{2,1,0:T(8,128)(2,1)}, u32[]{:S(2)}, u32[]{:S(2)}) collective-permute-start(bf16[12,1024,128]{2,1,0:T(8,128)(2,1)} %values.1.refs_8_), channel_id=1, source_target_pairs={{0,1},{1,0},{2,3},{3,2},{4,5},{5,4},{6,7},{7,6},{8,9},{9,8},{10,11... | collective-permute-start | bytes 9437192 | tf_op jit(solution)/shard_map/ppermute | solution.py:724
  118.7 25.6 %collective-permute-start.27 = (bf16[384,1024]{1,0:T(8,128)(2,1)S(1)}, bf16[384,1024]{1,0:T(8,128)(2,1)S(1)}, u32[]{:S(2)}, u32[]{:S(2)}) collective-permute-start(bf16[384,1024]{1,0:T(8,128)(2,1)S(1)} %collective-permute-done.23.refs_0_.refs_4_), channel_id=1, source_target_pairs={{0,8},{1,9},{2,10},{3,11},{4,12},{5,13},{6,14},{7,15},{8,16},{9,17... | collective-permute-start | bytes 2359304 | tf_op jit(solution)/shard_map/ppermute | solution.py:728
  121.5 25.3 %collective-permute-start.32 = (bf16[2,8,64,768]{3,2,1,0:T(8,128)(2,1)S(1)}, bf16[2,8,64,768]{3,2,1,0:T(8,128)(2,1)S(1)}, u32[]{:S(2)}, u32[]{:S(2)}) collective-permute-start(bf16[2,8,64,768]{3,2,1,0:T(8,128)(2,1)S(1)} %dynamic-slice_bitcast_fusion), channel_id=1, source_target_pairs={{0,1},{1,0},{2,3},{3,2},{4,5},{5,4},{6,7},{7,6},{8,9},{9,8},{10,11... | collective-permute-start | bytes 4718600 | tf_op jit(solution)/shard_map/ppermute | solution.py:724
  144.3 21.4 %collective-permute-start.29 = (bf16[384,1024]{1,0:T(8,128)(2,1)}, bf16[384,1024]{1,0:T(8,128)(2,1)S(1)}, u32[]{:S(2)}, u32[]{:S(2)}) collective-permute-start(bf16[384,1024]{1,0:T(8,128)(2,1)} %collective-permute-done.21.refs_3_.refs_7_), channel_id=1, source_target_pairs={{0,8},{1,9},{2,10},{3,11},{4,12},{5,13},{6,14},{7,15},{8,16},{9,17... | collective-permute-start | bytes 2359304 | tf_op jit(solution)/shard_map/ppermute | solution.py:728
  144.4 21.4 %collective-permute-start.30 = (bf16[384,1024]{1,0:T(8,128)(2,1)S(1)}, bf16[384,1024]{1,0:T(8,128)(2,1)}, u32[]{:S(2)}, u32[]{:S(2)}) collective-permute-start(bf16[384,1024]{1,0:T(8,128)(2,1)S(1)} %collective-permute-done.23.refs_0_.refs_4_), channel_id=1, source_target_pairs={{0,4},{1,5},{2,6},{3,7},{4,0},{5,1},{6,2},{7,3},{8,12},{9,13},{10,... | collective-permute-start | bytes 2359304 | tf_op jit(solution)/shard_map/ppermute | solution.py:724
  339.4 21.4 %collective-permute-start.37 = (bf16[384,1024]{1,0:T(8,128)(2,1)}, bf16[384,1024]{1,0:T(8,128)(2,1)S(1)}, u32[]{:S(2)}, u32[]{:S(2)}) collective-permute-start(bf16[384,1024]{1,0:T(8,128)(2,1)} %get-tuple-element.412), channel_id=1, source_target_pairs={{0,24},{1,25},{2,26},{3,27},{4,28},{5,29},{6,30},{7,31},{8,0},{9,1... | collective-permute-start | bytes 2359304 | tf_op jit(solution)/shard_map/ppermute | solution.py:728
  361.5 47.3 %collective-permute-start.43 = (bf16[12,1024,128]{2,1,0:T(8,128)(2,1)}, bf16[12,1024,128]{2,1,0:T(8,128)(2,1)}, u32[]{:S(2)}, u32[]{:S(2)}) collective-permute-start(bf16[12,1024,128]{2,1,0:T(8,128)(2,1)} %get-tuple-element.455), channel_id=1, source_target_pairs={{0,1},{1,0},{2,3},{3,2},{4,5},{5,4},{6,7},{7,6},{8,9},{9,8},{10,11... | collective-permute-start | bytes 9437192 | tf_op jit(solution)/shard_map/ppermute | solution.py:724
  365.5 27.7 %collective-permute-start.41 = (bf16[384,1024]{1,0:T(8,128)(2,1)}, bf16[384,1024]{1,0:T(8,128)(2,1)S(1)}, u32[]{:S(2)}, u32[]{:S(2)}) collective-permute-start(bf16[384,1024]{1,0:T(8,128)(2,1)} %get-tuple-element.451), channel_id=1, source_target_pairs={{0,2},{1,3},{2,0},{3,1},{4,6},{5,7},{6,4},{7,5},{8,10},{9,11},{10,... | collective-permute-start | bytes 2359304 | tf_op jit(solution)/shard_map/ppermute | solution.py:724
  366.6 27.5 %collective-permute-start.42 = (bf16[384,1024]{1,0:T(8,128)(2,1)}, bf16[384,1024]{1,0:T(8,128)(2,1)S(1)}, u32[]{:S(2)}, u32[]{:S(2)}) collective-permute-start(bf16[384,1024]{1,0:T(8,128)(2,1)} %get-tuple-element.452), channel_id=1, source_target_pairs={{0,4},{1,5},{2,6},{3,7},{4,0},{5,1},{6,2},{7,3},{8,12},{9,13},{10,... | collective-permute-start | bytes 2359304 | tf_op jit(solution)/shard_map/ppermute | solution.py:724
  367.6 41.2 %collective-permute-start.40 = (bf16[384,1024]{1,0:T(8,128)(2,1)}, bf16[384,1024]{1,0:T(8,128)(2,1)S(1)}, u32[]{:S(2)}, u32[]{:S(2)}) collective-permute-start(bf16[384,1024]{1,0:T(8,128)(2,1)} %get-tuple-element.445), channel_id=1, source_target_pairs={{0,24},{1,25},{2,26},{3,27},{4,28},{5,29},{6,30},{7,31},{8,0},{9,1... | collective-permute-start | bytes 2359304 | tf_op jit(solution)/shard_map/ppermute | solution.py:728
  413.4 20.9 %collective-permute-start.45 = (bf16[384,1024]{1,0:T(8,128)(2,1)}, bf16[384,1024]{1,0:T(8,128)(2,1)}, u32[]{:S(2)}, u32[]{:S(2)}) collective-permute-start(bf16[384,1024]{1,0:T(8,128)(2,1)} %get-tuple-element.470), channel_id=1, source_target_pairs={{0,2},{1,3},{2,0},{3,1},{4,6},{5,7},{6,4},{7,5},{8,10},{9,11},{10,... | collective-permute-start | bytes 2359304 | tf_op jit(solution)/shard_map/ppermute | solution.py:724
  446.2 26.1 %collective-permute-start.48 = (bf16[384,1024]{1,0:T(8,128)(2,1)}, bf16[384,1024]{1,0:T(8,128)(2,1)S(1)}, u32[]{:S(2)}, u32[]{:S(2)}) collective-permute-start(bf16[384,1024]{1,0:T(8,128)(2,1)} %get-tuple-element.495), channel_id=1, source_target_pairs={{0,24},{1,25},{2,26},{3,27},{4,28},{5,29},{6,30},{7,31},{8,0},{9,1... | collective-permute-start | bytes 2359304 | tf_op jit(solution)/shard_map/ppermute | solution.py:728
  449.4 27.1 %collective-permute-start.49 = (bf16[384,1024]{1,0:T(8,128)(2,1)}, bf16[384,1024]{1,0:T(8,128)(2,1)}, u32[]{:S(2)}, u32[]{:S(2)}) collective-permute-start(bf16[384,1024]{1,0:T(8,128)(2,1)} %get-tuple-element.496), channel_id=1, source_target_pairs={{0,2},{1,3},{2,0},{3,1},{4,6},{5,7},{6,4},{7,5},{8,10},{9,11},{10,... | collective-permute-start | bytes 2359304 | tf_op jit(solution)/shard_map/ppermute | solution.py:724
  450.3 26.2 %collective-permute-start.50 = (bf16[384,1024]{1,0:T(8,128)(2,1)}, bf16[384,1024]{1,0:T(8,128)(2,1)}, u32[]{:S(2)}, u32[]{:S(2)}) collective-permute-start(bf16[384,1024]{1,0:T(8,128)(2,1)} %get-tuple-element.497), channel_id=1, source_target_pairs={{0,4},{1,5},{2,6},{3,7},{4,0},{5,1},{6,2},{7,3},{8,12},{9,13},{10,... | collective-permute-start | bytes 2359304 | tf_op jit(solution)/shard_map/ppermute | solution.py:724
  481.4 32.3 %collective-permute-start.53 = (bf16[384,1024]{1,0:T(8,128)(2,1)}, bf16[384,1024]{1,0:T(8,128)(2,1)S(1)}, u32[]{:S(2)}, u32[]{:S(2)}) collective-permute-start(bf16[384,1024]{1,0:T(8,128)(2,1)} %get-tuple-element.505), channel_id=1, source_target_pairs={{0,24},{1,25},{2,26},{3,27},{4,28},{5,29},{6,30},{7,31},{8,0},{9,1... | collective-permute-start | bytes 2359304 | tf_op jit(solution)/shard_map/ppermute | solution.py:728
  484.7 29.0 %collective-permute-start.54 = (bf16[384,1024]{1,0:T(8,128)(2,1)}, bf16[384,1024]{1,0:T(8,128)(2,1)S(1)}, u32[]{:S(2)}, u32[]{:S(2)}) collective-permute-start(bf16[384,1024]{1,0:T(8,128)(2,1)} %get-tuple-element.506), channel_id=1, source_target_pairs={{0,2},{1,3},{2,0},{3,1},{4,6},{5,7},{6,4},{7,5},{8,10},{9,11},{10,... | collective-permute-start | bytes 2359304 | tf_op jit(solution)/shard_map/ppermute | solution.py:724
  485.9 27.8 %collective-permute-start.55 = (bf16[384,1024]{1,0:T(8,128)(2,1)}, bf16[384,1024]{1,0:T(8,128)(2,1)}, u32[]{:S(2)}, u32[]{:S(2)}) collective-permute-start(bf16[384,1024]{1,0:T(8,128)(2,1)} %get-tuple-element.507), channel_id=1, source_target_pairs={{0,4},{1,5},{2,6},{3,7},{4,0},{5,1},{6,2},{7,3},{8,12},{9,13},{10,... | collective-permute-start | bytes 2359304 | tf_op jit(solution)/shard_map/ppermute | solution.py:724
  (84 other events, 1181.7 us)
Sparse Core Ops, SparseCore 0:
  12.9 119.4 all-gather.2
  320.9 173.6 reduce-scatter.1

commit v9 on v8

--- a/solution.py
+++ b/solution.py
@@ -19,13 +19,14 @@
 F32 = jnp.float32
 VMEM = 61 << 20
 
-SUBS = 6
-RUNS = 8
+PARTS = 2
+SUBS = 6 // PARTS
+RUNS = 8 // PARTS
 HALF = 64
 HROWS = RUNS * HALF
 PLANES = 4
 PHEADS = HEADS // PLANES
-ROWS = 2 * LMAX
+ROWS = 4 * HROWS
 FSTEP = 768
 TILE = 512
 SIDE = WIDTH // 2
@@ -152,14 +153,14 @@
         mask[...] = (column < lane_lengths(sc, shape)).astype(F32).astype(BF16)
 
 
-def inverse_sums(sc, weights, mask):
+def inverse_sums(part, sc, weights, mask):
     shape = (HROWS, 4 * HEAD)
     line = lax.broadcasted_iota(jnp.int32, shape, 0)
-    position = 128 * (line // HALF) + HALF * sc[CORE] + line % HALF
+    position = 128 * (PARTS * (line // HALF) + part) + HALF * sc[CORE] + line % HALF
     return jnp.where(position < lane_lengths(sc, shape), 1.0 / dot(weights, mask[...], 1, 0), 0.0)
 
 
-def mix_kernel(carried, sc, *refs):
+def mix_kernel(part, carried, sc, *refs):
     shards, (v_own, v_far, *rest) = refs[:8], refs[8:]
     mixed, mean, raw, mask, sems = rest[2:] if carried else rest
     fill_mask(sc, mask)
@@ -167,15 +168,15 @@
     for head in range(PHEADS):
         weights = jnp.exp(raw[slot, head_rows(head)].astype(F32)).astype(BF16)
         values = jnp.concatenate([v_own[head], v_far[head]], axis=1)
-        found = dot(weights, values, 1, 0) * inverse_sums(sc, weights, mask)
+        found = dot(weights, values, 1, 0) * inverse_sums(part, sc, weights, mask)
         mean[head] = found
         mixed[head] = found.astype(BF16)
 
 
-def run_mix(sc, planes, shards, v_own, v_far, carry):
+def run_mix(part, sc, planes, shards, v_own, v_far, carry):
     carry = list(carry)
     return pl.pallas_call(
-        partial(mix_kernel, bool(carry)),
+        partial(mix_kernel, part, bool(carry)),
         grid_spec=pltpu.PrefetchScalarGridSpec(
             num_scalar_prefetch=1,
             grid=(2,),
@@ -202,43 +203,45 @@
     )(sc, *shards, v_own, v_far, *carry)
 
 
-def row_valid(sc, step):
+def row_valid(part, sc, step):
     line = lax.broadcasted_iota(jnp.int32, (4 * SPAN, 1), 0)
     item = line // SPAN
     row = step * SPAN + line % SPAN
     low = jnp.where(item == 0, sc[LENGTHS], sc[LENGTHS + 1])
     high = jnp.where(item == 2, sc[LENGTHS + 2], sc[LENGTHS + 3])
-    return 128 * (row // HALF) + HALF * sc[CORE] + row % HALF < jnp.where(item >= 2, high, low)
+    return 128 * (PARTS * (row // HALF) + part) + HALF * sc[CORE] + row % HALF < jnp.where(item >= 2, high, low)
 
 
 def four_items(own, far):
-    return jnp.concatenate([own[:, :, 0], far[...]], axis=0).reshape(4 * SPAN, WIDTH)
-
-
-def pre_kernel(sc, tok, tok_far, cot, cot_far, heads, weight, gain, mixed, resid, normed, grad):
+    return jnp.concatenate([own[:, :, 0, 0], far[:, :, 0]], axis=0).reshape(4 * SPAN, WIDTH)
+
+
+def pre_kernel(part, sc, tok, tok_far, cot, cot_far, heads, weight, gain, *refs):
+    mixed, resid, normed, grad = refs[-4:]
     step = pl.program_id(0)
     for item in range(4):
         lanes = slice(item * HEAD, (item + 1) * HEAD)
         for pair in range(HEADS // 2):
             both = jnp.concatenate([heads[2 * pair, :, lanes], heads[2 * pair + 1, :, lanes]], axis=1)
-            mixed[item, :, pair * 128 : (pair + 1) * 128] = both
+            mixed[0, item, :, pair * 128 : (pair + 1) * 128] = both
     res = four_items(tok, tok_far).astype(F32) + dot(mixed[...].reshape(4 * SPAN, WIDTH), weight[...], 1, 0)
-    resid[...] = res.astype(BF16).reshape(4, SPAN, WIDTH)
+    slab = (1, 4, SPAN, WIDTH)
+    resid[...] = res.astype(BF16).reshape(slab)
     scale = lax.rsqrt(jnp.mean(res * res, axis=-1, keepdims=True) + EPSILON)
-    valid = row_valid(sc, step)
-    normed[...] = jnp.where(valid, res * scale * gain[...], 0.0).astype(BF16).reshape(4, SPAN, WIDTH)
+    valid = row_valid(part, sc, step)
+    normed[...] = jnp.where(valid, res * scale * gain[...], 0.0).astype(BF16).reshape(slab)
     masked = jnp.where(valid, four_items(cot, cot_far).astype(F32), 0.0)
-    grad[...] = masked.astype(BF16).reshape(4, SPAN, WIDTH)
-
-
-def slab_spec(items=4):
-    return spec((items, SPAN, WIDTH), lambda r, s: (0, r, 0))
-
-
-def half_specs():
+    grad[...] = masked.astype(BF16).reshape(slab)
+
+
+def slab_spec(part, items=4):
+    return spec((1, items, SPAN, WIDTH), lambda r, s: (part, 0, r, 0))
+
+
+def half_specs(part):
     return [
-        spec((2, SPAN // HALF, 1, HALF, WIDTH), lambda r, s: (0, r, s[CORE], 0, 0)),
-        spec((2, SPAN // HALF, HALF, WIDTH), lambda r, s: (0, r, 0, 0)),
+        spec((2, SPAN // HALF, 1, 1, HALF, WIDTH), lambda r, s: (0, r, part, s[CORE], 0, 0)),
+        spec((2, SPAN // HALF, 1, HALF, WIDTH), lambda r, s: (0, r, part, 0, 0)),
     ]
 
 
@@ -246,32 +249,32 @@
     return spec((HEADS, SPAN, 4 * HEAD), lambda r, s: (0, r, 0))
 
 
-def run_pre(sc, tokens, tokens_far, cotangent, cotangent_far, heads, weight, gain):
-    return pl.pallas_call(
-        pre_kernel,
+def run_pre(part, sc, tokens, tokens_far, cotangent, cotangent_far, heads, weight, gain, carry):
+    own = lambda x: x.reshape(2, RUNS, PARTS, 2, HALF, WIDTH)
+    far = lambda x: x.reshape(2, RUNS, PARTS, HALF, WIDTH)
+    return pl.pallas_call(
+        partial(pre_kernel, part),
         grid_spec=pltpu.PrefetchScalarGridSpec(
             num_scalar_prefetch=1,
             grid=(HROWS // SPAN,),
-            in_specs=half_specs()
-            + half_specs()
-            + [heads_spec(), held((WIDTH, WIDTH)), held((1, WIDTH))],
-            out_specs=[slab_spec()] * 4,
-        ),
-        out_shape=[
-            jax.ShapeDtypeStruct((4, HROWS, WIDTH), BF16),
-            jax.ShapeDtypeStruct((4, HROWS, WIDTH), BF16),
-            jax.ShapeDtypeStruct((4, HROWS, WIDTH), BF16),
-            jax.ShapeDtypeStruct((4, HROWS, WIDTH), BF16),
-        ],
+            in_specs=half_specs(part)
+            + half_specs(part)
+            + [heads_spec(), held((WIDTH, WIDTH)), held((1, WIDTH))]
+            + anywhere(len(carry)),
+            out_specs=[slab_spec(part)] * 4,
+        ),
+        out_shape=[jax.ShapeDtypeStruct((PARTS, 4, HROWS, WIDTH), BF16)] * 4,
+        input_output_aliases={8 + i: i for i in range(len(carry))},
         compiler_params=params(VMEM),
         cost_estimate=pl.CostEstimate(
             flops=2 * ROWS * WIDTH * WIDTH, bytes_accessed=16 * ROWS * WIDTH, transcendentals=0
         ),
         name="pre",
-    )(sc, tokens, tokens_far, cotangent, cotangent_far, heads, weight, gain)
-
-
-def units_kernel(sc, normed, cot, w_up, w_down, active, up_grad, back, total):
+    )(sc, own(tokens), far(tokens_far), own(cotangent), far(cotangent_far), heads, weight, gain, *carry)
+
+
+def units_kernel(sc, normed, cot, w_up, w_down, *refs):
+    active, up_grad, back, total = refs[-4:]
     step = pl.program_id(0)
     for piece in range(ROWS // TILE):
         whole = slice(piece * TILE, (piece + 1) * TILE)
@@ -304,112 +307,179 @@
             back[whole] = (total[whole] + two_grad).astype(BF16)
 
 
-def run_units(sc, normed, cotangent, w_up, w_down):
-    columns = spec((ROWS, FSTEP), lambda f, s: (0, f))
+def run_units(part, sc, normed, cotangent, w_up, w_down, carry):
+    columns = spec((ROWS, FSTEP), lambda f, s: (part, f))
+    rows = pl.BlockSpec((ROWS, WIDTH), lambda f, s: (part, 0), pipeline_mode=pl.Buffered(1))
+    flat = lambda x: x.reshape(PARTS * ROWS, WIDTH)
     return pl.pallas_call(
         units_kernel,
         grid_spec=pltpu.PrefetchScalarGridSpec(
             num_scalar_prefetch=1,
             grid=(FF // FSTEP,),
             in_specs=[
-                held((ROWS, WIDTH)),
-                held((ROWS, WIDTH)),
+                rows,
+                rows,
                 spec((1, WIDTH, FSTEP), lambda f, s: (f, 0, 0)),
                 spec((FSTEP, WIDTH), lambda f, s: (f, 0)),
-            ],
+            ]
+            + anywhere(len(carry)),
             out_specs=[columns, columns, held((ROWS, WIDTH))],
             scratch_shapes=[pltpu.VMEM((ROWS, WIDTH), F32)],
         ),
         out_shape=[
-            jax.ShapeDtypeStruct((ROWS, FF), BF16),
-            jax.ShapeDtypeStruct((ROWS, FF), BF16),
+            jax.ShapeDtypeStruct((PARTS * ROWS, FF), BF16),
+            jax.ShapeDtypeStruct((PARTS * ROWS, FF), BF16),
             jax.ShapeDtypeStruct((ROWS, WIDTH), BF16),
         ],
+        input_output_aliases={5 + i: i for i in range(len(carry))},
         compiler_params=params(VMEM),
         cost_estimate=pl.CostEstimate(
             flops=6 * ROWS * WIDTH * FF, bytes_accessed=8 * ROWS * WIDTH + 4 * ROWS * FF, transcendentals=ROWS * FF
         ),
         name="units",
-    )(sc, normed.reshape(ROWS, WIDTH), cotangent.reshape(ROWS, WIDTH), w_up, w_down)
-
-
-def down_grad_kernel(active, cot, total):
+    )(sc, flat(normed), flat(cotangent), w_up, w_down, *carry)
+
+
+def own_lanes(sc):
+    return pl.ds(pl.multiple_of(sc[CORE] * SIDE, 128), SIDE)
+
+
+def far_lanes(sc):
+    return pl.ds(pl.multiple_of((1 - sc[CORE]) * SIDE, 128), SIDE)
+
+
+def down_grad_kernel(sc, active, cot, own, far, total):
     total[...] = dot(active[...], cot[...], 0, 0).astype(BF16)
-
-
-def run_down_grad(active, cotangent):
+    own[...] = total[:, own_lanes(sc)]
+    far[...] = total[:, far_lanes(sc)]
+
+
+def run_down_grad(sc, active, cotangent):
+    rows = PARTS * ROWS
     return pl.pallas_call(
         down_grad_kernel,
-        grid=(FF // 512,),
-        in_specs=[spec((ROWS, 512), lambda f: (0, f)), held((ROWS, WIDTH))],
-        out_specs=spec((512, WIDTH), lambda f: (f, 0)),
-        out_shape=jax.ShapeDtypeStruct((FF, WIDTH), BF16),
+        grid_spec=pltpu.PrefetchScalarGridSpec(
+            num_scalar_prefetch=1,
+            grid=(FF // 512,),
+            in_specs=[spec((rows, 512), lambda f, s: (0, f)), held((rows, WIDTH))],
+            out_specs=[spec((512, SIDE), lambda f, s: (f, 0))] * 2,
+            scratch_shapes=[pltpu.VMEM((512, WIDTH), BF16)],
+        ),
+        out_shape=[jax.ShapeDtypeStruct((FF, SIDE), BF16)] * 2,
         compiler_params=params(VMEM),
         cost_estimate=pl.CostEstimate(
-            flops=2 * ROWS * WIDTH * FF, bytes_accessed=2 * ROWS * (WIDTH + FF), transcendentals=0
+            flops=2 * rows * WIDTH * FF, bytes_accessed=2 * rows * (WIDTH + FF), transcendentals=0
         ),
         name="down_grad",
-    )(active, cotangent.reshape(ROWS, WIDTH))
-
-
-def up_grad_kernel(normed, up_grad, total):
-    total[0] = dot(normed[...], up_grad[...], 0, 0).astype(BF16)
-
-
-def run_up_grad(normed, up_grad):
+    )(sc, active, cotangent.reshape(rows, WIDTH))
+
+
+def up_grad_kernel(sc, normed, up_grad, own, far):
+    total = dot(normed[...], up_grad[...], 0, 0).astype(BF16)
+
+    @pl.when(pl.program_id(0) < 2)
+    def _():
+        own[...] = total
+
+    @pl.when(pl.program_id(0) >= 2)
+    def _():
+        far[...] = total
+
+
+def run_up_grad(sc, normed, up_grad):
+    rows = PARTS * ROWS
     return pl.pallas_call(
         up_grad_kernel,
-        grid=(FF // FSTEP,),
-        in_specs=[held((ROWS, WIDTH)), spec((ROWS, FSTEP), lambda f: (0, f))],
-        out_specs=spec((1, WIDTH, FSTEP), lambda f: (f, 0, 0)),
-        out_shape=jax.ShapeDtypeStruct((FF // FSTEP, WIDTH, FSTEP), BF16),
+        grid_spec=pltpu.PrefetchScalarGridSpec(
+            num_scalar_prefetch=1,
+            grid=(4,),
+            in_specs=[held((rows, WIDTH)), spec((rows, FF // 4), lambda f, s: (0, lax.rem(2 * s[CORE] + f, 4)))],
+            out_specs=[
+                spec((WIDTH, FF // 4), lambda f, s: (0, lax.min(f, 1))),
+                spec((WIDTH, FF // 4), lambda f, s: (0, lax.max(f - 2, 0))),
+            ],
+        ),
+        out_shape=[jax.ShapeDtypeStruct((WIDTH, FF // 2), BF16)] * 2,
         compiler_params=params(VMEM),
         cost_estimate=pl.CostEstimate(
-            flops=2 * ROWS * WIDTH * FF, bytes_accessed=2 * ROWS * (WIDTH + FF), transcendentals=0
+            flops=2 * rows * WIDTH * FF, bytes_accessed=2 * rows * (WIDTH + FF), transcendentals=0
         ),
         name="up_grad",
-    )(normed.reshape(ROWS, WIDTH), up_grad)
+    )(sc, normed.reshape(rows, WIDTH), up_grad)
+
+
+def out_grad_kernel(sc, mixed, res_own, res_far, own, far, total):
+    step = pl.program_id(0)
+    grad = jnp.concatenate([res_own[...].reshape(ROWS // 2, WIDTH), res_far[...].reshape(ROWS // 2, WIDTH)], axis=0)
+    found = dot(mixed[...].reshape(ROWS, WIDTH), grad, 0, 0)
+
+    @pl.when(step == 0)
+    def _():
+        total[...] = found
+
+    @pl.when(step > 0)
+    def _():
+        total[...] += found
+
+    @pl.when(step == PARTS - 1)
+    def _():
+        own[...] = total[:, own_lanes(sc)].astype(BF16)
+        far[...] = total[:, far_lanes(sc)].astype(BF16)
+
+
+def run_out_grad(sc, mixed, res_own, res_far):
+    block = lambda items: spec((1, items, HROWS, WIDTH), lambda p, s: (p, 0, 0, 0))
+    return pl.pallas_call(
+        out_grad_kernel,
+        grid_spec=pltpu.PrefetchScalarGridSpec(
+            num_scalar_prefetch=1,
+            grid=(PARTS,),
+            in_specs=[block(4), block(2), block(2)],
+            out_specs=[held((WIDTH, SIDE))] * 2,
+            scratch_shapes=[pltpu.VMEM((WIDTH, WIDTH), F32)],
+        ),
+        out_shape=[jax.ShapeDtypeStruct((WIDTH, SIDE), BF16)] * 2,
+        compiler_params=params(VMEM),
+        cost_estimate=pl.CostEstimate(
+            flops=2 * PARTS * ROWS * WIDTH * WIDTH, bytes_accessed=4 * PARTS * ROWS * WIDTH, transcendentals=0
+        ),
+        name="out_grad",
+    )(sc, mixed, res_own, res_far)
 
 
 def out_kernel(sc, active, resid, w_down, own, far):
-    step = pl.program_id(0)
     branch = dot(active[...].reshape(4 * SPAN, FF), w_down[...], 1, 0)
-    output = jnp.where(row_valid(sc, step), resid[...].reshape(4 * SPAN, WIDTH).astype(F32) + branch, 0.0)
-    output = output.astype(BF16).reshape(4, SPAN, WIDTH)
-    own[...] = output[:2]
-    far[...] = output[2:]
+    valid = row_valid(pl.program_id(0), sc, pl.program_id(1))
+    output = jnp.where(valid, resid[...].reshape(4 * SPAN, WIDTH).astype(F32) + branch, 0.0)
+    output = output.astype(BF16).reshape(1, 4, SPAN, WIDTH)
+    own[...] = output[:, :2]
+    far[...] = output[:, 2:]
 
 
 def run_out(sc, active, resid, w_down):
+    block = lambda items, lanes: spec((1, items, SPAN, lanes), lambda p, r, s: (p, 0, r, 0))
     return pl.pallas_call(
         out_kernel,
         grid_spec=pltpu.PrefetchScalarGridSpec(
             num_scalar_prefetch=1,
-            grid=(HROWS // SPAN,),
-            in_specs=[
-                spec((4, SPAN, FF), lambda r, s: (0, r, 0)),
-                slab_spec(),
-                held((FF, WIDTH)),
-            ],
-            out_specs=[slab_spec(2)] * 2,
-        ),
-        out_shape=[
-            jax.ShapeDtypeStruct((2, HROWS, WIDTH), BF16),
-            jax.ShapeDtypeStruct((2, HROWS, WIDTH), BF16),
-        ],
+            grid=(PARTS, HROWS // SPAN),
+            in_specs=[block(4, FF), block(4, WIDTH), held((FF, WIDTH))],
+            out_specs=[block(2, WIDTH)] * 2,
+        ),
+        out_shape=[jax.ShapeDtypeStruct((PARTS, 2, HROWS, WIDTH), BF16)] * 2,
         compiler_params=params(VMEM),
         cost_estimate=pl.CostEstimate(
-            flops=2 * ROWS * WIDTH * FF, bytes_accessed=ROWS * (2 * FF + 7 * WIDTH), transcendentals=0
+            flops=2 * PARTS * ROWS * WIDTH * FF, bytes_accessed=PARTS * ROWS * (2 * FF + 7 * WIDTH), transcendentals=0
         ),
         name="out",
-    )(sc, active.reshape(4, HROWS, FF), resid, w_down)
-
-
-def post_kernel(sc, resid, back, cot, mixed, weight, gain, *refs):
-    (res_own, res_far, heads, d_out, d_gain, total, spread) = refs
+    )(sc, active.reshape(PARTS, 4, HROWS, FF), resid, w_down)
+
+
+def post_kernel(part, sc, resid, back, cot, weight, gain, *refs):
+    (res_own, res_far, heads, d_gain, spread) = refs[-5:]
     step = pl.program_id(0)
-    shape, slab = (4 * SPAN, WIDTH), (4, SPAN, WIDTH)
-    valid = row_valid(sc, step)
+    shape, slab = (4 * SPAN, WIDTH), (1, 4, SPAN, WIDTH)
+    valid = row_valid(part, sc, step)
     res = resid[...].reshape(shape).astype(F32)
     scale = lax.rsqrt(jnp.mean(res * res, axis=-1, keepdims=True) + EPSILON)
     unit = res * scale
@@ -418,22 +488,19 @@
     masked = cot[...].reshape(shape).astype(F32)
     grad = masked + scale * (gained - unit * jnp.mean(gained * unit, axis=-1, keepdims=True))
     low = grad.astype(BF16)
-    res_own[...] = low.reshape(slab)[:2]
-    res_far[...] = low.reshape(slab)[2:]
+    res_own[...] = low.reshape(slab)[:, :2]
+    res_far[...] = low.reshape(slab)[:, 2:]
     gain_sum = jnp.sum(two_grad * unit, axis=0, keepdims=True)
-    out_sum = dot(mixed[...].reshape(shape), low, 0, 0)
 
     @pl.when(step == 0)
     def _():
         d_gain[...] = gain_sum
-        total[...] = out_sum
 
     @pl.when(step > 0)
     def _():
         d_gain[...] += gain_sum
-        total[...] += out_sum
-
-    spread[...] = dot(low, weight[...], 1, 1).astype(BF16).reshape(slab)
+
+    spread[...] = dot(low, weight[...], 1, 1).astype(BF16).reshape(4, SPAN, WIDTH)
     for pair in range(HEADS // 2):
         lanes = slice(pair * 128, (pair + 1) * 128)
         for side in range(2):
@@ -442,46 +509,38 @@
             heads[2 * pair, :, half] = jnp.concatenate([one[:, :HEAD], two[:, :HEAD]], axis=1)
             heads[2 * pair + 1, :, half] = jnp.concatenate([one[:, HEAD:], two[:, HEAD:]], axis=1)
 
-    @pl.when(step == pl.num_programs(0) - 1)
-    def _():
-        low = total[...].astype(BF16)
-        d_out[0] = low[:, :SIDE]
-        d_out[1] = low[:, SIDE:]
-
-
-def run_post(sc, resid, back, cotangent, mixed, weight, gain):
-    whole = (4, HROWS, WIDTH)
-    return pl.pallas_call(
-        post_kernel,
+
+def run_post(part, sc, resid, back, cotangent, weight, gain, carry):
+    return pl.pallas_call(
+        partial(post_kernel, part),
         grid_spec=pltpu.PrefetchScalarGridSpec(
             num_scalar_prefetch=1,
             grid=(HROWS // SPAN,),
-            in_specs=[slab_spec()] * 4 + [held((WIDTH, WIDTH)), held((1, WIDTH))],
-            out_specs=[slab_spec(2)] * 2
-            + [heads_spec(), held((2, WIDTH, SIDE)), held((1, WIDTH))],
-            scratch_shapes=[
-                pltpu.VMEM((WIDTH, WIDTH), F32),
-                pltpu.VMEM((4, SPAN, WIDTH), BF16),
-            ],
+            in_specs=[slab_spec(part), slab_spec(0), slab_spec(part), held((WIDTH, WIDTH)), held((1, WIDTH))]
+            + anywhere(len(carry)),
+            out_specs=[slab_spec(part, 2)] * 2 + [heads_spec(), held((1, WIDTH))],
+            scratch_shapes=[pltpu.VMEM((4, SPAN, WIDTH), BF16)],
         ),
         out_shape=[
-            jax.ShapeDtypeStruct((2, HROWS, WIDTH), BF16),
-            jax.ShapeDtypeStruct((2, HROWS, WIDTH), BF16),
+            jax.ShapeDtypeStruct((PARTS, 2, HROWS, WIDTH), BF16),
+            jax.ShapeDtypeStruct((PARTS, 2, HROWS, WIDTH), BF16),
             jax.ShapeDtypeStruct((HEADS, HROWS, 4 * HEAD), BF16),
-            jax.ShapeDtypeStruct((2, WIDTH, SIDE), BF16),
             jax.ShapeDtypeStruct((1, WIDTH), F32),
         ],
+        input_output_aliases={6 + i: i for i in range(len(carry))},
         compiler_params=params(VMEM),
         cost_estimate=pl.CostEstimate(
-            flops=4 * ROWS * WIDTH * WIDTH, bytes_accessed=28 * ROWS * WIDTH, transcendentals=0
+            flops=2 * ROWS * WIDTH * WIDTH, bytes_accessed=12 * ROWS * WIDTH, transcendentals=0
         ),
         name="post",
-    )(sc, resid, back.reshape(whole), cotangent, mixed, weight, gain)
-
-
-def unmix_kernel(carried, sc, *refs):
+    )(sc, resid, back.reshape(1, 4, HROWS, WIDTH), cotangent, weight, gain, *carry)
+
+
+def unmix_kernel(part, carried, added, sc, *refs):
     shards, (v_own, v_far, grad_heads, mean, *rest) = refs[:8], refs[8:]
     rest = rest[2:] if carried else rest
+    if added:
+        own_in, far_in, *rest = rest
     outs, (own, far, raw, grads, mask, adder, bound, sems, out_sems) = rest[:8], rest[8:]
     place = sc[PLACE]
     step = pl.program_id(0)
@@ -514,7 +573,7 @@
     high_lanes = lax.broadcasted_iota(jnp.int32, (HROWS, 128), 1) < 4
     for head in range(PHEADS):
         weights = jnp.exp(raw[slot, head_rows(head)].astype(F32)).astype(BF16)
-        low = (grad_heads[head].astype(F32) * inverse_sums(sc, weights, mask)).astype(BF16)
+        low = (grad_heads[head].astype(F32) * inverse_sums(part, sc, weights, mask)).astype(BF16)
         product = low.astype(F32) * mean[head]
         coarse = product.astype(BF16)
         fine = (product - coarse.astype(F32)).astype(BF16)
@@ -524,9 +583,12 @@
         left = jnp.concatenate([low, jnp.where(high_lanes, coarse, fine)], axis=1)
         score = dot(left, jnp.concatenate([v_own[head], v_far[head], bound[...]], axis=1), 1, 1)
         grads[slot, head_rows(head)] = (score * weights.astype(F32)).astype(BF16)
-        back = (dot(weights, low, 0, 0) * mask[...].astype(F32)).astype(BF16)
-        own[head] = back[:, : 2 * HEAD]
-        far[head] = back[:, 2 * HEAD :]
+        back = dot(weights, low, 0, 0) * mask[...].astype(F32)
+        for target, lanes in ((own, slice(0, 2 * HEAD)), (far, slice(2 * HEAD, 4 * HEAD))):
+            found = back[:, lanes]
+            if added:
+                found = found + (own_in if target is own else far_in)[head].astype(F32)
+            target[head] = found.astype(BF16)
     for which in range(2):
 
         @pl.when(step == which)
@@ -538,17 +600,18 @@
                     copy.wait()
 
 
-def run_unmix(sc, planes, shards, v_own, v_far, grad_heads, mean, carry):
-    carry = list(carry)
-    return pl.pallas_call(
-        partial(unmix_kernel, bool(carry)),
+def run_unmix(part, sc, planes, shards, v_own, v_far, grad_heads, mean, carry, add):
+    carry, add = list(carry), list(add)
+    return pl.pallas_call(
+        partial(unmix_kernel, part, bool(carry), bool(add)),
         grid_spec=pltpu.PrefetchScalarGridSpec(
             num_scalar_prefetch=1,
             grid=(2,),
             in_specs=anywhere(8)
             + [plane_spec(planes, LMAX, 2 * HEAD)] * 2
             + [plane_spec(planes, HROWS, 4 * HEAD)] * 2
-            + anywhere(len(carry)),
+            + anywhere(len(carry))
+            + [plane_spec(planes, LMAX, 2 * HEAD)] * len(add),
             out_specs=anywhere(8) + [plane_spec(planes, LMAX, 2 * HEAD)] * 2,
             scratch_shapes=[
                 pltpu.VMEM((2, 4 * SUBS * HALF, LMAX), BF16),
@@ -570,17 +633,18 @@
             transcendentals=HEADS * HROWS * LMAX // 2,
         ),
         name="unmix",
-    )(sc, *shards, v_own, v_far, grad_heads, mean, *carry)
+    )(sc, *shards, v_own, v_far, grad_heads, mean, *carry, *add)
 
 
 def close_kernel(sc, tok, res_own, res_got, out_own, out_got, own, far, gain, weight, *refs):
     (output, tok_grad, d_value, d_gain, total) = refs
     step = pl.program_id(0)
     core = sc[CORE]
-    output[:, :, core] = out_own[...].astype(F32)
-    output[:, :, 1 - core] = out_got[...].astype(F32)
-    tok_grad[:, :, core] = res_own[...].astype(F32)
-    tok_grad[:, :, 1 - core] = res_got[...].astype(F32)
+    for part in range(PARTS):
+        output[:, part, core] = out_own[part, :, 0].astype(F32)
+        output[:, part, 1 - core] = out_got[part, :, 0].astype(F32)
+        tok_grad[:, part, core] = res_own[part, :, 0].astype(F32)
+        tok_grad[:, part, 1 - core] = res_got[part, :, 0].astype(F32)
     runs = tok.shape[1]
     rows = runs * 128
     for item in range(2):
@@ -622,17 +686,17 @@
 
 
 def run_close(sc, tokens, res_own, res_got, out_own, out_got, own, far, gain, weight):
-    runs = 2
-    slab = (2, RUNS, 2, HALF, WIDTH)
-    half = (2, RUNS, HALF, WIDTH)
+    runs = PARTS
+    slab = (2, PARTS * RUNS, 2, HALF, WIDTH)
+    half = (PARTS, 2, RUNS, HALF, WIDTH)
     whole_spec = spec((2, runs, 2, HALF, WIDTH), lambda j, s: (0, j, 0, 0, 0))
-    half_spec = spec((2, runs, HALF, WIDTH), lambda j, s: (0, j, 0, 0))
+    half_spec = spec((PARTS, 2, 1, HALF, WIDTH), lambda j, s: (0, 0, j, 0, 0))
     back_spec = spec((HEADS, runs * 128, 2 * HEAD), lambda j, s: (0, j, 0))
     return pl.pallas_call(
         close_kernel,
         grid_spec=pltpu.PrefetchScalarGridSpec(
             num_scalar_prefetch=1,
-            grid=(RUNS // runs,),
+            grid=(RUNS,),
             in_specs=[whole_spec]
             + [half_spec] * 4
             + [back_spec, back_spec, held((1, WIDTH)), held((WIDTH, WIDTH))],
@@ -690,6 +754,48 @@
     )(sc, *pieces)
 
 
+PACK_DOWN, PACK_UP, PACK_OUT, PACK = 0, 192, 384, 432
+
+
+def chip_of(sc, k, rel):
+    return plane_of(k, sc) * 4 + (sc[PLACE] ^ rel)
+
+
+def collect_kernel(sc, *refs):
+    outs = refs[24:]
+    for k in range(PLANES):
+
+        @pl.when(pl.program_id(0) == k)
+        def _():
+            for rel in range(4):
+                down, down_got, up, up_got, out, out_got = refs[6 * rel : 6 * rel + 6]
+                packed = outs[4 * k + rel]
+                packed[PACK_DOWN:PACK_UP] = add_low(down[...], down_got[...])
+                for j in range(4):
+                    lanes = slice(j * SIDE, (j + 1) * SIDE)
+                    packed[PACK_UP + 48 * j : PACK_UP + 48 * (j + 1)] = add_low(up[:, lanes], up_got[:, lanes])
+                packed[PACK_OUT:PACK] = add_low(out[...], out_got[...])
+
+
+def run_collect(sc, *sides):
+    def rows(x, rel):
+        return spec((x.shape[0] // 16, x.shape[1]), lambda k, s: (chip_of(s, k, rel), 0))
+
+    return pl.pallas_call(
+        collect_kernel,
+        grid_spec=pltpu.PrefetchScalarGridSpec(
+            num_scalar_prefetch=1,
+            grid=(PLANES,),
+            in_specs=[rows(x, rel) for rel in range(4) for x in sides],
+            out_specs=[held((PACK, SIDE))] * 16,
+        ),
+        out_shape=[jax.ShapeDtypeStruct((PACK, SIDE), BF16)] * 16,
+        compiler_params=params(VMEM),
+        cost_estimate=pl.CostEstimate(flops=0, bytes_accessed=3 * 16 * PACK * SIDE * 2, transcendentals=0),
+        name="collect",
+    )(sc, *(x for _ in range(4) for x in sides))
+
+
 def add_kernel(groups, *refs):
     for group, total in zip(groups, refs[-len(groups) :]):
         value = refs[group[0]][...].astype(F32)
@@ -700,11 +806,10 @@
 
 def run_add(groups, values, dtype):
     rows, columns = values[0].shape
-    parts = 2 if columns == LMAX else 1
-    block = pl.BlockSpec((rows // parts, columns), lambda i: (i, 0))
+    block = pl.BlockSpec((rows, columns), lambda i: (i, 0))
     return pl.pallas_call(
         partial(add_kernel, groups),
-        grid=(parts,),
+        grid=(1,),
         in_specs=[block] * len(values),
         out_specs=[block] * len(groups),
         out_shape=[jax.ShapeDtypeStruct((rows, columns), dtype)] * len(groups),
@@ -791,7 +896,7 @@
     z, y, x = wide // 4, (wide // 2) % 2, wide % 2
     other = lambda value: swap(value, TO_CORE)
     side = partial(ordered, core, joined=jnp.concatenate)
-    slab = (2, RUNS, 2, HALF, WIDTH)
+    slab = (2, PARTS * RUNS, 2, HALF, WIDTH)
     tokens, grad_out = tokens.reshape(slab), grad_out.reshape(slab)
 
     packed = jnp.concatenate([w_out, w_down, *(w_up[:, j * WIDTH : (j + 1) * WIDTH] for j in range(4))])
@@ -801,13 +906,12 @@
     firsts = {(0, 0, 0): jnp.concatenate([w_value, gains])}
     rand = rand_mix.reshape(3, 2, HALF, LMAX)
     blocks = side(pick(rand, core, 1), other(pick(rand, 1 - core, 1)), 0)
-    firsts, rands, far_lengths = together(
-        (gather_step(firsts, 0), {(0, 0, 0): blocks.reshape(SUBS * HALF, LMAX)}, other(lengths))
-    )
+    starts = [{(0, 0, 0): blocks[part::PARTS].reshape(SUBS * HALF, LMAX)} for part in range(PARTS)]
+    firsts, starts, far_lengths = together((gather_step(firsts, 0), starts, other(lengths)))
     sc = jnp.concatenate([jnp.stack([core, z, wide % 4]).astype(jnp.int32), lengths, far_lengths])
     for step in range(1, 5):
         firsts = together(gather_step(firsts, step))
-    firsts, rands = together((firsts, rands))
+    firsts, rands = together((firsts, starts[0]))
 
     rands = gather_step(rands, 0)
     first = run_place(sc, in_order(firsts))
@@ -818,76 +922,152 @@
     gain_two = both[:, :, 24, 24:48].reshape(1, WIDTH).astype(F32)
     rands = gather_step(rands, 1)
     v_own = run_values(sc, tokens.reshape(2, LMAX, WIDTH), gain_one, value)
-    rands, v_own, tokens_far = together((rands, v_own, other(pick(tokens, 1 - core, 2))))
+    rands, v_own = together((rands, v_own))
     rands, v_own, v_far = together((gather_step(rands, 2), v_own, other(v_own)))
-    rands, v_far, grad_far = together((gather_step(rands, 3), v_far, other(pick(grad_out, 1 - core, 2))))
-    near = [rands[k, y_at, x_at] for k in range(2) for y_at in range(2) for x_at in range(2)]
-    rands = gather_step(rands, 4)
-    mixing = run_mix(sc, (0, 1), near, v_own, v_far, ())
-    rands, mixing = together((rands, mixing))
-    shares = in_order(rands)
-    heads, mean = run_mix(sc, (2, 3), shares[8:], v_own, v_far, mixing)
+    rands, v_far, tokens_far = together((gather_step(rands, 3), v_far, other(pick(tokens, 1 - core, 2))))
+    rands, grad_far = together((gather_step(rands, 4), other(pick(grad_out, 1 - core, 2))))
+
+    shares = [in_order(rands), None]
+    half_one, half_two = (0, 1), (2, 3)
+    rands = gather_step(starts[1], 0)
+    mixing = run_mix(0, sc, half_one, shares[0][:8], v_own, v_far, ())
+    heads, mean_zero = run_mix(0, sc, half_two, shares[0][8:], v_own, v_far, mixing)
+    rands, heads, mean_zero = together((rands, heads, mean_zero))
 
     out = packed[:, :24].reshape(WIDTH, WIDTH)
     down = packed[:, 24:120].reshape(FF, WIDTH)
     up = packed[:, 120:].reshape(32, 4, 24, WIDTH).transpose(1, 0, 2, 3).reshape(4, WIDTH, WIDTH)
-    mixed, resid, normed, masked = run_pre(sc, tokens, tokens_far, grad_out, grad_far, heads, out, gain_two)
-    active, up_grad, back = run_units(sc, normed, masked, up, down)
-
-    d_down = run_down_grad(active, masked).reshape(32, 96, WIDTH)
-    d_up = run_up_grad(normed, up_grad).reshape(4, 32, 24, WIDTH).transpose(1, 0, 2, 3).reshape(32, 96, WIDTH)
-    packed, back = together((jnp.concatenate([d_down, d_up], axis=1), back))
-    packed = lax.psum_scatter(packed, BOTH, scatter_dimension=0)
-
-    res_own, res_far, grad_heads, d_out, d_gain_two = run_post(sc, resid, back, masked, mixed, out, gain_two)
-    *far, back_own, back_far = run_unmix(
-        sc, (3, 2), shares[12:] + shares[8:12], v_own, v_far, grad_heads, mean, ()
-    )
-    far, back_own, back_far, res_got = together((far, back_own, back_far, other(res_far)))
-    have, got = scatter_send(by_place(far, (3, 2)), 0)
-    *near, back_own, back_far = run_unmix(
-        sc, (1, 0), shares[4:8] + shares[:4], v_own, v_far, grad_heads, mean, (back_own, back_far)
+    rands = gather_step(rands, 1)
+    slabs = run_pre(0, sc, tokens, tokens_far, grad_out, grad_far, heads, out, gain_two, ())
+    rands, slabs, down, up = together((rands, slabs, down, up))
+
+    rands = gather_step(rands, 2)
+    mixed, resid, normed, masked = slabs
+    *acts, back = run_units(0, sc, normed, masked, up, down, ())
+    rands, acts, back = together((rands, acts, back))
+
+    rands = gather_step(rands, 3)
+    *res, grad_heads, gain_sum = run_post(0, sc, resid, back, masked, out, gain_two, ())
+    rands, res, grad_heads, gain_sum = together((rands, res, grad_heads, gain_sum))
+
+    rands = gather_step(rands, 4)
+    backward = lambda part, planes, share, grad, mean, carry, add: run_unmix(
+        part, sc, planes, share, v_own, v_far, grad, mean, carry, add
+    )
+    far_planes, near_planes = (3, 2), (1, 0)
+    *far, own_sum, far_sum = backward(
+        0, far_planes, shares[0][12:] + shares[0][8:12], grad_heads, mean_zero, (), ()
+    )
+    *near, own_sum, far_sum = backward(
+        0, near_planes, shares[0][4:8] + shares[0][:4], grad_heads, mean_zero, (own_sum, far_sum), ()
+    )
+    rands, far, near, own_sum, far_sum = together((rands, far, near, own_sum, far_sum))
+    shares[1] = in_order(rands)
+
+    have, got = scatter_send(by_place(near[4:] + near[:4] + far[4:] + far[:4]), 0)
+    mixing = run_mix(1, sc, half_one, shares[1][:8], v_own, v_far, ())
+    heads, mean_one = run_mix(1, sc, half_two, shares[1][8:], v_own, v_far, mixing)
+    have, got, heads, mean_one = together((have, got, heads, mean_one))
+    have = scatter_add(have, got, 0)
+
+    have, got = scatter_send(have, 1)
+    slabs = run_pre(1, sc, tokens, tokens_far, grad_out, grad_far, heads, out, gain_two, slabs)
+    have, got, slabs = together((have, got, slabs))
+    have = scatter_add(have, got, 1)
+
+    have, got = scatter_send(have, 2)
+    mixed, resid, normed, masked = slabs
+    *acts, back = run_units(1, sc, normed, masked, up, down, acts)
+    have, got, acts, back = together((have, got, acts, back))
+    have = scatter_add(have, got, 2)
+
+    have, got = scatter_send(have, 3)
+    *res, grad_heads, d_gain_two = run_post(1, sc, resid, back, masked, out, gain_two, res)
+    d_gain_two = d_gain_two + gain_sum
+    have, got, res, grad_heads, d_gain_two = together((have, got, res, grad_heads, d_gain_two))
+    have = scatter_add(have, got, 3)
+    active, up_grad = acts
+    res_own, res_far = res
+
+    have, got = scatter_send(have, 4)
+    sums_zero = (own_sum, far_sum)
+    *far, own_sum, far_sum = backward(
+        1, far_planes, shares[1][12:] + shares[1][8:12], grad_heads, mean_one, (), sums_zero
+    )
+    have, got, far, own_sum, far_sum, res_got = together((have, got, far, own_sum, far_sum, other(res_far)))
+    rand_sums = [scatter_add(have, got, 4)[0, 0, 0]]
+
+    have, got = scatter_send(by_place(far, far_planes), 0)
+    *near, back_own, back_far = backward(
+        1, near_planes, shares[1][4:8] + shares[1][:4], grad_heads, mean_one, (own_sum, far_sum), sums_zero
     )
     have, got, near, back_own, back_far = together((have, got, near, back_own, back_far))
-    have = {**scatter_add(have, got, 0), **by_place(near, (1, 0))}
+    have = {**scatter_add(have, got, 0), **by_place(near, near_planes)}
 
     have, got = scatter_send(have, 1)
+    up_own, up_far = run_up_grad(sc, normed, up_grad)
+    have, got, up_own, up_far, back_got = together((have, got, up_own, up_far, other(back_far)))
+    have = scatter_add(have, got, 1)
+
+    have, got = scatter_send(have, 2)
+    down_own, down_far = run_down_grad(sc, active, masked)
+    have, got, down_own, down_far, up_got = together((have, got, down_own, down_far, other(up_far)))
+    have = scatter_add(have, got, 2)
+
+    have, got = scatter_send(have, 3)
+    d_out_own, d_out_far = run_out_grad(sc, mixed, res_own, res_far)
+    have, got, d_out_own, d_out_got, down_got = together((have, got, d_out_own, other(d_out_far), other(down_far)))
+    have = scatter_add(have, got, 3)
+
+    have, got = scatter_send(have, 4)
+    grads = run_collect(sc, down_own, down_got, up_own, up_got, d_out_own, d_out_got)
+    have, got, grads = together((have, got, grads))
+    rand_sums.append(scatter_add(have, got, 4)[0, 0, 0])
+
+    sums, got = scatter_send(by_place(grads), 0)
     out_own, out_far = run_out(sc, active, resid, down)
-    have, got, out_own, out_far, back_got = together((have, got, out_own, out_far, other(back_far)))
-    have = scatter_add(have, got, 1)
-
-    have, got = scatter_send(have, 2)
+    rand_sum = jnp.stack([x.reshape(SUBS, HALF, LMAX) for x in rand_sums], 1).reshape(2, 3, HALF, LMAX)
+    blocks, blocks_far = pick(rand_sum, core), other(pick(rand_sum, 1 - core))
+    sums, got, out_own, out_far, blocks, blocks_far = together((sums, got, out_own, out_far, blocks, blocks_far))
+    sums = scatter_add(sums, got, 0)
+
+    sums, got = scatter_send(sums, 1)
     output, tokens_grad, d_value, d_gain_one = run_close(
         sc, tokens, res_own, res_got, out_own, other(out_far), back_own, back_got, gain_one, value
     )
     gain_pair = jnp.concatenate([d_gain_one, d_gain_two]).reshape(2, 16, 1, 48).astype(BF16)
     gain_pair = jnp.pad(gain_pair, ((0, 0), (0, 0), (0, 15), (0, SIDE - 48)))
-    small = jnp.concatenate([d_value.reshape(2, 16, 48, SIDE), d_out.reshape(2, 16, 48, SIDE), gain_pair], 2)
-    have, got, small, output, tokens_grad = together((have, got, small, output, tokens_grad))
-    have = scatter_add(have, got, 2)
-
-    have, got = scatter_send(have, 3)
-    small = add_low(pick(small, core), other(pick(small, 1 - core))).reshape(4, 2, 2, 112, SIDE)
+    small = jnp.concatenate([d_value.reshape(2, 16, 48, SIDE), gain_pair], 2)
+    sums, got, small, output, tokens_grad = together((sums, got, small, output, tokens_grad))
+    sums = scatter_add(sums, got, 1)
+
+    sums, got = scatter_send(sums, 2)
+    small = add_low(pick(small, core), other(pick(small, 1 - core))).reshape(4, 2, 2, 64, SIDE)
     small = add_low(pick(small, x, 2), swap(pick(small, 1 - x, 2), TO_X))
-    have, got, small = together((have, got, small))
-    have = scatter_add(have, got, 3)
-
-    have, got = scatter_send(have, 4)
+    sums, got, small = together((sums, got, small))
+    sums = scatter_add(sums, got, 2)
+
+    sums, got = scatter_send(sums, 3)
     small = add_low(pick(small, y, 1), swap(pick(small, 1 - y, 1), TO_Y))
+    sums, got, small = together((sums, got, small))
+    sums = scatter_add(sums, got, 3)
+
+    sums, got = scatter_send(sums, 4)
     small_sum = pick(small, z).astype(F32)
     for k in range(1, PLANES):
         small_sum = small_sum + ring(pick(small, lax.rem(z + PLANES - k, PLANES)), -k).astype(F32)
-    have, got, small_sum = together((have, got, small_sum))
-    rand_sum = scatter_add(have, got, 4)[0, 0, 0].reshape(2, 3, HALF, LMAX)
-    blocks, blocks_far = pick(rand_sum, core), other(pick(rand_sum, 1 - core))
-    small_far = other(small_sum)
-
-    rows_of = lambda value: pick(value.reshape(2, 24, SIDE), core)
-    value_shard = side(rows_of(small_sum[:48]), rows_of(small_far[:48]), 1)
-    outproj_shard = side(rows_of(small_sum[48:96]), rows_of(small_far[48:96]), 1)
-    down_shard = packed[:96].astype(F32)
-    up_shard = packed[96:].reshape(4, 24, WIDTH).transpose(1, 0, 2).reshape(24, FF).astype(F32)
-    gains_pair = ordered(core, small_sum[96, :48], small_far[96, :48])
+    sums, got, small_sum = together((sums, got, small_sum))
+    big_sum = scatter_add(sums, got, 4)[0, 0, 0]
+    big_far, small_far = other(big_sum), other(small_sum)
+
+    rows_of = lambda value, rows: pick(value.reshape(-1, 2, rows, SIDE), core, 1)
+    mine = lambda own, far, rows: side(rows_of(own, rows)[0], rows_of(far, rows)[0], 1)
+    down_shard = mine(big_sum[PACK_DOWN:PACK_UP], big_far[PACK_DOWN:PACK_UP], 96)
+    up_side = lambda value: rows_of(value[PACK_UP:PACK_OUT], 24).transpose(1, 0, 2).reshape(24, 4 * SIDE)
+    up_shard = side(up_side(big_sum), up_side(big_far), 1)
+    outproj_shard = mine(big_sum[PACK_OUT:], big_far[PACK_OUT:], 24)
+    value_shard = mine(small_sum[:48], small_far[:48], 24)
+    gains_pair = ordered(core, small_sum[48, :48], small_far[48, :48])
     gain_pair = pick(gains_pair.reshape(2, 2, 24), core, 1)
 
     rand_shard = ordered(core, blocks, blocks_far, 1)

time: 538 us -> 586 us (1.089)
  Pallas kernels: 217 us -> 284 us
  waiting for transfers between devices: 192 us -> 128 us
  starting transfers between devices: 52.7 us -> 98.7 us
    pallas_call x13 -> x31, Pallas kernels: 130 us -> 195 us  [the longest x4 50.8 us: run_unmix(): pl.pallas_call(partial(unmix_kernel, part, bool(carry), bool(add)), grid_...]
    ppermute x18 -> x33, waiting for transfers between devices: 97.1 us -> 57.9 us  [ring(): lax.ppermute(x, BOTH, [(d, (d + 8 * way) % DEVICES) for d in range(DEVICE...]
    ppermute x44 -> x78, starting transfers between devices: 34.1 us -> 65.1 us  [swap(): return lax.ppermute(x, BOTH, [(d, d ^ bit) for d in range(DEVICES)])]
    ppermute x44 -> x78, waiting for transfers between devices: 94.5 us -> 70.1 us  [swap(): return lax.ppermute(x, BOTH, [(d, d ^ bit) for d in range(DEVICES)])]
    ppermute x18 -> x33, starting transfers between devices: 18.6 us -> 33.6 us  [ring(): lax.ppermute(x, BOTH, [(d, (d + 8 * way) % DEVICES) for d in range(DEVICE...]
    unnamed x93 -> x206, local copies, waits for them, and re-layouts: 10.7 us -> 13 us
    pallas_call x1 -> x2, Pallas kernels: 45 us -> 47.1 us  [run_units(): pl.pallas_call(units_kernel, grid_spec=pltpu.PrefetchScalarGridSpec(num_s...]
  transfers between devices with their start and end apart: 64 -> 112, of which waited for: 33 -> 40; matrix products, arithmetic and copies ran while one was open for 4% -> 5% of each run, Pallas kernels for 21% -> 48%
where the time goes in v9:
time: 586 us; the launch traced here: 576 us
  Pallas kernels  284 us (48%)
  waiting for transfers between devices  128 us (22%)
  starting transfers between devices  98.7 us (17%)
  local copies, waits for them, and re-layouts  35.7 us (6%)
  between operations  16.1 us (3%)
  other arithmetic  13 us (2%)
    ppermute x78, waiting for transfers between devices, swap(): return lax.ppermute(x, BOTH, [(d, d ^ bit) for d in range(DEVICES)])  70.1 us
    ppermute x78, starting transfers between devices, swap(): return lax.ppermute(x, BOTH, [(d, d ^ bit) for d in range(DEVICES)])  65.1 us
    ppermute x33, waiting for transfers between devices, ring(): lax.ppermute(x, BOTH, [(d, (d + 8 * way) % DEVICES) for d in range(DEVICE...  57.9 us
    pallas_call x4, Pallas kernels, run_unmix(): pl.pallas_call(partial(unmix_kernel, part, bool(carry), bool(add)), grid_...  50.8 us
    pallas_call x2, Pallas kernels, run_units(): pl.pallas_call(units_kernel, grid_spec=pltpu.PrefetchScalarGridSpec(num_s...  47.1 us
    pallas_call x15, Pallas kernels, run_add(): pl.pallas_call(partial(add_kernel, groups), grid=(1,), in_specs=[block] *...  37.3 us
    ppermute x33, starting transfers between devices, ring(): lax.ppermute(x, BOTH, [(d, (d + 8 * way) % DEVICES) for d in range(DEVICE...  33.6 us
    pallas_call x4, Pallas kernels, run_mix(): pl.pallas_call(partial(mix_kernel, part, bool(carry)), grid_spec=pltpu.Pr...  27.4 us
  transfers between devices with their start and end apart: 112, of which 40 were waited for; matrix products, arithmetic and copies ran while one was open for 5% of the time, Pallas kernels for 48%

profile of v9, /device:TPU:0, one launch (start us, length us, event | category | flops | bytes accessed | tf_op | source)
XLA Modules:
  0.0 575.7 jit_solution(2073847399628497639)
XLA Ops:
  61.5 9.2 %collective-permute-done.20.refs_1_.refs_5_ = bf16[192,1024]{1,0:T(8,128)(2,1)S(1)} collective-permute-done((bf16[192,1024]{1,0:T(8,128)(2,1)S(1)}, bf16[192,1024]{1,0:T(8,128)(2,1)S(1)}, u32[]{:S(2)}, u32[]{:S(2)}) %collective-permute-start.20) | collective-permute-done | bytes 393248 | tf_op jit(solution)/shard_map/ppermute | solution.py:829
  81.6 7.8 %values.1.refs_8_ = bf16[12,1024,128]{2,1,0:T(8,128)(2,1)} custom-call(s32[7]{0:T(128)} %concatenate.55.sc, bf16[2,1024,768]{2,1,0:T(8,128)(2,1)} %tok.1, f32[1,768]{1,0:T(1,128)} %reshape.244.gain, bf16[768,768]{1,0:T(8,128)(2,1)} %bitcast.184), custom_call_target="tpu_custom_call" | custom-call | flops 2415919104 | bytes 6291456 | tf_op jit(solution)/shard_map/values/pallas_call | solution.py:72
  103.6 7.6 %collective-permute-done.27.refs_6_.refs_2_ = bf16[192,1024]{1,0:T(8,128)(2,1)S(1)} collective-permute-done((bf16[192,1024]{1,0:T(8,128)(2,1)}, bf16[192,1024]{1,0:T(8,128)(2,1)S(1)}, u32[]{:S(2)}, u32[]{:S(2)}) %collective-permute-start.27) | collective-permute-done | bytes 393248 | tf_op jit(solution)/shard_map/ppermute | solution.py:829
  113.3 11.0 %collective-permute-done.29.refs_4_.refs_0_ = bf16[192,1024]{1,0:T(8,128)(2,1)S(1)} collective-permute-done((bf16[192,1024]{1,0:T(8,128)(2,1)S(1)}, bf16[192,1024]{1,0:T(8,128)(2,1)S(1)}, u32[]{:S(2)}, u32[]{:S(2)}) %collective-permute-start.29) | collective-permute-done | bytes 393248 | tf_op jit(solution)/shard_map/ppermute | solution.py:833
  126.8 9.1 %collective-permute-done.31.refs_7_.refs_3_ = bf16[192,1024]{1,0:T(8,128)(2,1)S(1)} collective-permute-done((bf16[192,1024]{1,0:T(8,128)(2,1)}, bf16[192,1024]{1,0:T(8,128)(2,1)S(1)}, u32[]{:S(2)}, u32[]{:S(2)}) %collective-permute-start.31) | collective-permute-done | bytes 393248 | tf_op jit(solution)/shard_map/ppermute | solution.py:833
  140.0 8.0 %collective-permute-done.35.refs_3_.refs_7_ = bf16[192,1024]{1,0:T(8,128)(2,1)S(1)} collective-permute-done((bf16[192,1024]{1,0:T(8,128)(2,1)S(1)}, bf16[192,1024]{1,0:T(8,128)(2,1)S(1)}, u32[]{:S(2)}, u32[]{:S(2)}) %collective-permute-start.35) | collective-permute-done | bytes 393248 | tf_op jit(solution)/shard_map/ppermute | solution.py:829
  177.3 7.6 %pre.2 = (bf16[2,4,256,768]{3,2,1,0:T(8,128)(2,1)}, bf16[2,4,256,768]{3,2,1,0:T(8,128)(2,1)}, bf16[2,4,256,768]{3,2,1,0:T(8,128)(2,1)}, bf16[2,4,256,768]{3,2,1,0:T(8,128)(2,1)}) custom-call(s32[7]{0:T(128)} %concatenate.55.sc, bf16[2,4,2,2,64,768]{5,4,3,2,1,0:T(8,128)(2,1)} %bitcast.144, bf16[2,4,2,64,768]{4,3,2,1,0:T(8,128)(2,1)} %bitcast.153, ...), custom_call_target="tpu_custom_call" | custom-call | flops 1207959552 | bytes 12582912 | tf_op jit(solution)/shard_map/pre/pallas_call | solution.py:255
  189.6 23.6 %units.2 = (bf16[2048,3072]{1,0:T(8,128)(2,1)}, bf16[2048,3072]{1,0:T(8,128)(2,1)}, bf16[1024,768]{1,0:T(8,128)(2,1)}) custom-call(s32[7]{0:T(128)} %concatenate.55.sc, bf16[2048,768]{1,0:T(8,128)(2,1)} %bitcast.177, bf16[2048,768]{1,0:T(8,128)(2,1)} %bitcast.137, bf16[4,768,768]{2,1,0:T(8,128)(2,1)} %bitcast.155, bf16[3072,768]{1,0:T(8,128)(2,1)} %bitcast.157), custom_call_target="tpu_custom_call" | custom-call | flops 14495514624 | bytes 18874368 | tf_op jit(solution)/shard_map/units/pallas_call | solution.py:314
  216.9 8.2 %post.2 = (bf16[2,2,256,768]{3,2,1,0:T(8,128)(2,1)}, bf16[2,2,256,768]{3,2,1,0:T(8,128)(2,1)}, bf16[12,256,256]{2,1,0:T(8,128)(2,1)}, f32[1,768]{1,0:T(1,128)}) custom-call(s32[7]{0:T(128)} %concatenate.55.sc, bf16[2,4,256,768]{3,2,1,0:T(8,128)(2,1)} %get-tuple-element.721.resid.refs_1_, bf16[1,4,256,768]{3,2,1,0:T(8,128)(2,1)} %bitcast.183, ...), custom_call_target="tpu_custom_call" | custom-call | flops 1207959552 | bytes 9437184 | tf_op jit(solution)/shard_map/post/pallas_call | solution.py:514
  230.5 12.3 %unmix.4 = (bf16[192,1024]{1,0:T(8,128)(2,1)}, bf16[192,1024]{1,0:T(8,128)(2,1)}, bf16[192,1024]{1,0:T(8,128)(2,1)}, bf16[192,1024]{1,0:T(8,128)(2,1)}, bf16[192...) custom-call(s32[7]{0:T(128)} %concatenate.55.sc, ...), custom_call_target="tpu_custom_call" | custom-call | flops 2415919104 | bytes 22020096 | tf_op jit(solution)/shard_map/unmix/pallas_call | solution.py:605
  242.9 12.4 %unmix.5 = (bf16[192,1024]{1,0:T(8,128)(2,1)}, bf16[192,1024]{1,0:T(8,128)(2,1)}, bf16[192,1024]{1,0:T(8,128)(2,1)}, bf16[192,1024]{1,0:T(8,128)(2,1)}, bf16[192...) custom-call(s32[7]{0:T(128)} %concatenate.55.sc, ...), custom_call_target="tpu_custom_call", output_to_operand_aliasing={{8}: (13, {}), {9}: (14, {})} | custom-call | flops 2415919104 | bytes 22020096 | tf_op jit(solution)/shard_map/unmix/pallas_call | solution.py:605
  266.5 6.9 %mix.7 = (bf16[12,256,256]{2,1,0:T(8,128)(2,1)}, f32[12,256,256]{2,1,0:T(8,128)}) custom-call(s32[7]{0:T(128)} %concatenate.55.sc, bf16[192,1024]{1,0:T(8,128)(2,1)} %copy-done.19, bf16[192,1024]{1,0:T(8,128)(2,1)} %copy-done.21, bf16[192,1024]{1,0:T(8,128)(2,1)} %copy-done.25, ...), custom_call_target="tpu_custom_call", output_to_operand_aliasing={{0}: (11, {}), {1}: (12, {})} | custom-call | flops 1610612736 | bytes 7077888 | tf_op jit(solution)/shard_map/mix/pallas_call | solution.py:178
  279.3 7.5 %pre.3 = (bf16[2,4,256,768]{3,2,1,0:T(8,128)(2,1)}, bf16[2,4,256,768]{3,2,1,0:T(8,128)(2,1)}, bf16[2,4,256,768]{3,2,1,0:T(8,128)(2,1)}, bf16[2,4,256,768]{3,2,1,0:T(8,128)(2,1)}) custom-call(s32[7]{0:T(128)} %concatenate.55.sc, bf16[2,4,2,2,64,768]{5,4,3,2,1,0:T(8,128)(2,1)} %bitcast.145, ...), custom_call_target="tpu_custom_call", output_to_operand_aliasing={{0}: (8, {}), {1}: (9, {}), {2}: (10, {}), {3}: (11, {})} | custom-call | flops 1207959552 | bytes 12582912 | tf_op jit(solution)/shard_map/pre/pallas_call | solution.py:255
  295.9 23.5 %units.3 = (bf16[2048,3072]{1,0:T(8,128)(2,1)}, bf16[2048,3072]{1,0:T(8,128)(2,1)}, bf16[1024,768]{1,0:T(8,128)(2,1)}) custom-call(s32[7]{0:T(128)} %concatenate.55.sc, bf16[2048,768]{1,0:T(8,128)(2,1)} %bitcast.178, bf16[2048,768]{1,0:T(8,128)(2,1)} %bitcast.138, bf16[4,768,768]{2,1,0:T(8,128)(2,1)} %bitcast.156, ...), custom_call_target="tpu_custom_call", output_to_operand_aliasing={{0}: (5, {}), {1}: (6, {})} | custom-call | flops 14495514624 | bytes 18874368 | tf_op jit(solution)/shard_map/units/pallas_call | solution.py:314
  326.1 8.4 %post.3 = (bf16[2,2,256,768]{3,2,1,0:T(8,128)(2,1)}, bf16[2,2,256,768]{3,2,1,0:T(8,128)(2,1)}, bf16[12,256,256]{2,1,0:T(8,128)(2,1)}, f32[1,768]{1,0:T(1,128)}) custom-call(s32[7]{0:T(128)} %concatenate.55.sc, bf16[2,4,256,768]{3,2,1,0:T(8,128)(2,1)} %get-tuple-element.857.resid, ...), custom_call_target="tpu_custom_call", output_to_operand_aliasing={{0}: (6, {}), {1}: (7, {})} | custom-call | flops 1207959552 | bytes 9437184 | tf_op jit(solution)/shard_map/post/pallas_call | solution.py:514
  342.8 13.1 %unmix.6 = (bf16[192,1024]{1,0:T(8,128)(2,1)}, bf16[192,1024]{1,0:T(8,128)(2,1)}, bf16[192,1024]{1,0:T(8,128)(2,1)}, bf16[192,1024]{1,0:T(8,128)(2,1)}, bf16[192...) custom-call(s32[7]{0:T(128)} %concatenate.55.sc, ...), custom_call_target="tpu_custom_call" | custom-call | flops 2415919104 | bytes 22020096 | tf_op jit(solution)/shard_map/unmix/pallas_call | solution.py:605
  358.9 13.1 %unmix.7 = (bf16[192,1024]{1,0:T(8,128)(2,1)}, bf16[192,1024]{1,0:T(8,128)(2,1)}, bf16[192,1024]{1,0:T(8,128)(2,1)}, bf16[192,1024]{1,0:T(8,128)(2,1)}, bf16[192...) custom-call(s32[7]{0:T(128)} %concatenate.55.sc, ...), custom_call_target="tpu_custom_call", output_to_operand_aliasing={{8}: (13, {}), {9}: (14, {})} | custom-call | flops 2415919104 | bytes 22020096 | tf_op jit(solution)/shard_map/unmix/pallas_call | solution.py:605
  378.1 16.3 %up_grad.1 = (bf16[768,1536]{1,0:T(8,128)(2,1)}, bf16[768,1536]{1,0:T(8,128)(2,1)}) custom-call(s32[7]{0:T(128)} %concatenate.55.sc, bf16[2048,768]{1,0:T(8,128)(2,1)} %bitcast.179, bf16[2048,3072]{1,0:T(8,128)(2,1)} %get-tuple-element.928.up_grad), custom_call_target="tpu_custom_call" | custom-call | flops 9663676416 | bytes 15728640 | tf_op jit(solution)/shard_map/up_grad/pallas_call | solution.py:391
  401.2 15.6 %down_grad.1 = (bf16[3072,384]{1,0:T(8,128)(2,1)}, bf16[3072,384]{1,0:T(8,128)(2,1)}) custom-call(s32[7]{0:T(128)} %concatenate.55.sc, bf16[2048,3072]{1,0:T(8,128)(2,1)} %get-tuple-element.948.active, bf16[2048,768]{1,0:T(8,128)(2,1)} %bitcast.139), custom_call_target="tpu_custom_call" | custom-call | flops 9663676416 | bytes 15728640 | tf_op jit(solution)/shard_map/down_grad/pallas_call | solution.py:359
  416.9 7.0 %out_grad.1 = (bf16[768,384]{1,0:T(8,128)(2,1)}, bf16[768,384]{1,0:T(8,128)(2,1)}) custom-call(s32[7]{0:T(128)} %concatenate.55.sc, bf16[2,4,256,768]{3,2,1,0:T(8,128)(2,1)} %get-tuple-element.964.mixed, bf16[2,2,256,768]{3,2,1,0:T(8,128)(2,1)} %get-tuple-element.965.res_own, bf16[2,2,256,768]{3,2,1,0:T(8,128)(2,1)} %get-tuple-element.889.res_far), custom_call_target="tpu_custom_call" | custom-call | flops 2415919104 | bytes 6291456 | tf_op jit(solution)/shard_map/out_grad/pallas_call | solution.py:432
  431.0 7.4 %collective-permute-done.78.refs_0_ = bf16[192,1024]{1,0:T(8,128)(2,1)S(1)} collective-permute-done((bf16[192,1024]{1,0:T(8,128)(2,1)}, bf16[192,1024]{1,0:T(8,128)(2,1)S(1)}, u32[]{:S(2)}, u32[]{:S(2)}) %collective-permute-start.78) | collective-permute-done | bytes 393248 | tf_op jit(solution)/shard_map/ppermute | solution.py:833
  450.4 8.6 %collect.1 = (bf16[432,384]{1,0:T(8,128)(2,1)}, bf16[432,384]{1,0:T(8,128)(2,1)}, bf16[432,384]{1,0:T(8,128)(2,1)}, bf16[432,384]{1,0:T(8,128)(2,1)}, bf16[432,3...) custom-call(s32[7]{0:T(128)} %concatenate.55.sc, ...), custom_call_target="tpu_custom_call" | custom-call | bytes 15925248 | tf_op jit(solution)/shard_map/collect/pallas_call | solution.py:784
  465.4 16.1 %out.1 = (bf16[2,2,256,768]{3,2,1,0:T(8,128)(2,1)}, bf16[2,2,256,768]{3,2,1,0:T(8,128)(2,1)}) custom-call(s32[7]{0:T(128)} %concatenate.55.sc, bf16[2,4,256,3072]{3,2,1,0:T(8,128)(2,1)} %bitcast.199, bf16[2,4,256,768]{3,2,1,0:T(8,128)(2,1)} %get-tuple-element.857.resid, bf16[3072,768]{1,0:T(8,128)(2,1)} %bitcast.159), custom_call_target="tpu_custom_call" | custom-call | flops 9663676416 | bytes 23592960 | tf_op jit(solution)/shard_map/out/pallas_call | solution.py:461
  487.8 15.6 %close.1 = (f32[2,8,2,64,768]{4,3,2,1,0:T(8,128)}, f32[2,8,2,64,768]{4,3,2,1,0:T(8,128)}, bf16[2,768,384]{2,1,0:T(8,128)(2,1)}, f32[1,768]{1,0:T(1,128)}) custom-call(s32[7]{0:T(128)} %concatenate.55.sc, bf16[2,8,2,64,768]{4,3,2,1,0:T(8,128)(2,1)} %bitcast.146, bf16[2,2,4,64,768]{4,3,2,1,0:T(8,128)(2,1)} %bitcast.181, ...), custom_call_target="tpu_custom_call" | custom-call | flops 4831838208 | bytes 29884416 | tf_op jit(solution)/shard_map/close/pallas_call | solution.py:695
  (501 shorter events, 283.7 us)
Async XLA Ops:
  7.2 158.6 %all-gather.3.cloned.1.call-start = ((), (), s32[]{:S(2)}) async-start(), calls=%async_computation | async-start | bytes 10948608 | tf_op jit(solution)/shard_map/all_gather | solution.py:903
  76.6 21.1 %collective-permute-start.26 = (bf16[192,1024]{1,0:T(8,128)(2,1)}, bf16[192,1024]{1,0:T(8,128)(2,1)S(1)}, u32[]{:S(2)}, u32[]{:S(2)}) collective-permute-start(bf16[192,1024]{1,0:T(8,128)(2,1)} %collective-permute-done.22.refs_4_.refs_0_), channel_id=1, source_target_pairs={{0,8},{1,9},{2,10},{3,11},{4,12},{5,13},{6,14},{7,15},{8,16},{9,17... | collective-permute-start | bytes 1179656 | tf_op jit(solution)/shard_map/ppermute | solution.py:833
  97.6 26.6 %collective-permute-start.30 = (bf16[12,1024,128]{2,1,0:T(8,128)(2,1)}, bf16[12,1024,128]{2,1,0:T(8,128)(2,1)}, u32[]{:S(2)}, u32[]{:S(2)}) collective-permute-start(bf16[12,1024,128]{2,1,0:T(8,128)(2,1)} %values.1.refs_8_), channel_id=1, source_target_pairs={{0,1},{1,0},{2,3},{3,2},{4,5},{5,4},{6,7},{7,6},{8,9},{9,8},{10,11... | collective-permute-start | bytes 9437192 | tf_op jit(solution)/shard_map/ppermute | solution.py:829
  99.4 27.4 %collective-permute-start.34 = (bf16[2,8,64,768]{3,2,1,0:T(8,128)(2,1)S(1)}, bf16[2,8,64,768]{3,2,1,0:T(8,128)(2,1)S(1)}, u32[]{:S(2)}, u32[]{:S(2)}) collective-permute-start(bf16[2,8,64,768]{3,2,1,0:T(8,128)(2,1)S(1)} %dynamic-slice_bitcast_fusion.1), channel_id=1, source_target_pairs={{0,1},{1,0},{2,3},{3,2},{4,5},{5,4},{6,7},{7,6},{8,9},{9,8},{10,11... | collective-permute-start | bytes 4718600 | tf_op jit(solution)/shard_map/ppermute | solution.py:829
  101.4 37.2 %collective-permute-start.38 = (bf16[2,8,64,768]{3,2,1,0:T(8,128)(2,1)S(1)}, bf16[2,8,64,768]{3,2,1,0:T(8,128)(2,1)}, u32[]{:S(2)}, u32[]{:S(2)}) collective-permute-start(bf16[2,8,64,768]{3,2,1,0:T(8,128)(2,1)S(1)} %dynamic-slice_bitcast_fusion), channel_id=1, source_target_pairs={{0,1},{1,0},{2,3},{3,2},{4,5},{5,4},{6,7},{7,6},{8,9},{9,8},{10,11... | collective-permute-start | bytes 4718600 | tf_op jit(solution)/shard_map/ppermute | solution.py:829
  138.2 24.8 %collective-permute-start.5 = (bf16[192,1024]{1,0:T(8,128)(2,1)S(1)}, bf16[192,1024]{1,0:T(8,128)(2,1)}, u32[]{:S(2)}, u32[]{:S(2)}) collective-permute-start(bf16[192,1024]{1,0:T(8,128)(2,1)S(1)} %bitcast.160), channel_id=1, source_target_pairs={{0,2},{1,3},{2,0},{3,1},{4,6},{5,7},{6,4},{7,5},{8,10},{9,11},{10,... | collective-permute-start | bytes 1179656 | tf_op jit(solution)/shard_map/ppermute | solution.py:829
  138.6 24.4 %collective-permute-start.6 = (bf16[192,1024]{1,0:T(8,128)(2,1)S(1)}, bf16[192,1024]{1,0:T(8,128)(2,1)}, u32[]{:S(2)}, u32[]{:S(2)}) collective-permute-start(bf16[192,1024]{1,0:T(8,128)(2,1)S(1)} %bitcast.161), channel_id=1, source_target_pairs={{0,4},{1,5},{2,6},{3,7},{4,0},{5,1},{6,2},{7,3},{8,12},{9,13},{10,... | collective-permute-start | bytes 1179656 | tf_op jit(solution)/shard_map/ppermute | solution.py:829
  163.0 21.9 %collective-permute-start.40 = (bf16[192,1024]{1,0:T(8,128)(2,1)}, bf16[192,1024]{1,0:T(8,128)(2,1)S(1)}, u32[]{:S(2)}, u32[]{:S(2)}) collective-permute-start(bf16[192,1024]{1,0:T(8,128)(2,1)} %collective-permute-done.7.refs_4_.refs_0_), channel_id=1, source_target_pairs={{0,2},{1,3},{2,0},{3,1},{4,6},{5,7},{6,4},{7,5},{8,10},{9,11},{10,... | collective-permute-start | bytes 1179656 | tf_op jit(solution)/shard_map/ppermute | solution.py:829
  184.9 28.3 %collective-permute-start.43 = (bf16[192,1024]{1,0:T(8,128)(2,1)S(1)}, bf16[192,1024]{1,0:T(8,128)(2,1)S(1)}, u32[]{:S(2)}, u32[]{:S(2)}) collective-permute-start(bf16[192,1024]{1,0:T(8,128)(2,1)S(1)} %collective-permute-done.41.refs_0_.refs_4_), channel_id=1, source_target_pairs={{0,2},{1,3},{2,0},{3,1},{4,6},{5,7},{6,4},{7,5},{8,10},{9,11},{10,... | collective-permute-start | bytes 1179656 | tf_op jit(solution)/shard_map/ppermute | solution.py:829
  186.3 26.9 %collective-permute-start.44 = (bf16[192,1024]{1,0:T(8,128)(2,1)S(1)}, bf16[192,1024]{1,0:T(8,128)(2,1)S(1)}, u32[]{:S(2)}, u32[]{:S(2)}) collective-permute-start(bf16[192,1024]{1,0:T(8,128)(2,1)S(1)} %collective-permute-done.41.refs_0_.refs_4_), channel_id=1, source_target_pairs={{0,8},{1,9},{2,10},{3,11},{4,12},{5,13},{6,14},{7,15},{8,16},{9,17... | collective-permute-start | bytes 1179656 | tf_op jit(solution)/shard_map/ppermute | solution.py:833
  188.5 24.8 %collective-permute-start.42 = (bf16[192,1024]{1,0:T(8,128)(2,1)}, bf16[192,1024]{1,0:T(8,128)(2,1)S(1)}, u32[]{:S(2)}, u32[]{:S(2)}) collective-permute-start(bf16[192,1024]{1,0:T(8,128)(2,1)} %collective-permute-done.7.refs_4_.refs_0_), channel_id=1, source_target_pairs={{0,4},{1,5},{2,6},{3,7},{4,0},{5,1},{6,2},{7,3},{8,12},{9,13},{10,... | collective-permute-start | bytes 1179656 | tf_op jit(solution)/shard_map/ppermute | solution.py:829
  226.6 28.7 %collective-permute-start.48 = (bf16[192,1024]{1,0:T(8,128)(2,1)S(1)}, bf16[192,1024]{1,0:T(8,128)(2,1)S(1)}, u32[]{:S(2)}, u32[]{:S(2)}) collective-permute-start(bf16[192,1024]{1,0:T(8,128)(2,1)S(1)} %collective-permute-done.46.refs_2_.refs_6_), channel_id=1, source_target_pairs={{0,2},{1,3},{2,0},{3,1},{4,6},{5,7},{6,4},{7,5},{8,10},{9,11},{10,... | collective-permute-start | bytes 1179656 | tf_op jit(solution)/shard_map/ppermute | solution.py:829
  227.3 27.9 %collective-permute-start.49 = (bf16[192,1024]{1,0:T(8,128)(2,1)S(1)}, bf16[192,1024]{1,0:T(8,128)(2,1)S(1)}, u32[]{:S(2)}, u32[]{:S(2)}) collective-permute-start(bf16[192,1024]{1,0:T(8,128)(2,1)S(1)} %collective-permute-done.46.refs_2_.refs_6_), channel_id=1, source_target_pairs={{0,8},{1,9},{2,10},{3,11},{4,12},{5,13},{6,14},{7,15},{8,16},{9,17... | collective-permute-start | bytes 1179656 | tf_op jit(solution)/shard_map/ppermute | solution.py:833
  229.3 25.9 %collective-permute-start.50 = (bf16[192,1024]{1,0:T(8,128)(2,1)}, bf16[192,1024]{1,0:T(8,128)(2,1)S(1)}, u32[]{:S(2)}, u32[]{:S(2)}) collective-permute-start(bf16[192,1024]{1,0:T(8,128)(2,1)} %collective-permute-done.47.refs_5_.refs_1_), channel_id=1, source_target_pairs={{0,4},{1,5},{2,6},{3,7},{4,0},{5,1},{6,2},{7,3},{8,12},{9,13},{10,... | collective-permute-start | bytes 1179656 | tf_op jit(solution)/shard_map/ppermute | solution.py:829
  292.5 27.0 %collective-permute-start.57 = (bf16[192,1024]{1,0:T(8,128)(2,1)}, bf16[192,1024]{1,0:T(8,128)(2,1)S(1)}, u32[]{:S(2)}, u32[]{:S(2)}) collective-permute-start(bf16[192,1024]{1,0:T(8,128)(2,1)} %get-tuple-element.835), channel_id=1, source_target_pairs={{0,24},{1,25},{2,26},{3,27},{4,28},{5,29},{6,30},{7,31},{8,0},{9,1... | collective-permute-start | bytes 1179656 | tf_op jit(solution)/shard_map/ppermute | solution.py:833
  293.9 25.6 %collective-permute-start.58 = (bf16[192,1024]{1,0:T(8,128)(2,1)S(1)}, bf16[192,1024]{1,0:T(8,128)(2,1)S(1)}, u32[]{:S(2)}, u32[]{:S(2)}) collective-permute-start(bf16[192,1024]{1,0:T(8,128)(2,1)S(1)} %copy-done.94), channel_id=1, source_target_pairs={{0,2},{1,3},{2,0},{3,1},{4,6},{5,7},{6,4},{7,5},{8,10},{9,11},{10,... | collective-permute-start | bytes 1179656 | tf_op jit(solution)/shard_map/ppermute | solution.py:829
  294.7 24.8 %collective-permute-start.59 = (bf16[192,1024]{1,0:T(8,128)(2,1)S(1)}, bf16[192,1024]{1,0:T(8,128)(2,1)S(1)}, u32[]{:S(2)}, u32[]{:S(2)}) collective-permute-start(bf16[192,1024]{1,0:T(8,128)(2,1)S(1)} %copy-done.95), channel_id=1, source_target_pairs={{0,4},{1,5},{2,6},{3,7},{4,0},{5,1},{6,2},{7,3},{8,12},{9,13},{10,... | collective-permute-start | bytes 1179656 | tf_op jit(solution)/shard_map/ppermute | solution.py:829
  372.1 22.3 %collective-permute-start.73 = (bf16[12,1024,128]{2,1,0:T(8,128)(2,1)}, bf16[12,1024,128]{2,1,0:T(8,128)(2,1)}, u32[]{:S(2)}, u32[]{:S(2)}) collective-permute-start(bf16[12,1024,128]{2,1,0:T(8,128)(2,1)} %get-tuple-element.931), channel_id=1, source_target_pairs={{0,1},{1,0},{2,3},{3,2},{4,5},{5,4},{6,7},{7,6},{8,9},{9,8},{10,11... | collective-permute-start | bytes 9437192 | tf_op jit(solution)/shard_map/ppermute | solution.py:829
  372.2 22.1 %collective-permute-start.70 = (bf16[192,1024]{1,0:T(8,128)(2,1)}, bf16[192,1024]{1,0:T(8,128)(2,1)S(1)}, u32[]{:S(2)}, u32[]{:S(2)}) collective-permute-start(bf16[192,1024]{1,0:T(8,128)(2,1)} %get-tuple-element.920), channel_id=1, source_target_pairs={{0,24},{1,25},{2,26},{3,27},{4,28},{5,29},{6,30},{7,31},{8,0},{9,1... | collective-permute-start | bytes 1179656 | tf_op jit(solution)/shard_map/ppermute | solution.py:833
  395.3 21.6 %collective-permute-start.77 = (bf16[768,1536]{1,0:T(8,128)(2,1)}, bf16[768,1536]{1,0:T(8,128)(2,1)S(1)}, u32[]{:S(2)}, u32[]{:S(2)}) collective-permute-start(bf16[768,1536]{1,0:T(8,128)(2,1)} %get-tuple-element.951), channel_id=1, source_target_pairs={{0,1},{1,0},{2,3},{3,2},{4,5},{5,4},{6,7},{7,6},{8,9},{9,8},{10,11... | collective-permute-start | bytes 7077896 | tf_op jit(solution)/shard_map/ppermute | solution.py:829
  416.9 24.6 %collective-permute-start.82 = (bf16[3072,384]{1,0:T(8,128)(2,1)}, bf16[3072,384]{1,0:T(8,128)(2,1)}, u32[]{:S(2)}, u32[]{:S(2)}) collective-permute-start(bf16[3072,384]{1,0:T(8,128)(2,1)} %get-tuple-element.968), channel_id=1, source_target_pairs={{0,1},{1,0},{2,3},{3,2},{4,5},{5,4},{6,7},{7,6},{8,9},{9,8},{10,11... | collective-permute-start | bytes 7077896 | tf_op jit(solution)/shard_map/ppermute | solution.py:829
  459.1 22.4 %collective-permute-start.86 = (bf16[432,384]{1,0:T(8,128)(2,1)}, bf16[432,384]{1,0:T(8,128)(2,1)S(1)}, u32[]{:S(2)}, u32[]{:S(2)}) collective-permute-start(bf16[432,384]{1,0:T(8,128)(2,1)} %get-tuple-element.1013), channel_id=1, source_target_pairs={{0,24},{1,25},{2,26},{3,27},{4,28},{5,29},{6,30},{7,31},{8,0},{9,1... | collective-permute-start | bytes 995336 | tf_op jit(solution)/shard_map/ppermute | solution.py:833
  459.2 22.2 %collective-permute-start.87 = (bf16[432,384]{1,0:T(8,128)(2,1)}, bf16[432,384]{1,0:T(8,128)(2,1)S(1)}, u32[]{:S(2)}, u32[]{:S(2)}) collective-permute-start(bf16[432,384]{1,0:T(8,128)(2,1)} %get-tuple-element.1014), channel_id=1, source_target_pairs={{0,2},{1,3},{2,0},{3,1},{4,6},{5,7},{6,4},{7,5},{8,10},{9,11},{10,... | collective-permute-start | bytes 995336 | tf_op jit(solution)/shard_map/ppermute | solution.py:829
  482.1 23.7 %collective-permute-start.90 = (bf16[432,384]{1,0:T(8,128)(2,1)}, bf16[432,384]{1,0:T(8,128)(2,1)}, u32[]{:S(2)}, u32[]{:S(2)}) collective-permute-start(bf16[432,384]{1,0:T(8,128)(2,1)} %get-tuple-element.1036), channel_id=1, source_target_pairs={{0,24},{1,25},{2,26},{3,27},{4,28},{5,29},{6,30},{7,31},{8,0},{9,1... | collective-permute-start | bytes 995336 | tf_op jit(solution)/shard_map/ppermute | solution.py:833
  (188 other events, 2155.2 us)
Sparse Core Ops, SparseCore 0:
  12.9 100.7 all-gather.2

commit v10 on v7

--- a/solution.py
+++ b/solution.py
@@ -163,35 +163,41 @@
         mask[...] = (column < lane_lengths(sc, shape)).astype(F32).astype(BF16)
 
 
-def inverse_sums(sc, weights, mask):
+def mix_kernel(carried, sc, *refs):
+    shards, (v_own, v_far, *rest) = refs[:8], refs[8:]
+    mixed, mean, exps, inverse, raw, mask, sems = rest[4:] if carried else rest
+    fill_mask(sc, mask)
+    slot = take_plane(sc[PLACE], shards, raw, sems)
     shape = (HROWS, 4 * HEAD)
     line = lax.broadcasted_iota(jnp.int32, shape, 0)
     position = 128 * (line // HALF) + HALF * sc[CORE] + line % HALF
-    return jnp.where(position < lane_lengths(sc, shape), 1.0 / dot(weights, mask[...], 1, 0), 0.0)
-
-
-def mix_kernel(carried, sc, *refs):
-    shards, (v_own, v_far, *rest) = refs[:8], refs[8:]
-    mixed, mean, raw, mask, sems = rest[2:] if carried else rest
-    fill_mask(sc, mask)
-    slot = take_plane(sc[PLACE], shards, raw, sems)
+    valid = position < lane_lengths(sc, shape)
     for head in range(PHEADS):
         weights = jnp.exp(raw[slot, head_rows(head)].astype(F32)).astype(BF16)
-        values = jnp.concatenate([v_own[head], v_far[head]], axis=1)
-        found = dot(weights, values, 1, 0) * inverse_sums(sc, weights, mask)
+        exps[head] = weights
+        both = dot(weights, jnp.concatenate([v_own[head], v_far[head], mask[...]], axis=1), 1, 0)
+        flip = jnp.where(valid, 1.0 / both[:, 4 * HEAD :], 0.0)
+        found = both[:, : 4 * HEAD] * flip
+        inverse[head] = flip.astype(BF16)
         mean[head] = found
         mixed[head] = found.astype(BF16)
 
 
 def run_mix(sc, planes, shards, v_own, v_far, carry):
     carry = list(carry)
+    shape = (HEADS, HROWS, 4 * HEAD)
     return pl.pallas_call(
         partial(mix_kernel, bool(carry)),
         grid_spec=pltpu.PrefetchScalarGridSpec(
             num_scalar_prefetch=1,
             grid=(2,),
             in_specs=anywhere(8) + [plane_spec(planes, LMAX, 2 * HEAD)] * 2 + anywhere(len(carry)),
-            out_specs=[plane_spec(planes, HROWS, 4 * HEAD)] * 2,
+            out_specs=[
+                plane_spec(planes, HROWS, 4 * HEAD),
+                plane_spec(planes, HROWS, 4 * HEAD),
+                plane_spec(planes, HROWS, LMAX),
+                plane_spec(planes, HROWS, 4 * HEAD),
+            ],
             scratch_shapes=[
                 pltpu.VMEM((2, 4 * SUBS * HALF, LMAX), BF16),
                 pltpu.VMEM((LMAX, 4 * HEAD), BF16),
@@ -199,14 +205,16 @@
             ],
         ),
         out_shape=[
-            jax.ShapeDtypeStruct((HEADS, HROWS, 4 * HEAD), BF16),
-            jax.ShapeDtypeStruct((HEADS, HROWS, 4 * HEAD), F32),
+            jax.ShapeDtypeStruct(shape, BF16),
+            jax.ShapeDtypeStruct(shape, F32),
+            jax.ShapeDtypeStruct((HEADS, HROWS, LMAX), BF16),
+            jax.ShapeDtypeStruct(shape, BF16),
         ],
         input_output_aliases={11 + i: i for i in range(len(carry))},
         compiler_params=params(VMEM),
         cost_estimate=pl.CostEstimate(
             flops=2 * HEADS * HROWS * LMAX * 4 * HEAD,
-            bytes_accessed=HEADS * (HROWS * LMAX + 5 * HROWS * 256),
+            bytes_accessed=HEADS * (2 * HROWS * LMAX + 5 * HROWS * 256),
             transcendentals=HEADS * HROWS * LMAX // 2,
         ),
         name="mix",
@@ -414,11 +422,11 @@
 def up_grad_kernel(sc, normed, up_grad, own, far):
     total = dot(normed[...], up_grad[...], 0, 0).astype(BF16)
 
-    @pl.when(pl.program_id(0) < FSIDE)
+    @pl.when(pl.program_id(0) < 3)
     def _():
         own[...] = total
 
-    @pl.when(pl.program_id(0) >= FSIDE)
+    @pl.when(pl.program_id(0) >= 3)
     def _():
         far[...] = total
 
@@ -428,9 +436,12 @@
         up_grad_kernel,
         grid_spec=pltpu.PrefetchScalarGridSpec(
             num_scalar_prefetch=1,
-            grid=(2 * FSIDE,),
-            in_specs=[held((ROWS, WIDTH)), spec((ROWS, FSTEP), unit_columns)],
-            out_specs=[spec((WIDTH, FSTEP), early), spec((WIDTH, FSTEP), late)],
+            grid=(6,),
+            in_specs=[held((ROWS, WIDTH)), spec((ROWS, 512), lambda f, s: (0, lax.rem(3 * s[CORE] + f, 6)))],
+            out_specs=[
+                spec((WIDTH, 512), lambda f, s: (0, lax.min(f, 2))),
+                spec((WIDTH, 512), lambda f, s: (0, lax.max(f - 3, 0))),
+            ],
         ),
         out_shape=[jax.ShapeDtypeStruct((WIDTH, FF // 2), BF16)] * 2,
         compiler_params=params(VMEM),
@@ -439,6 +450,44 @@
         ),
         name="up_grad",
     )(sc, normed.reshape(ROWS, WIDTH), up_grad)
+
+
+def out_grad_kernel(sc, mixed, res_own, res_far, own, far, total):
+    step = pl.program_id(0)
+    grad = jnp.concatenate([res_own[...], res_far[...]], axis=0).reshape(4 * SPAN, WIDTH)
+    found = dot(mixed[...].reshape(4 * SPAN, WIDTH), grad, 0, 0)
+
+    @pl.when(step == 0)
+    def _():
+        total[...] = found
+
+    @pl.when(step > 0)
+    def _():
+        total[...] += found
+
+    @pl.when(step == pl.num_programs(0) - 1)
+    def _():
+        own[...] = total[:, own_lanes(sc)].astype(BF16)
+        far[...] = total[:, far_lanes(sc)].astype(BF16)
+
+
+def run_out_grad(sc, mixed, res_own, res_far):
+    return pl.pallas_call(
+        out_grad_kernel,
+        grid_spec=pltpu.PrefetchScalarGridSpec(
+            num_scalar_prefetch=1,
+            grid=(HROWS // SPAN,),
+            in_specs=[slab_spec(), slab_spec(2), slab_spec(2)],
+            out_specs=[held((WIDTH, SIDE))] * 2,
+            scratch_shapes=[pltpu.VMEM((WIDTH, WIDTH), F32)],
+        ),
+        out_shape=[jax.ShapeDtypeStruct((WIDTH, SIDE), BF16)] * 2,
+        compiler_params=params(VMEM),
+        cost_estimate=pl.CostEstimate(
+            flops=2 * ROWS * WIDTH * WIDTH, bytes_accessed=4 * ROWS * WIDTH, transcendentals=0
+        ),
+        name="out_grad",
+    )(sc, mixed, res_own, res_far)
 
 
 def out_kernel(sc, active, resid, dn_own, dn_far, own, far, w_down):
@@ -483,8 +532,8 @@
     )(sc, active.reshape(4, HROWS, FF), resid, *down)
 
 
-def post_kernel(sc, resid, back, cot, mixed, wo_own, wo_far, gain, *refs):
-    (res_own, res_far, heads, d_out_own, d_out_far, d_gain, weight, total, spread) = refs
+def post_kernel(sc, resid, back, cot, wo_own, wo_far, gain, *refs):
+    (res_own, res_far, heads, d_gain, weight, spread) = refs
     step = pl.program_id(0)
     whole_weight(sc, step, wo_own, wo_far, weight)
     shape, slab = (4 * SPAN, WIDTH), (4, SPAN, WIDTH)
@@ -500,17 +549,14 @@
     res_own[...] = low.reshape(slab)[:2]
     res_far[...] = low.reshape(slab)[2:]
     gain_sum = jnp.sum(two_grad * unit, axis=0, keepdims=True)
-    out_sum = dot(mixed[...].reshape(shape), low, 0, 0)
 
     @pl.when(step == 0)
     def _():
         d_gain[...] = gain_sum
-        total[...] = out_sum
 
     @pl.when(step > 0)
     def _():
         d_gain[...] += gain_sum
-        total[...] += out_sum
 
     spread[...] = dot(low, weight[...], 1, 1).astype(BF16).reshape(slab)
     for pair in range(HEADS // 2):
@@ -521,26 +567,18 @@
             heads[2 * pair, :, half] = jnp.concatenate([one[:, :HEAD], two[:, :HEAD]], axis=1)
             heads[2 * pair + 1, :, half] = jnp.concatenate([one[:, HEAD:], two[:, HEAD:]], axis=1)
 
-    @pl.when(step == pl.num_programs(0) - 1)
-    def _():
-        weight[...] = total[...].astype(BF16)
-        d_out_own[...] = weight[:, own_lanes(sc)]
-        d_out_far[...] = weight[:, far_lanes(sc)]
-
-
-def run_post(sc, resid, back, cotangent, mixed, wo, gain):
+
+def run_post(sc, resid, back, cotangent, wo, gain):
     whole = (4, HROWS, WIDTH)
     return pl.pallas_call(
         post_kernel,
         grid_spec=pltpu.PrefetchScalarGridSpec(
             num_scalar_prefetch=1,
             grid=(HROWS // SPAN,),
-            in_specs=[slab_spec()] * 4 + [held((WIDTH, SIDE)), held((WIDTH, SIDE)), held((1, WIDTH))],
-            out_specs=[slab_spec(2)] * 2
-            + [heads_spec(), held((WIDTH, SIDE)), held((WIDTH, SIDE)), held((1, WIDTH))],
+            in_specs=[slab_spec()] * 3 + [held((WIDTH, SIDE)), held((WIDTH, SIDE)), held((1, WIDTH))],
+            out_specs=[slab_spec(2)] * 2 + [heads_spec(), held((1, WIDTH))],
             scratch_shapes=[
                 pltpu.VMEM((WIDTH, WIDTH), BF16),
-                pltpu.VMEM((WIDTH, WIDTH), F32),
                 pltpu.VMEM((4, SPAN, WIDTH), BF16),
             ],
         ),
@@ -548,8 +586,6 @@
             jax.ShapeDtypeStruct((2, HROWS, WIDTH), BF16),
             jax.ShapeDtypeStruct((2, HROWS, WIDTH), BF16),
             jax.ShapeDtypeStruct((HEADS, HROWS, 4 * HEAD), BF16),
-            jax.ShapeDtypeStruct((WIDTH, SIDE), BF16),
-            jax.ShapeDtypeStruct((WIDTH, SIDE), BF16),
             jax.ShapeDtypeStruct((1, WIDTH), F32),
         ],
         compiler_params=params(VMEM),
@@ -557,13 +593,12 @@
             flops=4 * ROWS * WIDTH * WIDTH, bytes_accessed=28 * ROWS * WIDTH, transcendentals=0
         ),
         name="post",
-    )(sc, resid, back.reshape(whole), cotangent, mixed, *wo, gain)
-
-
-def unmix_kernel(carried, sc, *refs):
-    shards, (v_own, v_far, grad_heads, mean, *rest) = refs[:8], refs[8:]
-    rest = rest[2:] if carried else rest
-    outs, (own, far, raw, grads, mask, adder, bound, sems, out_sems) = rest[:8], rest[8:]
+    )(sc, resid, back.reshape(whole), cotangent, *wo, gain)
+
+
+def unmix_kernel(carried, sc, v_own, v_far, grad_heads, mean, exps, inverse, *refs):
+    refs = refs[2:] if carried else refs
+    outs, (own, far, grads, mask, adder, bound, out_sems) = refs[:8], refs[8:]
     place = sc[PLACE]
     step = pl.program_id(0)
 
@@ -591,11 +626,10 @@
         length = jnp.where(item % 4 == 3, sc[LENGTHS + 3], length)
         bound[...] = jnp.where((item < 8) & (row < length), 1.0, 0.0).astype(BF16)
 
-    slot = take_plane(place, shards, raw, sems)
     high_lanes = lax.broadcasted_iota(jnp.int32, (HROWS, 128), 1) < 4
     for head in range(PHEADS):
-        weights = jnp.exp(raw[slot, head_rows(head)].astype(F32)).astype(BF16)
-        low = (grad_heads[head].astype(F32) * inverse_sums(sc, weights, mask)).astype(BF16)
+        weights = exps[head]
+        low = (grad_heads[head].astype(F32) * inverse[head].astype(F32)).astype(BF16)
         product = low.astype(F32) * mean[head]
         coarse = product.astype(BF16)
         fine = (product - coarse.astype(F32)).astype(BF16)
@@ -604,7 +638,7 @@
         fine = (delta - coarse.astype(F32)).astype(BF16)
         left = jnp.concatenate([low, jnp.where(high_lanes, coarse, fine)], axis=1)
         score = dot(left, jnp.concatenate([v_own[head], v_far[head], bound[...]], axis=1), 1, 1)
-        grads[slot, head_rows(head)] = (score * weights.astype(F32)).astype(BF16)
+        grads[step, head_rows(head)] = (score * weights.astype(F32)).astype(BF16)
         back = (dot(weights, low, 0, 0) * mask[...].astype(F32)).astype(BF16)
         own[head] = back[:, : 2 * HEAD]
         far[head] = back[:, 2 * HEAD :]
@@ -619,39 +653,42 @@
                     copy.wait()
 
 
-def run_unmix(sc, planes, shards, v_own, v_far, grad_heads, mean, carry):
+def run_unmix(sc, planes, v_own, v_far, grad_heads, mean, exps, inverse, carry):
     carry = list(carry)
     return pl.pallas_call(
         partial(unmix_kernel, bool(carry)),
         grid_spec=pltpu.PrefetchScalarGridSpec(
             num_scalar_prefetch=1,
             grid=(2,),
-            in_specs=anywhere(8)
-            + [plane_spec(planes, LMAX, 2 * HEAD)] * 2
-            + [plane_spec(planes, HROWS, 4 * HEAD)] * 2
+            in_specs=[
+                plane_spec(planes, LMAX, 2 * HEAD),
+                plane_spec(planes, LMAX, 2 * HEAD),
+                plane_spec(planes, HROWS, 4 * HEAD),
+                plane_spec(planes, HROWS, 4 * HEAD),
+                plane_spec(planes, HROWS, LMAX),
+                plane_spec(planes, HROWS, 4 * HEAD),
+            ]
             + anywhere(len(carry)),
             out_specs=anywhere(8) + [plane_spec(planes, LMAX, 2 * HEAD)] * 2,
             scratch_shapes=[
-                pltpu.VMEM((2, 4 * SUBS * HALF, LMAX), BF16),
                 pltpu.VMEM((2, 4 * SUBS * HALF, LMAX), BF16),
                 pltpu.VMEM((LMAX, 4 * HEAD), BF16),
                 pltpu.VMEM((4 * HEAD, 128), BF16),
                 pltpu.VMEM((LMAX, 128), BF16),
                 pltpu.SemaphoreType.DMA((2, 4)),
-                pltpu.SemaphoreType.DMA((2, 4)),
             ],
         ),
         out_shape=[jax.ShapeDtypeStruct((SUBS * HALF, LMAX), BF16)] * 8
         + [jax.ShapeDtypeStruct((HEADS, LMAX, 2 * HEAD), BF16)] * 2,
-        input_output_aliases={13 + i: 8 + i for i in range(len(carry))},
+        input_output_aliases={7 + i: 8 + i for i in range(len(carry))},
         compiler_params=params(VMEM),
         cost_estimate=pl.CostEstimate(
             flops=3 * HEADS * HROWS * LMAX * 4 * HEAD,
-            bytes_accessed=HEADS * (2 * HROWS * LMAX + 4 * HROWS * 256 + 4 * LMAX * 256),
-            transcendentals=HEADS * HROWS * LMAX // 2,
+            bytes_accessed=HEADS * (2 * HROWS * LMAX + 5 * HROWS * 256 + 4 * LMAX * 256),
+            transcendentals=0,
         ),
         name="unmix",
-    )(sc, *shards, v_own, v_far, grad_heads, mean, *carry)
+    )(sc, v_own, v_far, grad_heads, mean, exps, inverse, *carry)
 
 
 def close_kernel(sc, tok, res_own, res_got, out_own, out_got, own, far, gain, w_own, w_far, *refs):
@@ -984,9 +1021,11 @@
 
     rand = rand_mix.reshape(3, 2, HALF, LMAX)
     blocks = side(pick(rand, core, 1), other(pick(rand, 1 - core, 1)), 0)
-    weights, rands = together((gather_step(weights, 0), {(0, 0, 0): blocks.reshape(SUBS * HALF, LMAX)}))
-    weights, tokens_far = together((gather_step(weights, 1), other(pick(tokens, 1 - core, 2))))
-    weights, grad_far = together((gather_step(weights, 2), other(pick(grad_out, 1 - core, 2))))
+    weights, rands, late_tokens, late_grad = together(
+        (gather_step(weights, 0), {(0, 0, 0): blocks.reshape(SUBS * HALF, LMAX)}, tokens, grad_out)
+    )
+    weights, tokens_far = together((gather_step(weights, 1), other(pick(late_tokens, 1 - core, 2))))
+    weights, grad_far = together((gather_step(weights, 2), other(pick(late_grad, 1 - core, 2))))
     weights, far_lengths = together((gather_step(weights, 3), other(lengths)))
     sc = jnp.concatenate([near_sc[:5], far_lengths])
     weights, rands = together((gather_step(weights, 4), rands))
@@ -1003,28 +1042,23 @@
     v_own = run_values(sc, tokens.reshape(2, LMAX, WIDTH), gain_one, value, value_far)
     rands, v_own, out, down, up = together((rands, v_own, (out, other(out)), down, up))
     rands, v_own, v_far, down, up = together((gather_step(rands, 2), v_own, other(v_own), down, up))
-    rands, v_far, down, up = together((gather_step(rands, 3), v_far, (down, other(down)), up))
+    rands, v_far, down, up = together((gather_step(rands, 3), v_far, down, up))
     near = [rands[k, y_at, x_at] for k in range(2) for y_at in range(2) for x_at in range(2)]
     rands = gather_step(rands, 4)
     mixing = run_mix(sc, (0, 1), near, v_own, v_far, ())
-    rands, up, mixing = together((rands, (up, other(up)), mixing))
-    shares = in_order(rands)
-    heads, mean = run_mix(sc, (2, 3), shares[8:], v_own, v_far, mixing)
+    rands, down, up, mixing = together((rands, down, up, mixing))
+    heads, mean, exps, inverse = run_mix(sc, (2, 3), in_order(rands)[8:], v_own, v_far, mixing)
+    down, up = (down, other(down)), (up, other(up))
 
     mixed, resid, normed, masked = run_pre(sc, tokens, tokens_far, grad_out, grad_far, heads, out, gain_two)
     active, up_grad, back = run_units(sc, normed, masked, up, down)
-    res_own, res_far, grad_heads, d_out_own, d_out_far, d_gain_two = run_post(
-        sc, resid, back, masked, mixed, out, gain_two
-    )
-
-    *far, back_own, back_far = run_unmix(
-        sc, (3, 2), shares[12:] + shares[8:12], v_own, v_far, grad_heads, mean, ()
-    )
-    far, back_own, back_far, res_got, d_out_got = together((far, back_own, back_far, other(res_far), other(d_out_far)))
+    res_own, res_far, grad_heads, d_gain_two = run_post(sc, resid, back, masked, out, gain_two)
+
+    backward = lambda planes, carry: run_unmix(sc, planes, v_own, v_far, grad_heads, mean, exps, inverse, carry)
+    *far, back_own, back_far = backward((3, 2), ())
+    far, back_own, back_far, res_got = together((far, back_own, back_far, other(res_far)))
     have, got = scatter_send(by_place(far, (3, 2)), 0)
-    *near, back_own, back_far = run_unmix(
-        sc, (1, 0), shares[4:8] + shares[:4], v_own, v_far, grad_heads, mean, (back_own, back_far)
-    )
+    *near, back_own, back_far = backward((1, 0), (back_own, back_far))
     have, got, near, back_own, back_far = together((have, got, near, back_own, back_far))
     have = {**scatter_add(have, got, 0), **by_place(near, (1, 0))}
 
@@ -1039,41 +1073,39 @@
     have = scatter_add(have, got, 2)
 
     have, got = scatter_send(have, 3)
+    d_out_own, d_out_far = run_out_grad(sc, mixed, res_own, res_far)
+    packed = run_collect(sc, down_own, other(down_far), up_own, up_got, d_out_own, other(d_out_far))
+    have, got, packed = together((have, got, packed))
+    have = scatter_add(have, got, 3)
+
+    have, got = scatter_send(have, 4)
     out_own, out_far = run_out(sc, active, resid, down)
-    have, got, out_own, out_far, down_got = together((have, got, out_own, out_far, other(down_far)))
-    have = scatter_add(have, got, 3)
-
-    have, got = scatter_send(have, 4)
-    packed = run_collect(sc, down_own, down_got, up_own, up_got, d_out_own, d_out_got)
-    have, got, packed, out_got = together((have, got, packed, other(out_far)))
+    have, got, packed, out_own, out_far = together((have, got, packed, out_own, out_far))
     rand_sum = scatter_add(have, got, 4)[0, 0, 0].reshape(2, 3, HALF, LMAX)
 
     sums, got = scatter_send(by_place(packed), 0)
+    sums, got = scatter_send(scatter_add(sums, got, 0), 1)
     output, tokens_grad, d_value, d_gain_one = run_close(
-        sc, tokens, res_own, res_got, out_own, out_got, back_own, back_got, gain_one, value, value_far
-    )
-    blocks, blocks_far = pick(rand_sum, core), other(pick(rand_sum, 1 - core))
-    sums, got, output, tokens_grad, d_value, d_gain_one, blocks, blocks_far = together(
-        (sums, got, output, tokens_grad, d_value, d_gain_one, blocks, blocks_far)
-    )
-    sums = scatter_add(sums, got, 0)
-
-    sums, got = scatter_send(sums, 1)
+        sc, tokens, res_own, res_got, out_own, other(out_far), back_own, back_got, gain_one, value, value_far
+    )
+    sums, got, output, tokens_grad, d_value, d_gain_one = together(
+        (sums, got, output, tokens_grad, d_value, d_gain_one)
+    )
+    sums = scatter_add(sums, got, 1)
+
+    sums, got = scatter_send(sums, 2)
     gain_pair = jnp.concatenate([d_gain_one, d_gain_two]).reshape(2, 16, 1, 48).astype(BF16)
     gain_pair = jnp.pad(gain_pair, ((0, 0), (0, 0), (0, 15), (0, SIDE - 48)))
     small = jnp.concatenate([d_value.reshape(2, 16, 48, SIDE), gain_pair], 2)
     small = add_low(pick(small, core), other(pick(small, 1 - core))).reshape(4, 2, 2, 64, SIDE)
-    sums, got, small = together((sums, got, small))
-    sums = scatter_add(sums, got, 1)
-
-    sums, got = scatter_send(sums, 2)
     small = add_low(pick(small, x, 2), swap(pick(small, 1 - x, 2), TO_X))
     sums, got, small = together((sums, got, small))
     sums = scatter_add(sums, got, 2)
 
     sums, got = scatter_send(sums, 3)
     small = add_low(pick(small, y, 1), swap(pick(small, 1 - y, 1), TO_Y))
-    sums, got, small = together((sums, got, small))
+    blocks, blocks_far = pick(rand_sum, core), other(pick(rand_sum, 1 - core))
+    sums, got, small, blocks, blocks_far = together((sums, got, small, blocks, blocks_far))
     sums = scatter_add(sums, got, 3)
 
     sums, got = scatter_send(sums, 4)

time: 527 us -> 514 us (0.975)
  waiting for transfers between devices: 160 us -> 147 us
  starting transfers between devices: 74.8 us -> 81.4 us
    ppermute x66, waiting for transfers between devices: 98.4 us -> 81.8 us  [swap(): return lax.ppermute(x, BOTH, [(d, d ^ bit) for d in range(DEVICES)])]
    pallas_call x0 -> x1, Pallas kernels: none -> 7.71 us  [run_out_grad(): pl.pallas_call(out_grad_kernel, grid_spec=pltpu.PrefetchScalarGridSpec(nu...]
    pallas_call x2, Pallas kernels: 34.6 us -> 27.5 us  [run_unmix(): pl.pallas_call(partial(unmix_kernel, bool(carry)), grid_spec=pltpu.Prefet...]
    pallas_call x1, Pallas kernels: 18.4 us -> 12.7 us  [run_post(): pl.pallas_call(post_kernel, grid_spec=pltpu.PrefetchScalarGridSpec(num_sc...]
    ppermute x66, starting transfers between devices: 43 us -> 48.6 us  [swap(): return lax.ppermute(x, BOTH, [(d, d ^ bit) for d in range(DEVICES)])]
  transfers between devices with their start and end apart: 89 -> 89, of which waited for: 46 -> 48; matrix products, arithmetic and copies ran while one was open for 3% -> 3% of each run, Pallas kernels for 30% -> 36%
where the time goes in v10:
time: 514 us; the launch traced here: 508 us
  Pallas kernels  247 us (48%)
  waiting for transfers between devices  147 us (29%)
  starting transfers between devices  81.4 us (16%)
  local copies, waits for them, and re-layouts  22.7 us (4%)
  other arithmetic  8.89 us (2%)
    ppermute x66, waiting for transfers between devices, swap(): return lax.ppermute(x, BOTH, [(d, d ^ bit) for d in range(DEVICES)])  81.8 us
    ppermute x23, waiting for transfers between devices, ring(): lax.ppermute(x, BOTH, [(d, (d + 8 * way) % DEVICES) for d in range(DEVICE...  65.1 us
    ppermute x66, starting transfers between devices, swap(): return lax.ppermute(x, BOTH, [(d, d ^ bit) for d in range(DEVICES)])  48.6 us
    pallas_call x1, Pallas kernels, run_units(): pl.pallas_call(units_kernel, grid_spec=pltpu.PrefetchScalarGridSpec(num_s...  46 us
    ppermute x23, starting transfers between devices, ring(): lax.ppermute(x, BOTH, [(d, (d + 8 * way) % DEVICES) for d in range(DEVICE...  32.8 us
    pallas_call x10, Pallas kernels, run_add(): pl.pallas_call(partial(add_kernel, groups), grid=(parts,), in_specs=[bloc...  28.6 us
    pallas_call x2, Pallas kernels, run_unmix(): pl.pallas_call(partial(unmix_kernel, bool(carry)), grid_spec=pltpu.Prefet...  27.5 us
    pallas_call x2, Pallas kernels, run_mix(): pl.pallas_call(partial(mix_kernel, bool(carry)), grid_spec=pltpu.Prefetch...  21.2 us
  transfers between devices with their start and end apart: 89, of which 48 were waited for; matrix products, arithmetic and copies ran while one was open for 3% of the time, Pallas kernels for 36%

profile of v10, /device:TPU:0, one launch (start us, length us, event | category | flops | bytes accessed | tf_op | source)
XLA Modules:
  0.0 507.9 jit_solution(361654987965638792)
XLA Ops:
  16.6 6.2 %collective-permute-done.5.refs_1_ = bf16[496,384]{1,0:T(8,128)(2,1)S(1)} collective-permute-done((bf16[496,384]{1,0:T(8,128)(2,1)}, bf16[496,384]{1,0:T(8,128)(2,1)S(1)}, u32[]{:S(2)}, u32[]{:S(2)}) %collective-permute-start.5) | collective-permute-done | bytes 380960 | tf_op jit(solution)/shard_map/ppermute | solution.py:943
  31.6 9.6 %collective-permute-done.10.refs_5_ = bf16[496,384]{1,0:T(8,128)(2,1)S(1)} collective-permute-done((bf16[496,384]{1,0:T(8,128)(2,1)S(1)}, bf16[496,384]{1,0:T(8,128)(2,1)S(1)}, u32[]{:S(2)}, u32[]{:S(2)}) %collective-permute-start.10) | collective-permute-done | bytes 380960 | tf_op jit(solution)/shard_map/ppermute | solution.py:943
  45.4 7.5 %collective-permute-done.13.refs_6_ = bf16[496,384]{1,0:T(8,128)(2,1)S(1)} collective-permute-done((bf16[496,384]{1,0:T(8,128)(2,1)S(1)}, bf16[496,384]{1,0:T(8,128)(2,1)S(1)}, u32[]{:S(2)}, u32[]{:S(2)}) %collective-permute-start.13) | collective-permute-done | bytes 380960 | tf_op jit(solution)/shard_map/ppermute | solution.py:943
  59.3 6.6 %collective-permute-done.17.refs_7_ = bf16[496,384]{1,0:T(8,128)(2,1)S(1)} collective-permute-done((bf16[496,384]{1,0:T(8,128)(2,1)S(1)}, bf16[496,384]{1,0:T(8,128)(2,1)S(1)}, u32[]{:S(2)}, u32[]{:S(2)}) %collective-permute-start.17) | collective-permute-done | bytes 380960 | tf_op jit(solution)/shard_map/ppermute | solution.py:947
  68.1 5.6 %collective-permute-done.21.refs_11_ = bf16[496,384]{1,0:T(8,128)(2,1)S(1)} collective-permute-done((bf16[496,384]{1,0:T(8,128)(2,1)S(1)}, bf16[496,384]{1,0:T(8,128)(2,1)S(1)}, u32[]{:S(2)}, u32[]{:S(2)}) %collective-permute-start.21) | collective-permute-done | bytes 380960 | tf_op jit(solution)/shard_map/ppermute | solution.py:943
  82.0 7.2 %place.1 = (bf16[3072,384]{1,0:T(8,128)(2,1)}, bf16[768,1536]{1,0:T(8,128)(2,1)}, bf16[768,384]{1,0:T(8,128)(2,1)}, bf16[768,384]{1,0:T(8,128)(2,1)}, bf16[256,384]{1,0:T(8,128)(2,1)}) custom-call(s32[7]{0:T(128)} %concatenate.54.sc, bf16[496,384]{1,0:T(8,128)(2,1)} %pack.1.refs_0_, bf16[496,384]{1,0:T(8,128)(2,1)} %copy-done.25, ...), custom_call_target="tpu_custom_call" | custom-call | bytes 12189696 | tf_op jit(solution)/shard_map/place/pallas_call | solution.py:847
  99.7 7.8 %values.1.refs_8_.v_own = bf16[12,1024,128]{2,1,0:T(8,128)(2,1)} custom-call(s32[7]{0:T(128)} %concatenate.54.sc, bf16[2,1024,768]{2,1,0:T(8,128)(2,1)} %tok.1, f32[1,768]{1,0:T(1,128)} %reshape.205.gain, bf16[768,384]{1,0:T(8,128)(2,1)} %get-tuple-element.433.w_own, bf16[768,384]{1,0:T(8,128)(2,1)} %copy-done.60), custom_call_target="tpu_custom_call" | custom-call | flops 2415919104 | bytes 6291456 | tf_op jit(solution)/shard_map/values/pallas_call | solution.py:80
  120.6 15.5 %collective-permute-done.32.refs_6_ = bf16[384,1024]{1,0:T(8,128)(2,1)S(1)} collective-permute-done((bf16[384,1024]{1,0:T(8,128)(2,1)}, bf16[384,1024]{1,0:T(8,128)(2,1)S(1)}, u32[]{:S(2)}, u32[]{:S(2)}) %collective-permute-start.32) | collective-permute-done | bytes 786464 | tf_op jit(solution)/shard_map/ppermute | solution.py:943
  142.9 17.1 %collective-permute-done.36.refs_7_ = bf16[384,1024]{1,0:T(8,128)(2,1)S(1)} collective-permute-done((bf16[384,1024]{1,0:T(8,128)(2,1)S(1)}, bf16[384,1024]{1,0:T(8,128)(2,1)S(1)}, u32[]{:S(2)}, u32[]{:S(2)}) %collective-permute-start.36) | collective-permute-done | bytes 786464 | tf_op jit(solution)/shard_map/ppermute | solution.py:947
  163.3 10.6 %mix.2 = (bf16[12,512,256]{2,1,0:T(8,128)(2,1)}, f32[12,512,256]{2,1,0:T(8,128)}, bf16[12,512,1024]{2,1,0:T(8,128)(2,1)}, bf16[12,512,256]{2,1,0:T(8,128)(2,1)}) custom-call(s32[7]{0:T(128)} %concatenate.54.sc, bf16[384,1024]{1,0:T(8,128)(2,1)} %bitcast.114, bf16[384,1024]{1,0:T(8,128)(2,1)} %collective-permute-done.24.refs_1_, ...), custom_call_target="tpu_custom_call" | custom-call | flops 3221225472 | bytes 20447232 | tf_op jit(solution)/shard_map/mix/pallas_call | solution.py:189
  174.0 4.9 collective-permute-done.39.refs_3_
  182.5 10.6 %mix.3 = (bf16[12,512,256]{2,1,0:T(8,128)(2,1)}, f32[12,512,256]{2,1,0:T(8,128)}, bf16[12,512,1024]{2,1,0:T(8,128)(2,1)}, bf16[12,512,256]{2,1,0:T(8,128)(2,1)}) custom-call(s32[7]{0:T(128)} %concatenate.54.sc, bf16[384,1024]{1,0:T(8,128)(2,1)} %copy-done.21, ...), custom_call_target="tpu_custom_call", output_to_operand_aliasing={{0}: (11, {}), {1}: (12, {}), {2}: (13, {}), {3}: (14, {})} | custom-call | flops 3221225472 | bytes 20447232 | tf_op jit(solution)/shard_map/mix/pallas_call | solution.py:189
  193.1 12.4 %pre.1 = (bf16[4,512,768]{2,1,0:T(8,128)(2,1)}, bf16[4,512,768]{2,1,0:T(8,128)(2,1)}, bf16[4,512,768]{2,1,0:T(8,128)(2,1)}, bf16[4,512,768]{2,1,0:T(8,128)(2,1)}) custom-call(s32[7]{0:T(128)} %concatenate.54.sc, bf16[2,8,2,64,768]{4,3,2,1,0:T(8,128)(2,1)} %bitcast.108, bf16[2,8,64,768]{3,2,1,0:T(8,128)(2,1)} %copy-done.6, ...), custom_call_target="tpu_custom_call" | custom-call | flops 2415919104 | bytes 25165824 | tf_op jit(solution)/shard_map/pre/pallas_call | solution.py:270
  206.9 46.0 %units.1 = (bf16[2048,3072]{1,0:T(8,128)(2,1)}, bf16[2048,3072]{1,0:T(8,128)(2,1)}, bf16[2048,768]{1,0:T(8,128)(2,1)}) custom-call(s32[7]{0:T(128)} %concatenate.54.sc, bf16[2048,768]{1,0:T(8,128)(2,1)} %bitcast.136, bf16[2048,768]{1,0:T(8,128)(2,1)} %bitcast.134, bf16[768,1536]{1,0:T(8,128)(2,1)} %get-tuple-element.502.up_own, ...), custom_call_target="tpu_custom_call" | custom-call | flops 28991029248 | bytes 37748736 | tf_op jit(solution)/shard_map/units/pallas_call | solution.py:364
  252.9 12.7 %post.1 = (bf16[2,512,768]{2,1,0:T(8,128)(2,1)}, bf16[2,512,768]{2,1,0:T(8,128)(2,1)}, bf16[12,512,256]{2,1,0:T(8,128)(2,1)}, f32[1,768]{1,0:T(1,128)}) custom-call(s32[7]{0:T(128)} %concatenate.54.sc, bf16[4,512,768]{2,1,0:T(8,128)(2,1)} %get-tuple-element.499.resid, bf16[4,512,768]{2,1,0:T(8,128)(2,1)} %bitcast.142, ...), custom_call_target="tpu_custom_call" | custom-call | flops 4831838208 | bytes 44040192 | tf_op jit(solution)/shard_map/post/pallas_call | solution.py:573
  265.7 13.9 %unmix.2 = (bf16[384,1024]{1,0:T(8,128)(2,1)}, bf16[384,1024]{1,0:T(8,128)(2,1)}, bf16[384,1024]{1,0:T(8,128)(2,1)}, bf16[384,1024]{1,0:T(8,128)(2,1)}, bf16[384...) custom-call(s32[7]{0:T(128)} %concatenate.54.sc, ...), custom_call_target="tpu_custom_call" | custom-call | flops 4831838208 | bytes 33030144 | tf_op jit(solution)/shard_map/unmix/pallas_call | solution.py:658
  285.6 13.6 %unmix.3 = (bf16[384,1024]{1,0:T(8,128)(2,1)}, bf16[384,1024]{1,0:T(8,128)(2,1)}, bf16[384,1024]{1,0:T(8,128)(2,1)}, bf16[384,1024]{1,0:T(8,128)(2,1)}, bf16[384...) custom-call(s32[7]{0:T(128)} %concatenate.54.sc, ...), custom_call_target="tpu_custom_call", output_to_operand_aliasing={{8}: (7, {}), {9}: (8, {})} | custom-call | flops 4831838208 | bytes 33030144 | tf_op jit(solution)/shard_map/unmix/pallas_call | solution.py:658
  312.1 16.1 %up_grad.1 = (bf16[768,1536]{1,0:T(8,128)(2,1)}, bf16[768,1536]{1,0:T(8,128)(2,1)}) custom-call(s32[7]{0:T(128)} %concatenate.54.sc, bf16[2048,768]{1,0:T(8,128)(2,1)} %bitcast.137, bf16[2048,3072]{1,0:T(8,128)(2,1)} %get-tuple-element.558.up_grad), custom_call_target="tpu_custom_call" | custom-call | flops 9663676416 | bytes 15728640 | tf_op jit(solution)/shard_map/up_grad/pallas_call | solution.py:435
  338.0 15.6 %down_grad.1 = (bf16[3072,384]{1,0:T(8,128)(2,1)}, bf16[3072,384]{1,0:T(8,128)(2,1)}) custom-call(s32[7]{0:T(128)} %concatenate.54.sc, bf16[2048,3072]{1,0:T(8,128)(2,1)} %get-tuple-element.578.active, bf16[2048,768]{1,0:T(8,128)(2,1)} %bitcast.135), custom_call_target="tpu_custom_call" | custom-call | flops 9663676416 | bytes 15728640 | tf_op jit(solution)/shard_map/down_grad/pallas_call | solution.py:404
  364.5 7.7 %out_grad.1 = (bf16[768,384]{1,0:T(8,128)(2,1)}, bf16[768,384]{1,0:T(8,128)(2,1)}) custom-call(s32[7]{0:T(128)} %concatenate.54.sc, bf16[4,512,768]{2,1,0:T(8,128)(2,1)} %get-tuple-element.598.mixed, bf16[2,512,768]{2,1,0:T(8,128)(2,1)} %get-tuple-element.599.res_own, bf16[2,512,768]{2,1,0:T(8,128)(2,1)} %get-tuple-element.519.res_far), custom_call_target="tpu_custom_call" | custom-call | flops 2415919104 | bytes 6291456 | tf_op jit(solution)/shard_map/out_grad/pallas_call | solution.py:475
  375.3 8.6 %collect.1 = (bf16[432,384]{1,0:T(8,128)(2,1)}, bf16[432,384]{1,0:T(8,128)(2,1)}, bf16[432,384]{1,0:T(8,128)(2,1)}, bf16[432,384]{1,0:T(8,128)(2,1)}, bf16[432,3...) custom-call(s32[7]{0:T(128)} %concatenate.54.sc, ...), custom_call_target="tpu_custom_call" | custom-call | bytes 15925248 | tf_op jit(solution)/shard_map/collect/pallas_call | solution.py:897
  390.3 16.5 %out.3 = (bf16[2,512,768]{2,1,0:T(8,128)(2,1)}, bf16[2,512,768]{2,1,0:T(8,128)(2,1)}) custom-call(s32[7]{0:T(128)} %concatenate.54.sc, bf16[4,512,3072]{2,1,0:T(8,128)(2,1)} %bitcast.139, bf16[4,512,768]{2,1,0:T(8,128)(2,1)} %get-tuple-element.499.resid, bf16[3072,384]{1,0:T(8,128)(2,1)} %get-tuple-element.503.dn_own, bf16[3072,384]{1,0:T(8,128)(2,1)} %copy-done.58), custom_call_target="tpu_custom_call" | custom-call | flops 9663676416 | bytes 23592960 | tf_op jit(solution)/shard_map/out/pallas_call | solution.py:509
  414.1 5.0 collective-permute-done.65.refs_0_
  425.5 15.8 %close.1 = (f32[2,8,2,64,768]{4,3,2,1,0:T(8,128)}, f32[2,8,2,64,768]{4,3,2,1,0:T(8,128)}, bf16[2,768,384]{2,1,0:T(8,128)(2,1)}, f32[1,768]{1,0:T(1,128)}) custom-call(s32[7]{0:T(128)} %concatenate.54.sc, bf16[2,8,2,64,768]{4,3,2,1,0:T(8,128)(2,1)} %bitcast.109, bf16[2,8,64,768]{3,2,1,0:T(8,128)(2,1)} %bitcast.143, bf16[2,8,64,768]{3,2,1,0:T(8,128)(2,1)} %bitcast.138, ...), custom_call_target="tpu_custom_call" | custom-call | flops 4831838208 | bytes 29884416 | tf_op jit(solution)/shard_map/close/pallas_call | solution.py:750
  (352 shorter events, 213.1 us)
Async XLA Ops:
  115.9 23.7 %collective-permute-start.35 = (bf16[12,1024,128]{2,1,0:T(8,128)(2,1)}, bf16[12,1024,128]{2,1,0:T(8,128)(2,1)}, u32[]{:S(2)}, u32[]{:S(2)}) collective-permute-start(bf16[12,1024,128]{2,1,0:T(8,128)(2,1)} %values.1.refs_8_.v_own), channel_id=1, source_target_pairs={{0,1},{1,0},{2,3},{3,2},{4,5},{5,4},{6,7},{7,6},{8,9},{9,8},{10,11... | collective-permute-start | bytes 9437192 | tf_op jit(solution)/shard_map/ppermute | solution.py:943
  115.9 20.2 %collective-permute-start.32 = (bf16[384,1024]{1,0:T(8,128)(2,1)}, bf16[384,1024]{1,0:T(8,128)(2,1)S(1)}, u32[]{:S(2)}, u32[]{:S(2)}) collective-permute-start(bf16[384,1024]{1,0:T(8,128)(2,1)} %collective-permute-done.26.refs_4_), channel_id=1, source_target_pairs={{0,4},{1,5},{2,6},{3,7},{4,0},{5,1},{6,2},{7,3},{8,12},{9,13},{10,... | collective-permute-start | bytes 2359304 | tf_op jit(solution)/shard_map/ppermute | solution.py:943
  116.4 19.9 %collective-permute-start.33 = (bf16[384,1024]{1,0:T(8,128)(2,1)}, bf16[384,1024]{1,0:T(8,128)(2,1)S(1)}, u32[]{:S(2)}, u32[]{:S(2)}) collective-permute-start(bf16[384,1024]{1,0:T(8,128)(2,1)} %copy-done.21), channel_id=1, source_target_pairs={{0,2},{1,3},{2,0},{3,1},{4,6},{5,7},{6,4},{7,5},{8,10},{9,11},{10,... | collective-permute-start | bytes 2359304 | tf_op jit(solution)/shard_map/ppermute | solution.py:943
  118.2 21.4 %collective-permute-start.34 = (bf16[384,1024]{1,0:T(8,128)(2,1)}, bf16[384,1024]{1,0:T(8,128)(2,1)S(1)}, u32[]{:S(2)}, u32[]{:S(2)}) collective-permute-start(bf16[384,1024]{1,0:T(8,128)(2,1)} %copy-done.21), channel_id=1, source_target_pairs={{0,8},{1,9},{2,10},{3,11},{4,12},{5,13},{6,14},{7,15},{8,16},{9,17... | collective-permute-start | bytes 2359304 | tf_op jit(solution)/shard_map/ppermute | solution.py:947
  139.6 20.4 %collective-permute-start.36 = (bf16[384,1024]{1,0:T(8,128)(2,1)S(1)}, bf16[384,1024]{1,0:T(8,128)(2,1)S(1)}, u32[]{:S(2)}, u32[]{:S(2)}) collective-permute-start(bf16[384,1024]{1,0:T(8,128)(2,1)S(1)} %collective-permute-done.28.refs_3_), channel_id=1, source_target_pairs={{0,8},{1,9},{2,10},{3,11},{4,12},{5,13},{6,14},{7,15},{8,16},{9,17... | collective-permute-start | bytes 2359304 | tf_op jit(solution)/shard_map/ppermute | solution.py:947
  140.2 20.6 %collective-permute-start.37 = (bf16[384,1024]{1,0:T(8,128)(2,1)}, bf16[384,1024]{1,0:T(8,128)(2,1)}, u32[]{:S(2)}, u32[]{:S(2)}) collective-permute-start(bf16[384,1024]{1,0:T(8,128)(2,1)} %copy-done.21), channel_id=1, source_target_pairs={{0,4},{1,5},{2,6},{3,7},{4,0},{5,1},{6,2},{7,3},{8,12},{9,13},{10,... | collective-permute-start | bytes 2359304 | tf_op jit(solution)/shard_map/ppermute | solution.py:943
  161.3 20.0 %collective-permute-start.40 = (bf16[384,1024]{1,0:T(8,128)(2,1)}, bf16[384,1024]{1,0:T(8,128)(2,1)}, u32[]{:S(2)}, u32[]{:S(2)}) collective-permute-start(bf16[384,1024]{1,0:T(8,128)(2,1)} %collective-permute-done.37.refs_2_), channel_id=1, source_target_pairs={{0,8},{1,9},{2,10},{3,11},{4,12},{5,13},{6,14},{7,15},{8,16},{9,17... | collective-permute-start | bytes 2359304 | tf_op jit(solution)/shard_map/ppermute | solution.py:947
  181.3 24.2 %collective-permute-start.42 = (bf16[768,1536]{1,0:T(8,128)(2,1)}, bf16[768,1536]{1,0:T(8,128)(2,1)}, u32[]{:S(2)}, u32[]{:S(2)}) collective-permute-start(bf16[768,1536]{1,0:T(8,128)(2,1)} %get-tuple-element.502.up_own), channel_id=1, source_target_pairs={{0,1},{1,0},{2,3},{3,2},{4,5},{5,4},{6,7},{7,6},{8,9},{9,8},{10,11... | collective-permute-start | bytes 7077896 | tf_op jit(solution)/shard_map/ppermute | solution.py:943
  181.3 24.2 %collective-permute-start.43 = (bf16[3072,384]{1,0:T(8,128)(2,1)}, bf16[3072,384]{1,0:T(8,128)(2,1)S(1)}, u32[]{:S(2)}, u32[]{:S(2)}) collective-permute-start(bf16[3072,384]{1,0:T(8,128)(2,1)} %get-tuple-element.503.dn_own), channel_id=1, source_target_pairs={{0,1},{1,0},{2,3},{3,2},{4,5},{5,4},{6,7},{7,6},{8,9},{9,8},{10,11... | collective-permute-start | bytes 7077896 | tf_op jit(solution)/shard_map/ppermute | solution.py:943
  280.8 20.1 %collective-permute-start.45 = (bf16[384,1024]{1,0:T(8,128)(2,1)}, bf16[384,1024]{1,0:T(8,128)(2,1)S(1)}, u32[]{:S(2)}, u32[]{:S(2)}) collective-permute-start(bf16[384,1024]{1,0:T(8,128)(2,1)} %get-tuple-element.525), channel_id=1, source_target_pairs={{0,24},{1,25},{2,26},{3,27},{4,28},{5,29},{6,30},{7,31},{8,0},{9,1... | collective-permute-start | bytes 2359304 | tf_op jit(solution)/shard_map/ppermute | solution.py:947
  282.4 19.9 %collective-permute-start.46 = (bf16[384,1024]{1,0:T(8,128)(2,1)}, bf16[384,1024]{1,0:T(8,128)(2,1)S(1)}, u32[]{:S(2)}, u32[]{:S(2)}) collective-permute-start(bf16[384,1024]{1,0:T(8,128)(2,1)} %get-tuple-element.526), channel_id=1, source_target_pairs={{0,2},{1,3},{2,0},{3,1},{4,6},{5,7},{6,4},{7,5},{8,10},{9,11},{10,... | collective-permute-start | bytes 2359304 | tf_op jit(solution)/shard_map/ppermute | solution.py:943
  284.1 19.6 %collective-permute-start.47 = (bf16[384,1024]{1,0:T(8,128)(2,1)}, bf16[384,1024]{1,0:T(8,128)(2,1)S(1)}, u32[]{:S(2)}, u32[]{:S(2)}) collective-permute-start(bf16[384,1024]{1,0:T(8,128)(2,1)} %get-tuple-element.527), channel_id=1, source_target_pairs={{0,4},{1,5},{2,6},{3,7},{4,0},{5,1},{6,2},{7,3},{8,12},{9,13},{10,... | collective-permute-start | bytes 2359304 | tf_op jit(solution)/shard_map/ppermute | solution.py:943
  303.7 24.8 %collective-permute-start.51 = (bf16[12,1024,128]{2,1,0:T(8,128)(2,1)}, bf16[12,1024,128]{2,1,0:T(8,128)(2,1)}, u32[]{:S(2)}, u32[]{:S(2)}) collective-permute-start(bf16[12,1024,128]{2,1,0:T(8,128)(2,1)} %get-tuple-element.561), channel_id=1, source_target_pairs={{0,1},{1,0},{2,3},{3,2},{4,5},{5,4},{6,7},{7,6},{8,9},{9,8},{10,11... | collective-permute-start | bytes 9437192 | tf_op jit(solution)/shard_map/ppermute | solution.py:943
  307.7 20.5 %collective-permute-start.49 = (bf16[384,1024]{1,0:T(8,128)(2,1)}, bf16[384,1024]{1,0:T(8,128)(2,1)S(1)}, u32[]{:S(2)}, u32[]{:S(2)}) collective-permute-start(bf16[384,1024]{1,0:T(8,128)(2,1)} %get-tuple-element.556), channel_id=1, source_target_pairs={{0,2},{1,3},{2,0},{3,1},{4,6},{5,7},{6,4},{7,5},{8,10},{9,11},{10,... | collective-permute-start | bytes 2359304 | tf_op jit(solution)/shard_map/ppermute | solution.py:943
  308.2 19.9 %collective-permute-start.50 = (bf16[384,1024]{1,0:T(8,128)(2,1)}, bf16[384,1024]{1,0:T(8,128)(2,1)S(1)}, u32[]{:S(2)}, u32[]{:S(2)}) collective-permute-start(bf16[384,1024]{1,0:T(8,128)(2,1)} %get-tuple-element.557), channel_id=1, source_target_pairs={{0,4},{1,5},{2,6},{3,7},{4,0},{5,1},{6,2},{7,3},{8,12},{9,13},{10,... | collective-permute-start | bytes 2359304 | tf_op jit(solution)/shard_map/ppermute | solution.py:943
  329.6 27.7 %collective-permute-start.55 = (bf16[768,1536]{1,0:T(8,128)(2,1)}, bf16[768,1536]{1,0:T(8,128)(2,1)S(1)}, u32[]{:S(2)}, u32[]{:S(2)}) collective-permute-start(bf16[768,1536]{1,0:T(8,128)(2,1)} %get-tuple-element.581), channel_id=1, source_target_pairs={{0,1},{1,0},{2,3},{3,2},{4,5},{5,4},{6,7},{7,6},{8,9},{9,8},{10,11... | collective-permute-start | bytes 7077896 | tf_op jit(solution)/shard_map/ppermute | solution.py:943
  333.1 21.8 %collective-permute-start.52 = (bf16[384,1024]{1,0:T(8,128)(2,1)}, bf16[384,1024]{1,0:T(8,128)(2,1)}, u32[]{:S(2)}, u32[]{:S(2)}) collective-permute-start(bf16[384,1024]{1,0:T(8,128)(2,1)} %get-tuple-element.575), channel_id=1, source_target_pairs={{0,24},{1,25},{2,26},{3,27},{4,28},{5,29},{6,30},{7,31},{8,0},{9,1... | collective-permute-start | bytes 2359304 | tf_op jit(solution)/shard_map/ppermute | solution.py:947
  337.2 20.0 %collective-permute-start.53 = (bf16[384,1024]{1,0:T(8,128)(2,1)}, bf16[384,1024]{1,0:T(8,128)(2,1)}, u32[]{:S(2)}, u32[]{:S(2)}) collective-permute-start(bf16[384,1024]{1,0:T(8,128)(2,1)} %get-tuple-element.576), channel_id=1, source_target_pairs={{0,2},{1,3},{2,0},{3,1},{4,6},{5,7},{6,4},{7,5},{8,10},{9,11},{10,... | collective-permute-start | bytes 2359304 | tf_op jit(solution)/shard_map/ppermute | solution.py:943
  337.5 19.7 %collective-permute-start.54 = (bf16[384,1024]{1,0:T(8,128)(2,1)}, bf16[384,1024]{1,0:T(8,128)(2,1)}, u32[]{:S(2)}, u32[]{:S(2)}) collective-permute-start(bf16[384,1024]{1,0:T(8,128)(2,1)} %get-tuple-element.577), channel_id=1, source_target_pairs={{0,4},{1,5},{2,6},{3,7},{4,0},{5,1},{6,2},{7,3},{8,12},{9,13},{10,... | collective-permute-start | bytes 2359304 | tf_op jit(solution)/shard_map/ppermute | solution.py:943
  361.2 22.7 %collective-permute-start.56 = (bf16[384,1024]{1,0:T(8,128)(2,1)}, bf16[384,1024]{1,0:T(8,128)(2,1)}, u32[]{:S(2)}, u32[]{:S(2)}) collective-permute-start(bf16[384,1024]{1,0:T(8,128)(2,1)} %get-tuple-element.591), channel_id=1, source_target_pairs={{0,24},{1,25},{2,26},{3,27},{4,28},{5,29},{6,30},{7,31},{8,0},{9,1... | collective-permute-start | bytes 2359304 | tf_op jit(solution)/shard_map/ppermute | solution.py:947
  363.6 20.3 %collective-permute-start.57 = (bf16[384,1024]{1,0:T(8,128)(2,1)}, bf16[384,1024]{1,0:T(8,128)(2,1)}, u32[]{:S(2)}, u32[]{:S(2)}) collective-permute-start(bf16[384,1024]{1,0:T(8,128)(2,1)} %get-tuple-element.592), channel_id=1, source_target_pairs={{0,2},{1,3},{2,0},{3,1},{4,6},{5,7},{6,4},{7,5},{8,10},{9,11},{10,... | collective-permute-start | bytes 2359304 | tf_op jit(solution)/shard_map/ppermute | solution.py:943
  364.0 20.0 %collective-permute-start.58 = (bf16[384,1024]{1,0:T(8,128)(2,1)}, bf16[384,1024]{1,0:T(8,128)(2,1)}, u32[]{:S(2)}, u32[]{:S(2)}) collective-permute-start(bf16[384,1024]{1,0:T(8,128)(2,1)} %get-tuple-element.593), channel_id=1, source_target_pairs={{0,4},{1,5},{2,6},{3,7},{4,0},{5,1},{6,2},{7,3},{8,12},{9,13},{10,... | collective-permute-start | bytes 2359304 | tf_op jit(solution)/shard_map/ppermute | solution.py:943
  387.1 19.8 %collective-permute-start.61 = (bf16[384,1024]{1,0:T(8,128)(2,1)}, bf16[384,1024]{1,0:T(8,128)(2,1)S(1)}, u32[]{:S(2)}, u32[]{:S(2)}) collective-permute-start(bf16[384,1024]{1,0:T(8,128)(2,1)} %get-tuple-element.624), channel_id=1, source_target_pairs={{0,24},{1,25},{2,26},{3,27},{4,28},{5,29},{6,30},{7,31},{8,0},{9,1... | collective-permute-start | bytes 2359304 | tf_op jit(solution)/shard_map/ppermute | solution.py:947
  412.3 29.0 %collective-permute-start.64 = (bf16[432,384]{1,0:T(8,128)(2,1)}, bf16[432,384]{1,0:T(8,128)(2,1)}, u32[]{:S(2)}, u32[]{:S(2)}) collective-permute-start(bf16[432,384]{1,0:T(8,128)(2,1)} %get-tuple-element.655), channel_id=1, source_target_pairs={{0,24},{1,25},{2,26},{3,27},{4,28},{5,29},{6,30},{7,31},{8,0},{9,1... | collective-permute-start | bytes 995336 | tf_op jit(solution)/shard_map/ppermute | solution.py:947
  (126 other events, 1611.3 us)

commit v11 on v10

--- a/solution.py
+++ b/solution.py
@@ -18,6 +18,7 @@
 BF16 = jnp.bfloat16
 F32 = jnp.float32
 VMEM = 61 << 20
+LESS = 34 << 20
 
 SUBS = 6
 RUNS = 8
@@ -411,7 +412,7 @@
             scratch_shapes=[pltpu.VMEM((512, WIDTH), BF16)],
         ),
         out_shape=[jax.ShapeDtypeStruct((FF, SIDE), BF16)] * 2,
-        compiler_params=params(VMEM),
+        compiler_params=params(LESS),
         cost_estimate=pl.CostEstimate(
             flops=2 * ROWS * WIDTH * FF, bytes_accessed=2 * ROWS * (WIDTH + FF), transcendentals=0
         ),
@@ -444,7 +445,7 @@
             ],
         ),
         out_shape=[jax.ShapeDtypeStruct((WIDTH, FF // 2), BF16)] * 2,
-        compiler_params=params(VMEM),
+        compiler_params=params(LESS),
         cost_estimate=pl.CostEstimate(
             flops=2 * ROWS * WIDTH * FF, bytes_accessed=2 * ROWS * (WIDTH + FF), transcendentals=0
         ),
@@ -482,7 +483,7 @@
             scratch_shapes=[pltpu.VMEM((WIDTH, WIDTH), F32)],
         ),
         out_shape=[jax.ShapeDtypeStruct((WIDTH, SIDE), BF16)] * 2,
-        compiler_params=params(VMEM),
+        compiler_params=params(LESS),
         cost_estimate=pl.CostEstimate(
             flops=2 * ROWS * WIDTH * WIDTH, bytes_accessed=4 * ROWS * WIDTH, transcendentals=0
         ),
@@ -524,7 +525,7 @@
             jax.ShapeDtypeStruct((2, HROWS, WIDTH), BF16),
             jax.ShapeDtypeStruct((2, HROWS, WIDTH), BF16),
         ],
-        compiler_params=params(VMEM),
+        compiler_params=params(LESS),
         cost_estimate=pl.CostEstimate(
             flops=2 * ROWS * WIDTH * FF, bytes_accessed=ROWS * (2 * FF + 7 * WIDTH), transcendentals=0
         ),
@@ -764,7 +765,7 @@
             jax.ShapeDtypeStruct((2, WIDTH, SIDE), BF16),
             jax.ShapeDtypeStruct((1, WIDTH), F32),
         ],
-        compiler_params=params(VMEM),
+        compiler_params=params(LESS),
         cost_estimate=pl.CostEstimate(
             flops=4 * 2 * LMAX * WIDTH * WIDTH, bytes_accessed=38 * LMAX * WIDTH, transcendentals=0
         ),
@@ -903,7 +904,7 @@
             out_specs=[held((PACK_VALUE, SIDE))] * 16,
         ),
         out_shape=[jax.ShapeDtypeStruct((PACK_VALUE, SIDE), BF16)] * 16,
-        compiler_params=params(VMEM),
+        compiler_params=params(LESS),
         cost_estimate=pl.CostEstimate(flops=0, bytes_accessed=3 * 16 * PACK_VALUE * SIDE * 2, transcendentals=0),
         name="collect",
     )(sc, *(x for _ in range(4) for x in sides))
@@ -918,18 +919,16 @@
 
 
 def run_add(groups, values, dtype):
-    rows, columns = values[0].shape
-    parts = 2 if columns == LMAX else 1
-    block = pl.BlockSpec((rows // parts, columns), lambda i: (i, 0))
+    shape = values[0].shape
+    here = pl.BlockSpec(memory_space=pltpu.VMEM)
     return pl.pallas_call(
         partial(add_kernel, groups),
-        grid=(parts,),
-        in_specs=[block] * len(values),
-        out_specs=[block] * len(groups),
-        out_shape=[jax.ShapeDtypeStruct((rows, columns), dtype)] * len(groups),
-        compiler_params=params(VMEM),
+        in_specs=[here] * len(values),
+        out_specs=[here] * len(groups),
+        out_shape=[jax.ShapeDtypeStruct(shape, dtype)] * len(groups),
+        compiler_params=params(LESS),
         cost_estimate=pl.CostEstimate(
-            flops=0, bytes_accessed=2 * rows * columns * (len(values) + len(groups)), transcendentals=0
+            flops=0, bytes_accessed=2 * shape[0] * shape[1] * (len(values) + len(groups)), transcendentals=0
         ),
         name="add",
     )(*values)
@@ -1079,12 +1078,12 @@
     have = scatter_add(have, got, 3)
 
     have, got = scatter_send(have, 4)
+    sums, sums_got = scatter_send(by_place(packed), 0)
     out_own, out_far = run_out(sc, active, resid, down)
-    have, got, packed, out_own, out_far = together((have, got, packed, out_own, out_far))
+    have, got, sums, sums_got, out_own, out_far = together((have, got, sums, sums_got, out_own, out_far))
     rand_sum = scatter_add(have, got, 4)[0, 0, 0].reshape(2, 3, HALF, LMAX)
 
-    sums, got = scatter_send(by_place(packed), 0)
-    sums, got = scatter_send(scatter_add(sums, got, 0), 1)
+    sums, got = scatter_send(scatter_add(sums, sums_got, 0), 1)
     output, tokens_grad, d_value, d_gain_one = run_close(
         sc, tokens, res_own, res_got, out_own, other(out_far), back_own, back_got, gain_one, value, value_far
     )

time: 514 us -> 495 us (0.963)
  Pallas kernels: 247 us -> 208 us
  local copies, waits for them, and re-layouts: 22.7 us -> 42.4 us
  starting transfers between devices: 81.4 us -> 73.3 us
    pallas_call x10, Pallas kernels: 28.6 us -> 5.58 us  [run_add(): pl.pallas_call(partial(add_kernel, groups), in_specs=[here] * len(values)...]
    unnamed x124 -> x188, local copies, waits for them, and re-layouts: 10.3 us -> 28.4 us
    ppermute x66, waiting for transfers between devices: 81.8 us -> 94.7 us  [swap(): return lax.ppermute(x, BOTH, [(d, d ^ bit) for d in range(DEVICES)])]
    ppermute x23, waiting for transfers between devices: 65.1 us -> 56.4 us  [ring(): lax.ppermute(x, BOTH, [(d, (d + 8 * way) % DEVICES) for d in range(DEVICE...]
    pallas_call x1, Pallas kernels: 8.63 us -> 2.11 us  [run_collect(): pl.pallas_call(collect_kernel, grid_spec=pltpu.PrefetchScalarGridSpec(num...]
    ppermute x23, starting transfers between devices: 32.8 us -> 26.5 us  [ring(): lax.ppermute(x, BOTH, [(d, (d + 8 * way) % DEVICES) for d in range(DEVICE...]
  transfers between devices with their start and end apart: 89 -> 89, of which waited for: 48 -> 50; matrix products, arithmetic and copies ran while one was open for 3% -> 3% of each run, Pallas kernels for 36% -> 30%
where the time goes in v11:
time: 495 us; the launch traced here: 489 us
  Pallas kernels  208 us (42%)
  waiting for transfers between devices  151 us (31%)
  starting transfers between devices  73.3 us (15%)
  local copies, waits for them, and re-layouts  42.4 us (9%)
  other arithmetic  13 us (3%)
    ppermute x66, waiting for transfers between devices, swap(): return lax.ppermute(x, BOTH, [(d, d ^ bit) for d in range(DEVICES)])  94.7 us
    ppermute x23, waiting for transfers between devices, ring(): lax.ppermute(x, BOTH, [(d, (d + 8 * way) % DEVICES) for d in range(DEVICE...  56.4 us
    ppermute x66, starting transfers between devices, swap(): return lax.ppermute(x, BOTH, [(d, d ^ bit) for d in range(DEVICES)])  46.7 us
    pallas_call x1, Pallas kernels, run_units(): pl.pallas_call(units_kernel, grid_spec=pltpu.PrefetchScalarGridSpec(num_s...  46.5 us
    unnamed x188, local copies, waits for them, and re-layouts  28.4 us
    pallas_call x2, Pallas kernels, run_unmix(): pl.pallas_call(partial(unmix_kernel, bool(carry)), grid_spec=pltpu.Prefet...  27.4 us
    ppermute x23, starting transfers between devices, ring(): lax.ppermute(x, BOTH, [(d, (d + 8 * way) % DEVICES) for d in range(DEVICE...  26.5 us
    pallas_call x2, Pallas kernels, run_mix(): pl.pallas_call(partial(mix_kernel, bool(carry)), grid_spec=pltpu.Prefetch...  21.2 us
  transfers between devices with their start and end apart: 89, of which 50 were waited for; matrix products, arithmetic and copies ran while one was open for 3% of the time, Pallas kernels for 30%

profile of v11, /device:TPU:0, one launch (start us, length us, event | category | flops | bytes accessed | tf_op | source)
XLA Modules:
  0.0 489.2 jit_solution(14458276781594913209)
XLA Ops:
  16.6 6.2 %collective-permute-done.5.refs_1_ = bf16[496,384]{1,0:T(8,128)(2,1)S(1)} collective-permute-done((bf16[496,384]{1,0:T(8,128)(2,1)}, bf16[496,384]{1,0:T(8,128)(2,1)S(1)}, u32[]{:S(2)}, u32[]{:S(2)}) %collective-permute-start.5) | collective-permute-done | bytes 380960 | tf_op jit(solution)/shard_map/ppermute | solution.py:942
  30.9 9.8 %collective-permute-done.10.refs_5_ = bf16[496,384]{1,0:T(8,128)(2,1)S(1)} collective-permute-done((bf16[496,384]{1,0:T(8,128)(2,1)S(1)}, bf16[496,384]{1,0:T(8,128)(2,1)S(1)}, u32[]{:S(2)}, u32[]{:S(2)}) %collective-permute-start.10) | collective-permute-done | bytes 380960 | tf_op jit(solution)/shard_map/ppermute | solution.py:942
  44.8 7.7 %collective-permute-done.13.refs_6_ = bf16[496,384]{1,0:T(8,128)(2,1)S(1)} collective-permute-done((bf16[496,384]{1,0:T(8,128)(2,1)S(1)}, bf16[496,384]{1,0:T(8,128)(2,1)S(1)}, u32[]{:S(2)}, u32[]{:S(2)}) %collective-permute-start.13) | collective-permute-done | bytes 380960 | tf_op jit(solution)/shard_map/ppermute | solution.py:942
  58.9 6.8 %collective-permute-done.17.refs_7_ = bf16[496,384]{1,0:T(8,128)(2,1)S(1)} collective-permute-done((bf16[496,384]{1,0:T(8,128)(2,1)S(1)}, bf16[496,384]{1,0:T(8,128)(2,1)S(1)}, u32[]{:S(2)}, u32[]{:S(2)}) %collective-permute-start.17) | collective-permute-done | bytes 380960 | tf_op jit(solution)/shard_map/ppermute | solution.py:946
  67.9 5.6 %collective-permute-done.21.refs_11_ = bf16[496,384]{1,0:T(8,128)(2,1)S(1)} collective-permute-done((bf16[496,384]{1,0:T(8,128)(2,1)S(1)}, bf16[496,384]{1,0:T(8,128)(2,1)S(1)}, u32[]{:S(2)}, u32[]{:S(2)}) %collective-permute-start.21) | collective-permute-done | bytes 380960 | tf_op jit(solution)/shard_map/ppermute | solution.py:942
  80.1 7.2 %place.1 = (bf16[3072,384]{1,0:T(8,128)(2,1)}, bf16[768,1536]{1,0:T(8,128)(2,1)}, bf16[768,384]{1,0:T(8,128)(2,1)}, bf16[768,384]{1,0:T(8,128)(2,1)}, bf16[256,384]{1,0:T(8,128)(2,1)}) custom-call(s32[7]{0:T(128)} %concatenate.54.sc, bf16[496,384]{1,0:T(8,128)(2,1)} %pack.1.refs_0_, bf16[496,384]{1,0:T(8,128)(2,1)} %copy-done.67, ...), custom_call_target="tpu_custom_call" | custom-call | bytes 12189696 | tf_op jit(solution)/shard_map/place/pallas_call | solution.py:848
  98.9 7.8 %values.1.refs_8_.v_own = bf16[12,1024,128]{2,1,0:T(8,128)(2,1)} custom-call(s32[7]{0:T(128)} %concatenate.54.sc, bf16[2,1024,768]{2,1,0:T(8,128)(2,1)} %tok.1, f32[1,768]{1,0:T(1,128)} %reshape.205.gain, bf16[768,384]{1,0:T(8,128)(2,1)} %get-tuple-element.433.w_own, bf16[768,384]{1,0:T(8,128)(2,1)} %copy-done.40), custom_call_target="tpu_custom_call" | custom-call | flops 2415919104 | bytes 6291456 | tf_op jit(solution)/shard_map/values/pallas_call | solution.py:81
  118.9 15.6 %collective-permute-done.32.refs_6_ = bf16[384,1024]{1,0:T(8,128)(2,1)} collective-permute-done((bf16[384,1024]{1,0:T(8,128)(2,1)}, bf16[384,1024]{1,0:T(8,128)(2,1)}, u32[]{:S(2)}, u32[]{:S(2)}) %collective-permute-start.32) | collective-permute-done | bytes 786464 | tf_op jit(solution)/shard_map/ppermute | solution.py:942
  140.5 18.0 %collective-permute-done.36.refs_7_ = bf16[384,1024]{1,0:T(8,128)(2,1)} collective-permute-done((bf16[384,1024]{1,0:T(8,128)(2,1)}, bf16[384,1024]{1,0:T(8,128)(2,1)}, u32[]{:S(2)}, u32[]{:S(2)}) %collective-permute-start.36) | collective-permute-done | bytes 786464 | tf_op jit(solution)/shard_map/ppermute | solution.py:946
  160.7 10.6 %mix.2 = (bf16[12,512,256]{2,1,0:T(8,128)(2,1)}, f32[12,512,256]{2,1,0:T(8,128)}, bf16[12,512,1024]{2,1,0:T(8,128)(2,1)}, bf16[12,512,256]{2,1,0:T(8,128)(2,1)}) custom-call(s32[7]{0:T(128)} %concatenate.54.sc, bf16[384,1024]{1,0:T(8,128)(2,1)} %bitcast.124, bf16[384,1024]{1,0:T(8,128)(2,1)} %collective-permute-done.24.refs_1_, ...), custom_call_target="tpu_custom_call" | custom-call | flops 3221225472 | bytes 20447232 | tf_op jit(solution)/shard_map/mix/pallas_call | solution.py:190
  171.3 5.1 %collective-permute-done.39.refs_3_ = bf16[384,1024]{1,0:T(8,128)(2,1)} collective-permute-done((bf16[384,1024]{1,0:T(8,128)(2,1)}, bf16[384,1024]{1,0:T(8,128)(2,1)}, u32[]{:S(2)}, u32[]{:S(2)}) %collective-permute-start.39) | collective-permute-done | bytes 786464 | tf_op jit(solution)/shard_map/ppermute | solution.py:942
  179.8 10.6 %mix.3 = (bf16[12,512,256]{2,1,0:T(8,128)(2,1)}, f32[12,512,256]{2,1,0:T(8,128)}, bf16[12,512,1024]{2,1,0:T(8,128)(2,1)}, bf16[12,512,256]{2,1,0:T(8,128)(2,1)}) custom-call(s32[7]{0:T(128)} %concatenate.54.sc, bf16[384,1024]{1,0:T(8,128)(2,1)} %collective-permute-done.30.refs_0_, ...), custom_call_target="tpu_custom_call", output_to_operand_aliasing={{0}: (11, {}), {1}: (12, {}), {2}: (13, {}), {3}: (14, {})} | custom-call | flops 3221225472 | bytes 20447232 | tf_op jit(solution)/shard_map/mix/pallas_call | solution.py:190
  190.4 12.4 %pre.1 = (bf16[4,512,768]{2,1,0:T(8,128)(2,1)}, bf16[4,512,768]{2,1,0:T(8,128)(2,1)}, bf16[4,512,768]{2,1,0:T(8,128)(2,1)}, bf16[4,512,768]{2,1,0:T(8,128)(2,1)}) custom-call(s32[7]{0:T(128)} %concatenate.54.sc, bf16[2,8,2,64,768]{4,3,2,1,0:T(8,128)(2,1)} %bitcast.106, bf16[2,8,64,768]{3,2,1,0:T(8,128)(2,1)} %copy-done.61, ...), custom_call_target="tpu_custom_call" | custom-call | flops 2415919104 | bytes 25165824 | tf_op jit(solution)/shard_map/pre/pallas_call | solution.py:271
  202.8 46.5 %units.1 = (bf16[2048,3072]{1,0:T(8,128)(2,1)}, bf16[2048,3072]{1,0:T(8,128)(2,1)}, bf16[2048,768]{1,0:T(8,128)(2,1)}) custom-call(s32[7]{0:T(128)} %concatenate.54.sc, bf16[2048,768]{1,0:T(8,128)(2,1)} %bitcast.112, bf16[2048,768]{1,0:T(8,128)(2,1)} %bitcast.110, bf16[768,1536]{1,0:T(8,128)(2,1)} %get-tuple-element.502.up_own, ...), custom_call_target="tpu_custom_call" | custom-call | flops 28991029248 | bytes 37748736 | tf_op jit(solution)/shard_map/units/pallas_call | solution.py:365
  249.3 12.7 %post.1 = (bf16[2,512,768]{2,1,0:T(8,128)(2,1)}, bf16[2,512,768]{2,1,0:T(8,128)(2,1)}, bf16[12,512,256]{2,1,0:T(8,128)(2,1)}, f32[1,768]{1,0:T(1,128)}) custom-call(s32[7]{0:T(128)} %concatenate.54.sc, bf16[4,512,768]{2,1,0:T(8,128)(2,1)} %get-tuple-element.499.resid, bf16[4,512,768]{2,1,0:T(8,128)(2,1)} %bitcast.144, ...), custom_call_target="tpu_custom_call" | custom-call | flops 4831838208 | bytes 44040192 | tf_op jit(solution)/shard_map/post/pallas_call | solution.py:574
  262.2 13.8 %unmix.2 = (bf16[384,1024]{1,0:T(8,128)(2,1)}, bf16[384,1024]{1,0:T(8,128)(2,1)}, bf16[384,1024]{1,0:T(8,128)(2,1)}, bf16[384,1024]{1,0:T(8,128)(2,1)}, bf16[384...) custom-call(s32[7]{0:T(128)} %concatenate.54.sc, ...), custom_call_target="tpu_custom_call" | custom-call | flops 4831838208 | bytes 33030144 | tf_op jit(solution)/shard_map/unmix/pallas_call | solution.py:659
  282.1 13.6 %unmix.3 = (bf16[384,1024]{1,0:T(8,128)(2,1)}, bf16[384,1024]{1,0:T(8,128)(2,1)}, bf16[384,1024]{1,0:T(8,128)(2,1)}, bf16[384,1024]{1,0:T(8,128)(2,1)}, bf16[384...) custom-call(s32[7]{0:T(128)} %concatenate.54.sc, ...), custom_call_target="tpu_custom_call", output_to_operand_aliasing={{8}: (7, {}), {9}: (8, {})} | custom-call | flops 4831838208 | bytes 33030144 | tf_op jit(solution)/shard_map/unmix/pallas_call | solution.py:659
  312.5 14.0 %up_grad.1 = (bf16[768,1536]{1,0:T(8,128)(2,1)S(1)}, bf16[768,1536]{1,0:T(8,128)(2,1)}) custom-call(s32[7]{0:T(128)S(1)} %copy-done.28, bf16[2048,768]{1,0:T(8,128)(2,1)S(1)} %bitcast.113, bf16[2048,3072]{1,0:T(8,128)(2,1)S(1)} %copy-done.55), custom_call_target="tpu_custom_call" | custom-call | flops 9663676416 | bytes 15728640 | tf_op jit(solution)/shard_map/up_grad/pallas_call | solution.py:436
  334.0 13.8 %down_grad.1 = (bf16[3072,384]{1,0:T(8,128)(2,1)S(1)}, bf16[3072,384]{1,0:T(8,128)(2,1)}) custom-call(s32[7]{0:T(128)S(1)} %copy-done.28, bf16[2048,3072]{1,0:T(8,128)(2,1)S(1)} %copy-done.50, bf16[2048,768]{1,0:T(8,128)(2,1)S(1)} %bitcast.111), custom_call_target="tpu_custom_call" | custom-call | flops 9663676416 | bytes 15728640 | tf_op jit(solution)/shard_map/down_grad/pallas_call | solution.py:405
  355.2 5.3 %out_grad.1 = (bf16[768,384]{1,0:T(8,128)(2,1)S(1)}, bf16[768,384]{1,0:T(8,128)(2,1)S(1)}) custom-call(s32[7]{0:T(128)S(1)} %copy-done.28, bf16[4,512,768]{2,1,0:T(8,128)(2,1)S(1)} %copy-done.31, bf16[2,512,768]{2,1,0:T(8,128)(2,1)S(1)} %copy-done.51, bf16[2,512,768]{2,1,0:T(8,128)(2,1)S(1)} %copy-done.38), custom_call_target="tpu_custom_call" | custom-call | flops 2415919104 | bytes 6291456 | tf_op jit(solution)/shard_map/out_grad/pallas_call | solution.py:476
  382.6 15.0 %out.3 = (bf16[2,512,768]{2,1,0:T(8,128)(2,1)S(1)}, bf16[2,512,768]{2,1,0:T(8,128)(2,1)S(1)}) custom-call(s32[7]{0:T(128)S(1)} %copy-done.28, bf16[4,512,3072]{2,1,0:T(8,128)(2,1)} %bitcast.116, bf16[4,512,768]{2,1,0:T(8,128)(2,1)S(1)} %copy-done.30, bf16[3072,384]{1,0:T(8,128)(2,1)S(1)} %copy-done.35, bf16[3072,384]{1,0:T(8,128)(2,1)} %collective-permute-done.43.dn_far), custom_call_target="tpu_custom_call" | custom-call | flops 9663676416 | bytes 23592960 | tf_op jit(solution)/shard_map/out/pallas_call | solution.py:510
  409.8 13.7 %close.1 = (f32[2,8,2,64,768]{4,3,2,1,0:T(8,128)}, f32[2,8,2,64,768]{4,3,2,1,0:T(8,128)}, bf16[2,768,384]{2,1,0:T(8,128)(2,1)S(1)}, f32[1,768]{1,0:T(1,128)S(1)}) custom-call(s32[7]{0:T(128)S(1)} %copy-done.28, bf16[2,8,2,64,768]{4,3,2,1,0:T(8,128)(2,1)S(1)} %bitcast.107, bf16[2,8,64,768]{3,2,1,0:T(8,128)(2,1)S(1)} %bitcast.117, ...), custom_call_target="tpu_custom_call" | custom-call | flops 4831838208 | bytes 29884416 | tf_op jit(solution)/shard_map/close/pallas_call | solution.py:751
  443.4 5.4 %collective-permute-done.75 = bf16[4,2,64,384]{3,2,1,0:T(8,128)(2,1)} collective-permute-done((bf16[4,2,64,384]{3,2,1,0:T(8,128)(2,1)}, bf16[4,2,64,384]{3,2,1,0:T(8,128)(2,1)}, u32[]{:S(2)}, u32[]{:S(2)}) %collective-permute-start.75) | collective-permute-done | bytes 393248 | tf_op jit(solution)/shard_map/ppermute | solution.py:942
  450.0 5.1 %collective-permute-done.72.refs_1_ = bf16[432,384]{1,0:T(8,128)(2,1)S(1)} collective-permute-done((bf16[432,384]{1,0:T(8,128)(2,1)S(1)}, bf16[432,384]{1,0:T(8,128)(2,1)S(1)}, u32[]{:S(2)}, u32[]{:S(2)}) %collective-permute-start.72) | collective-permute-done | bytes 331808 | tf_op jit(solution)/shard_map/ppermute | solution.py:942
  (416 shorter events, 204.9 us)
Async XLA Ops:
  114.2 23.6 %collective-permute-start.35 = (bf16[12,1024,128]{2,1,0:T(8,128)(2,1)}, bf16[12,1024,128]{2,1,0:T(8,128)(2,1)}, u32[]{:S(2)}, u32[]{:S(2)}) collective-permute-start(bf16[12,1024,128]{2,1,0:T(8,128)(2,1)} %values.1.refs_8_.v_own), channel_id=1, source_target_pairs={{0,1},{1,0},{2,3},{3,2},{4,5},{5,4},{6,7},{7,6},{8,9},{9,8},{10,11... | collective-permute-start | bytes 9437192 | tf_op jit(solution)/shard_map/ppermute | solution.py:942
  114.2 20.3 %collective-permute-start.32 = (bf16[384,1024]{1,0:T(8,128)(2,1)}, bf16[384,1024]{1,0:T(8,128)(2,1)}, u32[]{:S(2)}, u32[]{:S(2)}) collective-permute-start(bf16[384,1024]{1,0:T(8,128)(2,1)} %collective-permute-done.26.refs_4_), channel_id=1, source_target_pairs={{0,4},{1,5},{2,6},{3,7},{4,0},{5,1},{6,2},{7,3},{8,12},{9,13},{10,... | collective-permute-start | bytes 2359304 | tf_op jit(solution)/shard_map/ppermute | solution.py:942
  114.7 20.0 %collective-permute-start.33 = (bf16[384,1024]{1,0:T(8,128)(2,1)}, bf16[384,1024]{1,0:T(8,128)(2,1)}, u32[]{:S(2)}, u32[]{:S(2)}) collective-permute-start(bf16[384,1024]{1,0:T(8,128)(2,1)} %collective-permute-done.30.refs_0_), channel_id=1, source_target_pairs={{0,2},{1,3},{2,0},{3,1},{4,6},{5,7},{6,4},{7,5},{8,10},{9,11},{10,... | collective-permute-start | bytes 2359304 | tf_op jit(solution)/shard_map/ppermute | solution.py:942
  116.4 21.4 %collective-permute-start.34 = (bf16[384,1024]{1,0:T(8,128)(2,1)}, bf16[384,1024]{1,0:T(8,128)(2,1)S(1)}, u32[]{:S(2)}, u32[]{:S(2)}) collective-permute-start(bf16[384,1024]{1,0:T(8,128)(2,1)} %collective-permute-done.30.refs_0_), channel_id=1, source_target_pairs={{0,8},{1,9},{2,10},{3,11},{4,12},{5,13},{6,14},{7,15},{8,16},{9,17... | collective-permute-start | bytes 2359304 | tf_op jit(solution)/shard_map/ppermute | solution.py:946
  137.8 20.7 %collective-permute-start.36 = (bf16[384,1024]{1,0:T(8,128)(2,1)}, bf16[384,1024]{1,0:T(8,128)(2,1)}, u32[]{:S(2)}, u32[]{:S(2)}) collective-permute-start(bf16[384,1024]{1,0:T(8,128)(2,1)} %collective-permute-done.28.refs_3_), channel_id=1, source_target_pairs={{0,8},{1,9},{2,10},{3,11},{4,12},{5,13},{6,14},{7,15},{8,16},{9,17... | collective-permute-start | bytes 2359304 | tf_op jit(solution)/shard_map/ppermute | solution.py:946
  138.5 20.0 %collective-permute-start.37 = (bf16[384,1024]{1,0:T(8,128)(2,1)}, bf16[384,1024]{1,0:T(8,128)(2,1)}, u32[]{:S(2)}, u32[]{:S(2)}) collective-permute-start(bf16[384,1024]{1,0:T(8,128)(2,1)} %collective-permute-done.30.refs_0_), channel_id=1, source_target_pairs={{0,4},{1,5},{2,6},{3,7},{4,0},{5,1},{6,2},{7,3},{8,12},{9,13},{10,... | collective-permute-start | bytes 2359304 | tf_op jit(solution)/shard_map/ppermute | solution.py:942
  178.6 24.2 %collective-permute-start.42 = (bf16[768,1536]{1,0:T(8,128)(2,1)}, bf16[768,1536]{1,0:T(8,128)(2,1)}, u32[]{:S(2)}, u32[]{:S(2)}) collective-permute-start(bf16[768,1536]{1,0:T(8,128)(2,1)} %get-tuple-element.502.up_own), channel_id=1, source_target_pairs={{0,1},{1,0},{2,3},{3,2},{4,5},{5,4},{6,7},{7,6},{8,9},{9,8},{10,11... | collective-permute-start | bytes 7077896 | tf_op jit(solution)/shard_map/ppermute | solution.py:942
  178.6 24.2 %collective-permute-start.43 = (bf16[3072,384]{1,0:T(8,128)(2,1)S(1)}, bf16[3072,384]{1,0:T(8,128)(2,1)}, u32[]{:S(2)}, u32[]{:S(2)}) collective-permute-start(bf16[3072,384]{1,0:T(8,128)(2,1)S(1)} %copy-done.34), channel_id=1, source_target_pairs={{0,1},{1,0},{2,3},{3,2},{4,5},{5,4},{6,7},{7,6},{8,9},{9,8},{10,11... | collective-permute-start | bytes 7077896 | tf_op jit(solution)/shard_map/ppermute | solution.py:942
  277.2 20.1 %collective-permute-start.45 = (bf16[384,1024]{1,0:T(8,128)(2,1)}, bf16[384,1024]{1,0:T(8,128)(2,1)S(1)}, u32[]{:S(2)}, u32[]{:S(2)}) collective-permute-start(bf16[384,1024]{1,0:T(8,128)(2,1)} %get-tuple-element.525), channel_id=1, source_target_pairs={{0,24},{1,25},{2,26},{3,27},{4,28},{5,29},{6,30},{7,31},{8,0},{9,1... | collective-permute-start | bytes 2359304 | tf_op jit(solution)/shard_map/ppermute | solution.py:946
  300.3 26.3 %collective-permute-start.51 = (bf16[12,1024,128]{2,1,0:T(8,128)(2,1)}, bf16[12,1024,128]{2,1,0:T(8,128)(2,1)}, u32[]{:S(2)}, u32[]{:S(2)}) collective-permute-start(bf16[12,1024,128]{2,1,0:T(8,128)(2,1)} %get-tuple-element.561), channel_id=1, source_target_pairs={{0,1},{1,0},{2,3},{3,2},{4,5},{5,4},{6,7},{7,6},{8,9},{9,8},{10,11... | collective-permute-start | bytes 9437192 | tf_op jit(solution)/shard_map/ppermute | solution.py:942
  302.1 24.4 %collective-permute-start.49 = (bf16[384,1024]{1,0:T(8,128)(2,1)S(1)}, bf16[384,1024]{1,0:T(8,128)(2,1)S(1)}, u32[]{:S(2)}, u32[]{:S(2)}) collective-permute-start(bf16[384,1024]{1,0:T(8,128)(2,1)S(1)} %get-tuple-element.556), channel_id=1, source_target_pairs={{0,2},{1,3},{2,0},{3,1},{4,6},{5,7},{6,4},{7,5},{8,10},{9,11},{10,... | collective-permute-start | bytes 2359304 | tf_op jit(solution)/shard_map/ppermute | solution.py:942
  302.5 24.0 %collective-permute-start.50 = (bf16[384,1024]{1,0:T(8,128)(2,1)S(1)}, bf16[384,1024]{1,0:T(8,128)(2,1)S(1)}, u32[]{:S(2)}, u32[]{:S(2)}) collective-permute-start(bf16[384,1024]{1,0:T(8,128)(2,1)S(1)} %get-tuple-element.557), channel_id=1, source_target_pairs={{0,4},{1,5},{2,6},{3,7},{4,0},{5,1},{6,2},{7,3},{8,12},{9,13},{10,... | collective-permute-start | bytes 2359304 | tf_op jit(solution)/shard_map/ppermute | solution.py:942
  304.1 22.4 %collective-permute-start.48 = (bf16[384,1024]{1,0:T(8,128)(2,1)S(1)}, bf16[384,1024]{1,0:T(8,128)(2,1)S(1)}, u32[]{:S(2)}, u32[]{:S(2)}) collective-permute-start(bf16[384,1024]{1,0:T(8,128)(2,1)S(1)} %copy-done.92), channel_id=1, source_target_pairs={{0,24},{1,25},{2,26},{3,27},{4,28},{5,29},{6,30},{7,31},{8,0},{9,1... | collective-permute-start | bytes 2359304 | tf_op jit(solution)/shard_map/ppermute | solution.py:946
  326.6 22.0 %collective-permute-start.55 = (bf16[768,1536]{1,0:T(8,128)(2,1)}, bf16[768,1536]{1,0:T(8,128)(2,1)S(1)}, u32[]{:S(2)}, u32[]{:S(2)}) collective-permute-start(bf16[768,1536]{1,0:T(8,128)(2,1)} %get-tuple-element.581), channel_id=1, source_target_pairs={{0,1},{1,0},{2,3},{3,2},{4,5},{5,4},{6,7},{7,6},{8,9},{9,8},{10,11... | collective-permute-start | bytes 7077896 | tf_op jit(solution)/shard_map/ppermute | solution.py:942
  328.0 20.1 %collective-permute-start.52 = (bf16[384,1024]{1,0:T(8,128)(2,1)}, bf16[384,1024]{1,0:T(8,128)(2,1)S(1)}, u32[]{:S(2)}, u32[]{:S(2)}) collective-permute-start(bf16[384,1024]{1,0:T(8,128)(2,1)} %get-tuple-element.575), channel_id=1, source_target_pairs={{0,24},{1,25},{2,26},{3,27},{4,28},{5,29},{6,30},{7,31},{8,0},{9,1... | collective-permute-start | bytes 2359304 | tf_op jit(solution)/shard_map/ppermute | solution.py:946
  349.0 20.0 %collective-permute-start.56 = (bf16[384,1024]{1,0:T(8,128)(2,1)S(1)}, bf16[384,1024]{1,0:T(8,128)(2,1)S(1)}, u32[]{:S(2)}, u32[]{:S(2)}) collective-permute-start(bf16[384,1024]{1,0:T(8,128)(2,1)S(1)} %get-tuple-element.591), channel_id=1, source_target_pairs={{0,24},{1,25},{2,26},{3,27},{4,28},{5,29},{6,30},{7,31},{8,0},{9,1... | collective-permute-start | bytes 2359304 | tf_op jit(solution)/shard_map/ppermute | solution.py:946
  373.4 27.1 %collective-permute-start.61 = (bf16[384,1024]{1,0:T(8,128)(2,1)S(1)}, bf16[384,1024]{1,0:T(8,128)(2,1)S(1)}, u32[]{:S(2)}, u32[]{:S(2)}) collective-permute-start(bf16[384,1024]{1,0:T(8,128)(2,1)S(1)} %get-tuple-element.624), channel_id=1, source_target_pairs={{0,24},{1,25},{2,26},{3,27},{4,28},{5,29},{6,30},{7,31},{8,0},{9,1... | collective-permute-start | bytes 2359304 | tf_op jit(solution)/shard_map/ppermute | solution.py:946
  375.0 25.4 %collective-permute-start.62 = (bf16[384,1024]{1,0:T(8,128)(2,1)S(1)}, bf16[384,1024]{1,0:T(8,128)(2,1)S(1)}, u32[]{:S(2)}, u32[]{:S(2)}) collective-permute-start(bf16[384,1024]{1,0:T(8,128)(2,1)S(1)} %get-tuple-element.625), channel_id=1, source_target_pairs={{0,2},{1,3},{2,0},{3,1},{4,6},{5,7},{6,4},{7,5},{8,10},{9,11},{10,... | collective-permute-start | bytes 2359304 | tf_op jit(solution)/shard_map/ppermute | solution.py:942
  375.4 25.0 %collective-permute-start.63 = (bf16[384,1024]{1,0:T(8,128)(2,1)S(1)}, bf16[384,1024]{1,0:T(8,128)(2,1)S(1)}, u32[]{:S(2)}, u32[]{:S(2)}) collective-permute-start(bf16[384,1024]{1,0:T(8,128)(2,1)S(1)} %copy-done.90), channel_id=1, source_target_pairs={{0,4},{1,5},{2,6},{3,7},{4,0},{5,1},{6,2},{7,3},{8,12},{9,13},{10,... | collective-permute-start | bytes 2359304 | tf_op jit(solution)/shard_map/ppermute | solution.py:942
  376.4 23.7 %collective-permute-start.65 = (bf16[432,384]{1,0:T(8,128)(2,1)S(1)}, bf16[432,384]{1,0:T(8,128)(2,1)S(1)}, u32[]{:S(2)}, u32[]{:S(2)}) collective-permute-start(bf16[432,384]{1,0:T(8,128)(2,1)S(1)} %get-tuple-element.641), channel_id=1, source_target_pairs={{0,2},{1,3},{2,0},{3,1},{4,6},{5,7},{6,4},{7,5},{8,10},{9,11},{10,... | collective-permute-start | bytes 995336 | tf_op jit(solution)/shard_map/ppermute | solution.py:942
  400.8 22.7 %collective-permute-start.68 = (bf16[432,384]{1,0:T(8,128)(2,1)S(1)}, bf16[432,384]{1,0:T(8,128)(2,1)S(1)}, u32[]{:S(2)}, u32[]{:S(2)}) collective-permute-start(bf16[432,384]{1,0:T(8,128)(2,1)S(1)} %get-tuple-element.661), channel_id=1, source_target_pairs={{0,2},{1,3},{2,0},{3,1},{4,6},{5,7},{6,4},{7,5},{8,10},{9,11},{10,... | collective-permute-start | bytes 995336 | tf_op jit(solution)/shard_map/ppermute | solution.py:942
  402.3 21.9 %collective-permute-start.69 = (bf16[432,384]{1,0:T(8,128)(2,1)S(1)}, bf16[432,384]{1,0:T(8,128)(2,1)S(1)}, u32[]{:S(2)}, u32[]{:S(2)}) collective-permute-start(bf16[432,384]{1,0:T(8,128)(2,1)S(1)} %get-tuple-element.662), channel_id=1, source_target_pairs={{0,4},{1,5},{2,6},{3,7},{4,0},{5,1},{6,2},{7,3},{8,12},{9,13},{10,... | collective-permute-start | bytes 995336 | tf_op jit(solution)/shard_map/ppermute | solution.py:942
  403.2 21.7 %collective-permute-start.67 = (bf16[432,384]{1,0:T(8,128)(2,1)S(1)}, bf16[432,384]{1,0:T(8,128)(2,1)S(1)}, u32[]{:S(2)}, u32[]{:S(2)}) collective-permute-start(bf16[432,384]{1,0:T(8,128)(2,1)S(1)} %get-tuple-element.655), channel_id=1, source_target_pairs={{0,24},{1,25},{2,26},{3,27},{4,28},{5,29},{6,30},{7,31},{8,0},{9,1... | collective-permute-start | bytes 995336 | tf_op jit(solution)/shard_map/ppermute | solution.py:946
  443.4 21.5 %collective-permute-start.80 = (f32[3,64,1024]{2,1,0:T(8,128)}, f32[3,64,1024]{2,1,0:T(8,128)}, u32[]{:S(2)}, u32[]{:S(2)}) collective-permute-start(f32[3,64,1024]{2,1,0:T(8,128)} %get-tuple-element.727), channel_id=1, source_target_pairs={{0,1},{1,0},{2,3},{3,2},{4,5},{5,4},{6,7},{7,6},{8,9},{9,8},{10,11... | collective-permute-start | bytes 2359304 | tf_op jit(solution)/shard_map/ppermute | solution.py:942
  (158 other events, 2009.1 us)

commit v12 on v11

--- a/solution.py
+++ b/solution.py
@@ -317,7 +317,7 @@
     return (0, lax.max(f - FSIDE, 0))
 
 
-def units_kernel(sc, normed, cot, up_own, up_far, dn_own, dn_far, active, up_grad, back, w_up, w_down, total):
+def units_kernel(sc, normed, cot, up_own, up_far, dn_own, dn_far, active, up_grad, w_up, w_down):
     step = pl.program_id(0)
     w_down[:, own_lanes(sc)] = dn_own[...]
     w_down[:, far_lanes(sc)] = dn_far[...]
@@ -330,35 +330,20 @@
     def _():
         w_up[...] = up_far[...]
 
-    for piece in range(ROWS // TILE):
-        whole = slice(piece * TILE, (piece + 1) * TILE)
-        for row in range(piece * TILE, (piece + 1) * TILE, 256):
-            rows = slice(row, row + 256)
-            for column in range(0, FSTEP, 256):
-                columns = slice(column, column + 256)
-                up = dot(normed[rows], w_up[:, columns], 1, 0)
-                square = up * up
-                bend = jnp.tanh(up * (0.7978845608028654 + (0.044715 * 0.7978845608028654) * square))
-                share = 0.5 + 0.5 * bend
-                act = up * share
-                active[rows, columns] = act.astype(BF16)
-                slope = share + act * (1.0 - share) * (
-                    2 * 0.7978845608028654 + (6 * 0.044715 * 0.7978845608028654) * square
-                )
-                up_grad[rows, columns] = (dot(cot[rows], w_down[columns], 1, 1) * slope).astype(BF16)
-        two_grad = dot(up_grad[whole], w_up[...], 1, 1)
-
-        @pl.when(step == 0)
-        def _():
-            total[whole] = two_grad
-
-        @pl.when((step > 0) & (step < 2 * FSIDE - 1))
-        def _():
-            total[whole] += two_grad
-
-        @pl.when(step == 2 * FSIDE - 1)
-        def _():
-            back[whole] = (total[whole] + two_grad).astype(BF16)
+    for row in range(0, ROWS, 256):
+        rows = slice(row, row + 256)
+        for column in range(0, FSTEP, 256):
+            columns = slice(column, column + 256)
+            up = dot(normed[rows], w_up[:, columns], 1, 0)
+            square = up * up
+            bend = jnp.tanh(up * (0.7978845608028654 + (0.044715 * 0.7978845608028654) * square))
+            share = 0.5 + 0.5 * bend
+            act = up * share
+            active[rows, columns] = act.astype(BF16)
+            slope = share + act * (1.0 - share) * (
+                2 * 0.7978845608028654 + (6 * 0.044715 * 0.7978845608028654) * square
+            )
+            up_grad[rows, columns] = (dot(cot[rows], w_down[columns], 1, 1) * slope).astype(BF16)
 
 
 def run_units(sc, normed, cotangent, up, down):
@@ -375,21 +360,13 @@
                 spec((FSTEP, SIDE), unit_rows),
                 spec((FSTEP, SIDE), unit_rows),
             ],
-            out_specs=[spec((ROWS, FSTEP), unit_columns), spec((ROWS, FSTEP), unit_columns), held((ROWS, WIDTH))],
-            scratch_shapes=[
-                pltpu.VMEM((WIDTH, FSTEP), BF16),
-                pltpu.VMEM((FSTEP, WIDTH), BF16),
-                pltpu.VMEM((ROWS, WIDTH), F32),
-            ],
-        ),
-        out_shape=[
-            jax.ShapeDtypeStruct((ROWS, FF), BF16),
-            jax.ShapeDtypeStruct((ROWS, FF), BF16),
-            jax.ShapeDtypeStruct((ROWS, WIDTH), BF16),
-        ],
+            out_specs=[spec((ROWS, FSTEP), unit_columns), spec((ROWS, FSTEP), unit_columns)],
+            scratch_shapes=[pltpu.VMEM((WIDTH, FSTEP), BF16), pltpu.VMEM((FSTEP, WIDTH), BF16)],
+        ),
+        out_shape=[jax.ShapeDtypeStruct((ROWS, FF), BF16), jax.ShapeDtypeStruct((ROWS, FF), BF16)],
         compiler_params=params(VMEM),
         cost_estimate=pl.CostEstimate(
-            flops=6 * ROWS * WIDTH * FF, bytes_accessed=8 * ROWS * WIDTH + 4 * ROWS * FF, transcendentals=ROWS * FF
+            flops=4 * ROWS * WIDTH * FF, bytes_accessed=6 * ROWS * WIDTH + 4 * ROWS * FF, transcendentals=ROWS * FF
         ),
         name="units",
     )(sc, normed.reshape(ROWS, WIDTH), cotangent.reshape(ROWS, WIDTH), *up, *down)
@@ -412,7 +389,7 @@
             scratch_shapes=[pltpu.VMEM((512, WIDTH), BF16)],
         ),
         out_shape=[jax.ShapeDtypeStruct((FF, SIDE), BF16)] * 2,
-        compiler_params=params(LESS),
+        compiler_params=params(57 << 20),
         cost_estimate=pl.CostEstimate(
             flops=2 * ROWS * WIDTH * FF, bytes_accessed=2 * ROWS * (WIDTH + FF), transcendentals=0
         ),
@@ -445,7 +422,7 @@
             ],
         ),
         out_shape=[jax.ShapeDtypeStruct((WIDTH, FF // 2), BF16)] * 2,
-        compiler_params=params(LESS),
+        compiler_params=params(57 << 20),
         cost_estimate=pl.CostEstimate(
             flops=2 * ROWS * WIDTH * FF, bytes_accessed=2 * ROWS * (WIDTH + FF), transcendentals=0
         ),
@@ -533,7 +510,7 @@
     )(sc, active.reshape(4, HROWS, FF), resid, *down)
 
 
-def post_kernel(sc, resid, back, cot, wo_own, wo_far, gain, *refs):
+def post_kernel(sc, resid, grad_own, grad_far, cot, up_own, up_far, wo_own, wo_far, gain, *refs):
     (res_own, res_far, heads, d_gain, weight, spread) = refs
     step = pl.program_id(0)
     whole_weight(sc, step, wo_own, wo_far, weight)
@@ -542,7 +519,9 @@
     res = resid[...].reshape(shape).astype(F32)
     scale = lax.rsqrt(jnp.mean(res * res, axis=-1, keepdims=True) + EPSILON)
     unit = res * scale
-    two_grad = jnp.where(valid, back[...].reshape(shape).astype(F32), 0.0)
+    units = (4 * SPAN, FF // 2)
+    back = dot(grad_own[...].reshape(units), up_own[...], 1, 1) + dot(grad_far[...].reshape(units), up_far[...], 1, 1)
+    two_grad = jnp.where(valid, back, 0.0)
     gained = two_grad * gain[...]
     masked = cot[...].reshape(shape).astype(F32)
     grad = masked + scale * (gained - unit * jnp.mean(gained * unit, axis=-1, keepdims=True))
@@ -569,14 +548,25 @@
             heads[2 * pair + 1, :, half] = jnp.concatenate([one[:, HEAD:], two[:, HEAD:]], axis=1)
 
 
-def run_post(sc, resid, back, cotangent, wo, gain):
-    whole = (4, HROWS, WIDTH)
+def run_post(sc, resid, up_grad, cotangent, up, wo, gain):
+    side = lambda which: spec((4, SPAN, FF // 2), lambda r, s: (0, r, s[CORE] if which == 0 else 1 - s[CORE]))
+    up_grad = up_grad.reshape(4, HROWS, FF)
     return pl.pallas_call(
         post_kernel,
         grid_spec=pltpu.PrefetchScalarGridSpec(
             num_scalar_prefetch=1,
             grid=(HROWS // SPAN,),
-            in_specs=[slab_spec()] * 3 + [held((WIDTH, SIDE)), held((WIDTH, SIDE)), held((1, WIDTH))],
+            in_specs=[
+                slab_spec(),
+                side(0),
+                side(1),
+                slab_spec(),
+                held((WIDTH, FF // 2)),
+                held((WIDTH, FF // 2)),
+                held((WIDTH, SIDE)),
+                held((WIDTH, SIDE)),
+                held((1, WIDTH)),
+            ],
             out_specs=[slab_spec(2)] * 2 + [heads_spec(), held((1, WIDTH))],
             scratch_shapes=[
                 pltpu.VMEM((WIDTH, WIDTH), BF16),
@@ -591,10 +581,10 @@
         ],
         compiler_params=params(VMEM),
         cost_estimate=pl.CostEstimate(
-            flops=4 * ROWS * WIDTH * WIDTH, bytes_accessed=28 * ROWS * WIDTH, transcendentals=0
+            flops=2 * ROWS * WIDTH * (WIDTH + FF), bytes_accessed=ROWS * (16 * WIDTH + 2 * FF), transcendentals=0
         ),
         name="post",
-    )(sc, resid, back.reshape(whole), cotangent, *wo, gain)
+    )(sc, resid, up_grad, up_grad, cotangent, *up, *wo, gain)
 
 
 def unmix_kernel(carried, sc, v_own, v_far, grad_heads, mean, exps, inverse, *refs):
@@ -1050,8 +1040,8 @@
     down, up = (down, other(down)), (up, other(up))
 
     mixed, resid, normed, masked = run_pre(sc, tokens, tokens_far, grad_out, grad_far, heads, out, gain_two)
-    active, up_grad, back = run_units(sc, normed, masked, up, down)
-    res_own, res_far, grad_heads, d_gain_two = run_post(sc, resid, back, masked, out, gain_two)
+    active, up_grad = run_units(sc, normed, masked, up, down)
+    res_own, res_far, grad_heads, d_gain_two = run_post(sc, resid, up_grad, masked, up, out, gain_two)
 
     backward = lambda planes, carry: run_unmix(sc, planes, v_own, v_far, grad_heads, mean, exps, inverse, carry)
     *far, back_own, back_far = backward((3, 2), ())
@@ -1062,56 +1052,57 @@
     have = {**scatter_add(have, got, 0), **by_place(near, (1, 0))}
 
     have, got = scatter_send(have, 1)
+    out_own, out_far = run_out(sc, active, resid, down)
+    have, got, out_own, out_far, back_got = together((have, got, out_own, out_far, other(back_far)))
+    have = scatter_add(have, got, 1)
+
+    have, got = scatter_send(have, 2)
     up_own, up_far = run_up_grad(sc, normed, up_grad)
-    have, got, up_own, up_far, back_got = together((have, got, up_own, up_far, other(back_far)))
-    have = scatter_add(have, got, 1)
-
-    have, got = scatter_send(have, 2)
+    have, got, up_own, up_far, out_got = together((have, got, up_own, up_far, other(out_far)))
+    have = scatter_add(have, got, 2)
+
+    have, got = scatter_send(have, 3)
     down_own, down_far = run_down_grad(sc, active, masked)
     have, got, down_own, down_far, up_got = together((have, got, down_own, down_far, other(up_far)))
-    have = scatter_add(have, got, 2)
-
-    have, got = scatter_send(have, 3)
+    have = scatter_add(have, got, 3)
+
+    have, got = scatter_send(have, 4)
     d_out_own, d_out_far = run_out_grad(sc, mixed, res_own, res_far)
     packed = run_collect(sc, down_own, other(down_far), up_own, up_got, d_out_own, other(d_out_far))
     have, got, packed = together((have, got, packed))
-    have = scatter_add(have, got, 3)
-
-    have, got = scatter_send(have, 4)
-    sums, sums_got = scatter_send(by_place(packed), 0)
-    out_own, out_far = run_out(sc, active, resid, down)
-    have, got, sums, sums_got, out_own, out_far = together((have, got, sums, sums_got, out_own, out_far))
     rand_sum = scatter_add(have, got, 4)[0, 0, 0].reshape(2, 3, HALF, LMAX)
 
-    sums, got = scatter_send(scatter_add(sums, sums_got, 0), 1)
+    sums, got = scatter_send(by_place(packed), 0)
     output, tokens_grad, d_value, d_gain_one = run_close(
-        sc, tokens, res_own, res_got, out_own, other(out_far), back_own, back_got, gain_one, value, value_far
-    )
-    sums, got, output, tokens_grad, d_value, d_gain_one = together(
-        (sums, got, output, tokens_grad, d_value, d_gain_one)
-    )
-    sums = scatter_add(sums, got, 1)
-
-    sums, got = scatter_send(sums, 2)
+        sc, tokens, res_own, res_got, out_own, out_got, back_own, back_got, gain_one, value, value_far
+    )
     gain_pair = jnp.concatenate([d_gain_one, d_gain_two]).reshape(2, 16, 1, 48).astype(BF16)
     gain_pair = jnp.pad(gain_pair, ((0, 0), (0, 0), (0, 15), (0, SIDE - 48)))
     small = jnp.concatenate([d_value.reshape(2, 16, 48, SIDE), gain_pair], 2)
+    sums, got, output, tokens_grad, small = together((sums, got, output, tokens_grad, small))
+    sums = scatter_add(sums, got, 0)
+
+    sums, got = scatter_send(sums, 1)
     small = add_low(pick(small, core), other(pick(small, 1 - core))).reshape(4, 2, 2, 64, SIDE)
+    sums, got, small = together((sums, got, small))
+    sums = scatter_add(sums, got, 1)
+
+    sums, got = scatter_send(sums, 2)
     small = add_low(pick(small, x, 2), swap(pick(small, 1 - x, 2), TO_X))
     sums, got, small = together((sums, got, small))
     sums = scatter_add(sums, got, 2)
 
     sums, got = scatter_send(sums, 3)
     small = add_low(pick(small, y, 1), swap(pick(small, 1 - y, 1), TO_Y))
-    blocks, blocks_far = pick(rand_sum, core), other(pick(rand_sum, 1 - core))
-    sums, got, small, blocks, blocks_far = together((sums, got, small, blocks, blocks_far))
+    sums, got, small = together((sums, got, small))
     sums = scatter_add(sums, got, 3)
 
     sums, got = scatter_send(sums, 4)
     small_sum = pick(small, z).astype(F32)
     for k in range(1, PLANES):
         small_sum = small_sum + ring(pick(small, lax.rem(z + PLANES - k, PLANES)), -k).astype(F32)
-    sums, got, small_sum = together((sums, got, small_sum))
+    blocks, blocks_far = pick(rand_sum, core), other(pick(rand_sum, 1 - core))
+    sums, got, small_sum, blocks, blocks_far = together((sums, got, small_sum, blocks, blocks_far))
     big_sum = scatter_add(sums, got, 4)[0, 0, 0]
     big_far, small_far = other(big_sum), other(small_sum)
 

time: 495 us -> 503 us (1.016)
  Pallas kernels: 208 us -> 217 us
  waiting for transfers between devices: 151 us -> 143 us
    ppermute x66, waiting for transfers between devices: 94.7 us -> 67.7 us  [swap(): return lax.ppermute(x, BOTH, [(d, d ^ bit) for d in range(DEVICES)])]
    ppermute x23, waiting for transfers between devices: 56.4 us -> 75.6 us  [ring(): lax.ppermute(x, BOTH, [(d, (d + 8 * way) % DEVICES) for d in range(DEVICE...]
    pallas_call x1, Pallas kernels: 46.5 us -> 30.2 us  [run_units(): pl.pallas_call(units_kernel, grid_spec=pltpu.PrefetchScalarGridSpec(num_s...]
    pallas_call x1, Pallas kernels: 12.7 us -> 28.1 us  [run_post(): pl.pallas_call(post_kernel, grid_spec=pltpu.PrefetchScalarGridSpec(num_sc...]
    pallas_call x10, Pallas kernels: 5.58 us -> 11.7 us  [run_add(): pl.pallas_call(partial(add_kernel, groups), in_specs=[here] * len(values)...]
    unnamed x188 -> x198, local copies, waits for them, and re-layouts: 28.4 us -> 30.1 us
  transfers between devices with their start and end apart: 89 -> 89, of which waited for: 50 -> 39; matrix products, arithmetic and copies ran while one was open for 3% -> 4% of each run, Pallas kernels for 30% -> 32%
where the time goes in v12:
time: 503 us; the launch traced here: 496 us
  Pallas kernels  217 us (43%)
  waiting for transfers between devices  143 us (28%)
  starting transfers between devices  76.5 us (15%)
  local copies, waits for them, and re-layouts  44.5 us (9%)
  other arithmetic  13.2 us (3%)
    ppermute x23, waiting for transfers between devices, ring(): lax.ppermute(x, BOTH, [(d, (d + 8 * way) % DEVICES) for d in range(DEVICE...  75.6 us
    ppermute x66, waiting for transfers between devices, swap(): return lax.ppermute(x, BOTH, [(d, d ^ bit) for d in range(DEVICES)])  67.7 us
    ppermute x66, starting transfers between devices, swap(): return lax.ppermute(x, BOTH, [(d, d ^ bit) for d in range(DEVICES)])  48.8 us
    pallas_call x1, Pallas kernels, run_units(): pl.pallas_call(units_kernel, grid_spec=pltpu.PrefetchScalarGridSpec(num_s...  30.2 us
    unnamed x198, local copies, waits for them, and re-layouts  30.1 us
    pallas_call x1, Pallas kernels, run_post(): pl.pallas_call(post_kernel, grid_spec=pltpu.PrefetchScalarGridSpec(num_sc...  28.1 us
    ppermute x23, starting transfers between devices, ring(): lax.ppermute(x, BOTH, [(d, (d + 8 * way) % DEVICES) for d in range(DEVICE...  27.7 us
    pallas_call x2, Pallas kernels, run_unmix(): pl.pallas_call(partial(unmix_kernel, bool(carry)), grid_spec=pltpu.Prefet...  27.2 us
  transfers between devices with their start and end apart: 89, of which 39 were waited for; matrix products, arithmetic and copies ran while one was open for 4% of the time, Pallas kernels for 32%

profile of v12, /device:TPU:0, one launch (start us, length us, event | category | flops | bytes accessed | tf_op | source)
XLA Modules:
  0.0 496.5 jit_solution(4756160130090782952)
XLA Ops:
  16.5 8.3 %collective-permute-done.7.refs_4_ = bf16[496,384]{1,0:T(8,128)(2,1)S(1)} collective-permute-done((bf16[496,384]{1,0:T(8,128)(2,1)}, bf16[496,384]{1,0:T(8,128)(2,1)S(1)}, u32[]{:S(2)}, u32[]{:S(2)}) %collective-permute-start.7) | collective-permute-done | bytes 380960 | tf_op jit(solution)/shard_map/ppermute | solution.py:936
  31.5 7.3 %collective-permute-done.9.refs_3_ = bf16[496,384]{1,0:T(8,128)(2,1)S(1)} collective-permute-done((bf16[496,384]{1,0:T(8,128)(2,1)S(1)}, bf16[496,384]{1,0:T(8,128)(2,1)S(1)}, u32[]{:S(2)}, u32[]{:S(2)}) %collective-permute-start.9) | collective-permute-done | bytes 380960 | tf_op jit(solution)/shard_map/ppermute | solution.py:932
  45.0 6.2 %collective-permute-done.13.refs_6_ = bf16[496,384]{1,0:T(8,128)(2,1)S(1)} collective-permute-done((bf16[496,384]{1,0:T(8,128)(2,1)S(1)}, bf16[496,384]{1,0:T(8,128)(2,1)S(1)}, u32[]{:S(2)}, u32[]{:S(2)}) %collective-permute-start.13) | collective-permute-done | bytes 380960 | tf_op jit(solution)/shard_map/ppermute | solution.py:932
  57.5 6.4 %collective-permute-done.17.refs_7_ = bf16[496,384]{1,0:T(8,128)(2,1)S(1)} collective-permute-done((bf16[496,384]{1,0:T(8,128)(2,1)S(1)}, bf16[496,384]{1,0:T(8,128)(2,1)S(1)}, u32[]{:S(2)}, u32[]{:S(2)}) %collective-permute-start.17) | collective-permute-done | bytes 380960 | tf_op jit(solution)/shard_map/ppermute | solution.py:936
  66.7 5.0 %collective-permute-done.23.refs_15_ = bf16[496,384]{1,0:T(8,128)(2,1)S(1)} collective-permute-done((bf16[496,384]{1,0:T(8,128)(2,1)S(1)}, bf16[496,384]{1,0:T(8,128)(2,1)S(1)}, u32[]{:S(2)}, u32[]{:S(2)}) %collective-permute-start.23) | collective-permute-done | bytes 380960 | tf_op jit(solution)/shard_map/ppermute | solution.py:932
  78.0 7.2 %place.1 = (bf16[3072,384]{1,0:T(8,128)(2,1)}, bf16[768,1536]{1,0:T(8,128)(2,1)}, bf16[768,384]{1,0:T(8,128)(2,1)}, bf16[768,384]{1,0:T(8,128)(2,1)}, bf16[256,384]{1,0:T(8,128)(2,1)}) custom-call(s32[7]{0:T(128)} %concatenate.54.sc, bf16[496,384]{1,0:T(8,128)(2,1)} %pack.1.refs_0_, bf16[496,384]{1,0:T(8,128)(2,1)} %copy-done.77, ...), custom_call_target="tpu_custom_call" | custom-call | bytes 12189696 | tf_op jit(solution)/shard_map/place/pallas_call | solution.py:838
  95.8 7.8 %values.1.refs_8_.v_own = bf16[12,1024,128]{2,1,0:T(8,128)(2,1)} custom-call(s32[7]{0:T(128)} %concatenate.54.sc, bf16[2,1024,768]{2,1,0:T(8,128)(2,1)} %tok.1, f32[1,768]{1,0:T(1,128)} %reshape.205.gain, bf16[768,384]{1,0:T(8,128)(2,1)} %get-tuple-element.433.w_own, bf16[768,384]{1,0:T(8,128)(2,1)} %copy-done.54), custom_call_target="tpu_custom_call" | custom-call | flops 2415919104 | bytes 6291456 | tf_op jit(solution)/shard_map/values/pallas_call | solution.py:81
  112.5 18.2 %collective-permute-done.32.refs_6_ = bf16[384,1024]{1,0:T(8,128)(2,1)} collective-permute-done((bf16[384,1024]{1,0:T(8,128)(2,1)}, bf16[384,1024]{1,0:T(8,128)(2,1)}, u32[]{:S(2)}, u32[]{:S(2)}) %collective-permute-start.32) | collective-permute-done | bytes 786464 | tf_op jit(solution)/shard_map/ppermute | solution.py:932
  135.2 18.8 %collective-permute-done.36.refs_7_ = bf16[384,1024]{1,0:T(8,128)(2,1)} collective-permute-done((bf16[384,1024]{1,0:T(8,128)(2,1)}, bf16[384,1024]{1,0:T(8,128)(2,1)}, u32[]{:S(2)}, u32[]{:S(2)}) %collective-permute-start.36) | collective-permute-done | bytes 786464 | tf_op jit(solution)/shard_map/ppermute | solution.py:936
  156.3 10.6 %mix.2 = (bf16[12,512,256]{2,1,0:T(8,128)(2,1)}, f32[12,512,256]{2,1,0:T(8,128)}, bf16[12,512,1024]{2,1,0:T(8,128)(2,1)}, bf16[12,512,256]{2,1,0:T(8,128)(2,1)}) custom-call(s32[7]{0:T(128)} %concatenate.54.sc, bf16[384,1024]{1,0:T(8,128)(2,1)} %bitcast.119, bf16[384,1024]{1,0:T(8,128)(2,1)} %collective-permute-done.24.refs_1_, ...), custom_call_target="tpu_custom_call" | custom-call | flops 3221225472 | bytes 20447232 | tf_op jit(solution)/shard_map/mix/pallas_call | solution.py:190
  166.9 5.4 %collective-permute-done.41.refs_7_ = bf16[384,1024]{1,0:T(8,128)(2,1)} collective-permute-done((bf16[384,1024]{1,0:T(8,128)(2,1)}, bf16[384,1024]{1,0:T(8,128)(2,1)}, u32[]{:S(2)}, u32[]{:S(2)}) %collective-permute-start.41) | collective-permute-done | bytes 786464 | tf_op jit(solution)/shard_map/ppermute | solution.py:932
  176.6 10.6 %mix.3 = (bf16[12,512,256]{2,1,0:T(8,128)(2,1)}, f32[12,512,256]{2,1,0:T(8,128)}, bf16[12,512,1024]{2,1,0:T(8,128)(2,1)}, bf16[12,512,256]{2,1,0:T(8,128)(2,1)}) custom-call(s32[7]{0:T(128)} %concatenate.54.sc, bf16[384,1024]{1,0:T(8,128)(2,1)} %collective-permute-done.30.refs_0_, ...), custom_call_target="tpu_custom_call", output_to_operand_aliasing={{0}: (11, {}), {1}: (12, {}), {2}: (13, {}), {3}: (14, {})} | custom-call | flops 3221225472 | bytes 20447232 | tf_op jit(solution)/shard_map/mix/pallas_call | solution.py:190
  187.2 12.4 %pre.1 = (bf16[4,512,768]{2,1,0:T(8,128)(2,1)}, bf16[4,512,768]{2,1,0:T(8,128)(2,1)}, bf16[4,512,768]{2,1,0:T(8,128)(2,1)}, bf16[4,512,768]{2,1,0:T(8,128)(2,1)}) custom-call(s32[7]{0:T(128)} %concatenate.54.sc, bf16[2,8,2,64,768]{4,3,2,1,0:T(8,128)(2,1)} %bitcast.106, bf16[2,8,64,768]{3,2,1,0:T(8,128)(2,1)} %copy-done.69, ...), custom_call_target="tpu_custom_call" | custom-call | flops 2415919104 | bytes 25165824 | tf_op jit(solution)/shard_map/pre/pallas_call | solution.py:271
  199.7 30.2 %units.1 = (bf16[2048,3072]{1,0:T(8,128)(2,1)}, bf16[2048,3072]{1,0:T(8,128)(2,1)}) custom-call(s32[7]{0:T(128)} %concatenate.54.sc, bf16[2048,768]{1,0:T(8,128)(2,1)} %bitcast.139, bf16[2048,768]{1,0:T(8,128)(2,1)} %bitcast.137, bf16[768,1536]{1,0:T(8,128)(2,1)} %get-tuple-element.502.up_own, bf16[768,1536]{1,0:T(8,128)(2,1)} %collective-permute-done.42.up_far, ...), custom_call_target="tpu_custom_call" | custom-call | flops 19327352832 | bytes 34603008 | tf_op jit(solution)/shard_map/units/pallas_call | solution.py:350
  229.9 28.1 %post.1 = (bf16[2,512,768]{2,1,0:T(8,128)(2,1)}, bf16[2,512,768]{2,1,0:T(8,128)(2,1)}, bf16[12,512,256]{2,1,0:T(8,128)(2,1)}, f32[1,768]{1,0:T(1,128)}) custom-call(s32[7]{0:T(128)} %concatenate.54.sc, bf16[4,512,768]{2,1,0:T(8,128)(2,1)} %get-tuple-element.499.resid, bf16[4,512,3072]{2,1,0:T(8,128)(2,1)} %bitcast.142, bf16[4,512,3072]{2,1,0:T(8,128)(2,1)} %bitcast.143, ...), custom_call_target="tpu_custom_call" | custom-call | flops 12079595520 | bytes 37748736 | tf_op jit(solution)/shard_map/post/pallas_call | solution.py:554
  258.0 13.6 %unmix.2 = (bf16[384,1024]{1,0:T(8,128)(2,1)}, bf16[384,1024]{1,0:T(8,128)(2,1)}, bf16[384,1024]{1,0:T(8,128)(2,1)}, bf16[384,1024]{1,0:T(8,128)(2,1)}, bf16[384...) custom-call(s32[7]{0:T(128)} %concatenate.54.sc, ...), custom_call_target="tpu_custom_call" | custom-call | flops 4831838208 | bytes 33030144 | tf_op jit(solution)/shard_map/unmix/pallas_call | solution.py:649
  276.0 13.7 %unmix.3 = (bf16[384,1024]{1,0:T(8,128)(2,1)}, bf16[384,1024]{1,0:T(8,128)(2,1)}, bf16[384,1024]{1,0:T(8,128)(2,1)}, bf16[384,1024]{1,0:T(8,128)(2,1)}, bf16[384...) custom-call(s32[7]{0:T(128)} %concatenate.54.sc, ...), custom_call_target="tpu_custom_call", output_to_operand_aliasing={{8}: (7, {}), {9}: (8, {})} | custom-call | flops 4831838208 | bytes 33030144 | tf_op jit(solution)/shard_map/unmix/pallas_call | solution.py:649
  301.6 15.0 %out.3 = (bf16[2,512,768]{2,1,0:T(8,128)(2,1)S(1)}, bf16[2,512,768]{2,1,0:T(8,128)(2,1)S(1)}) custom-call(s32[7]{0:T(128)S(1)} %copy-done.38, bf16[4,512,3072]{2,1,0:T(8,128)(2,1)} %bitcast.141, bf16[4,512,768]{2,1,0:T(8,128)(2,1)S(1)} %copy-done.44, bf16[3072,384]{1,0:T(8,128)(2,1)S(1)} %copy-done.46, bf16[3072,384]{1,0:T(8,128)(2,1)} %collective-permute-done.43.dn_far), custom_call_target="tpu_custom_call" | custom-call | flops 9663676416 | bytes 23592960 | tf_op jit(solution)/shard_map/out/pallas_call | solution.py:487
  323.4 16.1 %up_grad.1 = (bf16[768,1536]{1,0:T(8,128)(2,1)}, bf16[768,1536]{1,0:T(8,128)(2,1)}) custom-call(s32[7]{0:T(128)} %concatenate.54.sc, bf16[2048,768]{1,0:T(8,128)(2,1)} %bitcast.140, bf16[2048,3072]{1,0:T(8,128)(2,1)} %get-tuple-element.504.up_grad), custom_call_target="tpu_custom_call" | custom-call | flops 9663676416 | bytes 15728640 | tf_op jit(solution)/shard_map/up_grad/pallas_call | solution.py:413
  351.7 15.6 %down_grad.1 = (bf16[3072,384]{1,0:T(8,128)(2,1)}, bf16[3072,384]{1,0:T(8,128)(2,1)}) custom-call(s32[7]{0:T(128)} %concatenate.54.sc, bf16[2048,3072]{1,0:T(8,128)(2,1)} %get-tuple-element.558.active, bf16[2048,768]{1,0:T(8,128)(2,1)} %bitcast.138), custom_call_target="tpu_custom_call" | custom-call | flops 9663676416 | bytes 15728640 | tf_op jit(solution)/shard_map/down_grad/pallas_call | solution.py:382
  379.5 5.3 %out_grad.1 = (bf16[768,384]{1,0:T(8,128)(2,1)S(1)}, bf16[768,384]{1,0:T(8,128)(2,1)S(1)}) custom-call(s32[7]{0:T(128)S(1)} %copy-done.39, bf16[4,512,768]{2,1,0:T(8,128)(2,1)S(1)} %copy-done.41, bf16[2,512,768]{2,1,0:T(8,128)(2,1)S(1)} %copy-done.60, bf16[2,512,768]{2,1,0:T(8,128)(2,1)S(1)} %copy-done.49), custom_call_target="tpu_custom_call" | custom-call | flops 2415919104 | bytes 6291456 | tf_op jit(solution)/shard_map/out_grad/pallas_call | solution.py:453
  405.7 13.0 %close.1 = (f32[2,8,2,64,768]{4,3,2,1,0:T(8,128)}, f32[2,8,2,64,768]{4,3,2,1,0:T(8,128)}, bf16[2,768,384]{2,1,0:T(8,128)(2,1)S(1)}, f32[1,768]{1,0:T(1,128)S(1)}) custom-call(s32[7]{0:T(128)S(1)} %copy-done.39, bf16[2,8,2,64,768]{4,3,2,1,0:T(8,128)(2,1)S(1)} %bitcast.107, bf16[2,8,64,768]{3,2,1,0:T(8,128)(2,1)S(1)} %bitcast.112, ...), custom_call_target="tpu_custom_call" | custom-call | flops 4831838208 | bytes 29884416 | tf_op jit(solution)/shard_map/close/pallas_call | solution.py:741
  427.1 5.1 %collective-permute-done.68.refs_0_ = bf16[432,384]{1,0:T(8,128)(2,1)S(1)} collective-permute-done((bf16[432,384]{1,0:T(8,128)(2,1)}, bf16[432,384]{1,0:T(8,128)(2,1)S(1)}, u32[]{:S(2)}, u32[]{:S(2)}) %collective-permute-start.68) | collective-permute-done | bytes 331808 | tf_op jit(solution)/shard_map/ppermute | solution.py:936
  475.3 4.6 collective-permute-done.85
  (426 shorter events, 209.9 us)
Async XLA Ops:
  110.4 22.6 %collective-permute-start.35 = (bf16[12,1024,128]{2,1,0:T(8,128)(2,1)}, bf16[12,1024,128]{2,1,0:T(8,128)(2,1)}, u32[]{:S(2)}, u32[]{:S(2)}) collective-permute-start(bf16[12,1024,128]{2,1,0:T(8,128)(2,1)} %values.1.refs_8_.v_own), channel_id=1, source_target_pairs={{0,1},{1,0},{2,3},{3,2},{4,5},{5,4},{6,7},{7,6},{8,9},{9,8},{10,11... | collective-permute-start | bytes 9437192 | tf_op jit(solution)/shard_map/ppermute | solution.py:932
  110.4 20.3 %collective-permute-start.32 = (bf16[384,1024]{1,0:T(8,128)(2,1)}, bf16[384,1024]{1,0:T(8,128)(2,1)}, u32[]{:S(2)}, u32[]{:S(2)}) collective-permute-start(bf16[384,1024]{1,0:T(8,128)(2,1)} %collective-permute-done.26.refs_4_), channel_id=1, source_target_pairs={{0,4},{1,5},{2,6},{3,7},{4,0},{5,1},{6,2},{7,3},{8,12},{9,13},{10,... | collective-permute-start | bytes 2359304 | tf_op jit(solution)/shard_map/ppermute | solution.py:932
  111.3 21.7 %collective-permute-start.34 = (bf16[384,1024]{1,0:T(8,128)(2,1)}, bf16[384,1024]{1,0:T(8,128)(2,1)S(1)}, u32[]{:S(2)}, u32[]{:S(2)}) collective-permute-start(bf16[384,1024]{1,0:T(8,128)(2,1)} %collective-permute-done.30.refs_0_), channel_id=1, source_target_pairs={{0,8},{1,9},{2,10},{3,11},{4,12},{5,13},{6,14},{7,15},{8,16},{9,17... | collective-permute-start | bytes 2359304 | tf_op jit(solution)/shard_map/ppermute | solution.py:936
  112.0 21.0 %collective-permute-start.33 = (bf16[384,1024]{1,0:T(8,128)(2,1)}, bf16[384,1024]{1,0:T(8,128)(2,1)S(1)}, u32[]{:S(2)}, u32[]{:S(2)}) collective-permute-start(bf16[384,1024]{1,0:T(8,128)(2,1)} %collective-permute-done.30.refs_0_), channel_id=1, source_target_pairs={{0,2},{1,3},{2,0},{3,1},{4,6},{5,7},{6,4},{7,5},{8,10},{9,11},{10,... | collective-permute-start | bytes 2359304 | tf_op jit(solution)/shard_map/ppermute | solution.py:932
  133.0 21.0 %collective-permute-start.36 = (bf16[384,1024]{1,0:T(8,128)(2,1)}, bf16[384,1024]{1,0:T(8,128)(2,1)}, u32[]{:S(2)}, u32[]{:S(2)}) collective-permute-start(bf16[384,1024]{1,0:T(8,128)(2,1)} %collective-permute-done.28.refs_3_), channel_id=1, source_target_pairs={{0,8},{1,9},{2,10},{3,11},{4,12},{5,13},{6,14},{7,15},{8,16},{9,17... | collective-permute-start | bytes 2359304 | tf_op jit(solution)/shard_map/ppermute | solution.py:936
  133.5 20.5 %collective-permute-start.37 = (bf16[384,1024]{1,0:T(8,128)(2,1)}, bf16[384,1024]{1,0:T(8,128)(2,1)}, u32[]{:S(2)}, u32[]{:S(2)}) collective-permute-start(bf16[384,1024]{1,0:T(8,128)(2,1)} %collective-permute-done.30.refs_0_), channel_id=1, source_target_pairs={{0,4},{1,5},{2,6},{3,7},{4,0},{5,1},{6,2},{7,3},{8,12},{9,13},{10,... | collective-permute-start | bytes 2359304 | tf_op jit(solution)/shard_map/ppermute | solution.py:932
  155.2 20.2 %collective-permute-start.40 = (bf16[384,1024]{1,0:T(8,128)(2,1)}, bf16[384,1024]{1,0:T(8,128)(2,1)}, u32[]{:S(2)}, u32[]{:S(2)}) collective-permute-start(bf16[384,1024]{1,0:T(8,128)(2,1)} %collective-permute-done.37.refs_2_), channel_id=1, source_target_pairs={{0,8},{1,9},{2,10},{3,11},{4,12},{5,13},{6,14},{7,15},{8,16},{9,17... | collective-permute-start | bytes 2359304 | tf_op jit(solution)/shard_map/ppermute | solution.py:936
  175.4 24.2 %collective-permute-start.42 = (bf16[768,1536]{1,0:T(8,128)(2,1)}, bf16[768,1536]{1,0:T(8,128)(2,1)}, u32[]{:S(2)}, u32[]{:S(2)}) collective-permute-start(bf16[768,1536]{1,0:T(8,128)(2,1)} %get-tuple-element.502.up_own), channel_id=1, source_target_pairs={{0,1},{1,0},{2,3},{3,2},{4,5},{5,4},{6,7},{7,6},{8,9},{9,8},{10,11... | collective-permute-start | bytes 7077896 | tf_op jit(solution)/shard_map/ppermute | solution.py:932
  175.5 24.2 %collective-permute-start.43 = (bf16[3072,384]{1,0:T(8,128)(2,1)S(1)}, bf16[3072,384]{1,0:T(8,128)(2,1)}, u32[]{:S(2)}, u32[]{:S(2)}) collective-permute-start(bf16[3072,384]{1,0:T(8,128)(2,1)S(1)} %copy-done.45), channel_id=1, source_target_pairs={{0,1},{1,0},{2,3},{3,2},{4,5},{5,4},{6,7},{7,6},{8,9},{9,8},{10,11... | collective-permute-start | bytes 7077896 | tf_op jit(solution)/shard_map/ppermute | solution.py:932
  272.8 20.1 %collective-permute-start.45 = (bf16[384,1024]{1,0:T(8,128)(2,1)}, bf16[384,1024]{1,0:T(8,128)(2,1)S(1)}, u32[]{:S(2)}, u32[]{:S(2)}) collective-permute-start(bf16[384,1024]{1,0:T(8,128)(2,1)} %get-tuple-element.525), channel_id=1, source_target_pairs={{0,24},{1,25},{2,26},{3,27},{4,28},{5,29},{6,30},{7,31},{8,0},{9,1... | collective-permute-start | bytes 2359304 | tf_op jit(solution)/shard_map/ppermute | solution.py:936
  294.8 23.6 %collective-permute-start.51 = (bf16[12,1024,128]{2,1,0:T(8,128)(2,1)}, bf16[12,1024,128]{2,1,0:T(8,128)(2,1)S(1)}, u32[]{:S(2)}, u32[]{:S(2)}) collective-permute-start(bf16[12,1024,128]{2,1,0:T(8,128)(2,1)} %get-tuple-element.561), channel_id=1, source_target_pairs={{0,1},{1,0},{2,3},{3,2},{4,5},{5,4},{6,7},{7,6},{8,9},{9,8},{10,11... | collective-permute-start | bytes 9437192 | tf_op jit(solution)/shard_map/ppermute | solution.py:932
  294.8 21.8 %collective-permute-start.48 = (bf16[384,1024]{1,0:T(8,128)(2,1)}, bf16[384,1024]{1,0:T(8,128)(2,1)S(1)}, u32[]{:S(2)}, u32[]{:S(2)}) collective-permute-start(bf16[384,1024]{1,0:T(8,128)(2,1)} %get-tuple-element.550), channel_id=1, source_target_pairs={{0,24},{1,25},{2,26},{3,27},{4,28},{5,29},{6,30},{7,31},{8,0},{9,1... | collective-permute-start | bytes 2359304 | tf_op jit(solution)/shard_map/ppermute | solution.py:936
  318.4 25.1 %collective-permute-start.55 = (bf16[2,512,768]{2,1,0:T(8,128)(2,1)S(1)}, bf16[2,512,768]{2,1,0:T(8,128)(2,1)S(1)}, u32[]{:S(2)}, u32[]{:S(2)}) collective-permute-start(bf16[2,512,768]{2,1,0:T(8,128)(2,1)S(1)} %get-tuple-element.580), channel_id=1, source_target_pairs={{0,1},{1,0},{2,3},{3,2},{4,5},{5,4},{6,7},{7,6},{8,9},{9,8},{10,11... | collective-permute-start | bytes 4718600 | tf_op jit(solution)/shard_map/ppermute | solution.py:932
  318.4 21.1 %collective-permute-start.53 = (bf16[384,1024]{1,0:T(8,128)(2,1)}, bf16[384,1024]{1,0:T(8,128)(2,1)S(1)}, u32[]{:S(2)}, u32[]{:S(2)}) collective-permute-start(bf16[384,1024]{1,0:T(8,128)(2,1)} %get-tuple-element.576), channel_id=1, source_target_pairs={{0,2},{1,3},{2,0},{3,1},{4,6},{5,7},{6,4},{7,5},{8,10},{9,11},{10,... | collective-permute-start | bytes 2359304 | tf_op jit(solution)/shard_map/ppermute | solution.py:932
  344.7 24.5 %collective-permute-start.59 = (bf16[768,1536]{1,0:T(8,128)(2,1)}, bf16[768,1536]{1,0:T(8,128)(2,1)S(1)}, u32[]{:S(2)}, u32[]{:S(2)}) collective-permute-start(bf16[768,1536]{1,0:T(8,128)(2,1)} %get-tuple-element.595), channel_id=1, source_target_pairs={{0,1},{1,0},{2,3},{3,2},{4,5},{5,4},{6,7},{7,6},{8,9},{9,8},{10,11... | collective-permute-start | bytes 7077896 | tf_op jit(solution)/shard_map/ppermute | solution.py:932
  344.7 22.6 %collective-permute-start.57 = (bf16[384,1024]{1,0:T(8,128)(2,1)}, bf16[384,1024]{1,0:T(8,128)(2,1)S(1)}, u32[]{:S(2)}, u32[]{:S(2)}) collective-permute-start(bf16[384,1024]{1,0:T(8,128)(2,1)} %get-tuple-element.591), channel_id=1, source_target_pairs={{0,2},{1,3},{2,0},{3,1},{4,6},{5,7},{6,4},{7,5},{8,10},{9,11},{10,... | collective-permute-start | bytes 2359304 | tf_op jit(solution)/shard_map/ppermute | solution.py:932
  345.3 22.1 %collective-permute-start.58 = (bf16[384,1024]{1,0:T(8,128)(2,1)}, bf16[384,1024]{1,0:T(8,128)(2,1)S(1)}, u32[]{:S(2)}, u32[]{:S(2)}) collective-permute-start(bf16[384,1024]{1,0:T(8,128)(2,1)} %copy-done.52), channel_id=1, source_target_pairs={{0,4},{1,5},{2,6},{3,7},{4,0},{5,1},{6,2},{7,3},{8,12},{9,13},{10,... | collective-permute-start | bytes 2359304 | tf_op jit(solution)/shard_map/ppermute | solution.py:932
  369.2 26.9 %collective-permute-start.62 = (bf16[384,1024]{1,0:T(8,128)(2,1)}, bf16[384,1024]{1,0:T(8,128)(2,1)S(1)}, u32[]{:S(2)}, u32[]{:S(2)}) collective-permute-start(bf16[384,1024]{1,0:T(8,128)(2,1)} %get-tuple-element.604), channel_id=1, source_target_pairs={{0,4},{1,5},{2,6},{3,7},{4,0},{5,1},{6,2},{7,3},{8,12},{9,13},{10,... | collective-permute-start | bytes 2359304 | tf_op jit(solution)/shard_map/ppermute | solution.py:932
  371.3 24.8 %collective-permute-start.60 = (bf16[384,1024]{1,0:T(8,128)(2,1)}, bf16[384,1024]{1,0:T(8,128)(2,1)S(1)}, u32[]{:S(2)}, u32[]{:S(2)}) collective-permute-start(bf16[384,1024]{1,0:T(8,128)(2,1)} %get-tuple-element.602), channel_id=1, source_target_pairs={{0,24},{1,25},{2,26},{3,27},{4,28},{5,29},{6,30},{7,31},{8,0},{9,1... | collective-permute-start | bytes 2359304 | tf_op jit(solution)/shard_map/ppermute | solution.py:936
  375.2 20.9 %collective-permute-start.61 = (bf16[384,1024]{1,0:T(8,128)(2,1)S(1)}, bf16[384,1024]{1,0:T(8,128)(2,1)S(1)}, u32[]{:S(2)}, u32[]{:S(2)}) collective-permute-start(bf16[384,1024]{1,0:T(8,128)(2,1)S(1)} %get-tuple-element.603), channel_id=1, source_target_pairs={{0,2},{1,3},{2,0},{3,1},{4,6},{5,7},{6,4},{7,5},{8,10},{9,11},{10,... | collective-permute-start | bytes 2359304 | tf_op jit(solution)/shard_map/ppermute | solution.py:932
  396.2 24.2 %collective-permute-start.65 = (bf16[432,384]{1,0:T(8,128)(2,1)}, bf16[432,384]{1,0:T(8,128)(2,1)}, u32[]{:S(2)}, u32[]{:S(2)}) collective-permute-start(bf16[432,384]{1,0:T(8,128)(2,1)} %get-tuple-element.642), channel_id=1, source_target_pairs={{0,24},{1,25},{2,26},{3,27},{4,28},{5,29},{6,30},{7,31},{8,0},{9,1... | collective-permute-start | bytes 995336 | tf_op jit(solution)/shard_map/ppermute | solution.py:936
  396.9 23.5 %collective-permute-start.66 = (bf16[432,384]{1,0:T(8,128)(2,1)}, bf16[432,384]{1,0:T(8,128)(2,1)}, u32[]{:S(2)}, u32[]{:S(2)}) collective-permute-start(bf16[432,384]{1,0:T(8,128)(2,1)} %get-tuple-element.643), channel_id=1, source_target_pairs={{0,2},{1,3},{2,0},{3,1},{4,6},{5,7},{6,4},{7,5},{8,10},{9,11},{10,... | collective-permute-start | bytes 995336 | tf_op jit(solution)/shard_map/ppermute | solution.py:932
  398.4 22.0 %collective-permute-start.67 = (bf16[432,384]{1,0:T(8,128)(2,1)}, bf16[432,384]{1,0:T(8,128)(2,1)}, u32[]{:S(2)}, u32[]{:S(2)}) collective-permute-start(bf16[432,384]{1,0:T(8,128)(2,1)} %get-tuple-element.644), channel_id=1, source_target_pairs={{0,4},{1,5},{2,6},{3,7},{4,0},{5,1},{6,2},{7,3},{8,12},{9,13},{10,... | collective-permute-start | bytes 995336 | tf_op jit(solution)/shard_map/ppermute | solution.py:932
  463.0 23.5 %collective-permute-start.86 = (f32[3,64,1024]{2,1,0:T(8,128)}, f32[3,64,1024]{2,1,0:T(8,128)}, u32[]{:S(2)}, u32[]{:S(2)}) collective-permute-start(f32[3,64,1024]{2,1,0:T(8,128)} %get-tuple-element.727), channel_id=1, source_target_pairs={{0,1},{1,0},{2,3},{3,2},{4,5},{5,4},{6,7},{7,6},{8,9},{9,8},{10,11... | collective-permute-start | bytes 2359304 | tf_op jit(solution)/shard_map/ppermute | solution.py:932
  (163 other events, 1888.2 us)

commit v13 on v12

--- a/solution.py
+++ b/solution.py
@@ -113,7 +113,7 @@
 
 def plane_spec(planes, rows, lanes):
     def index(step, sc):
-        return (plane_of(planes[0] + step * (planes[1] - planes[0]), sc), 0, 0)
+        return (plane_of(planes[0] + step * (planes[-1] - planes[0]) // max(len(planes) - 1, 1), sc), 0, 0)
 
     return spec((PHEADS, rows, lanes), index)
 
@@ -135,14 +135,15 @@
 
 def take_plane(place, shards, raw, sems):
     step = pl.program_id(0)
+    count = len(shards) // 4
 
     @pl.when(step == 0)
     def _():
-        for slot in range(2):
+        for slot in range(count):
             for copy in plane_fetch(place, shards, raw, sems, slot):
                 copy.start()
 
-    for slot in range(2):
+    for slot in range(count):
 
         @pl.when(step == slot)
         def _():
@@ -164,8 +165,8 @@
         mask[...] = (column < lane_lengths(sc, shape)).astype(F32).astype(BF16)
 
 
-def mix_kernel(carried, sc, *refs):
-    shards, (v_own, v_far, *rest) = refs[:8], refs[8:]
+def mix_kernel(count, carried, sc, *refs):
+    shards, (v_own, v_far, *rest) = refs[: 4 * count], refs[4 * count :]
     mixed, mean, exps, inverse, raw, mask, sems = rest[4:] if carried else rest
     fill_mask(sc, mask)
     slot = take_plane(sc[PLACE], shards, raw, sems)
@@ -185,14 +186,14 @@
 
 
 def run_mix(sc, planes, shards, v_own, v_far, carry):
-    carry = list(carry)
+    carry, count = list(carry), len(planes)
     shape = (HEADS, HROWS, 4 * HEAD)
     return pl.pallas_call(
-        partial(mix_kernel, bool(carry)),
+        partial(mix_kernel, count, bool(carry)),
         grid_spec=pltpu.PrefetchScalarGridSpec(
             num_scalar_prefetch=1,
-            grid=(2,),
-            in_specs=anywhere(8) + [plane_spec(planes, LMAX, 2 * HEAD)] * 2 + anywhere(len(carry)),
+            grid=(count,),
+            in_specs=anywhere(4 * count) + [plane_spec(planes, LMAX, 2 * HEAD)] * 2 + anywhere(len(carry)),
             out_specs=[
                 plane_spec(planes, HROWS, 4 * HEAD),
                 plane_spec(planes, HROWS, 4 * HEAD),
@@ -200,9 +201,9 @@
                 plane_spec(planes, HROWS, 4 * HEAD),
             ],
             scratch_shapes=[
-                pltpu.VMEM((2, 4 * SUBS * HALF, LMAX), BF16),
+                pltpu.VMEM((count, 4 * SUBS * HALF, LMAX), BF16),
                 pltpu.VMEM((LMAX, 4 * HEAD), BF16),
-                pltpu.SemaphoreType.DMA((2, 4)),
+                pltpu.SemaphoreType.DMA((count, 4)),
             ],
         ),
         out_shape=[
@@ -211,7 +212,7 @@
             jax.ShapeDtypeStruct((HEADS, HROWS, LMAX), BF16),
             jax.ShapeDtypeStruct(shape, BF16),
         ],
-        input_output_aliases={11 + i: i for i in range(len(carry))},
+        input_output_aliases={3 + 4 * count + i: i for i in range(len(carry))},
         compiler_params=params(VMEM),
         cost_estimate=pl.CostEstimate(
             flops=2 * HEADS * HROWS * LMAX * 4 * HEAD,
@@ -235,7 +236,7 @@
     return jnp.concatenate([own[:, :, 0], far[...]], axis=0).reshape(4 * SPAN, WIDTH)
 
 
-def pre_kernel(sc, tok, tok_far, cot, cot_far, heads, wo_own, wo_far, gain, mixed, resid, normed, grad, weight):
+def pre_kernel(sc, tok, tok_far, heads, wo_own, wo_far, gain, mixed, resid, normed, weight):
     step = pl.program_id(0)
     whole_weight(sc, step, wo_own, wo_far, weight)
     for item in range(4):
@@ -248,8 +249,6 @@
     scale = lax.rsqrt(jnp.mean(res * res, axis=-1, keepdims=True) + EPSILON)
     valid = row_valid(sc, step)
     normed[...] = jnp.where(valid, res * scale * gain[...], 0.0).astype(BF16).reshape(4, SPAN, WIDTH)
-    masked = jnp.where(valid, four_items(cot, cot_far).astype(F32), 0.0)
-    grad[...] = masked.astype(BF16).reshape(4, SPAN, WIDTH)
 
 
 def slab_spec(items=4):
@@ -267,20 +266,18 @@
     return spec((HEADS, SPAN, 4 * HEAD), lambda r, s: (0, r, 0))
 
 
-def run_pre(sc, tokens, tokens_far, cotangent, cotangent_far, heads, wo, gain):
+def run_pre(sc, tokens, tokens_far, heads, wo, gain):
     return pl.pallas_call(
         pre_kernel,
         grid_spec=pltpu.PrefetchScalarGridSpec(
             num_scalar_prefetch=1,
             grid=(HROWS // SPAN,),
             in_specs=half_specs()
-            + half_specs()
             + [heads_spec(), held((WIDTH, SIDE)), held((WIDTH, SIDE)), held((1, WIDTH))],
-            out_specs=[slab_spec()] * 4,
+            out_specs=[slab_spec()] * 3,
             scratch_shapes=[pltpu.VMEM((WIDTH, WIDTH), BF16)],
         ),
         out_shape=[
-            jax.ShapeDtypeStruct((4, HROWS, WIDTH), BF16),
             jax.ShapeDtypeStruct((4, HROWS, WIDTH), BF16),
             jax.ShapeDtypeStruct((4, HROWS, WIDTH), BF16),
             jax.ShapeDtypeStruct((4, HROWS, WIDTH), BF16),
@@ -290,7 +287,25 @@
             flops=2 * ROWS * WIDTH * WIDTH, bytes_accessed=16 * ROWS * WIDTH, transcendentals=0
         ),
         name="pre",
-    )(sc, tokens, tokens_far, cotangent, cotangent_far, heads, *wo, gain)
+    )(sc, tokens, tokens_far, heads, *wo, gain)
+
+
+def masked_kernel(sc, cot, cot_far, masked):
+    value = jnp.where(row_valid(sc, pl.program_id(0)), four_items(cot, cot_far).astype(F32), 0.0)
+    masked[...] = value.astype(BF16).reshape(4, SPAN, WIDTH)
+
+
+def run_masked(sc, cotangent, cotangent_far):
+    return pl.pallas_call(
+        masked_kernel,
+        grid_spec=pltpu.PrefetchScalarGridSpec(
+            num_scalar_prefetch=1, grid=(HROWS // SPAN,), in_specs=half_specs(), out_specs=slab_spec()
+        ),
+        out_shape=jax.ShapeDtypeStruct((4, HROWS, WIDTH), BF16),
+        compiler_params=params(VMEM),
+        cost_estimate=pl.CostEstimate(flops=0, bytes_accessed=4 * ROWS * WIDTH, transcendentals=0),
+        name="masked",
+    )(sc, cotangent, cotangent_far)
 
 
 def own_lanes(sc):
@@ -389,7 +404,7 @@
             scratch_shapes=[pltpu.VMEM((512, WIDTH), BF16)],
         ),
         out_shape=[jax.ShapeDtypeStruct((FF, SIDE), BF16)] * 2,
-        compiler_params=params(57 << 20),
+        compiler_params=params(VMEM),
         cost_estimate=pl.CostEstimate(
             flops=2 * ROWS * WIDTH * FF, bytes_accessed=2 * ROWS * (WIDTH + FF), transcendentals=0
         ),
@@ -422,7 +437,7 @@
             ],
         ),
         out_shape=[jax.ShapeDtypeStruct((WIDTH, FF // 2), BF16)] * 2,
-        compiler_params=params(57 << 20),
+        compiler_params=params(VMEM),
         cost_estimate=pl.CostEstimate(
             flops=2 * ROWS * WIDTH * FF, bytes_accessed=2 * ROWS * (WIDTH + FF), transcendentals=0
         ),
@@ -460,7 +475,7 @@
             scratch_shapes=[pltpu.VMEM((WIDTH, WIDTH), F32)],
         ),
         out_shape=[jax.ShapeDtypeStruct((WIDTH, SIDE), BF16)] * 2,
-        compiler_params=params(LESS),
+        compiler_params=params(VMEM),
         cost_estimate=pl.CostEstimate(
             flops=2 * ROWS * WIDTH * WIDTH, bytes_accessed=4 * ROWS * WIDTH, transcendentals=0
         ),
@@ -502,7 +517,7 @@
             jax.ShapeDtypeStruct((2, HROWS, WIDTH), BF16),
             jax.ShapeDtypeStruct((2, HROWS, WIDTH), BF16),
         ],
-        compiler_params=params(LESS),
+        compiler_params=params(VMEM),
         cost_estimate=pl.CostEstimate(
             flops=2 * ROWS * WIDTH * FF, bytes_accessed=ROWS * (2 * FF + 7 * WIDTH), transcendentals=0
         ),
@@ -587,9 +602,9 @@
     )(sc, resid, up_grad, up_grad, cotangent, *up, *wo, gain)
 
 
-def unmix_kernel(carried, sc, v_own, v_far, grad_heads, mean, exps, inverse, *refs):
+def unmix_kernel(count, carried, sc, v_own, v_far, grad_heads, mean, exps, inverse, *refs):
     refs = refs[2:] if carried else refs
-    outs, (own, far, grads, mask, adder, bound, out_sems) = refs[:8], refs[8:]
+    outs, (own, far, grads, mask, adder, bound, out_sems) = refs[: 4 * count], refs[4 * count :]
     place = sc[PLACE]
     step = pl.program_id(0)
 
@@ -633,24 +648,25 @@
         back = (dot(weights, low, 0, 0) * mask[...].astype(F32)).astype(BF16)
         own[head] = back[:, : 2 * HEAD]
         far[head] = back[:, 2 * HEAD :]
-    for which in range(2):
+    for which in range(count):
 
         @pl.when(step == which)
         def _():
             for copy in leave(which):
                 copy.start()
-            if which == 1:
-                for copy in leave(0) + leave(1):
-                    copy.wait()
+            if which == count - 1:
+                for slot in range(count):
+                    for copy in leave(slot):
+                        copy.wait()
 
 
 def run_unmix(sc, planes, v_own, v_far, grad_heads, mean, exps, inverse, carry):
-    carry = list(carry)
-    return pl.pallas_call(
-        partial(unmix_kernel, bool(carry)),
+    carry, count = list(carry), len(planes)
+    return pl.pallas_call(
+        partial(unmix_kernel, count, bool(carry)),
         grid_spec=pltpu.PrefetchScalarGridSpec(
             num_scalar_prefetch=1,
-            grid=(2,),
+            grid=(count,),
             in_specs=[
                 plane_spec(planes, LMAX, 2 * HEAD),
                 plane_spec(planes, LMAX, 2 * HEAD),
@@ -660,18 +676,18 @@
                 plane_spec(planes, HROWS, 4 * HEAD),
             ]
             + anywhere(len(carry)),
-            out_specs=anywhere(8) + [plane_spec(planes, LMAX, 2 * HEAD)] * 2,
+            out_specs=anywhere(4 * count) + [plane_spec(planes, LMAX, 2 * HEAD)] * 2,
             scratch_shapes=[
-                pltpu.VMEM((2, 4 * SUBS * HALF, LMAX), BF16),
+                pltpu.VMEM((count, 4 * SUBS * HALF, LMAX), BF16),
                 pltpu.VMEM((LMAX, 4 * HEAD), BF16),
                 pltpu.VMEM((4 * HEAD, 128), BF16),
                 pltpu.VMEM((LMAX, 128), BF16),
-                pltpu.SemaphoreType.DMA((2, 4)),
+                pltpu.SemaphoreType.DMA((count, 4)),
             ],
         ),
-        out_shape=[jax.ShapeDtypeStruct((SUBS * HALF, LMAX), BF16)] * 8
+        out_shape=[jax.ShapeDtypeStruct((SUBS * HALF, LMAX), BF16)] * (4 * count)
         + [jax.ShapeDtypeStruct((HEADS, LMAX, 2 * HEAD), BF16)] * 2,
-        input_output_aliases={7 + i: 8 + i for i in range(len(carry))},
+        input_output_aliases={7 + i: 4 * count + i for i in range(len(carry))},
         compiler_params=params(VMEM),
         cost_estimate=pl.CostEstimate(
             flops=3 * HEADS * HROWS * LMAX * 4 * HEAD,
@@ -755,7 +771,7 @@
             jax.ShapeDtypeStruct((2, WIDTH, SIDE), BF16),
             jax.ShapeDtypeStruct((1, WIDTH), F32),
         ],
-        compiler_params=params(LESS),
+        compiler_params=params(VMEM),
         cost_estimate=pl.CostEstimate(
             flops=4 * 2 * LMAX * WIDTH * WIDTH, bytes_accessed=38 * LMAX * WIDTH, transcendentals=0
         ),
@@ -952,8 +968,8 @@
     ((0, 0, 1), (0, 1, 0), (1, 0, 0)),
     ((1, 0, 1), (0, 1, 1), (2, 0, 0)),
     ((2, 0, 1), (1, 1, 0), (3, 0, 0)),
-    ((3, 0, 1), (2, 1, 0), (1, 1, 1)),
-    ((2, 1, 1), (3, 1, 1), (3, 1, 0)),
+    ((1, 1, 1), (2, 1, 1), (2, 1, 0)),
+    ((3, 0, 1), (3, 1, 0), (3, 1, 1)),
 )
 
 
@@ -1030,79 +1046,80 @@
     rands = gather_step(rands, 1)
     v_own = run_values(sc, tokens.reshape(2, LMAX, WIDTH), gain_one, value, value_far)
     rands, v_own, out, down, up = together((rands, v_own, (out, other(out)), down, up))
-    rands, v_own, v_far, down, up = together((gather_step(rands, 2), v_own, other(v_own), down, up))
-    rands, v_far, down, up = together((gather_step(rands, 3), v_far, down, up))
-    near = [rands[k, y_at, x_at] for k in range(2) for y_at in range(2) for x_at in range(2)]
+    rands, v_own, v_far, grad_far, down, up = together(
+        (gather_step(rands, 2), v_own, other(v_own), grad_far, down, up)
+    )
+    rands = gather_step(rands, 3)
+    masked = run_masked(sc, grad_out, grad_far)
+    rands, v_far, masked, down, up = together((rands, v_far, masked, down, up))
+    near = [rands[k, y_at, x_at] for k in range(3) for y_at in range(2) for x_at in range(2)]
     rands = gather_step(rands, 4)
-    mixing = run_mix(sc, (0, 1), near, v_own, v_far, ())
+    mixing = run_mix(sc, (0, 1, 2), near, v_own, v_far, ())
     rands, down, up, mixing = together((rands, down, up, mixing))
-    heads, mean, exps, inverse = run_mix(sc, (2, 3), in_order(rands)[8:], v_own, v_far, mixing)
+    heads, mean, exps, inverse = run_mix(sc, (3,), in_order(rands)[12:], v_own, v_far, mixing)
     down, up = (down, other(down)), (up, other(up))
 
-    mixed, resid, normed, masked = run_pre(sc, tokens, tokens_far, grad_out, grad_far, heads, out, gain_two)
+    mixed, resid, normed = run_pre(sc, tokens, tokens_far, heads, out, gain_two)
     active, up_grad = run_units(sc, normed, masked, up, down)
     res_own, res_far, grad_heads, d_gain_two = run_post(sc, resid, up_grad, masked, up, out, gain_two)
 
     backward = lambda planes, carry: run_unmix(sc, planes, v_own, v_far, grad_heads, mean, exps, inverse, carry)
-    *far, back_own, back_far = backward((3, 2), ())
+    *far, back_own, back_far = backward((3,), ())
     far, back_own, back_far, res_got = together((far, back_own, back_far, other(res_far)))
-    have, got = scatter_send(by_place(far, (3, 2)), 0)
-    *near, back_own, back_far = backward((1, 0), (back_own, back_far))
+    have, got = scatter_send(by_place(far, (3,)), 0)
+    *near, back_own, back_far = backward((2, 1, 0), (back_own, back_far))
     have, got, near, back_own, back_far = together((have, got, near, back_own, back_far))
-    have = {**scatter_add(have, got, 0), **by_place(near, (1, 0))}
+    have = scatter_add({**have, **by_place(near, (2, 1, 0))}, got, 0)
 
     have, got = scatter_send(have, 1)
-    out_own, out_far = run_out(sc, active, resid, down)
-    have, got, out_own, out_far, back_got = together((have, got, out_own, out_far, other(back_far)))
+    up_own, up_far = run_up_grad(sc, normed, up_grad)
+    have, got, up_own, up_far, back_got = together((have, got, up_own, up_far, other(back_far)))
     have = scatter_add(have, got, 1)
 
     have, got = scatter_send(have, 2)
-    up_own, up_far = run_up_grad(sc, normed, up_grad)
-    have, got, up_own, up_far, out_got = together((have, got, up_own, up_far, other(out_far)))
-    have = scatter_add(have, got, 2)
-
-    have, got = scatter_send(have, 3)
     down_own, down_far = run_down_grad(sc, active, masked)
     have, got, down_own, down_far, up_got = together((have, got, down_own, down_far, other(up_far)))
-    have = scatter_add(have, got, 3)
-
-    have, got = scatter_send(have, 4)
+    have = scatter_add(have, got, 2)
+
+    have, got = scatter_send(have, 3)
     d_out_own, d_out_far = run_out_grad(sc, mixed, res_own, res_far)
     packed = run_collect(sc, down_own, other(down_far), up_own, up_got, d_out_own, other(d_out_far))
     have, got, packed = together((have, got, packed))
+    have = scatter_add(have, got, 3)
+
+    have, got = scatter_send(have, 4)
+    sums, sums_got = scatter_send(by_place(packed), 0)
+    out_own, out_far = run_out(sc, active, resid, down)
+    have, got, sums, sums_got, out_own, out_far = together((have, got, sums, sums_got, out_own, out_far))
     rand_sum = scatter_add(have, got, 4)[0, 0, 0].reshape(2, 3, HALF, LMAX)
 
-    sums, got = scatter_send(by_place(packed), 0)
+    sums, got = scatter_send(scatter_add(sums, sums_got, 0), 1)
     output, tokens_grad, d_value, d_gain_one = run_close(
-        sc, tokens, res_own, res_got, out_own, out_got, back_own, back_got, gain_one, value, value_far
+        sc, tokens, res_own, res_got, out_own, other(out_far), back_own, back_got, gain_one, value, value_far
     )
     gain_pair = jnp.concatenate([d_gain_one, d_gain_two]).reshape(2, 16, 1, 48).astype(BF16)
     gain_pair = jnp.pad(gain_pair, ((0, 0), (0, 0), (0, 15), (0, SIDE - 48)))
     small = jnp.concatenate([d_value.reshape(2, 16, 48, SIDE), gain_pair], 2)
     sums, got, output, tokens_grad, small = together((sums, got, output, tokens_grad, small))
-    sums = scatter_add(sums, got, 0)
-
-    sums, got = scatter_send(sums, 1)
+    sums = scatter_add(sums, got, 1)
+
+    sums, got = scatter_send(sums, 2)
     small = add_low(pick(small, core), other(pick(small, 1 - core))).reshape(4, 2, 2, 64, SIDE)
     sums, got, small = together((sums, got, small))
-    sums = scatter_add(sums, got, 1)
-
-    sums, got = scatter_send(sums, 2)
+    sums = scatter_add(sums, got, 2)
+
+    sums, got = scatter_send(sums, 3)
     small = add_low(pick(small, x, 2), swap(pick(small, 1 - x, 2), TO_X))
-    sums, got, small = together((sums, got, small))
-    sums = scatter_add(sums, got, 2)
-
-    sums, got = scatter_send(sums, 3)
+    blocks, blocks_far = pick(rand_sum, core), other(pick(rand_sum, 1 - core))
+    sums, got, small, blocks, blocks_far = together((sums, got, small, blocks, blocks_far))
+    sums = scatter_add(sums, got, 3)
+
+    sums, got = scatter_send(sums, 4)
     small = add_low(pick(small, y, 1), swap(pick(small, 1 - y, 1), TO_Y))
     sums, got, small = together((sums, got, small))
-    sums = scatter_add(sums, got, 3)
-
-    sums, got = scatter_send(sums, 4)
     small_sum = pick(small, z).astype(F32)
     for k in range(1, PLANES):
         small_sum = small_sum + ring(pick(small, lax.rem(z + PLANES - k, PLANES)), -k).astype(F32)
-    blocks, blocks_far = pick(rand_sum, core), other(pick(rand_sum, 1 - core))
-    sums, got, small_sum, blocks, blocks_far = together((sums, got, small_sum, blocks, blocks_far))
     big_sum = scatter_add(sums, got, 4)[0, 0, 0]
     big_far, small_far = other(big_sum), other(small_sum)
 

time: 503 us -> 499 us (level)
  Pallas kernels: 217 us -> 235 us
  waiting for transfers between devices: 143 us -> 135 us
  local copies, waits for them, and re-layouts: 44.5 us -> 36.7 us
  starting transfers between devices: 76.5 us -> 70.8 us
    ppermute x23, waiting for transfers between devices: 75.6 us -> 48.7 us  [ring(): lax.ppermute(x, BOTH, [(d, (d + 8 * way) % DEVICES) for d in range(DEVICE...]
    ppermute x66, waiting for transfers between devices: 67.7 us -> 86.3 us  [swap(): return lax.ppermute(x, BOTH, [(d, d ^ bit) for d in range(DEVICES)])]
    pallas_call x4 -> x5, Pallas kernels: 48.4 us -> 56.5 us  [the longest x2 29.4 us: run_unmix(): pl.pallas_call(partial(unmix_kernel, count, bool(carry)), grid_spec=pltpu...]
    unnamed x198 -> x180, local copies, waits for them, and re-layouts: 30.1 us -> 25.3 us
  transfers between devices with their start and end apart: 89 -> 89, of which waited for: 39 -> 39; matrix products, arithmetic and copies ran while one was open for 4% -> 4% of each run, Pallas kernels for 32% -> 36%
where the time goes in v13:
time: 499 us; the launch traced here: 493 us
  Pallas kernels  235 us (47%)
  waiting for transfers between devices  135 us (27%)
  starting transfers between devices  70.8 us (14%)
  local copies, waits for them, and re-layouts  36.7 us (7%)
  other arithmetic  12.4 us (2%)
    ppermute x66, waiting for transfers between devices, swap(): return lax.ppermute(x, BOTH, [(d, d ^ bit) for d in range(DEVICES)])  86.3 us
    ppermute x23, waiting for transfers between devices, ring(): lax.ppermute(x, BOTH, [(d, (d + 8 * way) % DEVICES) for d in range(DEVICE...  48.7 us
    ppermute x66, starting transfers between devices, swap(): return lax.ppermute(x, BOTH, [(d, d ^ bit) for d in range(DEVICES)])  47.7 us
    pallas_call x1, Pallas kernels, run_units(): pl.pallas_call(units_kernel, grid_spec=pltpu.PrefetchScalarGridSpec(num_s...  30.2 us
    pallas_call x2, Pallas kernels, run_unmix(): pl.pallas_call(partial(unmix_kernel, count, bool(carry)), grid_spec=pltpu...  29.4 us
    pallas_call x1, Pallas kernels, run_post(): pl.pallas_call(post_kernel, grid_spec=pltpu.PrefetchScalarGridSpec(num_sc...  28.1 us
    unnamed x180, local copies, waits for them, and re-layouts  25.3 us
    ppermute x23, starting transfers between devices, ring(): lax.ppermute(x, BOTH, [(d, (d + 8 * way) % DEVICES) for d in range(DEVICE...  23.2 us
  transfers between devices with their start and end apart: 89, of which 39 were waited for; matrix products, arithmetic and copies ran while one was open for 4% of the time, Pallas kernels for 36%

profile of v13, /device:TPU:0, one launch (start us, length us, event | category | flops | bytes accessed | tf_op | source)
XLA Modules:
  0.0 492.5 jit_solution(5590533419940739930)
XLA Ops:
  16.5 8.3 %collective-permute-done.7.refs_4_ = bf16[496,384]{1,0:T(8,128)(2,1)S(1)} collective-permute-done((bf16[496,384]{1,0:T(8,128)(2,1)}, bf16[496,384]{1,0:T(8,128)(2,1)S(1)}, u32[]{:S(2)}, u32[]{:S(2)}) %collective-permute-start.7) | collective-permute-done | bytes 380960 | tf_op jit(solution)/shard_map/ppermute | solution.py:952
  32.3 7.1 %collective-permute-done.9.refs_3_ = bf16[496,384]{1,0:T(8,128)(2,1)S(1)} collective-permute-done((bf16[496,384]{1,0:T(8,128)(2,1)S(1)}, bf16[496,384]{1,0:T(8,128)(2,1)S(1)}, u32[]{:S(2)}, u32[]{:S(2)}) %collective-permute-start.9) | collective-permute-done | bytes 380960 | tf_op jit(solution)/shard_map/ppermute | solution.py:948
  45.6 5.9 %collective-permute-done.13.refs_6_ = bf16[496,384]{1,0:T(8,128)(2,1)S(1)} collective-permute-done((bf16[496,384]{1,0:T(8,128)(2,1)S(1)}, bf16[496,384]{1,0:T(8,128)(2,1)S(1)}, u32[]{:S(2)}, u32[]{:S(2)}) %collective-permute-start.13) | collective-permute-done | bytes 380960 | tf_op jit(solution)/shard_map/ppermute | solution.py:948
  67.6 7.1 %collective-permute-done.23.refs_15_ = bf16[496,384]{1,0:T(8,128)(2,1)S(1)} collective-permute-done((bf16[496,384]{1,0:T(8,128)(2,1)S(1)}, bf16[496,384]{1,0:T(8,128)(2,1)S(1)}, u32[]{:S(2)}, u32[]{:S(2)}) %collective-permute-start.23) | collective-permute-done | bytes 380960 | tf_op jit(solution)/shard_map/ppermute | solution.py:952
  78.2 7.2 %place.1 = (bf16[3072,384]{1,0:T(8,128)(2,1)}, bf16[768,1536]{1,0:T(8,128)(2,1)}, bf16[768,384]{1,0:T(8,128)(2,1)}, bf16[768,384]{1,0:T(8,128)(2,1)}, bf16[256,384]{1,0:T(8,128)(2,1)}) custom-call(s32[7]{0:T(128)} %concatenate.54.sc, bf16[496,384]{1,0:T(8,128)(2,1)} %pack.1.refs_0_, bf16[496,384]{1,0:T(8,128)(2,1)} %copy-done.65, ...), custom_call_target="tpu_custom_call" | custom-call | bytes 12189696 | tf_op jit(solution)/shard_map/place/pallas_call | solution.py:854
  95.7 7.8 %values.1.refs_12_.refs_4_.v_own = bf16[12,1024,128]{2,1,0:T(8,128)(2,1)} custom-call(s32[7]{0:T(128)} %concatenate.54.sc, bf16[2,1024,768]{2,1,0:T(8,128)(2,1)} %tok.1, f32[1,768]{1,0:T(1,128)} %reshape.205.gain, bf16[768,384]{1,0:T(8,128)(2,1)} %get-tuple-element.422.w_own, bf16[768,384]{1,0:T(8,128)(2,1)} %copy-done.88), custom_call_target="tpu_custom_call" | custom-call | flops 2415919104 | bytes 6291456 | tf_op jit(solution)/shard_map/values/pallas_call | solution.py:81
  114.0 16.7 %collective-permute-done.32.refs_6_ = bf16[384,1024]{1,0:T(8,128)(2,1)} collective-permute-done((bf16[384,1024]{1,0:T(8,128)(2,1)}, bf16[384,1024]{1,0:T(8,128)(2,1)}, u32[]{:S(2)}, u32[]{:S(2)}) %collective-permute-start.32) | collective-permute-done | bytes 786464 | tf_op jit(solution)/shard_map/ppermute | solution.py:948
  135.6 5.5 %masked.1.cot = bf16[4,512,768]{2,1,0:T(8,128)(2,1)} custom-call(s32[7]{0:T(128)} %concatenate.54.sc, bf16[2,8,2,64,768]{4,3,2,1,0:T(8,128)(2,1)} %bitcast.106, bf16[2,8,64,768]{3,2,1,0:T(8,128)(2,1)} %copy-done.54), custom_call_target="tpu_custom_call" | custom-call | bytes 6291456 | tf_op jit(solution)/shard_map/masked/pallas_call | solution.py:299
  141.1 11.8 %collective-permute-done.38.refs_11_ = bf16[384,1024]{1,0:T(8,128)(2,1)} collective-permute-done((bf16[384,1024]{1,0:T(8,128)(2,1)}, bf16[384,1024]{1,0:T(8,128)(2,1)}, u32[]{:S(2)}, u32[]{:S(2)}) %collective-permute-start.38) | collective-permute-done | bytes 786464 | tf_op jit(solution)/shard_map/ppermute | solution.py:948
  157.5 13.2 %mix.2 = (bf16[12,512,256]{2,1,0:T(8,128)(2,1)}, f32[12,512,256]{2,1,0:T(8,128)}, bf16[12,512,1024]{2,1,0:T(8,128)(2,1)}, bf16[12,512,256]{2,1,0:T(8,128)(2,1)}) custom-call(s32[7]{0:T(128)} %concatenate.54.sc, bf16[384,1024]{1,0:T(8,128)(2,1)} %bitcast.114, bf16[384,1024]{1,0:T(8,128)(2,1)} %collective-permute-done.24.refs_1_, ...), custom_call_target="tpu_custom_call" | custom-call | flops 3221225472 | bytes 20447232 | tf_op jit(solution)/shard_map/mix/pallas_call | solution.py:191
  170.7 4.8 collective-permute-done.41.refs_3_
  176.9 8.5 %mix.3 = (bf16[12,512,256]{2,1,0:T(8,128)(2,1)}, f32[12,512,256]{2,1,0:T(8,128)}, bf16[12,512,1024]{2,1,0:T(8,128)(2,1)}, bf16[12,512,256]{2,1,0:T(8,128)(2,1)}) custom-call(s32[7]{0:T(128)} %concatenate.54.sc, bf16[384,1024]{1,0:T(8,128)(2,1)} %copy-done.58, ...), custom_call_target="tpu_custom_call", output_to_operand_aliasing={{0}: (7, {}), {1}: (8, {}), {2}: (9, {}), {3}: (10, {})} | custom-call | flops 3221225472 | bytes 20447232 | tf_op jit(solution)/shard_map/mix/pallas_call | solution.py:191
  185.4 10.6 %pre.1 = (bf16[4,512,768]{2,1,0:T(8,128)(2,1)}, bf16[4,512,768]{2,1,0:T(8,128)(2,1)}, bf16[4,512,768]{2,1,0:T(8,128)(2,1)}) custom-call(s32[7]{0:T(128)} %concatenate.54.sc, bf16[2,8,2,64,768]{4,3,2,1,0:T(8,128)(2,1)} %bitcast.109, bf16[2,8,64,768]{3,2,1,0:T(8,128)(2,1)} %copy-done.53, bf16[12,512,256]{2,1,0:T(8,128)(2,1)} %get-tuple-element.482.heads, ...), custom_call_target="tpu_custom_call" | custom-call | flops 2415919104 | bytes 25165824 | tf_op jit(solution)/shard_map/pre/pallas_call | solution.py:270
  195.9 30.2 %units.1 = (bf16[2048,3072]{1,0:T(8,128)(2,1)}, bf16[2048,3072]{1,0:T(8,128)(2,1)}) custom-call(s32[7]{0:T(128)} %concatenate.54.sc, bf16[2048,768]{1,0:T(8,128)(2,1)} %bitcast.135, bf16[2048,768]{1,0:T(8,128)(2,1)} %bitcast.117, bf16[768,1536]{1,0:T(8,128)(2,1)} %get-tuple-element.488.up_own, bf16[768,1536]{1,0:T(8,128)(2,1)} %collective-permute-done.42.up_far, ...), custom_call_target="tpu_custom_call" | custom-call | flops 19327352832 | bytes 34603008 | tf_op jit(solution)/shard_map/units/pallas_call | solution.py:365
  226.1 28.1 %post.1 = (bf16[2,512,768]{2,1,0:T(8,128)(2,1)}, bf16[2,512,768]{2,1,0:T(8,128)(2,1)}, bf16[12,512,256]{2,1,0:T(8,128)(2,1)}, f32[1,768]{1,0:T(1,128)}) custom-call(s32[7]{0:T(128)} %concatenate.54.sc, bf16[4,512,768]{2,1,0:T(8,128)(2,1)} %get-tuple-element.485.resid, bf16[4,512,3072]{2,1,0:T(8,128)(2,1)} %bitcast.139, bf16[4,512,3072]{2,1,0:T(8,128)(2,1)} %bitcast.140, ...), custom_call_target="tpu_custom_call" | custom-call | flops 12079595520 | bytes 37748736 | tf_op jit(solution)/shard_map/post/pallas_call | solution.py:569
  254.3 9.9 %unmix.2 = (bf16[384,1024]{1,0:T(8,128)(2,1)}, bf16[384,1024]{1,0:T(8,128)(2,1)}, bf16[384,1024]{1,0:T(8,128)(2,1)}, bf16[384,1024]{1,0:T(8,128)(2,1)}, bf16[12,...) custom-call(s32[7]{0:T(128)} %concatenate.54.sc, bf16[12,1024,128]{2,1,0:T(8,128)(2,1)} %values.1.refs_12_.refs_4_.v_own, ...), custom_call_target="tpu_custom_call" | custom-call | flops 4831838208 | bytes 33030144 | tf_op jit(solution)/shard_map/unmix/pallas_call | solution.py:665
  269.2 19.5 %unmix.3 = (bf16[384,1024]{1,0:T(8,128)(2,1)}, bf16[384,1024]{1,0:T(8,128)(2,1)}, bf16[384,1024]{1,0:T(8,128)(2,1)}, bf16[384,1024]{1,0:T(8,128)(2,1)}, bf16[384...) custom-call(s32[7]{0:T(128)} %concatenate.54.sc, ...), custom_call_target="tpu_custom_call", output_to_operand_aliasing={{12}: (7, {}), {13}: (8, {})} | custom-call | flops 4831838208 | bytes 33030144 | tf_op jit(solution)/shard_map/unmix/pallas_call | solution.py:665
  295.7 16.3 %up_grad.1 = (bf16[768,1536]{1,0:T(8,128)(2,1)}, bf16[768,1536]{1,0:T(8,128)(2,1)}) custom-call(s32[7]{0:T(128)} %concatenate.54.sc, bf16[2048,768]{1,0:T(8,128)(2,1)} %bitcast.136, bf16[2048,3072]{1,0:T(8,128)(2,1)} %get-tuple-element.490.up_grad), custom_call_target="tpu_custom_call" | custom-call | flops 9663676416 | bytes 15728640 | tf_op jit(solution)/shard_map/up_grad/pallas_call | solution.py:428
  323.9 15.6 %down_grad.1 = (bf16[3072,384]{1,0:T(8,128)(2,1)}, bf16[3072,384]{1,0:T(8,128)(2,1)}) custom-call(s32[7]{0:T(128)} %concatenate.54.sc, bf16[2048,3072]{1,0:T(8,128)(2,1)} %get-tuple-element.558.active, bf16[2048,768]{1,0:T(8,128)(2,1)} %bitcast.118), custom_call_target="tpu_custom_call" | custom-call | flops 9663676416 | bytes 15728640 | tf_op jit(solution)/shard_map/down_grad/pallas_call | solution.py:397
  352.5 7.9 %out_grad.1 = (bf16[768,384]{1,0:T(8,128)(2,1)}, bf16[768,384]{1,0:T(8,128)(2,1)}) custom-call(s32[7]{0:T(128)} %concatenate.54.sc, bf16[4,512,768]{2,1,0:T(8,128)(2,1)} %get-tuple-element.578.mixed, bf16[2,512,768]{2,1,0:T(8,128)(2,1)} %get-tuple-element.579.res_own, bf16[2,512,768]{2,1,0:T(8,128)(2,1)} %get-tuple-element.501.res_far), custom_call_target="tpu_custom_call" | custom-call | flops 2415919104 | bytes 6291456 | tf_op jit(solution)/shard_map/out_grad/pallas_call | solution.py:468
  367.0 4.9 collect.1
  384.7 16.6 %out.3 = (bf16[2,512,768]{2,1,0:T(8,128)(2,1)}, bf16[2,512,768]{2,1,0:T(8,128)(2,1)}) custom-call(s32[7]{0:T(128)} %concatenate.54.sc, bf16[4,512,3072]{2,1,0:T(8,128)(2,1)} %bitcast.138, bf16[4,512,768]{2,1,0:T(8,128)(2,1)} %get-tuple-element.485.resid, bf16[3072,384]{1,0:T(8,128)(2,1)} %get-tuple-element.489.dn_own, ...), custom_call_target="tpu_custom_call" | custom-call | flops 9663676416 | bytes 23592960 | tf_op jit(solution)/shard_map/out/pallas_call | solution.py:502
  413.8 16.0 %close.1 = (f32[2,8,2,64,768]{4,3,2,1,0:T(8,128)}, f32[2,8,2,64,768]{4,3,2,1,0:T(8,128)}, bf16[2,768,384]{2,1,0:T(8,128)(2,1)}, f32[1,768]{1,0:T(1,128)}) custom-call(s32[7]{0:T(128)} %concatenate.54.sc, bf16[2,8,2,64,768]{4,3,2,1,0:T(8,128)(2,1)} %bitcast.110, bf16[2,8,64,768]{3,2,1,0:T(8,128)(2,1)} %bitcast.143, bf16[2,8,64,768]{3,2,1,0:T(8,128)(2,1)} %bitcast.137, ...), custom_call_target="tpu_custom_call" | custom-call | flops 4831838208 | bytes 29884416 | tf_op jit(solution)/shard_map/close/pallas_call | solution.py:757
  452.6 8.9 %collective-permute-done.78 = bf16[4,2,64,384]{3,2,1,0:T(8,128)(2,1)} collective-permute-done((bf16[4,2,64,384]{3,2,1,0:T(8,128)(2,1)}, bf16[4,2,64,384]{3,2,1,0:T(8,128)(2,1)}, u32[]{:S(2)}, u32[]{:S(2)}) %collective-permute-start.78) | collective-permute-done | bytes 393248 | tf_op jit(solution)/shard_map/ppermute | solution.py:948
  (409 shorter events, 202.3 us)
Async XLA Ops:
  110.3 23.5 %collective-permute-start.35 = (bf16[12,1024,128]{2,1,0:T(8,128)(2,1)}, bf16[12,1024,128]{2,1,0:T(8,128)(2,1)}, u32[]{:S(2)}, u32[]{:S(2)}) collective-permute-start(bf16[12,1024,128]{2,1,0:T(8,128)(2,1)} %values.1.refs_12_.refs_4_.v_own), channel_id=1, source_target_pairs={{0,1},{1,0},{2,3},{3,2},{4,5},{5,4},{6,7},{7,6},{8,9},{9,8},{10,11... | collective-permute-start | bytes 9437192 | tf_op jit(solution)/shard_map/ppermute | solution.py:948
  111.5 21.4 %collective-permute-start.34 = (bf16[384,1024]{1,0:T(8,128)(2,1)S(1)}, bf16[384,1024]{1,0:T(8,128)(2,1)S(1)}, u32[]{:S(2)}, u32[]{:S(2)}) collective-permute-start(bf16[384,1024]{1,0:T(8,128)(2,1)S(1)} %collective-permute-done.30.refs_8_), channel_id=1, source_target_pairs={{0,8},{1,9},{2,10},{3,11},{4,12},{5,13},{6,14},{7,15},{8,16},{9,17... | collective-permute-start | bytes 2359304 | tf_op jit(solution)/shard_map/ppermute | solution.py:952
  134.8 20.6 %collective-permute-start.37 = (bf16[384,1024]{1,0:T(8,128)(2,1)}, bf16[384,1024]{1,0:T(8,128)(2,1)}, u32[]{:S(2)}, u32[]{:S(2)}) collective-permute-start(bf16[384,1024]{1,0:T(8,128)(2,1)} %collective-permute-done.32.refs_6_), channel_id=1, source_target_pairs={{0,8},{1,9},{2,10},{3,11},{4,12},{5,13},{6,14},{7,15},{8,16},{9,17... | collective-permute-start | bytes 2359304 | tf_op jit(solution)/shard_map/ppermute | solution.py:952
  135.1 20.4 %collective-permute-start.36 = (bf16[384,1024]{1,0:T(8,128)(2,1)}, bf16[384,1024]{1,0:T(8,128)(2,1)}, u32[]{:S(2)}, u32[]{:S(2)}) collective-permute-start(bf16[384,1024]{1,0:T(8,128)(2,1)} %collective-permute-done.32.refs_6_), channel_id=1, source_target_pairs={{0,2},{1,3},{2,0},{3,1},{4,6},{5,7},{6,4},{7,5},{8,10},{9,11},{10,... | collective-permute-start | bytes 2359304 | tf_op jit(solution)/shard_map/ppermute | solution.py:948
  175.5 20.4 %collective-permute-start.42 = (bf16[768,1536]{1,0:T(8,128)(2,1)}, bf16[768,1536]{1,0:T(8,128)(2,1)}, u32[]{:S(2)}, u32[]{:S(2)}) collective-permute-start(bf16[768,1536]{1,0:T(8,128)(2,1)} %get-tuple-element.488.up_own), channel_id=1, source_target_pairs={{0,1},{1,0},{2,3},{3,2},{4,5},{5,4},{6,7},{7,6},{8,9},{9,8},{10,11... | collective-permute-start | bytes 7077896 | tf_op jit(solution)/shard_map/ppermute | solution.py:948
  175.6 20.4 %collective-permute-start.43 = (bf16[3072,384]{1,0:T(8,128)(2,1)}, bf16[3072,384]{1,0:T(8,128)(2,1)}, u32[]{:S(2)}, u32[]{:S(2)}) collective-permute-start(bf16[3072,384]{1,0:T(8,128)(2,1)} %get-tuple-element.489.dn_own), channel_id=1, source_target_pairs={{0,1},{1,0},{2,3},{3,2},{4,5},{5,4},{6,7},{7,6},{8,9},{9,8},{10,11... | collective-permute-start | bytes 7077896 | tf_op jit(solution)/shard_map/ppermute | solution.py:948
  265.4 23.3 %collective-permute-start.45 = (bf16[384,1024]{1,0:T(8,128)(2,1)}, bf16[384,1024]{1,0:T(8,128)(2,1)S(1)}, u32[]{:S(2)}, u32[]{:S(2)}) collective-permute-start(bf16[384,1024]{1,0:T(8,128)(2,1)} %get-tuple-element.503), channel_id=1, source_target_pairs={{0,24},{1,25},{2,26},{3,27},{4,28},{5,29},{6,30},{7,31},{8,0},{9,1... | collective-permute-start | bytes 2359304 | tf_op jit(solution)/shard_map/ppermute | solution.py:952
  267.7 21.0 %collective-permute-start.46 = (bf16[384,1024]{1,0:T(8,128)(2,1)}, bf16[384,1024]{1,0:T(8,128)(2,1)S(1)}, u32[]{:S(2)}, u32[]{:S(2)}) collective-permute-start(bf16[384,1024]{1,0:T(8,128)(2,1)} %get-tuple-element.504), channel_id=1, source_target_pairs={{0,2},{1,3},{2,0},{3,1},{4,6},{5,7},{6,4},{7,5},{8,10},{9,11},{10,... | collective-permute-start | bytes 2359304 | tf_op jit(solution)/shard_map/ppermute | solution.py:948
  268.2 20.5 %collective-permute-start.47 = (bf16[384,1024]{1,0:T(8,128)(2,1)}, bf16[384,1024]{1,0:T(8,128)(2,1)}, u32[]{:S(2)}, u32[]{:S(2)}) collective-permute-start(bf16[384,1024]{1,0:T(8,128)(2,1)} %get-tuple-element.505), channel_id=1, source_target_pairs={{0,4},{1,5},{2,6},{3,7},{4,0},{5,1},{6,2},{7,3},{8,12},{9,13},{10,... | collective-permute-start | bytes 2359304 | tf_op jit(solution)/shard_map/ppermute | solution.py:948
  288.7 26.5 %collective-permute-start.51 = (bf16[12,1024,128]{2,1,0:T(8,128)(2,1)}, bf16[12,1024,128]{2,1,0:T(8,128)(2,1)}, u32[]{:S(2)}, u32[]{:S(2)}) collective-permute-start(bf16[12,1024,128]{2,1,0:T(8,128)(2,1)} %get-tuple-element.542), channel_id=1, source_target_pairs={{0,1},{1,0},{2,3},{3,2},{4,5},{5,4},{6,7},{7,6},{8,9},{9,8},{10,11... | collective-permute-start | bytes 9437192 | tf_op jit(solution)/shard_map/ppermute | solution.py:948
  288.8 23.1 %collective-permute-start.48 = (bf16[384,1024]{1,0:T(8,128)(2,1)}, bf16[384,1024]{1,0:T(8,128)(2,1)}, u32[]{:S(2)}, u32[]{:S(2)}) collective-permute-start(bf16[384,1024]{1,0:T(8,128)(2,1)} %get-tuple-element.537), channel_id=1, source_target_pairs={{0,24},{1,25},{2,26},{3,27},{4,28},{5,29},{6,30},{7,31},{8,0},{9,1... | collective-permute-start | bytes 2359304 | tf_op jit(solution)/shard_map/ppermute | solution.py:952
  289.7 22.2 %collective-permute-start.49 = (bf16[384,1024]{1,0:T(8,128)(2,1)}, bf16[384,1024]{1,0:T(8,128)(2,1)}, u32[]{:S(2)}, u32[]{:S(2)}) collective-permute-start(bf16[384,1024]{1,0:T(8,128)(2,1)} %get-tuple-element.538), channel_id=1, source_target_pairs={{0,2},{1,3},{2,0},{3,1},{4,6},{5,7},{6,4},{7,5},{8,10},{9,11},{10,... | collective-permute-start | bytes 2359304 | tf_op jit(solution)/shard_map/ppermute | solution.py:948
  315.3 27.3 %collective-permute-start.55 = (bf16[768,1536]{1,0:T(8,128)(2,1)}, bf16[768,1536]{1,0:T(8,128)(2,1)S(1)}, u32[]{:S(2)}, u32[]{:S(2)}) collective-permute-start(bf16[768,1536]{1,0:T(8,128)(2,1)} %get-tuple-element.561), channel_id=1, source_target_pairs={{0,1},{1,0},{2,3},{3,2},{4,5},{5,4},{6,7},{7,6},{8,9},{9,8},{10,11... | collective-permute-start | bytes 7077896 | tf_op jit(solution)/shard_map/ppermute | solution.py:948
  315.3 24.2 %collective-permute-start.52 = (bf16[384,1024]{1,0:T(8,128)(2,1)}, bf16[384,1024]{1,0:T(8,128)(2,1)}, u32[]{:S(2)}, u32[]{:S(2)}) collective-permute-start(bf16[384,1024]{1,0:T(8,128)(2,1)} %copy-done.34), channel_id=1, source_target_pairs={{0,24},{1,25},{2,26},{3,27},{4,28},{5,29},{6,30},{7,31},{8,0},{9,1... | collective-permute-start | bytes 2359304 | tf_op jit(solution)/shard_map/ppermute | solution.py:952
  342.6 30.1 %collective-permute-start.57 = (bf16[384,1024]{1,0:T(8,128)(2,1)}, bf16[384,1024]{1,0:T(8,128)(2,1)}, u32[]{:S(2)}, u32[]{:S(2)}) collective-permute-start(bf16[384,1024]{1,0:T(8,128)(2,1)} %get-tuple-element.572), channel_id=1, source_target_pairs={{0,2},{1,3},{2,0},{3,1},{4,6},{5,7},{6,4},{7,5},{8,10},{9,11},{10,... | collective-permute-start | bytes 2359304 | tf_op jit(solution)/shard_map/ppermute | solution.py:948
  343.6 29.1 %collective-permute-start.58 = (bf16[384,1024]{1,0:T(8,128)(2,1)}, bf16[384,1024]{1,0:T(8,128)(2,1)}, u32[]{:S(2)}, u32[]{:S(2)}) collective-permute-start(bf16[384,1024]{1,0:T(8,128)(2,1)} %get-tuple-element.573), channel_id=1, source_target_pairs={{0,4},{1,5},{2,6},{3,7},{4,0},{5,1},{6,2},{7,3},{8,12},{9,13},{10,... | collective-permute-start | bytes 2359304 | tf_op jit(solution)/shard_map/ppermute | solution.py:948
  350.5 22.2 %collective-permute-start.56 = (bf16[384,1024]{1,0:T(8,128)(2,1)}, bf16[384,1024]{1,0:T(8,128)(2,1)}, u32[]{:S(2)}, u32[]{:S(2)}) collective-permute-start(bf16[384,1024]{1,0:T(8,128)(2,1)} %get-tuple-element.571), channel_id=1, source_target_pairs={{0,24},{1,25},{2,26},{3,27},{4,28},{5,29},{6,30},{7,31},{8,0},{9,1... | collective-permute-start | bytes 2359304 | tf_op jit(solution)/shard_map/ppermute | solution.py:952
  375.2 26.1 %collective-permute-start.65 = (bf16[432,384]{1,0:T(8,128)(2,1)}, bf16[432,384]{1,0:T(8,128)(2,1)}, u32[]{:S(2)}, u32[]{:S(2)}) collective-permute-start(bf16[432,384]{1,0:T(8,128)(2,1)} %get-tuple-element.621), channel_id=1, source_target_pairs={{0,2},{1,3},{2,0},{3,1},{4,6},{5,7},{6,4},{7,5},{8,10},{9,11},{10,... | collective-permute-start | bytes 995336 | tf_op jit(solution)/shard_map/ppermute | solution.py:948
  375.7 25.5 %collective-permute-start.66 = (bf16[432,384]{1,0:T(8,128)(2,1)}, bf16[432,384]{1,0:T(8,128)(2,1)}, u32[]{:S(2)}, u32[]{:S(2)}) collective-permute-start(bf16[432,384]{1,0:T(8,128)(2,1)} %get-tuple-element.622), channel_id=1, source_target_pairs={{0,4},{1,5},{2,6},{3,7},{4,0},{5,1},{6,2},{7,3},{8,12},{9,13},{10,... | collective-permute-start | bytes 995336 | tf_op jit(solution)/shard_map/ppermute | solution.py:948
  376.7 25.3 %collective-permute-start.63 = (bf16[384,1024]{1,0:T(8,128)(2,1)}, bf16[384,1024]{1,0:T(8,128)(2,1)S(1)}, u32[]{:S(2)}, u32[]{:S(2)}) collective-permute-start(bf16[384,1024]{1,0:T(8,128)(2,1)} %get-tuple-element.606), channel_id=1, source_target_pairs={{0,4},{1,5},{2,6},{3,7},{4,0},{5,1},{6,2},{7,3},{8,12},{9,13},{10,... | collective-permute-start | bytes 2359304 | tf_op jit(solution)/shard_map/ppermute | solution.py:948
  380.8 21.3 %collective-permute-start.61 = (bf16[384,1024]{1,0:T(8,128)(2,1)}, bf16[384,1024]{1,0:T(8,128)(2,1)S(1)}, u32[]{:S(2)}, u32[]{:S(2)}) collective-permute-start(bf16[384,1024]{1,0:T(8,128)(2,1)} %get-tuple-element.604), channel_id=1, source_target_pairs={{0,24},{1,25},{2,26},{3,27},{4,28},{5,29},{6,30},{7,31},{8,0},{9,1... | collective-permute-start | bytes 2359304 | tf_op jit(solution)/shard_map/ppermute | solution.py:952
  402.4 29.8 %collective-permute-start.67 = (bf16[432,384]{1,0:T(8,128)(2,1)}, bf16[432,384]{1,0:T(8,128)(2,1)}, u32[]{:S(2)}, u32[]{:S(2)}) collective-permute-start(bf16[432,384]{1,0:T(8,128)(2,1)} %copy-done.42), channel_id=1, source_target_pairs={{0,24},{1,25},{2,26},{3,27},{4,28},{5,29},{6,30},{7,31},{8,0},{9,1... | collective-permute-start | bytes 995336 | tf_op jit(solution)/shard_map/ppermute | solution.py:952
  406.6 25.7 %collective-permute-start.68 = (bf16[432,384]{1,0:T(8,128)(2,1)}, bf16[432,384]{1,0:T(8,128)(2,1)}, u32[]{:S(2)}, u32[]{:S(2)}) collective-permute-start(bf16[432,384]{1,0:T(8,128)(2,1)} %copy-done.41), channel_id=1, source_target_pairs={{0,2},{1,3},{2,0},{3,1},{4,6},{5,7},{6,4},{7,5},{8,10},{9,11},{10,... | collective-permute-start | bytes 995336 | tf_op jit(solution)/shard_map/ppermute | solution.py:948
  440.9 21.9 %collective-permute-start.79 = (f32[3,64,1024]{2,1,0:T(8,128)}, f32[3,64,1024]{2,1,0:T(8,128)}, u32[]{:S(2)}, u32[]{:S(2)}) collective-permute-start(f32[3,64,1024]{2,1,0:T(8,128)} %get-tuple-element.705), channel_id=1, source_target_pairs={{0,1},{1,0},{2,3},{3,2},{4,5},{5,4},{6,7},{7,6},{8,9},{9,8},{10,11... | collective-permute-start | bytes 2359304 | tf_op jit(solution)/shard_map/ppermute | solution.py:948
  (154 other events, 1714.2 us)

commit v14 on v13

--- a/solution.py
+++ b/solution.py
@@ -404,7 +404,7 @@
             scratch_shapes=[pltpu.VMEM((512, WIDTH), BF16)],
         ),
         out_shape=[jax.ShapeDtypeStruct((FF, SIDE), BF16)] * 2,
-        compiler_params=params(VMEM),
+        compiler_params=params(57 << 20),
         cost_estimate=pl.CostEstimate(
             flops=2 * ROWS * WIDTH * FF, bytes_accessed=2 * ROWS * (WIDTH + FF), transcendentals=0
         ),
@@ -437,7 +437,7 @@
             ],
         ),
         out_shape=[jax.ShapeDtypeStruct((WIDTH, FF // 2), BF16)] * 2,
-        compiler_params=params(VMEM),
+        compiler_params=params(57 << 20),
         cost_estimate=pl.CostEstimate(
             flops=2 * ROWS * WIDTH * FF, bytes_accessed=2 * ROWS * (WIDTH + FF), transcendentals=0
         ),
@@ -475,7 +475,7 @@
             scratch_shapes=[pltpu.VMEM((WIDTH, WIDTH), F32)],
         ),
         out_shape=[jax.ShapeDtypeStruct((WIDTH, SIDE), BF16)] * 2,
-        compiler_params=params(VMEM),
+        compiler_params=params(LESS),
         cost_estimate=pl.CostEstimate(
             flops=2 * ROWS * WIDTH * WIDTH, bytes_accessed=4 * ROWS * WIDTH, transcendentals=0
         ),
@@ -517,7 +517,7 @@
             jax.ShapeDtypeStruct((2, HROWS, WIDTH), BF16),
             jax.ShapeDtypeStruct((2, HROWS, WIDTH), BF16),
         ],
-        compiler_params=params(VMEM),
+        compiler_params=params(LESS),
         cost_estimate=pl.CostEstimate(
             flops=2 * ROWS * WIDTH * FF, bytes_accessed=ROWS * (2 * FF + 7 * WIDTH), transcendentals=0
         ),
@@ -742,9 +742,7 @@
 
     @pl.when(step == pl.num_programs(0) - 1)
     def _():
-        low = total[...].astype(BF16)
-        d_value[0] = low[:, :SIDE]
-        d_value[1] = low[:, SIDE:]
+        d_value[...] = total[...].astype(BF16)
 
 
 def run_close(sc, tokens, res_own, res_got, out_own, out_got, own, far, gain, w_own, w_far):
@@ -762,16 +760,16 @@
             in_specs=[whole_spec]
             + [half_spec] * 4
             + [back_spec, back_spec, held((1, WIDTH)), held((WIDTH, SIDE)), held((WIDTH, SIDE))],
-            out_specs=[whole_spec, whole_spec, held((2, WIDTH, SIDE)), held((1, WIDTH))],
+            out_specs=[whole_spec, whole_spec, held((WIDTH, WIDTH)), held((1, WIDTH))],
             scratch_shapes=[pltpu.VMEM((WIDTH, WIDTH), F32), pltpu.VMEM((WIDTH, WIDTH), BF16)],
         ),
         out_shape=[
             jax.ShapeDtypeStruct(slab, F32),
             jax.ShapeDtypeStruct(slab, F32),
-            jax.ShapeDtypeStruct((2, WIDTH, SIDE), BF16),
+            jax.ShapeDtypeStruct((WIDTH, WIDTH), BF16),
             jax.ShapeDtypeStruct((1, WIDTH), F32),
         ],
-        compiler_params=params(VMEM),
+        compiler_params=params(LESS),
         cost_estimate=pl.CostEstimate(
             flops=4 * 2 * LMAX * WIDTH * WIDTH, bytes_accessed=38 * LMAX * WIDTH, transcendentals=0
         ),
@@ -1097,31 +1095,36 @@
     output, tokens_grad, d_value, d_gain_one = run_close(
         sc, tokens, res_own, res_got, out_own, other(out_far), back_own, back_got, gain_one, value, value_far
     )
-    gain_pair = jnp.concatenate([d_gain_one, d_gain_two]).reshape(2, 16, 1, 48).astype(BF16)
-    gain_pair = jnp.pad(gain_pair, ((0, 0), (0, 0), (0, 15), (0, SIDE - 48)))
-    small = jnp.concatenate([d_value.reshape(2, 16, 48, SIDE), gain_pair], 2)
+    gain_pair = jnp.stack([d_gain_one.reshape(16, 2, 24), d_gain_two.reshape(16, 2, 24)], 2).reshape(16, 2, 1, 48)
+    gain_pair = jnp.pad(gain_pair.astype(BF16), ((0, 0), (0, 0), (0, 7), (0, WIDTH - 48)))
+    small = jnp.concatenate([d_value.reshape(16, 2, 24, WIDTH), gain_pair], 2).reshape(4, 2, 2, 2, 32, WIDTH)
     sums, got, output, tokens_grad, small = together((sums, got, output, tokens_grad, small))
     sums = scatter_add(sums, got, 1)
 
     sums, got = scatter_send(sums, 2)
-    small = add_low(pick(small, core), other(pick(small, 1 - core))).reshape(4, 2, 2, 64, SIDE)
+    share = lambda to_x, to_core: pick(pick(small, to_core, 3), to_x, 2)
+    small = (
+        share(x, core).astype(F32)
+        + other(share(x, 1 - core)).astype(F32)
+        + swap(share(1 - x, core), TO_X).astype(F32)
+        + swap(share(1 - x, 1 - core), TO_X | TO_CORE).astype(F32)
+    ).astype(BF16)
     sums, got, small = together((sums, got, small))
     sums = scatter_add(sums, got, 2)
 
     sums, got = scatter_send(sums, 3)
-    small = add_low(pick(small, x, 2), swap(pick(small, 1 - x, 2), TO_X))
+    small = add_low(pick(small, y, 1), swap(pick(small, 1 - y, 1), TO_Y))
     blocks, blocks_far = pick(rand_sum, core), other(pick(rand_sum, 1 - core))
     sums, got, small, blocks, blocks_far = together((sums, got, small, blocks, blocks_far))
     sums = scatter_add(sums, got, 3)
 
     sums, got = scatter_send(sums, 4)
-    small = add_low(pick(small, y, 1), swap(pick(small, 1 - y, 1), TO_Y))
-    sums, got, small = together((sums, got, small))
     small_sum = pick(small, z).astype(F32)
     for k in range(1, PLANES):
         small_sum = small_sum + ring(pick(small, lax.rem(z + PLANES - k, PLANES)), -k).astype(F32)
+    sums, got, small_sum = together((sums, got, small_sum))
     big_sum = scatter_add(sums, got, 4)[0, 0, 0]
-    big_far, small_far = other(big_sum), other(small_sum)
+    big_far = other(big_sum)
 
     rows_of = lambda value, rows: pick(value.reshape(-1, 2, rows, SIDE), core, 1)
     mine = lambda own, far, rows: side(rows_of(own, rows)[0], rows_of(far, rows)[0], 1)
@@ -1129,22 +1132,18 @@
     up_side = lambda value: rows_of(value[PACK_UP:PACK_OUT], 24).transpose(1, 0, 2).reshape(24, 4 * SIDE)
     up_shard = side(up_side(big_sum), up_side(big_far), 1)
     outproj_shard = mine(big_sum[PACK_OUT:PACK_VALUE], big_far[PACK_OUT:PACK_VALUE], 24)
-    value_shard = mine(small_sum[:48], small_far[:48], 24)
-    gains_pair = ordered(core, small_sum[48, :48], small_far[48, :48])
-    gain_pair = pick(gains_pair.reshape(2, 2, 24), core, 1)
-
     rand_shard = ordered(core, blocks, blocks_far, 1)
 
     return (
         output.reshape(2, LMAX, WIDTH),
         tokens_grad.reshape(2, LMAX, WIDTH),
         rand_shard.reshape(3 * 128, LMAX),
-        value_shard,
+        small_sum[:24],
         outproj_shard,
         up_shard,
         down_shard,
-        gain_pair[0],
-        gain_pair[1],
+        small_sum[24, :24],
+        small_sum[24, 24:48],
     )
 
 

time: 499 us -> 506 us (1.014)
  Pallas kernels: 235 us -> 221 us
  local copies, waits for them, and re-layouts: 36.7 us -> 48.5 us
  waiting for transfers between devices: 135 us -> 143 us
    unnamed x180 -> x207, local copies, waits for them, and re-layouts: 25.3 us -> 37.1 us
    ppermute x23, waiting for transfers between devices: 48.7 us -> 57.3 us  [ring(): lax.ppermute(x, BOTH, [(d, (d + 8 * way) % DEVICES) for d in range(DEVICE...]
    pallas_call x10, Pallas kernels: 15.2 us -> 8.6 us  [run_add(): pl.pallas_call(partial(add_kernel, groups), in_specs=[here] * len(values)...]
  transfers between devices with their start and end apart: 89 -> 89, of which waited for: 39 -> 36; matrix products, arithmetic and copies ran while one was open for 4% -> 3% of each run, Pallas kernels for 36% -> 32%
where the time goes in v14:
time: 506 us; the launch traced here: 499 us
  Pallas kernels  221 us (44%)
  waiting for transfers between devices  143 us (28%)
  starting transfers between devices  74.4 us (15%)
  local copies, waits for them, and re-layouts  48.5 us (10%)
  other arithmetic  10.1 us (2%)
    ppermute x66, waiting for transfers between devices, swap(): return lax.ppermute(x, BOTH, [(d, d ^ bit) for d in range(DEVICES)])  86.1 us
    ppermute x23, waiting for transfers between devices, ring(): lax.ppermute(x, BOTH, [(d, (d + 8 * way) % DEVICES) for d in range(DEVICE...  57.3 us
    ppermute x66, starting transfers between devices, swap(): return lax.ppermute(x, BOTH, [(d, d ^ bit) for d in range(DEVICES)])  49.8 us
    unnamed x207, local copies, waits for them, and re-layouts  37.1 us
    pallas_call x1, Pallas kernels, run_units(): pl.pallas_call(units_kernel, grid_spec=pltpu.PrefetchScalarGridSpec(num_s...  30.3 us
    pallas_call x2, Pallas kernels, run_unmix(): pl.pallas_call(partial(unmix_kernel, count, bool(carry)), grid_spec=pltpu...  29.5 us
    pallas_call x1, Pallas kernels, run_post(): pl.pallas_call(post_kernel, grid_spec=pltpu.PrefetchScalarGridSpec(num_sc...  28.1 us
    ppermute x23, starting transfers between devices, ring(): lax.ppermute(x, BOTH, [(d, (d + 8 * way) % DEVICES) for d in range(DEVICE...  24.6 us
  transfers between devices with their start and end apart: 89, of which 36 were waited for; matrix products, arithmetic and copies ran while one was open for 3% of the time, Pallas kernels for 32%

profile of v14, /device:TPU:0, one launch (start us, length us, event | category | flops | bytes accessed | tf_op | source)
XLA Modules:
  0.0 499.2 jit_solution(4330659871806716693)
XLA Ops:
  16.5 8.3 %collective-permute-done.7.refs_4_ = bf16[496,384]{1,0:T(8,128)(2,1)S(1)} collective-permute-done((bf16[496,384]{1,0:T(8,128)(2,1)}, bf16[496,384]{1,0:T(8,128)(2,1)S(1)}, u32[]{:S(2)}, u32[]{:S(2)}) %collective-permute-start.7) | collective-permute-done | bytes 380960 | tf_op jit(solution)/shard_map/ppermute | solution.py:950
  31.5 7.3 %collective-permute-done.9.refs_3_ = bf16[496,384]{1,0:T(8,128)(2,1)S(1)} collective-permute-done((bf16[496,384]{1,0:T(8,128)(2,1)S(1)}, bf16[496,384]{1,0:T(8,128)(2,1)S(1)}, u32[]{:S(2)}, u32[]{:S(2)}) %collective-permute-start.9) | collective-permute-done | bytes 380960 | tf_op jit(solution)/shard_map/ppermute | solution.py:946
  45.0 6.2 %collective-permute-done.13.refs_6_ = bf16[496,384]{1,0:T(8,128)(2,1)S(1)} collective-permute-done((bf16[496,384]{1,0:T(8,128)(2,1)S(1)}, bf16[496,384]{1,0:T(8,128)(2,1)S(1)}, u32[]{:S(2)}, u32[]{:S(2)}) %collective-permute-start.13) | collective-permute-done | bytes 380960 | tf_op jit(solution)/shard_map/ppermute | solution.py:946
  67.4 7.0 %collective-permute-done.23.refs_15_ = bf16[496,384]{1,0:T(8,128)(2,1)S(1)} collective-permute-done((bf16[496,384]{1,0:T(8,128)(2,1)S(1)}, bf16[496,384]{1,0:T(8,128)(2,1)S(1)}, u32[]{:S(2)}, u32[]{:S(2)}) %collective-permute-start.23) | collective-permute-done | bytes 380960 | tf_op jit(solution)/shard_map/ppermute | solution.py:950
  77.7 7.2 %place.1 = (bf16[3072,384]{1,0:T(8,128)(2,1)}, bf16[768,1536]{1,0:T(8,128)(2,1)}, bf16[768,384]{1,0:T(8,128)(2,1)}, bf16[768,384]{1,0:T(8,128)(2,1)}, bf16[256,384]{1,0:T(8,128)(2,1)}) custom-call(s32[7]{0:T(128)} %concatenate.47.sc, bf16[496,384]{1,0:T(8,128)(2,1)} %pack.1.refs_0_, bf16[496,384]{1,0:T(8,128)(2,1)} %copy-done.80, ...), custom_call_target="tpu_custom_call" | custom-call | bytes 12189696 | tf_op jit(solution)/shard_map/place/pallas_call | solution.py:852
  95.5 7.8 %values.1.refs_12_.refs_4_.v_own = bf16[12,1024,128]{2,1,0:T(8,128)(2,1)} custom-call(s32[7]{0:T(128)} %concatenate.47.sc, bf16[2,1024,768]{2,1,0:T(8,128)(2,1)} %tok.1, f32[1,768]{1,0:T(1,128)} %reshape.189.gain, bf16[768,384]{1,0:T(8,128)(2,1)} %get-tuple-element.422.w_own, bf16[768,384]{1,0:T(8,128)(2,1)} %copy-done.53), custom_call_target="tpu_custom_call" | custom-call | flops 2415919104 | bytes 6291456 | tf_op jit(solution)/shard_map/values/pallas_call | solution.py:81
  113.6 16.4 %collective-permute-done.32.refs_6_ = bf16[384,1024]{1,0:T(8,128)(2,1)} collective-permute-done((bf16[384,1024]{1,0:T(8,128)(2,1)S(1)}, bf16[384,1024]{1,0:T(8,128)(2,1)}, u32[]{:S(2)}, u32[]{:S(2)}) %collective-permute-start.32) | collective-permute-done | bytes 786464 | tf_op jit(solution)/shard_map/ppermute | solution.py:946
  134.8 5.5 %masked.1.cot = bf16[4,512,768]{2,1,0:T(8,128)(2,1)} custom-call(s32[7]{0:T(128)} %concatenate.47.sc, bf16[2,8,2,64,768]{4,3,2,1,0:T(8,128)(2,1)} %bitcast.108, bf16[2,8,64,768]{3,2,1,0:T(8,128)(2,1)} %copy-done.75), custom_call_target="tpu_custom_call" | custom-call | bytes 6291456 | tf_op jit(solution)/shard_map/masked/pallas_call | solution.py:299
  140.3 11.4 %collective-permute-done.38.refs_11_ = bf16[384,1024]{1,0:T(8,128)(2,1)} collective-permute-done((bf16[384,1024]{1,0:T(8,128)(2,1)}, bf16[384,1024]{1,0:T(8,128)(2,1)}, u32[]{:S(2)}, u32[]{:S(2)}) %collective-permute-start.38) | collective-permute-done | bytes 786464 | tf_op jit(solution)/shard_map/ppermute | solution.py:946
  156.3 13.2 %mix.2 = (bf16[12,512,256]{2,1,0:T(8,128)(2,1)}, f32[12,512,256]{2,1,0:T(8,128)}, bf16[12,512,1024]{2,1,0:T(8,128)(2,1)}, bf16[12,512,256]{2,1,0:T(8,128)(2,1)}) custom-call(s32[7]{0:T(128)} %concatenate.47.sc, bf16[384,1024]{1,0:T(8,128)(2,1)} %bitcast.113, bf16[384,1024]{1,0:T(8,128)(2,1)} %collective-permute-done.24.refs_1_, ...), custom_call_target="tpu_custom_call" | custom-call | flops 3221225472 | bytes 20447232 | tf_op jit(solution)/shard_map/mix/pallas_call | solution.py:191
  175.7 8.5 %mix.3 = (bf16[12,512,256]{2,1,0:T(8,128)(2,1)}, f32[12,512,256]{2,1,0:T(8,128)}, bf16[12,512,1024]{2,1,0:T(8,128)(2,1)}, bf16[12,512,256]{2,1,0:T(8,128)(2,1)}) custom-call(s32[7]{0:T(128)} %concatenate.47.sc, bf16[384,1024]{1,0:T(8,128)(2,1)} %collective-permute-done.34.refs_0_, ...), custom_call_target="tpu_custom_call", output_to_operand_aliasing={{0}: (7, {}), {1}: (8, {}), {2}: (9, {}), {3}: (10, {})} | custom-call | flops 3221225472 | bytes 20447232 | tf_op jit(solution)/shard_map/mix/pallas_call | solution.py:191
  184.1 10.6 %pre.1 = (bf16[4,512,768]{2,1,0:T(8,128)(2,1)}, bf16[4,512,768]{2,1,0:T(8,128)(2,1)}, bf16[4,512,768]{2,1,0:T(8,128)(2,1)}) custom-call(s32[7]{0:T(128)} %concatenate.47.sc, bf16[2,8,2,64,768]{4,3,2,1,0:T(8,128)(2,1)} %bitcast.101, bf16[2,8,64,768]{3,2,1,0:T(8,128)(2,1)} %copy-done.74, bf16[12,512,256]{2,1,0:T(8,128)(2,1)} %get-tuple-element.482.heads, ...), custom_call_target="tpu_custom_call" | custom-call | flops 2415919104 | bytes 25165824 | tf_op jit(solution)/shard_map/pre/pallas_call | solution.py:270
  194.7 30.3 %units.1 = (bf16[2048,3072]{1,0:T(8,128)(2,1)}, bf16[2048,3072]{1,0:T(8,128)(2,1)}) custom-call(s32[7]{0:T(128)} %concatenate.47.sc, bf16[2048,768]{1,0:T(8,128)(2,1)} %bitcast.130, bf16[2048,768]{1,0:T(8,128)(2,1)} %bitcast.114, bf16[768,1536]{1,0:T(8,128)(2,1)} %get-tuple-element.488.up_own, bf16[768,1536]{1,0:T(8,128)(2,1)} %collective-permute-done.42.up_far, ...), custom_call_target="tpu_custom_call" | custom-call | flops 19327352832 | bytes 34603008 | tf_op jit(solution)/shard_map/units/pallas_call | solution.py:365
  225.0 28.1 %post.1 = (bf16[2,512,768]{2,1,0:T(8,128)(2,1)}, bf16[2,512,768]{2,1,0:T(8,128)(2,1)}, bf16[12,512,256]{2,1,0:T(8,128)(2,1)}, f32[1,768]{1,0:T(1,128)}) custom-call(s32[7]{0:T(128)} %concatenate.47.sc, bf16[4,512,768]{2,1,0:T(8,128)(2,1)} %get-tuple-element.485.resid, bf16[4,512,3072]{2,1,0:T(8,128)(2,1)} %bitcast.133, bf16[4,512,3072]{2,1,0:T(8,128)(2,1)} %bitcast.134, ...), custom_call_target="tpu_custom_call" | custom-call | flops 12079595520 | bytes 37748736 | tf_op jit(solution)/shard_map/post/pallas_call | solution.py:569
  253.2 10.0 %unmix.2 = (bf16[384,1024]{1,0:T(8,128)(2,1)}, bf16[384,1024]{1,0:T(8,128)(2,1)}, bf16[384,1024]{1,0:T(8,128)(2,1)}, bf16[384,1024]{1,0:T(8,128)(2,1)}, bf16[12,...) custom-call(s32[7]{0:T(128)} %concatenate.47.sc, bf16[12,1024,128]{2,1,0:T(8,128)(2,1)} %values.1.refs_12_.refs_4_.v_own, ...), custom_call_target="tpu_custom_call" | custom-call | flops 4831838208 | bytes 33030144 | tf_op jit(solution)/shard_map/unmix/pallas_call | solution.py:665
  268.4 19.5 %unmix.3 = (bf16[384,1024]{1,0:T(8,128)(2,1)}, bf16[384,1024]{1,0:T(8,128)(2,1)}, bf16[384,1024]{1,0:T(8,128)(2,1)}, bf16[384,1024]{1,0:T(8,128)(2,1)}, bf16[384...) custom-call(s32[7]{0:T(128)} %concatenate.47.sc, ...), custom_call_target="tpu_custom_call", output_to_operand_aliasing={{12}: (7, {}), {13}: (8, {})} | custom-call | flops 4831838208 | bytes 33030144 | tf_op jit(solution)/shard_map/unmix/pallas_call | solution.py:665
  294.0 16.2 %up_grad.1 = (bf16[768,1536]{1,0:T(8,128)(2,1)}, bf16[768,1536]{1,0:T(8,128)(2,1)}) custom-call(s32[7]{0:T(128)} %concatenate.47.sc, bf16[2048,768]{1,0:T(8,128)(2,1)} %bitcast.131, bf16[2048,3072]{1,0:T(8,128)(2,1)} %get-tuple-element.490.up_grad), custom_call_target="tpu_custom_call" | custom-call | flops 9663676416 | bytes 15728640 | tf_op jit(solution)/shard_map/up_grad/pallas_call | solution.py:428
  318.8 15.7 %down_grad.1 = (bf16[3072,384]{1,0:T(8,128)(2,1)}, bf16[3072,384]{1,0:T(8,128)(2,1)}) custom-call(s32[7]{0:T(128)} %concatenate.47.sc, bf16[2048,3072]{1,0:T(8,128)(2,1)} %get-tuple-element.558.active, bf16[2048,768]{1,0:T(8,128)(2,1)} %bitcast.115), custom_call_target="tpu_custom_call" | custom-call | flops 9663676416 | bytes 15728640 | tf_op jit(solution)/shard_map/down_grad/pallas_call | solution.py:397
  344.6 5.3 %out_grad.1 = (bf16[768,384]{1,0:T(8,128)(2,1)S(1)}, bf16[768,384]{1,0:T(8,128)(2,1)S(1)}) custom-call(s32[7]{0:T(128)S(1)} %copy-done.43, bf16[4,512,768]{2,1,0:T(8,128)(2,1)S(1)} %copy-done.46, bf16[2,512,768]{2,1,0:T(8,128)(2,1)S(1)} %copy-done.65, bf16[2,512,768]{2,1,0:T(8,128)(2,1)S(1)} %copy-done.51), custom_call_target="tpu_custom_call" | custom-call | flops 2415919104 | bytes 6291456 | tf_op jit(solution)/shard_map/out_grad/pallas_call | solution.py:468
  372.5 15.7 %out.3 = (bf16[2,512,768]{2,1,0:T(8,128)(2,1)S(1)}, bf16[2,512,768]{2,1,0:T(8,128)(2,1)}) custom-call(s32[7]{0:T(128)S(1)} %copy-done.43, bf16[4,512,3072]{2,1,0:T(8,128)(2,1)} %bitcast.132, bf16[4,512,768]{2,1,0:T(8,128)(2,1)S(1)} %copy-done.45, bf16[3072,384]{1,0:T(8,128)(2,1)S(1)} %copy-done.48, bf16[3072,384]{1,0:T(8,128)(2,1)} %collective-permute-done.43.dn_far), custom_call_target="tpu_custom_call" | custom-call | flops 9663676416 | bytes 23592960 | tf_op jit(solution)/shard_map/out/pallas_call | solution.py:502
  415.2 13.5 %close.1 = (f32[2,8,2,64,768]{4,3,2,1,0:T(8,128)}, f32[2,8,2,64,768]{4,3,2,1,0:T(8,128)}, bf16[768,768]{1,0:T(8,128)(2,1)S(1)}, f32[1,768]{1,0:T(1,128)S(1)}) custom-call(s32[7]{0:T(128)S(1)} %copy-done.43, bf16[2,8,2,64,768]{4,3,2,1,0:T(8,128)(2,1)S(1)} %bitcast.102, bf16[2,8,64,768]{3,2,1,0:T(8,128)(2,1)S(1)} %bitcast.106, ...), custom_call_target="tpu_custom_call" | custom-call | flops 4831838208 | bytes 29884416 | tf_op jit(solution)/shard_map/close/pallas_call | solution.py:755
  446.3 8.4 %collective-permute-done.75 = bf16[4,2,32,768]{3,2,0,1:T(8,128)(2,1)} collective-permute-done((bf16[4,2,32,768]{3,2,0,1:T(8,128)(2,1)}, bf16[4,2,32,768]{3,2,0,1:T(8,128)(2,1)}, u32[]{:S(2)}, u32[]{:S(2)}) %collective-permute-start.75) | collective-permute-done | bytes 393248 | tf_op jit(solution)/shard_map/ppermute | solution.py:946
  464.1 5.1 %collective-permute-done.80 = bf16[4,32,768]{2,1,0:T(8,128)(2,1)} collective-permute-done((bf16[4,32,768]{2,1,0:T(8,128)(2,1)S(1)}, bf16[4,32,768]{2,1,0:T(8,128)(2,1)}, u32[]{:S(2)}, u32[]{:S(2)}) %collective-permute-start.80) | collective-permute-done | bytes 196640 | tf_op jit(solution)/shard_map/ppermute | solution.py:946
  480.2 6.8 %collective-permute-done.85 = bf16[32,768]{1,0:T(8,128)(2,1)S(1)} collective-permute-done((bf16[32,768]{1,0:T(8,128)(2,1)S(1)}, bf16[32,768]{1,0:T(8,128)(2,1)S(1)}, u32[]{:S(2)}, u32[]{:S(2)}) %collective-permute-start.85) | collective-permute-done | bytes 49184 | tf_op jit(solution)/shard_map/ppermute | solution.py:950
  (432 shorter events, 213.1 us)
Async XLA Ops:
  109.9 22.9 %collective-permute-start.35 = (bf16[12,1024,128]{2,1,0:T(8,128)(2,1)}, bf16[12,1024,128]{2,1,0:T(8,128)(2,1)}, u32[]{:S(2)}, u32[]{:S(2)}) collective-permute-start(bf16[12,1024,128]{2,1,0:T(8,128)(2,1)} %values.1.refs_12_.refs_4_.v_own), channel_id=1, source_target_pairs={{0,1},{1,0},{2,3},{3,2},{4,5},{5,4},{6,7},{7,6},{8,9},{9,8},{10,11... | collective-permute-start | bytes 9437192 | tf_op jit(solution)/shard_map/ppermute | solution.py:946
  110.9 21.7 %collective-permute-start.34 = (bf16[384,1024]{1,0:T(8,128)(2,1)}, bf16[384,1024]{1,0:T(8,128)(2,1)}, u32[]{:S(2)}, u32[]{:S(2)}) collective-permute-start(bf16[384,1024]{1,0:T(8,128)(2,1)} %collective-permute-done.30.refs_8_), channel_id=1, source_target_pairs={{0,8},{1,9},{2,10},{3,11},{4,12},{5,13},{6,14},{7,15},{8,16},{9,17... | collective-permute-start | bytes 2359304 | tf_op jit(solution)/shard_map/ppermute | solution.py:950
  133.7 20.6 %collective-permute-start.37 = (bf16[384,1024]{1,0:T(8,128)(2,1)}, bf16[384,1024]{1,0:T(8,128)(2,1)}, u32[]{:S(2)}, u32[]{:S(2)}) collective-permute-start(bf16[384,1024]{1,0:T(8,128)(2,1)} %collective-permute-done.32.refs_6_), channel_id=1, source_target_pairs={{0,8},{1,9},{2,10},{3,11},{4,12},{5,13},{6,14},{7,15},{8,16},{9,17... | collective-permute-start | bytes 2359304 | tf_op jit(solution)/shard_map/ppermute | solution.py:950
  174.5 20.3 %collective-permute-start.42 = (bf16[768,1536]{1,0:T(8,128)(2,1)}, bf16[768,1536]{1,0:T(8,128)(2,1)}, u32[]{:S(2)}, u32[]{:S(2)}) collective-permute-start(bf16[768,1536]{1,0:T(8,128)(2,1)} %get-tuple-element.488.up_own), channel_id=1, source_target_pairs={{0,1},{1,0},{2,3},{3,2},{4,5},{5,4},{6,7},{7,6},{8,9},{9,8},{10,11... | collective-permute-start | bytes 7077896 | tf_op jit(solution)/shard_map/ppermute | solution.py:946
  264.4 23.5 %collective-permute-start.45 = (bf16[384,1024]{1,0:T(8,128)(2,1)}, bf16[384,1024]{1,0:T(8,128)(2,1)S(1)}, u32[]{:S(2)}, u32[]{:S(2)}) collective-permute-start(bf16[384,1024]{1,0:T(8,128)(2,1)} %get-tuple-element.503), channel_id=1, source_target_pairs={{0,24},{1,25},{2,26},{3,27},{4,28},{5,29},{6,30},{7,31},{8,0},{9,1... | collective-permute-start | bytes 2359304 | tf_op jit(solution)/shard_map/ppermute | solution.py:950
  266.6 21.3 %collective-permute-start.46 = (bf16[384,1024]{1,0:T(8,128)(2,1)}, bf16[384,1024]{1,0:T(8,128)(2,1)S(1)}, u32[]{:S(2)}, u32[]{:S(2)}) collective-permute-start(bf16[384,1024]{1,0:T(8,128)(2,1)} %get-tuple-element.504), channel_id=1, source_target_pairs={{0,2},{1,3},{2,0},{3,1},{4,6},{5,7},{6,4},{7,5},{8,10},{9,11},{10,... | collective-permute-start | bytes 2359304 | tf_op jit(solution)/shard_map/ppermute | solution.py:946
  267.1 20.8 %collective-permute-start.47 = (bf16[384,1024]{1,0:T(8,128)(2,1)}, bf16[384,1024]{1,0:T(8,128)(2,1)}, u32[]{:S(2)}, u32[]{:S(2)}) collective-permute-start(bf16[384,1024]{1,0:T(8,128)(2,1)} %get-tuple-element.505), channel_id=1, source_target_pairs={{0,4},{1,5},{2,6},{3,7},{4,0},{5,1},{6,2},{7,3},{8,12},{9,13},{10,... | collective-permute-start | bytes 2359304 | tf_op jit(solution)/shard_map/ppermute | solution.py:946
  288.0 24.7 %collective-permute-start.51 = (bf16[12,1024,128]{2,1,0:T(8,128)(2,1)}, bf16[12,1024,128]{2,1,0:T(8,128)(2,1)}, u32[]{:S(2)}, u32[]{:S(2)}) collective-permute-start(bf16[12,1024,128]{2,1,0:T(8,128)(2,1)} %get-tuple-element.542), channel_id=1, source_target_pairs={{0,1},{1,0},{2,3},{3,2},{4,5},{5,4},{6,7},{7,6},{8,9},{9,8},{10,11... | collective-permute-start | bytes 9437192 | tf_op jit(solution)/shard_map/ppermute | solution.py:946
  288.0 22.2 %collective-permute-start.48 = (bf16[384,1024]{1,0:T(8,128)(2,1)}, bf16[384,1024]{1,0:T(8,128)(2,1)S(1)}, u32[]{:S(2)}, u32[]{:S(2)}) collective-permute-start(bf16[384,1024]{1,0:T(8,128)(2,1)} %get-tuple-element.537), channel_id=1, source_target_pairs={{0,24},{1,25},{2,26},{3,27},{4,28},{5,29},{6,30},{7,31},{8,0},{9,1... | collective-permute-start | bytes 2359304 | tf_op jit(solution)/shard_map/ppermute | solution.py:950
  288.6 22.5 %collective-permute-start.49 = (bf16[384,1024]{1,0:T(8,128)(2,1)}, bf16[384,1024]{1,0:T(8,128)(2,1)S(1)}, u32[]{:S(2)}, u32[]{:S(2)}) collective-permute-start(bf16[384,1024]{1,0:T(8,128)(2,1)} %get-tuple-element.538), channel_id=1, source_target_pairs={{0,2},{1,3},{2,0},{3,1},{4,6},{5,7},{6,4},{7,5},{8,10},{9,11},{10,... | collective-permute-start | bytes 2359304 | tf_op jit(solution)/shard_map/ppermute | solution.py:946
  312.7 24.4 %collective-permute-start.55 = (bf16[768,1536]{1,0:T(8,128)(2,1)}, bf16[768,1536]{1,0:T(8,128)(2,1)S(1)}, u32[]{:S(2)}, u32[]{:S(2)}) collective-permute-start(bf16[768,1536]{1,0:T(8,128)(2,1)} %get-tuple-element.561), channel_id=1, source_target_pairs={{0,1},{1,0},{2,3},{3,2},{4,5},{5,4},{6,7},{7,6},{8,9},{9,8},{10,11... | collective-permute-start | bytes 7077896 | tf_op jit(solution)/shard_map/ppermute | solution.py:946
  312.7 21.9 %collective-permute-start.52 = (bf16[384,1024]{1,0:T(8,128)(2,1)}, bf16[384,1024]{1,0:T(8,128)(2,1)S(1)}, u32[]{:S(2)}, u32[]{:S(2)}) collective-permute-start(bf16[384,1024]{1,0:T(8,128)(2,1)} %get-tuple-element.550), channel_id=1, source_target_pairs={{0,24},{1,25},{2,26},{3,27},{4,28},{5,29},{6,30},{7,31},{8,0},{9,1... | collective-permute-start | bytes 2359304 | tf_op jit(solution)/shard_map/ppermute | solution.py:950
  337.1 20.9 %collective-permute-start.57 = (bf16[384,1024]{1,0:T(8,128)(2,1)}, bf16[384,1024]{1,0:T(8,128)(2,1)S(1)}, u32[]{:S(2)}, u32[]{:S(2)}) collective-permute-start(bf16[384,1024]{1,0:T(8,128)(2,1)} %get-tuple-element.572), channel_id=1, source_target_pairs={{0,2},{1,3},{2,0},{3,1},{4,6},{5,7},{6,4},{7,5},{8,10},{9,11},{10,... | collective-permute-start | bytes 2359304 | tf_op jit(solution)/shard_map/ppermute | solution.py:946
  363.0 26.4 %collective-permute-start.65 = (bf16[432,384]{1,0:T(8,128)(2,1)S(1)}, bf16[432,384]{1,0:T(8,128)(2,1)S(1)}, u32[]{:S(2)}, u32[]{:S(2)}) collective-permute-start(bf16[432,384]{1,0:T(8,128)(2,1)S(1)} %get-tuple-element.621), channel_id=1, source_target_pairs={{0,2},{1,3},{2,0},{3,1},{4,6},{5,7},{6,4},{7,5},{8,10},{9,11},{10,... | collective-permute-start | bytes 995336 | tf_op jit(solution)/shard_map/ppermute | solution.py:946
  363.5 26.6 %collective-permute-start.66 = (bf16[432,384]{1,0:T(8,128)(2,1)S(1)}, bf16[432,384]{1,0:T(8,128)(2,1)S(1)}, u32[]{:S(2)}, u32[]{:S(2)}) collective-permute-start(bf16[432,384]{1,0:T(8,128)(2,1)S(1)} %get-tuple-element.622), channel_id=1, source_target_pairs={{0,4},{1,5},{2,6},{3,7},{4,0},{5,1},{6,2},{7,3},{8,12},{9,13},{10,... | collective-permute-start | bytes 995336 | tf_op jit(solution)/shard_map/ppermute | solution.py:946
  364.3 26.6 %collective-permute-start.63 = (bf16[384,1024]{1,0:T(8,128)(2,1)S(1)}, bf16[384,1024]{1,0:T(8,128)(2,1)S(1)}, u32[]{:S(2)}, u32[]{:S(2)}) collective-permute-start(bf16[384,1024]{1,0:T(8,128)(2,1)S(1)} %copy-done.101), channel_id=1, source_target_pairs={{0,4},{1,5},{2,6},{3,7},{4,0},{5,1},{6,2},{7,3},{8,12},{9,13},{10,... | collective-permute-start | bytes 2359304 | tf_op jit(solution)/shard_map/ppermute | solution.py:946
  366.0 25.7 %collective-permute-start.61 = (bf16[384,1024]{1,0:T(8,128)(2,1)S(1)}, bf16[384,1024]{1,0:T(8,128)(2,1)S(1)}, u32[]{:S(2)}, u32[]{:S(2)}) collective-permute-start(bf16[384,1024]{1,0:T(8,128)(2,1)S(1)} %get-tuple-element.604), channel_id=1, source_target_pairs={{0,24},{1,25},{2,26},{3,27},{4,28},{5,29},{6,30},{7,31},{8,0},{9,1... | collective-permute-start | bytes 2359304 | tf_op jit(solution)/shard_map/ppermute | solution.py:950
  372.0 20.7 %collective-permute-start.62 = (bf16[384,1024]{1,0:T(8,128)(2,1)S(1)}, bf16[384,1024]{1,0:T(8,128)(2,1)S(1)}, u32[]{:S(2)}, u32[]{:S(2)}) collective-permute-start(bf16[384,1024]{1,0:T(8,128)(2,1)S(1)} %get-tuple-element.605), channel_id=1, source_target_pairs={{0,2},{1,3},{2,0},{3,1},{4,6},{5,7},{6,4},{7,5},{8,10},{9,11},{10,... | collective-permute-start | bytes 2359304 | tf_op jit(solution)/shard_map/ppermute | solution.py:946
  393.7 38.0 %collective-permute-start.67 = (bf16[432,384]{1,0:T(8,128)(2,1)}, bf16[432,384]{1,0:T(8,128)(2,1)}, u32[]{:S(2)}, u32[]{:S(2)}) collective-permute-start(bf16[432,384]{1,0:T(8,128)(2,1)} %copy-done.62), channel_id=1, source_target_pairs={{0,24},{1,25},{2,26},{3,27},{4,28},{5,29},{6,30},{7,31},{8,0},{9,1... | collective-permute-start | bytes 995336 | tf_op jit(solution)/shard_map/ppermute | solution.py:950
  398.3 33.4 %collective-permute-start.68 = (bf16[432,384]{1,0:T(8,128)(2,1)}, bf16[432,384]{1,0:T(8,128)(2,1)}, u32[]{:S(2)}, u32[]{:S(2)}) collective-permute-start(bf16[432,384]{1,0:T(8,128)(2,1)} %copy-done.61), channel_id=1, source_target_pairs={{0,2},{1,3},{2,0},{3,1},{4,6},{5,7},{6,4},{7,5},{8,10},{9,11},{10,... | collective-permute-start | bytes 995336 | tf_op jit(solution)/shard_map/ppermute | solution.py:946
  406.2 25.5 %collective-permute-start.69 = (bf16[432,384]{1,0:T(8,128)(2,1)}, bf16[432,384]{1,0:T(8,128)(2,1)}, u32[]{:S(2)}, u32[]{:S(2)}) collective-permute-start(bf16[432,384]{1,0:T(8,128)(2,1)} %get-tuple-element.642), channel_id=1, source_target_pairs={{0,4},{1,5},{2,6},{3,7},{4,0},{5,1},{6,2},{7,3},{8,12},{9,13},{10,... | collective-permute-start | bytes 995336 | tf_op jit(solution)/shard_map/ppermute | solution.py:946
  438.7 22.4 %collective-permute-start.72 = (bf16[432,384]{1,0:T(8,128)(2,1)S(1)}, bf16[432,384]{1,0:T(8,128)(2,1)S(1)}, u32[]{:S(2)}, u32[]{:S(2)}) collective-permute-start(bf16[432,384]{1,0:T(8,128)(2,1)S(1)} %get-tuple-element.668), channel_id=1, source_target_pairs={{0,2},{1,3},{2,0},{3,1},{4,6},{5,7},{6,4},{7,5},{8,10},{9,11},{10,... | collective-permute-start | bytes 995336 | tf_op jit(solution)/shard_map/ppermute | solution.py:946
  439.3 21.8 %collective-permute-start.73 = (bf16[432,384]{1,0:T(8,128)(2,1)S(1)}, bf16[432,384]{1,0:T(8,128)(2,1)S(1)}, u32[]{:S(2)}, u32[]{:S(2)}) collective-permute-start(bf16[432,384]{1,0:T(8,128)(2,1)S(1)} %get-tuple-element.669), channel_id=1, source_target_pairs={{0,4},{1,5},{2,6},{3,7},{4,0},{5,1},{6,2},{7,3},{8,12},{9,13},{10,... | collective-permute-start | bytes 995336 | tf_op jit(solution)/shard_map/ppermute | solution.py:946
  445.0 25.2 %collective-permute-start.81 = (f32[3,64,1024]{2,1,0:T(8,128)}, f32[3,64,1024]{2,1,0:T(8,128)}, u32[]{:S(2)}, u32[]{:S(2)}) collective-permute-start(f32[3,64,1024]{2,1,0:T(8,128)} %get-tuple-element.705), channel_id=1, source_target_pairs={{0,1},{1,0},{2,3},{3,2},{4,5},{5,4},{6,7},{7,6},{8,9},{9,8},{10,11... | collective-permute-start | bytes 2359304 | tf_op jit(solution)/shard_map/ppermute | solution.py:946
  (167 other events, 1979.9 us)

commit v15 on v13

--- a/solution.py
+++ b/solution.py
@@ -404,7 +404,7 @@
             scratch_shapes=[pltpu.VMEM((512, WIDTH), BF16)],
         ),
         out_shape=[jax.ShapeDtypeStruct((FF, SIDE), BF16)] * 2,
-        compiler_params=params(VMEM),
+        compiler_params=params(LESS),
         cost_estimate=pl.CostEstimate(
             flops=2 * ROWS * WIDTH * FF, bytes_accessed=2 * ROWS * (WIDTH + FF), transcendentals=0
         ),
@@ -437,7 +437,7 @@
             ],
         ),
         out_shape=[jax.ShapeDtypeStruct((WIDTH, FF // 2), BF16)] * 2,
-        compiler_params=params(VMEM),
+        compiler_params=params(LESS),
         cost_estimate=pl.CostEstimate(
             flops=2 * ROWS * WIDTH * FF, bytes_accessed=2 * ROWS * (WIDTH + FF), transcendentals=0
         ),
@@ -475,7 +475,7 @@
             scratch_shapes=[pltpu.VMEM((WIDTH, WIDTH), F32)],
         ),
         out_shape=[jax.ShapeDtypeStruct((WIDTH, SIDE), BF16)] * 2,
-        compiler_params=params(VMEM),
+        compiler_params=params(LESS),
         cost_estimate=pl.CostEstimate(
             flops=2 * ROWS * WIDTH * WIDTH, bytes_accessed=4 * ROWS * WIDTH, transcendentals=0
         ),
@@ -517,7 +517,7 @@
             jax.ShapeDtypeStruct((2, HROWS, WIDTH), BF16),
             jax.ShapeDtypeStruct((2, HROWS, WIDTH), BF16),
         ],
-        compiler_params=params(VMEM),
+        compiler_params=params(LESS),
         cost_estimate=pl.CostEstimate(
             flops=2 * ROWS * WIDTH * FF, bytes_accessed=ROWS * (2 * FF + 7 * WIDTH), transcendentals=0
         ),
@@ -771,7 +771,7 @@
             jax.ShapeDtypeStruct((2, WIDTH, SIDE), BF16),
             jax.ShapeDtypeStruct((1, WIDTH), F32),
         ],
-        compiler_params=params(VMEM),
+        compiler_params=params(LESS),
         cost_estimate=pl.CostEstimate(
             flops=4 * 2 * LMAX * WIDTH * WIDTH, bytes_accessed=38 * LMAX * WIDTH, transcendentals=0
         ),
@@ -1003,7 +1003,12 @@
     sums = list(dict.fromkeys(targets))
     groups = [(len(got) + i, *(j for j in range(len(got)) if targets[j] == at)) for i, at in enumerate(sums)]
     values = [*got, *(have[at] for at in sums)]
-    return {**have, **dict(zip(sums, run_add(groups, values, F32 if step == len(STEPS) - 1 else BF16)))}
+    dtype = F32 if step == len(STEPS) - 1 else BF16
+    if values[0].shape[1] == LMAX:
+        totals = run_add(groups, values, dtype)
+    else:
+        totals = [sum(values[i].astype(F32) for i in group).astype(dtype) for group in groups]
+    return {**have, **dict(zip(sums, totals))}
 
 
 together = lax.optimization_barrier
@@ -1097,29 +1102,31 @@
     output, tokens_grad, d_value, d_gain_one = run_close(
         sc, tokens, res_own, res_got, out_own, other(out_far), back_own, back_got, gain_one, value, value_far
     )
+    sums, got, output, tokens_grad, d_value, d_gain_one = together(
+        (sums, got, output, tokens_grad, d_value, d_gain_one)
+    )
+    sums = scatter_add(sums, got, 1)
+
+    sums, got = scatter_send(sums, 2)
     gain_pair = jnp.concatenate([d_gain_one, d_gain_two]).reshape(2, 16, 1, 48).astype(BF16)
     gain_pair = jnp.pad(gain_pair, ((0, 0), (0, 0), (0, 15), (0, SIDE - 48)))
     small = jnp.concatenate([d_value.reshape(2, 16, 48, SIDE), gain_pair], 2)
-    sums, got, output, tokens_grad, small = together((sums, got, output, tokens_grad, small))
-    sums = scatter_add(sums, got, 1)
-
-    sums, got = scatter_send(sums, 2)
     small = add_low(pick(small, core), other(pick(small, 1 - core))).reshape(4, 2, 2, 64, SIDE)
+    small = add_low(pick(small, x, 2), swap(pick(small, 1 - x, 2), TO_X))
     sums, got, small = together((sums, got, small))
     sums = scatter_add(sums, got, 2)
 
     sums, got = scatter_send(sums, 3)
-    small = add_low(pick(small, x, 2), swap(pick(small, 1 - x, 2), TO_X))
+    small = add_low(pick(small, y, 1), swap(pick(small, 1 - y, 1), TO_Y))
     blocks, blocks_far = pick(rand_sum, core), other(pick(rand_sum, 1 - core))
     sums, got, small, blocks, blocks_far = together((sums, got, small, blocks, blocks_far))
     sums = scatter_add(sums, got, 3)
 
     sums, got = scatter_send(sums, 4)
-    small = add_low(pick(small, y, 1), swap(pick(small, 1 - y, 1), TO_Y))
-    sums, got, small = together((sums, got, small))
     small_sum = pick(small, z).astype(F32)
     for k in range(1, PLANES):
         small_sum = small_sum + ring(pick(small, lax.rem(z + PLANES - k, PLANES)), -k).astype(F32)
+    sums, got, small_sum = together((sums, got, small_sum))
     big_sum = scatter_add(sums, got, 4)[0, 0, 0]
     big_far, small_far = other(big_sum), other(small_sum)
 

time: 499 us -> 478 us (0.958)
  Pallas kernels: 235 us -> 210 us
    pallas_call x10 -> x5, Pallas kernels: 15.2 us -> 4.01 us  [run_add(): pl.pallas_call(partial(add_kernel, groups), in_specs=[here] * len(values)...]
    unnamed x180 -> x184, local copies, waits for them, and re-layouts: 25.3 us -> 26.8 us
  transfers between devices with their start and end apart: 89 -> 89, of which waited for: 39 -> 38; matrix products, arithmetic and copies ran while one was open for 4% -> 3% of each run, Pallas kernels for 36% -> 32%
where the time goes in v15:
time: 478 us; the launch traced here: 472 us
  Pallas kernels  210 us (44%)
  waiting for transfers between devices  139 us (29%)
  starting transfers between devices  74.5 us (16%)
  local copies, waits for them, and re-layouts  37 us (8%)
  other arithmetic  9.1 us (2%)
    ppermute x66, waiting for transfers between devices, swap(): return lax.ppermute(x, BOTH, [(d, d ^ bit) for d in range(DEVICES)])  88.4 us
    ppermute x23, waiting for transfers between devices, ring(): lax.ppermute(x, BOTH, [(d, (d + 8 * way) % DEVICES) for d in range(DEVICE...  50.5 us
    ppermute x66, starting transfers between devices, swap(): return lax.ppermute(x, BOTH, [(d, d ^ bit) for d in range(DEVICES)])  47.9 us
    pallas_call x1, Pallas kernels, run_units(): pl.pallas_call(units_kernel, grid_spec=pltpu.PrefetchScalarGridSpec(num_s...  30.3 us
    pallas_call x2, Pallas kernels, run_unmix(): pl.pallas_call(partial(unmix_kernel, count, bool(carry)), grid_spec=pltpu...  29.4 us
    pallas_call x1, Pallas kernels, run_post(): pl.pallas_call(post_kernel, grid_spec=pltpu.PrefetchScalarGridSpec(num_sc...  28.1 us
    unnamed x184, local copies, waits for them, and re-layouts  26.8 us
    ppermute x23, starting transfers between devices, ring(): lax.ppermute(x, BOTH, [(d, (d + 8 * way) % DEVICES) for d in range(DEVICE...  26.6 us
  transfers between devices with their start and end apart: 89, of which 38 were waited for; matrix products, arithmetic and copies ran while one was open for 3% of the time, Pallas kernels for 32%

profile of v15, /device:TPU:0, one launch (start us, length us, event | category | flops | bytes accessed | tf_op | source)
XLA Modules:
  0.0 472.0 jit_solution(6358662559920156341)
XLA Ops:
  16.6 8.3 %collective-permute-done.7.refs_4_ = bf16[496,384]{1,0:T(8,128)(2,1)S(1)} collective-permute-done((bf16[496,384]{1,0:T(8,128)(2,1)}, bf16[496,384]{1,0:T(8,128)(2,1)S(1)}, u32[]{:S(2)}, u32[]{:S(2)}) %collective-permute-start.7) | collective-permute-done | bytes 380960 | tf_op jit(solution)/shard_map/ppermute | solution.py:952
  31.6 7.5 %collective-permute-done.9.refs_3_ = bf16[496,384]{1,0:T(8,128)(2,1)S(1)} collective-permute-done((bf16[496,384]{1,0:T(8,128)(2,1)}, bf16[496,384]{1,0:T(8,128)(2,1)S(1)}, u32[]{:S(2)}, u32[]{:S(2)}) %collective-permute-start.9) | collective-permute-done | bytes 380960 | tf_op jit(solution)/shard_map/ppermute | solution.py:948
  45.1 6.2 %collective-permute-done.13.refs_6_ = bf16[496,384]{1,0:T(8,128)(2,1)S(1)} collective-permute-done((bf16[496,384]{1,0:T(8,128)(2,1)S(1)}, bf16[496,384]{1,0:T(8,128)(2,1)S(1)}, u32[]{:S(2)}, u32[]{:S(2)}) %collective-permute-start.13) | collective-permute-done | bytes 380960 | tf_op jit(solution)/shard_map/ppermute | solution.py:948
  67.4 7.1 %collective-permute-done.23.refs_15_ = bf16[496,384]{1,0:T(8,128)(2,1)S(1)} collective-permute-done((bf16[496,384]{1,0:T(8,128)(2,1)S(1)}, bf16[496,384]{1,0:T(8,128)(2,1)S(1)}, u32[]{:S(2)}, u32[]{:S(2)}) %collective-permute-start.23) | collective-permute-done | bytes 380960 | tf_op jit(solution)/shard_map/ppermute | solution.py:952
  77.8 7.2 %place.1 = (bf16[3072,384]{1,0:T(8,128)(2,1)}, bf16[768,1536]{1,0:T(8,128)(2,1)}, bf16[768,384]{1,0:T(8,128)(2,1)}, bf16[768,384]{1,0:T(8,128)(2,1)}, bf16[256,384]{1,0:T(8,128)(2,1)}) custom-call(s32[7]{0:T(128)} %concatenate.54.sc, bf16[496,384]{1,0:T(8,128)(2,1)} %pack.1.refs_0_, bf16[496,384]{1,0:T(8,128)(2,1)} %copy-done.61, ...), custom_call_target="tpu_custom_call" | custom-call | bytes 12189696 | tf_op jit(solution)/shard_map/place/pallas_call | solution.py:854
  95.6 7.8 %values.1.refs_12_.refs_4_.v_own = bf16[12,1024,128]{2,1,0:T(8,128)(2,1)} custom-call(s32[7]{0:T(128)} %concatenate.54.sc, bf16[2,1024,768]{2,1,0:T(8,128)(2,1)} %tok.1, f32[1,768]{1,0:T(1,128)} %reshape.205.gain, bf16[768,384]{1,0:T(8,128)(2,1)} %get-tuple-element.415.w_own, bf16[768,384]{1,0:T(8,128)(2,1)} %copy-done.37), custom_call_target="tpu_custom_call" | custom-call | flops 2415919104 | bytes 6291456 | tf_op jit(solution)/shard_map/values/pallas_call | solution.py:81
  113.7 16.7 %collective-permute-done.32.refs_6_ = bf16[384,1024]{1,0:T(8,128)(2,1)} collective-permute-done((bf16[384,1024]{1,0:T(8,128)(2,1)}, bf16[384,1024]{1,0:T(8,128)(2,1)}, u32[]{:S(2)}, u32[]{:S(2)}) %collective-permute-start.32) | collective-permute-done | bytes 786464 | tf_op jit(solution)/shard_map/ppermute | solution.py:948
  135.2 5.5 %masked.1.cot = bf16[4,512,768]{2,1,0:T(8,128)(2,1)} custom-call(s32[7]{0:T(128)} %concatenate.54.sc, bf16[2,8,2,64,768]{4,3,2,1,0:T(8,128)(2,1)} %bitcast.121, bf16[2,8,64,768]{3,2,1,0:T(8,128)(2,1)} %copy-done.54), custom_call_target="tpu_custom_call" | custom-call | bytes 6291456 | tf_op jit(solution)/shard_map/masked/pallas_call | solution.py:299
  140.7 11.8 %collective-permute-done.38.refs_11_ = bf16[384,1024]{1,0:T(8,128)(2,1)} collective-permute-done((bf16[384,1024]{1,0:T(8,128)(2,1)}, bf16[384,1024]{1,0:T(8,128)(2,1)}, u32[]{:S(2)}, u32[]{:S(2)}) %collective-permute-start.38) | collective-permute-done | bytes 786464 | tf_op jit(solution)/shard_map/ppermute | solution.py:948
  157.1 13.2 %mix.2 = (bf16[12,512,256]{2,1,0:T(8,128)(2,1)}, f32[12,512,256]{2,1,0:T(8,128)}, bf16[12,512,1024]{2,1,0:T(8,128)(2,1)}, bf16[12,512,256]{2,1,0:T(8,128)(2,1)}) custom-call(s32[7]{0:T(128)} %concatenate.54.sc, bf16[384,1024]{1,0:T(8,128)(2,1)} %bitcast.126, bf16[384,1024]{1,0:T(8,128)(2,1)} %collective-permute-done.24.refs_1_, ...), custom_call_target="tpu_custom_call" | custom-call | flops 3221225472 | bytes 20447232 | tf_op jit(solution)/shard_map/mix/pallas_call | solution.py:191
  170.3 5.0 %collective-permute-done.41.refs_3_ = bf16[384,1024]{1,0:T(8,128)(2,1)} collective-permute-done((bf16[384,1024]{1,0:T(8,128)(2,1)}, bf16[384,1024]{1,0:T(8,128)(2,1)}, u32[]{:S(2)}, u32[]{:S(2)}) %collective-permute-start.41) | collective-permute-done | bytes 786464 | tf_op jit(solution)/shard_map/ppermute | solution.py:952
  176.5 8.5 %mix.3 = (bf16[12,512,256]{2,1,0:T(8,128)(2,1)}, f32[12,512,256]{2,1,0:T(8,128)}, bf16[12,512,1024]{2,1,0:T(8,128)(2,1)}, bf16[12,512,256]{2,1,0:T(8,128)(2,1)}) custom-call(s32[7]{0:T(128)} %concatenate.54.sc, bf16[384,1024]{1,0:T(8,128)(2,1)} %copy-done.58, ...), custom_call_target="tpu_custom_call", output_to_operand_aliasing={{0}: (7, {}), {1}: (8, {}), {2}: (9, {}), {3}: (10, {})} | custom-call | flops 3221225472 | bytes 20447232 | tf_op jit(solution)/shard_map/mix/pallas_call | solution.py:191
  185.0 10.5 %pre.1 = (bf16[4,512,768]{2,1,0:T(8,128)(2,1)}, bf16[4,512,768]{2,1,0:T(8,128)(2,1)}, bf16[4,512,768]{2,1,0:T(8,128)(2,1)}) custom-call(s32[7]{0:T(128)} %concatenate.54.sc, bf16[2,8,2,64,768]{4,3,2,1,0:T(8,128)(2,1)} %bitcast.106, bf16[2,8,64,768]{3,2,1,0:T(8,128)(2,1)} %copy-done.53, bf16[12,512,256]{2,1,0:T(8,128)(2,1)} %get-tuple-element.475.heads, ...), custom_call_target="tpu_custom_call" | custom-call | flops 2415919104 | bytes 25165824 | tf_op jit(solution)/shard_map/pre/pallas_call | solution.py:270
  195.5 30.3 %units.1 = (bf16[2048,3072]{1,0:T(8,128)(2,1)}, bf16[2048,3072]{1,0:T(8,128)(2,1)}) custom-call(s32[7]{0:T(128)} %concatenate.54.sc, bf16[2048,768]{1,0:T(8,128)(2,1)} %bitcast.112, bf16[2048,768]{1,0:T(8,128)(2,1)} %bitcast.109, bf16[768,1536]{1,0:T(8,128)(2,1)} %get-tuple-element.481.up_own, bf16[768,1536]{1,0:T(8,128)(2,1)} %collective-permute-done.42.up_far, ...), custom_call_target="tpu_custom_call" | custom-call | flops 19327352832 | bytes 34603008 | tf_op jit(solution)/shard_map/units/pallas_call | solution.py:365
  225.8 28.1 %post.1 = (bf16[2,512,768]{2,1,0:T(8,128)(2,1)}, bf16[2,512,768]{2,1,0:T(8,128)(2,1)}, bf16[12,512,256]{2,1,0:T(8,128)(2,1)}, f32[1,768]{1,0:T(1,128)}) custom-call(s32[7]{0:T(128)} %concatenate.54.sc, bf16[4,512,768]{2,1,0:T(8,128)(2,1)} %get-tuple-element.478.resid, bf16[4,512,3072]{2,1,0:T(8,128)(2,1)} %bitcast.117, bf16[4,512,3072]{2,1,0:T(8,128)(2,1)} %bitcast.118, ...), custom_call_target="tpu_custom_call" | custom-call | flops 12079595520 | bytes 37748736 | tf_op jit(solution)/shard_map/post/pallas_call | solution.py:569
  253.9 9.9 %unmix.2 = (bf16[384,1024]{1,0:T(8,128)(2,1)}, bf16[384,1024]{1,0:T(8,128)(2,1)}, bf16[384,1024]{1,0:T(8,128)(2,1)}, bf16[384,1024]{1,0:T(8,128)(2,1)}, bf16[12,...) custom-call(s32[7]{0:T(128)} %concatenate.54.sc, bf16[12,1024,128]{2,1,0:T(8,128)(2,1)} %values.1.refs_12_.refs_4_.v_own, ...), custom_call_target="tpu_custom_call" | custom-call | flops 4831838208 | bytes 33030144 | tf_op jit(solution)/shard_map/unmix/pallas_call | solution.py:665
  269.1 19.5 %unmix.3 = (bf16[384,1024]{1,0:T(8,128)(2,1)}, bf16[384,1024]{1,0:T(8,128)(2,1)}, bf16[384,1024]{1,0:T(8,128)(2,1)}, bf16[384,1024]{1,0:T(8,128)(2,1)}, bf16[384...) custom-call(s32[7]{0:T(128)} %concatenate.54.sc, ...), custom_call_target="tpu_custom_call", output_to_operand_aliasing={{12}: (7, {}), {13}: (8, {})} | custom-call | flops 4831838208 | bytes 33030144 | tf_op jit(solution)/shard_map/unmix/pallas_call | solution.py:665
  301.3 14.2 %up_grad.1 = (bf16[768,1536]{1,0:T(8,128)(2,1)S(1)}, bf16[768,1536]{1,0:T(8,128)(2,1)}) custom-call(s32[7]{0:T(128)S(1)} %copy-done.25, bf16[2048,768]{1,0:T(8,128)(2,1)S(1)} %bitcast.113, bf16[2048,3072]{1,0:T(8,128)(2,1)S(1)} %copy-done.46), custom_call_target="tpu_custom_call" | custom-call | flops 9663676416 | bytes 15728640 | tf_op jit(solution)/shard_map/up_grad/pallas_call | solution.py:428
  323.8 12.9 %down_grad.1 = (bf16[3072,384]{1,0:T(8,128)(2,1)S(1)}, bf16[3072,384]{1,0:T(8,128)(2,1)S(1)}) custom-call(s32[7]{0:T(128)S(1)} %copy-done.25, bf16[2048,3072]{1,0:T(8,128)(2,1)S(1)} %copy-done.45, bf16[2048,768]{1,0:T(8,128)(2,1)S(1)} %bitcast.110), custom_call_target="tpu_custom_call" | custom-call | flops 9663676416 | bytes 15728640 | tf_op jit(solution)/shard_map/down_grad/pallas_call | solution.py:397
  344.9 5.3 %out_grad.1 = (bf16[768,384]{1,0:T(8,128)(2,1)S(1)}, bf16[768,384]{1,0:T(8,128)(2,1)S(1)}) custom-call(s32[7]{0:T(128)S(1)} %copy-done.25, bf16[4,512,768]{2,1,0:T(8,128)(2,1)S(1)} %copy-done.28, bf16[2,512,768]{2,1,0:T(8,128)(2,1)S(1)} %copy-done.47, bf16[2,512,768]{2,1,0:T(8,128)(2,1)S(1)} %copy-done.34), custom_call_target="tpu_custom_call" | custom-call | flops 2415919104 | bytes 6291456 | tf_op jit(solution)/shard_map/out_grad/pallas_call | solution.py:468
  374.2 15.0 %out.3 = (bf16[2,512,768]{2,1,0:T(8,128)(2,1)S(1)}, bf16[2,512,768]{2,1,0:T(8,128)(2,1)S(1)}) custom-call(s32[7]{0:T(128)S(1)} %copy-done.25, bf16[4,512,3072]{2,1,0:T(8,128)(2,1)} %bitcast.116, bf16[4,512,768]{2,1,0:T(8,128)(2,1)S(1)} %copy-done.27, bf16[3072,384]{1,0:T(8,128)(2,1)S(1)} %copy-done.31, bf16[3072,384]{1,0:T(8,128)(2,1)} %collective-permute-done.43.dn_far), custom_call_target="tpu_custom_call" | custom-call | flops 9663676416 | bytes 23592960 | tf_op jit(solution)/shard_map/out/pallas_call | solution.py:502
  400.0 13.4 %close.1 = (f32[2,8,2,64,768]{4,3,2,1,0:T(8,128)}, f32[2,8,2,64,768]{4,3,2,1,0:T(8,128)}, bf16[2,768,384]{2,1,0:T(8,128)(2,1)S(1)}, f32[1,768]{1,0:T(1,128)S(1)}) custom-call(s32[7]{0:T(128)S(1)} %copy-done.25, bf16[2,8,2,64,768]{4,3,2,1,0:T(8,128)(2,1)S(1)} %bitcast.107, bf16[2,8,64,768]{3,2,1,0:T(8,128)(2,1)S(1)} %bitcast.119, ...), custom_call_target="tpu_custom_call" | custom-call | flops 4831838208 | bytes 29884416 | tf_op jit(solution)/shard_map/close/pallas_call | solution.py:757
  424.5 9.4 %collective-permute-done.75 = bf16[4,2,64,384]{3,2,1,0:T(8,128)(2,1)S(1)} collective-permute-done((bf16[4,2,64,384]{3,2,1,0:T(8,128)(2,1)S(1)}, bf16[4,2,64,384]{3,2,1,0:T(8,128)(2,1)S(1)}, u32[]{:S(2)}, u32[]{:S(2)}) %collective-permute-start.75) | collective-permute-done | bytes 393248 | tf_op jit(solution)/shard_map/ppermute | solution.py:948
  434.0 6.3 %collective-permute-done.72 = bf16[432,384]{1,0:T(8,128)(2,1)S(1)} collective-permute-done((bf16[432,384]{1,0:T(8,128)(2,1)S(1)}, bf16[432,384]{1,0:T(8,128)(2,1)S(1)}, u32[]{:S(2)}, u32[]{:S(2)}) %collective-permute-start.72) | collective-permute-done | bytes 331808 | tf_op jit(solution)/shard_map/ppermute | solution.py:948
  (417 shorter events, 190.1 us)
Async XLA Ops:
  110.0 23.3 %collective-permute-start.35 = (bf16[12,1024,128]{2,1,0:T(8,128)(2,1)}, bf16[12,1024,128]{2,1,0:T(8,128)(2,1)}, u32[]{:S(2)}, u32[]{:S(2)}) collective-permute-start(bf16[12,1024,128]{2,1,0:T(8,128)(2,1)} %values.1.refs_12_.refs_4_.v_own), channel_id=1, source_target_pairs={{0,1},{1,0},{2,3},{3,2},{4,5},{5,4},{6,7},{7,6},{8,9},{9,8},{10,11... | collective-permute-start | bytes 9437192 | tf_op jit(solution)/shard_map/ppermute | solution.py:948
  110.1 20.3 %collective-permute-start.32 = (bf16[384,1024]{1,0:T(8,128)(2,1)}, bf16[384,1024]{1,0:T(8,128)(2,1)}, u32[]{:S(2)}, u32[]{:S(2)}) collective-permute-start(bf16[384,1024]{1,0:T(8,128)(2,1)} %collective-permute-done.26.refs_4_), channel_id=1, source_target_pairs={{0,4},{1,5},{2,6},{3,7},{4,0},{5,1},{6,2},{7,3},{8,12},{9,13},{10,... | collective-permute-start | bytes 2359304 | tf_op jit(solution)/shard_map/ppermute | solution.py:948
  111.1 21.4 %collective-permute-start.34 = (bf16[384,1024]{1,0:T(8,128)(2,1)S(1)}, bf16[384,1024]{1,0:T(8,128)(2,1)S(1)}, u32[]{:S(2)}, u32[]{:S(2)}) collective-permute-start(bf16[384,1024]{1,0:T(8,128)(2,1)S(1)} %collective-permute-done.30.refs_8_), channel_id=1, source_target_pairs={{0,8},{1,9},{2,10},{3,11},{4,12},{5,13},{6,14},{7,15},{8,16},{9,17... | collective-permute-start | bytes 2359304 | tf_op jit(solution)/shard_map/ppermute | solution.py:952
  134.5 20.6 %collective-permute-start.37 = (bf16[384,1024]{1,0:T(8,128)(2,1)}, bf16[384,1024]{1,0:T(8,128)(2,1)}, u32[]{:S(2)}, u32[]{:S(2)}) collective-permute-start(bf16[384,1024]{1,0:T(8,128)(2,1)} %collective-permute-done.32.refs_6_), channel_id=1, source_target_pairs={{0,8},{1,9},{2,10},{3,11},{4,12},{5,13},{6,14},{7,15},{8,16},{9,17... | collective-permute-start | bytes 2359304 | tf_op jit(solution)/shard_map/ppermute | solution.py:952
  134.7 20.5 %collective-permute-start.36 = (bf16[384,1024]{1,0:T(8,128)(2,1)}, bf16[384,1024]{1,0:T(8,128)(2,1)}, u32[]{:S(2)}, u32[]{:S(2)}) collective-permute-start(bf16[384,1024]{1,0:T(8,128)(2,1)} %collective-permute-done.32.refs_6_), channel_id=1, source_target_pairs={{0,2},{1,3},{2,0},{3,1},{4,6},{5,7},{6,4},{7,5},{8,10},{9,11},{10,... | collective-permute-start | bytes 2359304 | tf_op jit(solution)/shard_map/ppermute | solution.py:948
  175.3 20.2 %collective-permute-start.42 = (bf16[768,1536]{1,0:T(8,128)(2,1)}, bf16[768,1536]{1,0:T(8,128)(2,1)}, u32[]{:S(2)}, u32[]{:S(2)}) collective-permute-start(bf16[768,1536]{1,0:T(8,128)(2,1)} %get-tuple-element.481.up_own), channel_id=1, source_target_pairs={{0,1},{1,0},{2,3},{3,2},{4,5},{5,4},{6,7},{7,6},{8,9},{9,8},{10,11... | collective-permute-start | bytes 7077896 | tf_op jit(solution)/shard_map/ppermute | solution.py:948
  175.3 20.2 %collective-permute-start.43 = (bf16[3072,384]{1,0:T(8,128)(2,1)S(1)}, bf16[3072,384]{1,0:T(8,128)(2,1)}, u32[]{:S(2)}, u32[]{:S(2)}) collective-permute-start(bf16[3072,384]{1,0:T(8,128)(2,1)S(1)} %copy-done.30), channel_id=1, source_target_pairs={{0,1},{1,0},{2,3},{3,2},{4,5},{5,4},{6,7},{7,6},{8,9},{9,8},{10,11... | collective-permute-start | bytes 7077896 | tf_op jit(solution)/shard_map/ppermute | solution.py:948
  265.1 23.5 %collective-permute-start.45 = (bf16[384,1024]{1,0:T(8,128)(2,1)}, bf16[384,1024]{1,0:T(8,128)(2,1)S(1)}, u32[]{:S(2)}, u32[]{:S(2)}) collective-permute-start(bf16[384,1024]{1,0:T(8,128)(2,1)} %get-tuple-element.496), channel_id=1, source_target_pairs={{0,24},{1,25},{2,26},{3,27},{4,28},{5,29},{6,30},{7,31},{8,0},{9,1... | collective-permute-start | bytes 2359304 | tf_op jit(solution)/shard_map/ppermute | solution.py:952
  267.4 21.2 %collective-permute-start.46 = (bf16[384,1024]{1,0:T(8,128)(2,1)}, bf16[384,1024]{1,0:T(8,128)(2,1)S(1)}, u32[]{:S(2)}, u32[]{:S(2)}) collective-permute-start(bf16[384,1024]{1,0:T(8,128)(2,1)} %get-tuple-element.497), channel_id=1, source_target_pairs={{0,2},{1,3},{2,0},{3,1},{4,6},{5,7},{6,4},{7,5},{8,10},{9,11},{10,... | collective-permute-start | bytes 2359304 | tf_op jit(solution)/shard_map/ppermute | solution.py:948
  268.0 20.6 %collective-permute-start.47 = (bf16[384,1024]{1,0:T(8,128)(2,1)}, bf16[384,1024]{1,0:T(8,128)(2,1)}, u32[]{:S(2)}, u32[]{:S(2)}) collective-permute-start(bf16[384,1024]{1,0:T(8,128)(2,1)} %get-tuple-element.498), channel_id=1, source_target_pairs={{0,4},{1,5},{2,6},{3,7},{4,0},{5,1},{6,2},{7,3},{8,12},{9,13},{10,... | collective-permute-start | bytes 2359304 | tf_op jit(solution)/shard_map/ppermute | solution.py:948
  288.6 27.0 %collective-permute-start.51 = (bf16[12,1024,128]{2,1,0:T(8,128)(2,1)}, bf16[12,1024,128]{2,1,0:T(8,128)(2,1)}, u32[]{:S(2)}, u32[]{:S(2)}) collective-permute-start(bf16[12,1024,128]{2,1,0:T(8,128)(2,1)} %get-tuple-element.535), channel_id=1, source_target_pairs={{0,1},{1,0},{2,3},{3,2},{4,5},{5,4},{6,7},{7,6},{8,9},{9,8},{10,11... | collective-permute-start | bytes 9437192 | tf_op jit(solution)/shard_map/ppermute | solution.py:948
  288.7 26.9 %collective-permute-start.48 = (bf16[384,1024]{1,0:T(8,128)(2,1)}, bf16[384,1024]{1,0:T(8,128)(2,1)S(1)}, u32[]{:S(2)}, u32[]{:S(2)}) collective-permute-start(bf16[384,1024]{1,0:T(8,128)(2,1)} %get-tuple-element.530), channel_id=1, source_target_pairs={{0,24},{1,25},{2,26},{3,27},{4,28},{5,29},{6,30},{7,31},{8,0},{9,1... | collective-permute-start | bytes 2359304 | tf_op jit(solution)/shard_map/ppermute | solution.py:952
  289.5 26.1 %collective-permute-start.49 = (bf16[384,1024]{1,0:T(8,128)(2,1)}, bf16[384,1024]{1,0:T(8,128)(2,1)S(1)}, u32[]{:S(2)}, u32[]{:S(2)}) collective-permute-start(bf16[384,1024]{1,0:T(8,128)(2,1)} %get-tuple-element.531), channel_id=1, source_target_pairs={{0,2},{1,3},{2,0},{3,1},{4,6},{5,7},{6,4},{7,5},{8,10},{9,11},{10,... | collective-permute-start | bytes 2359304 | tf_op jit(solution)/shard_map/ppermute | solution.py:948
  294.0 21.6 %collective-permute-start.50 = (bf16[384,1024]{1,0:T(8,128)(2,1)S(1)}, bf16[384,1024]{1,0:T(8,128)(2,1)S(1)}, u32[]{:S(2)}, u32[]{:S(2)}) collective-permute-start(bf16[384,1024]{1,0:T(8,128)(2,1)S(1)} %get-tuple-element.532), channel_id=1, source_target_pairs={{0,4},{1,5},{2,6},{3,7},{4,0},{5,1},{6,2},{7,3},{8,12},{9,13},{10,... | collective-permute-start | bytes 2359304 | tf_op jit(solution)/shard_map/ppermute | solution.py:948
  315.6 22.3 %collective-permute-start.55 = (bf16[768,1536]{1,0:T(8,128)(2,1)}, bf16[768,1536]{1,0:T(8,128)(2,1)S(1)}, u32[]{:S(2)}, u32[]{:S(2)}) collective-permute-start(bf16[768,1536]{1,0:T(8,128)(2,1)} %get-tuple-element.554), channel_id=1, source_target_pairs={{0,1},{1,0},{2,3},{3,2},{4,5},{5,4},{6,7},{7,6},{8,9},{9,8},{10,11... | collective-permute-start | bytes 7077896 | tf_op jit(solution)/shard_map/ppermute | solution.py:948
  315.7 21.1 %collective-permute-start.52 = (bf16[384,1024]{1,0:T(8,128)(2,1)}, bf16[384,1024]{1,0:T(8,128)(2,1)S(1)}, u32[]{:S(2)}, u32[]{:S(2)}) collective-permute-start(bf16[384,1024]{1,0:T(8,128)(2,1)} %copy-done.35), channel_id=1, source_target_pairs={{0,24},{1,25},{2,26},{3,27},{4,28},{5,29},{6,30},{7,31},{8,0},{9,1... | collective-permute-start | bytes 2359304 | tf_op jit(solution)/shard_map/ppermute | solution.py:952
  337.9 20.2 %collective-permute-start.57 = (bf16[384,1024]{1,0:T(8,128)(2,1)}, bf16[384,1024]{1,0:T(8,128)(2,1)S(1)}, u32[]{:S(2)}, u32[]{:S(2)}) collective-permute-start(bf16[384,1024]{1,0:T(8,128)(2,1)} %get-tuple-element.565), channel_id=1, source_target_pairs={{0,2},{1,3},{2,0},{3,1},{4,6},{5,7},{6,4},{7,5},{8,10},{9,11},{10,... | collective-permute-start | bytes 2359304 | tf_op jit(solution)/shard_map/ppermute | solution.py:948
  363.2 26.0 %collective-permute-start.65 = (bf16[432,384]{1,0:T(8,128)(2,1)S(1)}, bf16[432,384]{1,0:T(8,128)(2,1)}, u32[]{:S(2)}, u32[]{:S(2)}) collective-permute-start(bf16[432,384]{1,0:T(8,128)(2,1)S(1)} %get-tuple-element.614), channel_id=1, source_target_pairs={{0,2},{1,3},{2,0},{3,1},{4,6},{5,7},{6,4},{7,5},{8,10},{9,11},{10,... | collective-permute-start | bytes 995336 | tf_op jit(solution)/shard_map/ppermute | solution.py:948
  363.8 25.5 %collective-permute-start.66 = (bf16[432,384]{1,0:T(8,128)(2,1)S(1)}, bf16[432,384]{1,0:T(8,128)(2,1)}, u32[]{:S(2)}, u32[]{:S(2)}) collective-permute-start(bf16[432,384]{1,0:T(8,128)(2,1)S(1)} %get-tuple-element.615), channel_id=1, source_target_pairs={{0,4},{1,5},{2,6},{3,7},{4,0},{5,1},{6,2},{7,3},{8,12},{9,13},{10,... | collective-permute-start | bytes 995336 | tf_op jit(solution)/shard_map/ppermute | solution.py:948
  364.9 24.4 %collective-permute-start.63 = (bf16[384,1024]{1,0:T(8,128)(2,1)}, bf16[384,1024]{1,0:T(8,128)(2,1)S(1)}, u32[]{:S(2)}, u32[]{:S(2)}) collective-permute-start(bf16[384,1024]{1,0:T(8,128)(2,1)} %get-tuple-element.599), channel_id=1, source_target_pairs={{0,4},{1,5},{2,6},{3,7},{4,0},{5,1},{6,2},{7,3},{8,12},{9,13},{10,... | collective-permute-start | bytes 2359304 | tf_op jit(solution)/shard_map/ppermute | solution.py:948
  366.3 23.0 %collective-permute-start.61 = (bf16[384,1024]{1,0:T(8,128)(2,1)S(1)}, bf16[384,1024]{1,0:T(8,128)(2,1)S(1)}, u32[]{:S(2)}, u32[]{:S(2)}) collective-permute-start(bf16[384,1024]{1,0:T(8,128)(2,1)S(1)} %get-tuple-element.597), channel_id=1, source_target_pairs={{0,24},{1,25},{2,26},{3,27},{4,28},{5,29},{6,30},{7,31},{8,0},{9,1... | collective-permute-start | bytes 2359304 | tf_op jit(solution)/shard_map/ppermute | solution.py:952
  389.6 23.9 %collective-permute-start.69 = (bf16[432,384]{1,0:T(8,128)(2,1)S(1)}, bf16[432,384]{1,0:T(8,128)(2,1)S(1)}, u32[]{:S(2)}, u32[]{:S(2)}) collective-permute-start(bf16[432,384]{1,0:T(8,128)(2,1)S(1)} %add_convert_fusion.6), channel_id=1, source_target_pairs={{0,4},{1,5},{2,6},{3,7},{4,0},{5,1},{6,2},{7,3},{8,12},{9,13},{10,... | collective-permute-start | bytes 995336 | tf_op jit(solution)/shard_map/ppermute | solution.py:948
  390.8 22.7 %collective-permute-start.67 = (bf16[432,384]{1,0:T(8,128)(2,1)S(1)}, bf16[432,384]{1,0:T(8,128)(2,1)S(1)}, u32[]{:S(2)}, u32[]{:S(2)}) collective-permute-start(bf16[432,384]{1,0:T(8,128)(2,1)S(1)} %get-tuple-element.630), channel_id=1, source_target_pairs={{0,24},{1,25},{2,26},{3,27},{4,28},{5,29},{6,30},{7,31},{8,0},{9,1... | collective-permute-start | bytes 995336 | tf_op jit(solution)/shard_map/ppermute | solution.py:952
  424.4 23.9 %collective-permute-start.80 = (f32[3,64,1024]{2,1,0:T(8,128)S(1)}, f32[3,64,1024]{2,1,0:T(8,128)S(1)}, u32[]{:S(2)}, u32[]{:S(2)}) collective-permute-start(f32[3,64,1024]{2,1,0:T(8,128)S(1)} %get-tuple-element.691), channel_id=1, source_target_pairs={{0,1},{1,0},{2,3},{3,2},{4,5},{5,4},{6,7},{7,6},{8,9},{9,8},{10,11... | collective-permute-start | bytes 2359304 | tf_op jit(solution)/shard_map/ppermute | solution.py:948
  (156 other events, 2098.1 us)

commit v16 on v15

--- a/solution.py
+++ b/solution.py
@@ -404,7 +404,7 @@
             scratch_shapes=[pltpu.VMEM((512, WIDTH), BF16)],
         ),
         out_shape=[jax.ShapeDtypeStruct((FF, SIDE), BF16)] * 2,
-        compiler_params=params(LESS),
+        compiler_params=params(57 << 20),
         cost_estimate=pl.CostEstimate(
             flops=2 * ROWS * WIDTH * FF, bytes_accessed=2 * ROWS * (WIDTH + FF), transcendentals=0
         ),
@@ -437,7 +437,7 @@
             ],
         ),
         out_shape=[jax.ShapeDtypeStruct((WIDTH, FF // 2), BF16)] * 2,
-        compiler_params=params(LESS),
+        compiler_params=params(57 << 20),
         cost_estimate=pl.CostEstimate(
             flops=2 * ROWS * WIDTH * FF, bytes_accessed=2 * ROWS * (WIDTH + FF), transcendentals=0
         ),
@@ -1087,20 +1087,20 @@
     have = scatter_add(have, got, 2)
 
     have, got = scatter_send(have, 3)
+    out_own, out_far = run_out(sc, active, resid, down)
+    have, got, out_own, out_far, down_got = together((have, got, out_own, out_far, other(down_far)))
+    have = scatter_add(have, got, 3)
+
+    have, got = scatter_send(have, 4)
     d_out_own, d_out_far = run_out_grad(sc, mixed, res_own, res_far)
-    packed = run_collect(sc, down_own, other(down_far), up_own, up_got, d_out_own, other(d_out_far))
-    have, got, packed = together((have, got, packed))
-    have = scatter_add(have, got, 3)
-
-    have, got = scatter_send(have, 4)
+    packed = run_collect(sc, down_own, down_got, up_own, up_got, d_out_own, other(d_out_far))
     sums, sums_got = scatter_send(by_place(packed), 0)
-    out_own, out_far = run_out(sc, active, resid, down)
-    have, got, sums, sums_got, out_own, out_far = together((have, got, sums, sums_got, out_own, out_far))
+    have, got, sums, sums_got, out_got = together((have, got, sums, sums_got, other(out_far)))
     rand_sum = scatter_add(have, got, 4)[0, 0, 0].reshape(2, 3, HALF, LMAX)
 
     sums, got = scatter_send(scatter_add(sums, sums_got, 0), 1)
     output, tokens_grad, d_value, d_gain_one = run_close(
-        sc, tokens, res_own, res_got, out_own, other(out_far), back_own, back_got, gain_one, value, value_far
+        sc, tokens, res_own, res_got, out_own, out_got, back_own, back_got, gain_one, value, value_far
     )
     sums, got, output, tokens_grad, d_value, d_gain_one = together(
         (sums, got, output, tokens_grad, d_value, d_gain_one)

time: 478 us -> 500 us (1.046)
  waiting for transfers between devices: 139 us -> 159 us
  Pallas kernels: 210 us -> 216 us
    ppermute x66, waiting for transfers between devices: 88.4 us -> 109 us  [swap(): return lax.ppermute(x, BOTH, [(d, d ^ bit) for d in range(DEVICES)])]
    unnamed x184 -> x220, local copies, waits for them, and re-layouts: 26.8 us -> 25.2 us
  transfers between devices with their start and end apart: 89 -> 89, of which waited for: 38 -> 37; matrix products, arithmetic and copies ran while one was open for 3% -> 2% of each run, Pallas kernels for 32% -> 32%
where the time goes in v16:
time: 500 us; the launch traced here: 494 us
  Pallas kernels  216 us (43%)
  waiting for transfers between devices  159 us (32%)
  starting transfers between devices  73.6 us (15%)
  local copies, waits for them, and re-layouts  35.4 us (7%)
  other arithmetic  8.01 us (2%)
    ppermute x66, waiting for transfers between devices, swap(): return lax.ppermute(x, BOTH, [(d, d ^ bit) for d in range(DEVICES)])  109 us
    ppermute x23, waiting for transfers between devices, ring(): lax.ppermute(x, BOTH, [(d, (d + 8 * way) % DEVICES) for d in range(DEVICE...  50.2 us
    ppermute x66, starting transfers between devices, swap(): return lax.ppermute(x, BOTH, [(d, d ^ bit) for d in range(DEVICES)])  49.2 us
    pallas_call x1, Pallas kernels, run_units(): pl.pallas_call(units_kernel, grid_spec=pltpu.PrefetchScalarGridSpec(num_s...  30.3 us
    pallas_call x2, Pallas kernels, run_unmix(): pl.pallas_call(partial(unmix_kernel, count, bool(carry)), grid_spec=pltpu...  29.4 us
    pallas_call x1, Pallas kernels, run_post(): pl.pallas_call(post_kernel, grid_spec=pltpu.PrefetchScalarGridSpec(num_sc...  28.1 us
    unnamed x220, local copies, waits for them, and re-layouts  25.2 us
    ppermute x23, starting transfers between devices, ring(): lax.ppermute(x, BOTH, [(d, (d + 8 * way) % DEVICES) for d in range(DEVICE...  24.4 us
  transfers between devices with their start and end apart: 89, of which 37 were waited for; matrix products, arithmetic and copies ran while one was open for 2% of the time, Pallas kernels for 32%

profile of v16, /device:TPU:0, one launch (start us, length us, event | category | flops | bytes accessed | tf_op | source)
XLA Modules:
  0.0 494.2 jit_solution(8869373638962598093)
XLA Ops:
  16.5 8.3 %collective-permute-done.7.refs_4_ = bf16[496,384]{1,0:T(8,128)(2,1)S(1)} collective-permute-done((bf16[496,384]{1,0:T(8,128)(2,1)}, bf16[496,384]{1,0:T(8,128)(2,1)S(1)}, u32[]{:S(2)}, u32[]{:S(2)}) %collective-permute-start.7) | collective-permute-done | bytes 380960 | tf_op jit(solution)/shard_map/ppermute | solution.py:952
  31.5 7.5 %collective-permute-done.9.refs_3_ = bf16[496,384]{1,0:T(8,128)(2,1)S(1)} collective-permute-done((bf16[496,384]{1,0:T(8,128)(2,1)}, bf16[496,384]{1,0:T(8,128)(2,1)S(1)}, u32[]{:S(2)}, u32[]{:S(2)}) %collective-permute-start.9) | collective-permute-done | bytes 380960 | tf_op jit(solution)/shard_map/ppermute | solution.py:948
  45.0 6.2 %collective-permute-done.13.refs_6_ = bf16[496,384]{1,0:T(8,128)(2,1)S(1)} collective-permute-done((bf16[496,384]{1,0:T(8,128)(2,1)S(1)}, bf16[496,384]{1,0:T(8,128)(2,1)S(1)}, u32[]{:S(2)}, u32[]{:S(2)}) %collective-permute-start.13) | collective-permute-done | bytes 380960 | tf_op jit(solution)/shard_map/ppermute | solution.py:948
  67.4 7.1 %collective-permute-done.23.refs_15_ = bf16[496,384]{1,0:T(8,128)(2,1)S(1)} collective-permute-done((bf16[496,384]{1,0:T(8,128)(2,1)S(1)}, bf16[496,384]{1,0:T(8,128)(2,1)S(1)}, u32[]{:S(2)}, u32[]{:S(2)}) %collective-permute-start.23) | collective-permute-done | bytes 380960 | tf_op jit(solution)/shard_map/ppermute | solution.py:952
  77.7 7.2 %place.1 = (bf16[3072,384]{1,0:T(8,128)(2,1)}, bf16[768,1536]{1,0:T(8,128)(2,1)}, bf16[768,384]{1,0:T(8,128)(2,1)}, bf16[768,384]{1,0:T(8,128)(2,1)}, bf16[256,384]{1,0:T(8,128)(2,1)}) custom-call(s32[7]{0:T(128)} %concatenate.54.sc, bf16[496,384]{1,0:T(8,128)(2,1)} %pack.1.refs_0_, bf16[496,384]{1,0:T(8,128)(2,1)} %copy-done.79, ...), custom_call_target="tpu_custom_call" | custom-call | bytes 12189696 | tf_op jit(solution)/shard_map/place/pallas_call | solution.py:854
  95.5 7.8 %values.1.refs_12_.refs_4_.v_own = bf16[12,1024,128]{2,1,0:T(8,128)(2,1)} custom-call(s32[7]{0:T(128)} %concatenate.54.sc, bf16[2,1024,768]{2,1,0:T(8,128)(2,1)} %tok.1, f32[1,768]{1,0:T(1,128)} %reshape.205.gain, bf16[768,384]{1,0:T(8,128)(2,1)} %get-tuple-element.401.w_own, bf16[768,384]{1,0:T(8,128)(2,1)} %copy-done.55), custom_call_target="tpu_custom_call" | custom-call | flops 2415919104 | bytes 6291456 | tf_op jit(solution)/shard_map/values/pallas_call | solution.py:81
  113.7 16.7 %collective-permute-done.32.refs_6_ = bf16[384,1024]{1,0:T(8,128)(2,1)} collective-permute-done((bf16[384,1024]{1,0:T(8,128)(2,1)}, bf16[384,1024]{1,0:T(8,128)(2,1)}, u32[]{:S(2)}, u32[]{:S(2)}) %collective-permute-start.32) | collective-permute-done | bytes 786464 | tf_op jit(solution)/shard_map/ppermute | solution.py:948
  135.1 5.5 %masked.1.cot = bf16[4,512,768]{2,1,0:T(8,128)(2,1)} custom-call(s32[7]{0:T(128)} %concatenate.54.sc, bf16[2,8,2,64,768]{4,3,2,1,0:T(8,128)(2,1)} %bitcast.114, bf16[2,8,64,768]{3,2,1,0:T(8,128)(2,1)} %copy-done.72), custom_call_target="tpu_custom_call" | custom-call | bytes 6291456 | tf_op jit(solution)/shard_map/masked/pallas_call | solution.py:299
  140.6 11.8 %collective-permute-done.38.refs_11_ = bf16[384,1024]{1,0:T(8,128)(2,1)} collective-permute-done((bf16[384,1024]{1,0:T(8,128)(2,1)}, bf16[384,1024]{1,0:T(8,128)(2,1)}, u32[]{:S(2)}, u32[]{:S(2)}) %collective-permute-start.38) | collective-permute-done | bytes 786464 | tf_op jit(solution)/shard_map/ppermute | solution.py:948
  157.0 13.2 %mix.2 = (bf16[12,512,256]{2,1,0:T(8,128)(2,1)}, f32[12,512,256]{2,1,0:T(8,128)}, bf16[12,512,1024]{2,1,0:T(8,128)(2,1)}, bf16[12,512,256]{2,1,0:T(8,128)(2,1)}) custom-call(s32[7]{0:T(128)} %concatenate.54.sc, bf16[384,1024]{1,0:T(8,128)(2,1)} %bitcast.119, bf16[384,1024]{1,0:T(8,128)(2,1)} %collective-permute-done.24.refs_1_, ...), custom_call_target="tpu_custom_call" | custom-call | flops 3221225472 | bytes 20447232 | tf_op jit(solution)/shard_map/mix/pallas_call | solution.py:191
  176.4 8.5 %mix.3 = (bf16[12,512,256]{2,1,0:T(8,128)(2,1)}, f32[12,512,256]{2,1,0:T(8,128)}, bf16[12,512,1024]{2,1,0:T(8,128)(2,1)}, bf16[12,512,256]{2,1,0:T(8,128)(2,1)}) custom-call(s32[7]{0:T(128)} %concatenate.54.sc, bf16[384,1024]{1,0:T(8,128)(2,1)} %copy-done.76, ...), custom_call_target="tpu_custom_call", output_to_operand_aliasing={{0}: (7, {}), {1}: (8, {}), {2}: (9, {}), {3}: (10, {})} | custom-call | flops 3221225472 | bytes 20447232 | tf_op jit(solution)/shard_map/mix/pallas_call | solution.py:191
  184.9 10.6 %pre.1 = (bf16[4,512,768]{2,1,0:T(8,128)(2,1)}, bf16[4,512,768]{2,1,0:T(8,128)(2,1)}, bf16[4,512,768]{2,1,0:T(8,128)(2,1)}) custom-call(s32[7]{0:T(128)} %concatenate.54.sc, bf16[2,8,2,64,768]{4,3,2,1,0:T(8,128)(2,1)} %bitcast.106, bf16[2,8,64,768]{3,2,1,0:T(8,128)(2,1)} %copy-done.71, bf16[12,512,256]{2,1,0:T(8,128)(2,1)} %get-tuple-element.461.heads, ...), custom_call_target="tpu_custom_call" | custom-call | flops 2415919104 | bytes 25165824 | tf_op jit(solution)/shard_map/pre/pallas_call | solution.py:270
  195.5 30.3 %units.1 = (bf16[2048,3072]{1,0:T(8,128)(2,1)}, bf16[2048,3072]{1,0:T(8,128)(2,1)}) custom-call(s32[7]{0:T(128)} %concatenate.54.sc, bf16[2048,768]{1,0:T(8,128)(2,1)} %bitcast.140, bf16[2048,768]{1,0:T(8,128)(2,1)} %bitcast.122, bf16[768,1536]{1,0:T(8,128)(2,1)} %get-tuple-element.467.up_own, bf16[768,1536]{1,0:T(8,128)(2,1)} %collective-permute-done.42.up_far, ...), custom_call_target="tpu_custom_call" | custom-call | flops 19327352832 | bytes 34603008 | tf_op jit(solution)/shard_map/units/pallas_call | solution.py:365
  225.8 28.1 %post.1 = (bf16[2,512,768]{2,1,0:T(8,128)(2,1)}, bf16[2,512,768]{2,1,0:T(8,128)(2,1)}, bf16[12,512,256]{2,1,0:T(8,128)(2,1)}, f32[1,768]{1,0:T(1,128)}) custom-call(s32[7]{0:T(128)} %concatenate.54.sc, bf16[4,512,768]{2,1,0:T(8,128)(2,1)} %get-tuple-element.464.resid, bf16[4,512,3072]{2,1,0:T(8,128)(2,1)} %bitcast.143, bf16[4,512,3072]{2,1,0:T(8,128)(2,1)} %bitcast.144, ...), custom_call_target="tpu_custom_call" | custom-call | flops 12079595520 | bytes 37748736 | tf_op jit(solution)/shard_map/post/pallas_call | solution.py:569
  254.0 10.0 %unmix.2 = (bf16[384,1024]{1,0:T(8,128)(2,1)}, bf16[384,1024]{1,0:T(8,128)(2,1)}, bf16[384,1024]{1,0:T(8,128)(2,1)}, bf16[384,1024]{1,0:T(8,128)(2,1)}, bf16[12,...) custom-call(s32[7]{0:T(128)} %concatenate.54.sc, bf16[12,1024,128]{2,1,0:T(8,128)(2,1)} %values.1.refs_12_.refs_4_.v_own, ...), custom_call_target="tpu_custom_call" | custom-call | flops 4831838208 | bytes 33030144 | tf_op jit(solution)/shard_map/unmix/pallas_call | solution.py:665
  269.1 19.4 %unmix.3 = (bf16[384,1024]{1,0:T(8,128)(2,1)}, bf16[384,1024]{1,0:T(8,128)(2,1)}, bf16[384,1024]{1,0:T(8,128)(2,1)}, bf16[384,1024]{1,0:T(8,128)(2,1)}, bf16[384...) custom-call(s32[7]{0:T(128)} %concatenate.54.sc, ...), custom_call_target="tpu_custom_call", output_to_operand_aliasing={{12}: (7, {}), {13}: (8, {})} | custom-call | flops 4831838208 | bytes 33030144 | tf_op jit(solution)/shard_map/unmix/pallas_call | solution.py:665
  294.8 16.3 %up_grad.1 = (bf16[768,1536]{1,0:T(8,128)(2,1)}, bf16[768,1536]{1,0:T(8,128)(2,1)}) custom-call(s32[7]{0:T(128)} %concatenate.54.sc, bf16[2048,768]{1,0:T(8,128)(2,1)} %bitcast.141, bf16[2048,3072]{1,0:T(8,128)(2,1)} %get-tuple-element.469.up_grad), custom_call_target="tpu_custom_call" | custom-call | flops 9663676416 | bytes 15728640 | tf_op jit(solution)/shard_map/up_grad/pallas_call | solution.py:428
  319.7 15.7 %down_grad.1 = (bf16[3072,384]{1,0:T(8,128)(2,1)}, bf16[3072,384]{1,0:T(8,128)(2,1)}) custom-call(s32[7]{0:T(128)} %concatenate.54.sc, bf16[2048,3072]{1,0:T(8,128)(2,1)} %get-tuple-element.537.active, bf16[2048,768]{1,0:T(8,128)(2,1)} %bitcast.123), custom_call_target="tpu_custom_call" | custom-call | flops 9663676416 | bytes 15728640 | tf_op jit(solution)/shard_map/down_grad/pallas_call | solution.py:397
  355.4 15.0 %out.3 = (bf16[2,512,768]{2,1,0:T(8,128)(2,1)S(1)}, bf16[2,512,768]{2,1,0:T(8,128)(2,1)S(1)}) custom-call(s32[7]{0:T(128)S(1)} %copy-done.42, bf16[4,512,3072]{2,1,0:T(8,128)(2,1)} %bitcast.142, bf16[4,512,768]{2,1,0:T(8,128)(2,1)S(1)} %copy-done.45, bf16[3072,384]{1,0:T(8,128)(2,1)S(1)} %copy-done.48, bf16[3072,384]{1,0:T(8,128)(2,1)} %collective-permute-done.43.dn_far), custom_call_target="tpu_custom_call" | custom-call | flops 9663676416 | bytes 23592960 | tf_op jit(solution)/shard_map/out/pallas_call | solution.py:502
  387.1 19.5 %collective-permute-done.65 = bf16[432,384]{1,0:T(8,128)(2,1)S(1)} collective-permute-done((bf16[432,384]{1,0:T(8,128)(2,1)S(1)}, bf16[432,384]{1,0:T(8,128)(2,1)S(1)}, u32[]{:S(2)}, u32[]{:S(2)}) %collective-permute-start.65) | collective-permute-done | bytes 331808 | tf_op jit(solution)/shard_map/ppermute | solution.py:948
  407.5 7.6 %collective-permute-done.66 = bf16[432,384]{1,0:T(8,128)(2,1)S(1)} collective-permute-done((bf16[432,384]{1,0:T(8,128)(2,1)S(1)}, bf16[432,384]{1,0:T(8,128)(2,1)S(1)}, u32[]{:S(2)}, u32[]{:S(2)}) %collective-permute-start.66) | collective-permute-done | bytes 331808 | tf_op jit(solution)/shard_map/ppermute | solution.py:948
  419.3 13.7 %close.1 = (f32[2,8,2,64,768]{4,3,2,1,0:T(8,128)}, f32[2,8,2,64,768]{4,3,2,1,0:T(8,128)}, bf16[2,768,384]{2,1,0:T(8,128)(2,1)S(1)}, f32[1,768]{1,0:T(1,128)S(1)}) custom-call(s32[7]{0:T(128)S(1)} %copy-done.43, bf16[2,8,2,64,768]{4,3,2,1,0:T(8,128)(2,1)S(1)} %bitcast.107, bf16[2,8,64,768]{3,2,1,0:T(8,128)(2,1)S(1)} %bitcast.112, ...), custom_call_target="tpu_custom_call" | custom-call | flops 4831838208 | bytes 29884416 | tf_op jit(solution)/shard_map/close/pallas_call | solution.py:757
  446.1 8.3 %collective-permute-done.75 = bf16[4,2,64,384]{3,2,1,0:T(8,128)(2,1)S(1)} collective-permute-done((bf16[4,2,64,384]{3,2,1,0:T(8,128)(2,1)S(1)}, bf16[4,2,64,384]{3,2,1,0:T(8,128)(2,1)S(1)}, u32[]{:S(2)}, u32[]{:S(2)}) %collective-permute-start.75) | collective-permute-done | bytes 393248 | tf_op jit(solution)/shard_map/ppermute | solution.py:948
  454.5 6.3 %collective-permute-done.72 = bf16[432,384]{1,0:T(8,128)(2,1)S(1)} collective-permute-done((bf16[432,384]{1,0:T(8,128)(2,1)S(1)}, bf16[432,384]{1,0:T(8,128)(2,1)S(1)}, u32[]{:S(2)}, u32[]{:S(2)}) %collective-permute-start.72) | collective-permute-done | bytes 331808 | tf_op jit(solution)/shard_map/ppermute | solution.py:948
  (453 shorter events, 191.4 us)
Async XLA Ops:
  110.0 23.3 %collective-permute-start.35 = (bf16[12,1024,128]{2,1,0:T(8,128)(2,1)}, bf16[12,1024,128]{2,1,0:T(8,128)(2,1)}, u32[]{:S(2)}, u32[]{:S(2)}) collective-permute-start(bf16[12,1024,128]{2,1,0:T(8,128)(2,1)} %values.1.refs_12_.refs_4_.v_own), channel_id=1, source_target_pairs={{0,1},{1,0},{2,3},{3,2},{4,5},{5,4},{6,7},{7,6},{8,9},{9,8},{10,11... | collective-permute-start | bytes 9437192 | tf_op jit(solution)/shard_map/ppermute | solution.py:948
  110.1 20.3 %collective-permute-start.32 = (bf16[384,1024]{1,0:T(8,128)(2,1)}, bf16[384,1024]{1,0:T(8,128)(2,1)}, u32[]{:S(2)}, u32[]{:S(2)}) collective-permute-start(bf16[384,1024]{1,0:T(8,128)(2,1)} %collective-permute-done.26.refs_4_), channel_id=1, source_target_pairs={{0,4},{1,5},{2,6},{3,7},{4,0},{5,1},{6,2},{7,3},{8,12},{9,13},{10,... | collective-permute-start | bytes 2359304 | tf_op jit(solution)/shard_map/ppermute | solution.py:948
  111.0 21.4 %collective-permute-start.34 = (bf16[384,1024]{1,0:T(8,128)(2,1)S(1)}, bf16[384,1024]{1,0:T(8,128)(2,1)S(1)}, u32[]{:S(2)}, u32[]{:S(2)}) collective-permute-start(bf16[384,1024]{1,0:T(8,128)(2,1)S(1)} %collective-permute-done.30.refs_8_), channel_id=1, source_target_pairs={{0,8},{1,9},{2,10},{3,11},{4,12},{5,13},{6,14},{7,15},{8,16},{9,17... | collective-permute-start | bytes 2359304 | tf_op jit(solution)/shard_map/ppermute | solution.py:952
  134.5 20.6 %collective-permute-start.37 = (bf16[384,1024]{1,0:T(8,128)(2,1)}, bf16[384,1024]{1,0:T(8,128)(2,1)}, u32[]{:S(2)}, u32[]{:S(2)}) collective-permute-start(bf16[384,1024]{1,0:T(8,128)(2,1)} %collective-permute-done.32.refs_6_), channel_id=1, source_target_pairs={{0,8},{1,9},{2,10},{3,11},{4,12},{5,13},{6,14},{7,15},{8,16},{9,17... | collective-permute-start | bytes 2359304 | tf_op jit(solution)/shard_map/ppermute | solution.py:952
  134.6 20.5 %collective-permute-start.36 = (bf16[384,1024]{1,0:T(8,128)(2,1)}, bf16[384,1024]{1,0:T(8,128)(2,1)}, u32[]{:S(2)}, u32[]{:S(2)}) collective-permute-start(bf16[384,1024]{1,0:T(8,128)(2,1)} %collective-permute-done.32.refs_6_), channel_id=1, source_target_pairs={{0,2},{1,3},{2,0},{3,1},{4,6},{5,7},{6,4},{7,5},{8,10},{9,11},{10,... | collective-permute-start | bytes 2359304 | tf_op jit(solution)/shard_map/ppermute | solution.py:948
  175.2 20.3 %collective-permute-start.42 = (bf16[768,1536]{1,0:T(8,128)(2,1)}, bf16[768,1536]{1,0:T(8,128)(2,1)}, u32[]{:S(2)}, u32[]{:S(2)}) collective-permute-start(bf16[768,1536]{1,0:T(8,128)(2,1)} %get-tuple-element.467.up_own), channel_id=1, source_target_pairs={{0,1},{1,0},{2,3},{3,2},{4,5},{5,4},{6,7},{7,6},{8,9},{9,8},{10,11... | collective-permute-start | bytes 7077896 | tf_op jit(solution)/shard_map/ppermute | solution.py:948
  265.2 23.3 %collective-permute-start.45 = (bf16[384,1024]{1,0:T(8,128)(2,1)}, bf16[384,1024]{1,0:T(8,128)(2,1)S(1)}, u32[]{:S(2)}, u32[]{:S(2)}) collective-permute-start(bf16[384,1024]{1,0:T(8,128)(2,1)} %get-tuple-element.482), channel_id=1, source_target_pairs={{0,24},{1,25},{2,26},{3,27},{4,28},{5,29},{6,30},{7,31},{8,0},{9,1... | collective-permute-start | bytes 2359304 | tf_op jit(solution)/shard_map/ppermute | solution.py:952
  267.5 21.1 %collective-permute-start.46 = (bf16[384,1024]{1,0:T(8,128)(2,1)}, bf16[384,1024]{1,0:T(8,128)(2,1)S(1)}, u32[]{:S(2)}, u32[]{:S(2)}) collective-permute-start(bf16[384,1024]{1,0:T(8,128)(2,1)} %get-tuple-element.483), channel_id=1, source_target_pairs={{0,2},{1,3},{2,0},{3,1},{4,6},{5,7},{6,4},{7,5},{8,10},{9,11},{10,... | collective-permute-start | bytes 2359304 | tf_op jit(solution)/shard_map/ppermute | solution.py:948
  268.0 20.5 %collective-permute-start.47 = (bf16[384,1024]{1,0:T(8,128)(2,1)}, bf16[384,1024]{1,0:T(8,128)(2,1)}, u32[]{:S(2)}, u32[]{:S(2)}) collective-permute-start(bf16[384,1024]{1,0:T(8,128)(2,1)} %get-tuple-element.484), channel_id=1, source_target_pairs={{0,4},{1,5},{2,6},{3,7},{4,0},{5,1},{6,2},{7,3},{8,12},{9,13},{10,... | collective-permute-start | bytes 2359304 | tf_op jit(solution)/shard_map/ppermute | solution.py:948
  288.5 24.9 %collective-permute-start.51 = (bf16[12,1024,128]{2,1,0:T(8,128)(2,1)}, bf16[12,1024,128]{2,1,0:T(8,128)(2,1)}, u32[]{:S(2)}, u32[]{:S(2)}) collective-permute-start(bf16[12,1024,128]{2,1,0:T(8,128)(2,1)} %get-tuple-element.521), channel_id=1, source_target_pairs={{0,1},{1,0},{2,3},{3,2},{4,5},{5,4},{6,7},{7,6},{8,9},{9,8},{10,11... | collective-permute-start | bytes 9437192 | tf_op jit(solution)/shard_map/ppermute | solution.py:948
  288.6 22.4 %collective-permute-start.48 = (bf16[384,1024]{1,0:T(8,128)(2,1)}, bf16[384,1024]{1,0:T(8,128)(2,1)S(1)}, u32[]{:S(2)}, u32[]{:S(2)}) collective-permute-start(bf16[384,1024]{1,0:T(8,128)(2,1)} %get-tuple-element.516), channel_id=1, source_target_pairs={{0,24},{1,25},{2,26},{3,27},{4,28},{5,29},{6,30},{7,31},{8,0},{9,1... | collective-permute-start | bytes 2359304 | tf_op jit(solution)/shard_map/ppermute | solution.py:952
  289.5 22.5 %collective-permute-start.49 = (bf16[384,1024]{1,0:T(8,128)(2,1)}, bf16[384,1024]{1,0:T(8,128)(2,1)S(1)}, u32[]{:S(2)}, u32[]{:S(2)}) collective-permute-start(bf16[384,1024]{1,0:T(8,128)(2,1)} %get-tuple-element.517), channel_id=1, source_target_pairs={{0,2},{1,3},{2,0},{3,1},{4,6},{5,7},{6,4},{7,5},{8,10},{9,11},{10,... | collective-permute-start | bytes 2359304 | tf_op jit(solution)/shard_map/ppermute | solution.py:948
  313.4 24.6 %collective-permute-start.55 = (bf16[768,1536]{1,0:T(8,128)(2,1)}, bf16[768,1536]{1,0:T(8,128)(2,1)S(1)}, u32[]{:S(2)}, u32[]{:S(2)}) collective-permute-start(bf16[768,1536]{1,0:T(8,128)(2,1)} %get-tuple-element.540), channel_id=1, source_target_pairs={{0,1},{1,0},{2,3},{3,2},{4,5},{5,4},{6,7},{7,6},{8,9},{9,8},{10,11... | collective-permute-start | bytes 7077896 | tf_op jit(solution)/shard_map/ppermute | solution.py:948
  313.4 22.0 %collective-permute-start.52 = (bf16[384,1024]{1,0:T(8,128)(2,1)S(1)}, bf16[384,1024]{1,0:T(8,128)(2,1)S(1)}, u32[]{:S(2)}, u32[]{:S(2)}) collective-permute-start(bf16[384,1024]{1,0:T(8,128)(2,1)S(1)} %copy-done.53), channel_id=1, source_target_pairs={{0,24},{1,25},{2,26},{3,27},{4,28},{5,29},{6,30},{7,31},{8,0},{9,1... | collective-permute-start | bytes 2359304 | tf_op jit(solution)/shard_map/ppermute | solution.py:952
  338.1 35.3 %collective-permute-start.59 = (bf16[3072,384]{1,0:T(8,128)(2,1)}, bf16[3072,384]{1,0:T(8,128)(2,1)S(1)}, u32[]{:S(2)}, u32[]{:S(2)}) collective-permute-start(bf16[3072,384]{1,0:T(8,128)(2,1)} %get-tuple-element.555), channel_id=1, source_target_pairs={{0,1},{1,0},{2,3},{3,2},{4,5},{5,4},{6,7},{7,6},{8,9},{9,8},{10,11... | collective-permute-start | bytes 7077896 | tf_op jit(solution)/shard_map/ppermute | solution.py:948
  347.0 26.4 %collective-permute-start.63 = (bf16[768,384]{1,0:T(8,128)(2,1)S(1)}, bf16[768,384]{1,0:T(8,128)(2,1)S(1)}, u32[]{:S(2)}, u32[]{:S(2)}) collective-permute-start(bf16[768,384]{1,0:T(8,128)(2,1)S(1)} %get-tuple-element.572), channel_id=1, source_target_pairs={{0,1},{1,0},{2,3},{3,2},{4,5},{5,4},{6,7},{7,6},{8,9},{9,8},{10,11... | collective-permute-start | bytes 1769480 | tf_op jit(solution)/shard_map/ppermute | solution.py:948
  347.3 24.3 %collective-permute-start.57 = (bf16[384,1024]{1,0:T(8,128)(2,1)}, bf16[384,1024]{1,0:T(8,128)(2,1)S(1)}, u32[]{:S(2)}, u32[]{:S(2)}) collective-permute-start(bf16[384,1024]{1,0:T(8,128)(2,1)} %get-tuple-element.551), channel_id=1, source_target_pairs={{0,2},{1,3},{2,0},{3,1},{4,6},{5,7},{6,4},{7,5},{8,10},{9,11},{10,... | collective-permute-start | bytes 2359304 | tf_op jit(solution)/shard_map/ppermute | solution.py:948
  348.3 23.3 %collective-permute-start.58 = (bf16[384,1024]{1,0:T(8,128)(2,1)S(1)}, bf16[384,1024]{1,0:T(8,128)(2,1)S(1)}, u32[]{:S(2)}, u32[]{:S(2)}) collective-permute-start(bf16[384,1024]{1,0:T(8,128)(2,1)S(1)} %copy-done.108), channel_id=1, source_target_pairs={{0,4},{1,5},{2,6},{3,7},{4,0},{5,1},{6,2},{7,3},{8,12},{9,13},{10,... | collective-permute-start | bytes 2359304 | tf_op jit(solution)/shard_map/ppermute | solution.py:948
  351.6 20.8 %collective-permute-start.56 = (bf16[384,1024]{1,0:T(8,128)(2,1)S(1)}, bf16[384,1024]{1,0:T(8,128)(2,1)S(1)}, u32[]{:S(2)}, u32[]{:S(2)}) collective-permute-start(bf16[384,1024]{1,0:T(8,128)(2,1)S(1)} %get-tuple-element.550), channel_id=1, source_target_pairs={{0,24},{1,25},{2,26},{3,27},{4,28},{5,29},{6,30},{7,31},{8,0},{9,1... | collective-permute-start | bytes 2359304 | tf_op jit(solution)/shard_map/ppermute | solution.py:952
  373.4 41.7 %collective-permute-start.67 = (bf16[2,512,768]{2,1,0:T(8,128)(2,1)S(1)}, bf16[2,512,768]{2,1,0:T(8,128)(2,1)S(1)}, u32[]{:S(2)}, u32[]{:S(2)}) collective-permute-start(bf16[2,512,768]{2,1,0:T(8,128)(2,1)S(1)} %get-tuple-element.589), channel_id=1, source_target_pairs={{0,1},{1,0},{2,3},{3,2},{4,5},{5,4},{6,7},{7,6},{8,9},{9,8},{10,11... | collective-permute-start | bytes 4718600 | tf_op jit(solution)/shard_map/ppermute | solution.py:948
  378.3 36.8 %collective-permute-start.62 = (bf16[384,1024]{1,0:T(8,128)(2,1)S(1)}, bf16[384,1024]{1,0:T(8,128)(2,1)S(1)}, u32[]{:S(2)}, u32[]{:S(2)}) collective-permute-start(bf16[384,1024]{1,0:T(8,128)(2,1)S(1)} %copy-done.107), channel_id=1, source_target_pairs={{0,4},{1,5},{2,6},{3,7},{4,0},{5,1},{6,2},{7,3},{8,12},{9,13},{10,... | collective-permute-start | bytes 2359304 | tf_op jit(solution)/shard_map/ppermute | solution.py:948
  379.9 35.2 %collective-permute-start.60 = (bf16[384,1024]{1,0:T(8,128)(2,1)S(1)}, bf16[384,1024]{1,0:T(8,128)(2,1)S(1)}, u32[]{:S(2)}, u32[]{:S(2)}) collective-permute-start(bf16[384,1024]{1,0:T(8,128)(2,1)S(1)} %get-tuple-element.562), channel_id=1, source_target_pairs={{0,24},{1,25},{2,26},{3,27},{4,28},{5,29},{6,30},{7,31},{8,0},{9,1... | collective-permute-start | bytes 2359304 | tf_op jit(solution)/shard_map/ppermute | solution.py:952
  380.4 34.7 %collective-permute-start.61 = (bf16[384,1024]{1,0:T(8,128)(2,1)S(1)}, bf16[384,1024]{1,0:T(8,128)(2,1)S(1)}, u32[]{:S(2)}, u32[]{:S(2)}) collective-permute-start(bf16[384,1024]{1,0:T(8,128)(2,1)S(1)} %get-tuple-element.563), channel_id=1, source_target_pairs={{0,2},{1,3},{2,0},{3,1},{4,6},{5,7},{6,4},{7,5},{8,10},{9,11},{10,... | collective-permute-start | bytes 2359304 | tf_op jit(solution)/shard_map/ppermute | solution.py:948
  446.0 22.2 %collective-permute-start.80 = (f32[3,64,1024]{2,1,0:T(8,128)S(1)}, f32[3,64,1024]{2,1,0:T(8,128)S(1)}, u32[]{:S(2)}, u32[]{:S(2)}) collective-permute-start(f32[3,64,1024]{2,1,0:T(8,128)S(1)} %get-tuple-element.663), channel_id=1, source_target_pairs={{0,1},{1,0},{2,3},{3,2},{4,5},{5,4},{6,7},{7,6},{8,9},{9,8},{10,11... | collective-permute-start | bytes 2359304 | tf_op jit(solution)/shard_map/ppermute | solution.py:948
  (174 other events, 2495.5 us)

commit v17 on v15

--- a/solution.py
+++ b/solution.py
@@ -404,7 +404,7 @@
             scratch_shapes=[pltpu.VMEM((512, WIDTH), BF16)],
         ),
         out_shape=[jax.ShapeDtypeStruct((FF, SIDE), BF16)] * 2,
-        compiler_params=params(LESS),
+        compiler_params=params(57 << 20),
         cost_estimate=pl.CostEstimate(
             flops=2 * ROWS * WIDTH * FF, bytes_accessed=2 * ROWS * (WIDTH + FF), transcendentals=0
         ),
@@ -437,7 +437,7 @@
             ],
         ),
         out_shape=[jax.ShapeDtypeStruct((WIDTH, FF // 2), BF16)] * 2,
-        compiler_params=params(LESS),
+        compiler_params=params(57 << 20),
         cost_estimate=pl.CostEstimate(
             flops=2 * ROWS * WIDTH * FF, bytes_accessed=2 * ROWS * (WIDTH + FF), transcendentals=0
         ),
@@ -1093,25 +1093,26 @@
     have = scatter_add(have, got, 3)
 
     have, got = scatter_send(have, 4)
-    sums, sums_got = scatter_send(by_place(packed), 0)
     out_own, out_far = run_out(sc, active, resid, down)
-    have, got, sums, sums_got, out_own, out_far = together((have, got, sums, sums_got, out_own, out_far))
+    have, got, packed, out_own, out_far = together((have, got, packed, out_own, out_far))
     rand_sum = scatter_add(have, got, 4)[0, 0, 0].reshape(2, 3, HALF, LMAX)
 
-    sums, got = scatter_send(scatter_add(sums, sums_got, 0), 1)
+    sums, got = scatter_send(by_place(packed), 0)
     output, tokens_grad, d_value, d_gain_one = run_close(
         sc, tokens, res_own, res_got, out_own, other(out_far), back_own, back_got, gain_one, value, value_far
     )
-    sums, got, output, tokens_grad, d_value, d_gain_one = together(
-        (sums, got, output, tokens_grad, d_value, d_gain_one)
-    )
-    sums = scatter_add(sums, got, 1)
-
-    sums, got = scatter_send(sums, 2)
     gain_pair = jnp.concatenate([d_gain_one, d_gain_two]).reshape(2, 16, 1, 48).astype(BF16)
     gain_pair = jnp.pad(gain_pair, ((0, 0), (0, 0), (0, 15), (0, SIDE - 48)))
     small = jnp.concatenate([d_value.reshape(2, 16, 48, SIDE), gain_pair], 2)
+    sums, got, output, tokens_grad, small = together((sums, got, output, tokens_grad, small))
+    sums = scatter_add(sums, got, 0)
+
+    sums, got = scatter_send(sums, 1)
     small = add_low(pick(small, core), other(pick(small, 1 - core))).reshape(4, 2, 2, 64, SIDE)
+    sums, got, small = together((sums, got, small))
+    sums = scatter_add(sums, got, 1)
+
+    sums, got = scatter_send(sums, 2)
     small = add_low(pick(small, x, 2), swap(pick(small, 1 - x, 2), TO_X))
     sums, got, small = together((sums, got, small))
     sums = scatter_add(sums, got, 2)

time: 478 us -> 480 us (level)
  Pallas kernels: 210 us -> 217 us
  local copies, waits for them, and re-layouts: 37 us -> 31.5 us
    unnamed x184 -> x198, local copies, waits for them, and re-layouts: 26.8 us -> 21.3 us
  transfers between devices with their start and end apart: 89 -> 89, of which waited for: 38 -> 41; matrix products, arithmetic and copies ran while one was open for 3% -> 3% of each run, Pallas kernels for 32% -> 33%
where the time goes in v17:
time: 480 us; the launch traced here: 474 us
  Pallas kernels  217 us (45%)
  waiting for transfers between devices  136 us (28%)
  starting transfers between devices  77.9 us (16%)
  local copies, waits for them, and re-layouts  31.5 us (7%)
  other arithmetic  9.36 us (2%)
    ppermute x66, waiting for transfers between devices, swap(): return lax.ppermute(x, BOTH, [(d, d ^ bit) for d in range(DEVICES)])  89.1 us
    ppermute x66, starting transfers between devices, swap(): return lax.ppermute(x, BOTH, [(d, d ^ bit) for d in range(DEVICES)])  47.6 us
    ppermute x23, waiting for transfers between devices, ring(): lax.ppermute(x, BOTH, [(d, (d + 8 * way) % DEVICES) for d in range(DEVICE...  46.8 us
    ppermute x23, starting transfers between devices, ring(): lax.ppermute(x, BOTH, [(d, (d + 8 * way) % DEVICES) for d in range(DEVICE...  30.3 us
    pallas_call x1, Pallas kernels, run_units(): pl.pallas_call(units_kernel, grid_spec=pltpu.PrefetchScalarGridSpec(num_s...  30.2 us
    pallas_call x2, Pallas kernels, run_unmix(): pl.pallas_call(partial(unmix_kernel, count, bool(carry)), grid_spec=pltpu...  29.5 us
    pallas_call x1, Pallas kernels, run_post(): pl.pallas_call(post_kernel, grid_spec=pltpu.PrefetchScalarGridSpec(num_sc...  28.1 us
    pallas_call x2, Pallas kernels, run_mix(): pl.pallas_call(partial(mix_kernel, count, bool(carry)), grid_spec=pltpu.P...  21.7 us
  transfers between devices with their start and end apart: 89, of which 41 were waited for; matrix products, arithmetic and copies ran while one was open for 3% of the time, Pallas kernels for 33%

profile of v17, /device:TPU:0, one launch (start us, length us, event | category | flops | bytes accessed | tf_op | source)
XLA Modules:
  0.0 473.7 jit_solution(3491302564963648226)
XLA Ops:
  16.6 8.3 %collective-permute-done.7.refs_4_ = bf16[496,384]{1,0:T(8,128)(2,1)S(1)} collective-permute-done((bf16[496,384]{1,0:T(8,128)(2,1)}, bf16[496,384]{1,0:T(8,128)(2,1)S(1)}, u32[]{:S(2)}, u32[]{:S(2)}) %collective-permute-start.7) | collective-permute-done | bytes 380960 | tf_op jit(solution)/shard_map/ppermute | solution.py:952
  31.6 7.5 %collective-permute-done.9.refs_3_ = bf16[496,384]{1,0:T(8,128)(2,1)S(1)} collective-permute-done((bf16[496,384]{1,0:T(8,128)(2,1)}, bf16[496,384]{1,0:T(8,128)(2,1)S(1)}, u32[]{:S(2)}, u32[]{:S(2)}) %collective-permute-start.9) | collective-permute-done | bytes 380960 | tf_op jit(solution)/shard_map/ppermute | solution.py:948
  45.1 6.2 %collective-permute-done.13.refs_6_ = bf16[496,384]{1,0:T(8,128)(2,1)S(1)} collective-permute-done((bf16[496,384]{1,0:T(8,128)(2,1)S(1)}, bf16[496,384]{1,0:T(8,128)(2,1)S(1)}, u32[]{:S(2)}, u32[]{:S(2)}) %collective-permute-start.13) | collective-permute-done | bytes 380960 | tf_op jit(solution)/shard_map/ppermute | solution.py:948
  67.4 7.1 %collective-permute-done.23.refs_15_ = bf16[496,384]{1,0:T(8,128)(2,1)S(1)} collective-permute-done((bf16[496,384]{1,0:T(8,128)(2,1)S(1)}, bf16[496,384]{1,0:T(8,128)(2,1)S(1)}, u32[]{:S(2)}, u32[]{:S(2)}) %collective-permute-start.23) | collective-permute-done | bytes 380960 | tf_op jit(solution)/shard_map/ppermute | solution.py:952
  77.8 7.2 %place.1 = (bf16[3072,384]{1,0:T(8,128)(2,1)}, bf16[768,1536]{1,0:T(8,128)(2,1)}, bf16[768,384]{1,0:T(8,128)(2,1)}, bf16[768,384]{1,0:T(8,128)(2,1)}, bf16[256,384]{1,0:T(8,128)(2,1)}) custom-call(s32[7]{0:T(128)} %concatenate.54.sc, bf16[496,384]{1,0:T(8,128)(2,1)} %pack.1.refs_0_, bf16[496,384]{1,0:T(8,128)(2,1)} %copy-done.76, ...), custom_call_target="tpu_custom_call" | custom-call | bytes 12189696 | tf_op jit(solution)/shard_map/place/pallas_call | solution.py:854
  95.6 7.8 %values.1.refs_12_.refs_4_.v_own = bf16[12,1024,128]{2,1,0:T(8,128)(2,1)} custom-call(s32[7]{0:T(128)} %concatenate.54.sc, bf16[2,1024,768]{2,1,0:T(8,128)(2,1)} %tok.1, f32[1,768]{1,0:T(1,128)} %reshape.205.gain, bf16[768,384]{1,0:T(8,128)(2,1)} %get-tuple-element.431.w_own, bf16[768,384]{1,0:T(8,128)(2,1)} %copy-done.48), custom_call_target="tpu_custom_call" | custom-call | flops 2415919104 | bytes 6291456 | tf_op jit(solution)/shard_map/values/pallas_call | solution.py:81
  113.7 16.7 %collective-permute-done.32.refs_6_ = bf16[384,1024]{1,0:T(8,128)(2,1)} collective-permute-done((bf16[384,1024]{1,0:T(8,128)(2,1)}, bf16[384,1024]{1,0:T(8,128)(2,1)}, u32[]{:S(2)}, u32[]{:S(2)}) %collective-permute-start.32) | collective-permute-done | bytes 786464 | tf_op jit(solution)/shard_map/ppermute | solution.py:948
  135.2 5.6 %masked.1.cot = bf16[4,512,768]{2,1,0:T(8,128)(2,1)} custom-call(s32[7]{0:T(128)} %concatenate.54.sc, bf16[2,8,2,64,768]{4,3,2,1,0:T(8,128)(2,1)} %bitcast.114, bf16[2,8,64,768]{3,2,1,0:T(8,128)(2,1)} %copy-done.69), custom_call_target="tpu_custom_call" | custom-call | bytes 6291456 | tf_op jit(solution)/shard_map/masked/pallas_call | solution.py:299
  140.8 11.7 %collective-permute-done.38.refs_11_ = bf16[384,1024]{1,0:T(8,128)(2,1)} collective-permute-done((bf16[384,1024]{1,0:T(8,128)(2,1)}, bf16[384,1024]{1,0:T(8,128)(2,1)}, u32[]{:S(2)}, u32[]{:S(2)}) %collective-permute-start.38) | collective-permute-done | bytes 786464 | tf_op jit(solution)/shard_map/ppermute | solution.py:948
  157.1 13.2 %mix.2 = (bf16[12,512,256]{2,1,0:T(8,128)(2,1)}, f32[12,512,256]{2,1,0:T(8,128)}, bf16[12,512,1024]{2,1,0:T(8,128)(2,1)}, bf16[12,512,256]{2,1,0:T(8,128)(2,1)}) custom-call(s32[7]{0:T(128)} %concatenate.54.sc, bf16[384,1024]{1,0:T(8,128)(2,1)} %bitcast.119, bf16[384,1024]{1,0:T(8,128)(2,1)} %collective-permute-done.24.refs_1_, ...), custom_call_target="tpu_custom_call" | custom-call | flops 3221225472 | bytes 20447232 | tf_op jit(solution)/shard_map/mix/pallas_call | solution.py:191
  170.3 5.0 %collective-permute-done.41.refs_3_ = bf16[384,1024]{1,0:T(8,128)(2,1)} collective-permute-done((bf16[384,1024]{1,0:T(8,128)(2,1)}, bf16[384,1024]{1,0:T(8,128)(2,1)}, u32[]{:S(2)}, u32[]{:S(2)}) %collective-permute-start.41) | collective-permute-done | bytes 786464 | tf_op jit(solution)/shard_map/ppermute | solution.py:952
  176.5 8.5 %mix.3 = (bf16[12,512,256]{2,1,0:T(8,128)(2,1)}, f32[12,512,256]{2,1,0:T(8,128)}, bf16[12,512,1024]{2,1,0:T(8,128)(2,1)}, bf16[12,512,256]{2,1,0:T(8,128)(2,1)}) custom-call(s32[7]{0:T(128)} %concatenate.54.sc, bf16[384,1024]{1,0:T(8,128)(2,1)} %copy-done.73, ...), custom_call_target="tpu_custom_call", output_to_operand_aliasing={{0}: (7, {}), {1}: (8, {}), {2}: (9, {}), {3}: (10, {})} | custom-call | flops 3221225472 | bytes 20447232 | tf_op jit(solution)/shard_map/mix/pallas_call | solution.py:191
  185.0 10.6 %pre.1 = (bf16[4,512,768]{2,1,0:T(8,128)(2,1)}, bf16[4,512,768]{2,1,0:T(8,128)(2,1)}, bf16[4,512,768]{2,1,0:T(8,128)(2,1)}) custom-call(s32[7]{0:T(128)} %concatenate.54.sc, bf16[2,8,2,64,768]{4,3,2,1,0:T(8,128)(2,1)} %bitcast.106, bf16[2,8,64,768]{3,2,1,0:T(8,128)(2,1)} %copy-done.68, bf16[12,512,256]{2,1,0:T(8,128)(2,1)} %get-tuple-element.491.heads, ...), custom_call_target="tpu_custom_call" | custom-call | flops 2415919104 | bytes 25165824 | tf_op jit(solution)/shard_map/pre/pallas_call | solution.py:270
  195.6 30.2 %units.1 = (bf16[2048,3072]{1,0:T(8,128)(2,1)}, bf16[2048,3072]{1,0:T(8,128)(2,1)}) custom-call(s32[7]{0:T(128)} %concatenate.54.sc, bf16[2048,768]{1,0:T(8,128)(2,1)} %bitcast.140, bf16[2048,768]{1,0:T(8,128)(2,1)} %bitcast.122, bf16[768,1536]{1,0:T(8,128)(2,1)} %get-tuple-element.497.up_own, bf16[768,1536]{1,0:T(8,128)(2,1)} %collective-permute-done.42.up_far, ...), custom_call_target="tpu_custom_call" | custom-call | flops 19327352832 | bytes 34603008 | tf_op jit(solution)/shard_map/units/pallas_call | solution.py:365
  225.8 28.1 %post.1 = (bf16[2,512,768]{2,1,0:T(8,128)(2,1)}, bf16[2,512,768]{2,1,0:T(8,128)(2,1)}, bf16[12,512,256]{2,1,0:T(8,128)(2,1)}, f32[1,768]{1,0:T(1,128)}) custom-call(s32[7]{0:T(128)} %concatenate.54.sc, bf16[4,512,768]{2,1,0:T(8,128)(2,1)} %get-tuple-element.494.resid, bf16[4,512,3072]{2,1,0:T(8,128)(2,1)} %bitcast.143, bf16[4,512,3072]{2,1,0:T(8,128)(2,1)} %bitcast.144, ...), custom_call_target="tpu_custom_call" | custom-call | flops 12079595520 | bytes 37748736 | tf_op jit(solution)/shard_map/post/pallas_call | solution.py:569
  253.9 9.9 %unmix.2 = (bf16[384,1024]{1,0:T(8,128)(2,1)}, bf16[384,1024]{1,0:T(8,128)(2,1)}, bf16[384,1024]{1,0:T(8,128)(2,1)}, bf16[384,1024]{1,0:T(8,128)(2,1)}, bf16[12,...) custom-call(s32[7]{0:T(128)} %concatenate.54.sc, bf16[12,1024,128]{2,1,0:T(8,128)(2,1)} %values.1.refs_12_.refs_4_.v_own, ...), custom_call_target="tpu_custom_call" | custom-call | flops 4831838208 | bytes 33030144 | tf_op jit(solution)/shard_map/unmix/pallas_call | solution.py:665
  269.1 19.6 %unmix.3 = (bf16[384,1024]{1,0:T(8,128)(2,1)}, bf16[384,1024]{1,0:T(8,128)(2,1)}, bf16[384,1024]{1,0:T(8,128)(2,1)}, bf16[384,1024]{1,0:T(8,128)(2,1)}, bf16[384...) custom-call(s32[7]{0:T(128)} %concatenate.54.sc, ...), custom_call_target="tpu_custom_call", output_to_operand_aliasing={{12}: (7, {}), {13}: (8, {})} | custom-call | flops 4831838208 | bytes 33030144 | tf_op jit(solution)/shard_map/unmix/pallas_call | solution.py:665
  294.9 16.3 %up_grad.1 = (bf16[768,1536]{1,0:T(8,128)(2,1)}, bf16[768,1536]{1,0:T(8,128)(2,1)}) custom-call(s32[7]{0:T(128)} %concatenate.54.sc, bf16[2048,768]{1,0:T(8,128)(2,1)} %bitcast.141, bf16[2048,3072]{1,0:T(8,128)(2,1)} %get-tuple-element.499.up_grad), custom_call_target="tpu_custom_call" | custom-call | flops 9663676416 | bytes 15728640 | tf_op jit(solution)/shard_map/up_grad/pallas_call | solution.py:428
  319.7 15.7 %down_grad.1 = (bf16[3072,384]{1,0:T(8,128)(2,1)}, bf16[3072,384]{1,0:T(8,128)(2,1)}) custom-call(s32[7]{0:T(128)} %concatenate.54.sc, bf16[2048,3072]{1,0:T(8,128)(2,1)} %get-tuple-element.567.active, bf16[2048,768]{1,0:T(8,128)(2,1)} %bitcast.123), custom_call_target="tpu_custom_call" | custom-call | flops 9663676416 | bytes 15728640 | tf_op jit(solution)/shard_map/down_grad/pallas_call | solution.py:397
  347.5 5.3 %out_grad.1 = (bf16[768,384]{1,0:T(8,128)(2,1)S(1)}, bf16[768,384]{1,0:T(8,128)(2,1)S(1)}) custom-call(s32[7]{0:T(128)S(1)} %copy-done.36, bf16[4,512,768]{2,1,0:T(8,128)(2,1)S(1)} %copy-done.39, bf16[2,512,768]{2,1,0:T(8,128)(2,1)S(1)} %copy-done.60, bf16[2,512,768]{2,1,0:T(8,128)(2,1)S(1)} %copy-done.44), custom_call_target="tpu_custom_call" | custom-call | flops 2415919104 | bytes 6291456 | tf_op jit(solution)/shard_map/out_grad/pallas_call | solution.py:468
  368.0 15.0 %out.3 = (bf16[2,512,768]{2,1,0:T(8,128)(2,1)S(1)}, bf16[2,512,768]{2,1,0:T(8,128)(2,1)S(1)}) custom-call(s32[7]{0:T(128)S(1)} %copy-done.36, bf16[4,512,3072]{2,1,0:T(8,128)(2,1)} %bitcast.142, bf16[4,512,768]{2,1,0:T(8,128)(2,1)S(1)} %copy-done.38, bf16[3072,384]{1,0:T(8,128)(2,1)S(1)} %copy-done.41, bf16[3072,384]{1,0:T(8,128)(2,1)} %collective-permute-done.43.dn_far), custom_call_target="tpu_custom_call" | custom-call | flops 9663676416 | bytes 23592960 | tf_op jit(solution)/shard_map/out/pallas_call | solution.py:502
  390.6 13.7 %close.1 = (f32[2,8,2,64,768]{4,3,2,1,0:T(8,128)}, f32[2,8,2,64,768]{4,3,2,1,0:T(8,128)}, bf16[2,768,384]{2,1,0:T(8,128)(2,1)S(1)}, f32[1,768]{1,0:T(1,128)S(1)}) custom-call(s32[7]{0:T(128)S(1)} %copy-done.36, bf16[2,8,2,64,768]{4,3,2,1,0:T(8,128)(2,1)S(1)} %bitcast.107, bf16[2,8,64,768]{3,2,1,0:T(8,128)(2,1)S(1)} %bitcast.112, ...), custom_call_target="tpu_custom_call" | custom-call | flops 4831838208 | bytes 29884416 | tf_op jit(solution)/shard_map/close/pallas_call | solution.py:757
  416.3 5.3 %collective-permute-done.70 = bf16[432,384]{1,0:T(8,128)(2,1)S(1)} collective-permute-done((bf16[432,384]{1,0:T(8,128)(2,1)S(1)}, bf16[432,384]{1,0:T(8,128)(2,1)S(1)}, u32[]{:S(2)}, u32[]{:S(2)}) %collective-permute-start.70) | collective-permute-done | bytes 331808 | tf_op jit(solution)/shard_map/ppermute | solution.py:948
  429.5 7.5 %collective-permute-done.75 = bf16[4,2,64,384]{3,2,1,0:T(8,128)(2,1)S(1)} collective-permute-done((bf16[4,2,64,384]{3,2,1,0:T(8,128)(2,1)S(1)}, bf16[4,2,64,384]{3,2,1,0:T(8,128)(2,1)S(1)}, u32[]{:S(2)}, u32[]{:S(2)}) %collective-permute-start.75) | collective-permute-done | bytes 393248 | tf_op jit(solution)/shard_map/ppermute | solution.py:948
  (431 shorter events, 189.5 us)
Async XLA Ops:
  110.1 23.4 %collective-permute-start.35 = (bf16[12,1024,128]{2,1,0:T(8,128)(2,1)}, bf16[12,1024,128]{2,1,0:T(8,128)(2,1)}, u32[]{:S(2)}, u32[]{:S(2)}) collective-permute-start(bf16[12,1024,128]{2,1,0:T(8,128)(2,1)} %values.1.refs_12_.refs_4_.v_own), channel_id=1, source_target_pairs={{0,1},{1,0},{2,3},{3,2},{4,5},{5,4},{6,7},{7,6},{8,9},{9,8},{10,11... | collective-permute-start | bytes 9437192 | tf_op jit(solution)/shard_map/ppermute | solution.py:948
  110.1 20.3 %collective-permute-start.32 = (bf16[384,1024]{1,0:T(8,128)(2,1)}, bf16[384,1024]{1,0:T(8,128)(2,1)}, u32[]{:S(2)}, u32[]{:S(2)}) collective-permute-start(bf16[384,1024]{1,0:T(8,128)(2,1)} %collective-permute-done.26.refs_4_), channel_id=1, source_target_pairs={{0,4},{1,5},{2,6},{3,7},{4,0},{5,1},{6,2},{7,3},{8,12},{9,13},{10,... | collective-permute-start | bytes 2359304 | tf_op jit(solution)/shard_map/ppermute | solution.py:948
  111.1 21.4 %collective-permute-start.34 = (bf16[384,1024]{1,0:T(8,128)(2,1)S(1)}, bf16[384,1024]{1,0:T(8,128)(2,1)S(1)}, u32[]{:S(2)}, u32[]{:S(2)}) collective-permute-start(bf16[384,1024]{1,0:T(8,128)(2,1)S(1)} %collective-permute-done.30.refs_8_), channel_id=1, source_target_pairs={{0,8},{1,9},{2,10},{3,11},{4,12},{5,13},{6,14},{7,15},{8,16},{9,17... | collective-permute-start | bytes 2359304 | tf_op jit(solution)/shard_map/ppermute | solution.py:952
  134.5 20.6 %collective-permute-start.37 = (bf16[384,1024]{1,0:T(8,128)(2,1)}, bf16[384,1024]{1,0:T(8,128)(2,1)}, u32[]{:S(2)}, u32[]{:S(2)}) collective-permute-start(bf16[384,1024]{1,0:T(8,128)(2,1)} %collective-permute-done.32.refs_6_), channel_id=1, source_target_pairs={{0,8},{1,9},{2,10},{3,11},{4,12},{5,13},{6,14},{7,15},{8,16},{9,17... | collective-permute-start | bytes 2359304 | tf_op jit(solution)/shard_map/ppermute | solution.py:952
  134.7 20.5 %collective-permute-start.36 = (bf16[384,1024]{1,0:T(8,128)(2,1)}, bf16[384,1024]{1,0:T(8,128)(2,1)}, u32[]{:S(2)}, u32[]{:S(2)}) collective-permute-start(bf16[384,1024]{1,0:T(8,128)(2,1)} %collective-permute-done.32.refs_6_), channel_id=1, source_target_pairs={{0,2},{1,3},{2,0},{3,1},{4,6},{5,7},{6,4},{7,5},{8,10},{9,11},{10,... | collective-permute-start | bytes 2359304 | tf_op jit(solution)/shard_map/ppermute | solution.py:948
  155.2 20.1 %collective-permute-start.41 = (bf16[384,1024]{1,0:T(8,128)(2,1)}, bf16[384,1024]{1,0:T(8,128)(2,1)}, u32[]{:S(2)}, u32[]{:S(2)}) collective-permute-start(bf16[384,1024]{1,0:T(8,128)(2,1)} %collective-permute-done.38.refs_11_), channel_id=1, source_target_pairs={{0,8},{1,9},{2,10},{3,11},{4,12},{5,13},{6,14},{7,15},{8,16},{9,17... | collective-permute-start | bytes 2359304 | tf_op jit(solution)/shard_map/ppermute | solution.py:952
  155.6 19.7 %collective-permute-start.40 = (bf16[384,1024]{1,0:T(8,128)(2,1)}, bf16[384,1024]{1,0:T(8,128)(2,1)}, u32[]{:S(2)}, u32[]{:S(2)}) collective-permute-start(bf16[384,1024]{1,0:T(8,128)(2,1)} %copy-done.73), channel_id=1, source_target_pairs={{0,4},{1,5},{2,6},{3,7},{4,0},{5,1},{6,2},{7,3},{8,12},{9,13},{10,... | collective-permute-start | bytes 2359304 | tf_op jit(solution)/shard_map/ppermute | solution.py:948
  175.3 20.2 %collective-permute-start.42 = (bf16[768,1536]{1,0:T(8,128)(2,1)}, bf16[768,1536]{1,0:T(8,128)(2,1)}, u32[]{:S(2)}, u32[]{:S(2)}) collective-permute-start(bf16[768,1536]{1,0:T(8,128)(2,1)} %get-tuple-element.497.up_own), channel_id=1, source_target_pairs={{0,1},{1,0},{2,3},{3,2},{4,5},{5,4},{6,7},{7,6},{8,9},{9,8},{10,11... | collective-permute-start | bytes 7077896 | tf_op jit(solution)/shard_map/ppermute | solution.py:948
  175.3 20.2 %collective-permute-start.43 = (bf16[3072,384]{1,0:T(8,128)(2,1)S(1)}, bf16[3072,384]{1,0:T(8,128)(2,1)}, u32[]{:S(2)}, u32[]{:S(2)}) collective-permute-start(bf16[3072,384]{1,0:T(8,128)(2,1)S(1)} %copy-done.40), channel_id=1, source_target_pairs={{0,1},{1,0},{2,3},{3,2},{4,5},{5,4},{6,7},{7,6},{8,9},{9,8},{10,11... | collective-permute-start | bytes 7077896 | tf_op jit(solution)/shard_map/ppermute | solution.py:948
  265.1 23.6 %collective-permute-start.45 = (bf16[384,1024]{1,0:T(8,128)(2,1)}, bf16[384,1024]{1,0:T(8,128)(2,1)S(1)}, u32[]{:S(2)}, u32[]{:S(2)}) collective-permute-start(bf16[384,1024]{1,0:T(8,128)(2,1)} %get-tuple-element.512), channel_id=1, source_target_pairs={{0,24},{1,25},{2,26},{3,27},{4,28},{5,29},{6,30},{7,31},{8,0},{9,1... | collective-permute-start | bytes 2359304 | tf_op jit(solution)/shard_map/ppermute | solution.py:952
  267.4 21.3 %collective-permute-start.46 = (bf16[384,1024]{1,0:T(8,128)(2,1)}, bf16[384,1024]{1,0:T(8,128)(2,1)S(1)}, u32[]{:S(2)}, u32[]{:S(2)}) collective-permute-start(bf16[384,1024]{1,0:T(8,128)(2,1)} %get-tuple-element.513), channel_id=1, source_target_pairs={{0,2},{1,3},{2,0},{3,1},{4,6},{5,7},{6,4},{7,5},{8,10},{9,11},{10,... | collective-permute-start | bytes 2359304 | tf_op jit(solution)/shard_map/ppermute | solution.py:948
  268.0 20.7 %collective-permute-start.47 = (bf16[384,1024]{1,0:T(8,128)(2,1)}, bf16[384,1024]{1,0:T(8,128)(2,1)}, u32[]{:S(2)}, u32[]{:S(2)}) collective-permute-start(bf16[384,1024]{1,0:T(8,128)(2,1)} %get-tuple-element.514), channel_id=1, source_target_pairs={{0,4},{1,5},{2,6},{3,7},{4,0},{5,1},{6,2},{7,3},{8,12},{9,13},{10,... | collective-permute-start | bytes 2359304 | tf_op jit(solution)/shard_map/ppermute | solution.py:948
  288.7 24.9 %collective-permute-start.51 = (bf16[12,1024,128]{2,1,0:T(8,128)(2,1)}, bf16[12,1024,128]{2,1,0:T(8,128)(2,1)}, u32[]{:S(2)}, u32[]{:S(2)}) collective-permute-start(bf16[12,1024,128]{2,1,0:T(8,128)(2,1)} %get-tuple-element.551), channel_id=1, source_target_pairs={{0,1},{1,0},{2,3},{3,2},{4,5},{5,4},{6,7},{7,6},{8,9},{9,8},{10,11... | collective-permute-start | bytes 9437192 | tf_op jit(solution)/shard_map/ppermute | solution.py:948
  288.8 22.4 %collective-permute-start.48 = (bf16[384,1024]{1,0:T(8,128)(2,1)}, bf16[384,1024]{1,0:T(8,128)(2,1)S(1)}, u32[]{:S(2)}, u32[]{:S(2)}) collective-permute-start(bf16[384,1024]{1,0:T(8,128)(2,1)} %get-tuple-element.546), channel_id=1, source_target_pairs={{0,24},{1,25},{2,26},{3,27},{4,28},{5,29},{6,30},{7,31},{8,0},{9,1... | collective-permute-start | bytes 2359304 | tf_op jit(solution)/shard_map/ppermute | solution.py:952
  289.4 22.7 %collective-permute-start.49 = (bf16[384,1024]{1,0:T(8,128)(2,1)}, bf16[384,1024]{1,0:T(8,128)(2,1)S(1)}, u32[]{:S(2)}, u32[]{:S(2)}) collective-permute-start(bf16[384,1024]{1,0:T(8,128)(2,1)} %get-tuple-element.547), channel_id=1, source_target_pairs={{0,2},{1,3},{2,0},{3,1},{4,6},{5,7},{6,4},{7,5},{8,10},{9,11},{10,... | collective-permute-start | bytes 2359304 | tf_op jit(solution)/shard_map/ppermute | solution.py:948
  313.6 25.4 %collective-permute-start.55 = (bf16[768,1536]{1,0:T(8,128)(2,1)}, bf16[768,1536]{1,0:T(8,128)(2,1)S(1)}, u32[]{:S(2)}, u32[]{:S(2)}) collective-permute-start(bf16[768,1536]{1,0:T(8,128)(2,1)} %get-tuple-element.570), channel_id=1, source_target_pairs={{0,1},{1,0},{2,3},{3,2},{4,5},{5,4},{6,7},{7,6},{8,9},{9,8},{10,11... | collective-permute-start | bytes 7077896 | tf_op jit(solution)/shard_map/ppermute | solution.py:948
  313.6 21.8 %collective-permute-start.52 = (bf16[384,1024]{1,0:T(8,128)(2,1)S(1)}, bf16[384,1024]{1,0:T(8,128)(2,1)S(1)}, u32[]{:S(2)}, u32[]{:S(2)}) collective-permute-start(bf16[384,1024]{1,0:T(8,128)(2,1)S(1)} %copy-done.46), channel_id=1, source_target_pairs={{0,24},{1,25},{2,26},{3,27},{4,28},{5,29},{6,30},{7,31},{8,0},{9,1... | collective-permute-start | bytes 2359304 | tf_op jit(solution)/shard_map/ppermute | solution.py:952
  317.4 20.1 %collective-permute-start.53 = (bf16[384,1024]{1,0:T(8,128)(2,1)}, bf16[384,1024]{1,0:T(8,128)(2,1)S(1)}, u32[]{:S(2)}, u32[]{:S(2)}) collective-permute-start(bf16[384,1024]{1,0:T(8,128)(2,1)} %get-tuple-element.565), channel_id=1, source_target_pairs={{0,2},{1,3},{2,0},{3,1},{4,6},{5,7},{6,4},{7,5},{8,10},{9,11},{10,... | collective-permute-start | bytes 2359304 | tf_op jit(solution)/shard_map/ppermute | solution.py:948
  339.0 20.6 %collective-permute-start.57 = (bf16[384,1024]{1,0:T(8,128)(2,1)}, bf16[384,1024]{1,0:T(8,128)(2,1)S(1)}, u32[]{:S(2)}, u32[]{:S(2)}) collective-permute-start(bf16[384,1024]{1,0:T(8,128)(2,1)} %get-tuple-element.581), channel_id=1, source_target_pairs={{0,2},{1,3},{2,0},{3,1},{4,6},{5,7},{6,4},{7,5},{8,10},{9,11},{10,... | collective-permute-start | bytes 2359304 | tf_op jit(solution)/shard_map/ppermute | solution.py:948
  340.2 19.9 %collective-permute-start.58 = (bf16[384,1024]{1,0:T(8,128)(2,1)}, bf16[384,1024]{1,0:T(8,128)(2,1)S(1)}, u32[]{:S(2)}, u32[]{:S(2)}) collective-permute-start(bf16[384,1024]{1,0:T(8,128)(2,1)} %get-tuple-element.582), channel_id=1, source_target_pairs={{0,4},{1,5},{2,6},{3,7},{4,0},{5,1},{6,2},{7,3},{8,12},{9,13},{10,... | collective-permute-start | bytes 2359304 | tf_op jit(solution)/shard_map/ppermute | solution.py:948
  362.1 22.1 %collective-permute-start.63 = (bf16[384,1024]{1,0:T(8,128)(2,1)S(1)}, bf16[384,1024]{1,0:T(8,128)(2,1)S(1)}, u32[]{:S(2)}, u32[]{:S(2)}) collective-permute-start(bf16[384,1024]{1,0:T(8,128)(2,1)S(1)} %copy-done.97), channel_id=1, source_target_pairs={{0,4},{1,5},{2,6},{3,7},{4,0},{5,1},{6,2},{7,3},{8,12},{9,13},{10,... | collective-permute-start | bytes 2359304 | tf_op jit(solution)/shard_map/ppermute | solution.py:948
  363.8 20.5 %collective-permute-start.61 = (bf16[384,1024]{1,0:T(8,128)(2,1)S(1)}, bf16[384,1024]{1,0:T(8,128)(2,1)S(1)}, u32[]{:S(2)}, u32[]{:S(2)}) collective-permute-start(bf16[384,1024]{1,0:T(8,128)(2,1)S(1)} %get-tuple-element.613), channel_id=1, source_target_pairs={{0,24},{1,25},{2,26},{3,27},{4,28},{5,29},{6,30},{7,31},{8,0},{9,1... | collective-permute-start | bytes 2359304 | tf_op jit(solution)/shard_map/ppermute | solution.py:952
  385.3 20.6 %collective-permute-start.64 = (bf16[432,384]{1,0:T(8,128)(2,1)}, bf16[432,384]{1,0:T(8,128)(2,1)}, u32[]{:S(2)}, u32[]{:S(2)}) collective-permute-start(bf16[432,384]{1,0:T(8,128)(2,1)} %get-tuple-element.647), channel_id=1, source_target_pairs={{0,24},{1,25},{2,26},{3,27},{4,28},{5,29},{6,30},{7,31},{8,0},{9,1... | collective-permute-start | bytes 995336 | tf_op jit(solution)/shard_map/ppermute | solution.py:952
  429.4 19.6 %collective-permute-start.80 = (f32[3,64,1024]{2,1,0:T(8,128)S(1)}, f32[3,64,1024]{2,1,0:T(8,128)S(1)}, u32[]{:S(2)}, u32[]{:S(2)}) collective-permute-start(f32[3,64,1024]{2,1,0:T(8,128)S(1)} %get-tuple-element.723), channel_id=1, source_target_pairs={{0,1},{1,0},{2,3},{3,2},{4,5},{5,4},{6,7},{7,6},{8,9},{9,8},{10,11... | collective-permute-start | bytes 2359304 | tf_op jit(solution)/shard_map/ppermute | solution.py:948
  (163 other events, 2005.6 us)

commit v18 on v17

--- a/solution.py
+++ b/solution.py
@@ -111,11 +111,14 @@
     return lax.rem(sc[PLANE] + PLANES - k, PLANES)
 
 
-def plane_spec(planes, rows, lanes):
+def plane_spec(planes, per, rows, lanes):
+    parts = PHEADS // per
+
     def index(step, sc):
-        return (plane_of(planes[0] + step * (planes[-1] - planes[0]) // max(len(planes) - 1, 1), sc), 0, 0)
-
-    return spec((PHEADS, rows, lanes), index)
+        k = planes[0] + step // parts * (planes[-1] - planes[0]) // max(len(planes) - 1, 1)
+        return (plane_of(k, sc) * parts + step % parts, 0, 0)
+
+    return spec((per, rows, lanes), index)
 
 
 def anywhere(count):
@@ -133,7 +136,7 @@
     ]
 
 
-def take_plane(place, shards, raw, sems):
+def take_plane(place, shards, raw, sems, parts):
     step = pl.program_id(0)
     count = len(shards) // 4
 
@@ -145,37 +148,31 @@
 
     for slot in range(count):
 
-        @pl.when(step == slot)
+        @pl.when(step == slot * parts)
         def _():
             for copy in plane_fetch(place, shards, raw, sems, slot):
                 copy.wait()
 
-    return step
-
-
-def head_rows(head):
-    return slice(head * HROWS, (head + 1) * HROWS)
-
-
-def fill_mask(sc, mask):
-    @pl.when(pl.program_id(0) == 0)
-    def _():
-        shape = (LMAX, 4 * HEAD)
-        column = lax.broadcasted_iota(jnp.int32, shape, 0)
-        mask[...] = (column < lane_lengths(sc, shape)).astype(F32).astype(BF16)
-
-
-def mix_kernel(count, carried, sc, *refs):
-    shards, (v_own, v_far, *rest) = refs[: 4 * count], refs[4 * count :]
-    mixed, mean, exps, inverse, raw, mask, sems = rest[4:] if carried else rest
-    fill_mask(sc, mask)
-    slot = take_plane(sc[PLACE], shards, raw, sems)
+    return step // parts
+
+
+def head_rows(per, head):
+    if per == PHEADS:
+        return pl.ds(head * HROWS, HROWS)
+    first = pl.program_id(0) % (PHEADS // per) * per
+    return pl.ds(pl.multiple_of((first + head) * HROWS, HROWS), HROWS)
+
+
+def mix_kernel(count, per, carried, sc, *refs):
+    shards, (v_own, v_far, mask, *rest) = refs[: 4 * count], refs[4 * count :]
+    mixed, mean, exps, inverse, raw, sems = rest[4:] if carried else rest
+    slot = take_plane(sc[PLACE], shards, raw, sems, PHEADS // per)
     shape = (HROWS, 4 * HEAD)
     line = lax.broadcasted_iota(jnp.int32, shape, 0)
     position = 128 * (line // HALF) + HALF * sc[CORE] + line % HALF
     valid = position < lane_lengths(sc, shape)
-    for head in range(PHEADS):
-        weights = jnp.exp(raw[slot, head_rows(head)].astype(F32)).astype(BF16)
+    for head in range(per):
+        weights = jnp.exp(raw[slot, head_rows(per, head)].astype(F32)).astype(BF16)
         exps[head] = weights
         both = dot(weights, jnp.concatenate([v_own[head], v_far[head], mask[...]], axis=1), 1, 0)
         flip = jnp.where(valid, 1.0 / both[:, 4 * HEAD :], 0.0)
@@ -185,24 +182,26 @@
         mixed[head] = found.astype(BF16)
 
 
-def run_mix(sc, planes, shards, v_own, v_far, carry):
+def run_mix(sc, planes, shards, v_own, v_far, mask, carry):
     carry, count = list(carry), len(planes)
+    per = 1 if count == 1 else PHEADS
     shape = (HEADS, HROWS, 4 * HEAD)
     return pl.pallas_call(
-        partial(mix_kernel, count, bool(carry)),
+        partial(mix_kernel, count, per, bool(carry)),
         grid_spec=pltpu.PrefetchScalarGridSpec(
             num_scalar_prefetch=1,
-            grid=(count,),
-            in_specs=anywhere(4 * count) + [plane_spec(planes, LMAX, 2 * HEAD)] * 2 + anywhere(len(carry)),
+            grid=(count * PHEADS // per,),
+            in_specs=anywhere(4 * count) + [plane_spec(planes, per, LMAX, 2 * HEAD)] * 2
+            + [held((LMAX, 4 * HEAD))]
+            + anywhere(len(carry)),
             out_specs=[
-                plane_spec(planes, HROWS, 4 * HEAD),
-                plane_spec(planes, HROWS, 4 * HEAD),
-                plane_spec(planes, HROWS, LMAX),
-                plane_spec(planes, HROWS, 4 * HEAD),
+                plane_spec(planes, per, HROWS, 4 * HEAD),
+                plane_spec(planes, per, HROWS, 4 * HEAD),
+                plane_spec(planes, per, HROWS, LMAX),
+                plane_spec(planes, per, HROWS, 4 * HEAD),
             ],
             scratch_shapes=[
                 pltpu.VMEM((count, 4 * SUBS * HALF, LMAX), BF16),
-                pltpu.VMEM((LMAX, 4 * HEAD), BF16),
                 pltpu.SemaphoreType.DMA((count, 4)),
             ],
         ),
@@ -212,7 +211,7 @@
             jax.ShapeDtypeStruct((HEADS, HROWS, LMAX), BF16),
             jax.ShapeDtypeStruct(shape, BF16),
         ],
-        input_output_aliases={3 + 4 * count + i: i for i in range(len(carry))},
+        input_output_aliases={4 + 4 * count + i: i for i in range(len(carry))},
         compiler_params=params(VMEM),
         cost_estimate=pl.CostEstimate(
             flops=2 * HEADS * HROWS * LMAX * 4 * HEAD,
@@ -220,7 +219,7 @@
             transcendentals=HEADS * HROWS * LMAX // 2,
         ),
         name="mix",
-    )(sc, *shards, v_own, v_far, *carry)
+    )(sc, *shards, v_own, v_far, mask, *carry)
 
 
 def row_valid(sc, step):
@@ -602,9 +601,9 @@
     )(sc, resid, up_grad, up_grad, cotangent, *up, *wo, gain)
 
 
-def unmix_kernel(count, carried, sc, v_own, v_far, grad_heads, mean, exps, inverse, *refs):
+def unmix_kernel(count, per, carried, sc, v_own, v_far, grad_heads, mean, exps, inverse, mask, adder, bound, *refs):
     refs = refs[2:] if carried else refs
-    outs, (own, far, grads, mask, adder, bound, out_sems) = refs[: 4 * count], refs[4 * count :]
+    outs, (own, far, grads, out_sems) = refs[: 4 * count], refs[4 * count :]
     place = sc[PLACE]
     step = pl.program_id(0)
 
@@ -618,22 +617,10 @@
             for rel in range(4)
         ]
 
-    fill_mask(sc, mask)
-
-    @pl.when(step == 0)
-    def _():
-        lane = lax.broadcasted_iota(jnp.int32, (4 * HEAD, 128), 0) // HEAD
-        column = lax.broadcasted_iota(jnp.int32, (4 * HEAD, 128), 1)
-        adder[...] = jnp.where((lane == column) | (lane + 4 == column), -1.0, 0.0).astype(BF16)
-        row = lax.broadcasted_iota(jnp.int32, (LMAX, 128), 0)
-        item = lax.broadcasted_iota(jnp.int32, (LMAX, 128), 1)
-        length = jnp.where(item % 4 == 0, sc[LENGTHS], sc[LENGTHS + 1])
-        length = jnp.where(item % 4 == 2, sc[LENGTHS + 2], length)
-        length = jnp.where(item % 4 == 3, sc[LENGTHS + 3], length)
-        bound[...] = jnp.where((item < 8) & (row < length), 1.0, 0.0).astype(BF16)
-
+    parts = PHEADS // per
+    slot = step // parts
     high_lanes = lax.broadcasted_iota(jnp.int32, (HROWS, 128), 1) < 4
-    for head in range(PHEADS):
+    for head in range(per):
         weights = exps[head]
         low = (grad_heads[head].astype(F32) * inverse[head].astype(F32)).astype(BF16)
         product = low.astype(F32) * mean[head]
@@ -644,13 +631,13 @@
         fine = (delta - coarse.astype(F32)).astype(BF16)
         left = jnp.concatenate([low, jnp.where(high_lanes, coarse, fine)], axis=1)
         score = dot(left, jnp.concatenate([v_own[head], v_far[head], bound[...]], axis=1), 1, 1)
-        grads[step, head_rows(head)] = (score * weights.astype(F32)).astype(BF16)
+        grads[slot, head_rows(per, head)] = (score * weights.astype(F32)).astype(BF16)
         back = (dot(weights, low, 0, 0) * mask[...].astype(F32)).astype(BF16)
         own[head] = back[:, : 2 * HEAD]
         far[head] = back[:, 2 * HEAD :]
     for which in range(count):
 
-        @pl.when(step == which)
+        @pl.when(step == which * parts + parts - 1)
         def _():
             for copy in leave(which):
                 copy.start()
@@ -660,34 +647,35 @@
                         copy.wait()
 
 
-def run_unmix(sc, planes, v_own, v_far, grad_heads, mean, exps, inverse, carry):
+def run_unmix(sc, planes, v_own, v_far, grad_heads, mean, exps, inverse, masks, carry):
     carry, count = list(carry), len(planes)
-    return pl.pallas_call(
-        partial(unmix_kernel, count, bool(carry)),
+    per = 1 if count == 1 else PHEADS
+    return pl.pallas_call(
+        partial(unmix_kernel, count, per, bool(carry)),
         grid_spec=pltpu.PrefetchScalarGridSpec(
             num_scalar_prefetch=1,
-            grid=(count,),
+            grid=(count * PHEADS // per,),
             in_specs=[
-                plane_spec(planes, LMAX, 2 * HEAD),
-                plane_spec(planes, LMAX, 2 * HEAD),
-                plane_spec(planes, HROWS, 4 * HEAD),
-                plane_spec(planes, HROWS, 4 * HEAD),
-                plane_spec(planes, HROWS, LMAX),
-                plane_spec(planes, HROWS, 4 * HEAD),
+                plane_spec(planes, per, LMAX, 2 * HEAD),
+                plane_spec(planes, per, LMAX, 2 * HEAD),
+                plane_spec(planes, per, HROWS, 4 * HEAD),
+                plane_spec(planes, per, HROWS, 4 * HEAD),
+                plane_spec(planes, per, HROWS, LMAX),
+                plane_spec(planes, per, HROWS, 4 * HEAD),
+                held((LMAX, 4 * HEAD)),
+                held((4 * HEAD, 128)),
+                held((LMAX, 128)),
             ]
             + anywhere(len(carry)),
-            out_specs=anywhere(4 * count) + [plane_spec(planes, LMAX, 2 * HEAD)] * 2,
+            out_specs=anywhere(4 * count) + [plane_spec(planes, per, LMAX, 2 * HEAD)] * 2,
             scratch_shapes=[
                 pltpu.VMEM((count, 4 * SUBS * HALF, LMAX), BF16),
-                pltpu.VMEM((LMAX, 4 * HEAD), BF16),
-                pltpu.VMEM((4 * HEAD, 128), BF16),
-                pltpu.VMEM((LMAX, 128), BF16),
                 pltpu.SemaphoreType.DMA((count, 4)),
             ],
         ),
         out_shape=[jax.ShapeDtypeStruct((SUBS * HALF, LMAX), BF16)] * (4 * count)
         + [jax.ShapeDtypeStruct((HEADS, LMAX, 2 * HEAD), BF16)] * 2,
-        input_output_aliases={7 + i: 4 * count + i for i in range(len(carry))},
+        input_output_aliases={10 + i: 4 * count + i for i in range(len(carry))},
         compiler_params=params(VMEM),
         cost_estimate=pl.CostEstimate(
             flops=3 * HEADS * HROWS * LMAX * 4 * HEAD,
@@ -695,7 +683,7 @@
             transcendentals=0,
         ),
         name="unmix",
-    )(sc, v_own, v_far, grad_heads, mean, exps, inverse, *carry)
+    )(sc, v_own, v_far, grad_heads, mean, exps, inverse, *masks, *carry)
 
 
 def close_kernel(sc, tok, res_own, res_got, out_own, out_got, own, far, gain, w_own, w_far, *refs):
@@ -1014,6 +1002,15 @@
 together = lax.optimization_barrier
 
 
+def item_masks(lengths):
+    lane, column = jnp.arange(4 * HEAD) // HEAD, jnp.arange(128)
+    position = jnp.arange(LMAX)[:, None]
+    wide = position < jnp.repeat(lengths, HEAD)[None]
+    adder = jnp.where((lane[:, None] == column[None] % 4) & (column[None] < 8), -1.0, 0.0)
+    narrow = (position < jnp.tile(lengths, 32)[None]) & (column[None] < 8)
+    return wide.astype(BF16), adder.astype(BF16), narrow.astype(BF16)
+
+
 def chip_shards(tokens, lengths, rand_mix, w_value, w_out, w_up, w_down, gain_mix, gain_ffn, grad_out):
     wide = lax.axis_index("wide")
     core = lax.axis_index("narrow")
@@ -1038,7 +1035,8 @@
     weights, grad_far = together((gather_step(weights, 2), other(pick(late_grad, 1 - core, 2))))
     weights, far_lengths = together((gather_step(weights, 3), other(lengths)))
     sc = jnp.concatenate([near_sc[:5], far_lengths])
-    weights, rands = together((gather_step(weights, 4), rands))
+    masks = item_masks(sc[3:])
+    weights, rands, masks = together((gather_step(weights, 4), rands, masks))
 
     rands = gather_step(rands, 0)
     down, up, out, value, gain_rows = place_weights(sc, in_order(weights))
@@ -1059,16 +1057,18 @@
     rands, v_far, masked, down, up = together((rands, v_far, masked, down, up))
     near = [rands[k, y_at, x_at] for k in range(3) for y_at in range(2) for x_at in range(2)]
     rands = gather_step(rands, 4)
-    mixing = run_mix(sc, (0, 1, 2), near, v_own, v_far, ())
+    mixing = run_mix(sc, (0, 1, 2), near, v_own, v_far, masks[0], ())
     rands, down, up, mixing = together((rands, down, up, mixing))
-    heads, mean, exps, inverse = run_mix(sc, (3,), in_order(rands)[12:], v_own, v_far, mixing)
+    heads, mean, exps, inverse = run_mix(sc, (3,), in_order(rands)[12:], v_own, v_far, masks[0], mixing)
     down, up = (down, other(down)), (up, other(up))
 
     mixed, resid, normed = run_pre(sc, tokens, tokens_far, heads, out, gain_two)
     active, up_grad = run_units(sc, normed, masked, up, down)
     res_own, res_far, grad_heads, d_gain_two = run_post(sc, resid, up_grad, masked, up, out, gain_two)
 
-    backward = lambda planes, carry: run_unmix(sc, planes, v_own, v_far, grad_heads, mean, exps, inverse, carry)
+    backward = lambda planes, carry: run_unmix(
+        sc, planes, v_own, v_far, grad_heads, mean, exps, inverse, masks, carry
+    )
     *far, back_own, back_far = backward((3,), ())
     far, back_own, back_far, res_got = together((far, back_own, back_far, other(res_far)))
     have, got = scatter_send(by_place(far, (3,)), 0)
@@ -1087,19 +1087,21 @@
     have = scatter_add(have, got, 2)
 
     have, got = scatter_send(have, 3)
+    out_own, out_far = run_out(sc, active, resid, down)
+    have, got, out_own, out_far, down_got, res_own, res_far = together(
+        (have, got, out_own, out_far, other(down_far), res_own, res_far)
+    )
+    have = scatter_add(have, got, 3)
+
+    have, got = scatter_send(have, 4)
     d_out_own, d_out_far = run_out_grad(sc, mixed, res_own, res_far)
-    packed = run_collect(sc, down_own, other(down_far), up_own, up_got, d_out_own, other(d_out_far))
-    have, got, packed = together((have, got, packed))
-    have = scatter_add(have, got, 3)
-
-    have, got = scatter_send(have, 4)
-    out_own, out_far = run_out(sc, active, resid, down)
-    have, got, packed, out_own, out_far = together((have, got, packed, out_own, out_far))
+    packed = run_collect(sc, down_own, down_got, up_own, up_got, d_out_own, other(d_out_far))
+    have, got, packed, out_got = together((have, got, packed, other(out_far)))
     rand_sum = scatter_add(have, got, 4)[0, 0, 0].reshape(2, 3, HALF, LMAX)
 
     sums, got = scatter_send(by_place(packed), 0)
     output, tokens_grad, d_value, d_gain_one = run_close(
-        sc, tokens, res_own, res_got, out_own, other(out_far), back_own, back_got, gain_one, value, value_far
+        sc, tokens, res_own, res_got, out_own, out_got, back_own, back_got, gain_one, value, value_far
     )
     gain_pair = jnp.concatenate([d_gain_one, d_gain_two]).reshape(2, 16, 1, 48).astype(BF16)
     gain_pair = jnp.pad(gain_pair, ((0, 0), (0, 0), (0, 15), (0, SIDE - 48)))

time: 480 us -> 487 us (1.015)
  waiting for transfers between devices: 136 us -> 144 us
  starting transfers between devices: 77.9 us -> 70.8 us
    ppermute x66, waiting for transfers between devices: 89.1 us -> 109 us  [swap(): return lax.ppermute(x, BOTH, [(d, d ^ bit) for d in range(DEVICES)])]
    ppermute x23, waiting for transfers between devices: 46.8 us -> 34.9 us  [ring(): lax.ppermute(x, BOTH, [(d, (d + 8 * way) % DEVICES) for d in range(DEVICE...]
    ppermute x23, starting transfers between devices: 30.3 us -> 21.1 us  [ring(): lax.ppermute(x, BOTH, [(d, (d + 8 * way) % DEVICES) for d in range(DEVICE...]
    unnamed x198 -> x182, local copies, waits for them, and re-layouts: 21.3 us -> 24.2 us
  transfers between devices with their start and end apart: 89 -> 89, of which waited for: 41 -> 47; matrix products, arithmetic and copies ran while one was open for 3% -> 4% of each run, Pallas kernels for 33% -> 33%
where the time goes in v18:
time: 487 us; the launch traced here: 480 us
  Pallas kernels  217 us (45%)
  waiting for transfers between devices  144 us (30%)
  starting transfers between devices  70.8 us (15%)
  local copies, waits for them, and re-layouts  34.6 us (7%)
  other arithmetic  12 us (2%)
    ppermute x66, waiting for transfers between devices, swap(): return lax.ppermute(x, BOTH, [(d, d ^ bit) for d in range(DEVICES)])  109 us
    ppermute x66, starting transfers between devices, swap(): return lax.ppermute(x, BOTH, [(d, d ^ bit) for d in range(DEVICES)])  49.8 us
    ppermute x23, waiting for transfers between devices, ring(): lax.ppermute(x, BOTH, [(d, (d + 8 * way) % DEVICES) for d in range(DEVICE...  34.9 us
    pallas_call x1, Pallas kernels, run_units(): pl.pallas_call(units_kernel, grid_spec=pltpu.PrefetchScalarGridSpec(num_s...  30.2 us
    pallas_call x2, Pallas kernels, run_unmix(): pl.pallas_call(partial(unmix_kernel, count, per, bool(carry)), grid_spec=...  29.9 us
    pallas_call x1, Pallas kernels, run_post(): pl.pallas_call(post_kernel, grid_spec=pltpu.PrefetchScalarGridSpec(num_sc...  28.3 us
    unnamed x182, local copies, waits for them, and re-layouts  24.2 us
    pallas_call x2, Pallas kernels, run_mix(): pl.pallas_call(partial(mix_kernel, count, per, bool(carry)), grid_spec=pl...  21.5 us
  transfers between devices with their start and end apart: 89, of which 47 were waited for; matrix products, arithmetic and copies ran while one was open for 4% of the time, Pallas kernels for 33%

profile of v18, /device:TPU:0, one launch (start us, length us, event | category | flops | bytes accessed | tf_op | source)
XLA Modules:
  0.0 480.1 jit_solution(6534040920927692498)
XLA Ops:
  16.5 6.2 %collective-permute-done.5.refs_1_ = bf16[496,384]{1,0:T(8,128)(2,1)S(1)} collective-permute-done((bf16[496,384]{1,0:T(8,128)(2,1)}, bf16[496,384]{1,0:T(8,128)(2,1)S(1)}, u32[]{:S(2)}, u32[]{:S(2)}) %collective-permute-start.5) | collective-permute-done | bytes 380960 | tf_op jit(solution)/shard_map/ppermute | solution.py:936
  30.8 10.0 %collective-permute-done.10.refs_5_ = bf16[496,384]{1,0:T(8,128)(2,1)S(1)} collective-permute-done((bf16[496,384]{1,0:T(8,128)(2,1)}, bf16[496,384]{1,0:T(8,128)(2,1)S(1)}, u32[]{:S(2)}, u32[]{:S(2)}) %collective-permute-start.10) | collective-permute-done | bytes 380960 | tf_op jit(solution)/shard_map/ppermute | solution.py:936
  45.0 7.8 %collective-permute-done.13.refs_6_ = bf16[496,384]{1,0:T(8,128)(2,1)S(1)} collective-permute-done((bf16[496,384]{1,0:T(8,128)(2,1)}, bf16[496,384]{1,0:T(8,128)(2,1)S(1)}, u32[]{:S(2)}, u32[]{:S(2)}) %collective-permute-start.13) | collective-permute-done | bytes 380960 | tf_op jit(solution)/shard_map/ppermute | solution.py:936
  58.7 5.4 %collective-permute-done.17.refs_7_ = bf16[496,384]{1,0:T(8,128)(2,1)S(1)} collective-permute-done((bf16[496,384]{1,0:T(8,128)(2,1)S(1)}, bf16[496,384]{1,0:T(8,128)(2,1)S(1)}, u32[]{:S(2)}, u32[]{:S(2)}) %collective-permute-start.17) | collective-permute-done | bytes 380960 | tf_op jit(solution)/shard_map/ppermute | solution.py:936
  81.1 7.2 %place.1 = (bf16[3072,384]{1,0:T(8,128)(2,1)}, bf16[768,1536]{1,0:T(8,128)(2,1)}, bf16[768,384]{1,0:T(8,128)(2,1)}, bf16[768,384]{1,0:T(8,128)(2,1)}, bf16[256,384]{1,0:T(8,128)(2,1)}) custom-call(s32[7]{0:T(128)} %concatenate.57.sc, bf16[496,384]{1,0:T(8,128)(2,1)} %pack.1.refs_0_, bf16[496,384]{1,0:T(8,128)(2,1)} %copy-done.68, ...), custom_call_target="tpu_custom_call" | custom-call | bytes 12189696 | tf_op jit(solution)/shard_map/place/pallas_call | solution.py:842
  100.4 7.8 %values.1.refs_12_.refs_4_.v_own = bf16[12,1024,128]{2,1,0:T(8,128)(2,1)} custom-call(s32[7]{0:T(128)} %concatenate.57.sc, bf16[2,1024,768]{2,1,0:T(8,128)(2,1)} %tok.1, f32[1,768]{1,0:T(1,128)} %reshape.241.gain, bf16[768,384]{1,0:T(8,128)(2,1)} %get-tuple-element.422.w_own, bf16[768,384]{1,0:T(8,128)(2,1)} %copy-done.42), custom_call_target="tpu_custom_call" | custom-call | flops 2415919104 | bytes 6291456 | tf_op jit(solution)/shard_map/values/pallas_call | solution.py:81
  116.1 19.1 %collective-permute-done.32.refs_6_ = bf16[384,1024]{1,0:T(8,128)(2,1)} collective-permute-done((bf16[384,1024]{1,0:T(8,128)(2,1)}, bf16[384,1024]{1,0:T(8,128)(2,1)}, u32[]{:S(2)}, u32[]{:S(2)}) %collective-permute-start.32) | collective-permute-done | bytes 786464 | tf_op jit(solution)/shard_map/ppermute | solution.py:936
  141.1 5.5 %masked.1.cot = bf16[4,512,768]{2,1,0:T(8,128)(2,1)} custom-call(s32[7]{0:T(128)} %concatenate.57.sc, bf16[2,8,2,64,768]{4,3,2,1,0:T(8,128)(2,1)} %bitcast.114, bf16[2,8,64,768]{3,2,1,0:T(8,128)(2,1)} %copy-done.63), custom_call_target="tpu_custom_call" | custom-call | bytes 6291456 | tf_op jit(solution)/shard_map/masked/pallas_call | solution.py:298
  146.7 10.4 %collective-permute-done.36.refs_7_ = bf16[384,1024]{1,0:T(8,128)(2,1)} collective-permute-done((bf16[384,1024]{1,0:T(8,128)(2,1)}, bf16[384,1024]{1,0:T(8,128)(2,1)}, u32[]{:S(2)}, u32[]{:S(2)}) %collective-permute-start.36) | collective-permute-done | bytes 786464 | tf_op jit(solution)/shard_map/ppermute | solution.py:936
  162.3 13.4 %mix.2 = (bf16[12,512,256]{2,1,0:T(8,128)(2,1)}, f32[12,512,256]{2,1,0:T(8,128)}, bf16[12,512,1024]{2,1,0:T(8,128)(2,1)}, bf16[12,512,256]{2,1,0:T(8,128)(2,1)}) custom-call(s32[7]{0:T(128)} %concatenate.57.sc, bf16[384,1024]{1,0:T(8,128)(2,1)} %bitcast.119, bf16[384,1024]{1,0:T(8,128)(2,1)} %collective-permute-done.24.refs_1_, ...), custom_call_target="tpu_custom_call" | custom-call | flops 3221225472 | bytes 20447232 | tf_op jit(solution)/shard_map/mix/pallas_call | solution.py:189
  182.4 8.1 %mix.3 = (bf16[12,512,256]{2,1,0:T(8,128)(2,1)}, f32[12,512,256]{2,1,0:T(8,128)}, bf16[12,512,1024]{2,1,0:T(8,128)(2,1)}, bf16[12,512,256]{2,1,0:T(8,128)(2,1)}) custom-call(s32[7]{0:T(128)} %concatenate.57.sc, bf16[384,1024]{1,0:T(8,128)(2,1)} %copy-done.67, ...), custom_call_target="tpu_custom_call", output_to_operand_aliasing={{0}: (8, {}), {1}: (9, {}), {2}: (10, {}), {3}: (11, {})} | custom-call | flops 3221225472 | bytes 20447232 | tf_op jit(solution)/shard_map/mix/pallas_call | solution.py:189
  190.5 10.6 %pre.1 = (bf16[4,512,768]{2,1,0:T(8,128)(2,1)}, bf16[4,512,768]{2,1,0:T(8,128)(2,1)}, bf16[4,512,768]{2,1,0:T(8,128)(2,1)}) custom-call(s32[7]{0:T(128)} %concatenate.57.sc, bf16[2,8,2,64,768]{4,3,2,1,0:T(8,128)(2,1)} %bitcast.106, bf16[2,8,64,768]{3,2,1,0:T(8,128)(2,1)} %copy-done.62, bf16[12,512,256]{2,1,0:T(8,128)(2,1)} %get-tuple-element.483.heads, ...), custom_call_target="tpu_custom_call" | custom-call | flops 2415919104 | bytes 25165824 | tf_op jit(solution)/shard_map/pre/pallas_call | solution.py:269
  201.0 30.2 %units.1 = (bf16[2048,3072]{1,0:T(8,128)(2,1)}, bf16[2048,3072]{1,0:T(8,128)(2,1)}) custom-call(s32[7]{0:T(128)} %concatenate.57.sc, bf16[2048,768]{1,0:T(8,128)(2,1)} %bitcast.140, bf16[2048,768]{1,0:T(8,128)(2,1)} %bitcast.122, bf16[768,1536]{1,0:T(8,128)(2,1)} %get-tuple-element.489.up_own, bf16[768,1536]{1,0:T(8,128)(2,1)} %collective-permute-done.42.up_far, ...), custom_call_target="tpu_custom_call" | custom-call | flops 19327352832 | bytes 34603008 | tf_op jit(solution)/shard_map/units/pallas_call | solution.py:364
  231.3 28.3 %post.1 = (bf16[2,512,768]{2,1,0:T(8,128)(2,1)}, bf16[2,512,768]{2,1,0:T(8,128)(2,1)}, bf16[12,512,256]{2,1,0:T(8,128)(2,1)}, f32[1,768]{1,0:T(1,128)}) custom-call(s32[7]{0:T(128)} %concatenate.57.sc, bf16[4,512,768]{2,1,0:T(8,128)(2,1)} %get-tuple-element.486.resid, bf16[4,512,3072]{2,1,0:T(8,128)(2,1)} %bitcast.143, bf16[4,512,3072]{2,1,0:T(8,128)(2,1)} %bitcast.144, ...), custom_call_target="tpu_custom_call" | custom-call | flops 12079595520 | bytes 37748736 | tf_op jit(solution)/shard_map/post/pallas_call | solution.py:568
  259.6 9.8 %unmix.2 = (bf16[384,1024]{1,0:T(8,128)(2,1)}, bf16[384,1024]{1,0:T(8,128)(2,1)}, bf16[384,1024]{1,0:T(8,128)(2,1)}, bf16[384,1024]{1,0:T(8,128)(2,1)}, bf16[12,...) custom-call(s32[7]{0:T(128)} %concatenate.57.sc, bf16[12,1024,128]{2,1,0:T(8,128)(2,1)} %values.1.refs_12_.refs_4_.v_own, ...), custom_call_target="tpu_custom_call" | custom-call | flops 4831838208 | bytes 33030144 | tf_op jit(solution)/shard_map/unmix/pallas_call | solution.py:653
  272.5 20.1 %unmix.3 = (bf16[384,1024]{1,0:T(8,128)(2,1)}, bf16[384,1024]{1,0:T(8,128)(2,1)}, bf16[384,1024]{1,0:T(8,128)(2,1)}, bf16[384,1024]{1,0:T(8,128)(2,1)}, bf16[384...) custom-call(s32[7]{0:T(128)} %concatenate.57.sc, ...), custom_call_target="tpu_custom_call", output_to_operand_aliasing={{12}: (10, {}), {13}: (11, {})} | custom-call | flops 4831838208 | bytes 33030144 | tf_op jit(solution)/shard_map/unmix/pallas_call | solution.py:653
  298.5 16.1 %up_grad.1 = (bf16[768,1536]{1,0:T(8,128)(2,1)}, bf16[768,1536]{1,0:T(8,128)(2,1)}) custom-call(s32[7]{0:T(128)} %concatenate.57.sc, bf16[2048,768]{1,0:T(8,128)(2,1)} %bitcast.141, bf16[2048,3072]{1,0:T(8,128)(2,1)} %get-tuple-element.491.up_grad), custom_call_target="tpu_custom_call" | custom-call | flops 9663676416 | bytes 15728640 | tf_op jit(solution)/shard_map/up_grad/pallas_call | solution.py:427
  323.1 15.9 %down_grad.1 = (bf16[3072,384]{1,0:T(8,128)(2,1)}, bf16[3072,384]{1,0:T(8,128)(2,1)}) custom-call(s32[7]{0:T(128)} %concatenate.57.sc, bf16[2048,3072]{1,0:T(8,128)(2,1)} %get-tuple-element.561.active, bf16[2048,768]{1,0:T(8,128)(2,1)} %bitcast.123), custom_call_target="tpu_custom_call" | custom-call | flops 9663676416 | bytes 15728640 | tf_op jit(solution)/shard_map/down_grad/pallas_call | solution.py:396
  348.8 15.0 %out.3 = (bf16[2,512,768]{2,1,0:T(8,128)(2,1)S(1)}, bf16[2,512,768]{2,1,0:T(8,128)(2,1)S(1)}) custom-call(s32[7]{0:T(128)S(1)} %copy-done.30, bf16[4,512,3072]{2,1,0:T(8,128)(2,1)} %bitcast.142, bf16[4,512,768]{2,1,0:T(8,128)(2,1)S(1)} %copy-done.33, bf16[3072,384]{1,0:T(8,128)(2,1)S(1)} %copy-done.35, bf16[3072,384]{1,0:T(8,128)(2,1)} %collective-permute-done.43.dn_far), custom_call_target="tpu_custom_call" | custom-call | flops 9663676416 | bytes 23592960 | tf_op jit(solution)/shard_map/out/pallas_call | solution.py:501
  369.5 5.3 %out_grad.1 = (bf16[768,384]{1,0:T(8,128)(2,1)S(1)}, bf16[768,384]{1,0:T(8,128)(2,1)S(1)}) custom-call(s32[7]{0:T(128)S(1)} %copy-done.30, bf16[4,512,768]{2,1,0:T(8,128)(2,1)S(1)} %copy-done.32, bf16[2,512,768]{2,1,0:T(8,128)(2,1)S(1)} %copy-done.54, bf16[2,512,768]{2,1,0:T(8,128)(2,1)S(1)} %copy-done.38), custom_call_target="tpu_custom_call" | custom-call | flops 2415919104 | bytes 6291456 | tf_op jit(solution)/shard_map/out_grad/pallas_call | solution.py:467
  396.6 13.6 %close.1 = (f32[2,8,2,64,768]{4,3,2,1,0:T(8,128)}, f32[2,8,2,64,768]{4,3,2,1,0:T(8,128)}, bf16[2,768,384]{2,1,0:T(8,128)(2,1)S(1)}, f32[1,768]{1,0:T(1,128)S(1)}) custom-call(s32[7]{0:T(128)S(1)} %copy-done.30, bf16[2,8,2,64,768]{4,3,2,1,0:T(8,128)(2,1)S(1)} %bitcast.107, bf16[2,8,64,768]{3,2,1,0:T(8,128)(2,1)S(1)} %bitcast.112, ...), custom_call_target="tpu_custom_call" | custom-call | flops 4831838208 | bytes 29884416 | tf_op jit(solution)/shard_map/close/pallas_call | solution.py:745
  420.6 6.9 %collective-permute-done.70 = bf16[432,384]{1,0:T(8,128)(2,1)S(1)} collective-permute-done((bf16[432,384]{1,0:T(8,128)(2,1)S(1)}, bf16[432,384]{1,0:T(8,128)(2,1)S(1)}, u32[]{:S(2)}, u32[]{:S(2)}) %collective-permute-start.70) | collective-permute-done | bytes 331808 | tf_op jit(solution)/shard_map/ppermute | solution.py:936
  434.2 5.6 %collective-permute-done.75 = bf16[4,2,64,384]{3,2,1,0:T(8,128)(2,1)S(1)} collective-permute-done((bf16[4,2,64,384]{3,2,1,0:T(8,128)(2,1)S(1)}, bf16[4,2,64,384]{3,2,1,0:T(8,128)(2,1)S(1)}, u32[]{:S(2)}, u32[]{:S(2)}) %collective-permute-start.75) | collective-permute-done | bytes 393248 | tf_op jit(solution)/shard_map/ppermute | solution.py:936
  440.0 5.4 %collective-permute-done.73 = bf16[432,384]{1,0:T(8,128)(2,1)S(1)} collective-permute-done((bf16[432,384]{1,0:T(8,128)(2,1)S(1)}, bf16[432,384]{1,0:T(8,128)(2,1)S(1)}, u32[]{:S(2)}, u32[]{:S(2)}) %collective-permute-start.73) | collective-permute-done | bytes 331808 | tf_op jit(solution)/shard_map/ppermute | solution.py:936
  (426 shorter events, 194.3 us)
Async XLA Ops:
  115.0 23.2 %collective-permute-start.35 = (bf16[12,1024,128]{2,1,0:T(8,128)(2,1)}, bf16[12,1024,128]{2,1,0:T(8,128)(2,1)}, u32[]{:S(2)}, u32[]{:S(2)}) collective-permute-start(bf16[12,1024,128]{2,1,0:T(8,128)(2,1)} %values.1.refs_12_.refs_4_.v_own), channel_id=1, source_target_pairs={{0,1},{1,0},{2,3},{3,2},{4,5},{5,4},{6,7},{7,6},{8,9},{9,8},{10,11... | collective-permute-start | bytes 9437192 | tf_op jit(solution)/shard_map/ppermute | solution.py:936
  115.0 20.3 %collective-permute-start.32 = (bf16[384,1024]{1,0:T(8,128)(2,1)}, bf16[384,1024]{1,0:T(8,128)(2,1)}, u32[]{:S(2)}, u32[]{:S(2)}) collective-permute-start(bf16[384,1024]{1,0:T(8,128)(2,1)} %collective-permute-done.26.refs_4_), channel_id=1, source_target_pairs={{0,4},{1,5},{2,6},{3,7},{4,0},{5,1},{6,2},{7,3},{8,12},{9,13},{10,... | collective-permute-start | bytes 2359304 | tf_op jit(solution)/shard_map/ppermute | solution.py:936
  116.1 21.2 %collective-permute-start.34 = (bf16[384,1024]{1,0:T(8,128)(2,1)S(1)}, bf16[384,1024]{1,0:T(8,128)(2,1)S(1)}, u32[]{:S(2)}, u32[]{:S(2)}) collective-permute-start(bf16[384,1024]{1,0:T(8,128)(2,1)S(1)} %collective-permute-done.30.refs_8_), channel_id=1, source_target_pairs={{0,8},{1,9},{2,10},{3,11},{4,12},{5,13},{6,14},{7,15},{8,16},{9,17... | collective-permute-start | bytes 2359304 | tf_op jit(solution)/shard_map/ppermute | solution.py:940
  139.5 20.4 %collective-permute-start.37 = (bf16[384,1024]{1,0:T(8,128)(2,1)}, bf16[384,1024]{1,0:T(8,128)(2,1)}, u32[]{:S(2)}, u32[]{:S(2)}) collective-permute-start(bf16[384,1024]{1,0:T(8,128)(2,1)} %collective-permute-done.32.refs_6_), channel_id=1, source_target_pairs={{0,8},{1,9},{2,10},{3,11},{4,12},{5,13},{6,14},{7,15},{8,16},{9,17... | collective-permute-start | bytes 2359304 | tf_op jit(solution)/shard_map/ppermute | solution.py:940
  139.5 20.4 %collective-permute-start.38 = (bf16[384,1024]{1,0:T(8,128)(2,1)}, bf16[384,1024]{1,0:T(8,128)(2,1)}, u32[]{:S(2)}, u32[]{:S(2)}) collective-permute-start(bf16[384,1024]{1,0:T(8,128)(2,1)} %collective-permute-done.33.refs_9_), channel_id=1, source_target_pairs={{0,4},{1,5},{2,6},{3,7},{4,0},{5,1},{6,2},{7,3},{8,12},{9,13},{10,... | collective-permute-start | bytes 2359304 | tf_op jit(solution)/shard_map/ppermute | solution.py:936
  270.6 22.0 %collective-permute-start.45 = (bf16[384,1024]{1,0:T(8,128)(2,1)}, bf16[384,1024]{1,0:T(8,128)(2,1)S(1)}, u32[]{:S(2)}, u32[]{:S(2)}) collective-permute-start(bf16[384,1024]{1,0:T(8,128)(2,1)} %get-tuple-element.506), channel_id=1, source_target_pairs={{0,24},{1,25},{2,26},{3,27},{4,28},{5,29},{6,30},{7,31},{8,0},{9,1... | collective-permute-start | bytes 2359304 | tf_op jit(solution)/shard_map/ppermute | solution.py:940
  270.6 22.0 %collective-permute-start.46 = (bf16[384,1024]{1,0:T(8,128)(2,1)}, bf16[384,1024]{1,0:T(8,128)(2,1)S(1)}, u32[]{:S(2)}, u32[]{:S(2)}) collective-permute-start(bf16[384,1024]{1,0:T(8,128)(2,1)} %get-tuple-element.507), channel_id=1, source_target_pairs={{0,2},{1,3},{2,0},{3,1},{4,6},{5,7},{6,4},{7,5},{8,10},{9,11},{10,... | collective-permute-start | bytes 2359304 | tf_op jit(solution)/shard_map/ppermute | solution.py:936
  272.1 20.6 %collective-permute-start.47 = (bf16[384,1024]{1,0:T(8,128)(2,1)}, bf16[384,1024]{1,0:T(8,128)(2,1)}, u32[]{:S(2)}, u32[]{:S(2)}) collective-permute-start(bf16[384,1024]{1,0:T(8,128)(2,1)} %get-tuple-element.508), channel_id=1, source_target_pairs={{0,4},{1,5},{2,6},{3,7},{4,0},{5,1},{6,2},{7,3},{8,12},{9,13},{10,... | collective-permute-start | bytes 2359304 | tf_op jit(solution)/shard_map/ppermute | solution.py:936
  292.6 25.4 %collective-permute-start.51 = (bf16[12,1024,128]{2,1,0:T(8,128)(2,1)}, bf16[12,1024,128]{2,1,0:T(8,128)(2,1)}, u32[]{:S(2)}, u32[]{:S(2)}) collective-permute-start(bf16[12,1024,128]{2,1,0:T(8,128)(2,1)} %get-tuple-element.545), channel_id=1, source_target_pairs={{0,1},{1,0},{2,3},{3,2},{4,5},{5,4},{6,7},{7,6},{8,9},{9,8},{10,11... | collective-permute-start | bytes 9437192 | tf_op jit(solution)/shard_map/ppermute | solution.py:936
  296.3 19.9 %collective-permute-start.50 = (bf16[384,1024]{1,0:T(8,128)(2,1)S(1)}, bf16[384,1024]{1,0:T(8,128)(2,1)S(1)}, u32[]{:S(2)}, u32[]{:S(2)}) collective-permute-start(bf16[384,1024]{1,0:T(8,128)(2,1)S(1)} %get-tuple-element.542), channel_id=1, source_target_pairs={{0,4},{1,5},{2,6},{3,7},{4,0},{5,1},{6,2},{7,3},{8,12},{9,13},{10,... | collective-permute-start | bytes 2359304 | tf_op jit(solution)/shard_map/ppermute | solution.py:936
  297.9 20.1 %collective-permute-start.48 = (bf16[384,1024]{1,0:T(8,128)(2,1)}, bf16[384,1024]{1,0:T(8,128)(2,1)S(1)}, u32[]{:S(2)}, u32[]{:S(2)}) collective-permute-start(bf16[384,1024]{1,0:T(8,128)(2,1)} %get-tuple-element.540), channel_id=1, source_target_pairs={{0,24},{1,25},{2,26},{3,27},{4,28},{5,29},{6,30},{7,31},{8,0},{9,1... | collective-permute-start | bytes 2359304 | tf_op jit(solution)/shard_map/ppermute | solution.py:940
  297.9 20.1 %collective-permute-start.49 = (bf16[384,1024]{1,0:T(8,128)(2,1)}, bf16[384,1024]{1,0:T(8,128)(2,1)S(1)}, u32[]{:S(2)}, u32[]{:S(2)}) collective-permute-start(bf16[384,1024]{1,0:T(8,128)(2,1)} %get-tuple-element.541), channel_id=1, source_target_pairs={{0,2},{1,3},{2,0},{3,1},{4,6},{5,7},{6,4},{7,5},{8,10},{9,11},{10,... | collective-permute-start | bytes 2359304 | tf_op jit(solution)/shard_map/ppermute | solution.py:936
  318.0 22.4 %collective-permute-start.55 = (bf16[768,1536]{1,0:T(8,128)(2,1)}, bf16[768,1536]{1,0:T(8,128)(2,1)S(1)}, u32[]{:S(2)}, u32[]{:S(2)}) collective-permute-start(bf16[768,1536]{1,0:T(8,128)(2,1)} %get-tuple-element.564), channel_id=1, source_target_pairs={{0,1},{1,0},{2,3},{3,2},{4,5},{5,4},{6,7},{7,6},{8,9},{9,8},{10,11... | collective-permute-start | bytes 7077896 | tf_op jit(solution)/shard_map/ppermute | solution.py:936
  319.5 20.1 %collective-permute-start.53 = (bf16[384,1024]{1,0:T(8,128)(2,1)}, bf16[384,1024]{1,0:T(8,128)(2,1)S(1)}, u32[]{:S(2)}, u32[]{:S(2)}) collective-permute-start(bf16[384,1024]{1,0:T(8,128)(2,1)} %get-tuple-element.559), channel_id=1, source_target_pairs={{0,2},{1,3},{2,0},{3,1},{4,6},{5,7},{6,4},{7,5},{8,10},{9,11},{10,... | collective-permute-start | bytes 2359304 | tf_op jit(solution)/shard_map/ppermute | solution.py:936
  340.4 24.5 %collective-permute-start.59 = (bf16[3072,384]{1,0:T(8,128)(2,1)}, bf16[3072,384]{1,0:T(8,128)(2,1)S(1)}, u32[]{:S(2)}, u32[]{:S(2)}) collective-permute-start(bf16[3072,384]{1,0:T(8,128)(2,1)} %get-tuple-element.579), channel_id=1, source_target_pairs={{0,1},{1,0},{2,3},{3,2},{4,5},{5,4},{6,7},{7,6},{8,9},{9,8},{10,11... | collective-permute-start | bytes 7077896 | tf_op jit(solution)/shard_map/ppermute | solution.py:936
  340.9 23.0 %collective-permute-start.56 = (bf16[384,1024]{1,0:T(8,128)(2,1)S(1)}, bf16[384,1024]{1,0:T(8,128)(2,1)S(1)}, u32[]{:S(2)}, u32[]{:S(2)}) collective-permute-start(bf16[384,1024]{1,0:T(8,128)(2,1)S(1)} %get-tuple-element.574), channel_id=1, source_target_pairs={{0,24},{1,25},{2,26},{3,27},{4,28},{5,29},{6,30},{7,31},{8,0},{9,1... | collective-permute-start | bytes 2359304 | tf_op jit(solution)/shard_map/ppermute | solution.py:940
  344.8 19.9 %collective-permute-start.57 = (bf16[384,1024]{1,0:T(8,128)(2,1)}, bf16[384,1024]{1,0:T(8,128)(2,1)S(1)}, u32[]{:S(2)}, u32[]{:S(2)}) collective-permute-start(bf16[384,1024]{1,0:T(8,128)(2,1)} %get-tuple-element.575), channel_id=1, source_target_pairs={{0,2},{1,3},{2,0},{3,1},{4,6},{5,7},{6,4},{7,5},{8,10},{9,11},{10,... | collective-permute-start | bytes 2359304 | tf_op jit(solution)/shard_map/ppermute | solution.py:936
  364.9 23.9 %collective-permute-start.64 = (bf16[2,512,768]{2,1,0:T(8,128)(2,1)S(1)}, bf16[2,512,768]{2,1,0:T(8,128)(2,1)S(1)}, u32[]{:S(2)}, u32[]{:S(2)}) collective-permute-start(bf16[2,512,768]{2,1,0:T(8,128)(2,1)S(1)} %get-tuple-element.615), channel_id=1, source_target_pairs={{0,1},{1,0},{2,3},{3,2},{4,5},{5,4},{6,7},{7,6},{8,9},{9,8},{10,11... | collective-permute-start | bytes 4718600 | tf_op jit(solution)/shard_map/ppermute | solution.py:936
  365.4 23.3 %collective-permute-start.60 = (bf16[384,1024]{1,0:T(8,128)(2,1)S(1)}, bf16[384,1024]{1,0:T(8,128)(2,1)S(1)}, u32[]{:S(2)}, u32[]{:S(2)}) collective-permute-start(bf16[384,1024]{1,0:T(8,128)(2,1)S(1)} %get-tuple-element.587), channel_id=1, source_target_pairs={{0,24},{1,25},{2,26},{3,27},{4,28},{5,29},{6,30},{7,31},{8,0},{9,1... | collective-permute-start | bytes 2359304 | tf_op jit(solution)/shard_map/ppermute | solution.py:940
  367.2 21.6 %collective-permute-start.61 = (bf16[384,1024]{1,0:T(8,128)(2,1)S(1)}, bf16[384,1024]{1,0:T(8,128)(2,1)S(1)}, u32[]{:S(2)}, u32[]{:S(2)}) collective-permute-start(bf16[384,1024]{1,0:T(8,128)(2,1)S(1)} %get-tuple-element.588), channel_id=1, source_target_pairs={{0,2},{1,3},{2,0},{3,1},{4,6},{5,7},{6,4},{7,5},{8,10},{9,11},{10,... | collective-permute-start | bytes 2359304 | tf_op jit(solution)/shard_map/ppermute | solution.py:936
  367.9 20.9 %collective-permute-start.62 = (bf16[384,1024]{1,0:T(8,128)(2,1)S(1)}, bf16[384,1024]{1,0:T(8,128)(2,1)S(1)}, u32[]{:S(2)}, u32[]{:S(2)}) collective-permute-start(bf16[384,1024]{1,0:T(8,128)(2,1)S(1)} %copy-done.88), channel_id=1, source_target_pairs={{0,4},{1,5},{2,6},{3,7},{4,0},{5,1},{6,2},{7,3},{8,12},{9,13},{10,... | collective-permute-start | bytes 2359304 | tf_op jit(solution)/shard_map/ppermute | solution.py:936
  388.8 23.1 %collective-permute-start.65 = (bf16[432,384]{1,0:T(8,128)(2,1)}, bf16[432,384]{1,0:T(8,128)(2,1)}, u32[]{:S(2)}, u32[]{:S(2)}) collective-permute-start(bf16[432,384]{1,0:T(8,128)(2,1)} %get-tuple-element.629), channel_id=1, source_target_pairs={{0,24},{1,25},{2,26},{3,27},{4,28},{5,29},{6,30},{7,31},{8,0},{9,1... | collective-permute-start | bytes 995336 | tf_op jit(solution)/shard_map/ppermute | solution.py:940
  389.0 22.9 %collective-permute-start.66 = (bf16[432,384]{1,0:T(8,128)(2,1)}, bf16[432,384]{1,0:T(8,128)(2,1)}, u32[]{:S(2)}, u32[]{:S(2)}) collective-permute-start(bf16[432,384]{1,0:T(8,128)(2,1)} %get-tuple-element.630), channel_id=1, source_target_pairs={{0,2},{1,3},{2,0},{3,1},{4,6},{5,7},{6,4},{7,5},{8,10},{9,11},{10,... | collective-permute-start | bytes 995336 | tf_op jit(solution)/shard_map/ppermute | solution.py:936
  389.7 22.2 %collective-permute-start.67 = (bf16[432,384]{1,0:T(8,128)(2,1)}, bf16[432,384]{1,0:T(8,128)(2,1)}, u32[]{:S(2)}, u32[]{:S(2)}) collective-permute-start(bf16[432,384]{1,0:T(8,128)(2,1)} %get-tuple-element.631), channel_id=1, source_target_pairs={{0,4},{1,5},{2,6},{3,7},{4,0},{5,1},{6,2},{7,3},{8,12},{9,13},{10,... | collective-permute-start | bytes 995336 | tf_op jit(solution)/shard_map/ppermute | solution.py:936
  (155 other events, 1620.2 us)

commit v19 on v17

--- a/solution.py
+++ b/solution.py
@@ -698,13 +698,11 @@
     )(sc, v_own, v_far, grad_heads, mean, exps, inverse, *carry)
 
 
-def close_kernel(sc, tok, res_own, res_got, out_own, out_got, own, far, gain, w_own, w_far, *refs):
-    (output, tok_grad, d_value, d_gain, total, weight) = refs
+def close_kernel(sc, tok, res_own, res_got, own, far, gain, w_own, w_far, *refs):
+    (tok_grad, d_value, d_gain, total, weight) = refs
     step = pl.program_id(0)
     whole_weight(sc, step, w_own, w_far, weight)
     core = sc[CORE]
-    output[:, :, core] = out_own[...].astype(F32)
-    output[:, :, 1 - core] = out_got[...].astype(F32)
     tok_grad[:, :, core] = res_own[...].astype(F32)
     tok_grad[:, :, 1 - core] = res_got[...].astype(F32)
     runs = tok.shape[1]
@@ -747,7 +745,7 @@
         d_value[1] = low[:, SIDE:]
 
 
-def run_close(sc, tokens, res_own, res_got, out_own, out_got, own, far, gain, w_own, w_far):
+def run_close(sc, tokens, res_own, res_got, own, far, gain, w_own, w_far):
     runs = 2
     slab = (2, RUNS, 2, HALF, WIDTH)
     half = (2, RUNS, HALF, WIDTH)
@@ -760,13 +758,12 @@
             num_scalar_prefetch=1,
             grid=(RUNS // runs,),
             in_specs=[whole_spec]
-            + [half_spec] * 4
+            + [half_spec] * 2
             + [back_spec, back_spec, held((1, WIDTH)), held((WIDTH, SIDE)), held((WIDTH, SIDE))],
-            out_specs=[whole_spec, whole_spec, held((2, WIDTH, SIDE)), held((1, WIDTH))],
+            out_specs=[whole_spec, held((2, WIDTH, SIDE)), held((1, WIDTH))],
             scratch_shapes=[pltpu.VMEM((WIDTH, WIDTH), F32), pltpu.VMEM((WIDTH, WIDTH), BF16)],
         ),
         out_shape=[
-            jax.ShapeDtypeStruct(slab, F32),
             jax.ShapeDtypeStruct(slab, F32),
             jax.ShapeDtypeStruct((2, WIDTH, SIDE), BF16),
             jax.ShapeDtypeStruct((1, WIDTH), F32),
@@ -779,13 +776,36 @@
     )(
         sc,
         tokens.reshape(slab),
-        *(x.reshape(half) for x in (res_own, res_got, out_own, out_got)),
+        *(x.reshape(half) for x in (res_own, res_got)),
         own,
         far,
         gain,
         w_own,
         w_far,
     )
+
+
+def join_kernel(sc, own, got, output):
+    output[:, :, sc[CORE]] = own[...].astype(F32)
+    output[:, :, 1 - sc[CORE]] = got[...].astype(F32)
+
+
+def run_join(sc, own, got):
+    half = (2, RUNS, HALF, WIDTH)
+    half_spec = spec((2, 2, HALF, WIDTH), lambda j, s: (0, j, 0, 0))
+    return pl.pallas_call(
+        join_kernel,
+        grid_spec=pltpu.PrefetchScalarGridSpec(
+            num_scalar_prefetch=1,
+            grid=(RUNS // 2,),
+            in_specs=[half_spec, half_spec],
+            out_specs=spec((2, 2, 2, HALF, WIDTH), lambda j, s: (0, j, 0, 0, 0)),
+        ),
+        out_shape=jax.ShapeDtypeStruct((2, RUNS, 2, HALF, WIDTH), F32),
+        compiler_params=params(LESS),
+        cost_estimate=pl.CostEstimate(flops=0, bytes_accessed=12 * LMAX * WIDTH, transcendentals=0),
+        name="join",
+    )(sc, own.reshape(half), got.reshape(half))
 
 
 PACK_DOWN, PACK_UP, PACK_OUT, PACK_VALUE, PACK_GAIN, PACK = 0, 192, 384, 432, 480, 496
@@ -1098,18 +1118,19 @@
     rand_sum = scatter_add(have, got, 4)[0, 0, 0].reshape(2, 3, HALF, LMAX)
 
     sums, got = scatter_send(by_place(packed), 0)
-    output, tokens_grad, d_value, d_gain_one = run_close(
-        sc, tokens, res_own, res_got, out_own, other(out_far), back_own, back_got, gain_one, value, value_far
+    tokens_grad, d_value, d_gain_one = run_close(
+        sc, tokens, res_own, res_got, back_own, back_got, gain_one, value, value_far
     )
     gain_pair = jnp.concatenate([d_gain_one, d_gain_two]).reshape(2, 16, 1, 48).astype(BF16)
     gain_pair = jnp.pad(gain_pair, ((0, 0), (0, 0), (0, 15), (0, SIDE - 48)))
     small = jnp.concatenate([d_value.reshape(2, 16, 48, SIDE), gain_pair], 2)
-    sums, got, output, tokens_grad, small = together((sums, got, output, tokens_grad, small))
+    sums, got, tokens_grad, small, out_got = together((sums, got, tokens_grad, small, other(out_far)))
     sums = scatter_add(sums, got, 0)
 
     sums, got = scatter_send(sums, 1)
     small = add_low(pick(small, core), other(pick(small, 1 - core))).reshape(4, 2, 2, 64, SIDE)
-    sums, got, small = together((sums, got, small))
+    output = run_join(sc, out_own, out_got)
+    sums, got, small, output = together((sums, got, small, output))
     sums = scatter_add(sums, got, 1)
 
     sums, got = scatter_send(sums, 2)

time: 480 us -> 480 us (level)
  waiting for transfers between devices: 136 us -> 127 us
    ppermute x66, waiting for transfers between devices: 89.1 us -> 81.8 us  [swap(): return lax.ppermute(x, BOTH, [(d, d ^ bit) for d in range(DEVICES)])]
    unnamed x198 -> x196, local copies, waits for them, and re-layouts: 21.3 us -> 25 us
  transfers between devices with their start and end apart: 89 -> 89, of which waited for: 41 -> 39; matrix products, arithmetic and copies ran while one was open for 3% -> 3% of each run, Pallas kernels for 33% -> 34%
where the time goes in v19:
time: 480 us; the launch traced here: 474 us
  Pallas kernels  220 us (46%)
  waiting for transfers between devices  127 us (26%)
  starting transfers between devices  78.5 us (16%)
  local copies, waits for them, and re-layouts  34.5 us (7%)
  other arithmetic  11.2 us (2%)
    ppermute x66, waiting for transfers between devices, swap(): return lax.ppermute(x, BOTH, [(d, d ^ bit) for d in range(DEVICES)])  81.8 us
    ppermute x66, starting transfers between devices, swap(): return lax.ppermute(x, BOTH, [(d, d ^ bit) for d in range(DEVICES)])  48.9 us
    ppermute x23, waiting for transfers between devices, ring(): lax.ppermute(x, BOTH, [(d, (d + 8 * way) % DEVICES) for d in range(DEVICE...  45.4 us
    pallas_call x1, Pallas kernels, run_units(): pl.pallas_call(units_kernel, grid_spec=pltpu.PrefetchScalarGridSpec(num_s...  30.3 us
    ppermute x23, starting transfers between devices, ring(): lax.ppermute(x, BOTH, [(d, (d + 8 * way) % DEVICES) for d in range(DEVICE...  29.7 us
    pallas_call x2, Pallas kernels, run_unmix(): pl.pallas_call(partial(unmix_kernel, count, bool(carry)), grid_spec=pltpu...  29.5 us
    pallas_call x1, Pallas kernels, run_post(): pl.pallas_call(post_kernel, grid_spec=pltpu.PrefetchScalarGridSpec(num_sc...  28.1 us
    unnamed x196, local copies, waits for them, and re-layouts  25 us
  transfers between devices with their start and end apart: 89, of which 39 were waited for; matrix products, arithmetic and copies ran while one was open for 3% of the time, Pallas kernels for 34%

profile of v19, /device:TPU:0, one launch (start us, length us, event | category | flops | bytes accessed | tf_op | source)
XLA Modules:
  0.0 473.6 jit_solution(9209796580949369310)
XLA Ops:
  16.6 8.3 %collective-permute-done.7.refs_4_ = bf16[496,384]{1,0:T(8,128)(2,1)S(1)} collective-permute-done((bf16[496,384]{1,0:T(8,128)(2,1)}, bf16[496,384]{1,0:T(8,128)(2,1)S(1)}, u32[]{:S(2)}, u32[]{:S(2)}) %collective-permute-start.7) | collective-permute-done | bytes 380960 | tf_op jit(solution)/shard_map/ppermute | solution.py:972
  31.6 7.5 %collective-permute-done.9.refs_3_ = bf16[496,384]{1,0:T(8,128)(2,1)S(1)} collective-permute-done((bf16[496,384]{1,0:T(8,128)(2,1)}, bf16[496,384]{1,0:T(8,128)(2,1)S(1)}, u32[]{:S(2)}, u32[]{:S(2)}) %collective-permute-start.9) | collective-permute-done | bytes 380960 | tf_op jit(solution)/shard_map/ppermute | solution.py:968
  45.1 6.2 %collective-permute-done.13.refs_6_ = bf16[496,384]{1,0:T(8,128)(2,1)S(1)} collective-permute-done((bf16[496,384]{1,0:T(8,128)(2,1)S(1)}, bf16[496,384]{1,0:T(8,128)(2,1)S(1)}, u32[]{:S(2)}, u32[]{:S(2)}) %collective-permute-start.13) | collective-permute-done | bytes 380960 | tf_op jit(solution)/shard_map/ppermute | solution.py:968
  67.4 7.1 %collective-permute-done.23.refs_15_ = bf16[496,384]{1,0:T(8,128)(2,1)S(1)} collective-permute-done((bf16[496,384]{1,0:T(8,128)(2,1)S(1)}, bf16[496,384]{1,0:T(8,128)(2,1)S(1)}, u32[]{:S(2)}, u32[]{:S(2)}) %collective-permute-start.23) | collective-permute-done | bytes 380960 | tf_op jit(solution)/shard_map/ppermute | solution.py:972
  77.8 7.2 %place.1 = (bf16[3072,384]{1,0:T(8,128)(2,1)}, bf16[768,1536]{1,0:T(8,128)(2,1)}, bf16[768,384]{1,0:T(8,128)(2,1)}, bf16[768,384]{1,0:T(8,128)(2,1)}, bf16[256,384]{1,0:T(8,128)(2,1)}) custom-call(s32[7]{0:T(128)} %concatenate.54.sc, bf16[496,384]{1,0:T(8,128)(2,1)} %pack.1.refs_0_, bf16[496,384]{1,0:T(8,128)(2,1)} %copy-done.75, ...), custom_call_target="tpu_custom_call" | custom-call | bytes 12189696 | tf_op jit(solution)/shard_map/place/pallas_call | solution.py:874
  95.6 7.8 %values.1.refs_12_.refs_4_.v_own = bf16[12,1024,128]{2,1,0:T(8,128)(2,1)} custom-call(s32[7]{0:T(128)} %concatenate.54.sc, bf16[2,1024,768]{2,1,0:T(8,128)(2,1)} %tok.1, f32[1,768]{1,0:T(1,128)} %reshape.205.gain, bf16[768,384]{1,0:T(8,128)(2,1)} %get-tuple-element.431.w_own, bf16[768,384]{1,0:T(8,128)(2,1)} %copy-done.49), custom_call_target="tpu_custom_call" | custom-call | flops 2415919104 | bytes 6291456 | tf_op jit(solution)/shard_map/values/pallas_call | solution.py:81
  113.7 16.7 %collective-permute-done.32.refs_6_ = bf16[384,1024]{1,0:T(8,128)(2,1)} collective-permute-done((bf16[384,1024]{1,0:T(8,128)(2,1)}, bf16[384,1024]{1,0:T(8,128)(2,1)}, u32[]{:S(2)}, u32[]{:S(2)}) %collective-permute-start.32) | collective-permute-done | bytes 786464 | tf_op jit(solution)/shard_map/ppermute | solution.py:968
  135.2 5.5 %masked.1.cot = bf16[4,512,768]{2,1,0:T(8,128)(2,1)} custom-call(s32[7]{0:T(128)} %concatenate.54.sc, bf16[2,8,2,64,768]{4,3,2,1,0:T(8,128)(2,1)} %bitcast.114, bf16[2,8,64,768]{3,2,1,0:T(8,128)(2,1)} %copy-done.68), custom_call_target="tpu_custom_call" | custom-call | bytes 6291456 | tf_op jit(solution)/shard_map/masked/pallas_call | solution.py:299
  140.8 11.7 %collective-permute-done.38.refs_11_ = bf16[384,1024]{1,0:T(8,128)(2,1)} collective-permute-done((bf16[384,1024]{1,0:T(8,128)(2,1)}, bf16[384,1024]{1,0:T(8,128)(2,1)}, u32[]{:S(2)}, u32[]{:S(2)}) %collective-permute-start.38) | collective-permute-done | bytes 786464 | tf_op jit(solution)/shard_map/ppermute | solution.py:968
  157.1 13.2 %mix.2 = (bf16[12,512,256]{2,1,0:T(8,128)(2,1)}, f32[12,512,256]{2,1,0:T(8,128)}, bf16[12,512,1024]{2,1,0:T(8,128)(2,1)}, bf16[12,512,256]{2,1,0:T(8,128)(2,1)}) custom-call(s32[7]{0:T(128)} %concatenate.54.sc, bf16[384,1024]{1,0:T(8,128)(2,1)} %bitcast.120, bf16[384,1024]{1,0:T(8,128)(2,1)} %collective-permute-done.24.refs_1_, ...), custom_call_target="tpu_custom_call" | custom-call | flops 3221225472 | bytes 20447232 | tf_op jit(solution)/shard_map/mix/pallas_call | solution.py:191
  170.3 5.0 %collective-permute-done.41.refs_3_ = bf16[384,1024]{1,0:T(8,128)(2,1)} collective-permute-done((bf16[384,1024]{1,0:T(8,128)(2,1)}, bf16[384,1024]{1,0:T(8,128)(2,1)}, u32[]{:S(2)}, u32[]{:S(2)}) %collective-permute-start.41) | collective-permute-done | bytes 786464 | tf_op jit(solution)/shard_map/ppermute | solution.py:972
  176.5 8.5 %mix.3 = (bf16[12,512,256]{2,1,0:T(8,128)(2,1)}, f32[12,512,256]{2,1,0:T(8,128)}, bf16[12,512,1024]{2,1,0:T(8,128)(2,1)}, bf16[12,512,256]{2,1,0:T(8,128)(2,1)}) custom-call(s32[7]{0:T(128)} %concatenate.54.sc, bf16[384,1024]{1,0:T(8,128)(2,1)} %copy-done.72, ...), custom_call_target="tpu_custom_call", output_to_operand_aliasing={{0}: (7, {}), {1}: (8, {}), {2}: (9, {}), {3}: (10, {})} | custom-call | flops 3221225472 | bytes 20447232 | tf_op jit(solution)/shard_map/mix/pallas_call | solution.py:191
  185.0 10.6 %pre.1 = (bf16[4,512,768]{2,1,0:T(8,128)(2,1)}, bf16[4,512,768]{2,1,0:T(8,128)(2,1)}, bf16[4,512,768]{2,1,0:T(8,128)(2,1)}) custom-call(s32[7]{0:T(128)} %concatenate.54.sc, bf16[2,8,2,64,768]{4,3,2,1,0:T(8,128)(2,1)} %bitcast.106, bf16[2,8,64,768]{3,2,1,0:T(8,128)(2,1)} %copy-done.67, bf16[12,512,256]{2,1,0:T(8,128)(2,1)} %get-tuple-element.491.heads, ...), custom_call_target="tpu_custom_call" | custom-call | flops 2415919104 | bytes 25165824 | tf_op jit(solution)/shard_map/pre/pallas_call | solution.py:270
  195.6 30.3 %units.1 = (bf16[2048,3072]{1,0:T(8,128)(2,1)}, bf16[2048,3072]{1,0:T(8,128)(2,1)}) custom-call(s32[7]{0:T(128)} %concatenate.54.sc, bf16[2048,768]{1,0:T(8,128)(2,1)} %bitcast.141, bf16[2048,768]{1,0:T(8,128)(2,1)} %bitcast.123, bf16[768,1536]{1,0:T(8,128)(2,1)} %get-tuple-element.497.up_own, bf16[768,1536]{1,0:T(8,128)(2,1)} %collective-permute-done.42.up_far, ...), custom_call_target="tpu_custom_call" | custom-call | flops 19327352832 | bytes 34603008 | tf_op jit(solution)/shard_map/units/pallas_call | solution.py:365
  225.8 28.1 %post.1 = (bf16[2,512,768]{2,1,0:T(8,128)(2,1)}, bf16[2,512,768]{2,1,0:T(8,128)(2,1)}, bf16[12,512,256]{2,1,0:T(8,128)(2,1)}, f32[1,768]{1,0:T(1,128)}) custom-call(s32[7]{0:T(128)} %concatenate.54.sc, bf16[4,512,768]{2,1,0:T(8,128)(2,1)} %get-tuple-element.494.resid, bf16[4,512,3072]{2,1,0:T(8,128)(2,1)} %bitcast.144, bf16[4,512,3072]{2,1,0:T(8,128)(2,1)} %bitcast.145, ...), custom_call_target="tpu_custom_call" | custom-call | flops 12079595520 | bytes 37748736 | tf_op jit(solution)/shard_map/post/pallas_call | solution.py:569
  254.0 9.9 %unmix.2 = (bf16[384,1024]{1,0:T(8,128)(2,1)}, bf16[384,1024]{1,0:T(8,128)(2,1)}, bf16[384,1024]{1,0:T(8,128)(2,1)}, bf16[384,1024]{1,0:T(8,128)(2,1)}, bf16[12,...) custom-call(s32[7]{0:T(128)} %concatenate.54.sc, bf16[12,1024,128]{2,1,0:T(8,128)(2,1)} %values.1.refs_12_.refs_4_.v_own, ...), custom_call_target="tpu_custom_call" | custom-call | flops 4831838208 | bytes 33030144 | tf_op jit(solution)/shard_map/unmix/pallas_call | solution.py:665
  269.2 19.6 %unmix.3 = (bf16[384,1024]{1,0:T(8,128)(2,1)}, bf16[384,1024]{1,0:T(8,128)(2,1)}, bf16[384,1024]{1,0:T(8,128)(2,1)}, bf16[384,1024]{1,0:T(8,128)(2,1)}, bf16[384...) custom-call(s32[7]{0:T(128)} %concatenate.54.sc, ...), custom_call_target="tpu_custom_call", output_to_operand_aliasing={{12}: (7, {}), {13}: (8, {})} | custom-call | flops 4831838208 | bytes 33030144 | tf_op jit(solution)/shard_map/unmix/pallas_call | solution.py:665
  295.0 16.3 %up_grad.1 = (bf16[768,1536]{1,0:T(8,128)(2,1)}, bf16[768,1536]{1,0:T(8,128)(2,1)}) custom-call(s32[7]{0:T(128)} %concatenate.54.sc, bf16[2048,768]{1,0:T(8,128)(2,1)} %bitcast.142, bf16[2048,3072]{1,0:T(8,128)(2,1)} %get-tuple-element.499.up_grad), custom_call_target="tpu_custom_call" | custom-call | flops 9663676416 | bytes 15728640 | tf_op jit(solution)/shard_map/up_grad/pallas_call | solution.py:428
  319.7 15.7 %down_grad.1 = (bf16[3072,384]{1,0:T(8,128)(2,1)}, bf16[3072,384]{1,0:T(8,128)(2,1)}) custom-call(s32[7]{0:T(128)} %concatenate.54.sc, bf16[2048,3072]{1,0:T(8,128)(2,1)} %get-tuple-element.567.active, bf16[2048,768]{1,0:T(8,128)(2,1)} %bitcast.124), custom_call_target="tpu_custom_call" | custom-call | flops 9663676416 | bytes 15728640 | tf_op jit(solution)/shard_map/down_grad/pallas_call | solution.py:397
  345.6 5.3 %out_grad.1 = (bf16[768,384]{1,0:T(8,128)(2,1)S(1)}, bf16[768,384]{1,0:T(8,128)(2,1)S(1)}) custom-call(s32[7]{0:T(128)S(1)} %copy-done.37, bf16[4,512,768]{2,1,0:T(8,128)(2,1)S(1)} %copy-done.40, bf16[2,512,768]{2,1,0:T(8,128)(2,1)S(1)} %copy-done.61, bf16[2,512,768]{2,1,0:T(8,128)(2,1)S(1)} %copy-done.45), custom_call_target="tpu_custom_call" | custom-call | flops 2415919104 | bytes 6291456 | tf_op jit(solution)/shard_map/out_grad/pallas_call | solution.py:468
  367.7 15.7 %out.3 = (bf16[2,512,768]{2,1,0:T(8,128)(2,1)S(1)}, bf16[2,512,768]{2,1,0:T(8,128)(2,1)}) custom-call(s32[7]{0:T(128)S(1)} %copy-done.37, bf16[4,512,3072]{2,1,0:T(8,128)(2,1)} %bitcast.143, bf16[4,512,768]{2,1,0:T(8,128)(2,1)S(1)} %copy-done.39, bf16[3072,384]{1,0:T(8,128)(2,1)S(1)} %copy-done.42, bf16[3072,384]{1,0:T(8,128)(2,1)} %collective-permute-done.43.dn_far), custom_call_target="tpu_custom_call" | custom-call | flops 9663676416 | bytes 23592960 | tf_op jit(solution)/shard_map/out/pallas_call | solution.py:502
  387.3 12.4 %close.1 = (f32[2,8,2,64,768]{4,3,2,1,0:T(8,128)}, bf16[2,768,384]{2,1,0:T(8,128)(2,1)S(1)}, f32[1,768]{1,0:T(1,128)S(1)}) custom-call(s32[7]{0:T(128)S(1)} %copy-done.37, bf16[2,8,2,64,768]{4,3,2,1,0:T(8,128)(2,1)S(1)} %bitcast.107, bf16[2,8,64,768]{3,2,1,0:T(8,128)(2,1)S(1)} %bitcast.113, bf16[2,8,64,768]{3,2,1,0:T(8,128)(2,1)S(1)} %bitcast.112, ...), custom_call_target="tpu_custom_call" | custom-call | flops 4831838208 | bytes 29884416 | tf_op jit(solution)/shard_map/close/pallas_call | solution.py:755
  427.8 7.6 %collective-permute-done.75 = bf16[4,2,64,384]{3,2,1,0:T(8,128)(2,1)S(1)} collective-permute-done((bf16[4,2,64,384]{3,2,1,0:T(8,128)(2,1)S(1)}, bf16[4,2,64,384]{3,2,1,0:T(8,128)(2,1)S(1)}, u32[]{:S(2)}, u32[]{:S(2)}) %collective-permute-start.75) | collective-permute-done | bytes 393248 | tf_op jit(solution)/shard_map/ppermute | solution.py:968
  435.6 5.1 %collective-permute-done.73 = bf16[432,384]{1,0:T(8,128)(2,1)S(1)} collective-permute-done((bf16[432,384]{1,0:T(8,128)(2,1)S(1)}, bf16[432,384]{1,0:T(8,128)(2,1)S(1)}, u32[]{:S(2)}, u32[]{:S(2)}) %collective-permute-start.73) | collective-permute-done | bytes 331808 | tf_op jit(solution)/shard_map/ppermute | solution.py:968
  (430 shorter events, 190.3 us)
Async XLA Ops:
  110.1 23.3 %collective-permute-start.35 = (bf16[12,1024,128]{2,1,0:T(8,128)(2,1)}, bf16[12,1024,128]{2,1,0:T(8,128)(2,1)}, u32[]{:S(2)}, u32[]{:S(2)}) collective-permute-start(bf16[12,1024,128]{2,1,0:T(8,128)(2,1)} %values.1.refs_12_.refs_4_.v_own), channel_id=1, source_target_pairs={{0,1},{1,0},{2,3},{3,2},{4,5},{5,4},{6,7},{7,6},{8,9},{9,8},{10,11... | collective-permute-start | bytes 9437192 | tf_op jit(solution)/shard_map/ppermute | solution.py:968
  110.1 20.3 %collective-permute-start.32 = (bf16[384,1024]{1,0:T(8,128)(2,1)}, bf16[384,1024]{1,0:T(8,128)(2,1)}, u32[]{:S(2)}, u32[]{:S(2)}) collective-permute-start(bf16[384,1024]{1,0:T(8,128)(2,1)} %collective-permute-done.26.refs_4_), channel_id=1, source_target_pairs={{0,4},{1,5},{2,6},{3,7},{4,0},{5,1},{6,2},{7,3},{8,12},{9,13},{10,... | collective-permute-start | bytes 2359304 | tf_op jit(solution)/shard_map/ppermute | solution.py:968
  111.1 21.4 %collective-permute-start.34 = (bf16[384,1024]{1,0:T(8,128)(2,1)S(1)}, bf16[384,1024]{1,0:T(8,128)(2,1)S(1)}, u32[]{:S(2)}, u32[]{:S(2)}) collective-permute-start(bf16[384,1024]{1,0:T(8,128)(2,1)S(1)} %collective-permute-done.30.refs_8_), channel_id=1, source_target_pairs={{0,8},{1,9},{2,10},{3,11},{4,12},{5,13},{6,14},{7,15},{8,16},{9,17... | collective-permute-start | bytes 2359304 | tf_op jit(solution)/shard_map/ppermute | solution.py:972
  134.5 20.6 %collective-permute-start.37 = (bf16[384,1024]{1,0:T(8,128)(2,1)}, bf16[384,1024]{1,0:T(8,128)(2,1)}, u32[]{:S(2)}, u32[]{:S(2)}) collective-permute-start(bf16[384,1024]{1,0:T(8,128)(2,1)} %collective-permute-done.32.refs_6_), channel_id=1, source_target_pairs={{0,8},{1,9},{2,10},{3,11},{4,12},{5,13},{6,14},{7,15},{8,16},{9,17... | collective-permute-start | bytes 2359304 | tf_op jit(solution)/shard_map/ppermute | solution.py:972
  134.7 20.5 %collective-permute-start.36 = (bf16[384,1024]{1,0:T(8,128)(2,1)}, bf16[384,1024]{1,0:T(8,128)(2,1)}, u32[]{:S(2)}, u32[]{:S(2)}) collective-permute-start(bf16[384,1024]{1,0:T(8,128)(2,1)} %collective-permute-done.32.refs_6_), channel_id=1, source_target_pairs={{0,2},{1,3},{2,0},{3,1},{4,6},{5,7},{6,4},{7,5},{8,10},{9,11},{10,... | collective-permute-start | bytes 2359304 | tf_op jit(solution)/shard_map/ppermute | solution.py:968
  155.2 20.1 %collective-permute-start.41 = (bf16[384,1024]{1,0:T(8,128)(2,1)}, bf16[384,1024]{1,0:T(8,128)(2,1)}, u32[]{:S(2)}, u32[]{:S(2)}) collective-permute-start(bf16[384,1024]{1,0:T(8,128)(2,1)} %collective-permute-done.38.refs_11_), channel_id=1, source_target_pairs={{0,8},{1,9},{2,10},{3,11},{4,12},{5,13},{6,14},{7,15},{8,16},{9,17... | collective-permute-start | bytes 2359304 | tf_op jit(solution)/shard_map/ppermute | solution.py:972
  155.6 19.7 %collective-permute-start.40 = (bf16[384,1024]{1,0:T(8,128)(2,1)}, bf16[384,1024]{1,0:T(8,128)(2,1)}, u32[]{:S(2)}, u32[]{:S(2)}) collective-permute-start(bf16[384,1024]{1,0:T(8,128)(2,1)} %copy-done.72), channel_id=1, source_target_pairs={{0,4},{1,5},{2,6},{3,7},{4,0},{5,1},{6,2},{7,3},{8,12},{9,13},{10,... | collective-permute-start | bytes 2359304 | tf_op jit(solution)/shard_map/ppermute | solution.py:968
  175.3 20.2 %collective-permute-start.42 = (bf16[768,1536]{1,0:T(8,128)(2,1)}, bf16[768,1536]{1,0:T(8,128)(2,1)}, u32[]{:S(2)}, u32[]{:S(2)}) collective-permute-start(bf16[768,1536]{1,0:T(8,128)(2,1)} %get-tuple-element.497.up_own), channel_id=1, source_target_pairs={{0,1},{1,0},{2,3},{3,2},{4,5},{5,4},{6,7},{7,6},{8,9},{9,8},{10,11... | collective-permute-start | bytes 7077896 | tf_op jit(solution)/shard_map/ppermute | solution.py:968
  175.3 20.2 %collective-permute-start.43 = (bf16[3072,384]{1,0:T(8,128)(2,1)S(1)}, bf16[3072,384]{1,0:T(8,128)(2,1)}, u32[]{:S(2)}, u32[]{:S(2)}) collective-permute-start(bf16[3072,384]{1,0:T(8,128)(2,1)S(1)} %copy-done.41), channel_id=1, source_target_pairs={{0,1},{1,0},{2,3},{3,2},{4,5},{5,4},{6,7},{7,6},{8,9},{9,8},{10,11... | collective-permute-start | bytes 7077896 | tf_op jit(solution)/shard_map/ppermute | solution.py:968
  265.1 23.6 %collective-permute-start.45 = (bf16[384,1024]{1,0:T(8,128)(2,1)}, bf16[384,1024]{1,0:T(8,128)(2,1)S(1)}, u32[]{:S(2)}, u32[]{:S(2)}) collective-permute-start(bf16[384,1024]{1,0:T(8,128)(2,1)} %get-tuple-element.512), channel_id=1, source_target_pairs={{0,24},{1,25},{2,26},{3,27},{4,28},{5,29},{6,30},{7,31},{8,0},{9,1... | collective-permute-start | bytes 2359304 | tf_op jit(solution)/shard_map/ppermute | solution.py:972
  267.5 21.3 %collective-permute-start.46 = (bf16[384,1024]{1,0:T(8,128)(2,1)}, bf16[384,1024]{1,0:T(8,128)(2,1)S(1)}, u32[]{:S(2)}, u32[]{:S(2)}) collective-permute-start(bf16[384,1024]{1,0:T(8,128)(2,1)} %get-tuple-element.513), channel_id=1, source_target_pairs={{0,2},{1,3},{2,0},{3,1},{4,6},{5,7},{6,4},{7,5},{8,10},{9,11},{10,... | collective-permute-start | bytes 2359304 | tf_op jit(solution)/shard_map/ppermute | solution.py:968
  268.1 20.7 %collective-permute-start.47 = (bf16[384,1024]{1,0:T(8,128)(2,1)}, bf16[384,1024]{1,0:T(8,128)(2,1)}, u32[]{:S(2)}, u32[]{:S(2)}) collective-permute-start(bf16[384,1024]{1,0:T(8,128)(2,1)} %get-tuple-element.514), channel_id=1, source_target_pairs={{0,4},{1,5},{2,6},{3,7},{4,0},{5,1},{6,2},{7,3},{8,12},{9,13},{10,... | collective-permute-start | bytes 2359304 | tf_op jit(solution)/shard_map/ppermute | solution.py:968
  288.8 24.9 %collective-permute-start.51 = (bf16[12,1024,128]{2,1,0:T(8,128)(2,1)}, bf16[12,1024,128]{2,1,0:T(8,128)(2,1)}, u32[]{:S(2)}, u32[]{:S(2)}) collective-permute-start(bf16[12,1024,128]{2,1,0:T(8,128)(2,1)} %get-tuple-element.551), channel_id=1, source_target_pairs={{0,1},{1,0},{2,3},{3,2},{4,5},{5,4},{6,7},{7,6},{8,9},{9,8},{10,11... | collective-permute-start | bytes 9437192 | tf_op jit(solution)/shard_map/ppermute | solution.py:968
  288.9 22.4 %collective-permute-start.48 = (bf16[384,1024]{1,0:T(8,128)(2,1)}, bf16[384,1024]{1,0:T(8,128)(2,1)S(1)}, u32[]{:S(2)}, u32[]{:S(2)}) collective-permute-start(bf16[384,1024]{1,0:T(8,128)(2,1)} %get-tuple-element.546), channel_id=1, source_target_pairs={{0,24},{1,25},{2,26},{3,27},{4,28},{5,29},{6,30},{7,31},{8,0},{9,1... | collective-permute-start | bytes 2359304 | tf_op jit(solution)/shard_map/ppermute | solution.py:972
  289.5 22.6 %collective-permute-start.49 = (bf16[384,1024]{1,0:T(8,128)(2,1)}, bf16[384,1024]{1,0:T(8,128)(2,1)S(1)}, u32[]{:S(2)}, u32[]{:S(2)}) collective-permute-start(bf16[384,1024]{1,0:T(8,128)(2,1)} %get-tuple-element.547), channel_id=1, source_target_pairs={{0,2},{1,3},{2,0},{3,1},{4,6},{5,7},{6,4},{7,5},{8,10},{9,11},{10,... | collective-permute-start | bytes 2359304 | tf_op jit(solution)/shard_map/ppermute | solution.py:968
  294.1 19.5 %collective-permute-start.50 = (bf16[384,1024]{1,0:T(8,128)(2,1)S(1)}, bf16[384,1024]{1,0:T(8,128)(2,1)S(1)}, u32[]{:S(2)}, u32[]{:S(2)}) collective-permute-start(bf16[384,1024]{1,0:T(8,128)(2,1)S(1)} %get-tuple-element.548), channel_id=1, source_target_pairs={{0,4},{1,5},{2,6},{3,7},{4,0},{5,1},{6,2},{7,3},{8,12},{9,13},{10,... | collective-permute-start | bytes 2359304 | tf_op jit(solution)/shard_map/ppermute | solution.py:968
  313.6 24.5 %collective-permute-start.55 = (bf16[768,1536]{1,0:T(8,128)(2,1)}, bf16[768,1536]{1,0:T(8,128)(2,1)S(1)}, u32[]{:S(2)}, u32[]{:S(2)}) collective-permute-start(bf16[768,1536]{1,0:T(8,128)(2,1)} %get-tuple-element.570), channel_id=1, source_target_pairs={{0,1},{1,0},{2,3},{3,2},{4,5},{5,4},{6,7},{7,6},{8,9},{9,8},{10,11... | collective-permute-start | bytes 7077896 | tf_op jit(solution)/shard_map/ppermute | solution.py:968
  313.6 21.8 %collective-permute-start.52 = (bf16[384,1024]{1,0:T(8,128)(2,1)S(1)}, bf16[384,1024]{1,0:T(8,128)(2,1)S(1)}, u32[]{:S(2)}, u32[]{:S(2)}) collective-permute-start(bf16[384,1024]{1,0:T(8,128)(2,1)S(1)} %copy-done.47), channel_id=1, source_target_pairs={{0,24},{1,25},{2,26},{3,27},{4,28},{5,29},{6,30},{7,31},{8,0},{9,1... | collective-permute-start | bytes 2359304 | tf_op jit(solution)/shard_map/ppermute | solution.py:972
  317.5 20.1 %collective-permute-start.53 = (bf16[384,1024]{1,0:T(8,128)(2,1)}, bf16[384,1024]{1,0:T(8,128)(2,1)S(1)}, u32[]{:S(2)}, u32[]{:S(2)}) collective-permute-start(bf16[384,1024]{1,0:T(8,128)(2,1)} %get-tuple-element.565), channel_id=1, source_target_pairs={{0,2},{1,3},{2,0},{3,1},{4,6},{5,7},{6,4},{7,5},{8,10},{9,11},{10,... | collective-permute-start | bytes 2359304 | tf_op jit(solution)/shard_map/ppermute | solution.py:968
  318.6 19.6 %collective-permute-start.54 = (bf16[384,1024]{1,0:T(8,128)(2,1)}, bf16[384,1024]{1,0:T(8,128)(2,1)S(1)}, u32[]{:S(2)}, u32[]{:S(2)}) collective-permute-start(bf16[384,1024]{1,0:T(8,128)(2,1)} %get-tuple-element.566), channel_id=1, source_target_pairs={{0,4},{1,5},{2,6},{3,7},{4,0},{5,1},{6,2},{7,3},{8,12},{9,13},{10,... | collective-permute-start | bytes 2359304 | tf_op jit(solution)/shard_map/ppermute | solution.py:968
  338.2 21.8 %collective-permute-start.57 = (bf16[384,1024]{1,0:T(8,128)(2,1)}, bf16[384,1024]{1,0:T(8,128)(2,1)S(1)}, u32[]{:S(2)}, u32[]{:S(2)}) collective-permute-start(bf16[384,1024]{1,0:T(8,128)(2,1)} %get-tuple-element.581), channel_id=1, source_target_pairs={{0,2},{1,3},{2,0},{3,1},{4,6},{5,7},{6,4},{7,5},{8,10},{9,11},{10,... | collective-permute-start | bytes 2359304 | tf_op jit(solution)/shard_map/ppermute | solution.py:968
  339.3 20.7 %collective-permute-start.58 = (bf16[384,1024]{1,0:T(8,128)(2,1)}, bf16[384,1024]{1,0:T(8,128)(2,1)S(1)}, u32[]{:S(2)}, u32[]{:S(2)}) collective-permute-start(bf16[384,1024]{1,0:T(8,128)(2,1)} %get-tuple-element.582), channel_id=1, source_target_pairs={{0,4},{1,5},{2,6},{3,7},{4,0},{5,1},{6,2},{7,3},{8,12},{9,13},{10,... | collective-permute-start | bytes 2359304 | tf_op jit(solution)/shard_map/ppermute | solution.py:968
  360.1 23.2 %collective-permute-start.63 = (bf16[384,1024]{1,0:T(8,128)(2,1)S(1)}, bf16[384,1024]{1,0:T(8,128)(2,1)S(1)}, u32[]{:S(2)}, u32[]{:S(2)}) collective-permute-start(bf16[384,1024]{1,0:T(8,128)(2,1)S(1)} %copy-done.96), channel_id=1, source_target_pairs={{0,4},{1,5},{2,6},{3,7},{4,0},{5,1},{6,2},{7,3},{8,12},{9,13},{10,... | collective-permute-start | bytes 2359304 | tf_op jit(solution)/shard_map/ppermute | solution.py:968
  361.8 21.6 %collective-permute-start.61 = (bf16[384,1024]{1,0:T(8,128)(2,1)S(1)}, bf16[384,1024]{1,0:T(8,128)(2,1)S(1)}, u32[]{:S(2)}, u32[]{:S(2)}) collective-permute-start(bf16[384,1024]{1,0:T(8,128)(2,1)S(1)} %get-tuple-element.613), channel_id=1, source_target_pairs={{0,24},{1,25},{2,26},{3,27},{4,28},{5,29},{6,30},{7,31},{8,0},{9,1... | collective-permute-start | bytes 2359304 | tf_op jit(solution)/shard_map/ppermute | solution.py:972
  (162 other events, 1826.7 us)

commit v20 on v19

--- a/solution.py
+++ b/solution.py
@@ -927,7 +927,7 @@
             num_scalar_prefetch=1,
             grid=(PLANES,),
             in_specs=[rows(x, rel) for rel in range(4) for x in sides],
-            out_specs=[held((PACK_VALUE, SIDE))] * 16,
+            out_specs=[pl.BlockSpec(memory_space=pltpu.VMEM)] * 16,
         ),
         out_shape=[jax.ShapeDtypeStruct((PACK_VALUE, SIDE), BF16)] * 16,
         compiler_params=params(LESS),

time: 480 us -> 480 us (level)
  no operation moved by 1% of the time
where the time goes in v20:
time: 480 us; the launch traced here: 474 us
  Pallas kernels  220 us (46%)
  waiting for transfers between devices  127 us (26%)
  starting transfers between devices  78.5 us (16%)
  local copies, waits for them, and re-layouts  34.5 us (7%)
  other arithmetic  11.2 us (2%)
    ppermute x66, waiting for transfers between devices, swap(): return lax.ppermute(x, BOTH, [(d, d ^ bit) for d in range(DEVICES)])  81.8 us
    ppermute x66, starting transfers between devices, swap(): return lax.ppermute(x, BOTH, [(d, d ^ bit) for d in range(DEVICES)])  48.9 us
    ppermute x23, waiting for transfers between devices, ring(): lax.ppermute(x, BOTH, [(d, (d + 8 * way) % DEVICES) for d in range(DEVICE...  45.4 us
    pallas_call x1, Pallas kernels, run_units(): pl.pallas_call(units_kernel, grid_spec=pltpu.PrefetchScalarGridSpec(num_s...  30.3 us
    ppermute x23, starting transfers between devices, ring(): lax.ppermute(x, BOTH, [(d, (d + 8 * way) % DEVICES) for d in range(DEVICE...  29.7 us
    pallas_call x2, Pallas kernels, run_unmix(): pl.pallas_call(partial(unmix_kernel, count, bool(carry)), grid_spec=pltpu...  29.5 us
    pallas_call x1, Pallas kernels, run_post(): pl.pallas_call(post_kernel, grid_spec=pltpu.PrefetchScalarGridSpec(num_sc...  28.1 us
    unnamed x196, local copies, waits for them, and re-layouts  25 us
  transfers between devices with their start and end apart: 89, of which 39 were waited for; matrix products, arithmetic and copies ran while one was open for 3% of the time, Pallas kernels for 34%

profile of v20, /device:TPU:0, one launch (start us, length us, event | category | flops | bytes accessed | tf_op | source)
XLA Modules:
  0.0 473.6 jit_solution(9209796580949369310)
XLA Ops:
  16.6 8.3 %collective-permute-done.7.refs_4_ = bf16[496,384]{1,0:T(8,128)(2,1)S(1)} collective-permute-done((bf16[496,384]{1,0:T(8,128)(2,1)}, bf16[496,384]{1,0:T(8,128)(2,1)S(1)}, u32[]{:S(2)}, u32[]{:S(2)}) %collective-permute-start.7) | collective-permute-done | bytes 380960 | tf_op jit(solution)/shard_map/ppermute | solution.py:972
  31.6 7.5 %collective-permute-done.9.refs_3_ = bf16[496,384]{1,0:T(8,128)(2,1)S(1)} collective-permute-done((bf16[496,384]{1,0:T(8,128)(2,1)}, bf16[496,384]{1,0:T(8,128)(2,1)S(1)}, u32[]{:S(2)}, u32[]{:S(2)}) %collective-permute-start.9) | collective-permute-done | bytes 380960 | tf_op jit(solution)/shard_map/ppermute | solution.py:968
  45.1 6.2 %collective-permute-done.13.refs_6_ = bf16[496,384]{1,0:T(8,128)(2,1)S(1)} collective-permute-done((bf16[496,384]{1,0:T(8,128)(2,1)S(1)}, bf16[496,384]{1,0:T(8,128)(2,1)S(1)}, u32[]{:S(2)}, u32[]{:S(2)}) %collective-permute-start.13) | collective-permute-done | bytes 380960 | tf_op jit(solution)/shard_map/ppermute | solution.py:968
  67.4 7.1 %collective-permute-done.23.refs_15_ = bf16[496,384]{1,0:T(8,128)(2,1)S(1)} collective-permute-done((bf16[496,384]{1,0:T(8,128)(2,1)S(1)}, bf16[496,384]{1,0:T(8,128)(2,1)S(1)}, u32[]{:S(2)}, u32[]{:S(2)}) %collective-permute-start.23) | collective-permute-done | bytes 380960 | tf_op jit(solution)/shard_map/ppermute | solution.py:972
  77.8 7.2 %place.1 = (bf16[3072,384]{1,0:T(8,128)(2,1)}, bf16[768,1536]{1,0:T(8,128)(2,1)}, bf16[768,384]{1,0:T(8,128)(2,1)}, bf16[768,384]{1,0:T(8,128)(2,1)}, bf16[256,384]{1,0:T(8,128)(2,1)}) custom-call(s32[7]{0:T(128)} %concatenate.54.sc, bf16[496,384]{1,0:T(8,128)(2,1)} %pack.1.refs_0_, bf16[496,384]{1,0:T(8,128)(2,1)} %copy-done.75, ...), custom_call_target="tpu_custom_call" | custom-call | bytes 12189696 | tf_op jit(solution)/shard_map/place/pallas_call | solution.py:874
  95.6 7.8 %values.1.refs_12_.refs_4_.v_own = bf16[12,1024,128]{2,1,0:T(8,128)(2,1)} custom-call(s32[7]{0:T(128)} %concatenate.54.sc, bf16[2,1024,768]{2,1,0:T(8,128)(2,1)} %tok.1, f32[1,768]{1,0:T(1,128)} %reshape.205.gain, bf16[768,384]{1,0:T(8,128)(2,1)} %get-tuple-element.431.w_own, bf16[768,384]{1,0:T(8,128)(2,1)} %copy-done.49), custom_call_target="tpu_custom_call" | custom-call | flops 2415919104 | bytes 6291456 | tf_op jit(solution)/shard_map/values/pallas_call | solution.py:81
  113.7 16.7 %collective-permute-done.32.refs_6_ = bf16[384,1024]{1,0:T(8,128)(2,1)} collective-permute-done((bf16[384,1024]{1,0:T(8,128)(2,1)}, bf16[384,1024]{1,0:T(8,128)(2,1)}, u32[]{:S(2)}, u32[]{:S(2)}) %collective-permute-start.32) | collective-permute-done | bytes 786464 | tf_op jit(solution)/shard_map/ppermute | solution.py:968
  135.2 5.5 %masked.1.cot = bf16[4,512,768]{2,1,0:T(8,128)(2,1)} custom-call(s32[7]{0:T(128)} %concatenate.54.sc, bf16[2,8,2,64,768]{4,3,2,1,0:T(8,128)(2,1)} %bitcast.114, bf16[2,8,64,768]{3,2,1,0:T(8,128)(2,1)} %copy-done.68), custom_call_target="tpu_custom_call" | custom-call | bytes 6291456 | tf_op jit(solution)/shard_map/masked/pallas_call | solution.py:299
  140.8 11.7 %collective-permute-done.38.refs_11_ = bf16[384,1024]{1,0:T(8,128)(2,1)} collective-permute-done((bf16[384,1024]{1,0:T(8,128)(2,1)}, bf16[384,1024]{1,0:T(8,128)(2,1)}, u32[]{:S(2)}, u32[]{:S(2)}) %collective-permute-start.38) | collective-permute-done | bytes 786464 | tf_op jit(solution)/shard_map/ppermute | solution.py:968
  157.1 13.2 %mix.2 = (bf16[12,512,256]{2,1,0:T(8,128)(2,1)}, f32[12,512,256]{2,1,0:T(8,128)}, bf16[12,512,1024]{2,1,0:T(8,128)(2,1)}, bf16[12,512,256]{2,1,0:T(8,128)(2,1)}) custom-call(s32[7]{0:T(128)} %concatenate.54.sc, bf16[384,1024]{1,0:T(8,128)(2,1)} %bitcast.120, bf16[384,1024]{1,0:T(8,128)(2,1)} %collective-permute-done.24.refs_1_, ...), custom_call_target="tpu_custom_call" | custom-call | flops 3221225472 | bytes 20447232 | tf_op jit(solution)/shard_map/mix/pallas_call | solution.py:191
  170.3 5.0 %collective-permute-done.41.refs_3_ = bf16[384,1024]{1,0:T(8,128)(2,1)} collective-permute-done((bf16[384,1024]{1,0:T(8,128)(2,1)}, bf16[384,1024]{1,0:T(8,128)(2,1)}, u32[]{:S(2)}, u32[]{:S(2)}) %collective-permute-start.41) | collective-permute-done | bytes 786464 | tf_op jit(solution)/shard_map/ppermute | solution.py:972
  176.5 8.5 %mix.3 = (bf16[12,512,256]{2,1,0:T(8,128)(2,1)}, f32[12,512,256]{2,1,0:T(8,128)}, bf16[12,512,1024]{2,1,0:T(8,128)(2,1)}, bf16[12,512,256]{2,1,0:T(8,128)(2,1)}) custom-call(s32[7]{0:T(128)} %concatenate.54.sc, bf16[384,1024]{1,0:T(8,128)(2,1)} %copy-done.72, ...), custom_call_target="tpu_custom_call", output_to_operand_aliasing={{0}: (7, {}), {1}: (8, {}), {2}: (9, {}), {3}: (10, {})} | custom-call | flops 3221225472 | bytes 20447232 | tf_op jit(solution)/shard_map/mix/pallas_call | solution.py:191
  185.0 10.6 %pre.1 = (bf16[4,512,768]{2,1,0:T(8,128)(2,1)}, bf16[4,512,768]{2,1,0:T(8,128)(2,1)}, bf16[4,512,768]{2,1,0:T(8,128)(2,1)}) custom-call(s32[7]{0:T(128)} %concatenate.54.sc, bf16[2,8,2,64,768]{4,3,2,1,0:T(8,128)(2,1)} %bitcast.106, bf16[2,8,64,768]{3,2,1,0:T(8,128)(2,1)} %copy-done.67, bf16[12,512,256]{2,1,0:T(8,128)(2,1)} %get-tuple-element.491.heads, ...), custom_call_target="tpu_custom_call" | custom-call | flops 2415919104 | bytes 25165824 | tf_op jit(solution)/shard_map/pre/pallas_call | solution.py:270
  195.6 30.3 %units.1 = (bf16[2048,3072]{1,0:T(8,128)(2,1)}, bf16[2048,3072]{1,0:T(8,128)(2,1)}) custom-call(s32[7]{0:T(128)} %concatenate.54.sc, bf16[2048,768]{1,0:T(8,128)(2,1)} %bitcast.141, bf16[2048,768]{1,0:T(8,128)(2,1)} %bitcast.123, bf16[768,1536]{1,0:T(8,128)(2,1)} %get-tuple-element.497.up_own, bf16[768,1536]{1,0:T(8,128)(2,1)} %collective-permute-done.42.up_far, ...), custom_call_target="tpu_custom_call" | custom-call | flops 19327352832 | bytes 34603008 | tf_op jit(solution)/shard_map/units/pallas_call | solution.py:365
  225.8 28.1 %post.1 = (bf16[2,512,768]{2,1,0:T(8,128)(2,1)}, bf16[2,512,768]{2,1,0:T(8,128)(2,1)}, bf16[12,512,256]{2,1,0:T(8,128)(2,1)}, f32[1,768]{1,0:T(1,128)}) custom-call(s32[7]{0:T(128)} %concatenate.54.sc, bf16[4,512,768]{2,1,0:T(8,128)(2,1)} %get-tuple-element.494.resid, bf16[4,512,3072]{2,1,0:T(8,128)(2,1)} %bitcast.144, bf16[4,512,3072]{2,1,0:T(8,128)(2,1)} %bitcast.145, ...), custom_call_target="tpu_custom_call" | custom-call | flops 12079595520 | bytes 37748736 | tf_op jit(solution)/shard_map/post/pallas_call | solution.py:569
  254.0 9.9 %unmix.2 = (bf16[384,1024]{1,0:T(8,128)(2,1)}, bf16[384,1024]{1,0:T(8,128)(2,1)}, bf16[384,1024]{1,0:T(8,128)(2,1)}, bf16[384,1024]{1,0:T(8,128)(2,1)}, bf16[12,...) custom-call(s32[7]{0:T(128)} %concatenate.54.sc, bf16[12,1024,128]{2,1,0:T(8,128)(2,1)} %values.1.refs_12_.refs_4_.v_own, ...), custom_call_target="tpu_custom_call" | custom-call | flops 4831838208 | bytes 33030144 | tf_op jit(solution)/shard_map/unmix/pallas_call | solution.py:665
  269.2 19.6 %unmix.3 = (bf16[384,1024]{1,0:T(8,128)(2,1)}, bf16[384,1024]{1,0:T(8,128)(2,1)}, bf16[384,1024]{1,0:T(8,128)(2,1)}, bf16[384,1024]{1,0:T(8,128)(2,1)}, bf16[384...) custom-call(s32[7]{0:T(128)} %concatenate.54.sc, ...), custom_call_target="tpu_custom_call", output_to_operand_aliasing={{12}: (7, {}), {13}: (8, {})} | custom-call | flops 4831838208 | bytes 33030144 | tf_op jit(solution)/shard_map/unmix/pallas_call | solution.py:665
  295.0 16.3 %up_grad.1 = (bf16[768,1536]{1,0:T(8,128)(2,1)}, bf16[768,1536]{1,0:T(8,128)(2,1)}) custom-call(s32[7]{0:T(128)} %concatenate.54.sc, bf16[2048,768]{1,0:T(8,128)(2,1)} %bitcast.142, bf16[2048,3072]{1,0:T(8,128)(2,1)} %get-tuple-element.499.up_grad), custom_call_target="tpu_custom_call" | custom-call | flops 9663676416 | bytes 15728640 | tf_op jit(solution)/shard_map/up_grad/pallas_call | solution.py:428
  319.7 15.7 %down_grad.1 = (bf16[3072,384]{1,0:T(8,128)(2,1)}, bf16[3072,384]{1,0:T(8,128)(2,1)}) custom-call(s32[7]{0:T(128)} %concatenate.54.sc, bf16[2048,3072]{1,0:T(8,128)(2,1)} %get-tuple-element.567.active, bf16[2048,768]{1,0:T(8,128)(2,1)} %bitcast.124), custom_call_target="tpu_custom_call" | custom-call | flops 9663676416 | bytes 15728640 | tf_op jit(solution)/shard_map/down_grad/pallas_call | solution.py:397
  345.6 5.3 %out_grad.1 = (bf16[768,384]{1,0:T(8,128)(2,1)S(1)}, bf16[768,384]{1,0:T(8,128)(2,1)S(1)}) custom-call(s32[7]{0:T(128)S(1)} %copy-done.37, bf16[4,512,768]{2,1,0:T(8,128)(2,1)S(1)} %copy-done.40, bf16[2,512,768]{2,1,0:T(8,128)(2,1)S(1)} %copy-done.61, bf16[2,512,768]{2,1,0:T(8,128)(2,1)S(1)} %copy-done.45), custom_call_target="tpu_custom_call" | custom-call | flops 2415919104 | bytes 6291456 | tf_op jit(solution)/shard_map/out_grad/pallas_call | solution.py:468
  367.7 15.7 %out.3 = (bf16[2,512,768]{2,1,0:T(8,128)(2,1)S(1)}, bf16[2,512,768]{2,1,0:T(8,128)(2,1)}) custom-call(s32[7]{0:T(128)S(1)} %copy-done.37, bf16[4,512,3072]{2,1,0:T(8,128)(2,1)} %bitcast.143, bf16[4,512,768]{2,1,0:T(8,128)(2,1)S(1)} %copy-done.39, bf16[3072,384]{1,0:T(8,128)(2,1)S(1)} %copy-done.42, bf16[3072,384]{1,0:T(8,128)(2,1)} %collective-permute-done.43.dn_far), custom_call_target="tpu_custom_call" | custom-call | flops 9663676416 | bytes 23592960 | tf_op jit(solution)/shard_map/out/pallas_call | solution.py:502
  387.3 12.4 %close.1 = (f32[2,8,2,64,768]{4,3,2,1,0:T(8,128)}, bf16[2,768,384]{2,1,0:T(8,128)(2,1)S(1)}, f32[1,768]{1,0:T(1,128)S(1)}) custom-call(s32[7]{0:T(128)S(1)} %copy-done.37, bf16[2,8,2,64,768]{4,3,2,1,0:T(8,128)(2,1)S(1)} %bitcast.107, bf16[2,8,64,768]{3,2,1,0:T(8,128)(2,1)S(1)} %bitcast.113, bf16[2,8,64,768]{3,2,1,0:T(8,128)(2,1)S(1)} %bitcast.112, ...), custom_call_target="tpu_custom_call" | custom-call | flops 4831838208 | bytes 29884416 | tf_op jit(solution)/shard_map/close/pallas_call | solution.py:755
  427.8 7.6 %collective-permute-done.75 = bf16[4,2,64,384]{3,2,1,0:T(8,128)(2,1)S(1)} collective-permute-done((bf16[4,2,64,384]{3,2,1,0:T(8,128)(2,1)S(1)}, bf16[4,2,64,384]{3,2,1,0:T(8,128)(2,1)S(1)}, u32[]{:S(2)}, u32[]{:S(2)}) %collective-permute-start.75) | collective-permute-done | bytes 393248 | tf_op jit(solution)/shard_map/ppermute | solution.py:968
  435.6 5.1 %collective-permute-done.73 = bf16[432,384]{1,0:T(8,128)(2,1)S(1)} collective-permute-done((bf16[432,384]{1,0:T(8,128)(2,1)S(1)}, bf16[432,384]{1,0:T(8,128)(2,1)S(1)}, u32[]{:S(2)}, u32[]{:S(2)}) %collective-permute-start.73) | collective-permute-done | bytes 331808 | tf_op jit(solution)/shard_map/ppermute | solution.py:968
  (430 shorter events, 190.3 us)
Async XLA Ops:
  110.1 23.3 %collective-permute-start.35 = (bf16[12,1024,128]{2,1,0:T(8,128)(2,1)}, bf16[12,1024,128]{2,1,0:T(8,128)(2,1)}, u32[]{:S(2)}, u32[]{:S(2)}) collective-permute-start(bf16[12,1024,128]{2,1,0:T(8,128)(2,1)} %values.1.refs_12_.refs_4_.v_own), channel_id=1, source_target_pairs={{0,1},{1,0},{2,3},{3,2},{4,5},{5,4},{6,7},{7,6},{8,9},{9,8},{10,11... | collective-permute-start | bytes 9437192 | tf_op jit(solution)/shard_map/ppermute | solution.py:968
  110.1 20.3 %collective-permute-start.32 = (bf16[384,1024]{1,0:T(8,128)(2,1)}, bf16[384,1024]{1,0:T(8,128)(2,1)}, u32[]{:S(2)}, u32[]{:S(2)}) collective-permute-start(bf16[384,1024]{1,0:T(8,128)(2,1)} %collective-permute-done.26.refs_4_), channel_id=1, source_target_pairs={{0,4},{1,5},{2,6},{3,7},{4,0},{5,1},{6,2},{7,3},{8,12},{9,13},{10,... | collective-permute-start | bytes 2359304 | tf_op jit(solution)/shard_map/ppermute | solution.py:968
  111.1 21.4 %collective-permute-start.34 = (bf16[384,1024]{1,0:T(8,128)(2,1)S(1)}, bf16[384,1024]{1,0:T(8,128)(2,1)S(1)}, u32[]{:S(2)}, u32[]{:S(2)}) collective-permute-start(bf16[384,1024]{1,0:T(8,128)(2,1)S(1)} %collective-permute-done.30.refs_8_), channel_id=1, source_target_pairs={{0,8},{1,9},{2,10},{3,11},{4,12},{5,13},{6,14},{7,15},{8,16},{9,17... | collective-permute-start | bytes 2359304 | tf_op jit(solution)/shard_map/ppermute | solution.py:972
  134.5 20.6 %collective-permute-start.37 = (bf16[384,1024]{1,0:T(8,128)(2,1)}, bf16[384,1024]{1,0:T(8,128)(2,1)}, u32[]{:S(2)}, u32[]{:S(2)}) collective-permute-start(bf16[384,1024]{1,0:T(8,128)(2,1)} %collective-permute-done.32.refs_6_), channel_id=1, source_target_pairs={{0,8},{1,9},{2,10},{3,11},{4,12},{5,13},{6,14},{7,15},{8,16},{9,17... | collective-permute-start | bytes 2359304 | tf_op jit(solution)/shard_map/ppermute | solution.py:972
  134.7 20.5 %collective-permute-start.36 = (bf16[384,1024]{1,0:T(8,128)(2,1)}, bf16[384,1024]{1,0:T(8,128)(2,1)}, u32[]{:S(2)}, u32[]{:S(2)}) collective-permute-start(bf16[384,1024]{1,0:T(8,128)(2,1)} %collective-permute-done.32.refs_6_), channel_id=1, source_target_pairs={{0,2},{1,3},{2,0},{3,1},{4,6},{5,7},{6,4},{7,5},{8,10},{9,11},{10,... | collective-permute-start | bytes 2359304 | tf_op jit(solution)/shard_map/ppermute | solution.py:968
  155.2 20.1 %collective-permute-start.41 = (bf16[384,1024]{1,0:T(8,128)(2,1)}, bf16[384,1024]{1,0:T(8,128)(2,1)}, u32[]{:S(2)}, u32[]{:S(2)}) collective-permute-start(bf16[384,1024]{1,0:T(8,128)(2,1)} %collective-permute-done.38.refs_11_), channel_id=1, source_target_pairs={{0,8},{1,9},{2,10},{3,11},{4,12},{5,13},{6,14},{7,15},{8,16},{9,17... | collective-permute-start | bytes 2359304 | tf_op jit(solution)/shard_map/ppermute | solution.py:972
  155.6 19.7 %collective-permute-start.40 = (bf16[384,1024]{1,0:T(8,128)(2,1)}, bf16[384,1024]{1,0:T(8,128)(2,1)}, u32[]{:S(2)}, u32[]{:S(2)}) collective-permute-start(bf16[384,1024]{1,0:T(8,128)(2,1)} %copy-done.72), channel_id=1, source_target_pairs={{0,4},{1,5},{2,6},{3,7},{4,0},{5,1},{6,2},{7,3},{8,12},{9,13},{10,... | collective-permute-start | bytes 2359304 | tf_op jit(solution)/shard_map/ppermute | solution.py:968
  175.3 20.2 %collective-permute-start.42 = (bf16[768,1536]{1,0:T(8,128)(2,1)}, bf16[768,1536]{1,0:T(8,128)(2,1)}, u32[]{:S(2)}, u32[]{:S(2)}) collective-permute-start(bf16[768,1536]{1,0:T(8,128)(2,1)} %get-tuple-element.497.up_own), channel_id=1, source_target_pairs={{0,1},{1,0},{2,3},{3,2},{4,5},{5,4},{6,7},{7,6},{8,9},{9,8},{10,11... | collective-permute-start | bytes 7077896 | tf_op jit(solution)/shard_map/ppermute | solution.py:968
  175.3 20.2 %collective-permute-start.43 = (bf16[3072,384]{1,0:T(8,128)(2,1)S(1)}, bf16[3072,384]{1,0:T(8,128)(2,1)}, u32[]{:S(2)}, u32[]{:S(2)}) collective-permute-start(bf16[3072,384]{1,0:T(8,128)(2,1)S(1)} %copy-done.41), channel_id=1, source_target_pairs={{0,1},{1,0},{2,3},{3,2},{4,5},{5,4},{6,7},{7,6},{8,9},{9,8},{10,11... | collective-permute-start | bytes 7077896 | tf_op jit(solution)/shard_map/ppermute | solution.py:968
  265.1 23.6 %collective-permute-start.45 = (bf16[384,1024]{1,0:T(8,128)(2,1)}, bf16[384,1024]{1,0:T(8,128)(2,1)S(1)}, u32[]{:S(2)}, u32[]{:S(2)}) collective-permute-start(bf16[384,1024]{1,0:T(8,128)(2,1)} %get-tuple-element.512), channel_id=1, source_target_pairs={{0,24},{1,25},{2,26},{3,27},{4,28},{5,29},{6,30},{7,31},{8,0},{9,1... | collective-permute-start | bytes 2359304 | tf_op jit(solution)/shard_map/ppermute | solution.py:972
  267.5 21.3 %collective-permute-start.46 = (bf16[384,1024]{1,0:T(8,128)(2,1)}, bf16[384,1024]{1,0:T(8,128)(2,1)S(1)}, u32[]{:S(2)}, u32[]{:S(2)}) collective-permute-start(bf16[384,1024]{1,0:T(8,128)(2,1)} %get-tuple-element.513), channel_id=1, source_target_pairs={{0,2},{1,3},{2,0},{3,1},{4,6},{5,7},{6,4},{7,5},{8,10},{9,11},{10,... | collective-permute-start | bytes 2359304 | tf_op jit(solution)/shard_map/ppermute | solution.py:968
  268.1 20.7 %collective-permute-start.47 = (bf16[384,1024]{1,0:T(8,128)(2,1)}, bf16[384,1024]{1,0:T(8,128)(2,1)}, u32[]{:S(2)}, u32[]{:S(2)}) collective-permute-start(bf16[384,1024]{1,0:T(8,128)(2,1)} %get-tuple-element.514), channel_id=1, source_target_pairs={{0,4},{1,5},{2,6},{3,7},{4,0},{5,1},{6,2},{7,3},{8,12},{9,13},{10,... | collective-permute-start | bytes 2359304 | tf_op jit(solution)/shard_map/ppermute | solution.py:968
  288.8 24.9 %collective-permute-start.51 = (bf16[12,1024,128]{2,1,0:T(8,128)(2,1)}, bf16[12,1024,128]{2,1,0:T(8,128)(2,1)}, u32[]{:S(2)}, u32[]{:S(2)}) collective-permute-start(bf16[12,1024,128]{2,1,0:T(8,128)(2,1)} %get-tuple-element.551), channel_id=1, source_target_pairs={{0,1},{1,0},{2,3},{3,2},{4,5},{5,4},{6,7},{7,6},{8,9},{9,8},{10,11... | collective-permute-start | bytes 9437192 | tf_op jit(solution)/shard_map/ppermute | solution.py:968
  288.9 22.4 %collective-permute-start.48 = (bf16[384,1024]{1,0:T(8,128)(2,1)}, bf16[384,1024]{1,0:T(8,128)(2,1)S(1)}, u32[]{:S(2)}, u32[]{:S(2)}) collective-permute-start(bf16[384,1024]{1,0:T(8,128)(2,1)} %get-tuple-element.546), channel_id=1, source_target_pairs={{0,24},{1,25},{2,26},{3,27},{4,28},{5,29},{6,30},{7,31},{8,0},{9,1... | collective-permute-start | bytes 2359304 | tf_op jit(solution)/shard_map/ppermute | solution.py:972
  289.5 22.6 %collective-permute-start.49 = (bf16[384,1024]{1,0:T(8,128)(2,1)}, bf16[384,1024]{1,0:T(8,128)(2,1)S(1)}, u32[]{:S(2)}, u32[]{:S(2)}) collective-permute-start(bf16[384,1024]{1,0:T(8,128)(2,1)} %get-tuple-element.547), channel_id=1, source_target_pairs={{0,2},{1,3},{2,0},{3,1},{4,6},{5,7},{6,4},{7,5},{8,10},{9,11},{10,... | collective-permute-start | bytes 2359304 | tf_op jit(solution)/shard_map/ppermute | solution.py:968
  294.1 19.5 %collective-permute-start.50 = (bf16[384,1024]{1,0:T(8,128)(2,1)S(1)}, bf16[384,1024]{1,0:T(8,128)(2,1)S(1)}, u32[]{:S(2)}, u32[]{:S(2)}) collective-permute-start(bf16[384,1024]{1,0:T(8,128)(2,1)S(1)} %get-tuple-element.548), channel_id=1, source_target_pairs={{0,4},{1,5},{2,6},{3,7},{4,0},{5,1},{6,2},{7,3},{8,12},{9,13},{10,... | collective-permute-start | bytes 2359304 | tf_op jit(solution)/shard_map/ppermute | solution.py:968
  313.6 24.5 %collective-permute-start.55 = (bf16[768,1536]{1,0:T(8,128)(2,1)}, bf16[768,1536]{1,0:T(8,128)(2,1)S(1)}, u32[]{:S(2)}, u32[]{:S(2)}) collective-permute-start(bf16[768,1536]{1,0:T(8,128)(2,1)} %get-tuple-element.570), channel_id=1, source_target_pairs={{0,1},{1,0},{2,3},{3,2},{4,5},{5,4},{6,7},{7,6},{8,9},{9,8},{10,11... | collective-permute-start | bytes 7077896 | tf_op jit(solution)/shard_map/ppermute | solution.py:968
  313.6 21.8 %collective-permute-start.52 = (bf16[384,1024]{1,0:T(8,128)(2,1)S(1)}, bf16[384,1024]{1,0:T(8,128)(2,1)S(1)}, u32[]{:S(2)}, u32[]{:S(2)}) collective-permute-start(bf16[384,1024]{1,0:T(8,128)(2,1)S(1)} %copy-done.47), channel_id=1, source_target_pairs={{0,24},{1,25},{2,26},{3,27},{4,28},{5,29},{6,30},{7,31},{8,0},{9,1... | collective-permute-start | bytes 2359304 | tf_op jit(solution)/shard_map/ppermute | solution.py:972
  317.5 20.1 %collective-permute-start.53 = (bf16[384,1024]{1,0:T(8,128)(2,1)}, bf16[384,1024]{1,0:T(8,128)(2,1)S(1)}, u32[]{:S(2)}, u32[]{:S(2)}) collective-permute-start(bf16[384,1024]{1,0:T(8,128)(2,1)} %get-tuple-element.565), channel_id=1, source_target_pairs={{0,2},{1,3},{2,0},{3,1},{4,6},{5,7},{6,4},{7,5},{8,10},{9,11},{10,... | collective-permute-start | bytes 2359304 | tf_op jit(solution)/shard_map/ppermute | solution.py:968
  318.6 19.6 %collective-permute-start.54 = (bf16[384,1024]{1,0:T(8,128)(2,1)}, bf16[384,1024]{1,0:T(8,128)(2,1)S(1)}, u32[]{:S(2)}, u32[]{:S(2)}) collective-permute-start(bf16[384,1024]{1,0:T(8,128)(2,1)} %get-tuple-element.566), channel_id=1, source_target_pairs={{0,4},{1,5},{2,6},{3,7},{4,0},{5,1},{6,2},{7,3},{8,12},{9,13},{10,... | collective-permute-start | bytes 2359304 | tf_op jit(solution)/shard_map/ppermute | solution.py:968
  338.2 21.8 %collective-permute-start.57 = (bf16[384,1024]{1,0:T(8,128)(2,1)}, bf16[384,1024]{1,0:T(8,128)(2,1)S(1)}, u32[]{:S(2)}, u32[]{:S(2)}) collective-permute-start(bf16[384,1024]{1,0:T(8,128)(2,1)} %get-tuple-element.581), channel_id=1, source_target_pairs={{0,2},{1,3},{2,0},{3,1},{4,6},{5,7},{6,4},{7,5},{8,10},{9,11},{10,... | collective-permute-start | bytes 2359304 | tf_op jit(solution)/shard_map/ppermute | solution.py:968
  339.3 20.7 %collective-permute-start.58 = (bf16[384,1024]{1,0:T(8,128)(2,1)}, bf16[384,1024]{1,0:T(8,128)(2,1)S(1)}, u32[]{:S(2)}, u32[]{:S(2)}) collective-permute-start(bf16[384,1024]{1,0:T(8,128)(2,1)} %get-tuple-element.582), channel_id=1, source_target_pairs={{0,4},{1,5},{2,6},{3,7},{4,0},{5,1},{6,2},{7,3},{8,12},{9,13},{10,... | collective-permute-start | bytes 2359304 | tf_op jit(solution)/shard_map/ppermute | solution.py:968
  360.1 23.2 %collective-permute-start.63 = (bf16[384,1024]{1,0:T(8,128)(2,1)S(1)}, bf16[384,1024]{1,0:T(8,128)(2,1)S(1)}, u32[]{:S(2)}, u32[]{:S(2)}) collective-permute-start(bf16[384,1024]{1,0:T(8,128)(2,1)S(1)} %copy-done.96), channel_id=1, source_target_pairs={{0,4},{1,5},{2,6},{3,7},{4,0},{5,1},{6,2},{7,3},{8,12},{9,13},{10,... | collective-permute-start | bytes 2359304 | tf_op jit(solution)/shard_map/ppermute | solution.py:968
  361.8 21.6 %collective-permute-start.61 = (bf16[384,1024]{1,0:T(8,128)(2,1)S(1)}, bf16[384,1024]{1,0:T(8,128)(2,1)S(1)}, u32[]{:S(2)}, u32[]{:S(2)}) collective-permute-start(bf16[384,1024]{1,0:T(8,128)(2,1)S(1)} %get-tuple-element.613), channel_id=1, source_target_pairs={{0,24},{1,25},{2,26},{3,27},{4,28},{5,29},{6,30},{7,31},{8,0},{9,1... | collective-permute-start | bytes 2359304 | tf_op jit(solution)/shard_map/ppermute | solution.py:972
  (162 other events, 1826.7 us)

commit v21 on v19

--- a/solution.py
+++ b/solution.py
@@ -1113,29 +1113,28 @@
     have = scatter_add(have, got, 3)
 
     have, got = scatter_send(have, 4)
+    sums, sums_got = scatter_send(by_place(packed), 0)
     out_own, out_far = run_out(sc, active, resid, down)
-    have, got, packed, out_own, out_far = together((have, got, packed, out_own, out_far))
+    have, got, sums, sums_got, out_own, out_far = together((have, got, sums, sums_got, out_own, out_far))
     rand_sum = scatter_add(have, got, 4)[0, 0, 0].reshape(2, 3, HALF, LMAX)
 
-    sums, got = scatter_send(by_place(packed), 0)
+    sums, got = scatter_send(scatter_add(sums, sums_got, 0), 1)
     tokens_grad, d_value, d_gain_one = run_close(
         sc, tokens, res_own, res_got, back_own, back_got, gain_one, value, value_far
     )
+    sums, got, tokens_grad, d_value, d_gain_one, out_got = together(
+        (sums, got, tokens_grad, d_value, d_gain_one, other(out_far))
+    )
+    sums = scatter_add(sums, got, 1)
+
+    sums, got = scatter_send(sums, 2)
     gain_pair = jnp.concatenate([d_gain_one, d_gain_two]).reshape(2, 16, 1, 48).astype(BF16)
     gain_pair = jnp.pad(gain_pair, ((0, 0), (0, 0), (0, 15), (0, SIDE - 48)))
     small = jnp.concatenate([d_value.reshape(2, 16, 48, SIDE), gain_pair], 2)
-    sums, got, tokens_grad, small, out_got = together((sums, got, tokens_grad, small, other(out_far)))
-    sums = scatter_add(sums, got, 0)
-
-    sums, got = scatter_send(sums, 1)
     small = add_low(pick(small, core), other(pick(small, 1 - core))).reshape(4, 2, 2, 64, SIDE)
+    small = add_low(pick(small, x, 2), swap(pick(small, 1 - x, 2), TO_X))
     output = run_join(sc, out_own, out_got)
     sums, got, small, output = together((sums, got, small, output))
-    sums = scatter_add(sums, got, 1)
-
-    sums, got = scatter_send(sums, 2)
-    small = add_low(pick(small, x, 2), swap(pick(small, 1 - x, 2), TO_X))
-    sums, got, small = together((sums, got, small))
     sums = scatter_add(sums, got, 2)
 
     sums, got = scatter_send(sums, 3)

time: 480 us -> 479 us (level)
  waiting for transfers between devices: 127 us -> 135 us
    ppermute x23, waiting for transfers between devices: 45.4 us -> 50.5 us  [ring(): lax.ppermute(x, BOTH, [(d, (d + 8 * way) % DEVICES) for d in range(DEVICE...]
    unnamed x196 -> x206, local copies, waits for them, and re-layouts: 25 us -> 24.5 us
where the time goes in v21:
time: 479 us; the launch traced here: 473 us
  Pallas kernels  218 us (46%)
  waiting for transfers between devices  135 us (28%)
  starting transfers between devices  74.1 us (15%)
  local copies, waits for them, and re-layouts  34 us (7%)
  other arithmetic  10.1 us (2%)
    ppermute x66, waiting for transfers between devices, swap(): return lax.ppermute(x, BOTH, [(d, d ^ bit) for d in range(DEVICES)])  84.2 us
    ppermute x23, waiting for transfers between devices, ring(): lax.ppermute(x, BOTH, [(d, (d + 8 * way) % DEVICES) for d in range(DEVICE...  50.5 us
    ppermute x66, starting transfers between devices, swap(): return lax.ppermute(x, BOTH, [(d, d ^ bit) for d in range(DEVICES)])  47.7 us
    pallas_call x1, Pallas kernels, run_units(): pl.pallas_call(units_kernel, grid_spec=pltpu.PrefetchScalarGridSpec(num_s...  30.2 us
    pallas_call x2, Pallas kernels, run_unmix(): pl.pallas_call(partial(unmix_kernel, count, bool(carry)), grid_spec=pltpu...  29.4 us
    pallas_call x1, Pallas kernels, run_post(): pl.pallas_call(post_kernel, grid_spec=pltpu.PrefetchScalarGridSpec(num_sc...  28.1 us
    ppermute x23, starting transfers between devices, ring(): lax.ppermute(x, BOTH, [(d, (d + 8 * way) % DEVICES) for d in range(DEVICE...  26.4 us
    unnamed x206, local copies, waits for them, and re-layouts  24.5 us
  transfers between devices with their start and end apart: 89, of which 39 were waited for; matrix products, arithmetic and copies ran while one was open for 3% of the time, Pallas kernels for 34%

profile of v21, /device:TPU:0, one launch (start us, length us, event | category | flops | bytes accessed | tf_op | source)
XLA Modules:
  0.0 473.2 jit_solution(5550303184675213749)
XLA Ops:
  16.5 8.3 %collective-permute-done.7.refs_4_ = bf16[496,384]{1,0:T(8,128)(2,1)S(1)} collective-permute-done((bf16[496,384]{1,0:T(8,128)(2,1)}, bf16[496,384]{1,0:T(8,128)(2,1)S(1)}, u32[]{:S(2)}, u32[]{:S(2)}) %collective-permute-start.7) | collective-permute-done | bytes 380960 | tf_op jit(solution)/shard_map/ppermute | solution.py:972
  31.5 7.5 %collective-permute-done.9.refs_3_ = bf16[496,384]{1,0:T(8,128)(2,1)S(1)} collective-permute-done((bf16[496,384]{1,0:T(8,128)(2,1)}, bf16[496,384]{1,0:T(8,128)(2,1)S(1)}, u32[]{:S(2)}, u32[]{:S(2)}) %collective-permute-start.9) | collective-permute-done | bytes 380960 | tf_op jit(solution)/shard_map/ppermute | solution.py:968
  45.0 6.2 %collective-permute-done.13.refs_6_ = bf16[496,384]{1,0:T(8,128)(2,1)S(1)} collective-permute-done((bf16[496,384]{1,0:T(8,128)(2,1)S(1)}, bf16[496,384]{1,0:T(8,128)(2,1)S(1)}, u32[]{:S(2)}, u32[]{:S(2)}) %collective-permute-start.13) | collective-permute-done | bytes 380960 | tf_op jit(solution)/shard_map/ppermute | solution.py:968
  67.4 7.1 %collective-permute-done.23.refs_15_ = bf16[496,384]{1,0:T(8,128)(2,1)S(1)} collective-permute-done((bf16[496,384]{1,0:T(8,128)(2,1)S(1)}, bf16[496,384]{1,0:T(8,128)(2,1)S(1)}, u32[]{:S(2)}, u32[]{:S(2)}) %collective-permute-start.23) | collective-permute-done | bytes 380960 | tf_op jit(solution)/shard_map/ppermute | solution.py:972
  77.7 7.2 %place.1 = (bf16[3072,384]{1,0:T(8,128)(2,1)}, bf16[768,1536]{1,0:T(8,128)(2,1)}, bf16[768,384]{1,0:T(8,128)(2,1)}, bf16[768,384]{1,0:T(8,128)(2,1)}, bf16[256,384]{1,0:T(8,128)(2,1)}) custom-call(s32[7]{0:T(128)} %concatenate.54.sc, bf16[496,384]{1,0:T(8,128)(2,1)} %pack.1.refs_0_, bf16[496,384]{1,0:T(8,128)(2,1)} %copy-done.71, ...), custom_call_target="tpu_custom_call" | custom-call | bytes 12189696 | tf_op jit(solution)/shard_map/place/pallas_call | solution.py:874
  95.5 7.8 %values.1.refs_12_.refs_4_.v_own = bf16[12,1024,128]{2,1,0:T(8,128)(2,1)} custom-call(s32[7]{0:T(128)} %concatenate.54.sc, bf16[2,1024,768]{2,1,0:T(8,128)(2,1)} %tok.1, f32[1,768]{1,0:T(1,128)} %reshape.205.gain, bf16[768,384]{1,0:T(8,128)(2,1)} %get-tuple-element.415.w_own, bf16[768,384]{1,0:T(8,128)(2,1)} %copy-done.45), custom_call_target="tpu_custom_call" | custom-call | flops 2415919104 | bytes 6291456 | tf_op jit(solution)/shard_map/values/pallas_call | solution.py:81
  113.7 16.7 %collective-permute-done.32.refs_6_ = bf16[384,1024]{1,0:T(8,128)(2,1)} collective-permute-done((bf16[384,1024]{1,0:T(8,128)(2,1)}, bf16[384,1024]{1,0:T(8,128)(2,1)}, u32[]{:S(2)}, u32[]{:S(2)}) %collective-permute-start.32) | collective-permute-done | bytes 786464 | tf_op jit(solution)/shard_map/ppermute | solution.py:968
  135.2 5.5 %masked.1.cot = bf16[4,512,768]{2,1,0:T(8,128)(2,1)} custom-call(s32[7]{0:T(128)} %concatenate.54.sc, bf16[2,8,2,64,768]{4,3,2,1,0:T(8,128)(2,1)} %bitcast.114, bf16[2,8,64,768]{3,2,1,0:T(8,128)(2,1)} %copy-done.64), custom_call_target="tpu_custom_call" | custom-call | bytes 6291456 | tf_op jit(solution)/shard_map/masked/pallas_call | solution.py:299
  140.7 11.8 %collective-permute-done.38.refs_11_ = bf16[384,1024]{1,0:T(8,128)(2,1)} collective-permute-done((bf16[384,1024]{1,0:T(8,128)(2,1)}, bf16[384,1024]{1,0:T(8,128)(2,1)}, u32[]{:S(2)}, u32[]{:S(2)}) %collective-permute-start.38) | collective-permute-done | bytes 786464 | tf_op jit(solution)/shard_map/ppermute | solution.py:968
  157.1 13.2 %mix.2 = (bf16[12,512,256]{2,1,0:T(8,128)(2,1)}, f32[12,512,256]{2,1,0:T(8,128)}, bf16[12,512,1024]{2,1,0:T(8,128)(2,1)}, bf16[12,512,256]{2,1,0:T(8,128)(2,1)}) custom-call(s32[7]{0:T(128)} %concatenate.54.sc, bf16[384,1024]{1,0:T(8,128)(2,1)} %bitcast.120, bf16[384,1024]{1,0:T(8,128)(2,1)} %collective-permute-done.24.refs_1_, ...), custom_call_target="tpu_custom_call" | custom-call | flops 3221225472 | bytes 20447232 | tf_op jit(solution)/shard_map/mix/pallas_call | solution.py:191
  170.2 5.0 %collective-permute-done.41.refs_3_ = bf16[384,1024]{1,0:T(8,128)(2,1)} collective-permute-done((bf16[384,1024]{1,0:T(8,128)(2,1)}, bf16[384,1024]{1,0:T(8,128)(2,1)}, u32[]{:S(2)}, u32[]{:S(2)}) %collective-permute-start.41) | collective-permute-done | bytes 786464 | tf_op jit(solution)/shard_map/ppermute | solution.py:972
  176.4 8.5 %mix.3 = (bf16[12,512,256]{2,1,0:T(8,128)(2,1)}, f32[12,512,256]{2,1,0:T(8,128)}, bf16[12,512,1024]{2,1,0:T(8,128)(2,1)}, bf16[12,512,256]{2,1,0:T(8,128)(2,1)}) custom-call(s32[7]{0:T(128)} %concatenate.54.sc, bf16[384,1024]{1,0:T(8,128)(2,1)} %copy-done.68, ...), custom_call_target="tpu_custom_call", output_to_operand_aliasing={{0}: (7, {}), {1}: (8, {}), {2}: (9, {}), {3}: (10, {})} | custom-call | flops 3221225472 | bytes 20447232 | tf_op jit(solution)/shard_map/mix/pallas_call | solution.py:191
  184.9 10.6 %pre.1 = (bf16[4,512,768]{2,1,0:T(8,128)(2,1)}, bf16[4,512,768]{2,1,0:T(8,128)(2,1)}, bf16[4,512,768]{2,1,0:T(8,128)(2,1)}) custom-call(s32[7]{0:T(128)} %concatenate.54.sc, bf16[2,8,2,64,768]{4,3,2,1,0:T(8,128)(2,1)} %bitcast.106, bf16[2,8,64,768]{3,2,1,0:T(8,128)(2,1)} %copy-done.63, bf16[12,512,256]{2,1,0:T(8,128)(2,1)} %get-tuple-element.475.heads, ...), custom_call_target="tpu_custom_call" | custom-call | flops 2415919104 | bytes 25165824 | tf_op jit(solution)/shard_map/pre/pallas_call | solution.py:270
  195.5 30.2 %units.1 = (bf16[2048,3072]{1,0:T(8,128)(2,1)}, bf16[2048,3072]{1,0:T(8,128)(2,1)}) custom-call(s32[7]{0:T(128)} %concatenate.54.sc, bf16[2048,768]{1,0:T(8,128)(2,1)} %bitcast.141, bf16[2048,768]{1,0:T(8,128)(2,1)} %bitcast.123, bf16[768,1536]{1,0:T(8,128)(2,1)} %get-tuple-element.481.up_own, bf16[768,1536]{1,0:T(8,128)(2,1)} %collective-permute-done.42.up_far, ...), custom_call_target="tpu_custom_call" | custom-call | flops 19327352832 | bytes 34603008 | tf_op jit(solution)/shard_map/units/pallas_call | solution.py:365
  225.8 28.1 %post.1 = (bf16[2,512,768]{2,1,0:T(8,128)(2,1)}, bf16[2,512,768]{2,1,0:T(8,128)(2,1)}, bf16[12,512,256]{2,1,0:T(8,128)(2,1)}, f32[1,768]{1,0:T(1,128)}) custom-call(s32[7]{0:T(128)} %concatenate.54.sc, bf16[4,512,768]{2,1,0:T(8,128)(2,1)} %get-tuple-element.478.resid, bf16[4,512,3072]{2,1,0:T(8,128)(2,1)} %bitcast.144, bf16[4,512,3072]{2,1,0:T(8,128)(2,1)} %bitcast.145, ...), custom_call_target="tpu_custom_call" | custom-call | flops 12079595520 | bytes 37748736 | tf_op jit(solution)/shard_map/post/pallas_call | solution.py:569
  253.9 9.9 %unmix.2 = (bf16[384,1024]{1,0:T(8,128)(2,1)}, bf16[384,1024]{1,0:T(8,128)(2,1)}, bf16[384,1024]{1,0:T(8,128)(2,1)}, bf16[384,1024]{1,0:T(8,128)(2,1)}, bf16[12,...) custom-call(s32[7]{0:T(128)} %concatenate.54.sc, bf16[12,1024,128]{2,1,0:T(8,128)(2,1)} %values.1.refs_12_.refs_4_.v_own, ...), custom_call_target="tpu_custom_call" | custom-call | flops 4831838208 | bytes 33030144 | tf_op jit(solution)/shard_map/unmix/pallas_call | solution.py:665
  269.1 19.5 %unmix.3 = (bf16[384,1024]{1,0:T(8,128)(2,1)}, bf16[384,1024]{1,0:T(8,128)(2,1)}, bf16[384,1024]{1,0:T(8,128)(2,1)}, bf16[384,1024]{1,0:T(8,128)(2,1)}, bf16[384...) custom-call(s32[7]{0:T(128)} %concatenate.54.sc, ...), custom_call_target="tpu_custom_call", output_to_operand_aliasing={{12}: (7, {}), {13}: (8, {})} | custom-call | flops 4831838208 | bytes 33030144 | tf_op jit(solution)/shard_map/unmix/pallas_call | solution.py:665
  294.9 16.3 %up_grad.1 = (bf16[768,1536]{1,0:T(8,128)(2,1)}, bf16[768,1536]{1,0:T(8,128)(2,1)}) custom-call(s32[7]{0:T(128)} %concatenate.54.sc, bf16[2048,768]{1,0:T(8,128)(2,1)} %bitcast.142, bf16[2048,3072]{1,0:T(8,128)(2,1)} %get-tuple-element.483.up_grad), custom_call_target="tpu_custom_call" | custom-call | flops 9663676416 | bytes 15728640 | tf_op jit(solution)/shard_map/up_grad/pallas_call | solution.py:428
  319.6 15.7 %down_grad.1 = (bf16[3072,384]{1,0:T(8,128)(2,1)}, bf16[3072,384]{1,0:T(8,128)(2,1)}) custom-call(s32[7]{0:T(128)} %concatenate.54.sc, bf16[2048,3072]{1,0:T(8,128)(2,1)} %get-tuple-element.551.active, bf16[2048,768]{1,0:T(8,128)(2,1)} %bitcast.124), custom_call_target="tpu_custom_call" | custom-call | flops 9663676416 | bytes 15728640 | tf_op jit(solution)/shard_map/down_grad/pallas_call | solution.py:397
  345.4 5.3 %out_grad.1 = (bf16[768,384]{1,0:T(8,128)(2,1)S(1)}, bf16[768,384]{1,0:T(8,128)(2,1)S(1)}) custom-call(s32[7]{0:T(128)S(1)} %copy-done.33, bf16[4,512,768]{2,1,0:T(8,128)(2,1)S(1)} %copy-done.36, bf16[2,512,768]{2,1,0:T(8,128)(2,1)S(1)} %copy-done.57, bf16[2,512,768]{2,1,0:T(8,128)(2,1)S(1)} %copy-done.41), custom_call_target="tpu_custom_call" | custom-call | flops 2415919104 | bytes 6291456 | tf_op jit(solution)/shard_map/out_grad/pallas_call | solution.py:468
  374.5 15.0 %out.3 = (bf16[2,512,768]{2,1,0:T(8,128)(2,1)S(1)}, bf16[2,512,768]{2,1,0:T(8,128)(2,1)S(1)}) custom-call(s32[7]{0:T(128)S(1)} %copy-done.33, bf16[4,512,3072]{2,1,0:T(8,128)(2,1)} %bitcast.143, bf16[4,512,768]{2,1,0:T(8,128)(2,1)S(1)} %copy-done.35, bf16[3072,384]{1,0:T(8,128)(2,1)S(1)} %copy-done.38, bf16[3072,384]{1,0:T(8,128)(2,1)} %collective-permute-done.43.dn_far), custom_call_target="tpu_custom_call" | custom-call | flops 9663676416 | bytes 23592960 | tf_op jit(solution)/shard_map/out/pallas_call | solution.py:502
  396.5 12.4 %close.1 = (f32[2,8,2,64,768]{4,3,2,1,0:T(8,128)}, bf16[2,768,384]{2,1,0:T(8,128)(2,1)S(1)}, f32[1,768]{1,0:T(1,128)S(1)}) custom-call(s32[7]{0:T(128)S(1)} %copy-done.33, bf16[2,8,2,64,768]{4,3,2,1,0:T(8,128)(2,1)S(1)} %bitcast.107, bf16[2,8,64,768]{3,2,1,0:T(8,128)(2,1)S(1)} %bitcast.113, bf16[2,8,64,768]{3,2,1,0:T(8,128)(2,1)S(1)} %bitcast.112, ...), custom_call_target="tpu_custom_call" | custom-call | flops 4831838208 | bytes 29884416 | tf_op jit(solution)/shard_map/close/pallas_call | solution.py:755
  429.5 5.7 %collective-permute-done.75 = bf16[4,2,64,384]{3,2,1,0:T(8,128)(2,1)S(1)} collective-permute-done((bf16[4,2,64,384]{3,2,1,0:T(8,128)(2,1)S(1)}, bf16[4,2,64,384]{3,2,1,0:T(8,128)(2,1)S(1)}, u32[]{:S(2)}, u32[]{:S(2)}) %collective-permute-start.75) | collective-permute-done | bytes 393248 | tf_op jit(solution)/shard_map/ppermute | solution.py:968
  435.3 6.3 %collective-permute-done.72 = bf16[432,384]{1,0:T(8,128)(2,1)S(1)} collective-permute-done((bf16[432,384]{1,0:T(8,128)(2,1)S(1)}, bf16[432,384]{1,0:T(8,128)(2,1)S(1)}, u32[]{:S(2)}, u32[]{:S(2)}) %collective-permute-start.72) | collective-permute-done | bytes 331808 | tf_op jit(solution)/shard_map/ppermute | solution.py:968
  (440 shorter events, 191.3 us)
Async XLA Ops:
  110.0 23.4 %collective-permute-start.35 = (bf16[12,1024,128]{2,1,0:T(8,128)(2,1)}, bf16[12,1024,128]{2,1,0:T(8,128)(2,1)}, u32[]{:S(2)}, u32[]{:S(2)}) collective-permute-start(bf16[12,1024,128]{2,1,0:T(8,128)(2,1)} %values.1.refs_12_.refs_4_.v_own), channel_id=1, source_target_pairs={{0,1},{1,0},{2,3},{3,2},{4,5},{5,4},{6,7},{7,6},{8,9},{9,8},{10,11... | collective-permute-start | bytes 9437192 | tf_op jit(solution)/shard_map/ppermute | solution.py:968
  110.1 20.3 %collective-permute-start.32 = (bf16[384,1024]{1,0:T(8,128)(2,1)}, bf16[384,1024]{1,0:T(8,128)(2,1)}, u32[]{:S(2)}, u32[]{:S(2)}) collective-permute-start(bf16[384,1024]{1,0:T(8,128)(2,1)} %collective-permute-done.26.refs_4_), channel_id=1, source_target_pairs={{0,4},{1,5},{2,6},{3,7},{4,0},{5,1},{6,2},{7,3},{8,12},{9,13},{10,... | collective-permute-start | bytes 2359304 | tf_op jit(solution)/shard_map/ppermute | solution.py:968
  111.0 21.4 %collective-permute-start.34 = (bf16[384,1024]{1,0:T(8,128)(2,1)S(1)}, bf16[384,1024]{1,0:T(8,128)(2,1)S(1)}, u32[]{:S(2)}, u32[]{:S(2)}) collective-permute-start(bf16[384,1024]{1,0:T(8,128)(2,1)S(1)} %collective-permute-done.30.refs_8_), channel_id=1, source_target_pairs={{0,8},{1,9},{2,10},{3,11},{4,12},{5,13},{6,14},{7,15},{8,16},{9,17... | collective-permute-start | bytes 2359304 | tf_op jit(solution)/shard_map/ppermute | solution.py:972
  134.5 20.6 %collective-permute-start.37 = (bf16[384,1024]{1,0:T(8,128)(2,1)}, bf16[384,1024]{1,0:T(8,128)(2,1)}, u32[]{:S(2)}, u32[]{:S(2)}) collective-permute-start(bf16[384,1024]{1,0:T(8,128)(2,1)} %collective-permute-done.32.refs_6_), channel_id=1, source_target_pairs={{0,8},{1,9},{2,10},{3,11},{4,12},{5,13},{6,14},{7,15},{8,16},{9,17... | collective-permute-start | bytes 2359304 | tf_op jit(solution)/shard_map/ppermute | solution.py:972
  134.6 20.5 %collective-permute-start.36 = (bf16[384,1024]{1,0:T(8,128)(2,1)}, bf16[384,1024]{1,0:T(8,128)(2,1)}, u32[]{:S(2)}, u32[]{:S(2)}) collective-permute-start(bf16[384,1024]{1,0:T(8,128)(2,1)} %collective-permute-done.32.refs_6_), channel_id=1, source_target_pairs={{0,2},{1,3},{2,0},{3,1},{4,6},{5,7},{6,4},{7,5},{8,10},{9,11},{10,... | collective-permute-start | bytes 2359304 | tf_op jit(solution)/shard_map/ppermute | solution.py:968
  155.1 20.1 %collective-permute-start.41 = (bf16[384,1024]{1,0:T(8,128)(2,1)}, bf16[384,1024]{1,0:T(8,128)(2,1)}, u32[]{:S(2)}, u32[]{:S(2)}) collective-permute-start(bf16[384,1024]{1,0:T(8,128)(2,1)} %collective-permute-done.38.refs_11_), channel_id=1, source_target_pairs={{0,8},{1,9},{2,10},{3,11},{4,12},{5,13},{6,14},{7,15},{8,16},{9,17... | collective-permute-start | bytes 2359304 | tf_op jit(solution)/shard_map/ppermute | solution.py:972
  175.3 20.3 %collective-permute-start.42 = (bf16[768,1536]{1,0:T(8,128)(2,1)}, bf16[768,1536]{1,0:T(8,128)(2,1)}, u32[]{:S(2)}, u32[]{:S(2)}) collective-permute-start(bf16[768,1536]{1,0:T(8,128)(2,1)} %get-tuple-element.481.up_own), channel_id=1, source_target_pairs={{0,1},{1,0},{2,3},{3,2},{4,5},{5,4},{6,7},{7,6},{8,9},{9,8},{10,11... | collective-permute-start | bytes 7077896 | tf_op jit(solution)/shard_map/ppermute | solution.py:968
  175.3 20.3 %collective-permute-start.43 = (bf16[3072,384]{1,0:T(8,128)(2,1)S(1)}, bf16[3072,384]{1,0:T(8,128)(2,1)}, u32[]{:S(2)}, u32[]{:S(2)}) collective-permute-start(bf16[3072,384]{1,0:T(8,128)(2,1)S(1)} %copy-done.37), channel_id=1, source_target_pairs={{0,1},{1,0},{2,3},{3,2},{4,5},{5,4},{6,7},{7,6},{8,9},{9,8},{10,11... | collective-permute-start | bytes 7077896 | tf_op jit(solution)/shard_map/ppermute | solution.py:968
  265.1 23.5 %collective-permute-start.45 = (bf16[384,1024]{1,0:T(8,128)(2,1)}, bf16[384,1024]{1,0:T(8,128)(2,1)S(1)}, u32[]{:S(2)}, u32[]{:S(2)}) collective-permute-start(bf16[384,1024]{1,0:T(8,128)(2,1)} %get-tuple-element.496), channel_id=1, source_target_pairs={{0,24},{1,25},{2,26},{3,27},{4,28},{5,29},{6,30},{7,31},{8,0},{9,1... | collective-permute-start | bytes 2359304 | tf_op jit(solution)/shard_map/ppermute | solution.py:972
  267.4 21.2 %collective-permute-start.46 = (bf16[384,1024]{1,0:T(8,128)(2,1)}, bf16[384,1024]{1,0:T(8,128)(2,1)S(1)}, u32[]{:S(2)}, u32[]{:S(2)}) collective-permute-start(bf16[384,1024]{1,0:T(8,128)(2,1)} %get-tuple-element.497), channel_id=1, source_target_pairs={{0,2},{1,3},{2,0},{3,1},{4,6},{5,7},{6,4},{7,5},{8,10},{9,11},{10,... | collective-permute-start | bytes 2359304 | tf_op jit(solution)/shard_map/ppermute | solution.py:968
  268.0 20.7 %collective-permute-start.47 = (bf16[384,1024]{1,0:T(8,128)(2,1)}, bf16[384,1024]{1,0:T(8,128)(2,1)}, u32[]{:S(2)}, u32[]{:S(2)}) collective-permute-start(bf16[384,1024]{1,0:T(8,128)(2,1)} %get-tuple-element.498), channel_id=1, source_target_pairs={{0,4},{1,5},{2,6},{3,7},{4,0},{5,1},{6,2},{7,3},{8,12},{9,13},{10,... | collective-permute-start | bytes 2359304 | tf_op jit(solution)/shard_map/ppermute | solution.py:968
  288.6 24.8 %collective-permute-start.51 = (bf16[12,1024,128]{2,1,0:T(8,128)(2,1)}, bf16[12,1024,128]{2,1,0:T(8,128)(2,1)}, u32[]{:S(2)}, u32[]{:S(2)}) collective-permute-start(bf16[12,1024,128]{2,1,0:T(8,128)(2,1)} %get-tuple-element.535), channel_id=1, source_target_pairs={{0,1},{1,0},{2,3},{3,2},{4,5},{5,4},{6,7},{7,6},{8,9},{9,8},{10,11... | collective-permute-start | bytes 9437192 | tf_op jit(solution)/shard_map/ppermute | solution.py:968
  288.7 22.4 %collective-permute-start.48 = (bf16[384,1024]{1,0:T(8,128)(2,1)}, bf16[384,1024]{1,0:T(8,128)(2,1)S(1)}, u32[]{:S(2)}, u32[]{:S(2)}) collective-permute-start(bf16[384,1024]{1,0:T(8,128)(2,1)} %get-tuple-element.530), channel_id=1, source_target_pairs={{0,24},{1,25},{2,26},{3,27},{4,28},{5,29},{6,30},{7,31},{8,0},{9,1... | collective-permute-start | bytes 2359304 | tf_op jit(solution)/shard_map/ppermute | solution.py:972
  289.5 22.6 %collective-permute-start.49 = (bf16[384,1024]{1,0:T(8,128)(2,1)}, bf16[384,1024]{1,0:T(8,128)(2,1)S(1)}, u32[]{:S(2)}, u32[]{:S(2)}) collective-permute-start(bf16[384,1024]{1,0:T(8,128)(2,1)} %get-tuple-element.531), channel_id=1, source_target_pairs={{0,2},{1,3},{2,0},{3,1},{4,6},{5,7},{6,4},{7,5},{8,10},{9,11},{10,... | collective-permute-start | bytes 2359304 | tf_op jit(solution)/shard_map/ppermute | solution.py:968
  313.5 24.6 %collective-permute-start.55 = (bf16[768,1536]{1,0:T(8,128)(2,1)}, bf16[768,1536]{1,0:T(8,128)(2,1)S(1)}, u32[]{:S(2)}, u32[]{:S(2)}) collective-permute-start(bf16[768,1536]{1,0:T(8,128)(2,1)} %get-tuple-element.554), channel_id=1, source_target_pairs={{0,1},{1,0},{2,3},{3,2},{4,5},{5,4},{6,7},{7,6},{8,9},{9,8},{10,11... | collective-permute-start | bytes 7077896 | tf_op jit(solution)/shard_map/ppermute | solution.py:968
  313.5 21.9 %collective-permute-start.52 = (bf16[384,1024]{1,0:T(8,128)(2,1)S(1)}, bf16[384,1024]{1,0:T(8,128)(2,1)S(1)}, u32[]{:S(2)}, u32[]{:S(2)}) collective-permute-start(bf16[384,1024]{1,0:T(8,128)(2,1)S(1)} %copy-done.43), channel_id=1, source_target_pairs={{0,24},{1,25},{2,26},{3,27},{4,28},{5,29},{6,30},{7,31},{8,0},{9,1... | collective-permute-start | bytes 2359304 | tf_op jit(solution)/shard_map/ppermute | solution.py:972
  317.3 20.1 %collective-permute-start.53 = (bf16[384,1024]{1,0:T(8,128)(2,1)}, bf16[384,1024]{1,0:T(8,128)(2,1)S(1)}, u32[]{:S(2)}, u32[]{:S(2)}) collective-permute-start(bf16[384,1024]{1,0:T(8,128)(2,1)} %get-tuple-element.549), channel_id=1, source_target_pairs={{0,2},{1,3},{2,0},{3,1},{4,6},{5,7},{6,4},{7,5},{8,10},{9,11},{10,... | collective-permute-start | bytes 2359304 | tf_op jit(solution)/shard_map/ppermute | solution.py:968
  338.1 20.2 %collective-permute-start.57 = (bf16[384,1024]{1,0:T(8,128)(2,1)}, bf16[384,1024]{1,0:T(8,128)(2,1)S(1)}, u32[]{:S(2)}, u32[]{:S(2)}) collective-permute-start(bf16[384,1024]{1,0:T(8,128)(2,1)} %get-tuple-element.565), channel_id=1, source_target_pairs={{0,2},{1,3},{2,0},{3,1},{4,6},{5,7},{6,4},{7,5},{8,10},{9,11},{10,... | collective-permute-start | bytes 2359304 | tf_op jit(solution)/shard_map/ppermute | solution.py:968
  363.7 25.8 %collective-permute-start.65 = (bf16[432,384]{1,0:T(8,128)(2,1)S(1)}, bf16[432,384]{1,0:T(8,128)(2,1)S(1)}, u32[]{:S(2)}, u32[]{:S(2)}) collective-permute-start(bf16[432,384]{1,0:T(8,128)(2,1)S(1)} %get-tuple-element.614), channel_id=1, source_target_pairs={{0,2},{1,3},{2,0},{3,1},{4,6},{5,7},{6,4},{7,5},{8,10},{9,11},{10,... | collective-permute-start | bytes 995336 | tf_op jit(solution)/shard_map/ppermute | solution.py:968
  364.3 25.3 %collective-permute-start.66 = (bf16[432,384]{1,0:T(8,128)(2,1)S(1)}, bf16[432,384]{1,0:T(8,128)(2,1)S(1)}, u32[]{:S(2)}, u32[]{:S(2)}) collective-permute-start(bf16[432,384]{1,0:T(8,128)(2,1)S(1)} %get-tuple-element.615), channel_id=1, source_target_pairs={{0,4},{1,5},{2,6},{3,7},{4,0},{5,1},{6,2},{7,3},{8,12},{9,13},{10,... | collective-permute-start | bytes 995336 | tf_op jit(solution)/shard_map/ppermute | solution.py:968
  365.2 24.4 %collective-permute-start.63 = (bf16[384,1024]{1,0:T(8,128)(2,1)S(1)}, bf16[384,1024]{1,0:T(8,128)(2,1)S(1)}, u32[]{:S(2)}, u32[]{:S(2)}) collective-permute-start(bf16[384,1024]{1,0:T(8,128)(2,1)S(1)} %copy-done.101), channel_id=1, source_target_pairs={{0,4},{1,5},{2,6},{3,7},{4,0},{5,1},{6,2},{7,3},{8,12},{9,13},{10,... | collective-permute-start | bytes 2359304 | tf_op jit(solution)/shard_map/ppermute | solution.py:968
  366.8 22.8 %collective-permute-start.61 = (bf16[384,1024]{1,0:T(8,128)(2,1)S(1)}, bf16[384,1024]{1,0:T(8,128)(2,1)S(1)}, u32[]{:S(2)}, u32[]{:S(2)}) collective-permute-start(bf16[384,1024]{1,0:T(8,128)(2,1)S(1)} %get-tuple-element.597), channel_id=1, source_target_pairs={{0,24},{1,25},{2,26},{3,27},{4,28},{5,29},{6,30},{7,31},{8,0},{9,1... | collective-permute-start | bytes 2359304 | tf_op jit(solution)/shard_map/ppermute | solution.py:972
  389.6 20.3 %collective-permute-start.70 = (bf16[2,512,768]{2,1,0:T(8,128)(2,1)S(1)}, bf16[2,512,768]{2,1,0:T(8,128)(2,1)S(1)}, u32[]{:S(2)}, u32[]{:S(2)}) collective-permute-start(bf16[2,512,768]{2,1,0:T(8,128)(2,1)S(1)} %get-tuple-element.640), channel_id=1, source_target_pairs={{0,1},{1,0},{2,3},{3,2},{4,5},{5,4},{6,7},{7,6},{8,9},{9,8},{10,11... | collective-permute-start | bytes 4718600 | tf_op jit(solution)/shard_map/ppermute | solution.py:968
  425.6 23.9 %collective-permute-start.80 = (f32[3,64,1024]{2,1,0:T(8,128)S(1)}, f32[3,64,1024]{2,1,0:T(8,128)S(1)}, u32[]{:S(2)}, u32[]{:S(2)}) collective-permute-start(f32[3,64,1024]{2,1,0:T(8,128)S(1)} %get-tuple-element.691), channel_id=1, source_target_pairs={{0,1},{1,0},{2,3},{3,2},{4,5},{5,4},{6,7},{7,6},{8,9},{9,8},{10,11... | collective-permute-start | bytes 2359304 | tf_op jit(solution)/shard_map/ppermute | solution.py:968
  (167 other events, 1997.2 us)

commit v22 on v15

--- a/solution.py
+++ b/solution.py
@@ -742,9 +742,7 @@
 
     @pl.when(step == pl.num_programs(0) - 1)
     def _():
-        low = total[...].astype(BF16)
-        d_value[0] = low[:, :SIDE]
-        d_value[1] = low[:, SIDE:]
+        d_value[...] = total[...].astype(BF16)
 
 
 def run_close(sc, tokens, res_own, res_got, out_own, out_got, own, far, gain, w_own, w_far):
@@ -762,13 +760,13 @@
             in_specs=[whole_spec]
             + [half_spec] * 4
             + [back_spec, back_spec, held((1, WIDTH)), held((WIDTH, SIDE)), held((WIDTH, SIDE))],
-            out_specs=[whole_spec, whole_spec, held((2, WIDTH, SIDE)), held((1, WIDTH))],
+            out_specs=[whole_spec, whole_spec, held((WIDTH, WIDTH)), held((1, WIDTH))],
             scratch_shapes=[pltpu.VMEM((WIDTH, WIDTH), F32), pltpu.VMEM((WIDTH, WIDTH), BF16)],
         ),
         out_shape=[
             jax.ShapeDtypeStruct(slab, F32),
             jax.ShapeDtypeStruct(slab, F32),
-            jax.ShapeDtypeStruct((2, WIDTH, SIDE), BF16),
+            jax.ShapeDtypeStruct((WIDTH, WIDTH), BF16),
             jax.ShapeDtypeStruct((1, WIDTH), F32),
         ],
         compiler_params=params(LESS),
@@ -1108,10 +1106,10 @@
     sums = scatter_add(sums, got, 1)
 
     sums, got = scatter_send(sums, 2)
-    gain_pair = jnp.concatenate([d_gain_one, d_gain_two]).reshape(2, 16, 1, 48).astype(BF16)
-    gain_pair = jnp.pad(gain_pair, ((0, 0), (0, 0), (0, 15), (0, SIDE - 48)))
-    small = jnp.concatenate([d_value.reshape(2, 16, 48, SIDE), gain_pair], 2)
-    small = add_low(pick(small, core), other(pick(small, 1 - core))).reshape(4, 2, 2, 64, SIDE)
+    gain_pair = jnp.stack([d_gain_one.reshape(16, 2, 24), d_gain_two.reshape(16, 2, 24)], 2).reshape(16, 2, 1, 48)
+    gain_pair = jnp.pad(gain_pair.astype(BF16), ((0, 0), (0, 0), (0, 7), (0, WIDTH - 48)))
+    small = jnp.concatenate([d_value.reshape(16, 2, 24, WIDTH), gain_pair], 2).reshape(4, 2, 2, 2, 32, WIDTH)
+    small = add_low(pick(small, core, 3), other(pick(small, 1 - core, 3)))
     small = add_low(pick(small, x, 2), swap(pick(small, 1 - x, 2), TO_X))
     sums, got, small = together((sums, got, small))
     sums = scatter_add(sums, got, 2)
@@ -1128,7 +1126,7 @@
         small_sum = small_sum + ring(pick(small, lax.rem(z + PLANES - k, PLANES)), -k).astype(F32)
     sums, got, small_sum = together((sums, got, small_sum))
     big_sum = scatter_add(sums, got, 4)[0, 0, 0]
-    big_far, small_far = other(big_sum), other(small_sum)
+    big_far = other(big_sum.astype(BF16)).astype(F32)
 
     rows_of = lambda value, rows: pick(value.reshape(-1, 2, rows, SIDE), core, 1)
     mine = lambda own, far, rows: side(rows_of(own, rows)[0], rows_of(far, rows)[0], 1)
@@ -1136,22 +1134,18 @@
     up_side = lambda value: rows_of(value[PACK_UP:PACK_OUT], 24).transpose(1, 0, 2).reshape(24, 4 * SIDE)
     up_shard = side(up_side(big_sum), up_side(big_far), 1)
     outproj_shard = mine(big_sum[PACK_OUT:PACK_VALUE], big_far[PACK_OUT:PACK_VALUE], 24)
-    value_shard = mine(small_sum[:48], small_far[:48], 24)
-    gains_pair = ordered(core, small_sum[48, :48], small_far[48, :48])
-    gain_pair = pick(gains_pair.reshape(2, 2, 24), core, 1)
-
     rand_shard = ordered(core, blocks, blocks_far, 1)
 
     return (
         output.reshape(2, LMAX, WIDTH),
         tokens_grad.reshape(2, LMAX, WIDTH),
         rand_shard.reshape(3 * 128, LMAX),
-        value_shard,
+        small_sum[:24],
         outproj_shard,
         up_shard,
         down_shard,
-        gain_pair[0],
-        gain_pair[1],
+        small_sum[24, :24],
+        small_sum[24, 24:48],
     )
 
 

time: 478 us -> 497 us (1.040)
  local copies, waits for them, and re-layouts: 37 us -> 52.5 us
  other arithmetic: 9.1 us -> 14.5 us
    unnamed x184 -> x208, local copies, waits for them, and re-layouts: 26.8 us -> 43.4 us
    ppermute x66 -> x65, waiting for transfers between devices: 88.4 us -> 82.6 us  [swap(): return lax.ppermute(x, BOTH, [(d, d ^ bit) for d in range(DEVICES)])]
    ppermute x66 -> x65, starting transfers between devices: 47.9 us -> 46.9 us  [swap(): return lax.ppermute(x, BOTH, [(d, d ^ bit) for d in range(DEVICES)])]
  transfers between devices with their start and end apart: 89 -> 88, of which waited for: 38 -> 34; matrix products, arithmetic and copies ran while one was open for 3% -> 3% of each run, Pallas kernels for 32% -> 31%
where the time goes in v22:
time: 497 us; the launch traced here: 491 us
  Pallas kernels  212 us (43%)
  waiting for transfers between devices  136 us (27%)
  starting transfers between devices  74.1 us (15%)
  local copies, waits for them, and re-layouts  52.5 us (11%)
  other arithmetic  14.5 us (3%)
    ppermute x65, waiting for transfers between devices, swap(): return lax.ppermute(x, BOTH, [(d, d ^ bit) for d in range(DEVICES)])  82.6 us
    ppermute x23, waiting for transfers between devices, ring(): lax.ppermute(x, BOTH, [(d, (d + 8 * way) % DEVICES) for d in range(DEVICE...  53.1 us
    ppermute x65, starting transfers between devices, swap(): return lax.ppermute(x, BOTH, [(d, d ^ bit) for d in range(DEVICES)])  46.9 us
    unnamed x208, local copies, waits for them, and re-layouts  43.4 us
    pallas_call x1, Pallas kernels, run_units(): pl.pallas_call(units_kernel, grid_spec=pltpu.PrefetchScalarGridSpec(num_s...  30.2 us
    pallas_call x2, Pallas kernels, run_unmix(): pl.pallas_call(partial(unmix_kernel, count, bool(carry)), grid_spec=pltpu...  29.5 us
    pallas_call x1, Pallas kernels, run_post(): pl.pallas_call(post_kernel, grid_spec=pltpu.PrefetchScalarGridSpec(num_sc...  28.1 us
    ppermute x23, starting transfers between devices, ring(): lax.ppermute(x, BOTH, [(d, (d + 8 * way) % DEVICES) for d in range(DEVICE...  27.2 us
  transfers between devices with their start and end apart: 88, of which 34 were waited for; matrix products, arithmetic and copies ran while one was open for 3% of the time, Pallas kernels for 31%

profile of v22, /device:TPU:0, one launch (start us, length us, event | category | flops | bytes accessed | tf_op | source)
XLA Modules:
  0.0 490.9 jit_solution(15144365963151231741)
XLA Ops:
  16.5 8.3 %collective-permute-done.7.refs_4_ = bf16[496,384]{1,0:T(8,128)(2,1)S(1)} collective-permute-done((bf16[496,384]{1,0:T(8,128)(2,1)}, bf16[496,384]{1,0:T(8,128)(2,1)S(1)}, u32[]{:S(2)}, u32[]{:S(2)}) %collective-permute-start.7) | collective-permute-done | bytes 380960 | tf_op jit(solution)/shard_map/ppermute | solution.py:950
  31.5 7.5 %collective-permute-done.9.refs_3_ = bf16[496,384]{1,0:T(8,128)(2,1)S(1)} collective-permute-done((bf16[496,384]{1,0:T(8,128)(2,1)}, bf16[496,384]{1,0:T(8,128)(2,1)S(1)}, u32[]{:S(2)}, u32[]{:S(2)}) %collective-permute-start.9) | collective-permute-done | bytes 380960 | tf_op jit(solution)/shard_map/ppermute | solution.py:946
  45.0 6.2 %collective-permute-done.13.refs_6_ = bf16[496,384]{1,0:T(8,128)(2,1)S(1)} collective-permute-done((bf16[496,384]{1,0:T(8,128)(2,1)S(1)}, bf16[496,384]{1,0:T(8,128)(2,1)S(1)}, u32[]{:S(2)}, u32[]{:S(2)}) %collective-permute-start.13) | collective-permute-done | bytes 380960 | tf_op jit(solution)/shard_map/ppermute | solution.py:946
  67.4 7.1 %collective-permute-done.23.refs_15_ = bf16[496,384]{1,0:T(8,128)(2,1)S(1)} collective-permute-done((bf16[496,384]{1,0:T(8,128)(2,1)S(1)}, bf16[496,384]{1,0:T(8,128)(2,1)S(1)}, u32[]{:S(2)}, u32[]{:S(2)}) %collective-permute-start.23) | collective-permute-done | bytes 380960 | tf_op jit(solution)/shard_map/ppermute | solution.py:950
  77.7 7.2 %place.1 = (bf16[3072,384]{1,0:T(8,128)(2,1)}, bf16[768,1536]{1,0:T(8,128)(2,1)}, bf16[768,384]{1,0:T(8,128)(2,1)}, bf16[768,384]{1,0:T(8,128)(2,1)}, bf16[256,384]{1,0:T(8,128)(2,1)}) custom-call(s32[7]{0:T(128)} %concatenate.47.sc, bf16[496,384]{1,0:T(8,128)(2,1)} %pack.1.refs_0_, bf16[496,384]{1,0:T(8,128)(2,1)} %copy-done.76, ...), custom_call_target="tpu_custom_call" | custom-call | bytes 12189696 | tf_op jit(solution)/shard_map/place/pallas_call | solution.py:852
  95.5 7.8 %values.1.refs_12_.refs_4_.v_own = bf16[12,1024,128]{2,1,0:T(8,128)(2,1)} custom-call(s32[7]{0:T(128)} %concatenate.47.sc, bf16[2,1024,768]{2,1,0:T(8,128)(2,1)} %tok.1, f32[1,768]{1,0:T(1,128)} %reshape.183.gain, bf16[768,384]{1,0:T(8,128)(2,1)} %get-tuple-element.415.w_own, bf16[768,384]{1,0:T(8,128)(2,1)} %copy-done.49), custom_call_target="tpu_custom_call" | custom-call | flops 2415919104 | bytes 6291456 | tf_op jit(solution)/shard_map/values/pallas_call | solution.py:81
  113.7 16.7 %collective-permute-done.32.refs_6_ = bf16[384,1024]{1,0:T(8,128)(2,1)} collective-permute-done((bf16[384,1024]{1,0:T(8,128)(2,1)}, bf16[384,1024]{1,0:T(8,128)(2,1)}, u32[]{:S(2)}, u32[]{:S(2)}) %collective-permute-start.32) | collective-permute-done | bytes 786464 | tf_op jit(solution)/shard_map/ppermute | solution.py:946
  135.2 5.5 %masked.1.cot = bf16[4,512,768]{2,1,0:T(8,128)(2,1)} custom-call(s32[7]{0:T(128)} %concatenate.47.sc, bf16[2,8,2,64,768]{4,3,2,1,0:T(8,128)(2,1)} %bitcast.119, bf16[2,8,64,768]{3,2,1,0:T(8,128)(2,1)} %copy-done.69), custom_call_target="tpu_custom_call" | custom-call | bytes 6291456 | tf_op jit(solution)/shard_map/masked/pallas_call | solution.py:299
  140.7 11.8 %collective-permute-done.38.refs_11_ = bf16[384,1024]{1,0:T(8,128)(2,1)} collective-permute-done((bf16[384,1024]{1,0:T(8,128)(2,1)}, bf16[384,1024]{1,0:T(8,128)(2,1)}, u32[]{:S(2)}, u32[]{:S(2)}) %collective-permute-start.38) | collective-permute-done | bytes 786464 | tf_op jit(solution)/shard_map/ppermute | solution.py:946
  157.1 13.2 %mix.2 = (bf16[12,512,256]{2,1,0:T(8,128)(2,1)}, f32[12,512,256]{2,1,0:T(8,128)}, bf16[12,512,1024]{2,1,0:T(8,128)(2,1)}, bf16[12,512,256]{2,1,0:T(8,128)(2,1)}) custom-call(s32[7]{0:T(128)} %concatenate.47.sc, bf16[384,1024]{1,0:T(8,128)(2,1)} %bitcast.124, bf16[384,1024]{1,0:T(8,128)(2,1)} %collective-permute-done.24.refs_1_, ...), custom_call_target="tpu_custom_call" | custom-call | flops 3221225472 | bytes 20447232 | tf_op jit(solution)/shard_map/mix/pallas_call | solution.py:191
  170.2 5.0 %collective-permute-done.41.refs_3_ = bf16[384,1024]{1,0:T(8,128)(2,1)} collective-permute-done((bf16[384,1024]{1,0:T(8,128)(2,1)}, bf16[384,1024]{1,0:T(8,128)(2,1)}, u32[]{:S(2)}, u32[]{:S(2)}) %collective-permute-start.41) | collective-permute-done | bytes 786464 | tf_op jit(solution)/shard_map/ppermute | solution.py:950
  176.4 8.5 %mix.3 = (bf16[12,512,256]{2,1,0:T(8,128)(2,1)}, f32[12,512,256]{2,1,0:T(8,128)}, bf16[12,512,1024]{2,1,0:T(8,128)(2,1)}, bf16[12,512,256]{2,1,0:T(8,128)(2,1)}) custom-call(s32[7]{0:T(128)} %concatenate.47.sc, bf16[384,1024]{1,0:T(8,128)(2,1)} %copy-done.73, ...), custom_call_target="tpu_custom_call", output_to_operand_aliasing={{0}: (7, {}), {1}: (8, {}), {2}: (9, {}), {3}: (10, {})} | custom-call | flops 3221225472 | bytes 20447232 | tf_op jit(solution)/shard_map/mix/pallas_call | solution.py:191
  184.9 10.6 %pre.1 = (bf16[4,512,768]{2,1,0:T(8,128)(2,1)}, bf16[4,512,768]{2,1,0:T(8,128)(2,1)}, bf16[4,512,768]{2,1,0:T(8,128)(2,1)}) custom-call(s32[7]{0:T(128)} %concatenate.47.sc, bf16[2,8,2,64,768]{4,3,2,1,0:T(8,128)(2,1)} %bitcast.105, bf16[2,8,64,768]{3,2,1,0:T(8,128)(2,1)} %copy-done.68, bf16[12,512,256]{2,1,0:T(8,128)(2,1)} %get-tuple-element.475.heads, ...), custom_call_target="tpu_custom_call" | custom-call | flops 2415919104 | bytes 25165824 | tf_op jit(solution)/shard_map/pre/pallas_call | solution.py:270
  195.5 30.2 %units.1 = (bf16[2048,3072]{1,0:T(8,128)(2,1)}, bf16[2048,3072]{1,0:T(8,128)(2,1)}) custom-call(s32[7]{0:T(128)} %concatenate.47.sc, bf16[2048,768]{1,0:T(8,128)(2,1)} %bitcast.111, bf16[2048,768]{1,0:T(8,128)(2,1)} %bitcast.108, bf16[768,1536]{1,0:T(8,128)(2,1)} %get-tuple-element.481.up_own, bf16[768,1536]{1,0:T(8,128)(2,1)} %collective-permute-done.42.up_far, ...), custom_call_target="tpu_custom_call" | custom-call | flops 19327352832 | bytes 34603008 | tf_op jit(solution)/shard_map/units/pallas_call | solution.py:365
  225.8 28.1 %post.1 = (bf16[2,512,768]{2,1,0:T(8,128)(2,1)}, bf16[2,512,768]{2,1,0:T(8,128)(2,1)}, bf16[12,512,256]{2,1,0:T(8,128)(2,1)}, f32[1,768]{1,0:T(1,128)}) custom-call(s32[7]{0:T(128)} %concatenate.47.sc, bf16[4,512,768]{2,1,0:T(8,128)(2,1)} %get-tuple-element.478.resid, bf16[4,512,3072]{2,1,0:T(8,128)(2,1)} %bitcast.115, bf16[4,512,3072]{2,1,0:T(8,128)(2,1)} %bitcast.116, ...), custom_call_target="tpu_custom_call" | custom-call | flops 12079595520 | bytes 37748736 | tf_op jit(solution)/shard_map/post/pallas_call | solution.py:569
  253.9 10.0 %unmix.2 = (bf16[384,1024]{1,0:T(8,128)(2,1)}, bf16[384,1024]{1,0:T(8,128)(2,1)}, bf16[384,1024]{1,0:T(8,128)(2,1)}, bf16[384,1024]{1,0:T(8,128)(2,1)}, bf16[12,...) custom-call(s32[7]{0:T(128)} %concatenate.47.sc, bf16[12,1024,128]{2,1,0:T(8,128)(2,1)} %values.1.refs_12_.refs_4_.v_own, ...), custom_call_target="tpu_custom_call" | custom-call | flops 4831838208 | bytes 33030144 | tf_op jit(solution)/shard_map/unmix/pallas_call | solution.py:665
  269.2 19.5 %unmix.3 = (bf16[384,1024]{1,0:T(8,128)(2,1)}, bf16[384,1024]{1,0:T(8,128)(2,1)}, bf16[384,1024]{1,0:T(8,128)(2,1)}, bf16[384,1024]{1,0:T(8,128)(2,1)}, bf16[384...) custom-call(s32[7]{0:T(128)} %concatenate.47.sc, ...), custom_call_target="tpu_custom_call", output_to_operand_aliasing={{12}: (7, {}), {13}: (8, {})} | custom-call | flops 4831838208 | bytes 33030144 | tf_op jit(solution)/shard_map/unmix/pallas_call | solution.py:665
  301.4 14.2 %up_grad.1 = (bf16[768,1536]{1,0:T(8,128)(2,1)S(1)}, bf16[768,1536]{1,0:T(8,128)(2,1)}) custom-call(s32[7]{0:T(128)S(1)} %copy-done.36, bf16[2048,768]{1,0:T(8,128)(2,1)S(1)} %bitcast.112, bf16[2048,3072]{1,0:T(8,128)(2,1)S(1)} %copy-done.60), custom_call_target="tpu_custom_call" | custom-call | flops 9663676416 | bytes 15728640 | tf_op jit(solution)/shard_map/up_grad/pallas_call | solution.py:428
  324.2 12.9 %down_grad.1 = (bf16[3072,384]{1,0:T(8,128)(2,1)S(1)}, bf16[3072,384]{1,0:T(8,128)(2,1)S(1)}) custom-call(s32[7]{0:T(128)S(1)} %copy-done.36, bf16[2048,3072]{1,0:T(8,128)(2,1)S(1)} %copy-done.59, bf16[2048,768]{1,0:T(8,128)(2,1)S(1)} %bitcast.109), custom_call_target="tpu_custom_call" | custom-call | flops 9663676416 | bytes 15728640 | tf_op jit(solution)/shard_map/down_grad/pallas_call | solution.py:397
  349.3 5.3 %out_grad.1 = (bf16[768,384]{1,0:T(8,128)(2,1)S(1)}, bf16[768,384]{1,0:T(8,128)(2,1)S(1)}) custom-call(s32[7]{0:T(128)S(1)} %copy-done.36, bf16[4,512,768]{2,1,0:T(8,128)(2,1)S(1)} %copy-done.41, bf16[2,512,768]{2,1,0:T(8,128)(2,1)S(1)} %copy-done.61, bf16[2,512,768]{2,1,0:T(8,128)(2,1)S(1)} %copy-done.47), custom_call_target="tpu_custom_call" | custom-call | flops 2415919104 | bytes 6291456 | tf_op jit(solution)/shard_map/out_grad/pallas_call | solution.py:468
  378.6 15.7 %out.3 = (bf16[2,512,768]{2,1,0:T(8,128)(2,1)S(1)}, bf16[2,512,768]{2,1,0:T(8,128)(2,1)}) custom-call(s32[7]{0:T(128)S(1)} %copy-done.36, bf16[4,512,3072]{2,1,0:T(8,128)(2,1)} %bitcast.114, bf16[4,512,768]{2,1,0:T(8,128)(2,1)S(1)} %copy-done.38, bf16[3072,384]{1,0:T(8,128)(2,1)S(1)} %copy-done.44, bf16[3072,384]{1,0:T(8,128)(2,1)} %collective-permute-done.43.dn_far), custom_call_target="tpu_custom_call" | custom-call | flops 9663676416 | bytes 23592960 | tf_op jit(solution)/shard_map/out/pallas_call | solution.py:502
  418.7 13.3 %close.1 = (f32[2,8,2,64,768]{4,3,2,1,0:T(8,128)}, f32[2,8,2,64,768]{4,3,2,1,0:T(8,128)}, bf16[768,768]{1,0:T(8,128)(2,1)S(1)}, f32[1,768]{1,0:T(1,128)S(1)}) custom-call(s32[7]{0:T(128)S(1)} %copy-done.36, bf16[2,8,2,64,768]{4,3,2,1,0:T(8,128)(2,1)S(1)} %bitcast.106, bf16[2,8,64,768]{3,2,1,0:T(8,128)(2,1)S(1)} %bitcast.117, ...), custom_call_target="tpu_custom_call" | custom-call | flops 4831838208 | bytes 29884416 | tf_op jit(solution)/shard_map/close/pallas_call | solution.py:755
  445.2 8.5 %collective-permute-done.75 = bf16[4,2,32,768]{3,2,0,1:T(8,128)(2,1)S(1)} collective-permute-done((bf16[4,2,32,768]{3,2,0,1:T(8,128)(2,1)S(1)}, bf16[4,2,32,768]{3,2,0,1:T(8,128)(2,1)S(1)}, u32[]{:S(2)}, u32[]{:S(2)}) %collective-permute-start.75) | collective-permute-done | bytes 393248 | tf_op jit(solution)/shard_map/ppermute | solution.py:946
  453.8 6.3 %collective-permute-done.72 = bf16[432,384]{1,0:T(8,128)(2,1)S(1)} collective-permute-done((bf16[432,384]{1,0:T(8,128)(2,1)S(1)}, bf16[432,384]{1,0:T(8,128)(2,1)S(1)}, u32[]{:S(2)}, u32[]{:S(2)}) %collective-permute-start.72) | collective-permute-done | bytes 331808 | tf_op jit(solution)/shard_map/ppermute | solution.py:946
  (435 shorter events, 209.5 us)
Async XLA Ops:
  110.0 23.4 %collective-permute-start.35 = (bf16[12,1024,128]{2,1,0:T(8,128)(2,1)}, bf16[12,1024,128]{2,1,0:T(8,128)(2,1)}, u32[]{:S(2)}, u32[]{:S(2)}) collective-permute-start(bf16[12,1024,128]{2,1,0:T(8,128)(2,1)} %values.1.refs_12_.refs_4_.v_own), channel_id=1, source_target_pairs={{0,1},{1,0},{2,3},{3,2},{4,5},{5,4},{6,7},{7,6},{8,9},{9,8},{10,11... | collective-permute-start | bytes 9437192 | tf_op jit(solution)/shard_map/ppermute | solution.py:946
  111.0 21.4 %collective-permute-start.34 = (bf16[384,1024]{1,0:T(8,128)(2,1)S(1)}, bf16[384,1024]{1,0:T(8,128)(2,1)S(1)}, u32[]{:S(2)}, u32[]{:S(2)}) collective-permute-start(bf16[384,1024]{1,0:T(8,128)(2,1)S(1)} %collective-permute-done.30.refs_8_), channel_id=1, source_target_pairs={{0,8},{1,9},{2,10},{3,11},{4,12},{5,13},{6,14},{7,15},{8,16},{9,17... | collective-permute-start | bytes 2359304 | tf_op jit(solution)/shard_map/ppermute | solution.py:950
  134.5 20.6 %collective-permute-start.37 = (bf16[384,1024]{1,0:T(8,128)(2,1)}, bf16[384,1024]{1,0:T(8,128)(2,1)}, u32[]{:S(2)}, u32[]{:S(2)}) collective-permute-start(bf16[384,1024]{1,0:T(8,128)(2,1)} %collective-permute-done.32.refs_6_), channel_id=1, source_target_pairs={{0,8},{1,9},{2,10},{3,11},{4,12},{5,13},{6,14},{7,15},{8,16},{9,17... | collective-permute-start | bytes 2359304 | tf_op jit(solution)/shard_map/ppermute | solution.py:950
  134.6 20.5 %collective-permute-start.36 = (bf16[384,1024]{1,0:T(8,128)(2,1)}, bf16[384,1024]{1,0:T(8,128)(2,1)}, u32[]{:S(2)}, u32[]{:S(2)}) collective-permute-start(bf16[384,1024]{1,0:T(8,128)(2,1)} %collective-permute-done.32.refs_6_), channel_id=1, source_target_pairs={{0,2},{1,3},{2,0},{3,1},{4,6},{5,7},{6,4},{7,5},{8,10},{9,11},{10,... | collective-permute-start | bytes 2359304 | tf_op jit(solution)/shard_map/ppermute | solution.py:946
  265.1 23.6 %collective-permute-start.45 = (bf16[384,1024]{1,0:T(8,128)(2,1)}, bf16[384,1024]{1,0:T(8,128)(2,1)S(1)}, u32[]{:S(2)}, u32[]{:S(2)}) collective-permute-start(bf16[384,1024]{1,0:T(8,128)(2,1)} %get-tuple-element.496), channel_id=1, source_target_pairs={{0,24},{1,25},{2,26},{3,27},{4,28},{5,29},{6,30},{7,31},{8,0},{9,1... | collective-permute-start | bytes 2359304 | tf_op jit(solution)/shard_map/ppermute | solution.py:950
  267.5 21.2 %collective-permute-start.46 = (bf16[384,1024]{1,0:T(8,128)(2,1)}, bf16[384,1024]{1,0:T(8,128)(2,1)S(1)}, u32[]{:S(2)}, u32[]{:S(2)}) collective-permute-start(bf16[384,1024]{1,0:T(8,128)(2,1)} %get-tuple-element.497), channel_id=1, source_target_pairs={{0,2},{1,3},{2,0},{3,1},{4,6},{5,7},{6,4},{7,5},{8,10},{9,11},{10,... | collective-permute-start | bytes 2359304 | tf_op jit(solution)/shard_map/ppermute | solution.py:946
  268.0 20.7 %collective-permute-start.47 = (bf16[384,1024]{1,0:T(8,128)(2,1)}, bf16[384,1024]{1,0:T(8,128)(2,1)}, u32[]{:S(2)}, u32[]{:S(2)}) collective-permute-start(bf16[384,1024]{1,0:T(8,128)(2,1)} %get-tuple-element.498), channel_id=1, source_target_pairs={{0,4},{1,5},{2,6},{3,7},{4,0},{5,1},{6,2},{7,3},{8,12},{9,13},{10,... | collective-permute-start | bytes 2359304 | tf_op jit(solution)/shard_map/ppermute | solution.py:946
  288.7 27.0 %collective-permute-start.51 = (bf16[12,1024,128]{2,1,0:T(8,128)(2,1)}, bf16[12,1024,128]{2,1,0:T(8,128)(2,1)S(1)}, u32[]{:S(2)}, u32[]{:S(2)}) collective-permute-start(bf16[12,1024,128]{2,1,0:T(8,128)(2,1)} %get-tuple-element.535), channel_id=1, source_target_pairs={{0,1},{1,0},{2,3},{3,2},{4,5},{5,4},{6,7},{7,6},{8,9},{9,8},{10,11... | collective-permute-start | bytes 9437192 | tf_op jit(solution)/shard_map/ppermute | solution.py:946
  288.8 26.9 %collective-permute-start.48 = (bf16[384,1024]{1,0:T(8,128)(2,1)}, bf16[384,1024]{1,0:T(8,128)(2,1)S(1)}, u32[]{:S(2)}, u32[]{:S(2)}) collective-permute-start(bf16[384,1024]{1,0:T(8,128)(2,1)} %get-tuple-element.530), channel_id=1, source_target_pairs={{0,24},{1,25},{2,26},{3,27},{4,28},{5,29},{6,30},{7,31},{8,0},{9,1... | collective-permute-start | bytes 2359304 | tf_op jit(solution)/shard_map/ppermute | solution.py:950
  289.5 26.1 %collective-permute-start.49 = (bf16[384,1024]{1,0:T(8,128)(2,1)}, bf16[384,1024]{1,0:T(8,128)(2,1)S(1)}, u32[]{:S(2)}, u32[]{:S(2)}) collective-permute-start(bf16[384,1024]{1,0:T(8,128)(2,1)} %get-tuple-element.531), channel_id=1, source_target_pairs={{0,2},{1,3},{2,0},{3,1},{4,6},{5,7},{6,4},{7,5},{8,10},{9,11},{10,... | collective-permute-start | bytes 2359304 | tf_op jit(solution)/shard_map/ppermute | solution.py:946
  294.0 21.6 %collective-permute-start.50 = (bf16[384,1024]{1,0:T(8,128)(2,1)}, bf16[384,1024]{1,0:T(8,128)(2,1)S(1)}, u32[]{:S(2)}, u32[]{:S(2)}) collective-permute-start(bf16[384,1024]{1,0:T(8,128)(2,1)} %get-tuple-element.532), channel_id=1, source_target_pairs={{0,4},{1,5},{2,6},{3,7},{4,0},{5,1},{6,2},{7,3},{8,12},{9,13},{10,... | collective-permute-start | bytes 2359304 | tf_op jit(solution)/shard_map/ppermute | solution.py:946
  315.7 24.1 %collective-permute-start.55 = (bf16[768,1536]{1,0:T(8,128)(2,1)}, bf16[768,1536]{1,0:T(8,128)(2,1)S(1)}, u32[]{:S(2)}, u32[]{:S(2)}) collective-permute-start(bf16[768,1536]{1,0:T(8,128)(2,1)} %get-tuple-element.554), channel_id=1, source_target_pairs={{0,1},{1,0},{2,3},{3,2},{4,5},{5,4},{6,7},{7,6},{8,9},{9,8},{10,11... | collective-permute-start | bytes 7077896 | tf_op jit(solution)/shard_map/ppermute | solution.py:946
  315.8 21.3 %collective-permute-start.52 = (bf16[384,1024]{1,0:T(8,128)(2,1)}, bf16[384,1024]{1,0:T(8,128)(2,1)S(1)}, u32[]{:S(2)}, u32[]{:S(2)}) collective-permute-start(bf16[384,1024]{1,0:T(8,128)(2,1)} %get-tuple-element.543), channel_id=1, source_target_pairs={{0,24},{1,25},{2,26},{3,27},{4,28},{5,29},{6,30},{7,31},{8,0},{9,1... | collective-permute-start | bytes 2359304 | tf_op jit(solution)/shard_map/ppermute | solution.py:950
  317.3 20.7 %collective-permute-start.53 = (bf16[384,1024]{1,0:T(8,128)(2,1)}, bf16[384,1024]{1,0:T(8,128)(2,1)S(1)}, u32[]{:S(2)}, u32[]{:S(2)}) collective-permute-start(bf16[384,1024]{1,0:T(8,128)(2,1)} %get-tuple-element.549), channel_id=1, source_target_pairs={{0,2},{1,3},{2,0},{3,1},{4,6},{5,7},{6,4},{7,5},{8,10},{9,11},{10,... | collective-permute-start | bytes 2359304 | tf_op jit(solution)/shard_map/ppermute | solution.py:946
  339.8 22.0 %collective-permute-start.57 = (bf16[384,1024]{1,0:T(8,128)(2,1)}, bf16[384,1024]{1,0:T(8,128)(2,1)S(1)}, u32[]{:S(2)}, u32[]{:S(2)}) collective-permute-start(bf16[384,1024]{1,0:T(8,128)(2,1)} %get-tuple-element.565), channel_id=1, source_target_pairs={{0,2},{1,3},{2,0},{3,1},{4,6},{5,7},{6,4},{7,5},{8,10},{9,11},{10,... | collective-permute-start | bytes 2359304 | tf_op jit(solution)/shard_map/ppermute | solution.py:946
  340.8 21.0 %collective-permute-start.58 = (bf16[384,1024]{1,0:T(8,128)(2,1)}, bf16[384,1024]{1,0:T(8,128)(2,1)S(1)}, u32[]{:S(2)}, u32[]{:S(2)}) collective-permute-start(bf16[384,1024]{1,0:T(8,128)(2,1)} %get-tuple-element.566), channel_id=1, source_target_pairs={{0,4},{1,5},{2,6},{3,7},{4,0},{5,1},{6,2},{7,3},{8,12},{9,13},{10,... | collective-permute-start | bytes 2359304 | tf_op jit(solution)/shard_map/ppermute | solution.py:946
  369.1 26.4 %collective-permute-start.65 = (bf16[432,384]{1,0:T(8,128)(2,1)S(1)}, bf16[432,384]{1,0:T(8,128)(2,1)S(1)}, u32[]{:S(2)}, u32[]{:S(2)}) collective-permute-start(bf16[432,384]{1,0:T(8,128)(2,1)S(1)} %get-tuple-element.614), channel_id=1, source_target_pairs={{0,2},{1,3},{2,0},{3,1},{4,6},{5,7},{6,4},{7,5},{8,10},{9,11},{10,... | collective-permute-start | bytes 995336 | tf_op jit(solution)/shard_map/ppermute | solution.py:946
  369.6 25.9 %collective-permute-start.66 = (bf16[432,384]{1,0:T(8,128)(2,1)S(1)}, bf16[432,384]{1,0:T(8,128)(2,1)S(1)}, u32[]{:S(2)}, u32[]{:S(2)}) collective-permute-start(bf16[432,384]{1,0:T(8,128)(2,1)S(1)} %get-tuple-element.615), channel_id=1, source_target_pairs={{0,4},{1,5},{2,6},{3,7},{4,0},{5,1},{6,2},{7,3},{8,12},{9,13},{10,... | collective-permute-start | bytes 995336 | tf_op jit(solution)/shard_map/ppermute | solution.py:946
  370.5 25.0 %collective-permute-start.63 = (bf16[384,1024]{1,0:T(8,128)(2,1)S(1)}, bf16[384,1024]{1,0:T(8,128)(2,1)S(1)}, u32[]{:S(2)}, u32[]{:S(2)}) collective-permute-start(bf16[384,1024]{1,0:T(8,128)(2,1)S(1)} %copy-done.101), channel_id=1, source_target_pairs={{0,4},{1,5},{2,6},{3,7},{4,0},{5,1},{6,2},{7,3},{8,12},{9,13},{10,... | collective-permute-start | bytes 2359304 | tf_op jit(solution)/shard_map/ppermute | solution.py:946
  372.1 24.3 %collective-permute-start.61 = (bf16[384,1024]{1,0:T(8,128)(2,1)S(1)}, bf16[384,1024]{1,0:T(8,128)(2,1)S(1)}, u32[]{:S(2)}, u32[]{:S(2)}) collective-permute-start(bf16[384,1024]{1,0:T(8,128)(2,1)S(1)} %get-tuple-element.597), channel_id=1, source_target_pairs={{0,24},{1,25},{2,26},{3,27},{4,28},{5,29},{6,30},{7,31},{8,0},{9,1... | collective-permute-start | bytes 2359304 | tf_op jit(solution)/shard_map/ppermute | solution.py:950
  399.6 33.4 %collective-permute-start.69 = (bf16[432,384]{1,0:T(8,128)(2,1)S(1)}, bf16[432,384]{1,0:T(8,128)(2,1)}, u32[]{:S(2)}, u32[]{:S(2)}) collective-permute-start(bf16[432,384]{1,0:T(8,128)(2,1)S(1)} %add_convert_fusion.6), channel_id=1, source_target_pairs={{0,4},{1,5},{2,6},{3,7},{4,0},{5,1},{6,2},{7,3},{8,12},{9,13},{10,... | collective-permute-start | bytes 995336 | tf_op jit(solution)/shard_map/ppermute | solution.py:946
  400.5 32.5 %collective-permute-start.67 = (bf16[432,384]{1,0:T(8,128)(2,1)}, bf16[432,384]{1,0:T(8,128)(2,1)}, u32[]{:S(2)}, u32[]{:S(2)}) collective-permute-start(bf16[432,384]{1,0:T(8,128)(2,1)} %copy-done.58), channel_id=1, source_target_pairs={{0,24},{1,25},{2,26},{3,27},{4,28},{5,29},{6,30},{7,31},{8,0},{9,1... | collective-permute-start | bytes 995336 | tf_op jit(solution)/shard_map/ppermute | solution.py:950
  405.0 28.0 %collective-permute-start.68 = (bf16[432,384]{1,0:T(8,128)(2,1)}, bf16[432,384]{1,0:T(8,128)(2,1)}, u32[]{:S(2)}, u32[]{:S(2)}) collective-permute-start(bf16[432,384]{1,0:T(8,128)(2,1)} %copy-done.57), channel_id=1, source_target_pairs={{0,2},{1,3},{2,0},{3,1},{4,6},{5,7},{6,4},{7,5},{8,10},{9,11},{10,... | collective-permute-start | bytes 995336 | tf_op jit(solution)/shard_map/ppermute | solution.py:946
  445.1 22.9 %collective-permute-start.80 = (f32[3,64,1024]{2,1,0:T(8,128)S(1)}, f32[3,64,1024]{2,1,0:T(8,128)S(1)}, u32[]{:S(2)}, u32[]{:S(2)}) collective-permute-start(f32[3,64,1024]{2,1,0:T(8,128)S(1)} %get-tuple-element.693), channel_id=1, source_target_pairs={{0,1},{1,0},{2,3},{3,2},{4,5},{5,4},{6,7},{7,6},{8,9},{9,8},{10,11... | collective-permute-start | bytes 2359304 | tf_op jit(solution)/shard_map/ppermute | solution.py:946
  (166 other events, 1925.9 us)
